TPU v7x, 32 devices: a whole 2x2x4 slice. The times are simulated.
32 devices in a mesh: section: 8 (over z, y), tensor: 4 (over x, core).
Axes of the slice: x: 2, y: 2, z: 4, core: 2. Of those that a mesh axis runs over, the one named last changes fastest.
Arguments:
- layer_input: bfloat16 [8, 512, 6144], P('section', None, 'tensor'), may hold values from -200 to 200
- grad_input: bfloat16 [8, 512, 6144], P('section', None, 'tensor'), may hold values from -8 to 8
- stashed: bfloat16 [8, 2, 512, 6144], P('section', None, None, 'tensor'), may hold values from -200 to 200
- eviction: int32 [8], P('section'), may hold values from 0 to 1, as said below
- query_gain: float32 [8, 6144], P('section', 'tensor'), may hold values from 0.5 to 2
- key_gain: float32 [8, 6144], P('section', 'tensor'), may hold values from 0.5 to 2
Outputs:
- layer_output: bfloat16 [8, 512, 6144], P('section', None, 'tensor')
- grad_output: bfloat16 [8, 512, 6144], P('section', None, 'tensor')
Inputs may be any that keep to these rules, and one draw needn't show every extreme that they name: `eviction`: section 0 always evicts.
All inputs are finite; a program needn't handle non-finite values.
Results may differ from a plain program's by a relative error of at most 0.0078.
Values may be sent and summed in bfloat16 or wider, within the bound.
No kernel may reach another device: no remote copies, remote signals or barrier semaphores. Data moves between devices by JAX's collectives and lax.ppermute only.
A program may use at most 128 MiB of HBM per device.

v0:
```python
import math

import jax
import jax.numpy as jnp
from jax import lax
from jax.sharding import PartitionSpec as P

HDIM = 128
DW = 6144


EPSILON = 1e-05


def passed_along(x, axis, by):
    size = lax.axis_size(axis)
    return lax.ppermute(x, axis, [(i, (i + by) % size) for i in range(size)])


def local_squares(activations):
    widened = activations.astype(jnp.float32)
    return jnp.sum(widened * widened, axis=-1)


def normalize(activations, square_total, gain_query, gain_key):
    widened = activations.astype(jnp.float32)
    factor = lax.rsqrt(square_total / DW + EPSILON)
    normed = widened * factor[:, None]
    queries = (normed * gain_query).astype(jnp.bfloat16)
    keys_all = (normed * gain_key).astype(jnp.bfloat16)
    values = normed.astype(jnp.bfloat16)
    return (widened, factor, queries, keys_all, values)


def split_heads(matrix):
    return matrix.reshape(matrix.shape[0], matrix.shape[1] // HDIM, HDIM)


def attention_weights(query_heads, key_heads):
    length = query_heads.shape[0]
    scores = jnp.einsum(
        "qhd,khd->hqk", query_heads, key_heads, preferred_element_type=jnp.float32
    ) * (1.0 / math.sqrt(HDIM))
    causal = jnp.arange(length)[:, None] >= jnp.arange(length)[None, :]
    scores = jnp.where(causal[None], scores, -1e30)
    shifted = scores - jnp.max(scores, axis=-1, keepdims=True)
    exponent = jnp.exp(shifted)
    return exponent / jnp.sum(exponent, axis=-1, keepdims=True)


def forward_layer(activations, square_total, gain_query, gain_key):
    widened, factor, queries, keys_all, values = normalize(
        activations, square_total, gain_query, gain_key
    )
    weights = attention_weights(split_heads(queries), split_heads(keys_all))
    rounded = weights.astype(jnp.bfloat16)
    mixed_heads = jnp.einsum(
        "hqk,khd->qhd", rounded, split_heads(values), preferred_element_type=jnp.float32
    )
    return (widened + mixed_heads.reshape(widened.shape)).astype(jnp.bfloat16)


def backward_terms(activations, square_total, upstream, gain_query, gain_key):
    widened, factor, queries, keys_all, values = normalize(
        activations, square_total, gain_query, gain_key
    )
    query_heads = split_heads(queries)
    key_heads = split_heads(keys_all)
    weights = attention_weights(query_heads, key_heads)
    rounded = weights.astype(jnp.bfloat16)
    grad_heads = split_heads(upstream)
    d_values = jnp.einsum("hqk,qhd->khd", rounded, grad_heads, preferred_element_type=jnp.float32)
    d_weights = jnp.einsum(
        "qhd,khd->hqk", grad_heads, split_heads(values), preferred_element_type=jnp.float32
    )
    row_delta = jnp.sum(weights * d_weights, axis=-1, keepdims=True)
    d_scores = (weights * (d_weights - row_delta) * (1.0 / math.sqrt(HDIM))).astype(jnp.bfloat16)
    d_queries = jnp.einsum("hqk,khd->qhd", d_scores, key_heads, preferred_element_type=jnp.float32)
    d_keys = jnp.einsum("hqk,qhd->khd", d_scores, query_heads, preferred_element_type=jnp.float32)
    flat_shape = widened.shape
    d_normed = (
        d_queries.reshape(flat_shape) * gain_query
        + d_keys.reshape(flat_shape) * gain_key
        + d_values.reshape(flat_shape)
    )
    partial_inner = jnp.sum(d_normed * widened, axis=-1)
    return (widened, factor, d_normed, partial_inner)


def local(layer_input, grad_input, stashed, eviction, query_gain, key_gain):
    half_sections = lax.axis_size("section") // 2
    current = layer_input[0]
    upstream = grad_input[0]
    gain_query = query_gain[0]
    gain_key = key_gain[0]
    fetched = passed_along(stashed[0, 1], "section", -half_sections)
    chosen = jnp.where(eviction[0] == 1, fetched, stashed[0, 0])
    forward_total = lax.psum(local_squares(current), "tensor")
    recompute_total = lax.psum(local_squares(chosen), "tensor")
    output = forward_layer(current, forward_total, gain_query, gain_key)
    widened, factor, d_normed, partial_inner = backward_terms(
        chosen, recompute_total, upstream, gain_query, gain_key
    )
    inner_sum = lax.psum(partial_inner, "tensor")
    result = (
        upstream.astype(jnp.float32)
        + factor[:, None] * d_normed
        - widened * (factor**3)[:, None] * inner_sum[:, None] / DW
    )
    result = result.astype(jnp.bfloat16)
    passed = passed_along(result, "section", -1)
    return (output[None], passed[None])


def solution(mesh):
    placed = (
        P("section", None, "tensor"),
        P("section", None, "tensor"),
        P("section", None, None, "tensor"),
        P("section"),
        P("section", "tensor"),
        P("section", "tensor"),
    )
    return jax.shard_map(
        local,
        mesh=mesh,
        in_specs=placed,
        out_specs=(P("section", None, "tensor"), P("section", None, "tensor")),
        check_vma=False,
    )
```

profile of v0, /device:TPU:0, one launch (start us, length us, event | category | flops | bytes accessed | tf_op | source)
XLA Modules:
  0.0 206.2 jit_solution(16309120911475498252)
XLA Ops:
  0.6 2.1 %fusion.48 = (bf16[1,1,512,1536]{3,2,1,0:T(8,128)(2,1)S(1)}, bf16[1,1,512,1536]{3,2,1,0:T(8,128)(2,1)S(1)}) fusion(bf16[1,2,512,1536]{3,2,1,0:T(8,128)(2,1)} %param.8), kind=kLoop, calls=%fused_computation.73 | loop fusion | bytes 6291456 | tf_op jit(solution)/shard_map/slice | solution.py:97
  2.7 0.0 copy-start.4
  2.7 0.0 copy-start.5
  2.7 1.6 copy.53
  4.3 0.0 copy-start.3
  4.3 4.0 %collective-permute-start = (bf16[512,1536]{0,1:T(8,128)(2,1)}, bf16[512,1536]{0,1:T(8,128)(2,1)}, u32[]{:S(2)}, u32[]{:S(2)}) collective-permute-start(bf16[512,1536]{0,1:T(8,128)(2,1)} %bitcast.80), channel_id=1, source_target_pairs={{0,16},{4,20},{8,24},{12,28},{16,0},{20,4},{24,8},{28,12},{1,17},{... | collective-permute-start | bytes 4718600 | tf_op jit(solution)/shard_map/ppermute | solution.py:17
  8.4 1.6 copy.54
  10.6 0.0 copy-done.4
  10.6 0.0 copy-done.5
  10.7 0.0 copy-done.3
  10.7 1.6 copy.30
  12.3 1.7 copy.26
  14.0 0.1 iota_compare_fusion
  14.1 0.4 multiply_reduce_fusion
  14.5 62.3 %collective-permute-done = bf16[512,1536]{0,1:T(8,128)(2,1)} collective-permute-done((bf16[512,1536]{0,1:T(8,128)(2,1)}, bf16[512,1536]{0,1:T(8,128)(2,1)}, u32[]{:S(2)}, u32[]{:S(2)}) %collective-permute-start) | collective-permute-done | bytes 1572896 | tf_op jit(solution)/shard_map/ppermute | solution.py:17
  76.8 2.5 %fusion.25 = (f32[512]{0:T(512)S(1)}, bf16[512,1536]{0,1:T(8,128)(2,1)S(1)}) fusion(bf16[512,1536]{0,1:T(8,128)(2,1)} %collective-permute-done, bf16[1,1,512,1536]{2,3,1,0:T(8,128)(2,1)} %copy.54, pred[]{:T(512)} %bitcast.4), kind=kLoop, calls=%fused_computation.37 | loop fusion | flops 3145216 | bytes 4720641 | tf_op jit(solution)/shard_map/reduce_sum | solution.py:22
  79.3 6.0 %psum.22 = f32[512]{0:T(512)S(1)} all-reduce(f32[512]{0:T(512)S(1)} %get-tuple-element.8), channel_id=1, replica_groups=mesh['section'=8,'tensor'=4] {'tensor'}, use_global_device_ids=true, to_apply=%region_5.6 | all-reduce | flops 512 | bytes 4096 | tf_op jit(solution)/shard_map/psum | solution.py:99
  85.2 0.0 copy-start
  85.3 2.1 %fusion.20 = (bf16[512,1536]{0,1:T(8,128)(2,1)S(1)}, bf16[512,1536]{0,1:T(8,128)(2,1)}, bf16[512,1536]{0,1:T(8,128)(2,1)}) fusion(bf16[512,1536]{0,1:T(8,128)(2,1)S(1)} %get-tuple-element.9, f32[512]{0:T(512)S(1)} %get-tuple-element.16, f32[1536]{0:T(1024)S(1)} %reduce.2, f32[1536]{0:T(1024)S(1)} %reduce.1), kind=kLoop, calls=%fused_computation.32 | loop fusion | flops 5505024 | bytes 6305792 | tf_op jit(solution)/shard_map/convert_element_type | solution.py:31
  87.4 0.0 copy-done
  87.4 6.3 %fusion.53 = f32[12,512,512]{2,1,0:T(8,128)} fusion(bf16[512,12,128]{0,2,1:T(8,128)(2,1)S(1)} %bitcast.79, bf16[512,12,128]{0,2,1:T(8,128)(2,1)S(1)} %bitcast.78), kind=kOutput, calls=%fused_computation.78 | convolution fusion | flops 805306368 | bytes 15728640 | tf_op jit(solution)/shard_map/qhd,khd->hqk/dot_general | solution.py:73
  93.7 11.1 %fusion.49 = (f32[12,512]{1,0:T(8,128)S(1)}, f32[12,512,512]{1,2,0:T(8,128)}) fusion(pred[512,512]{0,1:T(8,128)(4,1)S(1)} %iota_compare_fusion, bf16[512,12,128]{0,2,1:T(8,128)(2,1)} %bitcast.81, bf16[512,12,128]{0,2,1:T(8,128)(2,1)} %bitcast.83), kind=kOutput, calls=%fused_computation.74 | convolution fusion | flops 817889792 | bytes 16015360 | tf_op jit(solution)/shard_map/sub | solution.py:46
  104.7 19.7 %fusion.19 = f32[12,128,512]{2,1,0:T(8,128)} fusion(bf16[512,12,128]{0,2,1:T(8,128)(2,1)} %bitcast.84, f32[12,512,512]{2,1,0:T(8,128)} %fusion.53, f32[12,512,512]{1,2,0:T(8,128)} %get-tuple-element.18, f32[12,512]{1,0:T(8,128)S(1)} %get-tuple-element.17), kind=kOutput, calls=%fused_computation.31 | convolution fusion | flops 827333120 | bytes 29908992 | tf_op jit(solution)/shard_map/hqk,khd->qhd/dot_general | solution.py:78
  124.5 19.9 %fusion.18 = f32[12,128,512]{2,1,0:T(8,128)} fusion(bf16[512,12,128]{0,2,1:T(8,128)(2,1)} %bitcast.82, f32[12,512,512]{2,1,0:T(8,128)} %fusion.53, f32[12,512,512]{1,2,0:T(8,128)} %get-tuple-element.18, f32[12,512]{1,0:T(8,128)S(1)} %get-tuple-element.17), kind=kOutput, calls=%fused_computation.30 | convolution fusion | flops 827333120 | bytes 29908992 | tf_op jit(solution)/shard_map/hqk,qhd->khd/dot_general | solution.py:79
  144.3 0.0 copy-start.1
  144.3 0.0 copy-start.2
  144.3 7.3 %fusion.8 = f32[12,512,128]{1,2,0:T(8,128)S(1)} fusion(bf16[512,12,128]{0,2,1:T(8,128)(2,1)} %bitcast.77, f32[12,512,512]{1,2,0:T(8,128)} %get-tuple-element.18, f32[12,512]{1,0:T(8,128)S(1)} %get-tuple-element.17), kind=kOutput, calls=%fused_computation.15 | convolution fusion | flops 811597824 | bytes 17326080 | tf_op jit(solution)/shard_map/hqk,qhd->khd/dot_general | solution.py:72
  151.6 0.0 copy-done.1
  151.6 0.0 copy-done.2
  151.7 2.4 %fusion.30 = (f32[512]{0:T(512)S(1)}, f32[512,1536]{0,1:T(8,128)}) fusion(bf16[512,1536]{0,1:T(8,128)(2,1)S(1)} %get-tuple-element.9, f32[12,512,128]{1,2,0:T(8,128)S(1)} %fusion.8, f32[1536]{0:T(1024)S(1)} %reduce.2, f32[12,128,512]{2,1,0:T(8,128)S(1)} %copy-done.2, f32[1536]{0:T(1024)S(1)} %reduce.1, f32[12,128,512]{2,1,0:T(8,128)S(1)} %copy-done.1), kind=kLoop, calls=%fused_computation.42 | loop fusion | flops 5504512 | bytes 14170112 | tf_op jit(solution)/shard_map/reduce_sum | solution.py:86
  154.1 6.5 %all-reduce = (f32[512]{0:T(512)S(1)}, f32[512]{0:T(512)S(1)}) all-reduce(f32[512]{0:T(512)S(1)} %multiply_reduce_fusion, f32[512]{0:T(512)S(1)} %get-tuple-element.6), channel_id=1, replica_groups=mesh['section'=8,'tensor'=4] {'tensor'}, use_global_device_ids=true, to_apply=%region_1.2 | all-reduce | flops 1024 | bytes 8192 | tf_op jit(solution)/shard_map/psum | solution.py:98
  160.6 4.4 %fusion.29 = bf16[512,1536]{0,1:T(8,128)(2,1)} fusion(bf16[512,1536]{0,1:T(8,128)(2,1)S(1)} %get-tuple-element.9, f32[512,1536]{0,1:T(8,128)} %get-tuple-element.7, bf16[1,512,1536]{1,2,0:T(8,128)(2,1)} %copy.30, f32[512]{0:T(512)S(1)} %get-tuple-element.5, f32[512]{0:T(512)S(1)} %get-tuple-element.15, f32[512]{0:T(512)S(1)} %get-tuple-element.16), kind=kLoop, calls=%fused_computation.41 | loop fusion | flops 7077888 | bytes 7870464 | tf_op jit(solution)/shard_map/convert_element_type | solution.py:110
  165.0 4.9 %collective-permute-start.1 = (bf16[512,1536]{0,1:T(8,128)(2,1)}, bf16[512,1536]{0,1:T(8,128)(2,1)}, u32[]{:S(2)}, u32[]{:S(2)}) collective-permute-start(bf16[512,1536]{0,1:T(8,128)(2,1)} %fusion.29), channel_id=1, source_target_pairs={{0,28},{4,0},{8,4},{12,8},{16,12},{20,16},{24,20},{28,24},{1,29},{... | collective-permute-start | bytes 4718600 | tf_op jit(solution)/shard_map/ppermute | solution.py:17
  169.9 1.9 fusion.33
  171.8 8.2 %fusion.50 = (f32[12,512]{1,0:T(8,128)S(1)}, f32[12,512,512]{1,2,0:T(8,128)}) fusion(f32[12,512,512]{1,2,0:T(8,128)S(1)} %fusion.33, pred[512,512]{0,1:T(8,128)(4,1)S(1)} %iota_compare_fusion), kind=kOutput, calls=%fused_computation.75 | output fusion | flops 18874880 | bytes 25452544 | tf_op jit(solution)/shard_map/sub | solution.py:46
  180.0 5.7 %fusion.14 = f32[12,128,512]{2,1,0:T(8,128)S(1)} fusion(f32[12,512,512]{1,2,0:T(8,128)} %get-tuple-element.20, f32[12,512]{1,0:T(8,128)S(1)} %get-tuple-element.19, f32[512]{0:T(512)S(1)} %add_rsqrt_fusion.1, bf16[512,12,128]{0,2,1:T(8,128)(2,1)S(1)} %bitcast.76), kind=kOutput, calls=%fused_computation.22 | convolution fusion | flops 813957120 | bytes 17328128 | tf_op jit(solution)/shard_map/hqk,khd->qhd/dot_general | solution.py:57
  185.7 0.6 fusion.32
  186.4 1.6 copy.41
  187.9 15.7 %collective-permute-done.1 = bf16[512,1536]{0,1:T(8,128)(2,1)} collective-permute-done((bf16[512,1536]{0,1:T(8,128)(2,1)}, bf16[512,1536]{0,1:T(8,128)(2,1)}, u32[]{:S(2)}, u32[]{:S(2)}) %collective-permute-start.1) | collective-permute-done | bytes 1572896 | tf_op jit(solution)/shard_map/ppermute | solution.py:17
  203.6 2.6 %copy.42 = bf16[1,512,1536]{2,1,0:T(8,128)(2,1)} copy(bf16[1,512,1536]{1,2,0:T(8,128)(2,1)} %bitcast.18) | data formatting | bytes 3145728
  (4 shorter events, 0.1 us)
Async XLA Ops:
  2.7 7.9 %copy-start.4 = (f32[1,1536]{1,0:T(1,128)S(1)}, f32[1,1536]{1,0:T(1,128)}, u32[]{:S(2)}) copy-start(f32[1,1536]{1,0:T(1,128)} %param.10) | copy-start | bytes 18436
  2.7 7.9 %copy-start.5 = (f32[1,1536]{1,0:T(1,128)S(1)}, f32[1,1536]{1,0:T(1,128)}, u32[]{:S(2)}) copy-start(f32[1,1536]{1,0:T(1,128)} %param.11) | copy-start | bytes 18436
  4.3 6.3 %copy-start.3 = (bf16[1,512,1536]{2,1,0:T(8,128)(2,1)S(1)}, bf16[1,512,1536]{2,1,0:T(8,128)(2,1)}, u32[]{:S(2)}) copy-start(bf16[1,512,1536]{2,1,0:T(8,128)(2,1)} %param.7) | copy-start | bytes 4718596
  4.3 72.4 %collective-permute-start = (bf16[512,1536]{0,1:T(8,128)(2,1)}, bf16[512,1536]{0,1:T(8,128)(2,1)}, u32[]{:S(2)}, u32[]{:S(2)}) collective-permute-start(bf16[512,1536]{0,1:T(8,128)(2,1)} %bitcast.80), channel_id=1, source_target_pairs={{0,16},{4,20},{8,24},{12,28},{16,0},{20,4},{24,8},{28,12},{1,17},{... | collective-permute-start | bytes 4718600 | tf_op jit(solution)/shard_map/ppermute | solution.py:17
  85.2 2.1 %copy-start = (bf16[1,512,1536]{1,2,0:T(8,128)(2,1)S(1)}, bf16[1,512,1536]{1,2,0:T(8,128)(2,1)}, u32[]{:S(2)}) copy-start(bf16[1,512,1536]{1,2,0:T(8,128)(2,1)} %copy.30) | copy-start | bytes 4718596
  144.3 7.3 %copy-start.1 = (f32[12,128,512]{2,1,0:T(8,128)S(1)}, f32[12,128,512]{2,1,0:T(8,128)}, u32[]{:S(2)}) copy-start(f32[12,128,512]{2,1,0:T(8,128)} %fusion.19) | copy-start | bytes 9437188
  144.3 7.3 %copy-start.2 = (f32[12,128,512]{2,1,0:T(8,128)S(1)}, f32[12,128,512]{2,1,0:T(8,128)}, u32[]{:S(2)}) copy-start(f32[12,128,512]{2,1,0:T(8,128)} %fusion.18) | copy-start | bytes 9437188
  165.0 38.7 %collective-permute-start.1 = (bf16[512,1536]{0,1:T(8,128)(2,1)}, bf16[512,1536]{0,1:T(8,128)(2,1)}, u32[]{:S(2)}, u32[]{:S(2)}) collective-permute-start(bf16[512,1536]{0,1:T(8,128)(2,1)} %fusion.29), channel_id=1, source_target_pairs={{0,28},{4,0},{8,4},{12,8},{16,12},{20,16},{24,20},{28,24},{1,29},{... | collective-permute-start | bytes 4718600 | tf_op jit(solution)/shard_map/ppermute | solution.py:17
where the time goes:
time: 206 us
  waiting for transfers between devices  78 us (38%)
  matrix products  71.8 us (35%)
  other arithmetic  20.8 us (10%)
  local copies, waits for them, and re-layouts  12.7 us (6%)
  blocking collectives  12.5 us (6%)
  starting transfers between devices  8.97 us (4%)
    ppermute x2, waiting for transfers between devices, passed_along(): return lax.ppermute(x, axis, [(i, (i + by) % size) for i in range(size)])  78 us
    dot_general x1, matrix products, backward_terms(): jnp.einsum('hqk,qhd->khd', d_scores, query_heads, preferred_element_type=...  19.9 us
    dot_general x1, matrix products, backward_terms(): jnp.einsum('hqk,khd->qhd', d_scores, key_heads, preferred_element_type=jn...  19.7 us
    sub x1, matrix products, attention_weights(): shifted = scores - jnp.max(scores, axis=-1, keepdims=True)  11.1 us
    unnamed x18, local copies, waits for them, and re-layouts  10.6 us
    ppermute x2, starting transfers between devices, passed_along(): return lax.ppermute(x, axis, [(i, (i + by) % size) for i in range(size)])  8.97 us
    sub x1, other arithmetic, attention_weights(): shifted = scores - jnp.max(scores, axis=-1, keepdims=True)  8.21 us
    dot_general x1, matrix products, backward_terms(): jnp.einsum('hqk,qhd->khd', rounded, grad_heads, preferred_element_type=jn...  7.3 us
  transfers between devices with their start and end apart: 2, of which 2 were waited for; matrix products, arithmetic and copies ran while one was open for 11% of the time, Pallas kernels for 0%

commit v1 on v0

v1 whole, which is shorter than its diff:
```python
import functools
import math

import jax
import jax.numpy as jnp
from jax import lax
from jax.experimental import pallas as pl
from jax.experimental.pallas import tpu as pltpu
from jax.sharding import PartitionSpec as P

HDIM = 128
EPSILON = 1e-05
SCALE = 1.0 / math.sqrt(HDIM)
LOG2E = math.log2(math.e)
VMEM = 48 * 1024 * 1024

F32 = jnp.float32
BF16 = jnp.bfloat16


def dot(a, b, contract):
    return lax.dot_general(a, b, ((contract[0], contract[1]), ((), ())), preferred_element_type=F32)


def nt(a, b):
    return dot(a, b, ((1,), (1,)))


def nn(a, b):
    return dot(a, b, ((1,), (0,)))


def block_of(tokens):
    return 256 if tokens % 256 == 0 else tokens


def masked(block, kept):
    return jnp.where(kept, block, -1e30)


def kept_keys(size):
    keys = lax.broadcasted_iota(jnp.int32, (size, size), 0)
    return keys <= lax.broadcasted_iota(jnp.int32, (size, size), 1)


def scores_of(keys, queries, j, size, kept):
    mine = queries[j * size : (j + 1) * size]
    diagonal = masked(nt(keys[j * size : (j + 1) * size], mine), kept)
    if j == 0:
        return [diagonal]
    return [nt(keys[: j * size], mine), diagonal]


def exponents(parts):
    top = functools.reduce(jnp.maximum, [jnp.max(p, axis=0, keepdims=True) for p in parts])
    exps = [jnp.exp2((p - top) * (SCALE * LOG2E)) for p in parts]
    total = sum(jnp.sum(e, axis=0, keepdims=True) for e in exps)
    return exps, total


def stacked(parts):
    return parts[0] if len(parts) == 1 else jnp.concatenate(parts, axis=0)


def normed_head(x, factor, gain_q, gain_k):
    wide = x.astype(F32)
    normed = wide * factor
    return wide, (normed * gain_q).astype(BF16), (normed * gain_k).astype(BF16), normed.astype(BF16)


def column_of(row):
    return jnp.broadcast_to(row, (HDIM, row.shape[1])).T[:, 0:1]


def forward_kernel(heads, x_ref, f_ref, gq_ref, gk_ref, o_ref):
    tokens = x_ref.shape[0]
    size = block_of(tokens)
    kept = kept_keys(size)
    factor = column_of(f_ref[...])
    for h in range(heads):
        lanes = slice(h * HDIM, (h + 1) * HDIM)
        wide, q, k, v = normed_head(x_ref[:, lanes], factor, gq_ref[:, lanes], gk_ref[:, lanes])
        vt = v.T
        for j in range(tokens // size):
            exps, total = exponents(scores_of(k, q, j, size, kept))
            mixed = nn(vt[:, : (j + 1) * size], stacked(exps).astype(BF16)) * (1.0 / total)
            rows = slice(j * size, (j + 1) * size)
            o_ref[rows, lanes] = (wide[rows] + mixed.T).astype(BF16)


def forward(x, factor, gain_q, gain_k, heads):
    tokens, width = x.shape
    lanes = heads * HDIM
    block = pl.BlockSpec((tokens, lanes), lambda i: (0, i))
    gain = pl.BlockSpec((1, lanes), lambda i: (0, i))
    n = width // HDIM
    return pl.pallas_call(
        functools.partial(forward_kernel, heads),
        out_shape=jax.ShapeDtypeStruct(x.shape, BF16),
        grid=(width // lanes,),
        in_specs=[block, pl.BlockSpec((1, tokens), lambda i: (0, 0)), gain, gain],
        out_specs=block,
        compiler_params=pltpu.CompilerParams(vmem_limit_bytes=VMEM),
        cost_estimate=pl.CostEstimate(
            flops=4 * n * tokens * tokens * HDIM, bytes_accessed=4 * tokens * width,
            transcendentals=n * tokens * tokens,
        ),
        name="forward",
    )(x, factor, gain_q, gain_k)


def backward_head(x, g, factor, gain_q, gain_k):
    tokens = x.shape[0]
    size = block_of(tokens)
    kept = kept_keys(size)
    wide, q, k, v = normed_head(x, factor, gain_q, gain_k)
    kt = k.T
    blocks = tokens // size
    d_q = []
    d_k = [None] * blocks
    d_v = [None] * blocks
    for j in range(blocks):
        rows = slice(j * size, (j + 1) * size)
        exps, total = exponents(scores_of(k, q, j, size, kept))
        inverse = 1.0 / total
        weights = [e * inverse for e in exps]
        grads = [nt(v[: j * size], g[rows])] if j else []
        grads.append(nt(v[rows], g[rows]))
        delta = sum(jnp.sum(w * d, axis=0, keepdims=True) for w, d in zip(weights, grads))
        scores = stacked([(w * ((d - delta) * SCALE)).astype(BF16) for w, d in zip(weights, grads)])
        rounded = stacked([w.astype(BF16) for w in weights])
        d_q.append(nn(kt[:, : (j + 1) * size], scores).T)
        part_k = nn(scores, q[rows])
        part_v = nn(rounded, g[rows])
        for i in range(j + 1):
            mine = slice(i * size, (i + 1) * size)
            d_k[i] = part_k[mine] if d_k[i] is None else d_k[i] + part_k[mine]
            d_v[i] = part_v[mine] if d_v[i] is None else d_v[i] + part_v[mine]
    d_normed = stacked(d_q) * gain_q + stacked(d_k) * gain_k + stacked(d_v)
    return wide, d_normed


def backward_kernel(heads, x_ref, g_ref, f_ref, gq_ref, gk_ref, a_ref, inner_ref):
    factor = column_of(f_ref[...])
    part = None
    for h in range(heads):
        lanes = slice(h * HDIM, (h + 1) * HDIM)
        g = g_ref[:, lanes]
        wide, d_normed = backward_head(x_ref[:, lanes], g, factor, gq_ref[:, lanes], gk_ref[:, lanes])
        a_ref[:, lanes] = g.astype(F32) + factor * d_normed
        product = d_normed * wide
        part = product if part is None else part + product
    inner = jnp.sum(part.T, axis=0, keepdims=True)

    @pl.when(pl.program_id(0) == 0)
    def _():
        inner_ref[...] = inner

    @pl.when(pl.program_id(0) > 0)
    def _():
        inner_ref[...] += inner


def backward(x, g, factor, gain_q, gain_k, heads):
    tokens, width = x.shape
    lanes = heads * HDIM
    block = pl.BlockSpec((tokens, lanes), lambda i: (0, i))
    gain = pl.BlockSpec((1, lanes), lambda i: (0, i))
    row = pl.BlockSpec((1, tokens), lambda i: (0, 0))
    n = width // HDIM
    return pl.pallas_call(
        functools.partial(backward_kernel, heads),
        out_shape=(jax.ShapeDtypeStruct(x.shape, F32), jax.ShapeDtypeStruct((1, tokens), F32)),
        grid=(width // lanes,),
        in_specs=[block, block, row, gain, gain],
        out_specs=(block, row),
        compiler_params=pltpu.CompilerParams(vmem_limit_bytes=VMEM),
        cost_estimate=pl.CostEstimate(
            flops=10 * n * tokens * tokens * HDIM, bytes_accessed=8 * tokens * width,
            transcendentals=n * tokens * tokens,
        ),
        name="backward",
    )(x, g, factor, gain_q, gain_k)


def passed_along(x, axis, by):
    size = lax.axis_size(axis)
    return lax.ppermute(x, axis, [(i, (i + by) % size) for i in range(size)])


def squares(x):
    wide = x.astype(F32)
    return jnp.sum(wide * wide, axis=-1)[None]


def local(width_all, layer_input, grad_input, stashed, eviction, query_gain, key_gain):
    half_sections = lax.axis_size("section") // 2
    current = layer_input[0]
    upstream = grad_input[0]
    heads_here = current.shape[1] // HDIM
    chunks = next(c for c in (4, 3, 2, 1) if heads_here % c == 0)
    heads = heads_here // chunks
    step = heads * HDIM
    evicted = eviction[0] == 1
    parts = [slice(c * step, (c + 1) * step) for c in range(chunks)]
    fetched = [passed_along(stashed[0, 1][:, p], "section", -half_sections) for p in parts]
    totals = lax.psum(
        jnp.concatenate([squares(current), squares(stashed[0, 0]), squares(stashed[0, 1])], axis=0), "tensor"
    )
    fetched_total = passed_along(totals[2:3], "section", -half_sections)
    chosen_total = jnp.where(evicted, fetched_total, totals[1:2])
    forward_factor = lax.rsqrt(totals[0:1] / width_all + EPSILON)
    factor = lax.rsqrt(chosen_total / width_all + EPSILON)
    output = forward(current, forward_factor, query_gain, key_gain, heads)
    terms = []
    inner = 0.0
    for p, f in zip(parts, fetched):
        x = jnp.where(evicted, f, stashed[0, 0][:, p])
        a, part = backward(x, upstream[:, p], factor, query_gain[:, p], key_gain[:, p], heads)
        terms.append((x, a))
        inner = inner + part
    inner = lax.psum(inner, "tensor")
    row = (factor**3 * inner / width_all).T
    passed = [passed_along((a - x.astype(F32) * row).astype(BF16), "section", -1) for x, a in terms]
    return (output[None], jnp.concatenate(passed, axis=1)[None])


def solution(mesh):
    placed = (
        P("section", None, "tensor"),
        P("section", None, "tensor"),
        P("section", None, None, "tensor"),
        P("section"),
        P("section", "tensor"),
        P("section", "tensor"),
    )

    def whole(layer_input, *others):
        return jax.shard_map(
            functools.partial(local, layer_input.shape[-1]),
            mesh=mesh,
            in_specs=placed,
            out_specs=(P("section", None, "tensor"), P("section", None, "tensor")),
            check_vma=False,
        )(layer_input, *others)

    return whole
```

time: 206 us -> 145 us (0.70)
  matrix products: 71.8 us -> 0 us
  Pallas kernels: 0 us -> 22.4 us
  other arithmetic: 20.8 us -> 6.27 us
  starting transfers between devices: 8.97 us -> 15.4 us
  local copies, waits for them, and re-layouts: 12.7 us -> 9.37 us
    dot_general x6 -> x0, matrix products: 60.8 us -> none  [the longest x1 19.9 us: backward_terms(): jnp.einsum('hqk,qhd->khd', d_scores, query_heads, preferred_element_type=...]
    pallas_call x0 -> x5, Pallas kernels: none -> 22.4 us  [the longest x4 14.3 us: backward(): pl.pallas_call(functools.partial(backward_kernel, heads), out_shape=(jax....]
    sub x1 -> x0, matrix products: 11.1 us -> none  [attention_weights(): shifted = scores - jnp.max(scores, axis=-1, keepdims=True)]
    sub x1 -> x0, other arithmetic: 8.21 us -> none  [attention_weights(): shifted = scores - jnp.max(scores, axis=-1, keepdims=True)]
    ppermute x2 -> x9, starting transfers between devices: 8.97 us -> 15.4 us  [passed_along(): return lax.ppermute(x, axis, [(i, (i + by) % size) for i in range(size)])]
    unnamed x18 -> x20, local copies, waits for them, and re-layouts: 10.6 us -> 4.79 us
    convert_element_type x3 -> x1, other arithmetic: 7.14 us -> 2.28 us  [local(): (a - x.astype(F32) * row).astype(BF16)]
    reduce_sum x3 -> x2, other arithmetic: 5.32 us -> 1.07 us  [squares(): return jnp.sum(wide * wide, axis=-1)[None]]
  transfers between devices with their start and end apart: 2 -> 9, of which waited for: 2 -> 5; matrix products, arithmetic and copies ran while one was open for 11% -> 1% of each run, Pallas kernels for 0% -> 6%
where the time goes in v1:
time: 145 us
  waiting for transfers between devices  78 us (54%)
  Pallas kernels  22.4 us (15%)
  starting transfers between devices  15.4 us (11%)
  blocking collectives  11.8 us (8%)
  local copies, waits for them, and re-layouts  9.37 us (6%)
  other arithmetic  6.27 us (4%)
    ppermute x9, waiting for transfers between devices, passed_along(): return lax.ppermute(x, axis, [(i, (i + by) % size) for i in range(size)])  78 us
    ppermute x9, starting transfers between devices, passed_along(): return lax.ppermute(x, axis, [(i, (i + by) % size) for i in range(size)])  15.4 us
    pallas_call x4, Pallas kernels, backward(): pl.pallas_call(functools.partial(backward_kernel, heads), out_shape=(jax....  14.3 us
    pallas_call x1, Pallas kernels, forward(): pl.pallas_call(functools.partial(forward_kernel, heads), out_shape=jax.Sh...  8.05 us
    psum x1, blocking collectives, local(): lax.psum(jnp.concatenate([squares(current), squares(stashed[0, 0]), squar...  5.98 us
    psum x1, blocking collectives, local(): inner = lax.psum(inner, 'tensor')  5.79 us
    unnamed x20, local copies, waits for them, and re-layouts  4.79 us
    squeeze x1, local copies, waits for them, and re-layouts, local(): stashed[0, 0]  3.23 us
  transfers between devices with their start and end apart: 9, of which 5 were waited for; matrix products, arithmetic and copies ran while one was open for 1% of the time, Pallas kernels for 6%

profile of v1, /device:TPU:0, one launch (start us, length us, event | category | flops | bytes accessed | tf_op | source)
XLA Modules:
  0.0 144.6 jit_solution(3261743789443870701)
XLA Ops:
  0.6 3.2 %slice_bitcast_fusion.1 = (bf16[512,1536]{1,0:T(8,128)(2,1)}, bf16[512,1536]{1,0:T(8,128)(2,1)S(1)}) fusion(bf16[1,2,512,1536]{3,2,1,0:T(8,128)(2,1)} %param.8), kind=kLoop, calls=%fused_computation.5 | loop fusion | bytes 6291456 | tf_op jit(solution)/shard_map/squeeze | solution.py:208
  3.9 0.0 copy-start.7
  3.9 1.2 fusion.8
  5.0 4.0 %collective-permute-start = (bf16[512,384]{1,0:T(8,128)(2,1)}, bf16[512,384]{1,0:T(8,128)(2,1)}, u32[]{:S(2)}, u32[]{:S(2)}) collective-permute-start(bf16[512,384]{1,0:T(8,128)(2,1)} %get-tuple-element.32), channel_id=1, source_target_pairs={{0,16},{4,20},{8,24},{12,28},{16,0},{20,4},{24,8},{28,12},{1,17},{... | collective-permute-start | bytes 1179656 | tf_op jit(solution)/shard_map/ppermute | solution.py:188
  9.1 0.0 collective-permute-start.2
  9.1 2.9 %collective-permute-start.3 = (bf16[512,384]{1,0:T(8,128)(2,1)}, bf16[512,384]{1,0:T(8,128)(2,1)}, u32[]{:S(2)}, u32[]{:S(2)}) collective-permute-start(bf16[512,384]{1,0:T(8,128)(2,1)} %get-tuple-element.31), channel_id=1, source_target_pairs={{0,16},{4,20},{8,24},{12,28},{16,0},{20,4},{24,8},{28,12},{1,17},{... | collective-permute-start | bytes 1179656 | tf_op jit(solution)/shard_map/ppermute | solution.py:188
  12.0 0.0 copy-start
  12.0 0.0 collective-permute-start.4
  12.1 0.0 copy-done.7
  12.1 0.7 multiply_reduce_fusion.1
  12.7 0.7 copy-done
  13.4 0.0 copy-start.9
  13.4 0.4 multiply_reduce_fusion.2
  13.8 6.0 %psum.14 = f32[3,512]{1,0:T(4,128)S(1)} all-reduce(f32[3,512]{1,0:T(4,128)S(1)} %pad_maximum_fusion), channel_id=1, replica_groups=mesh['section'=8,'tensor'=4] {'tensor'}, use_global_device_ids=true, to_apply=%region_3.0 | all-reduce | flops 1536 | bytes 12288 | tf_op jit(solution)/shard_map/psum | solution.py:207
  19.8 2.6 %collective-permute-start.1 = (f32[1,512]{1,0:T(1,128)S(1)}, f32[1,512]{1,0:T(1,128)S(1)}, u32[]{:S(2)}, u32[]{:S(2)}) collective-permute-start(f32[1,512]{1,0:T(1,128)S(1)} %slice.112), channel_id=1, source_target_pairs={{0,16},{4,20},{8,24},{12,28},{16,0},{20,4},{24,8},{28,12},{1,17},{... | collective-permute-start | bytes 6152 | tf_op jit(solution)/shard_map/ppermute | solution.py:188
  22.4 0.0 copy-done.9
  22.4 0.0 copy-start.5
  22.4 0.0 copy-start.6
  22.4 0.0 copy-start.8
  22.4 0.2 fusion.7
  22.6 0.5 copy-done.5
  23.1 0.0 copy-done.6
  23.8 53.8 %collective-permute-done.1 = f32[1,512]{1,0:T(1,128)S(1)} collective-permute-done((f32[1,512]{1,0:T(1,128)S(1)}, f32[1,512]{1,0:T(1,128)S(1)}, u32[]{:S(2)}, u32[]{:S(2)}) %collective-permute-start.1) | collective-permute-done | bytes 2080 | tf_op jit(solution)/shard_map/ppermute | solution.py:188
  77.6 0.0 collective-permute-done
  77.6 0.0 collective-permute-done.2
  77.6 0.0 collective-permute-done.3
  77.6 0.0 collective-permute-done.4
  77.6 0.0 copy-done.8
  77.6 1.6 %slice_select_fusion.2 = (bf16[512,384]{1,0:T(8,128)(2,1)S(1)}, bf16[512,384]{1,0:T(8,128)(2,1)S(1)}, bf16[512,384]{1,0:T(8,128)(2,1)S(1)}, bf16[512,384]{1,0:T(8,128)(2,1)S(1)}) fusion(bf16[512,384]{1,0:T(8,128)(2,1)} %collective-permute-done.2, bf16[512,1536]{1,0:T(8,128)(2,1)S(1)} %copy-done.8, pred[]{:T(512)} %bitcast.7, ...), kind=kLoop, calls=%fused_computation.12 | loop fusion | flops 786432 | bytes 4718593 | tf_op jit(solution)/shard_map/jit(_where)/select_n | solution.py:218
  79.2 3.5 %backward.5 = (f32[512,384]{1,0:T(8,128)S(1)}, f32[1,512]{1,0:T(1,128)S(1)}) custom-call(bf16[512,384]{1,0:T(8,128)(2,1)S(1)} %get-tuple-element.26.x_ref, bf16[512,384]{1,0:T(8,128)(2,1)S(1)} %get-tuple-element.22.g_ref, f32[1,512]{1,0:T(1,128)S(1)} %get-tuple-element.34.f_ref, f32[1,384]{1,0:T(1,128)S(1)} %get-tuple-element.51.gq_ref, ...), custom_call_target="tpu_custom_call" | custom-call | flops 1006632960 | bytes 1572864 | tf_op jit(solution)/shard_map/backward/pallas_call | solution.py:171
  82.8 0.0 copy-start.1
  82.8 0.9 copy-done.1
  83.7 3.5 %backward.6 = (f32[512,384]{1,0:T(8,128)S(1)}, f32[1,512]{1,0:T(1,128)S(1)}) custom-call(bf16[512,384]{1,0:T(8,128)(2,1)S(1)} %get-tuple-element.27.x_ref, bf16[512,384]{1,0:T(8,128)(2,1)S(1)} %get-tuple-element.24.g_ref, f32[1,512]{1,0:T(1,128)S(1)} %get-tuple-element.34.f_ref, f32[1,384]{1,0:T(1,128)S(1)} %get-tuple-element.48.gq_ref, ...), custom_call_target="tpu_custom_call" | custom-call | flops 1006632960 | bytes 1572864 | tf_op jit(solution)/shard_map/backward/pallas_call | solution.py:171
  87.2 0.0 copy-start.2
  87.2 0.9 copy-done.2
  88.1 3.5 %backward.7 = (f32[512,384]{1,0:T(8,128)S(1)}, f32[1,512]{1,0:T(1,128)S(1)}) custom-call(bf16[512,384]{1,0:T(8,128)(2,1)S(1)} %get-tuple-element.29.x_ref, bf16[512,384]{1,0:T(8,128)(2,1)S(1)} %get-tuple-element.23.g_ref, f32[1,512]{1,0:T(1,128)S(1)} %get-tuple-element.34.f_ref, f32[1,384]{1,0:T(1,128)S(1)} %get-tuple-element.49.gq_ref, ...), custom_call_target="tpu_custom_call" | custom-call | flops 1006632960 | bytes 1572864 | tf_op jit(solution)/shard_map/backward/pallas_call | solution.py:171
  91.7 0.0 copy-start.3
  91.7 0.9 copy-done.3
  92.6 3.7 %backward.4 = (f32[512,384]{1,0:T(8,128)S(1)}, f32[1,512]{1,0:T(1,128)S(1)}) custom-call(bf16[512,384]{1,0:T(8,128)(2,1)S(1)} %get-tuple-element.28.x_ref, bf16[512,384]{1,0:T(8,128)(2,1)S(1)} %get-tuple-element.25.g_ref, f32[1,512]{1,0:T(1,128)S(1)} %get-tuple-element.34.f_ref, f32[1,384]{1,0:T(1,128)S(1)} %get-tuple-element.50.gq_ref, ...), custom_call_target="tpu_custom_call" | custom-call | flops 1006632960 | bytes 1572864 | tf_op jit(solution)/shard_map/backward/pallas_call | solution.py:171
  96.3 0.0 copy-start.4
  96.3 0.9 copy-done.4
  97.2 5.8 %psum.15 = f32[1,512]{1,0:T(1,128)S(1)} all-reduce(f32[1,512]{1,0:T(1,128)S(1)} %add_add_fusion), channel_id=1, replica_groups=mesh['section'=8,'tensor'=4] {'tensor'}, use_global_device_ids=true, to_apply=%region_4.5 | all-reduce | flops 512 | bytes 4096 | tf_op jit(solution)/shard_map/psum | solution.py:222
  103.0 2.3 %subtract_convert_fusion.3 = (bf16[512,384]{1,0:T(8,128)(2,1)S(1)}, bf16[512,384]{1,0:T(8,128)(2,1)S(1)}, bf16[512,384]{1,0:T(8,128)(2,1)S(1)}, bf16[512,384]{1,0:T(8,128)(2,1)S(1)}) fusion(f32[512,384]{1,0:T(8,128)} %copy-done.4, bf16[512,384]{1,0:T(8,128)(2,1)S(1)} %get-tuple-element.28.x_ref, f32[512]{0:T(512)S(1)} %bitcast.21, f32[512,384]{1,0:T(8,128)} %copy-done.1, ...), kind=kLoop, calls=%fused_computation.9 | loop fusion | flops 3145728 | bytes 6293504 | tf_op jit(solution)/shard_map/convert_element_type | solution.py:224
  105.3 5.6 %collective-permute-start.5 = (bf16[512,384]{1,0:T(8,128)(2,1)S(1)}, bf16[512,384]{1,0:T(8,128)(2,1)S(1)}, u32[]{:S(2)}, u32[]{:S(2)}) collective-permute-start(bf16[512,384]{1,0:T(8,128)(2,1)S(1)} %get-tuple-element.44), channel_id=1, source_target_pairs={{0,28},{4,0},{8,4},{12,8},{16,12},{20,16},{24,20},{28,24},{1,29},{... | collective-permute-start | bytes 1179656 | tf_op jit(solution)/shard_map/ppermute | solution.py:188
  110.9 0.1 collective-permute-start.6
  111.0 0.1 collective-permute-start.7
  111.0 0.1 collective-permute-start.8
  111.1 8.1 %forward.1 = bf16[512,1536]{1,0:T(8,128)(2,1)} custom-call(bf16[512,1536]{1,0:T(8,128)(2,1)S(1)} %bitcast.19, f32[1,512]{1,0:T(1,128)S(1)} %get-tuple-element.35.f_ref, f32[1,1536]{1,0:T(1,128)S(1)} %copy-done.5, f32[1,1536]{1,0:T(1,128)S(1)} %copy-done.6), custom_call_target="tpu_custom_call" | custom-call | flops 1610612736 | bytes 3145728 | tf_op jit(solution)/shard_map/forward/pallas_call | solution.py:97
  119.1 1.3 collective-permute-done.5
  120.5 8.4 %collective-permute-done.6 = bf16[512,384]{1,0:T(8,128)(2,1)S(1)} collective-permute-done((bf16[512,384]{1,0:T(8,128)(2,1)S(1)}, bf16[512,384]{1,0:T(8,128)(2,1)S(1)}, u32[]{:S(2)}, u32[]{:S(2)}) %collective-permute-start.6) | collective-permute-done | bytes 393248 | tf_op jit(solution)/shard_map/ppermute | solution.py:188
  128.9 8.4 %collective-permute-done.7 = bf16[512,384]{1,0:T(8,128)(2,1)S(1)} collective-permute-done((bf16[512,384]{1,0:T(8,128)(2,1)S(1)}, bf16[512,384]{1,0:T(8,128)(2,1)S(1)}, u32[]{:S(2)}, u32[]{:S(2)}) %collective-permute-start.7) | collective-permute-done | bytes 393248 | tf_op jit(solution)/shard_map/ppermute | solution.py:188
  137.3 6.1 %collective-permute-done.8 = bf16[512,384]{1,0:T(8,128)(2,1)S(1)} collective-permute-done((bf16[512,384]{1,0:T(8,128)(2,1)S(1)}, bf16[512,384]{1,0:T(8,128)(2,1)S(1)}, u32[]{:S(2)}, u32[]{:S(2)}) %collective-permute-start.8) | collective-permute-done | bytes 393248 | tf_op jit(solution)/shard_map/ppermute | solution.py:188
  143.4 1.3 maximum_bitcast_fusion
  (6 shorter events, 0.1 us)
Async XLA Ops:
  3.9 8.2 %copy-start.7 = (bf16[1,2,512,1536]{3,2,1,0:T(8,128)(2,1)S(1)}, bf16[1,2,512,1536]{3,2,1,0:T(8,128)(2,1)}, u32[]{:S(2)}) copy-start(bf16[1,2,512,1536]{3,2,1,0:T(8,128)(2,1)} %param.8) | copy-start | bytes 9437188
  5.0 72.5 %collective-permute-start = (bf16[512,384]{1,0:T(8,128)(2,1)}, bf16[512,384]{1,0:T(8,128)(2,1)}, u32[]{:S(2)}, u32[]{:S(2)}) collective-permute-start(bf16[512,384]{1,0:T(8,128)(2,1)} %get-tuple-element.32), channel_id=1, source_target_pairs={{0,16},{4,20},{8,24},{12,28},{16,0},{20,4},{24,8},{28,12},{1,17},{... | collective-permute-start | bytes 1179656 | tf_op jit(solution)/shard_map/ppermute | solution.py:188
  9.1 68.5 %collective-permute-start.2 = (bf16[512,384]{1,0:T(8,128)(2,1)}, bf16[512,384]{1,0:T(8,128)(2,1)}, u32[]{:S(2)}, u32[]{:S(2)}) collective-permute-start(bf16[512,384]{1,0:T(8,128)(2,1)} %get-tuple-element.30), channel_id=1, source_target_pairs={{0,16},{4,20},{8,24},{12,28},{16,0},{20,4},{24,8},{28,12},{1,17},{... | collective-permute-start | bytes 1179656 | tf_op jit(solution)/shard_map/ppermute | solution.py:188
  9.1 68.5 %collective-permute-start.3 = (bf16[512,384]{1,0:T(8,128)(2,1)}, bf16[512,384]{1,0:T(8,128)(2,1)}, u32[]{:S(2)}, u32[]{:S(2)}) collective-permute-start(bf16[512,384]{1,0:T(8,128)(2,1)} %get-tuple-element.31), channel_id=1, source_target_pairs={{0,16},{4,20},{8,24},{12,28},{16,0},{20,4},{24,8},{28,12},{1,17},{... | collective-permute-start | bytes 1179656 | tf_op jit(solution)/shard_map/ppermute | solution.py:188
  12.0 1.4 copy-start
  12.0 65.6 %collective-permute-start.4 = (bf16[512,384]{1,0:T(8,128)(2,1)}, bf16[512,384]{1,0:T(8,128)(2,1)}, u32[]{:S(2)}, u32[]{:S(2)}) collective-permute-start(bf16[512,384]{1,0:T(8,128)(2,1)} %get-tuple-element.33), channel_id=1, source_target_pairs={{0,16},{4,20},{8,24},{12,28},{16,0},{20,4},{24,8},{28,12},{1,17},{... | collective-permute-start | bytes 1179656 | tf_op jit(solution)/shard_map/ppermute | solution.py:188
  13.4 9.0 %copy-start.9 = (bf16[1,512,1536]{2,1,0:T(8,128)(2,1)S(1)}, bf16[1,512,1536]{2,1,0:T(8,128)(2,1)}, u32[]{:S(2)}) copy-start(bf16[1,512,1536]{2,1,0:T(8,128)(2,1)} %param.7) | copy-start | bytes 4718596
  19.8 57.7 %collective-permute-start.1 = (f32[1,512]{1,0:T(1,128)S(1)}, f32[1,512]{1,0:T(1,128)S(1)}, u32[]{:S(2)}, u32[]{:S(2)}) collective-permute-start(f32[1,512]{1,0:T(1,128)S(1)} %slice.112), channel_id=1, source_target_pairs={{0,16},{4,20},{8,24},{12,28},{16,0},{20,4},{24,8},{28,12},{1,17},{... | collective-permute-start | bytes 6152 | tf_op jit(solution)/shard_map/ppermute | solution.py:188
  22.4 0.7 copy-start.5
  22.4 0.7 copy-start.6
  22.4 55.2 %copy-start.8 = (bf16[512,1536]{1,0:T(8,128)(2,1)S(1)}, bf16[512,1536]{1,0:T(8,128)(2,1)}, u32[]{:S(2)}) copy-start(bf16[512,1536]{1,0:T(8,128)(2,1)} %get-tuple-element.20) | copy-start | bytes 4718596
  82.8 0.9 copy-start.1
  87.2 0.9 copy-start.2
  91.7 0.9 copy-start.3
  96.3 0.9 copy-start.4
  105.3 15.2 %collective-permute-start.5 = (bf16[512,384]{1,0:T(8,128)(2,1)S(1)}, bf16[512,384]{1,0:T(8,128)(2,1)S(1)}, u32[]{:S(2)}, u32[]{:S(2)}) collective-permute-start(bf16[512,384]{1,0:T(8,128)(2,1)S(1)} %get-tuple-element.44), channel_id=1, source_target_pairs={{0,28},{4,0},{8,4},{12,8},{16,12},{20,16},{24,20},{28,24},{1,29},{... | collective-permute-start | bytes 1179656 | tf_op jit(solution)/shard_map/ppermute | solution.py:188
  110.9 18.0 %collective-permute-start.6 = (bf16[512,384]{1,0:T(8,128)(2,1)S(1)}, bf16[512,384]{1,0:T(8,128)(2,1)S(1)}, u32[]{:S(2)}, u32[]{:S(2)}) collective-permute-start(bf16[512,384]{1,0:T(8,128)(2,1)S(1)} %get-tuple-element.45), channel_id=1, source_target_pairs={{0,28},{4,0},{8,4},{12,8},{16,12},{20,16},{24,20},{28,24},{1,29},{... | collective-permute-start | bytes 1179656 | tf_op jit(solution)/shard_map/ppermute | solution.py:188
  111.0 26.4 %collective-permute-start.7 = (bf16[512,384]{1,0:T(8,128)(2,1)S(1)}, bf16[512,384]{1,0:T(8,128)(2,1)S(1)}, u32[]{:S(2)}, u32[]{:S(2)}) collective-permute-start(bf16[512,384]{1,0:T(8,128)(2,1)S(1)} %get-tuple-element.46), channel_id=1, source_target_pairs={{0,28},{4,0},{8,4},{12,8},{16,12},{20,16},{24,20},{28,24},{1,29},{... | collective-permute-start | bytes 1179656 | tf_op jit(solution)/shard_map/ppermute | solution.py:188
  111.0 32.3 %collective-permute-start.8 = (bf16[512,384]{1,0:T(8,128)(2,1)S(1)}, bf16[512,384]{1,0:T(8,128)(2,1)S(1)}, u32[]{:S(2)}, u32[]{:S(2)}) collective-permute-start(bf16[512,384]{1,0:T(8,128)(2,1)S(1)} %get-tuple-element.47), channel_id=1, source_target_pairs={{0,28},{4,0},{8,4},{12,8},{16,12},{20,16},{24,20},{28,24},{1,29},{... | collective-permute-start | bytes 1179656 | tf_op jit(solution)/shard_map/ppermute | solution.py:188

commit v2 on v1

--- a/solution.py
+++ b/solution.py
@@ -140,52 +140,135 @@
     return wide, d_normed
 
 
-def backward_kernel(heads, x_ref, g_ref, f_ref, gq_ref, gk_ref, a_ref, inner_ref):
-    factor = column_of(f_ref[...])
-    part = None
-    for h in range(heads):
-        lanes = slice(h * HDIM, (h + 1) * HDIM)
-        g = g_ref[:, lanes]
-        wide, d_normed = backward_head(x_ref[:, lanes], g, factor, gq_ref[:, lanes], gk_ref[:, lanes])
-        a_ref[:, lanes] = g.astype(F32) + factor * d_normed
-        product = d_normed * wide
-        part = product if part is None else part + product
-    inner = jnp.sum(part.T, axis=0, keepdims=True)
-
-    @pl.when(pl.program_id(0) == 0)
+def backward_kernel(heads, pick_ref, x_ref, g1_ref, g2_ref, f_ref, gq_ref, gk_ref, *rest):
+    a_ref, inner_ref = rest[-2:]
+    first = pl.program_id(0) == 0
+
+    @pl.when(jnp.logical_and(first, pick_ref[0] == 0))
     def _():
-        inner_ref[...] = inner
-
-    @pl.when(pl.program_id(0) > 0)
+        inner_ref[...] = jnp.zeros_like(inner_ref)
+
+    @pl.when(pick_ref[0] == 1)
     def _():
-        inner_ref[...] += inner
-
-
-def backward(x, g, factor, gain_q, gain_k, heads):
-    tokens, width = x.shape
+        factor = column_of(f_ref[...])
+        other = pick_ref[1] == 1
+        part = None
+        for h in range(heads):
+            lanes = slice(h * HDIM, (h + 1) * HDIM)
+            g = jnp.where(other, g2_ref[:, lanes], g1_ref[:, lanes])
+            wide, d_normed = backward_head(x_ref[:, lanes], g, factor, gq_ref[:, lanes], gk_ref[:, lanes])
+            a_ref[:, lanes] = g.astype(F32) + factor * d_normed
+            product = d_normed * wide
+            part = product if part is None else part + product
+        inner = jnp.sum(part.T, axis=0, keepdims=True)
+
+        @pl.when(first)
+        def _():
+            inner_ref[...] = inner
+
+        @pl.when(jnp.logical_not(first))
+        def _():
+            inner_ref[...] += inner
+
+
+def backward(pick, x, g1, g2, factor, gain_q, gain_k, heads, steps, starts, sofar=None, after=()):
+    tokens = x.shape[0]
+    width = gain_q.shape[1]
     lanes = heads * HDIM
-    block = pl.BlockSpec((tokens, lanes), lambda i: (0, i))
-    gain = pl.BlockSpec((1, lanes), lambda i: (0, i))
-    row = pl.BlockSpec((1, tokens), lambda i: (0, 0))
-    n = width // HDIM
+    x0, g10, g20, c0 = starts
+    at = lambda first: pl.BlockSpec((tokens, lanes), lambda i, pick: (0, first + i))
+    gain = pl.BlockSpec((1, lanes), lambda i, pick: (0, c0 + i))
+    row = pl.BlockSpec((1, tokens), lambda i, pick: (0, 0))
+    n = heads * steps
+    extra = (() if sofar is None else (sofar,)) + tuple(after)
     return pl.pallas_call(
         functools.partial(backward_kernel, heads),
-        out_shape=(jax.ShapeDtypeStruct(x.shape, F32), jax.ShapeDtypeStruct((1, tokens), F32)),
-        grid=(width // lanes,),
-        in_specs=[block, block, row, gain, gain],
-        out_specs=(block, row),
+        out_shape=(jax.ShapeDtypeStruct((tokens, width), F32), jax.ShapeDtypeStruct((1, tokens), F32)),
+        grid_spec=pltpu.PrefetchScalarGridSpec(
+            num_scalar_prefetch=1,
+            grid=(steps,),
+            in_specs=[at(x0), at(g10), at(g20), row, gain, gain] + [pl.BlockSpec(memory_space=pl.ANY)] * len(extra),
+            out_specs=(at(c0), row),
+        ),
+        input_output_aliases={} if sofar is None else {7: 0},
         compiler_params=pltpu.CompilerParams(vmem_limit_bytes=VMEM),
         cost_estimate=pl.CostEstimate(
-            flops=10 * n * tokens * tokens * HDIM, bytes_accessed=8 * tokens * width,
+            flops=10 * n * tokens * tokens * HDIM, bytes_accessed=10 * tokens * n * HDIM,
             transcendentals=n * tokens * tokens,
         ),
         name="backward",
-    )(x, g, factor, gain_q, gain_k)
-
-
-def passed_along(x, axis, by):
-    size = lax.axis_size(axis)
-    return lax.ppermute(x, axis, [(i, (i + by) % size) for i in range(size)])
+    )(pick, x, g1, g2, factor, gain_q, gain_k, *extra)
+
+
+def choose_kernel(mode_ref, own_ref, near_ref, far_ref, held_ref, next_ref, *rest):
+    sent_ref = rest[-2]
+    for m, ref in enumerate((own_ref, near_ref, far_ref, held_ref)):
+
+        @pl.when(mode_ref[0] == m)
+        def _():
+            sent_ref[...] = ref[...]
+
+    rest[-1][...] = next_ref[...]
+
+
+def choose(mode, stash, near, far, c, step, coming, after=()):
+    tokens = near.shape[0]
+    block = (tokens, step)
+    whole = lambda at: pl.BlockSpec(block, lambda i, mode: (0, at))
+    of_stash = lambda which, at: pl.BlockSpec((None, None, tokens, step), lambda i, mode: (0, which, 0, at))
+    return pl.pallas_call(
+        choose_kernel,
+        out_shape=[jax.ShapeDtypeStruct(block, BF16)] * 2,
+        grid_spec=pltpu.PrefetchScalarGridSpec(
+            num_scalar_prefetch=1,
+            grid=(1,),
+            in_specs=[of_stash(0, c), whole(0), whole(c), of_stash(1, c), of_stash(1, coming)]
+            + [pl.BlockSpec(memory_space=pl.ANY)] * len(after),
+            out_specs=[whole(0)] * 2,
+        ),
+        compiler_params=pltpu.CompilerParams(vmem_limit_bytes=VMEM),
+        cost_estimate=pl.CostEstimate(flops=0, bytes_accessed=14 * tokens * step, transcendentals=0),
+        name="choose",
+    )(mode, stash, near, far, stash, stash, *after)
+
+
+def finish_kernel(chunks, pieces, pick_ref, a_ref, row_ref, *rest):
+    o_ref = rest[-1]
+    xs, slots = rest[:chunks], rest[chunks : chunks + pieces]
+    row = column_of(row_ref[...])
+    lanes = xs[0].shape[1]
+    each = chunks // pieces
+    for c in range(chunks):
+
+        @pl.when(jnp.logical_and(pl.program_id(0) == c, pick_ref[0] == 0))
+        def _():
+            o_ref[...] = (a_ref[...] - xs[c][...].astype(F32) * row).astype(BF16)
+
+        @pl.when(jnp.logical_and(pl.program_id(0) == c, pick_ref[0] == 1))
+        def _():
+            at = (c % each) * lanes
+            o_ref[...] = slots[c // each][:, at : at + lanes]
+
+
+def finish(pick, a, row, xs, slots):
+    tokens, width = a.shape
+    chunks = len(xs)
+    lanes = width // chunks
+    block = pl.BlockSpec((tokens, lanes), lambda i, pick: (0, i))
+    still = lambda x: pl.BlockSpec(x.shape, lambda i, pick: (0, 0))
+    return pl.pallas_call(
+        functools.partial(finish_kernel, chunks, len(slots)),
+        out_shape=jax.ShapeDtypeStruct(a.shape, BF16),
+        grid_spec=pltpu.PrefetchScalarGridSpec(
+            num_scalar_prefetch=1,
+            grid=(chunks,),
+            in_specs=[block, still(row)] + [still(x) for x in xs] + [still(x) for x in slots],
+            out_specs=block,
+        ),
+        compiler_params=pltpu.CompilerParams(vmem_limit_bytes=VMEM),
+        cost_estimate=pl.CostEstimate(flops=2 * a.size, bytes_accessed=10 * a.size, transcendentals=0),
+        name="finish",
+    )(pick, a, row, *xs, *slots)
 
 
 def squares(x):
@@ -193,36 +276,91 @@
     return jnp.sum(wide * wide, axis=-1)[None]
 
 
+def send(x, pairs):
+    return lax.ppermute(x, "section", pairs)
+
+
 def local(width_all, layer_input, grad_input, stashed, eviction, query_gain, key_gain):
-    half_sections = lax.axis_size("section") // 2
+    n = lax.axis_size("section")
+    half = n // 2
+    special = (0, half)
+    me = lax.axis_index("section")
+    is_special = jnp.logical_or(me == 0, me == half)
+    evicted = eviction[0] == 1
+    word = lambda *flags: jnp.stack([f.astype(jnp.int32) for f in flags])
+
+    prior = [(s, (s - 1) % n) for s in range(n)]
+    inside = [(s, s - 1) for s in range(n) if s not in special]
+    within = inside + [(0, half - 1), (half, n - 1)]
+    across = [(half, half - 1), (0, n - 1)]
+    partner = [(s, (s + half) % n) for s in range(n)]
+    near_pairs = [p for p in partner if p[0] % 2 == 1]
+    far_pairs = [p for p in partner if p[0] % 2 == 0 and p[0] not in special]
+
     current = layer_input[0]
     upstream = grad_input[0]
-    heads_here = current.shape[1] // HDIM
+    tokens, width = current.shape
+    heads_here = width // HDIM
     chunks = next(c for c in (4, 3, 2, 1) if heads_here % c == 0)
+    pieces = 2 if chunks % 2 == 0 else 1
     heads = heads_here // chunks
     step = heads * HDIM
-    evicted = eviction[0] == 1
-    parts = [slice(c * step, (c + 1) * step) for c in range(chunks)]
-    fetched = [passed_along(stashed[0, 1][:, p], "section", -half_sections) for p in parts]
+    held = stashed[0, 1]
+    part = lambda x, c: x[:, c * step : (c + 1) * step]
+
+    near = {c: send(part(held, c), near_pairs) for c in range(min(2, chunks))}
+    far = send(held, far_pairs)
+    arrived = send(upstream, inside)
+
     totals = lax.psum(
-        jnp.concatenate([squares(current), squares(stashed[0, 0]), squares(stashed[0, 1])], axis=0), "tensor"
+        jnp.concatenate([squares(current), squares(stashed[0, 0]), squares(held)], axis=0), "tensor"
     )
-    fetched_total = passed_along(totals[2:3], "section", -half_sections)
+    factor_of = lambda total: lax.rsqrt(total / width_all + EPSILON)
+
+    kept_here = jnp.logical_and(me == half, jnp.logical_not(evicted))
+    own_factor = factor_of(totals[1:2])
+    own_a, own_inner = backward(
+        word(kept_here, kept_here), stashed[0, 0], upstream, upstream, own_factor, query_gain, key_gain,
+        heads, chunks, (0, 0, 0, 0),
+    )
+    own_inner = lax.psum(own_inner, "tensor")
+    own_row = (own_factor**3 * own_inner / width_all).T
+    slot = jnp.where(kept_here, (own_a - stashed[0, 0].astype(F32) * own_row).astype(BF16), upstream)
+    wide = width // pieces
+    slots = [send(slot[:, p * wide : (p + 1) * wide], across) for p in range(pieces)]
+
+    fetched_total = send(totals[2:3], partner)
     chosen_total = jnp.where(evicted, fetched_total, totals[1:2])
-    forward_factor = lax.rsqrt(totals[0:1] / width_all + EPSILON)
-    factor = lax.rsqrt(chosen_total / width_all + EPSILON)
-    output = forward(current, forward_factor, query_gain, key_gain, heads)
-    terms = []
-    inner = 0.0
-    for p, f in zip(parts, fetched):
-        x = jnp.where(evicted, f, stashed[0, 0][:, p])
-        a, part = backward(x, upstream[:, p], factor, query_gain[:, p], key_gain[:, p], heads)
-        terms.append((x, a))
-        inner = inner + part
+    flag = jnp.broadcast_to(eviction[0].astype(F32), (1, HDIM))
+    told = send(jnp.concatenate([chosen_total, query_gain, key_gain, flag], axis=1), prior)
+    factor = factor_of(told[:, :tokens])
+    gain_q = told[:, tokens : tokens + width]
+    gain_k = told[:, tokens + width : tokens + 2 * width]
+    after_evicted = told[0, tokens + 2 * width] == 1.0
+
+    output = forward(current, factor_of(totals[0:1]), query_gain, key_gain, heads)
+
+    mode = jnp.where(is_special, 3, jnp.where(evicted, jnp.where(me % 2 == 1, 1, 2), 0)).astype(jnp.int32)[None]
+    crossed = jnp.logical_or(me == half - 1, me == n - 1)
+    take = word(jnp.bool_(True), crossed)
+    xs = []
+    a, inner = None, 0.0
+    for c in range(chunks):
+        coming = min(c + 2, chunks - 1)
+        sent, following = choose(mode, stashed, near[c], far, c, step, coming)
+        if c + 2 < chunks:
+            near[c + 2] = send(following, near_pairs)
+        xs.append(send(sent, within))
+    each = chunks // pieces
+    for c in range(chunks):
+        a, share = backward(
+            take, xs[c], arrived, slots[c // each], factor, gain_q, gain_k, heads, 1, (0, c, c % each, c), a
+        )
+        inner = inner + share
     inner = lax.psum(inner, "tensor")
-    row = (factor**3 * inner / width_all).T
-    passed = [passed_along((a - x.astype(F32) * row).astype(BF16), "section", -1) for x, a in terms]
-    return (output[None], jnp.concatenate(passed, axis=1)[None])
+    done = word(jnp.logical_and(me == half - 1, jnp.logical_not(after_evicted)))
+    result = finish(done, a, factor**3 * inner / width_all, xs, slots)
+    return (output[None], result[None])
 
 
 def solution(mesh):

time: 145 us -> 185 us (1.28)
  waiting for transfers between devices: 78 us -> 29.2 us
  starting transfers between devices: 15.4 us -> 62.5 us
  Pallas kernels: 22.4 us -> 45.4 us
  blocking collectives: 11.8 us -> 20.2 us
  local copies, waits for them, and re-layouts: 9.37 us -> 14.4 us
  other arithmetic: 6.27 us -> 10 us
    ppermute x9 -> x14, waiting for transfers between devices: 78 us -> 29.2 us  [send(): return lax.ppermute(x, 'section', pairs)]
    ppermute x9 -> x14, starting transfers between devices: 15.4 us -> 62.5 us  [send(): return lax.ppermute(x, 'section', pairs)]
    pallas_call x0 -> x5, Pallas kernels: none -> 13 us  [the longest x4 7.86 us: choose(): pl.pallas_call(choose_kernel, out_shape=[jax.ShapeDtypeStruct(block, BF16...]
    pallas_call x4 -> x5, Pallas kernels: 14.3 us -> 24.3 us  [backward(): pl.pallas_call(functools.partial(backward_kernel, heads), out_shape=(jax....]
    psum x0 -> x1, blocking collectives: none -> 6.03 us  [local(): own_inner = lax.psum(own_inner, 'tensor')]
    unnamed x20 -> x30, local copies, waits for them, and re-layouts: 4.79 us -> 8.91 us
    reduce_sum x2, other arithmetic: 1.07 us -> 4.51 us  [squares(): return jnp.sum(wide * wide, axis=-1)[None]]
    psum x1, blocking collectives: 5.98 us -> 8.49 us  [local(): lax.psum(jnp.concatenate([squares(current), squares(stashed[0, 0]), squar...]
  transfers between devices with their start and end apart: 9 -> 14, of which waited for: 5 -> 1; matrix products, arithmetic and copies ran while one was open for 1% -> 6% of each run, Pallas kernels for 6% -> 19%
where the time goes in v2:
time: 185 us; the launch traced here: 184 us
  starting transfers between devices  62.5 us (34%)
  Pallas kernels  45.4 us (25%)
  waiting for transfers between devices  29.2 us (16%)
  blocking collectives  20.2 us (11%)
  local copies, waits for them, and re-layouts  14.4 us (8%)
  other arithmetic  10 us (5%)
  between operations  2.2 us (1%)
    ppermute x14, starting transfers between devices, send(): return lax.ppermute(x, 'section', pairs)  62.5 us
    ppermute x14, waiting for transfers between devices, send(): return lax.ppermute(x, 'section', pairs)  29.2 us
    pallas_call x5, Pallas kernels, backward(): pl.pallas_call(functools.partial(backward_kernel, heads), out_shape=(jax....  24.3 us
    unnamed x30, local copies, waits for them, and re-layouts  8.91 us
    psum x1, blocking collectives, local(): lax.psum(jnp.concatenate([squares(current), squares(stashed[0, 0]), squar...  8.49 us
    pallas_call x1, Pallas kernels, forward(): pl.pallas_call(functools.partial(forward_kernel, heads), out_shape=jax.Sh...  8.05 us
    pallas_call x4, Pallas kernels, choose(): pl.pallas_call(choose_kernel, out_shape=[jax.ShapeDtypeStruct(block, BF16...  7.86 us
    psum x1, blocking collectives, local(): own_inner = lax.psum(own_inner, 'tensor')  6.03 us
  transfers between devices with their start and end apart: 14, of which 1 were waited for; matrix products, arithmetic and copies ran while one was open for 6% of the time, Pallas kernels for 19%

profile of v2, /device:TPU:0, one launch (start us, length us, event | category | flops | bytes accessed | tf_op | source)
XLA Modules:
  0.0 183.9 jit_solution(7516198315946273562)
XLA Ops:
  0.6 0.0 copy-start
  0.6 1.9 %multiply_reduce_fusion.1 = f32[512]{0:T(512)S(1)} fusion(bf16[1,512,1536]{2,1,0:T(8,128)(2,1)} %param.6), kind=kLoop, calls=%fused_computation.6 | loop fusion | flops 2358784 | bytes 1574912 | tf_op jit(solution)/shard_map/reduce_sum | solution.py:276
  2.6 2.6 %fusion = (f32[512]{0:T(512)S(1)}, f32[512]{0:T(512)S(1)}) fusion(bf16[1,2,512,1536]{3,2,1,0:T(8,128)(2,1)} %next_ref.7), kind=kLoop, calls=%fused_computation.2 | loop fusion | flops 4717568 | bytes 3149824 | tf_op jit(solution)/shard_map/reduce_sum | solution.py:276
  5.2 8.5 %psum.21 = f32[3,512]{1,0:T(4,128)S(1)} all-reduce(f32[3,512]{1,0:T(4,128)S(1)} %pad_maximum_fusion), channel_id=1, replica_groups=mesh['section'=8,'tensor'=4] {'tensor'}, use_global_device_ids=true, to_apply=%region_3.0 | all-reduce | flops 1536 | bytes 12288 | tf_op jit(solution)/shard_map/psum | solution.py:315
  13.7 2.7 %collective-permute-start = (f32[1,512]{1,0:T(1,128)S(1)}, f32[1,512]{1,0:T(1,128)S(1)}, u32[]{:S(2)}, u32[]{:S(2)}) collective-permute-start(f32[1,512]{1,0:T(1,128)S(1)} %slice.56), channel_id=1, source_target_pairs={{0,16},{4,20},{8,24},{12,28},{16,0},{20,4},{24,8},{28,12},{1,17},{... | collective-permute-start | bytes 6152 | tf_op jit(solution)/shard_map/ppermute | solution.py:280
  16.3 1.4 collective-permute-start.6
  17.8 0.0 copy-done
  17.8 1.9 %slice_bitcast_fusion.1 = (bf16[512,1536]{1,0:T(8,128)(2,1)}, bf16[512,1536]{1,0:T(8,128)(2,1)}) fusion(bf16[1,2,512,1536]{3,2,1,0:T(8,128)(2,1)S(1)} %copy-done), kind=kLoop, calls=%fused_computation.9 | loop fusion | bytes 6291456 | tf_op jit(solution)/shard_map/squeeze | solution.py:316
  19.6 1.9 %collective-permute-start.3 = (bf16[512,1536]{1,0:T(8,128)(2,1)}, bf16[512,1536]{1,0:T(8,128)(2,1)}, u32[]{:S(2)}, u32[]{:S(2)}) collective-permute-start(bf16[512,1536]{1,0:T(8,128)(2,1)} %get-tuple-element.37), channel_id=1, source_target_pairs={{8,24},{24,8},{9,25},{25,9},{10,26},{26,10},{11,27},{27,11}} | collective-permute-start | bytes 4718600 | tf_op jit(solution)/shard_map/ppermute | solution.py:280
  21.5 2.1 %fusion.13 = (bf16[512,384]{1,0:T(8,128)(2,1)}, bf16[512,384]{1,0:T(8,128)(2,1)}) fusion(bf16[512,1536]{1,0:T(8,128)(2,1)} %get-tuple-element.37), kind=kLoop, calls=%fused_computation.30 | loop fusion | bytes 1572864 | tf_op jit(solution)/shard_map/slice | solution.py:309
  23.6 1.4 collective-permute-start.8
  25.0 1.4 collective-permute-start.2
  27.1 0.1 add_convert_fusion.1.pick_ref
  27.1 0.6 add_convert_fusion.pick_ref
  27.7 0.0 collective-permute-done
  27.7 0.6 add_rsqrt_fusion
  28.3 1.4 copy-done.7
  29.7 1.4 copy-done.8
  31.1 3.2 %backward.5 = (f32[512,1536]{1,0:T(8,128)}, f32[1,512]{1,0:T(1,128)S(1)}) custom-call(s32[2]{0:T(128)S(1)} %add_convert_fusion.1.pick_ref, bf16[512,1536]{1,0:T(8,128)(2,1)S(1)} %copy-done.8, bf16[512,1536]{1,0:T(8,128)(2,1)S(1)} %bitcast.29, bf16[512,1536]{1,0:T(8,128)(2,1)S(1)} %bitcast.30, f32[1,512]{1,0:T(1,128)S(1)} %get-tuple-element.44.f_ref, ...), custom_call_target="tpu_custom_call" | custom-call | flops 4026531840 | bytes 7864320 | tf_op jit(solution)/shard_map/backward/pallas_call | solution.py:184
  34.3 6.0 %psum.22 = f32[1,512]{1,0:T(1,128)S(1)} all-reduce(f32[1,512]{1,0:T(1,128)S(1)} %get-tuple-element.21), channel_id=1, replica_groups=mesh['section'=8,'tensor'=4] {'tensor'}, use_global_device_ids=true, to_apply=%region_4.0 | all-reduce | flops 512 | bytes 4096 | tf_op jit(solution)/shard_map/psum | solution.py:326
  40.3 3.0 %fusion.3 = bf16[512,1536]{1,0:T(8,128)(2,1)S(1)} fusion(f32[512,1536]{1,0:T(8,128)} %get-tuple-element.20, f32[512]{0:T(512)S(1)} %bitcast.32, pred[]{:T(512)} %and.14, bf16[1,512,1536]{2,1,0:T(8,128)(2,1)} %param.7, bf16[1,2,512,1536]{3,2,1,0:T(8,128)(2,1)S(1)} %copy-done), kind=kLoop, calls=%fused_computation.7 | loop fusion | flops 3932160 | bytes 7866369 | tf_op jit(solution)/shard_map/jit(_where)/select_n | solution.py:328
  43.3 1.0 fusion.12
  44.3 10.2 %collective-permute-start.12 = (bf16[512,768]{1,0:T(8,128)(2,1)S(1)}, bf16[512,768]{1,0:T(8,128)(2,1)S(1)}, u32[]{:S(2)}, u32[]{:S(2)}) collective-permute-start(bf16[512,768]{1,0:T(8,128)(2,1)S(1)} %get-tuple-element.38), channel_id=1, source_target_pairs={{16,12},{0,28},{17,13},{1,29},{18,14},{2,30},{19,15},{3,31}} | collective-permute-start | bytes 2359304 | tf_op jit(solution)/shard_map/ppermute | solution.py:280
  54.6 0.0 collective-permute-done.2.near_ref
  54.6 0.0 collective-permute-done.3.far_ref
  54.6 1.9 %choose.4 = (bf16[512,384]{1,0:T(8,128)(2,1)}, bf16[512,384]{1,0:T(8,128)(2,1)S(1)}) custom-call(s32[1]{0:T(128)} %bitcast.12.mode_ref, bf16[1,2,512,1536]{3,2,1,0:T(8,128)(2,1)S(1)} %copy-done, bf16[512,384]{1,0:T(8,128)(2,1)} %collective-permute-done.2.near_ref, bf16[512,1536]{1,0:T(8,128)(2,1)} %collective-permute-done.3.far_ref, ...), custom_call_target="tpu_custom_call" | custom-call | bytes 2752512 | tf_op jit(solution)/shard_map/choose/pallas_call | solution.py:219
  56.5 0.8 collective-permute-start.4
  57.3 0.0 collective-permute-done.8.near_ref
  57.4 1.9 %choose.6 = (bf16[512,384]{1,0:T(8,128)(2,1)}, bf16[512,384]{1,0:T(8,128)(2,1)S(1)}) custom-call(s32[1]{0:T(128)} %bitcast.12.mode_ref, bf16[1,2,512,1536]{3,2,1,0:T(8,128)(2,1)S(1)} %copy-done, bf16[512,384]{1,0:T(8,128)(2,1)} %collective-permute-done.8.near_ref, bf16[512,1536]{1,0:T(8,128)(2,1)} %collective-permute-done.3.far_ref, ...), custom_call_target="tpu_custom_call" | custom-call | bytes 2752512 | tf_op jit(solution)/shard_map/choose/pallas_call | solution.py:219
  59.3 0.7 collective-permute-start.9
  60.0 15.1 %collective-permute-start.1 = (f32[1,3712]{1,0:T(1,128)S(1)}, f32[1,3712]{1,0:T(1,128)S(1)}, u32[]{:S(2)}, u32[]{:S(2)}) collective-permute-start(f32[1,3712]{1,0:T(1,128)S(1)} %reshape_maximum_fusion), channel_id=1, source_target_pairs={{0,28},{4,0},{8,4},{12,8},{16,12},{20,16},{24,20},{28,24},{1,29},{... | collective-permute-start | bytes 44552 | tf_op jit(solution)/shard_map/ppermute | solution.py:280
  75.1 8.1 %forward.1 = bf16[512,1536]{1,0:T(8,128)(2,1)} custom-call(bf16[512,1536]{1,0:T(8,128)(2,1)S(1)} %bitcast.27, f32[1,512]{1,0:T(1,128)S(1)} %copy-done.13, f32[1,1536]{1,0:T(1,128)S(1)} %copy-done.10, f32[1,1536]{1,0:T(1,128)S(1)} %copy-done.11), custom_call_target="tpu_custom_call" | custom-call | flops 1610612736 | bytes 3145728 | tf_op jit(solution)/shard_map/forward/pallas_call | solution.py:97
  83.2 0.0 collective-permute-done.1
  83.2 21.9 %collective-permute-start.7 = (bf16[512,768]{1,0:T(8,128)(2,1)}, bf16[512,768]{1,0:T(8,128)(2,1)}, u32[]{:S(2)}, u32[]{:S(2)}) collective-permute-start(bf16[512,768]{1,0:T(8,128)(2,1)} %get-tuple-element.39), channel_id=1, source_target_pairs={{16,12},{0,28},{17,13},{1,29},{18,14},{2,30},{19,15},{3,31}} | collective-permute-start | bytes 2359304 | tf_op jit(solution)/shard_map/ppermute | solution.py:280
  105.1 0.0 collective-permute-done.4.near_ref
  105.1 2.4 %collective-permute-start.11 = (bf16[512,384]{1,0:T(8,128)(2,1)}, bf16[512,384]{1,0:T(8,128)(2,1)S(1)}, u32[]{:S(2)}, u32[]{:S(2)}) collective-permute-start(bf16[512,384]{1,0:T(8,128)(2,1)} %get-tuple-element.24), channel_id=1, source_target_pairs={{4,0},{8,4},{12,8},{20,16},{24,20},{28,24},{0,12},{16,28},{5,1},{9... | collective-permute-start | bytes 1179656 | tf_op jit(solution)/shard_map/ppermute | solution.py:280
  107.5 0.0 collective-permute-done.9.near_ref
  107.5 0.1 collective-permute-start.13
  107.6 2.0 %choose.5 = (bf16[512,384]{1,0:T(8,128)(2,1)}, bf16[512,384]{1,0:T(8,128)(2,1)}) custom-call(s32[1]{0:T(128)} %bitcast.12.mode_ref, bf16[1,2,512,1536]{3,2,1,0:T(8,128)(2,1)S(1)} %copy-done, bf16[512,384]{1,0:T(8,128)(2,1)S(1)} %collective-permute-done.4.near_ref, bf16[512,1536]{1,0:T(8,128)(2,1)} %collective-permute-done.3.far_ref, ...), custom_call_target="tpu_custom_call" | custom-call | bytes 2752512 | tf_op jit(solution)/shard_map/choose/pallas_call | solution.py:219
  109.6 2.0 %choose.7 = (bf16[512,384]{1,0:T(8,128)(2,1)}, bf16[512,384]{1,0:T(8,128)(2,1)}) custom-call(s32[1]{0:T(128)} %bitcast.12.mode_ref, bf16[1,2,512,1536]{3,2,1,0:T(8,128)(2,1)S(1)} %copy-done, bf16[512,384]{1,0:T(8,128)(2,1)S(1)} %collective-permute-done.9.near_ref, bf16[512,1536]{1,0:T(8,128)(2,1)} %collective-permute-done.3.far_ref, ...), custom_call_target="tpu_custom_call" | custom-call | bytes 2752512 | tf_op jit(solution)/shard_map/choose/pallas_call | solution.py:219
  111.5 0.0 collective-permute-done.12.g2_ref.rest_4_
  111.5 0.9 copy-done.2
  112.5 0.1 collective-permute-start.5
  112.5 0.0 collective-permute-done.6.g1_ref
  112.5 2.5 %collective-permute-start.10 = (bf16[512,384]{1,0:T(8,128)(2,1)}, bf16[512,384]{1,0:T(8,128)(2,1)}, u32[]{:S(2)}, u32[]{:S(2)}) collective-permute-start(bf16[512,384]{1,0:T(8,128)(2,1)} %get-tuple-element.23), channel_id=1, source_target_pairs={{4,0},{8,4},{12,8},{20,16},{24,20},{28,24},{0,12},{16,28},{5,1},{9... | collective-permute-start | bytes 1179656 | tf_op jit(solution)/shard_map/ppermute | solution.py:280
  115.0 0.6 fusion.7.f_ref
  115.6 0.6 slice.58
  116.9 29.1 %collective-permute-done.13.x_ref.rest_0_ = bf16[512,384]{1,0:T(8,128)(2,1)} collective-permute-done((bf16[512,384]{1,0:T(8,128)(2,1)}, bf16[512,384]{1,0:T(8,128)(2,1)}, u32[]{:S(2)}, u32[]{:S(2)}) %collective-permute-start.13) | collective-permute-done | bytes 393248 | tf_op jit(solution)/shard_map/ppermute | solution.py:280
  146.0 1.1 copy-done.3
  147.1 0.7 copy-done.9
  147.8 0.6 copy-done.12
  148.4 5.3 %backward.6 = (f32[512,1536]{1,0:T(8,128)S(1)}, f32[1,512]{1,0:T(1,128)S(1)}) custom-call(s32[2]{0:T(128)S(1)} %copy-done.12, bf16[512,384]{1,0:T(8,128)(2,1)} %collective-permute-done.13.x_ref.rest_0_, bf16[512,1536]{1,0:T(8,128)(2,1)} %collective-permute-done.6.g1_ref, bf16[512,768]{1,0:T(8,128)(2,1)S(1)} %copy-done.3, f32[1,512]{1,0:T(1,128)S(1)} %copy-done.9, ...), custom_call_target="tpu_custom_call" | custom-call | flops 1006632960 | bytes 1966080 | tf_op jit(solution)/shard_map/backward/pallas_call | solution.py:184
  153.6 0.0 collective-permute-done.11.x_ref.rest_1_
  153.7 5.1 %backward.7 = (f32[512,1536]{1,0:T(8,128)S(1)}, f32[1,512]{1,0:T(1,128)S(1)}) custom-call(s32[2]{0:T(128)S(1)} %copy-done.12, bf16[512,384]{1,0:T(8,128)(2,1)S(1)} %collective-permute-done.11.x_ref.rest_1_, bf16[512,1536]{1,0:T(8,128)(2,1)} %collective-permute-done.6.g1_ref, bf16[512,768]{1,0:T(8,128)(2,1)S(1)} %copy-done.4, ...), custom_call_target="tpu_custom_call", output_to_operand_aliasing={{0}: (7, {})} | custom-call | flops 1006632960 | bytes 1966080 | tf_op jit(solution)/shard_map/backward/pallas_call | solution.py:184
  158.8 0.0 collective-permute-done.7.g2_ref.rest_5_
  158.8 0.0 collective-permute-done.10.x_ref.rest_2_
  158.9 5.4 %backward.8 = (f32[512,1536]{1,0:T(8,128)S(1)}, f32[1,512]{1,0:T(1,128)S(1)}) custom-call(s32[2]{0:T(128)S(1)} %copy-done.12, bf16[512,384]{1,0:T(8,128)(2,1)} %collective-permute-done.10.x_ref.rest_2_, bf16[512,1536]{1,0:T(8,128)(2,1)} %collective-permute-done.6.g1_ref, ...), custom_call_target="tpu_custom_call", output_to_operand_aliasing={{0}: (7, {})} | custom-call | flops 1006632960 | bytes 1966080 | tf_op jit(solution)/shard_map/backward/pallas_call | solution.py:184
  164.2 0.0 collective-permute-done.5.x_ref.rest_3_
  164.3 5.4 %backward.9 = (f32[512,1536]{1,0:T(8,128)S(1)}, f32[1,512]{1,0:T(1,128)S(1)}) custom-call(s32[2]{0:T(128)S(1)} %copy-done.12, bf16[512,384]{1,0:T(8,128)(2,1)} %collective-permute-done.5.x_ref.rest_3_, bf16[512,1536]{1,0:T(8,128)(2,1)} %collective-permute-done.6.g1_ref, ...), custom_call_target="tpu_custom_call", output_to_operand_aliasing={{0}: (7, {})} | custom-call | flops 1006632960 | bytes 1966080 | tf_op jit(solution)/shard_map/backward/pallas_call | solution.py:184
  169.7 1.6 copy-done.1
  171.3 5.6 %psum.23 = f32[1,512]{1,0:T(1,128)S(1)} all-reduce(f32[1,512]{1,0:T(1,128)S(1)} %add_add_fusion), channel_id=1, replica_groups=mesh['section'=8,'tensor'=4] {'tensor'}, use_global_device_ids=true, to_apply=%region_5.6 | all-reduce | flops 512 | bytes 4096 | tf_op jit(solution)/shard_map/psum | solution.py:360
  176.9 0.7 fusion.10.row_ref
  177.6 1.1 copy-done.5
  178.7 5.1 %finish.1 = bf16[512,1536]{1,0:T(8,128)(2,1)} custom-call(s32[1]{0:T(128)} %bitcast.10.pick_ref, f32[512,1536]{1,0:T(8,128)} %copy-done.1, f32[1,512]{1,0:T(1,128)S(1)} %fusion.10.row_ref, bf16[512,384]{1,0:T(8,128)(2,1)} %collective-permute-done.13.x_ref.rest_0_, bf16[512,384]{1,0:T(8,128)(2,1)S(1)} %collective-permute-done.11.x_ref.rest_1_, ...), custom_call_target="tpu_custom_call" | custom-call | flops 1572864 | bytes 7864320 | tf_op jit(solution)/shard_map/finish/pallas_call | solution.py:259
  (28 shorter events, 0.1 us)
Async XLA Ops:
  0.6 17.1 %copy-start = (bf16[1,2,512,1536]{3,2,1,0:T(8,128)(2,1)S(1)}, bf16[1,2,512,1536]{3,2,1,0:T(8,128)(2,1)}, u32[]{:S(2)}) copy-start(bf16[1,2,512,1536]{3,2,1,0:T(8,128)(2,1)} %next_ref.7) | copy-start | bytes 9437188
  13.7 14.1 %collective-permute-start = (f32[1,512]{1,0:T(1,128)S(1)}, f32[1,512]{1,0:T(1,128)S(1)}, u32[]{:S(2)}, u32[]{:S(2)}) collective-permute-start(f32[1,512]{1,0:T(1,128)S(1)} %slice.56), channel_id=1, source_target_pairs={{0,16},{4,20},{8,24},{12,28},{16,0},{20,4},{24,8},{28,12},{1,17},{... | collective-permute-start | bytes 6152 | tf_op jit(solution)/shard_map/ppermute | solution.py:280
  16.3 12.0 %copy-start.10 = (f32[1,1536]{1,0:T(1,128)S(1)}, f32[1,1536]{1,0:T(1,128)}, u32[]{:S(2)}) copy-start(f32[1,1536]{1,0:T(1,128)} %gq_ref.3) | copy-start | bytes 18436
  16.3 12.0 %copy-start.11 = (f32[1,1536]{1,0:T(1,128)S(1)}, f32[1,1536]{1,0:T(1,128)}, u32[]{:S(2)}) copy-start(f32[1,1536]{1,0:T(1,128)} %gk_ref.3) | copy-start | bytes 18436
  16.3 96.2 %collective-permute-start.6 = (bf16[512,1536]{1,0:T(8,128)(2,1)}, bf16[512,1536]{1,0:T(8,128)(2,1)}, u32[]{:S(2)}, u32[]{:S(2)}) collective-permute-start(bf16[512,1536]{1,0:T(8,128)(2,1)} %bitcast.28), channel_id=1, source_target_pairs={{4,0},{8,4},{12,8},{20,16},{24,20},{28,24},{5,1},{9,5},{13,9},{21,... | collective-permute-start | bytes 4718600 | tf_op jit(solution)/shard_map/ppermute | solution.py:280
  19.6 34.9 %collective-permute-start.3 = (bf16[512,1536]{1,0:T(8,128)(2,1)}, bf16[512,1536]{1,0:T(8,128)(2,1)}, u32[]{:S(2)}, u32[]{:S(2)}) collective-permute-start(bf16[512,1536]{1,0:T(8,128)(2,1)} %get-tuple-element.37), channel_id=1, source_target_pairs={{8,24},{24,8},{9,25},{25,9},{10,26},{26,10},{11,27},{27,11}} | collective-permute-start | bytes 4718600 | tf_op jit(solution)/shard_map/ppermute | solution.py:280
  23.6 33.8 %collective-permute-start.8 = (bf16[512,384]{1,0:T(8,128)(2,1)}, bf16[512,384]{1,0:T(8,128)(2,1)}, u32[]{:S(2)}, u32[]{:S(2)}) collective-permute-start(bf16[512,384]{1,0:T(8,128)(2,1)} %get-tuple-element.40), channel_id=1, source_target_pairs={{4,20},{12,28},{20,4},{28,12},{5,21},{13,29},{21,5},{29,13},{6,22}... | collective-permute-start | bytes 1179656 | tf_op jit(solution)/shard_map/ppermute | solution.py:280
  25.0 29.6 %collective-permute-start.2 = (bf16[512,384]{1,0:T(8,128)(2,1)}, bf16[512,384]{1,0:T(8,128)(2,1)}, u32[]{:S(2)}, u32[]{:S(2)}) collective-permute-start(bf16[512,384]{1,0:T(8,128)(2,1)} %get-tuple-element.41), channel_id=1, source_target_pairs={{4,20},{12,28},{20,4},{28,12},{5,21},{13,29},{21,5},{29,13},{6,22}... | collective-permute-start | bytes 1179656 | tf_op jit(solution)/shard_map/ppermute | solution.py:280
  28.3 1.4 copy-start.7
  29.7 1.4 copy-start.8
  44.3 67.2 %collective-permute-start.12 = (bf16[512,768]{1,0:T(8,128)(2,1)S(1)}, bf16[512,768]{1,0:T(8,128)(2,1)S(1)}, u32[]{:S(2)}, u32[]{:S(2)}) collective-permute-start(bf16[512,768]{1,0:T(8,128)(2,1)S(1)} %get-tuple-element.38), channel_id=1, source_target_pairs={{16,12},{0,28},{17,13},{1,29},{18,14},{2,30},{19,15},{3,31}} | collective-permute-start | bytes 2359304 | tf_op jit(solution)/shard_map/ppermute | solution.py:280
  56.5 18.6 %copy-start.6 = (bf16[1,512,1536]{2,1,0:T(8,128)(2,1)S(1)}, bf16[1,512,1536]{2,1,0:T(8,128)(2,1)}, u32[]{:S(2)}) copy-start(bf16[1,512,1536]{2,1,0:T(8,128)(2,1)} %param.6) | copy-start | bytes 4718596
  56.5 18.6 %copy-start.13 = (f32[1,512]{1,0:T(1,128)S(1)}, f32[1,512]{1,0:T(1,128)}, u32[]{:S(2)}) copy-start(f32[1,512]{1,0:T(1,128)} %get-tuple-element.46.f_ref) | copy-start | bytes 6148
  56.5 48.6 %collective-permute-start.4 = (bf16[512,384]{1,0:T(8,128)(2,1)S(1)}, bf16[512,384]{1,0:T(8,128)(2,1)S(1)}, u32[]{:S(2)}, u32[]{:S(2)}) collective-permute-start(bf16[512,384]{1,0:T(8,128)(2,1)S(1)} %get-tuple-element.18), channel_id=1, source_target_pairs={{4,20},{12,28},{20,4},{28,12},{5,21},{13,29},{21,5},{29,13},{6,22}... | collective-permute-start | bytes 1179656 | tf_op jit(solution)/shard_map/ppermute | solution.py:280
  59.3 48.2 %collective-permute-start.9 = (bf16[512,384]{1,0:T(8,128)(2,1)S(1)}, bf16[512,384]{1,0:T(8,128)(2,1)S(1)}, u32[]{:S(2)}, u32[]{:S(2)}) collective-permute-start(bf16[512,384]{1,0:T(8,128)(2,1)S(1)} %get-tuple-element.22), channel_id=1, source_target_pairs={{4,20},{12,28},{20,4},{28,12},{5,21},{13,29},{21,5},{29,13},{6,22}... | collective-permute-start | bytes 1179656 | tf_op jit(solution)/shard_map/ppermute | solution.py:280
  60.0 23.2 %collective-permute-start.1 = (f32[1,3712]{1,0:T(1,128)S(1)}, f32[1,3712]{1,0:T(1,128)S(1)}, u32[]{:S(2)}, u32[]{:S(2)}) collective-permute-start(f32[1,3712]{1,0:T(1,128)S(1)} %reshape_maximum_fusion), channel_id=1, source_target_pairs={{0,28},{4,0},{8,4},{12,8},{16,12},{20,16},{24,20},{28,24},{1,29},{... | collective-permute-start | bytes 44552 | tf_op jit(solution)/shard_map/ppermute | solution.py:280
  83.2 32.4 %copy-start.14 = (f32[1,3712]{1,0:T(1,128)}, f32[1,3712]{1,0:T(1,128)S(1)}, u32[]{:S(2)}) copy-start(f32[1,3712]{1,0:T(1,128)S(1)} %collective-permute-done.1) | copy-start | bytes 44548
  83.2 75.6 %collective-permute-start.7 = (bf16[512,768]{1,0:T(8,128)(2,1)}, bf16[512,768]{1,0:T(8,128)(2,1)}, u32[]{:S(2)}, u32[]{:S(2)}) collective-permute-start(bf16[512,768]{1,0:T(8,128)(2,1)} %get-tuple-element.39), channel_id=1, source_target_pairs={{16,12},{0,28},{17,13},{1,29},{18,14},{2,30},{19,15},{3,31}} | collective-permute-start | bytes 2359304 | tf_op jit(solution)/shard_map/ppermute | solution.py:280
  105.1 48.5 %collective-permute-start.11 = (bf16[512,384]{1,0:T(8,128)(2,1)}, bf16[512,384]{1,0:T(8,128)(2,1)S(1)}, u32[]{:S(2)}, u32[]{:S(2)}) collective-permute-start(bf16[512,384]{1,0:T(8,128)(2,1)} %get-tuple-element.24), channel_id=1, source_target_pairs={{4,0},{8,4},{12,8},{20,16},{24,20},{28,24},{0,12},{16,28},{5,1},{9... | collective-permute-start | bytes 1179656 | tf_op jit(solution)/shard_map/ppermute | solution.py:280
  107.5 38.5 %collective-permute-start.13 = (bf16[512,384]{1,0:T(8,128)(2,1)}, bf16[512,384]{1,0:T(8,128)(2,1)}, u32[]{:S(2)}, u32[]{:S(2)}) collective-permute-start(bf16[512,384]{1,0:T(8,128)(2,1)} %get-tuple-element.25), channel_id=1, source_target_pairs={{4,0},{8,4},{12,8},{20,16},{24,20},{28,24},{0,12},{16,28},{5,1},{9... | collective-permute-start | bytes 1179656 | tf_op jit(solution)/shard_map/ppermute | solution.py:280
  111.5 0.9 copy-start.2
  112.5 51.8 %collective-permute-start.5 = (bf16[512,384]{1,0:T(8,128)(2,1)}, bf16[512,384]{1,0:T(8,128)(2,1)}, u32[]{:S(2)}, u32[]{:S(2)}) collective-permute-start(bf16[512,384]{1,0:T(8,128)(2,1)} %get-tuple-element.19), channel_id=1, source_target_pairs={{4,0},{8,4},{12,8},{20,16},{24,20},{28,24},{0,12},{16,28},{5,1},{9... | collective-permute-start | bytes 1179656 | tf_op jit(solution)/shard_map/ppermute | solution.py:280
  112.5 46.3 %collective-permute-start.10 = (bf16[512,384]{1,0:T(8,128)(2,1)}, bf16[512,384]{1,0:T(8,128)(2,1)}, u32[]{:S(2)}, u32[]{:S(2)}) collective-permute-start(bf16[512,384]{1,0:T(8,128)(2,1)} %get-tuple-element.23), channel_id=1, source_target_pairs={{4,0},{8,4},{12,8},{20,16},{24,20},{28,24},{0,12},{16,28},{5,1},{9... | collective-permute-start | bytes 1179656 | tf_op jit(solution)/shard_map/ppermute | solution.py:280
  146.0 1.1 copy-start.3
  147.1 0.7 copy-start.9
  147.8 0.6 copy-start.12
  148.4 5.3 %copy-start.4 = (bf16[512,768]{1,0:T(8,128)(2,1)S(1)}, bf16[512,768]{1,0:T(8,128)(2,1)}, u32[]{:S(2)}) copy-start(bf16[512,768]{1,0:T(8,128)(2,1)} %copy-done.2) | copy-start | bytes 2359300
  169.6 1.6 copy-start.1
  177.6 1.1 copy-start.5

commit v3 on v2

v3 whole, which is shorter than its diff:
```python
import functools
import math

import jax
import jax.numpy as jnp
from jax import lax
from jax.experimental import pallas as pl
from jax.experimental.pallas import tpu as pltpu
from jax.sharding import PartitionSpec as P

HDIM = 128
EPSILON = 1e-05
SCALE = 1.0 / math.sqrt(HDIM)
LOG2E = math.log2(math.e)
VMEM = 32 * 1024 * 1024

F32 = jnp.float32
BF16 = jnp.bfloat16


def dot(a, b, contract):
    return lax.dot_general(a, b, ((contract[0], contract[1]), ((), ())), preferred_element_type=F32)


def nt(a, b):
    return dot(a, b, ((1,), (1,)))


def nn(a, b):
    return dot(a, b, ((1,), (0,)))


def block_of(tokens):
    return 256 if tokens % 256 == 0 else tokens


def masked(block, kept):
    return jnp.where(kept, block, -1e30)


def kept_keys(size):
    keys = lax.broadcasted_iota(jnp.int32, (size, size), 0)
    return keys <= lax.broadcasted_iota(jnp.int32, (size, size), 1)


def scores_of(keys, queries, j, size, kept):
    mine = queries[j * size : (j + 1) * size]
    diagonal = masked(nt(keys[j * size : (j + 1) * size], mine), kept)
    if j == 0:
        return [diagonal]
    return [nt(keys[: j * size], mine), diagonal]


def exponents(parts):
    top = functools.reduce(jnp.maximum, [jnp.max(p, axis=0, keepdims=True) for p in parts])
    exps = [jnp.exp2((p - top) * (SCALE * LOG2E)) for p in parts]
    total = sum(jnp.sum(e, axis=0, keepdims=True) for e in exps)
    return exps, total


def stacked(parts):
    return parts[0] if len(parts) == 1 else jnp.concatenate(parts, axis=0)


def normed_head(x, factor, gain_q, gain_k):
    wide = x.astype(F32)
    normed = wide * factor
    return wide, (normed * gain_q).astype(BF16), (normed * gain_k).astype(BF16), normed.astype(BF16)


def column_of(row):
    return jnp.broadcast_to(row, (HDIM, row.shape[1])).T[:, 0:1]


def forward_kernel(heads, x_ref, f_ref, gq_ref, gk_ref, *rest):
    o_ref = rest[-1]
    tokens = x_ref.shape[0]
    size = block_of(tokens)
    kept = kept_keys(size)
    factor = column_of(f_ref[...])
    for h in range(heads):
        lanes = slice(h * HDIM, (h + 1) * HDIM)
        wide, q, k, v = normed_head(x_ref[:, lanes], factor, gq_ref[:, lanes], gk_ref[:, lanes])
        vt = v.T
        for j in range(tokens // size):
            exps, total = exponents(scores_of(k, q, j, size, kept))
            mixed = nn(vt[:, : (j + 1) * size], stacked(exps).astype(BF16)) * (1.0 / total)
            rows = slice(j * size, (j + 1) * size)
            o_ref[rows, lanes] = (wide[rows] + mixed.T).astype(BF16)


def forward(x, factor, gain_q, gain_k, heads, after=()):
    tokens, width = x.shape
    lanes = heads * HDIM
    block = pl.BlockSpec((tokens, lanes), lambda i: (0, i))
    gain = pl.BlockSpec((1, lanes), lambda i: (0, i))
    return pl.pallas_call(
        functools.partial(forward_kernel, heads),
        out_shape=jax.ShapeDtypeStruct(x.shape, BF16),
        grid=(width // lanes,),
        in_specs=[block, pl.BlockSpec((1, tokens), lambda i: (0, 0)), gain, gain]
        + [pl.BlockSpec(memory_space=pl.ANY)] * len(after),
        out_specs=block,
        compiler_params=pltpu.CompilerParams(vmem_limit_bytes=VMEM),
        name="forward",
    )(x, factor, gain_q, gain_k, *after)


def backward_head(x, g, factor, gain_q, gain_k):
    tokens = x.shape[0]
    size = block_of(tokens)
    kept = kept_keys(size)
    wide, q, k, v = normed_head(x, factor, gain_q, gain_k)
    kt = k.T
    blocks = tokens // size
    d_q = []
    d_k = [None] * blocks
    d_v = [None] * blocks
    for j in range(blocks):
        rows = slice(j * size, (j + 1) * size)
        exps, total = exponents(scores_of(k, q, j, size, kept))
        inverse = 1.0 / total
        weights = [e * inverse for e in exps]
        grads = [nt(v[: j * size], g[rows])] if j else []
        grads.append(nt(v[rows], g[rows]))
        delta = sum(jnp.sum(w * d, axis=0, keepdims=True) for w, d in zip(weights, grads))
        scores = stacked([(w * ((d - delta) * SCALE)).astype(BF16) for w, d in zip(weights, grads)])
        rounded = stacked([w.astype(BF16) for w in weights])
        d_q.append(nn(kt[:, : (j + 1) * size], scores).T)
        part_k = nn(scores, q[rows])
        part_v = nn(rounded, g[rows])
        for i in range(j + 1):
            mine = slice(i * size, (i + 1) * size)
            d_k[i] = part_k[mine] if d_k[i] is None else d_k[i] + part_k[mine]
            d_v[i] = part_v[mine] if d_v[i] is None else d_v[i] + part_v[mine]
    d_normed = stacked(d_q) * gain_q + stacked(d_k) * gain_k + stacked(d_v)
    return wide, d_normed


def chosen(index, refs, at):
    value = refs[0][at]
    for i, ref in enumerate(refs[1:]):
        value = jnp.where(index == i + 1, ref[at], value)
    return value


def backward_kernel(heads, n_x, n_g, pick_ref, *refs):
    x_refs, g_refs = refs[:n_x], refs[n_x : n_x + n_g]
    f_ref, gq_ref, gk_ref = refs[n_x + n_g : n_x + n_g + 3]
    a_ref, x_ref, inner_ref = refs[-3:]
    first = pl.program_id(0) == 0

    @pl.when(jnp.logical_and(first, pick_ref[0] == 0))
    def _():
        inner_ref[...] = jnp.zeros_like(inner_ref)

    @pl.when(pick_ref[0] == 1)
    def _():
        factor = column_of(f_ref[...])
        part = None
        for h in range(heads):
            lanes = slice(h * HDIM, (h + 1) * HDIM)
            here = (slice(None), lanes)
            x = chosen(pick_ref[1], x_refs, here)
            g = chosen(pick_ref[2], g_refs, here)
            wide, d_normed = backward_head(x, g, factor, gq_ref[:, lanes], gk_ref[:, lanes])
            a_ref[:, lanes] = g.astype(F32) + factor * d_normed
            x_ref[:, lanes] = x
            product = d_normed * wide
            part = product if part is None else part + product
        inner = jnp.sum(part.T, axis=0, keepdims=True)

        @pl.when(first)
        def _():
            inner_ref[...] = inner

        @pl.when(jnp.logical_not(first))
        def _():
            inner_ref[...] += inner


def backward(pick, xs, gs, factor, gain_q, gain_k, heads, steps, first, sofar=(), after=()):
    tokens = xs[0][0].shape[0]
    width = gain_q.shape[1]
    lanes = heads * HDIM
    at = lambda start: pl.BlockSpec((tokens, lanes), lambda i, pick: (0, start + i))
    gain = pl.BlockSpec((1, lanes), lambda i, pick: (0, first + i))
    row = pl.BlockSpec((1, tokens), lambda i, pick: (0, 0))
    extra = tuple(sofar) + tuple(after)
    before = 1 + len(xs) + len(gs) + 3
    return pl.pallas_call(
        functools.partial(backward_kernel, heads, len(xs), len(gs)),
        out_shape=(
            jax.ShapeDtypeStruct((tokens, width), F32),
            jax.ShapeDtypeStruct((tokens, width), BF16),
            jax.ShapeDtypeStruct((1, tokens), F32),
        ),
        grid_spec=pltpu.PrefetchScalarGridSpec(
            num_scalar_prefetch=1,
            grid=(steps,),
            in_specs=[at(b) for _, b in (*xs, *gs)] + [row, gain, gain]
            + [pl.BlockSpec(memory_space=pl.ANY)] * len(extra),
            out_specs=(at(first), at(first), row),
        ),
        input_output_aliases={before: 0, before + 1: 1} if sofar else {},
        compiler_params=pltpu.CompilerParams(vmem_limit_bytes=VMEM),
        name="backward",
    )(pick, *[x for x, _ in xs], *[g for g, _ in gs], factor, gain_q, gain_k, *extra)


def choose_kernel(mode_ref, *refs):
    for m, ref in enumerate(refs[:2]):

        @pl.when(mode_ref[0] == m)
        def _():
            refs[-2][...] = ref[...]

    refs[-1][...] = refs[2][...]


def choose(mode, stash, fetched, start, step, coming, after=()):
    tokens = fetched.shape[0]
    block = (tokens, step)
    whole = lambda at: pl.BlockSpec(block, lambda i, mode: (0, at))
    of_stash = lambda which, at: pl.BlockSpec((None, None, tokens, step), lambda i, mode: (0, which, 0, at))
    return pl.pallas_call(
        choose_kernel,
        out_shape=[jax.ShapeDtypeStruct(block, BF16)] * 2,
        grid_spec=pltpu.PrefetchScalarGridSpec(
            num_scalar_prefetch=1,
            grid=(1,),
            in_specs=[of_stash(0, start), whole(start), of_stash(1, coming)]
            + [pl.BlockSpec(memory_space=pl.ANY)] * len(after),
            out_specs=[whole(0)] * 2,
        ),
        compiler_params=pltpu.CompilerParams(vmem_limit_bytes=VMEM),
        name="choose",
    )(mode, stash, fetched, stash, *after)


def finish_kernel(pick_ref, a_ref, x_ref, row_ref, other_ref, o_ref):
    row = column_of(row_ref[...])

    @pl.when(pick_ref[0] == 0)
    def _():
        o_ref[...] = (a_ref[...] - x_ref[...].astype(F32) * row).astype(BF16)

    @pl.when(pick_ref[0] == 1)
    def _():
        o_ref[...] = other_ref[...]


def finish(pick, a, x, row, other, lanes):
    tokens, width = a.shape
    block = pl.BlockSpec((tokens, lanes), lambda i, pick: (0, i))
    return pl.pallas_call(
        finish_kernel,
        out_shape=jax.ShapeDtypeStruct(a.shape, BF16),
        grid_spec=pltpu.PrefetchScalarGridSpec(
            num_scalar_prefetch=1,
            grid=(width // lanes,),
            in_specs=[block, block, pl.BlockSpec((1, tokens), lambda i, pick: (0, 0)), block],
            out_specs=block,
        ),
        compiler_params=pltpu.CompilerParams(vmem_limit_bytes=VMEM),
        name="finish",
    )(pick, a, x, row, other)


def squares_kernel(current_ref, stash_ref, o_ref):
    def total(x):
        wide = x.astype(F32)
        square = wide * wide
        sums = sum(square[:, i : i + HDIM] for i in range(0, square.shape[1], HDIM))
        return jnp.sum(sums.T, axis=0, keepdims=True)

    rows = jnp.concatenate([total(current_ref[...]), total(stash_ref[0]), total(stash_ref[1])], axis=0)

    @pl.when(pl.program_id(0) == 0)
    def _():
        o_ref[...] = rows

    @pl.when(pl.program_id(0) > 0)
    def _():
        o_ref[...] += rows


def squares(current, stash, lanes):
    tokens, width = current.shape
    return pl.pallas_call(
        squares_kernel,
        out_shape=jax.ShapeDtypeStruct((3, tokens), F32),
        grid=(width // lanes,),
        in_specs=[
            pl.BlockSpec((tokens, lanes), lambda i: (0, i)),
            pl.BlockSpec((None, 2, tokens, lanes), lambda i: (0, 0, 0, i)),
        ],
        out_specs=pl.BlockSpec((3, tokens), lambda i: (0, 0)),
        compiler_params=pltpu.CompilerParams(vmem_limit_bytes=VMEM),
        name="squares",
    )(current, stash)


def send(x, pairs):
    return lax.ppermute(x, "section", pairs)


def local(width_all, layer_input, grad_input, stashed, eviction, query_gain, key_gain):
    n = lax.axis_size("section")
    half = n // 2
    special = (0, half)
    me = lax.axis_index("section")
    evicted = eviction[0] == 1
    word = lambda *flags: jnp.stack([jnp.asarray(f).astype(jnp.int32) for f in flags])

    prior = [(s, (s - 1) % n) for s in range(n)]
    inside = [(s, s - 1) for s in range(n) if s not in special]
    partner = [(s, (s + half) % n) for s in range(n)]
    to_partner = [p for p in partner if p[0] not in special]
    within = inside + [(half, n - 1), (0, half - 1)]
    direct = [((s + half) % n, s - 1) for s in range(n) if s not in special]

    current = layer_input[0]
    upstream = grad_input[0]
    tokens, width = current.shape
    heads_here = width // HDIM
    step = width // 3
    heads = heads_here // 3
    own, held = stashed[0, 0], stashed[0, 1]
    piece = lambda x, c: x[:, c * step : (c + 1) * step]

    is_special = jnp.logical_or(me == 0, me == half)
    fetched = send(held[:, : 2 * step], to_partner)
    early = send(jnp.where(is_special, held, upstream), within)
    kept = send(piece(own, 2), inside)
    upward = send(upstream, [(0, n - 1)])

    totals = lax.psum(squares(current, stashed, step), "tensor")
    factor_of = lambda total: lax.rsqrt(total / width_all + EPSILON)

    kept_here = jnp.logical_and(me == half, jnp.logical_not(evicted))
    own_factor = factor_of(totals[1:2])
    own_a, own_x, own_inner = backward(
        word(kept_here, 0, 0), [(own, 0)], [(upstream, 0)], own_factor, query_gain, key_gain, heads, 3, 0,
    )
    own_inner = lax.psum(own_inner, "tensor")
    slot = finish(
        word(jnp.logical_not(kept_here)), own_a, own_x, own_factor**3 * own_inner / width_all, upstream, step
    )
    downward = send(slot, [(half, half - 1)])

    fetched_total = send(totals[2:3], partner)
    chosen_total = jnp.where(evicted, fetched_total, totals[1:2])
    flag = jnp.broadcast_to(eviction[0].astype(F32), (1, HDIM))
    told = send(jnp.concatenate([chosen_total, query_gain, key_gain, flag], axis=1), prior)
    factor = factor_of(told[:, :tokens])
    gain_q = told[:, tokens : tokens + width]
    gain_k = told[:, tokens + width : tokens + 2 * width]
    after_evicted = told[0, tokens + 2 * width] == 1.0

    mode = eviction
    sent, last = choose(mode, stashed, fetched, 0, step, 2, (slot,))
    passed = [send(sent, inside)]
    straight = send(last, direct)
    sent, _ = choose(mode, stashed, fetched, 1, step, 2, (slot,))
    passed.append(send(sent, inside))

    output = forward(current, factor_of(totals[0:1]), query_gain, key_gain, heads, (sent,))

    crossed = jnp.logical_or(me == half - 1, me == n - 1)
    which_g = jnp.where(me == half - 1, 1, jnp.where(me == n - 1, 2, 0))
    take = word(1, jnp.where(crossed, 1, 0), which_g)
    take_last = word(1, jnp.where(crossed, 2, jnp.where(after_evicted, 0, 1)), which_g)
    gs = lambda c: [(early, c), (downward, c), (upward, c)]
    a, x, inner = backward(take, [(passed[0], 0), (early, 0)], gs(0), factor, gain_q, gain_k, heads, 1, 0)
    a, x, part = backward(
        take_last, [(straight, 0), (kept, 0), (early, 2)], gs(2), factor, gain_q, gain_k, heads, 1, 2, (a, x)
    )
    inner = inner + part
    a, x, part = backward(
        take, [(passed[1], 0), (early, 1)], gs(1), factor, gain_q, gain_k, heads, 1, 1, (a, x)
    )
    inner = lax.psum(inner + part, "tensor")
    done = word(jnp.logical_and(me == half - 1, jnp.logical_not(after_evicted)))
    result = finish(done, a, x, factor**3 * inner / width_all, downward, step)
    return (output[None], result[None])


def solution(mesh):
    placed = (
        P("section", None, "tensor"),
        P("section", None, "tensor"),
        P("section", None, None, "tensor"),
        P("section"),
        P("section", "tensor"),
        P("section", "tensor"),
    )

    def whole(layer_input, *others):
        return jax.shard_map(
            functools.partial(local, layer_input.shape[-1]),
            mesh=mesh,
            in_specs=placed,
            out_specs=(P("section", None, "tensor"), P("section", None, "tensor")),
            check_vma=False,
        )(layer_input, *others)

    return whole
```

time: 185 us -> 156 us (0.84)
  starting transfers between devices: 62.5 us -> 36 us
  other arithmetic: 10 us -> 2.98 us
  local copies, waits for them, and re-layouts: 14.4 us -> 18.9 us
  blocking collectives: 20.2 us -> 22.9 us
  waiting for transfers between devices: 29.2 us -> 27.3 us
    ppermute x14 -> x10, starting transfers between devices: 62.5 us -> 36 us  [send(): return lax.ppermute(x, 'section', pairs)]
    unnamed x30, local copies, waits for them, and re-layouts: 8.91 us -> 14.1 us
    reduce_sum x2 -> x0, other arithmetic: 4.51 us -> none  [squares(): return jnp.sum(wide * wide, axis=-1)[None]]
    pallas_call x4 -> x2, Pallas kernels: 7.86 us -> 3.99 us  [choose(): pl.pallas_call(choose_kernel, out_shape=[jax.ShapeDtypeStruct(block, BF16...]
    pallas_call x6 -> x7, Pallas kernels: 29.4 us -> 32.6 us  [the longest x4 23.6 us: backward(): pl.pallas_call(functools.partial(backward_kernel, heads, len(xs), len(gs)...]
    psum x2, blocking collectives: 14.1 us -> 16.8 us  [the longest x1 8.49 us: local(): totals = lax.psum(squares(current, stashed, step), 'tensor')]
    ppermute x14 -> x10, waiting for transfers between devices: 29.2 us -> 27.3 us  [send(): return lax.ppermute(x, 'section', pairs)]
  transfers between devices with their start and end apart: 14 -> 10, of which waited for: 1 -> 2; matrix products, arithmetic and copies ran while one was open for 6% -> 5% of each run, Pallas kernels for 19% -> 21%
where the time goes in v3:
time: 156 us; the launch traced here: 154 us
  Pallas kernels  44.1 us (28%)
  starting transfers between devices  36 us (23%)
  waiting for transfers between devices  27.3 us (18%)
  blocking collectives  22.9 us (15%)
  local copies, waits for them, and re-layouts  18.9 us (12%)
  other arithmetic  2.98 us (2%)
  between operations  2.22 us (1%)
    ppermute x10, starting transfers between devices, send(): return lax.ppermute(x, 'section', pairs)  36 us
    ppermute x10, waiting for transfers between devices, send(): return lax.ppermute(x, 'section', pairs)  27.3 us
    pallas_call x4, Pallas kernels, backward(): pl.pallas_call(functools.partial(backward_kernel, heads, len(xs), len(gs)...  23.6 us
    unnamed x30, local copies, waits for them, and re-layouts  14.1 us
    psum x1, blocking collectives, local(): totals = lax.psum(squares(current, stashed, step), 'tensor')  8.49 us
    psum x1, blocking collectives, local(): inner = lax.psum(inner + part, 'tensor')  8.35 us
    pallas_call x2, Pallas kernels, finish(): pl.pallas_call(finish_kernel, out_shape=jax.ShapeDtypeStruct(a.shape, BF1...  7.56 us
    pallas_call x1, Pallas kernels, forward(): pl.pallas_call(functools.partial(forward_kernel, heads), out_shape=jax.Sh...  7.45 us
  transfers between devices with their start and end apart: 10, of which 2 were waited for; matrix products, arithmetic and copies ran while one was open for 5% of the time, Pallas kernels for 21%

profile of v3, /device:TPU:0, one launch (start us, length us, event | category | flops | bytes accessed | tf_op | source)
XLA Modules:
  0.0 154.4 jit_solution(5198141818980086784)
XLA Ops:
  0.6 0.0 copy-start
  0.6 1.9 %copy-done = bf16[1,2,512,1536]{3,2,1,0:T(8,128)(2,1)S(1)} copy-done((bf16[1,2,512,1536]{3,2,1,0:T(8,128)(2,1)S(1)}, bf16[1,2,512,1536]{3,2,1,0:T(8,128)(2,1)}, u32[]{:S(2)}) %copy-start) | copy-done | bytes 3145752
  2.5 0.0 copy-start.5
  2.5 1.4 copy-done.5
  3.9 0.0 copy-start.1
  3.9 1.5 squares.1
  5.4 8.5 %psum.21 = f32[3,512]{1,0:T(4,128)S(1)} all-reduce(f32[3,512]{1,0:T(4,128)S(1)} %squares.1), channel_id=1, replica_groups=mesh['section'=8,'tensor'=4] {'tensor'}, use_global_device_ids=true, to_apply=%region_0.1 | all-reduce | flops 1536 | bytes 12288 | tf_op jit(solution)/shard_map/psum | solution.py:338
  14.0 2.7 %collective-permute-start.1 = (f32[1,512]{1,0:T(1,128)S(1)}, f32[1,512]{1,0:T(1,128)S(1)}, u32[]{:S(2)}, u32[]{:S(2)}) collective-permute-start(f32[1,512]{1,0:T(1,128)S(1)} %slice.48), channel_id=1, source_target_pairs={{0,16},{4,20},{8,24},{12,28},{16,0},{20,4},{24,8},{28,12},{1,17},{... | collective-permute-start | bytes 6152 | tf_op jit(solution)/shard_map/ppermute | solution.py:305
  16.6 0.0 copy-done.1
  16.6 1.3 slice_bitcast_fusion
  18.0 1.1 slice.46
  19.0 1.7 %collective-permute-start = (bf16[512,1024]{1,0:T(8,128)(2,1)}, bf16[512,1024]{1,0:T(8,128)(2,1)}, u32[]{:S(2)}, u32[]{:S(2)}) collective-permute-start(bf16[512,1024]{1,0:T(8,128)(2,1)} %slice.46), channel_id=1, source_target_pairs={{4,20},{8,24},{12,28},{20,4},{24,8},{28,12},{5,21},{9,25},{13,29},... | collective-permute-start | bytes 3145736 | tf_op jit(solution)/shard_map/ppermute | solution.py:305
  20.8 2.7 %broadcast_select_fusion = bf16[512,1536]{1,0:T(8,128)(2,1)} fusion(pred[]{:T(512)S(6)} %or.9, bf16[1,512,1536]{2,1,0:T(8,128)(2,1)} %param.7, bf16[1,2,512,1536]{3,2,1,0:T(8,128)(2,1)S(1)} %copy-done.1), kind=kLoop, calls=%fused_computation.2 | loop fusion | flops 786432 | bytes 4718593 | tf_op jit(solution)/shard_map/jit(_where)/select_n | solution.py:334
  23.5 3.1 %collective-permute-start.4 = (bf16[512,1536]{1,0:T(8,128)(2,1)}, bf16[512,1536]{1,0:T(8,128)(2,1)}, u32[]{:S(2)}, u32[]{:S(2)}) collective-permute-start(bf16[512,1536]{1,0:T(8,128)(2,1)} %broadcast_select_fusion), channel_id=1, source_target_pairs={{4,0},{8,4},{12,8},{20,16},{24,20},{28,24},{16,28},{0,12},{5,1},{9... | collective-permute-start | bytes 4718600 | tf_op jit(solution)/shard_map/ppermute | solution.py:305
  26.6 5.6 %collective-permute-start.6 = (bf16[512,1536]{1,0:T(8,128)(2,1)}, bf16[512,1536]{1,0:T(8,128)(2,1)}, u32[]{:S(2)}, u32[]{:S(2)}) collective-permute-start(bf16[512,1536]{1,0:T(8,128)(2,1)} %bitcast.6.refs_1_.other_ref), channel_id=1, source_target_pairs={{0,28},{1,29},{2,30},{3,31}} | collective-permute-start | bytes 4718600 | tf_op jit(solution)/shard_map/ppermute | solution.py:305
  32.9 0.0 collective-permute-done.1
  32.9 0.0 copy-done.11
  32.9 0.0 copy-done.12
  32.9 0.0 copy-start.4
  33.0 1.4 copy-done.4
  34.4 2.9 %backward.4 = (f32[512,1536]{1,0:T(8,128)S(1)}, bf16[512,1536]{1,0:T(8,128)(2,1)S(1)}, f32[1,512]{1,0:T(1,128)S(1)}) custom-call(s32[3]{0:T(128)S(1)} %pad_convert_fusion.pick_ref, bf16[512,1536]{1,0:T(8,128)(2,1)S(1)} %copy-done.4, bf16[512,1536]{1,0:T(8,128)(2,1)} %bitcast.6.refs_1_.other_ref, f32[1,512]{1,0:T(1,128)S(1)} %get-tuple-element.37.refs_2_, ...), custom_call_target="tpu_custom_call" | custom-call | tf_op jit(solution)/shard_map/backward/pallas_call | solution.py:191
  37.3 0.0 copy-start.7
  37.3 1.6 %copy-done.7 = f32[512,1536]{1,0:T(8,128)} copy-done((f32[512,1536]{1,0:T(8,128)}, f32[512,1536]{1,0:T(8,128)S(1)}, u32[]{:S(2)}) %copy-start.7) | copy-done | bytes 3145752
  38.9 1.1 copy-done.9
  40.1 6.0 %psum.22 = f32[1,512]{1,0:T(1,128)S(1)} all-reduce(f32[1,512]{1,0:T(1,128)S(1)} %get-tuple-element.19), channel_id=1, replica_groups=mesh['section'=8,'tensor'=4] {'tensor'}, use_global_device_ids=true, to_apply=%region_1.2 | all-reduce | flops 512 | bytes 4096 | tf_op jit(solution)/shard_map/psum | solution.py:346
  46.1 1.9 %copy-done.8 = f32[512,1536]{1,0:T(8,128)S(1)} copy-done((f32[512,1536]{1,0:T(8,128)S(1)}, f32[512,1536]{1,0:T(8,128)}, u32[]{:S(2)}) %copy-start.8) | copy-done | bytes 3145752
  48.0 1.4 copy-done.10
  49.4 3.7 %finish.2.refs_3_ = bf16[512,1536]{1,0:T(8,128)(2,1)} custom-call(s32[1]{0:T(128)} %bitcast.3.pick_ref, f32[512,1536]{1,0:T(8,128)S(1)} %copy-done.8, bf16[512,1536]{1,0:T(8,128)(2,1)S(1)} %copy-done.10, f32[1,512]{1,0:T(1,128)S(1)} %fusion.7.row_ref, bf16[512,1536]{1,0:T(8,128)(2,1)} %bitcast.6.refs_1_.other_ref), custom_call_target="tpu_custom_call" | custom-call | tf_op jit(solution)/shard_map/finish/pallas_call | solution.py:256
  53.2 1.8 %collective-permute-start.5 = (bf16[512,1536]{1,0:T(8,128)(2,1)}, bf16[512,1536]{1,0:T(8,128)(2,1)}, u32[]{:S(2)}, u32[]{:S(2)}) collective-permute-start(bf16[512,1536]{1,0:T(8,128)(2,1)} %finish.2.refs_3_), channel_id=1, source_target_pairs={{16,12},{17,13},{18,14},{19,15}} | collective-permute-start | bytes 4718600 | tf_op jit(solution)/shard_map/ppermute | solution.py:305
  55.0 0.0 collective-permute-done.refs_1_
  55.0 1.9 %choose.3 = (bf16[512,512]{1,0:T(8,128)(2,1)}, bf16[512,512]{1,0:T(8,128)(2,1)S(1)}) custom-call(s32[1]{0:T(128)S(6)} %copy.16.mode_ref, bf16[1,2,512,1536]{3,2,1,0:T(8,128)(2,1)S(1)} %copy-done.1, bf16[512,1024]{1,0:T(8,128)(2,1)} %collective-permute-done.refs_1_, bf16[1,2,512,1536]{3,2,1,0:T(8,128)(2,1)S(1)} %copy-done.1, bf16[512,1536]{1,0:T(8,128)(2,1)} %finish.2.refs_3_), custom_call_target="tpu_custom_call" | custom-call | tf_op jit(solution)/shard_map/choose/pallas_call | solution.py:226
  56.9 0.8 copy-done.13
  57.7 1.3 collective-permute-start.9
  59.0 16.0 %collective-permute-start.2 = (f32[1,3712]{1,0:T(1,128)S(1)}, f32[1,3712]{1,0:T(1,128)S(1)}, u32[]{:S(2)}, u32[]{:S(2)}) collective-permute-start(f32[1,3712]{1,0:T(1,128)S(1)} %reshape_maximum_fusion), channel_id=1, source_target_pairs={{0,28},{4,0},{8,4},{12,8},{16,12},{20,16},{24,20},{28,24},{1,29},{... | collective-permute-start | bytes 44552 | tf_op jit(solution)/shard_map/ppermute | solution.py:305
  75.0 0.1 fusion.8.pick_ref
  75.1 1.9 %slice.53 = bf16[512,512]{1,0:T(8,128)(2,1)} slice(bf16[512,1536]{1,0:T(8,128)(2,1)} %get-tuple-element.32.refs_0_), slice={[0:512], [1024:1536]} | slice | bytes 1048576 | tf_op jit(solution)/shard_map/slice | solution.py:330
  77.0 18.4 %collective-permute-done.2 = f32[1,3712]{1,0:T(1,128)S(1)} collective-permute-done((f32[1,3712]{1,0:T(1,128)S(1)}, f32[1,3712]{1,0:T(1,128)S(1)}, u32[]{:S(2)}, u32[]{:S(2)}) %collective-permute-start.2) | collective-permute-done | bytes 14880 | tf_op jit(solution)/shard_map/ppermute | solution.py:305
  95.4 1.3 collective-permute-start.8
  96.7 0.5 slice.49
  97.9 0.0 copy-start.14
  97.9 0.0 copy-start.6
  97.9 2.1 %choose.2 = (bf16[512,512]{1,0:T(8,128)(2,1)S(1)}, bf16[512,512]{1,0:T(8,128)(2,1)}) custom-call(s32[1]{0:T(128)S(6)} %copy.16.mode_ref, bf16[1,2,512,1536]{3,2,1,0:T(8,128)(2,1)S(1)} %copy-done.1, bf16[512,1024]{1,0:T(8,128)(2,1)} %collective-permute-done.refs_1_, bf16[1,2,512,1536]{3,2,1,0:T(8,128)(2,1)S(1)} %copy-done.1, bf16[512,1536]{1,0:T(8,128)(2,1)} %finish.2.refs_3_), custom_call_target="tpu_custom_call" | custom-call | tf_op jit(solution)/shard_map/choose/pallas_call | solution.py:226
  100.0 0.0 collective-permute-done.9.refs_0_
  100.0 0.0 copy-done.14
  100.0 1.3 collective-permute-start.7
  101.3 0.0 collective-permute-done.4.refs_1_.refs_2_.refs_3_
  101.3 1.3 collective-permute-start.3
  102.6 0.1 fusion.9.pick_ref
  102.7 0.0 copy-done.6
  102.7 7.4 %forward.1 = bf16[512,1536]{1,0:T(8,128)(2,1)} custom-call(bf16[512,1536]{1,0:T(8,128)(2,1)S(1)} %bitcast.22, f32[1,512]{1,0:T(1,128)S(1)} %get-tuple-element.38.f_ref, f32[1,1536]{1,0:T(1,128)S(1)} %copy-done.11, f32[1,1536]{1,0:T(1,128)S(1)} %copy-done.12, bf16[512,512]{1,0:T(8,128)(2,1)S(1)} %get-tuple-element.20.rest_0_), custom_call_target="tpu_custom_call" | custom-call | tf_op jit(solution)/shard_map/forward/pallas_call | solution.py:97
  110.1 0.0 collective-permute-done.6.refs_4_.refs_5_
  110.1 0.0 collective-permute-done.5.refs_3_.refs_4_.other_ref
  110.1 6.9 %backward.5 = (f32[512,1536]{1,0:T(8,128)S(1)}, bf16[512,1536]{1,0:T(8,128)(2,1)S(1)}, f32[1,512]{1,0:T(1,128)S(1)}) custom-call(s32[3]{0:T(128)S(1)} %fusion.8.pick_ref, bf16[512,512]{1,0:T(8,128)(2,1)} %collective-permute-done.9.refs_0_, bf16[512,1536]{1,0:T(8,128)(2,1)} %collective-permute-done.4.refs_1_.refs_2_.refs_3_, ...), custom_call_target="tpu_custom_call" | custom-call | tf_op jit(solution)/shard_map/backward/pallas_call | solution.py:191
  117.0 0.0 collective-permute-done.8.refs_1_
  117.1 8.9 %collective-permute-done.7.refs_0_ = bf16[512,512]{1,0:T(8,128)(2,1)S(1)} collective-permute-done((bf16[512,512]{1,0:T(8,128)(2,1)S(1)}, bf16[512,512]{1,0:T(8,128)(2,1)S(1)}, u32[]{:S(2)}, u32[]{:S(2)}) %collective-permute-start.7) | collective-permute-done | bytes 524320 | tf_op jit(solution)/shard_map/ppermute | solution.py:305
  125.9 7.0 %backward.6 = (f32[512,1536]{1,0:T(8,128)S(1)}, bf16[512,1536]{1,0:T(8,128)(2,1)S(1)}, f32[1,512]{1,0:T(1,128)S(1)}) custom-call(s32[3]{0:T(128)S(1)} %fusion.9.pick_ref, bf16[512,512]{1,0:T(8,128)(2,1)S(1)} %collective-permute-done.7.refs_0_, bf16[512,512]{1,0:T(8,128)(2,1)} %collective-permute-done.8.refs_1_, ...), custom_call_target="tpu_custom_call", output_to_operand_aliasing={{0}: (10, {}), {1}: (11, {})} | custom-call | tf_op jit(solution)/shard_map/backward/pallas_call | solution.py:191
  132.9 0.0 collective-permute-done.3.refs_0_
  132.9 6.8 %backward.7 = (f32[512,1536]{1,0:T(8,128)S(1)}, bf16[512,1536]{1,0:T(8,128)(2,1)S(1)}, f32[1,512]{1,0:T(1,128)S(1)}) custom-call(s32[3]{0:T(128)S(1)} %fusion.8.pick_ref, bf16[512,512]{1,0:T(8,128)(2,1)S(1)} %collective-permute-done.3.refs_0_, ...), custom_call_target="tpu_custom_call", output_to_operand_aliasing={{0}: (9, {}), {1}: (10, {})} | custom-call | tf_op jit(solution)/shard_map/backward/pallas_call | solution.py:191
  139.7 0.0 copy-start.2
  139.7 1.1 copy-done.2
  140.8 8.3 %psum.23 = f32[1,512]{1,0:T(1,128)S(1)} all-reduce(f32[1,512]{1,0:T(1,128)S(1)} %add_add_fusion), channel_id=1, replica_groups=mesh['section'=8,'tensor'=4] {'tensor'}, use_global_device_ids=true, to_apply=%region_2.3 | all-reduce | flops 512 | bytes 4096 | tf_op jit(solution)/shard_map/psum | solution.py:383
  149.2 0.0 copy-start.3
  149.2 1.4 copy-done.3
  150.6 3.8 %finish.3 = bf16[512,1536]{1,0:T(8,128)(2,1)} custom-call(s32[1]{0:T(128)} %bitcast.10.pick_ref, f32[512,1536]{1,0:T(8,128)S(1)} %get-tuple-element.27.a_ref, bf16[512,1536]{1,0:T(8,128)(2,1)S(1)} %copy-done.3, f32[1,512]{1,0:T(1,128)S(1)} %fusion.6.row_ref, bf16[512,1536]{1,0:T(8,128)(2,1)} %collective-permute-done.5.refs_3_.refs_4_.other_ref), custom_call_target="tpu_custom_call" | custom-call | tf_op jit(solution)/shard_map/finish/pallas_call | solution.py:256
  (17 shorter events, 0.1 us)
Async XLA Ops:
  0.6 1.9 %copy-start = (bf16[1,2,512,1536]{3,2,1,0:T(8,128)(2,1)S(1)}, bf16[1,2,512,1536]{3,2,1,0:T(8,128)(2,1)}, u32[]{:S(2)}) copy-start(bf16[1,2,512,1536]{3,2,1,0:T(8,128)(2,1)} %refs_2_.3) | copy-start | bytes 9437188
  2.5 1.4 copy-start.5
  3.9 12.7 %copy-start.1 = (bf16[1,2,512,1536]{3,2,1,0:T(8,128)(2,1)S(1)}, bf16[1,2,512,1536]{3,2,1,0:T(8,128)(2,1)}, u32[]{:S(2)}) copy-start(bf16[1,2,512,1536]{3,2,1,0:T(8,128)(2,1)} %refs_2_.3) | copy-start | bytes 9437188
  14.0 18.9 %collective-permute-start.1 = (f32[1,512]{1,0:T(1,128)S(1)}, f32[1,512]{1,0:T(1,128)S(1)}, u32[]{:S(2)}, u32[]{:S(2)}) collective-permute-start(f32[1,512]{1,0:T(1,128)S(1)} %slice.48), channel_id=1, source_target_pairs={{0,16},{4,20},{8,24},{12,28},{16,0},{20,4},{24,8},{28,12},{1,17},{... | collective-permute-start | bytes 6152 | tf_op jit(solution)/shard_map/ppermute | solution.py:305
  19.0 35.9 %collective-permute-start = (bf16[512,1024]{1,0:T(8,128)(2,1)}, bf16[512,1024]{1,0:T(8,128)(2,1)}, u32[]{:S(2)}, u32[]{:S(2)}) collective-permute-start(bf16[512,1024]{1,0:T(8,128)(2,1)} %slice.46), channel_id=1, source_target_pairs={{4,20},{8,24},{12,28},{20,4},{24,8},{28,12},{5,21},{9,25},{13,29},... | collective-permute-start | bytes 3145736 | tf_op jit(solution)/shard_map/ppermute | solution.py:305
  20.8 12.2 %copy-start.11 = (f32[1,1536]{1,0:T(1,128)S(1)}, f32[1,1536]{1,0:T(1,128)}, u32[]{:S(2)}) copy-start(f32[1,1536]{1,0:T(1,128)} %gq_ref.1) | copy-start | bytes 18436
  20.8 12.2 %copy-start.12 = (f32[1,1536]{1,0:T(1,128)S(1)}, f32[1,1536]{1,0:T(1,128)}, u32[]{:S(2)}) copy-start(f32[1,1536]{1,0:T(1,128)} %gk_ref.1) | copy-start | bytes 18436
  23.5 77.8 %collective-permute-start.4 = (bf16[512,1536]{1,0:T(8,128)(2,1)}, bf16[512,1536]{1,0:T(8,128)(2,1)}, u32[]{:S(2)}, u32[]{:S(2)}) collective-permute-start(bf16[512,1536]{1,0:T(8,128)(2,1)} %broadcast_select_fusion), channel_id=1, source_target_pairs={{4,0},{8,4},{12,8},{20,16},{24,20},{28,24},{16,28},{0,12},{5,1},{9... | collective-permute-start | bytes 4718600 | tf_op jit(solution)/shard_map/ppermute | solution.py:305
  26.6 83.5 %collective-permute-start.6 = (bf16[512,1536]{1,0:T(8,128)(2,1)}, bf16[512,1536]{1,0:T(8,128)(2,1)}, u32[]{:S(2)}, u32[]{:S(2)}) collective-permute-start(bf16[512,1536]{1,0:T(8,128)(2,1)} %bitcast.6.refs_1_.other_ref), channel_id=1, source_target_pairs={{0,28},{1,29},{2,30},{3,31}} | collective-permute-start | bytes 4718600 | tf_op jit(solution)/shard_map/ppermute | solution.py:305
  32.9 1.4 copy-start.4
  37.3 1.6 %copy-start.7 = (f32[512,1536]{1,0:T(8,128)}, f32[512,1536]{1,0:T(8,128)S(1)}, u32[]{:S(2)}) copy-start(f32[512,1536]{1,0:T(8,128)S(1)} %get-tuple-element.17.a_ref) | copy-start | bytes 9437188
  38.9 1.1 copy-start.9
  46.1 1.9 %copy-start.8 = (f32[512,1536]{1,0:T(8,128)S(1)}, f32[512,1536]{1,0:T(8,128)}, u32[]{:S(2)}) copy-start(f32[512,1536]{1,0:T(8,128)} %copy-done.7) | copy-start | bytes 9437188
  48.0 1.4 copy-start.10
  53.2 57.0 %collective-permute-start.5 = (bf16[512,1536]{1,0:T(8,128)(2,1)}, bf16[512,1536]{1,0:T(8,128)(2,1)}, u32[]{:S(2)}, u32[]{:S(2)}) collective-permute-start(bf16[512,1536]{1,0:T(8,128)(2,1)} %finish.2.refs_3_), channel_id=1, source_target_pairs={{16,12},{17,13},{18,14},{19,15}} | collective-permute-start | bytes 4718600 | tf_op jit(solution)/shard_map/ppermute | solution.py:305
  56.9 0.8 copy-start.13
  57.7 42.3 %collective-permute-start.9 = (bf16[512,512]{1,0:T(8,128)(2,1)}, bf16[512,512]{1,0:T(8,128)(2,1)}, u32[]{:S(2)}, u32[]{:S(2)}) collective-permute-start(bf16[512,512]{1,0:T(8,128)(2,1)} %get-tuple-element.22), channel_id=1, source_target_pairs={{4,0},{8,4},{12,8},{20,16},{24,20},{28,24},{5,1},{9,5},{13,9},{21,... | collective-permute-start | bytes 1572872 | tf_op jit(solution)/shard_map/ppermute | solution.py:305
  59.0 36.4 %collective-permute-start.2 = (f32[1,3712]{1,0:T(1,128)S(1)}, f32[1,3712]{1,0:T(1,128)S(1)}, u32[]{:S(2)}, u32[]{:S(2)}) collective-permute-start(f32[1,3712]{1,0:T(1,128)S(1)} %reshape_maximum_fusion), channel_id=1, source_target_pairs={{0,28},{4,0},{8,4},{12,8},{16,12},{20,16},{24,20},{28,24},{1,29},{... | collective-permute-start | bytes 44552 | tf_op jit(solution)/shard_map/ppermute | solution.py:305
  95.4 21.7 %collective-permute-start.8 = (bf16[512,512]{1,0:T(8,128)(2,1)}, bf16[512,512]{1,0:T(8,128)(2,1)}, u32[]{:S(2)}, u32[]{:S(2)}) collective-permute-start(bf16[512,512]{1,0:T(8,128)(2,1)} %slice.53), channel_id=1, source_target_pairs={{4,0},{8,4},{12,8},{20,16},{24,20},{28,24},{5,1},{9,5},{13,9},{21,... | collective-permute-start | bytes 1572872 | tf_op jit(solution)/shard_map/ppermute | solution.py:305
  97.9 2.1 %copy-start.14 = (bf16[512,512]{1,0:T(8,128)(2,1)S(1)}, bf16[512,512]{1,0:T(8,128)(2,1)}, u32[]{:S(2)}) copy-start(bf16[512,512]{1,0:T(8,128)(2,1)} %copy-done.13) | copy-start | bytes 1572868
  97.9 4.8 %copy-start.6 = (bf16[1,512,1536]{2,1,0:T(8,128)(2,1)S(1)}, bf16[1,512,1536]{2,1,0:T(8,128)(2,1)}, u32[]{:S(2)}) copy-start(bf16[1,512,1536]{2,1,0:T(8,128)(2,1)} %param.6) | copy-start | bytes 4718596
  100.0 25.9 %collective-permute-start.7 = (bf16[512,512]{1,0:T(8,128)(2,1)S(1)}, bf16[512,512]{1,0:T(8,128)(2,1)S(1)}, u32[]{:S(2)}, u32[]{:S(2)}) collective-permute-start(bf16[512,512]{1,0:T(8,128)(2,1)S(1)} %copy-done.14), channel_id=1, source_target_pairs={{20,0},{24,4},{28,8},{4,16},{8,20},{12,24},{21,1},{25,5},{29,9},{5... | collective-permute-start | bytes 1572872 | tf_op jit(solution)/shard_map/ppermute | solution.py:305
  101.3 31.6 %collective-permute-start.3 = (bf16[512,512]{1,0:T(8,128)(2,1)S(1)}, bf16[512,512]{1,0:T(8,128)(2,1)S(1)}, u32[]{:S(2)}, u32[]{:S(2)}) collective-permute-start(bf16[512,512]{1,0:T(8,128)(2,1)S(1)} %get-tuple-element.20.rest_0_), channel_id=1, source_target_pairs={{4,0},{8,4},{12,8},{20,16},{24,20},{28,24},{5,1},{9,5},{13,9},{21,... | collective-permute-start | bytes 1572872 | tf_op jit(solution)/shard_map/ppermute | solution.py:305
  139.7 1.1 copy-start.2
  149.2 1.4 copy-start.3

commit v4 on v3

--- a/solution.py
+++ b/solution.py
@@ -164,7 +164,7 @@
             x = chosen(pick_ref[1], x_refs, here)
             g = chosen(pick_ref[2], g_refs, here)
             wide, d_normed = backward_head(x, g, factor, gq_ref[:, lanes], gk_ref[:, lanes])
-            a_ref[:, lanes] = g.astype(F32) + factor * d_normed
+            a_ref[:, lanes] = g.astype(F32) + jnp.where(pick_ref[3] == 1, 0.0, factor * d_normed)
             x_ref[:, lanes] = x
             product = d_normed * wide
             part = product if part is None else part + product
@@ -209,16 +209,16 @@
 
 
 def choose_kernel(mode_ref, *refs):
-    for m, ref in enumerate(refs[:2]):
+    for m, ref in enumerate(refs[:3]):
 
         @pl.when(mode_ref[0] == m)
         def _():
             refs[-2][...] = ref[...]
 
-    refs[-1][...] = refs[2][...]
-
-
-def choose(mode, stash, fetched, start, step, coming, after=()):
+    refs[-1][...] = refs[3][...]
+
+
+def choose(mode, stash, fetched, slot, start, step, coming, after=()):
     tokens = fetched.shape[0]
     block = (tokens, step)
     whole = lambda at: pl.BlockSpec(block, lambda i, mode: (0, at))
@@ -229,13 +229,13 @@
         grid_spec=pltpu.PrefetchScalarGridSpec(
             num_scalar_prefetch=1,
             grid=(1,),
-            in_specs=[of_stash(0, start), whole(start), of_stash(1, coming)]
+            in_specs=[of_stash(0, start), whole(start), whole(start), of_stash(1, coming)]
             + [pl.BlockSpec(memory_space=pl.ANY)] * len(after),
             out_specs=[whole(0)] * 2,
         ),
         compiler_params=pltpu.CompilerParams(vmem_limit_bytes=VMEM),
         name="choose",
-    )(mode, stash, fetched, stash, *after)
+    )(mode, stash, fetched, slot, stash, *after)
 
 
 def finish_kernel(pick_ref, a_ref, x_ref, row_ref, other_ref, o_ref):
@@ -313,10 +313,10 @@
     evicted = eviction[0] == 1
     word = lambda *flags: jnp.stack([jnp.asarray(f).astype(jnp.int32) for f in flags])
 
-    prior = [(s, (s - 1) % n) for s in range(n)]
     inside = [(s, s - 1) for s in range(n) if s not in special]
     partner = [(s, (s + half) % n) for s in range(n)]
     to_partner = [p for p in partner if p[0] not in special]
+    prior = [(s, (s - 1) % n) for s in range(n)]
     within = inside + [(half, n - 1), (0, half - 1)]
     direct = [((s + half) % n, s - 1) for s in range(n) if s not in special]
 
@@ -332,8 +332,6 @@
     is_special = jnp.logical_or(me == 0, me == half)
     fetched = send(held[:, : 2 * step], to_partner)
     early = send(jnp.where(is_special, held, upstream), within)
-    kept = send(piece(own, 2), inside)
-    upward = send(upstream, [(0, n - 1)])
 
     totals = lax.psum(squares(current, stashed, step), "tensor")
     factor_of = lambda total: lax.rsqrt(total / width_all + EPSILON)
@@ -341,48 +339,53 @@
     kept_here = jnp.logical_and(me == half, jnp.logical_not(evicted))
     own_factor = factor_of(totals[1:2])
     own_a, own_x, own_inner = backward(
-        word(kept_here, 0, 0), [(own, 0)], [(upstream, 0)], own_factor, query_gain, key_gain, heads, 3, 0,
+        word(kept_here, 0, 0, 0), [(own, 0)], [(upstream, 0)], own_factor, query_gain, key_gain, heads, 3, 0,
     )
     own_inner = lax.psum(own_inner, "tensor")
     slot = finish(
         word(jnp.logical_not(kept_here)), own_a, own_x, own_factor**3 * own_inner / width_all, upstream, step
     )
-    downward = send(slot, [(half, half - 1)])
-
-    fetched_total = send(totals[2:3], partner)
-    chosen_total = jnp.where(evicted, fetched_total, totals[1:2])
+    kept = send(jnp.where(is_special, piece(slot, 2), piece(own, 2)), prior)
+
     flag = jnp.broadcast_to(eviction[0].astype(F32), (1, HDIM))
-    told = send(jnp.concatenate([chosen_total, query_gain, key_gain, flag], axis=1), prior)
-    factor = factor_of(told[:, :tokens])
-    gain_q = told[:, tokens : tokens + width]
-    gain_k = told[:, tokens + width : tokens + 2 * width]
-    after_evicted = told[0, tokens + 2 * width] == 1.0
-
-    mode = eviction
-    sent, last = choose(mode, stashed, fetched, 0, step, 2, (slot,))
-    passed = [send(sent, inside)]
+    facts = lax.all_gather(
+        jnp.concatenate([totals[1:2], totals[2:3], query_gain, key_gain, flag], axis=1), "section", axis=0, tiled=True
+    )
+    mode = jnp.where(is_special, 2, eviction)
+    sent, last = choose(mode, stashed, fetched, slot, 0, step, 2)
     straight = send(last, direct)
-    sent, _ = choose(mode, stashed, fetched, 1, step, 2, (slot,))
-    passed.append(send(sent, inside))
+    passed = [send(sent, prior)]
+    sent, _ = choose(mode, stashed, fetched, slot, 1, step, 2)
+    passed.append(send(sent, prior))
 
     output = forward(current, factor_of(totals[0:1]), query_gain, key_gain, heads, (sent,))
 
+    facts, _ = lax.optimization_barrier((facts, sent))
+    told = lax.dynamic_slice_in_dim(facts, lax.rem(me + 1, n), 1, axis=0)
+    held_total = lax.dynamic_slice_in_dim(facts, lax.rem(me + 1 + half, n), 1, axis=0)[:, tokens : 2 * tokens]
+    gain_q = told[:, 2 * tokens : 2 * tokens + width]
+    gain_k = told[:, 2 * tokens + width : 2 * tokens + 2 * width]
+    after_evicted = told[0, 2 * tokens + 2 * width] == 1.0
+    factor = factor_of(jnp.where(after_evicted, held_total, told[:, :tokens]))
+
     crossed = jnp.logical_or(me == half - 1, me == n - 1)
-    which_g = jnp.where(me == half - 1, 1, jnp.where(me == n - 1, 2, 0))
-    take = word(1, jnp.where(crossed, 1, 0), which_g)
-    take_last = word(1, jnp.where(crossed, 2, jnp.where(after_evicted, 0, 1)), which_g)
-    gs = lambda c: [(early, c), (downward, c), (upward, c)]
-    a, x, inner = backward(take, [(passed[0], 0), (early, 0)], gs(0), factor, gain_q, gain_k, heads, 1, 0)
+    done = jnp.logical_and(me == half - 1, jnp.logical_not(after_evicted))
+    take = word(1, crossed, crossed, done)
+    take_last = word(1, jnp.where(crossed, 2, jnp.where(after_evicted, 0, 1)), crossed, done)
+    a, x, inner = backward(
+        take, [(passed[0], 0), (early, 0)], [(early, 0), (passed[0], 0)], factor, gain_q, gain_k, heads, 1, 0
+    )
     a, x, part = backward(
-        take_last, [(straight, 0), (kept, 0), (early, 2)], gs(2), factor, gain_q, gain_k, heads, 1, 2, (a, x)
+        take_last, [(straight, 0), (kept, 0), (early, 2)], [(early, 2), (kept, 0)],
+        factor, gain_q, gain_k, heads, 1, 2, (a, x),
     )
     inner = inner + part
     a, x, part = backward(
-        take, [(passed[1], 0), (early, 1)], gs(1), factor, gain_q, gain_k, heads, 1, 1, (a, x)
+        take, [(passed[1], 0), (early, 1)], [(early, 1), (passed[1], 0)], factor, gain_q, gain_k, heads, 1, 1, (a, x)
     )
     inner = lax.psum(inner + part, "tensor")
-    done = word(jnp.logical_and(me == half - 1, jnp.logical_not(after_evicted)))
-    result = finish(done, a, x, factor**3 * inner / width_all, downward, step)
+    row = jnp.where(done, 0.0, factor**3 * inner / width_all)
+    result = finish(word(0), a, x, row, early, step)
     return (output[None], result[None])
 
 

time: 156 us -> 175 us (1.12)
  blocking collectives: 22.9 us -> 73 us
  starting transfers between devices: 36 us -> 14.8 us
  waiting for transfers between devices: 27.3 us -> 13.2 us
  local copies, waits for them, and re-layouts: 18.9 us -> 26.1 us
  Pallas kernels: 44.1 us -> 39.4 us
  other arithmetic: 2.98 us -> 5.11 us
    all_gather x0 -> x1, blocking collectives: none -> 54.7 us  [local(): lax.all_gather(jnp.concatenate([totals[1:2], totals[2:3], query_gain, key...]
    ppermute x10 -> x6, starting transfers between devices: 36 us -> 14.8 us  [send(): return lax.ppermute(x, 'section', pairs)]
    ppermute x10 -> x6, waiting for transfers between devices: 27.3 us -> 13.2 us  [send(): return lax.ppermute(x, 'section', pairs)]
    unnamed x30 -> x46, local copies, waits for them, and re-layouts: 14.1 us -> 20.9 us
    psum x1, blocking collectives: 8.35 us -> 5.64 us  [local(): inner = lax.psum(inner + part, 'tensor')]
    pallas_call x2, Pallas kernels: 7.56 us -> 4.91 us  [finish(): pl.pallas_call(finish_kernel, out_shape=jax.ShapeDtypeStruct(a.shape, BF1...]
    pallas_call x4, Pallas kernels: 23.6 us -> 21.3 us  [backward(): pl.pallas_call(functools.partial(backward_kernel, heads, len(xs), len(gs)...]
    squeeze x1, local copies, waits for them, and re-layouts: 1.35 us -> 3.38 us  [local(): own, held = (stashed[0, 0], stashed[0, 1])]
  transfers between devices with their start and end apart: 10 -> 6, of which waited for: 2 -> 1; matrix products, arithmetic and copies ran while one was open for 5% -> 3% of each run, Pallas kernels for 21% -> 17%
where the time goes in v4:
time: 175 us; the launch traced here: 174 us
  blocking collectives  73 us (42%)
  Pallas kernels  39.4 us (23%)
  local copies, waits for them, and re-layouts  26.1 us (15%)
  starting transfers between devices  14.8 us (8%)
  waiting for transfers between devices  13.2 us (8%)
  other arithmetic  5.11 us (3%)
  between operations  2.22 us (1%)
    all_gather x1, blocking collectives, local(): lax.all_gather(jnp.concatenate([totals[1:2], totals[2:3], query_gain, key...  54.7 us
    pallas_call x4, Pallas kernels, backward(): pl.pallas_call(functools.partial(backward_kernel, heads, len(xs), len(gs)...  21.3 us
    unnamed x46, local copies, waits for them, and re-layouts  20.9 us
    ppermute x6, starting transfers between devices, send(): return lax.ppermute(x, 'section', pairs)  14.8 us
    ppermute x6, waiting for transfers between devices, send(): return lax.ppermute(x, 'section', pairs)  13.2 us
    pallas_call x1, Pallas kernels, forward(): pl.pallas_call(functools.partial(forward_kernel, heads), out_shape=jax.Sh...  7.46 us
    psum x1, blocking collectives, local(): totals = lax.psum(squares(current, stashed, step), 'tensor')  6.53 us
    psum x1, blocking collectives, local(): own_inner = lax.psum(own_inner, 'tensor')  6.19 us
  transfers between devices with their start and end apart: 6, of which 1 were waited for; matrix products, arithmetic and copies ran while one was open for 3% of the time, Pallas kernels for 17%

profile of v4, /device:TPU:0, one launch (start us, length us, event | category | flops | bytes accessed | tf_op | source)
XLA Modules:
  0.0 173.9 jit_solution(10146600274261803626)
XLA Ops:
  0.6 0.0 copy-start
  0.6 3.4 %slice_bitcast_fusion = (bf16[512,1536]{1,0:T(8,128)(2,1)}, bf16[512,1536]{1,0:T(8,128)(2,1)S(1)}) fusion(bf16[1,2,512,1536]{3,2,1,0:T(8,128)(2,1)} %refs_3_.5), kind=kLoop, calls=%fused_computation | loop fusion | bytes 6291456 | tf_op jit(solution)/shard_map/squeeze | solution.py:329
  4.0 1.2 slice.54
  5.2 1.6 collective-permute-start
  6.8 0.0 copy-done
  6.8 2.8 %broadcast_select_fusion = bf16[512,1536]{1,0:T(8,128)(2,1)} fusion(pred[]{:T(512)} %or.6, bf16[1,512,1536]{2,1,0:T(8,128)(2,1)} %param.7, bf16[1,2,512,1536]{3,2,1,0:T(8,128)(2,1)S(1)} %copy-done), kind=kLoop, calls=%fused_computation.2 | loop fusion | flops 786432 | bytes 4718593 | tf_op jit(solution)/shard_map/jit(_where)/select_n | solution.py:334
  9.6 6.9 %collective-permute-start.2 = (bf16[512,1536]{1,0:T(8,128)(2,1)}, bf16[512,1536]{1,0:T(8,128)(2,1)}, u32[]{:S(2)}, u32[]{:S(2)}) collective-permute-start(bf16[512,1536]{1,0:T(8,128)(2,1)} %broadcast_select_fusion), channel_id=1, source_target_pairs={{4,0},{8,4},{12,8},{20,16},{24,20},{28,24},{16,28},{0,12},{5,1},{9... | collective-permute-start | bytes 4718600 | tf_op jit(solution)/shard_map/ppermute | solution.py:305
  17.2 0.0 copy-start.9
  17.2 1.4 copy-done.9
  18.6 1.5 squares.1
  20.1 6.5 %psum.21 = f32[3,512]{1,0:T(4,128)S(1)} all-reduce(f32[3,512]{1,0:T(4,128)S(1)} %squares.1), channel_id=1, replica_groups=mesh['section'=8,'tensor'=4] {'tensor'}, use_global_device_ids=true, to_apply=%region_0.1 | all-reduce | flops 1536 | bytes 12288 | tf_op jit(solution)/shard_map/psum | solution.py:336
  26.7 0.1 pad_add_fusion.2.pick_ref
  26.7 0.0 copy-done.19
  26.8 0.0 copy-done.20
  26.8 1.4 copy-done.4
  28.2 1.4 copy-done.8
  29.6 1.2 backward.4
  30.8 0.0 copy-start.11
  30.8 1.6 copy-done.11
  32.4 1.1 copy-done.15
  33.5 6.2 %psum.22 = f32[1,512]{1,0:T(1,128)S(1)} all-reduce(f32[1,512]{1,0:T(1,128)S(1)} %get-tuple-element.20), channel_id=1, replica_groups=mesh['section'=8,'tensor'=4] {'tensor'}, use_global_device_ids=true, to_apply=%region_1.2 | all-reduce | flops 512 | bytes 4096 | tf_op jit(solution)/shard_map/psum | solution.py:344
  39.8 1.4 copy-done.5
  41.2 1.9 %copy-done.12 = f32[512,1536]{1,0:T(8,128)S(1)} copy-done((f32[512,1536]{1,0:T(8,128)S(1)}, f32[512,1536]{1,0:T(8,128)}, u32[]{:S(2)}) %copy-start.12) | copy-done | bytes 3145752
  43.0 1.4 copy-done.16
  44.5 1.1 finish.2.refs_2_
  45.5 1.9 %slice_select_fusion = bf16[512,512]{1,0:T(8,128)(2,1)} fusion(bf16[512,1536]{1,0:T(8,128)(2,1)} %get-tuple-element.34.refs_0_, bf16[512,1536]{1,0:T(8,128)(2,1)S(1)} %finish.2.refs_2_, pred[]{:T(512)} %or.6), kind=kLoop, calls=%fused_computation.3 | loop fusion | flops 262144 | bytes 1572865 | tf_op jit(solution)/shard_map/jit(_where)/select_n | solution.py:348
  47.4 1.1 copy-done.1
  48.6 0.0 collective-permute-start.4
  48.6 54.7 %all-gather = f32[8,1,4224]{2,1,0:T(1,128)S(1)} all-gather(f32[1,1,4224]{2,1,0:T(1,128)S(1)} %bitcast.34), channel_id=1, replica_groups=mesh['section'=8,'tensor'=4] {'section'}, dimensions={0}, use_global_device_ids=true | all-gather | bytes 152064 | tf_op jit(solution)/shard_map/all_gather | solution.py:351
  103.3 0.0 collective-permute-done.refs_1_
  103.3 0.0 copy-start.2
  103.3 1.4 copy-done.2
  104.7 1.9 %choose.2 = (bf16[512,512]{1,0:T(8,128)(2,1)S(1)}, bf16[512,512]{1,0:T(8,128)(2,1)}) custom-call(s32[1]{0:T(128)S(6)} %select_n.55.mode_ref, bf16[1,2,512,1536]{3,2,1,0:T(8,128)(2,1)S(1)} %copy-done, bf16[512,1024]{1,0:T(8,128)(2,1)} %collective-permute-done.refs_1_, bf16[512,1536]{1,0:T(8,128)(2,1)S(1)} %copy-done.2, bf16[1,2,512,1536]{3,2,1,0:T(8,128)(2,1)S(1)} %copy-done), custom_call_target="tpu_custom_call" | custom-call | tf_op jit(solution)/shard_map/choose/pallas_call | solution.py:226
  106.7 0.8 copy-done.17
  107.5 0.6 dynamic-slice
  108.7 5.0 %collective-permute-start.1 = (bf16[512,512]{1,0:T(8,128)(2,1)}, bf16[512,512]{1,0:T(8,128)(2,1)}, u32[]{:S(2)}, u32[]{:S(2)}) collective-permute-start(bf16[512,512]{1,0:T(8,128)(2,1)} %copy-done.17), channel_id=1, source_target_pairs={{0,28},{4,0},{8,4},{12,8},{16,12},{20,16},{24,20},{28,24},{1,29},{... | collective-permute-start | bytes 1572872 | tf_op jit(solution)/shard_map/ppermute | solution.py:305
  113.8 1.4 copy-done.3
  115.2 2.2 %choose.3 = (bf16[512,512]{1,0:T(8,128)(2,1)}, bf16[512,512]{1,0:T(8,128)(2,1)}) custom-call(s32[1]{0:T(128)S(6)} %select_n.55.mode_ref, bf16[1,2,512,1536]{3,2,1,0:T(8,128)(2,1)S(1)} %copy-done, bf16[512,1024]{1,0:T(8,128)(2,1)} %collective-permute-done.refs_1_, bf16[512,1536]{1,0:T(8,128)(2,1)S(1)} %copy-done.3, bf16[1,2,512,1536]{3,2,1,0:T(8,128)(2,1)S(1)} %copy-done), custom_call_target="tpu_custom_call" | custom-call | tf_op jit(solution)/shard_map/choose/pallas_call | solution.py:226
  117.4 0.0 collective-permute-start.5
  117.4 1.3 collective-permute-start.3
  118.7 0.0 copy-done.10
  118.7 0.0 copy-done.18
  118.7 7.5 %forward.1 = bf16[512,1536]{1,0:T(8,128)(2,1)} custom-call(bf16[512,1536]{1,0:T(8,128)(2,1)S(1)} %bitcast.27, f32[1,512]{1,0:T(1,128)S(1)} %get-tuple-element.40.f_ref, f32[1,1536]{1,0:T(1,128)S(1)} %copy-done.19, f32[1,1536]{1,0:T(1,128)S(1)} %copy-done.20, bf16[512,512]{1,0:T(8,128)(2,1)S(1)} %copy-done.18), custom_call_target="tpu_custom_call" | custom-call | tf_op jit(solution)/shard_map/forward/pallas_call | solution.py:97
  126.2 0.1 fusion.9.pick_ref
  126.3 0.1 fusion.11.pick_ref
  126.3 0.1 fusion.7.refs_4_.refs_5_
  126.4 0.1 fusion.12
  126.5 13.2 %collective-permute-done.5.refs_0_.refs_3_ = bf16[512,512]{1,0:T(8,128)(2,1)S(1)} collective-permute-done((bf16[512,512]{1,0:T(8,128)(2,1)}, bf16[512,512]{1,0:T(8,128)(2,1)S(1)}, u32[]{:S(2)}, u32[]{:S(2)}) %collective-permute-start.5) | collective-permute-done | bytes 524320 | tf_op jit(solution)/shard_map/ppermute | solution.py:305
  139.7 0.8 copy-done.13
  140.5 0.0 collective-permute-done.2.refs_1_.refs_2_.refs_3_.other_ref
  140.5 1.0 copy-done.14
  141.6 6.5 %backward.5 = (f32[512,1536]{1,0:T(8,128)S(1)}, bf16[512,1536]{1,0:T(8,128)(2,1)S(1)}, f32[1,512]{1,0:T(1,128)S(1)}) custom-call(s32[4]{0:T(128)S(1)} %fusion.9.pick_ref, bf16[512,512]{1,0:T(8,128)(2,1)S(1)} %copy-done.14, bf16[512,1536]{1,0:T(8,128)(2,1)} %collective-permute-done.2.refs_1_.refs_2_.refs_3_.other_ref, ...), custom_call_target="tpu_custom_call" | custom-call | tf_op jit(solution)/shard_map/backward/pallas_call | solution.py:191
  148.1 0.0 collective-permute-done.4.refs_1_.refs_4_
  148.1 0.0 collective-permute-done.3.refs_0_
  148.1 6.9 %backward.6 = (f32[512,1536]{1,0:T(8,128)S(1)}, bf16[512,1536]{1,0:T(8,128)(2,1)S(1)}, f32[1,512]{1,0:T(1,128)S(1)}) custom-call(s32[4]{0:T(128)S(1)} %fusion.11.pick_ref, bf16[512,512]{1,0:T(8,128)(2,1)} %collective-permute-done.3.refs_0_, bf16[512,512]{1,0:T(8,128)(2,1)} %collective-permute-done.4.refs_1_.refs_4_, ...), custom_call_target="tpu_custom_call", output_to_operand_aliasing={{0}: (9, {}), {1}: (10, {})} | custom-call | tf_op jit(solution)/shard_map/backward/pallas_call | solution.py:191
  155.0 0.0 collective-permute-done.1.refs_0_.refs_3_
  155.0 6.7 %backward.7 = (f32[512,1536]{1,0:T(8,128)S(1)}, bf16[512,1536]{1,0:T(8,128)(2,1)S(1)}, f32[1,512]{1,0:T(1,128)S(1)}) custom-call(s32[4]{0:T(128)S(1)} %fusion.9.pick_ref, bf16[512,512]{1,0:T(8,128)(2,1)} %collective-permute-done.1.refs_0_.refs_3_, ...), custom_call_target="tpu_custom_call", output_to_operand_aliasing={{0}: (8, {}), {1}: (9, {})} | custom-call | tf_op jit(solution)/shard_map/backward/pallas_call | solution.py:191
  161.8 0.0 copy-start.6
  161.8 1.1 copy-done.6
  162.9 5.6 %psum.23 = f32[1,512]{1,0:T(1,128)S(1)} all-reduce(f32[1,512]{1,0:T(1,128)S(1)} %add_add_fusion), channel_id=1, replica_groups=mesh['section'=8,'tensor'=4] {'tensor'}, use_global_device_ids=true, to_apply=%region_2.3 | all-reduce | flops 512 | bytes 4096 | tf_op jit(solution)/shard_map/psum | solution.py:386
  168.6 0.1 broadcast_select_fusion.1.row_ref
  168.7 0.0 copy-start.7
  168.7 1.4 copy-done.7
  170.1 3.8 %finish.3 = bf16[512,1536]{1,0:T(8,128)(2,1)} custom-call(s32[1]{0:T(128)} %constant.39.clone.1.pick_ref, f32[512,1536]{1,0:T(8,128)S(1)} %get-tuple-element.29.a_ref, bf16[512,1536]{1,0:T(8,128)(2,1)S(1)} %copy-done.7, f32[1,512]{1,0:T(1,128)S(1)} %broadcast_select_fusion.1.row_ref, bf16[512,1536]{1,0:T(8,128)(2,1)} %collective-permute-done.2.refs_1_.refs_2_.refs_3_.other_ref), custom_call_target="tpu_custom_call" | custom-call | tf_op jit(solution)/shard_map/finish/pallas_call | solution.py:256
  (24 shorter events, 0.1 us)
Async XLA Ops:
  0.6 6.2 %copy-start = (bf16[1,2,512,1536]{3,2,1,0:T(8,128)(2,1)S(1)}, bf16[1,2,512,1536]{3,2,1,0:T(8,128)(2,1)}, u32[]{:S(2)}) copy-start(bf16[1,2,512,1536]{3,2,1,0:T(8,128)(2,1)} %refs_3_.5) | copy-start | bytes 9437188
  5.2 98.1 %collective-permute-start = (bf16[512,1024]{1,0:T(8,128)(2,1)}, bf16[512,1024]{1,0:T(8,128)(2,1)}, u32[]{:S(2)}, u32[]{:S(2)}) collective-permute-start(bf16[512,1024]{1,0:T(8,128)(2,1)} %slice.54), channel_id=1, source_target_pairs={{4,20},{8,24},{12,28},{20,4},{24,8},{28,12},{5,21},{9,25},{13,29},... | collective-permute-start | bytes 3145736 | tf_op jit(solution)/shard_map/ppermute | solution.py:305
  9.6 130.9 %collective-permute-start.2 = (bf16[512,1536]{1,0:T(8,128)(2,1)}, bf16[512,1536]{1,0:T(8,128)(2,1)}, u32[]{:S(2)}, u32[]{:S(2)}) collective-permute-start(bf16[512,1536]{1,0:T(8,128)(2,1)} %broadcast_select_fusion), channel_id=1, source_target_pairs={{4,0},{8,4},{12,8},{20,16},{24,20},{28,24},{16,28},{0,12},{5,1},{9... | collective-permute-start | bytes 4718600 | tf_op jit(solution)/shard_map/ppermute | solution.py:305
  17.2 1.4 copy-start.9
  18.6 8.2 %copy-start.19 = (f32[1,1536]{1,0:T(1,128)S(1)}, f32[1,1536]{1,0:T(1,128)}, u32[]{:S(2)}) copy-start(f32[1,1536]{1,0:T(1,128)} %gq_ref.1) | copy-start | bytes 18436
  18.6 8.2 %copy-start.20 = (f32[1,1536]{1,0:T(1,128)S(1)}, f32[1,1536]{1,0:T(1,128)}, u32[]{:S(2)}) copy-start(f32[1,1536]{1,0:T(1,128)} %gk_ref.1) | copy-start | bytes 18436
  26.8 1.4 copy-start.4
  28.2 1.4 copy-start.8
  30.8 1.6 copy-start.11
  32.4 1.1 copy-start.15
  39.7 1.4 copy-start.5
  41.2 1.9 %copy-start.12 = (f32[512,1536]{1,0:T(8,128)S(1)}, f32[512,1536]{1,0:T(8,128)}, u32[]{:S(2)}) copy-start(f32[512,1536]{1,0:T(8,128)} %copy-done.11) | copy-start | bytes 9437188
  43.0 1.4 copy-start.16
  47.4 1.1 copy-start.1
  48.6 99.5 %collective-permute-start.4 = (bf16[512,512]{1,0:T(8,128)(2,1)}, bf16[512,512]{1,0:T(8,128)(2,1)}, u32[]{:S(2)}, u32[]{:S(2)}) collective-permute-start(bf16[512,512]{1,0:T(8,128)(2,1)} %slice_select_fusion), channel_id=1, source_target_pairs={{0,28},{4,0},{8,4},{12,8},{16,12},{20,16},{24,20},{28,24},{1,29},{... | collective-permute-start | bytes 1572872 | tf_op jit(solution)/shard_map/ppermute | solution.py:305
  103.3 1.4 copy-start.2
  106.7 0.8 copy-start.17
  108.7 46.3 %collective-permute-start.1 = (bf16[512,512]{1,0:T(8,128)(2,1)}, bf16[512,512]{1,0:T(8,128)(2,1)}, u32[]{:S(2)}, u32[]{:S(2)}) collective-permute-start(bf16[512,512]{1,0:T(8,128)(2,1)} %copy-done.17), channel_id=1, source_target_pairs={{0,28},{4,0},{8,4},{12,8},{16,12},{20,16},{24,20},{28,24},{1,29},{... | collective-permute-start | bytes 1572872 | tf_op jit(solution)/shard_map/ppermute | solution.py:305
  113.7 1.4 copy-start.3
  115.2 3.6 %copy-start.10 = (bf16[1,512,1536]{2,1,0:T(8,128)(2,1)S(1)}, bf16[1,512,1536]{2,1,0:T(8,128)(2,1)}, u32[]{:S(2)}) copy-start(bf16[1,512,1536]{2,1,0:T(8,128)(2,1)} %param.6) | copy-start | bytes 4718596
  115.2 3.6 %copy-start.18 = (bf16[512,512]{1,0:T(8,128)(2,1)S(1)}, bf16[512,512]{1,0:T(8,128)(2,1)}, u32[]{:S(2)}) copy-start(bf16[512,512]{1,0:T(8,128)(2,1)} %copy-done.17) | copy-start | bytes 1572868
  117.4 22.3 %collective-permute-start.5 = (bf16[512,512]{1,0:T(8,128)(2,1)}, bf16[512,512]{1,0:T(8,128)(2,1)S(1)}, u32[]{:S(2)}, u32[]{:S(2)}) collective-permute-start(bf16[512,512]{1,0:T(8,128)(2,1)} %get-tuple-element.24), channel_id=1, source_target_pairs={{0,28},{4,0},{8,4},{12,8},{16,12},{20,16},{24,20},{28,24},{1,29},{... | collective-permute-start | bytes 1572872 | tf_op jit(solution)/shard_map/ppermute | solution.py:305
  117.4 30.7 %collective-permute-start.3 = (bf16[512,512]{1,0:T(8,128)(2,1)}, bf16[512,512]{1,0:T(8,128)(2,1)}, u32[]{:S(2)}, u32[]{:S(2)}) collective-permute-start(bf16[512,512]{1,0:T(8,128)(2,1)} %get-tuple-element.23), channel_id=1, source_target_pairs={{20,0},{24,4},{28,8},{4,16},{8,20},{12,24},{21,1},{25,5},{29,9},{5... | collective-permute-start | bytes 1572872 | tf_op jit(solution)/shard_map/ppermute | solution.py:305
  139.7 0.8 copy-start.13
  140.5 1.0 copy-start.14
  161.8 1.1 copy-start.6
  168.7 1.4 copy-start.7

commit v5 on v4

--- a/solution.py
+++ b/solution.py
@@ -13,6 +13,7 @@
 SCALE = 1.0 / math.sqrt(HDIM)
 LOG2E = math.log2(math.e)
 VMEM = 32 * 1024 * 1024
+MOST = 60 * 1024 * 1024
 
 F32 = jnp.float32
 BF16 = jnp.bfloat16
@@ -137,75 +138,101 @@
     return wide, d_normed
 
 
-def chosen(index, refs, at):
-    value = refs[0][at]
-    for i, ref in enumerate(refs[1:]):
-        value = jnp.where(index == i + 1, ref[at], value)
+def selected(which, refs, at):
+    values = [ref[lanes_of(start + at, HDIM)] for ref, start in refs]
+    value = values[0]
+    for i, other in enumerate(values[1:]):
+        value = jnp.where(which == i + 1, other, value)
     return value
 
 
-def backward_kernel(heads, n_x, n_g, pick_ref, *refs):
-    x_refs, g_refs = refs[:n_x], refs[n_x : n_x + n_g]
-    f_ref, gq_ref, gk_ref = refs[n_x + n_g : n_x + n_g + 3]
+def lanes_of(start, size):
+    return (slice(None), slice(start, start + size))
+
+
+def backward_piece(pick_ref, xs, gs, f_ref, gq_ref, gk_ref, a_ref, x_ref, heads, first):
+    factor = column_of(f_ref[...])
+    part = None
+    for h in range(heads):
+        mine = lanes_of(first + h * HDIM, HDIM)
+        x = selected(pick_ref[1], xs, h * HDIM)
+        g = selected(pick_ref[2], gs, h * HDIM)
+        wide, d_normed = backward_head(x, g, factor, gq_ref[mine], gk_ref[mine])
+        a_ref[mine] = g.astype(F32) + jnp.where(pick_ref[3] == 1, 0.0, factor * d_normed)
+        x_ref[mine] = x
+        product = d_normed * wide
+        part = product if part is None else part + product
+    return jnp.sum(part.T, axis=0, keepdims=True)
+
+
+def backward_kernel(heads, first, x_at, g_at, pick_ref, *refs):
+    n_x, n_g = len(x_at), len(g_at)
+    xs = list(zip(refs[:n_x], x_at))
+    gs = list(zip(refs[n_x : n_x + n_g], g_at))
     a_ref, x_ref, inner_ref = refs[-3:]
-    first = pl.program_id(0) == 0
-
-    @pl.when(jnp.logical_and(first, pick_ref[0] == 0))
-    def _():
-        inner_ref[...] = jnp.zeros_like(inner_ref)
-
-    @pl.when(pick_ref[0] == 1)
-    def _():
-        factor = column_of(f_ref[...])
-        part = None
-        for h in range(heads):
-            lanes = slice(h * HDIM, (h + 1) * HDIM)
-            here = (slice(None), lanes)
-            x = chosen(pick_ref[1], x_refs, here)
-            g = chosen(pick_ref[2], g_refs, here)
-            wide, d_normed = backward_head(x, g, factor, gq_ref[:, lanes], gk_ref[:, lanes])
-            a_ref[:, lanes] = g.astype(F32) + jnp.where(pick_ref[3] == 1, 0.0, factor * d_normed)
-            x_ref[:, lanes] = x
-            product = d_normed * wide
-            part = product if part is None else part + product
-        inner = jnp.sum(part.T, axis=0, keepdims=True)
-
-        @pl.when(first)
-        def _():
-            inner_ref[...] = inner
-
-        @pl.when(jnp.logical_not(first))
-        def _():
-            inner_ref[...] += inner
-
-
-def backward(pick, xs, gs, factor, gain_q, gain_k, heads, steps, first, sofar=(), after=()):
+    inner_ref[...] = backward_piece(pick_ref, xs, gs, *refs[n_x + n_g : n_x + n_g + 3], a_ref, x_ref, heads, first)
+
+
+IN_VMEM = pl.BlockSpec(memory_space=pltpu.VMEM)
+
+
+def backward(pick, xs, gs, factor, gain_q, gain_k, heads, first, sofar=(), after=()):
     tokens = xs[0][0].shape[0]
     width = gain_q.shape[1]
-    lanes = heads * HDIM
-    at = lambda start: pl.BlockSpec((tokens, lanes), lambda i, pick: (0, start + i))
-    gain = pl.BlockSpec((1, lanes), lambda i, pick: (0, first + i))
-    row = pl.BlockSpec((1, tokens), lambda i, pick: (0, 0))
-    extra = tuple(sofar) + tuple(after)
     before = 1 + len(xs) + len(gs) + 3
     return pl.pallas_call(
-        functools.partial(backward_kernel, heads, len(xs), len(gs)),
+        functools.partial(backward_kernel, heads, first, tuple(at for _, at in xs), tuple(at for _, at in gs)),
         out_shape=(
             jax.ShapeDtypeStruct((tokens, width), F32),
             jax.ShapeDtypeStruct((tokens, width), BF16),
             jax.ShapeDtypeStruct((1, tokens), F32),
         ),
-        grid_spec=pltpu.PrefetchScalarGridSpec(
-            num_scalar_prefetch=1,
-            grid=(steps,),
-            in_specs=[at(b) for _, b in (*xs, *gs)] + [row, gain, gain]
-            + [pl.BlockSpec(memory_space=pl.ANY)] * len(extra),
-            out_specs=(at(first), at(first), row),
-        ),
+        in_specs=[pl.BlockSpec(memory_space=pltpu.SMEM)] + [IN_VMEM] * (before - 1 + len(sofar))
+        + [pl.BlockSpec(memory_space=pl.ANY)] * len(after),
+        out_specs=(IN_VMEM, IN_VMEM, IN_VMEM),
         input_output_aliases={before: 0, before + 1: 1} if sofar else {},
         compiler_params=pltpu.CompilerParams(vmem_limit_bytes=VMEM),
         name="backward",
-    )(pick, *[x for x, _ in xs], *[g for g, _ in gs], factor, gain_q, gain_k, *extra)
+    )(pick, *[x for x, _ in xs], *[g for g, _ in gs], factor, gain_q, gain_k, *sofar, *after)
+
+
+def early_kernel(heads, pick_ref, x_ref, g_ref, f_ref, gq_ref, gk_ref, a_ref, inner_ref, x_scratch):
+    first = pl.program_id(0) == 0
+
+    @pl.when(first)
+    def _():
+        inner_ref[...] = jnp.zeros_like(inner_ref)
+
+    @pl.when(pick_ref[0] == 1)
+    def _():
+        inner_ref[...] += backward_piece(
+            pick_ref, [(x_ref, 0)], [(g_ref, 0)], f_ref, gq_ref, gk_ref, a_ref, x_scratch, heads, 0
+        )
+
+
+def early_backward(pick, stash, g, factor, gain_q, gain_k, heads):
+    tokens, width = g.shape
+    lanes = heads * HDIM
+    at = lambda i, pick: (0, i * pick[0])
+    block = pl.BlockSpec((tokens, lanes), at)
+    row = pl.BlockSpec((1, tokens), lambda i, pick: (0, 0))
+    gain = pl.BlockSpec((1, lanes), at)
+    return pl.pallas_call(
+        functools.partial(early_kernel, heads),
+        out_shape=(jax.ShapeDtypeStruct((tokens, width), F32), jax.ShapeDtypeStruct((1, tokens), F32)),
+        grid_spec=pltpu.PrefetchScalarGridSpec(
+            num_scalar_prefetch=1,
+            grid=(width // lanes,),
+            in_specs=[
+                pl.BlockSpec((None, None, tokens, lanes), lambda i, pick: (0, 0, 0, i * pick[0])),
+                block, row, gain, gain,
+            ],
+            out_specs=(block, row),
+            scratch_shapes=[pltpu.VMEM((tokens, lanes), BF16)],
+        ),
+        compiler_params=pltpu.CompilerParams(vmem_limit_bytes=MOST),
+        name="early_backward",
+    )(pick, stash, g, factor, gain_q, gain_k)
 
 
 def choose_kernel(mode_ref, *refs):
@@ -238,36 +265,75 @@
     )(mode, stash, fetched, slot, stash, *after)
 
 
-def finish_kernel(pick_ref, a_ref, x_ref, row_ref, other_ref, o_ref):
+def finish_kernel(lanes, a_ref, x_ref, row_ref, o_ref):
     row = column_of(row_ref[...])
+    at = (slice(None), pl.ds(pl.program_id(0) * lanes, lanes))
+    o_ref[...] = (a_ref[at] - x_ref[at].astype(F32) * row).astype(BF16)
+
+
+def finish(a, x, row, lanes):
+    tokens, width = a.shape
+    return pl.pallas_call(
+        functools.partial(finish_kernel, lanes),
+        out_shape=jax.ShapeDtypeStruct(a.shape, BF16),
+        grid=(width // lanes,),
+        in_specs=[IN_VMEM] * 3,
+        out_specs=pl.BlockSpec((tokens, lanes), lambda i: (0, i)),
+        compiler_params=pltpu.CompilerParams(vmem_limit_bytes=VMEM),
+        name="finish",
+    )(a, x, row)
+
+
+def slot_kernel(pick_ref, a_ref, x_ref, g_ref, row_ref, o_ref):
+    @pl.when(pick_ref[0] == 1)
+    def _():
+        row = column_of(row_ref[...])
+        o_ref[...] = (a_ref[...] - x_ref[...].astype(F32) * row).astype(BF16)
 
     @pl.when(pick_ref[0] == 0)
     def _():
-        o_ref[...] = (a_ref[...] - x_ref[...].astype(F32) * row).astype(BF16)
-
-    @pl.when(pick_ref[0] == 1)
-    def _():
-        o_ref[...] = other_ref[...]
-
-
-def finish(pick, a, x, row, other, lanes):
-    tokens, width = a.shape
+        o_ref[...] = g_ref[...]
+
+
+def kept_kernel(last, pick_ref, a_ref, x_ref, g_ref, row_ref, o_ref, kept_ref):
+    slot_kernel(pick_ref, a_ref, x_ref, g_ref, row_ref, o_ref)
+
+    @pl.when(jnp.logical_and(pl.program_id(0) == last, pick_ref[1] == 1))
+    def _():
+        kept_ref[...] = o_ref[...]
+
+    @pl.when(jnp.logical_and(pl.program_id(0) == last, pick_ref[1] == 0))
+    def _():
+        kept_ref[...] = x_ref[...]
+
+
+def slot_of(pick, a, stash, g, row, lanes):
+    tokens, width = g.shape
+    last = width // lanes - 1
     block = pl.BlockSpec((tokens, lanes), lambda i, pick: (0, i))
     return pl.pallas_call(
-        finish_kernel,
-        out_shape=jax.ShapeDtypeStruct(a.shape, BF16),
+        functools.partial(kept_kernel, last),
+        out_shape=(jax.ShapeDtypeStruct((tokens, width), BF16), jax.ShapeDtypeStruct((tokens, lanes), BF16)),
         grid_spec=pltpu.PrefetchScalarGridSpec(
             num_scalar_prefetch=1,
             grid=(width // lanes,),
-            in_specs=[block, block, pl.BlockSpec((1, tokens), lambda i, pick: (0, 0)), block],
-            out_specs=block,
+            in_specs=[
+                pl.BlockSpec((tokens, lanes), lambda i, pick: (0, i * pick[0])),
+                pl.BlockSpec((None, None, tokens, lanes), lambda i, pick: (0, 0, 0, i)),
+                block,
+                pl.BlockSpec((1, tokens), lambda i, pick: (0, 0)),
+            ],
+            out_specs=(block, pl.BlockSpec((tokens, lanes), lambda i, pick: (0, 0))),
         ),
-        compiler_params=pltpu.CompilerParams(vmem_limit_bytes=VMEM),
-        name="finish",
-    )(pick, a, x, row, other)
-
-
-def squares_kernel(current_ref, stash_ref, o_ref):
+        compiler_params=pltpu.CompilerParams(vmem_limit_bytes=MOST),
+        name="slot",
+    )(pick, a, stash, g, row)
+
+
+def open_kernel(pieces, pick_ref, current_ref, stash_ref, g_ref, gq_ref, gk_ref, rows_ref, told_ref, away_ref, early_ref):
+    step = pl.program_id(0)
+    tokens, lanes = current_ref.shape
+
     def total(x):
         wide = x.astype(F32)
         square = wide * wide
@@ -276,29 +342,69 @@
 
     rows = jnp.concatenate([total(current_ref[...]), total(stash_ref[0]), total(stash_ref[1])], axis=0)
 
-    @pl.when(pl.program_id(0) == 0)
-    def _():
-        o_ref[...] = rows
-
-    @pl.when(pl.program_id(0) > 0)
-    def _():
-        o_ref[...] += rows
-
-
-def squares(current, stash, lanes):
+    @pl.when(step == 0)
+    def _():
+        rows_ref[...] = rows
+
+    @pl.when(step > 0)
+    def _():
+        rows_ref[...] += rows
+
+    @pl.when(step < pieces - 1)
+    def _():
+        away_ref[...] = stash_ref[1]
+
+    @pl.when(pick_ref[0] == 1)
+    def _():
+        early_ref[...] = stash_ref[1]
+
+    @pl.when(pick_ref[0] == 0)
+    def _():
+        early_ref[...] = g_ref[...]
+
+    @pl.when(step == pieces - 1)
+    def _():
+        width = gq_ref.shape[1]
+        told_ref[:, :tokens] = rows_ref[1:2, :]
+        told_ref[:, tokens : tokens + width] = gq_ref[...]
+        told_ref[:, tokens + width : tokens + 2 * width] = gk_ref[...]
+        told_ref[:, tokens + 2 * width :] = jnp.full((1, HDIM), pick_ref[1].astype(F32))
+
+
+def opened(pick, current, stash, g, gain_q, gain_k, lanes):
     tokens, width = current.shape
-    return pl.pallas_call(
-        squares_kernel,
-        out_shape=jax.ShapeDtypeStruct((3, tokens), F32),
-        grid=(width // lanes,),
-        in_specs=[
-            pl.BlockSpec((tokens, lanes), lambda i: (0, i)),
-            pl.BlockSpec((None, 2, tokens, lanes), lambda i: (0, 0, 0, i)),
-        ],
-        out_specs=pl.BlockSpec((3, tokens), lambda i: (0, 0)),
-        compiler_params=pltpu.CompilerParams(vmem_limit_bytes=VMEM),
-        name="squares",
-    )(current, stash)
+    pieces = width // lanes
+    block = pl.BlockSpec((tokens, lanes), lambda i, pick: (0, i))
+    still = lambda *shape: pl.BlockSpec(shape, lambda i, pick: (0, 0))
+    told = tokens + 2 * width + HDIM
+    return pl.pallas_call(
+        functools.partial(open_kernel, pieces),
+        out_shape=(
+            jax.ShapeDtypeStruct((3, tokens), F32),
+            jax.ShapeDtypeStruct((1, told), F32),
+            jax.ShapeDtypeStruct((tokens, width - lanes), BF16),
+            jax.ShapeDtypeStruct((tokens, width), BF16),
+        ),
+        grid_spec=pltpu.PrefetchScalarGridSpec(
+            num_scalar_prefetch=1,
+            grid=(pieces,),
+            in_specs=[
+                block,
+                pl.BlockSpec((None, 2, tokens, lanes), lambda i, pick: (0, 0, 0, i)),
+                block,
+                still(1, width),
+                still(1, width),
+            ],
+            out_specs=(
+                still(3, tokens),
+                still(1, told),
+                pl.BlockSpec((tokens, lanes), lambda i, pick: (0, jnp.minimum(i, pieces - 2))),
+                block,
+            ),
+        ),
+        compiler_params=pltpu.CompilerParams(vmem_limit_bytes=MOST),
+        name="opened",
+    )(pick, current, stash, g, gain_q, gain_k)
 
 
 def send(x, pairs):
@@ -326,31 +432,34 @@
     heads_here = width // HDIM
     step = width // 3
     heads = heads_here // 3
-    own, held = stashed[0, 0], stashed[0, 1]
-    piece = lambda x, c: x[:, c * step : (c + 1) * step]
 
     is_special = jnp.logical_or(me == 0, me == half)
-    fetched = send(held[:, : 2 * step], to_partner)
-    early = send(jnp.where(is_special, held, upstream), within)
-
-    totals = lax.psum(squares(current, stashed, step), "tensor")
-    factor_of = lambda total: lax.rsqrt(total / width_all + EPSILON)
+    rows, told, away, first = opened(
+        word(is_special, evicted), current, stashed, upstream, query_gain, key_gain, step
+    )
+    told = send(told, prior)
+    held_row = send(rows[2:3], [((s + half) % n, (s - 1) % n) for s in range(n)])
+    fetched = send(away, to_partner)
+    early = send(first, within)
+
+    gain_q = told[:, tokens : tokens + width]
+    gain_k = told[:, tokens + width : tokens + 2 * width]
+    after_evicted = told[0, tokens + 2 * width] == 1.0
+    chosen_row = jnp.where(after_evicted, held_row, told[:, :tokens])
+    totals = lax.psum(jnp.concatenate([rows[:2], chosen_row], axis=0), "tensor")
+    factors = lax.rsqrt(totals / width_all + EPSILON)
+    forward_factor, own_factor, factor = factors[0:1], factors[1:2], factors[2:3]
 
     kept_here = jnp.logical_and(me == half, jnp.logical_not(evicted))
-    own_factor = factor_of(totals[1:2])
-    own_a, own_x, own_inner = backward(
-        word(kept_here, 0, 0, 0), [(own, 0)], [(upstream, 0)], own_factor, query_gain, key_gain, heads, 3, 0,
+    own_a, own_inner = early_backward(
+        word(kept_here, 0, 0, 0), stashed, upstream, own_factor, query_gain, key_gain, heads
     )
     own_inner = lax.psum(own_inner, "tensor")
-    slot = finish(
-        word(jnp.logical_not(kept_here)), own_a, own_x, own_factor**3 * own_inner / width_all, upstream, step
-    )
-    kept = send(jnp.where(is_special, piece(slot, 2), piece(own, 2)), prior)
-
-    flag = jnp.broadcast_to(eviction[0].astype(F32), (1, HDIM))
-    facts = lax.all_gather(
-        jnp.concatenate([totals[1:2], totals[2:3], query_gain, key_gain, flag], axis=1), "section", axis=0, tiled=True
-    )
+    slot, last = slot_of(
+        word(kept_here, is_special), own_a, stashed, upstream, own_factor**3 * own_inner / width_all, step
+    )
+    kept = send(last, prior)
+
     mode = jnp.where(is_special, 2, eviction)
     sent, last = choose(mode, stashed, fetched, slot, 0, step, 2)
     straight = send(last, direct)
@@ -358,34 +467,27 @@
     sent, _ = choose(mode, stashed, fetched, slot, 1, step, 2)
     passed.append(send(sent, prior))
 
-    output = forward(current, factor_of(totals[0:1]), query_gain, key_gain, heads, (sent,))
-
-    facts, _ = lax.optimization_barrier((facts, sent))
-    told = lax.dynamic_slice_in_dim(facts, lax.rem(me + 1, n), 1, axis=0)
-    held_total = lax.dynamic_slice_in_dim(facts, lax.rem(me + 1 + half, n), 1, axis=0)[:, tokens : 2 * tokens]
-    gain_q = told[:, 2 * tokens : 2 * tokens + width]
-    gain_k = told[:, 2 * tokens + width : 2 * tokens + 2 * width]
-    after_evicted = told[0, 2 * tokens + 2 * width] == 1.0
-    factor = factor_of(jnp.where(after_evicted, held_total, told[:, :tokens]))
+    output = forward(current, forward_factor, query_gain, key_gain, heads, (sent,))
 
     crossed = jnp.logical_or(me == half - 1, me == n - 1)
     done = jnp.logical_and(me == half - 1, jnp.logical_not(after_evicted))
     take = word(1, crossed, crossed, done)
     take_last = word(1, jnp.where(crossed, 2, jnp.where(after_evicted, 0, 1)), crossed, done)
+    facts = (factor, gain_q, gain_k)
     a, x, inner = backward(
-        take, [(passed[0], 0), (early, 0)], [(early, 0), (passed[0], 0)], factor, gain_q, gain_k, heads, 1, 0
+        take, [(passed[0], 0), (early, 0)], [(early, 0), (passed[0], 0)], *facts, heads, 0,
+        after=(output,),
     )
     a, x, part = backward(
-        take_last, [(straight, 0), (kept, 0), (early, 2)], [(early, 2), (kept, 0)],
-        factor, gain_q, gain_k, heads, 1, 2, (a, x),
+        take_last, [(straight, 0), (kept, 0), (early, 2 * step)], [(early, 2 * step), (kept, 0)], *facts, heads,
+        2 * step, (a, x),
     )
     inner = inner + part
     a, x, part = backward(
-        take, [(passed[1], 0), (early, 1)], [(early, 1), (passed[1], 0)], factor, gain_q, gain_k, heads, 1, 1, (a, x)
+        take, [(passed[1], 0), (early, step)], [(early, step), (passed[1], 0)], *facts, heads, step, (a, x)
     )
     inner = lax.psum(inner + part, "tensor")
-    row = jnp.where(done, 0.0, factor**3 * inner / width_all)
-    result = finish(word(0), a, x, row, early, step)
+    result = finish(a, x, jnp.where(done, 0.0, factor**3 * inner / width_all), step)
     return (output[None], result[None])
 
 

time: 175 us -> 147 us (0.84)
  the two profiles are of different devices: /device:TPU:0 before, /device:TPU:22 now
where the time goes in v5:
time: 147 us; the launch traced here: 146 us
  waiting for transfers between devices  55.9 us (38%)
  Pallas kernels  47.1 us (32%)
  blocking collectives  18.2 us (12%)
  starting transfers between devices  12.4 us (8%)
  local copies, waits for them, and re-layouts  7.88 us (5%)
  other arithmetic  2.63 us (2%)
  between operations  2.13 us (1%)
    ppermute x8, waiting for transfers between devices, send(): return lax.ppermute(x, 'section', pairs)  55.9 us
    pallas_call x3, Pallas kernels, backward(): pl.pallas_call(functools.partial(backward_kernel, heads, first, tuple((at...  19.7 us
    ppermute x8, starting transfers between devices, send(): return lax.ppermute(x, 'section', pairs)  12.4 us
    pallas_call x1, Pallas kernels, forward(): pl.pallas_call(functools.partial(forward_kernel, heads), out_shape=jax.Sh...  7.46 us
    pallas_call x1, Pallas kernels, opened(): pl.pallas_call(functools.partial(open_kernel, pieces), out_shape=(jax.Sha...  6.42 us
    psum x1, blocking collectives, local(): totals = lax.psum(jnp.concatenate([rows[:2], chosen_row], axis=0), 'tensor')  6.2 us
    psum x1, blocking collectives, local(): own_inner = lax.psum(own_inner, 'tensor')  6.08 us
    psum x1, blocking collectives, local(): inner = lax.psum(inner + part, 'tensor')  5.95 us
  transfers between devices with their start and end apart: 8, of which 2 were waited for; matrix products, arithmetic and copies ran while one was open for 3% of the time, Pallas kernels for 22%

profile of v5, /device:TPU:22, one launch (start us, length us, event | category | flops | bytes accessed | tf_op | source)
XLA Modules:
  0.0 146.2 jit_solution(21109834663196448)
XLA Ops:
  1.3 0.6 pad_add_fusion.2.pick_ref
  1.9 6.4 %opened.1 = (f32[3,512]{1,0:T(4,128)}, f32[1,3712]{1,0:T(1,128)}, bf16[512,1024]{1,0:T(8,128)(2,1)}, bf16[512,1536]{1,0:T(8,128)(2,1)}) custom-call(s32[2]{0:T(128)} %pad_add_fusion.2.pick_ref, bf16[512,1536]{1,0:T(8,128)(2,1)} %bitcast.11, bf16[1,2,512,1536]{3,2,1,0:T(8,128)(2,1)} %refs_3_.3, bf16[512,1536]{1,0:T(8,128)(2,1)} %bitcast.14, ...), custom_call_target="tpu_custom_call" | custom-call | tf_op jit(solution)/shard_map/opened/pallas_call | solution.py:380
  8.3 0.7 slice.29
  9.0 0.3 collective-permute-start.1
  9.3 2.8 %collective-permute-start = (f32[1,3712]{1,0:T(1,128)}, f32[1,3712]{1,0:T(1,128)S(1)}, u32[]{:S(2)}, u32[]{:S(2)}) collective-permute-start(f32[1,3712]{1,0:T(1,128)} %get-tuple-element.23), channel_id=1, source_target_pairs={{0,28},{4,0},{8,4},{12,8},{16,12},{20,16},{24,20},{28,24},{1,29},{... | collective-permute-start | bytes 44552 | tf_op jit(solution)/shard_map/ppermute | solution.py:411
  12.0 2.2 %collective-permute-start.2 = (bf16[512,1024]{1,0:T(8,128)(2,1)}, bf16[512,1024]{1,0:T(8,128)(2,1)}, u32[]{:S(2)}, u32[]{:S(2)}) collective-permute-start(bf16[512,1024]{1,0:T(8,128)(2,1)} %get-tuple-element.24), channel_id=1, source_target_pairs={{4,20},{8,24},{12,28},{20,4},{24,8},{28,12},{5,21},{9,25},{13,29},... | collective-permute-start | bytes 3145736 | tf_op jit(solution)/shard_map/ppermute | solution.py:411
  14.3 0.8 collective-permute-start.4
  15.1 0.6 pad_add_fusion.3.pick_ref
  15.7 0.7 pad_add_fusion.4.pick_ref
  16.4 0.7 slice.27
  17.1 0.0 collective-permute-done
  17.1 0.5 slice.36
  18.2 0.0 collective-permute-done.1
  18.3 6.2 %psum.21 = f32[3,512]{1,0:T(4,128)S(1)} all-reduce(f32[3,512]{1,0:T(4,128)S(1)} %pad_maximum_fusion), channel_id=1, replica_groups=mesh['section'=8,'tensor'=4] {'tensor'}, use_global_device_ids=true, to_apply=%region_0.1 | all-reduce | flops 1536 | bytes 12288 | tf_op jit(solution)/shard_map/psum | solution.py:449
  24.5 0.6 slice.39.f_ref
  25.1 2.9 %early_backward.1 = (f32[512,1536]{1,0:T(8,128)}, f32[1,512]{1,0:T(1,128)}) custom-call(s32[4]{0:T(128)} %pad_add_fusion.4.pick_ref, bf16[1,2,512,1536]{3,2,1,0:T(8,128)(2,1)} %refs_3_.3, bf16[512,1536]{1,0:T(8,128)(2,1)} %bitcast.15, f32[1,512]{1,0:T(1,128)} %slice.39.f_ref, f32[1,1536]{1,0:T(1,128)} %gq_ref.5, f32[1,1536]{1,0:T(1,128)} %gk_ref.5), custom_call_target="tpu_custom_call" | custom-call | tf_op jit(solution)/shard_map/early_backward/pallas_call | solution.py:220
  28.0 6.1 %psum.22 = f32[1,512]{1,0:T(1,128)S(1)} all-reduce(f32[1,512]{1,0:T(1,128)} %get-tuple-element.26), channel_id=1, replica_groups=mesh['section'=8,'tensor'=4] {'tensor'}, use_global_device_ids=true, to_apply=%region_1.2 | all-reduce | flops 512 | bytes 4096 | tf_op jit(solution)/shard_map/psum | solution.py:457
  34.1 0.6 fusion.8
  34.7 0.0 copy-start
  34.7 5.2 %slot.1 = (bf16[512,1536]{1,0:T(8,128)(2,1)}, bf16[512,512]{1,0:T(8,128)(2,1)}) custom-call(s32[2]{0:T(128)} %pad_add_fusion.3.pick_ref, f32[512,1536]{1,0:T(8,128)} %get-tuple-element.25.a_ref, bf16[1,2,512,1536]{3,2,1,0:T(8,128)(2,1)} %refs_3_.3, bf16[512,1536]{1,0:T(8,128)(2,1)} %bitcast.16, f32[1,512]{1,0:T(1,128)} %get-tuple-element.45.row_ref), custom_call_target="tpu_custom_call" | custom-call | tf_op jit(solution)/shard_map/slot/pallas_call | solution.py:314
  39.9 2.3 %collective-permute-start.6 = (bf16[512,512]{1,0:T(8,128)(2,1)}, bf16[512,512]{1,0:T(8,128)(2,1)}, u32[]{:S(2)}, u32[]{:S(2)}) collective-permute-start(bf16[512,512]{1,0:T(8,128)(2,1)} %get-tuple-element.31), channel_id=1, source_target_pairs={{0,28},{4,0},{8,4},{12,8},{16,12},{20,16},{24,20},{28,24},{1,29},{... | collective-permute-start | bytes 1572872 | tf_op jit(solution)/shard_map/ppermute | solution.py:411
  42.1 0.1 fusion.4.pick_ref
  42.2 16.7 %collective-permute-done.2.refs_1_ = bf16[512,1024]{1,0:T(8,128)(2,1)} collective-permute-done((bf16[512,1024]{1,0:T(8,128)(2,1)}, bf16[512,1024]{1,0:T(8,128)(2,1)}, u32[]{:S(2)}, u32[]{:S(2)}) %collective-permute-start.2) | collective-permute-done | bytes 1048608 | tf_op jit(solution)/shard_map/ppermute | solution.py:411
  58.9 0.0 copy-done
  58.9 0.0 copy-start.3
  58.9 1.4 copy-done.3
  60.3 1.1 choose.3
  61.5 1.9 %collective-permute-start.5 = (bf16[512,512]{1,0:T(8,128)(2,1)S(1)}, bf16[512,512]{1,0:T(8,128)(2,1)S(1)}, u32[]{:S(2)}, u32[]{:S(2)}) collective-permute-start(bf16[512,512]{1,0:T(8,128)(2,1)S(1)} %get-tuple-element.30), channel_id=1, source_target_pairs={{20,0},{24,4},{28,8},{4,16},{8,20},{12,24},{21,1},{25,5},{29,9},{5... | collective-permute-start | bytes 1572872 | tf_op jit(solution)/shard_map/ppermute | solution.py:411
  63.4 0.0 copy-start.4
  63.4 0.0 copy-start.6
  63.4 0.0 copy-start.7
  63.4 0.1 collective-permute-start.7
  63.5 2.0 %choose.2 = (bf16[512,512]{1,0:T(8,128)(2,1)S(1)}, bf16[512,512]{1,0:T(8,128)(2,1)}) custom-call(s32[1]{0:T(128)S(6)} %select_n.32.mode_ref, bf16[1,2,512,1536]{3,2,1,0:T(8,128)(2,1)S(1)} %copy-done, bf16[512,1024]{1,0:T(8,128)(2,1)} %collective-permute-done.2.refs_1_, bf16[512,1536]{1,0:T(8,128)(2,1)S(1)} %copy-done.3, bf16[1,2,512,1536]{3,2,1,0:T(8,128)(2,1)S(1)} %copy-done), custom_call_target="tpu_custom_call" | custom-call | tf_op jit(solution)/shard_map/choose/pallas_call | solution.py:253
  65.5 2.1 %collective-permute-start.3 = (bf16[512,512]{1,0:T(8,128)(2,1)S(1)}, bf16[512,512]{1,0:T(8,128)(2,1)S(1)}, u32[]{:S(2)}, u32[]{:S(2)}) collective-permute-start(bf16[512,512]{1,0:T(8,128)(2,1)S(1)} %get-tuple-element.28.rest_0_), channel_id=1, source_target_pairs={{0,28},{4,0},{8,4},{12,8},{16,12},{20,16},{24,20},{28,24},{1,29},{... | collective-permute-start | bytes 1572872 | tf_op jit(solution)/shard_map/ppermute | solution.py:411
  67.6 0.1 fusion.6.pick_ref
  67.7 0.0 copy-done.4
  67.7 0.0 copy-done.6
  67.7 0.0 copy-done.7
  67.7 7.5 %forward.1.refs_7_ = bf16[512,1536]{1,0:T(8,128)(2,1)} custom-call(bf16[512,1536]{1,0:T(8,128)(2,1)S(1)} %bitcast.12, f32[1,512]{1,0:T(1,128)S(1)} %get-tuple-element.46.f_ref, f32[1,1536]{1,0:T(1,128)S(1)} %copy-done.6, f32[1,1536]{1,0:T(1,128)S(1)} %copy-done.7, bf16[512,512]{1,0:T(8,128)(2,1)S(1)} %get-tuple-element.28.rest_0_), custom_call_target="tpu_custom_call" | custom-call | tf_op jit(solution)/shard_map/forward/pallas_call | solution.py:98
  75.2 39.2 %collective-permute-done.7.refs_0_.refs_3_ = bf16[512,512]{1,0:T(8,128)(2,1)S(1)} collective-permute-done((bf16[512,512]{1,0:T(8,128)(2,1)S(1)}, bf16[512,512]{1,0:T(8,128)(2,1)S(1)}, u32[]{:S(2)}, u32[]{:S(2)}) %collective-permute-start.7) | collective-permute-done | bytes 524320 | tf_op jit(solution)/shard_map/ppermute | solution.py:411
  114.4 0.0 collective-permute-done.4.refs_1_.refs_2_.refs_3_
  114.4 0.0 copy-start.5
  114.4 1.4 copy-done.5
  115.8 6.5 %backward.3 = (f32[512,1536]{1,0:T(8,128)S(1)}, bf16[512,1536]{1,0:T(8,128)(2,1)S(1)}, f32[1,512]{1,0:T(1,128)S(1)}) custom-call(s32[4]{0:T(128)S(1)} %fusion.4.pick_ref, bf16[512,512]{1,0:T(8,128)(2,1)S(1)} %collective-permute-done.7.refs_0_.refs_3_, bf16[512,1536]{1,0:T(8,128)(2,1)} %collective-permute-done.4.refs_1_.refs_2_.refs_3_, ...), custom_call_target="tpu_custom_call" | custom-call | tf_op jit(solution)/shard_map/backward/pallas_call | solution.py:183
  122.3 0.0 collective-permute-done.6.refs_1_.refs_4_
  122.3 0.0 collective-permute-done.5.refs_0_
  122.4 6.7 %backward.4 = (f32[512,1536]{1,0:T(8,128)S(1)}, bf16[512,1536]{1,0:T(8,128)(2,1)S(1)}, f32[1,512]{1,0:T(1,128)S(1)}) custom-call(s32[4]{0:T(128)S(1)} %fusion.6.pick_ref, bf16[512,512]{1,0:T(8,128)(2,1)S(1)} %collective-permute-done.5.refs_0_, ...), custom_call_target="tpu_custom_call", output_to_operand_aliasing={{0}: (9, {}), {1}: (10, {})} | custom-call | tf_op jit(solution)/shard_map/backward/pallas_call | solution.py:183
  129.1 0.0 collective-permute-done.3.refs_0_.refs_3_
  129.1 6.5 %backward.5 = (f32[512,1536]{1,0:T(8,128)S(1)}, bf16[512,1536]{1,0:T(8,128)(2,1)S(1)}, f32[1,512]{1,0:T(1,128)S(1)}) custom-call(s32[4]{0:T(128)S(1)} %fusion.4.pick_ref, bf16[512,512]{1,0:T(8,128)(2,1)S(1)} %collective-permute-done.3.refs_0_.refs_3_, ...), custom_call_target="tpu_custom_call", output_to_operand_aliasing={{0}: (8, {}), {1}: (9, {})} | custom-call | tf_op jit(solution)/shard_map/backward/pallas_call | solution.py:183
  135.6 0.0 copy-start.1
  135.6 1.1 copy-done.1
  136.7 5.9 %psum.23 = f32[1,512]{1,0:T(1,128)S(1)} all-reduce(f32[1,512]{1,0:T(1,128)S(1)} %add_add_fusion), channel_id=1, replica_groups=mesh['section'=8,'tensor'=4] {'tensor'}, use_global_device_ids=true, to_apply=%region_2.3 | all-reduce | flops 512 | bytes 4096 | tf_op jit(solution)/shard_map/psum | solution.py:489
  142.7 0.0 copy-start.2
  142.7 1.4 copy-done.2
  144.1 2.1 %finish.1 = bf16[512,1536]{1,0:T(8,128)(2,1)} custom-call(f32[512,1536]{1,0:T(8,128)S(1)} %get-tuple-element.37.a_ref, bf16[512,1536]{1,0:T(8,128)(2,1)S(1)} %copy-done.2, f32[1,512]{1,0:T(1,128)S(1)} %broadcast_select_fusion.row_ref), custom_call_target="tpu_custom_call" | custom-call | tf_op jit(solution)/shard_map/finish/pallas_call | solution.py:276
  (7 shorter events, 0.0 us)
Async XLA Ops:
  9.0 9.2 %collective-permute-start.1 = (f32[1,512]{1,0:T(1,128)S(1)}, f32[1,512]{1,0:T(1,128)S(1)}, u32[]{:S(2)}, u32[]{:S(2)}) collective-permute-start(f32[1,512]{1,0:T(1,128)S(1)} %slice.29), channel_id=1, source_target_pairs={{16,28},{20,0},{24,4},{28,8},{0,12},{4,16},{8,20},{12,24},{17,29},... | collective-permute-start | bytes 6152 | tf_op jit(solution)/shard_map/ppermute | solution.py:411
  9.3 7.8 %collective-permute-start = (f32[1,3712]{1,0:T(1,128)}, f32[1,3712]{1,0:T(1,128)S(1)}, u32[]{:S(2)}, u32[]{:S(2)}) collective-permute-start(f32[1,3712]{1,0:T(1,128)} %get-tuple-element.23), channel_id=1, source_target_pairs={{0,28},{4,0},{8,4},{12,8},{16,12},{20,16},{24,20},{28,24},{1,29},{... | collective-permute-start | bytes 44552 | tf_op jit(solution)/shard_map/ppermute | solution.py:411
  12.0 46.9 %collective-permute-start.2 = (bf16[512,1024]{1,0:T(8,128)(2,1)}, bf16[512,1024]{1,0:T(8,128)(2,1)}, u32[]{:S(2)}, u32[]{:S(2)}) collective-permute-start(bf16[512,1024]{1,0:T(8,128)(2,1)} %get-tuple-element.24), channel_id=1, source_target_pairs={{4,20},{8,24},{12,28},{20,4},{24,8},{28,12},{5,21},{9,25},{13,29},... | collective-permute-start | bytes 3145736 | tf_op jit(solution)/shard_map/ppermute | solution.py:411
  14.3 100.1 %collective-permute-start.4 = (bf16[512,1536]{1,0:T(8,128)(2,1)}, bf16[512,1536]{1,0:T(8,128)(2,1)}, u32[]{:S(2)}, u32[]{:S(2)}) collective-permute-start(bf16[512,1536]{1,0:T(8,128)(2,1)} %get-tuple-element.29), channel_id=1, source_target_pairs={{4,0},{8,4},{12,8},{20,16},{24,20},{28,24},{16,28},{0,12},{5,1},{9... | collective-permute-start | bytes 4718600 | tf_op jit(solution)/shard_map/ppermute | solution.py:411
  34.7 24.2 %copy-start = (bf16[1,2,512,1536]{3,2,1,0:T(8,128)(2,1)S(1)}, bf16[1,2,512,1536]{3,2,1,0:T(8,128)(2,1)}, u32[]{:S(2)}) copy-start(bf16[1,2,512,1536]{3,2,1,0:T(8,128)(2,1)} %refs_3_.3) | copy-start | bytes 9437188
  39.9 82.5 %collective-permute-start.6 = (bf16[512,512]{1,0:T(8,128)(2,1)}, bf16[512,512]{1,0:T(8,128)(2,1)}, u32[]{:S(2)}, u32[]{:S(2)}) collective-permute-start(bf16[512,512]{1,0:T(8,128)(2,1)} %get-tuple-element.31), channel_id=1, source_target_pairs={{0,28},{4,0},{8,4},{12,8},{16,12},{20,16},{24,20},{28,24},{1,29},{... | collective-permute-start | bytes 1572872 | tf_op jit(solution)/shard_map/ppermute | solution.py:411
  58.9 1.4 copy-start.3
  61.5 60.9 %collective-permute-start.5 = (bf16[512,512]{1,0:T(8,128)(2,1)S(1)}, bf16[512,512]{1,0:T(8,128)(2,1)S(1)}, u32[]{:S(2)}, u32[]{:S(2)}) collective-permute-start(bf16[512,512]{1,0:T(8,128)(2,1)S(1)} %get-tuple-element.30), channel_id=1, source_target_pairs={{20,0},{24,4},{28,8},{4,16},{8,20},{12,24},{21,1},{25,5},{29,9},{5... | collective-permute-start | bytes 1572872 | tf_op jit(solution)/shard_map/ppermute | solution.py:411
  63.4 4.3 %copy-start.4 = (bf16[1,512,1536]{2,1,0:T(8,128)(2,1)S(1)}, bf16[1,512,1536]{2,1,0:T(8,128)(2,1)}, u32[]{:S(2)}) copy-start(bf16[1,512,1536]{2,1,0:T(8,128)(2,1)} %param.6) | copy-start | bytes 4718596
  63.4 4.3 %copy-start.6 = (f32[1,1536]{1,0:T(1,128)S(1)}, f32[1,1536]{1,0:T(1,128)}, u32[]{:S(2)}) copy-start(f32[1,1536]{1,0:T(1,128)} %gq_ref.5) | copy-start | bytes 18436
  63.4 4.3 %copy-start.7 = (f32[1,1536]{1,0:T(1,128)S(1)}, f32[1,1536]{1,0:T(1,128)}, u32[]{:S(2)}) copy-start(f32[1,1536]{1,0:T(1,128)} %gk_ref.5) | copy-start | bytes 18436
  63.4 51.0 %collective-permute-start.7 = (bf16[512,512]{1,0:T(8,128)(2,1)S(1)}, bf16[512,512]{1,0:T(8,128)(2,1)S(1)}, u32[]{:S(2)}, u32[]{:S(2)}) collective-permute-start(bf16[512,512]{1,0:T(8,128)(2,1)S(1)} %get-tuple-element.32), channel_id=1, source_target_pairs={{0,28},{4,0},{8,4},{12,8},{16,12},{20,16},{24,20},{28,24},{1,29},{... | collective-permute-start | bytes 1572872 | tf_op jit(solution)/shard_map/ppermute | solution.py:411
  65.5 63.6 %collective-permute-start.3 = (bf16[512,512]{1,0:T(8,128)(2,1)S(1)}, bf16[512,512]{1,0:T(8,128)(2,1)S(1)}, u32[]{:S(2)}, u32[]{:S(2)}) collective-permute-start(bf16[512,512]{1,0:T(8,128)(2,1)S(1)} %get-tuple-element.28.rest_0_), channel_id=1, source_target_pairs={{0,28},{4,0},{8,4},{12,8},{16,12},{20,16},{24,20},{28,24},{1,29},{... | collective-permute-start | bytes 1572872 | tf_op jit(solution)/shard_map/ppermute | solution.py:411
  114.4 1.4 copy-start.5
  135.6 1.1 copy-start.1
  142.7 1.4 copy-start.2

commit v6 on v1

--- a/solution.py
+++ b/solution.py
@@ -12,7 +12,8 @@
 EPSILON = 1e-05
 SCALE = 1.0 / math.sqrt(HDIM)
 LOG2E = math.log2(math.e)
-VMEM = 48 * 1024 * 1024
+VMEM = 32 * 1024 * 1024
+MOST = 60 * 1024 * 1024
 
 F32 = jnp.float32
 BF16 = jnp.bfloat16
@@ -72,7 +73,8 @@
     return jnp.broadcast_to(row, (HDIM, row.shape[1])).T[:, 0:1]
 
 
-def forward_kernel(heads, x_ref, f_ref, gq_ref, gk_ref, o_ref):
+def forward_kernel(heads, x_ref, f_ref, gq_ref, gk_ref, *rest):
+    o_ref = rest[-1]
     tokens = x_ref.shape[0]
     size = block_of(tokens)
     kept = kept_keys(size)
@@ -88,25 +90,21 @@
             o_ref[rows, lanes] = (wide[rows] + mixed.T).astype(BF16)
 
 
-def forward(x, factor, gain_q, gain_k, heads):
+def forward(x, factor, gain_q, gain_k, heads, after=()):
     tokens, width = x.shape
     lanes = heads * HDIM
     block = pl.BlockSpec((tokens, lanes), lambda i: (0, i))
     gain = pl.BlockSpec((1, lanes), lambda i: (0, i))
-    n = width // HDIM
     return pl.pallas_call(
         functools.partial(forward_kernel, heads),
         out_shape=jax.ShapeDtypeStruct(x.shape, BF16),
         grid=(width // lanes,),
-        in_specs=[block, pl.BlockSpec((1, tokens), lambda i: (0, 0)), gain, gain],
+        in_specs=[block, pl.BlockSpec((1, tokens), lambda i: (0, 0)), gain, gain]
+        + [pl.BlockSpec(memory_space=pl.ANY)] * len(after),
         out_specs=block,
         compiler_params=pltpu.CompilerParams(vmem_limit_bytes=VMEM),
-        cost_estimate=pl.CostEstimate(
-            flops=4 * n * tokens * tokens * HDIM, bytes_accessed=4 * tokens * width,
-            transcendentals=n * tokens * tokens,
-        ),
         name="forward",
-    )(x, factor, gain_q, gain_k)
+    )(x, factor, gain_q, gain_k, *after)
 
 
 def backward_head(x, g, factor, gain_q, gain_k):
@@ -140,89 +138,163 @@
     return wide, d_normed
 
 
-def backward_kernel(heads, x_ref, g_ref, f_ref, gq_ref, gk_ref, a_ref, inner_ref):
+def selected(which, refs, at):
+    values = [ref[lanes_of(start + at, HDIM)] for ref, start in refs]
+    value = values[0]
+    for i, other in enumerate(values[1:]):
+        value = jnp.where(which == i + 1, other, value)
+    return value
+
+
+def lanes_of(start, size):
+    return (slice(None), slice(start, start + size))
+
+
+def backward_piece(pick_ref, xs, gs, f_ref, gq_ref, gk_ref, a_ref, x_ref, heads, first):
     factor = column_of(f_ref[...])
     part = None
     for h in range(heads):
-        lanes = slice(h * HDIM, (h + 1) * HDIM)
-        g = g_ref[:, lanes]
-        wide, d_normed = backward_head(x_ref[:, lanes], g, factor, gq_ref[:, lanes], gk_ref[:, lanes])
-        a_ref[:, lanes] = g.astype(F32) + factor * d_normed
+        mine = lanes_of(first + h * HDIM, HDIM)
+        x = selected(pick_ref[1], xs, h * HDIM)
+        g = selected(pick_ref[2], gs, h * HDIM)
+        wide, d_normed = backward_head(x, g, factor, gq_ref[mine], gk_ref[mine])
+        a_ref[mine] = g.astype(F32) + jnp.where(pick_ref[3] == 1, 0.0, factor * d_normed)
+        x_ref[mine] = x
         product = d_normed * wide
         part = product if part is None else part + product
-    inner = jnp.sum(part.T, axis=0, keepdims=True)
-
-    @pl.when(pl.program_id(0) == 0)
+    return jnp.sum(part.T, axis=0, keepdims=True)
+
+
+def backward_kernel(heads, first, x_at, g_at, pick_ref, *refs):
+    n_x, n_g = len(x_at), len(g_at)
+    xs = list(zip(refs[:n_x], x_at))
+    gs = list(zip(refs[n_x : n_x + n_g], g_at))
+    a_ref, x_ref, inner_ref = refs[-3:]
+    inner_ref[...] = backward_piece(pick_ref, xs, gs, *refs[n_x + n_g : n_x + n_g + 3], a_ref, x_ref, heads, first)
+
+
+IN_VMEM = pl.BlockSpec(memory_space=pltpu.VMEM)
+
+
+def backward(pick, xs, gs, factor, gain_q, gain_k, heads, first, sofar=(), after=()):
+    tokens = xs[0][0].shape[0]
+    width = gain_q.shape[1]
+    before = 1 + len(xs) + len(gs) + 3
+    return pl.pallas_call(
+        functools.partial(backward_kernel, heads, first, tuple(at for _, at in xs), tuple(at for _, at in gs)),
+        out_shape=(
+            jax.ShapeDtypeStruct((tokens, width), F32),
+            jax.ShapeDtypeStruct((tokens, width), BF16),
+            jax.ShapeDtypeStruct((1, tokens), F32),
+        ),
+        in_specs=[pl.BlockSpec(memory_space=pltpu.SMEM)] + [IN_VMEM] * (before - 1 + len(sofar))
+        + [pl.BlockSpec(memory_space=pl.ANY)] * len(after),
+        out_specs=(IN_VMEM, IN_VMEM, IN_VMEM),
+        input_output_aliases={before: 0, before + 1: 1} if sofar else {},
+        compiler_params=pltpu.CompilerParams(vmem_limit_bytes=VMEM),
+        name="backward",
+    )(pick, *[x for x, _ in xs], *[g for g, _ in gs], factor, gain_q, gain_k, *sofar, *after)
+
+
+def finish_kernel(lanes, a_ref, x_ref, row_ref, o_ref):
+    row = column_of(row_ref[...])
+    at = (slice(None), pl.ds(pl.program_id(0) * lanes, lanes))
+    o_ref[...] = (a_ref[at] - x_ref[at].astype(F32) * row).astype(BF16)
+
+
+def finish(a, x, row, lanes):
+    tokens, width = a.shape
+    return pl.pallas_call(
+        functools.partial(finish_kernel, lanes),
+        out_shape=jax.ShapeDtypeStruct(a.shape, BF16),
+        grid=(width // lanes,),
+        in_specs=[IN_VMEM] * 3,
+        out_specs=pl.BlockSpec((tokens, lanes), lambda i: (0, i)),
+        compiler_params=pltpu.CompilerParams(vmem_limit_bytes=VMEM),
+        name="finish",
+    )(a, x, row)
+
+
+def open_kernel(pieces, current_ref, stash_ref, rows_ref, *out_refs):
+    step = pl.program_id(0)
+
+    def total(x):
+        wide = x.astype(F32)
+        square = wide * wide
+        sums = sum(square[:, i : i + HDIM] for i in range(0, square.shape[1], HDIM))
+        return jnp.sum(sums.T, axis=0, keepdims=True)
+
+    rows = jnp.concatenate([total(current_ref[...]), total(stash_ref[0]), total(stash_ref[1])], axis=0)
+
+    @pl.when(step == 0)
     def _():
-        inner_ref[...] = inner
-
-    @pl.when(pl.program_id(0) > 0)
+        rows_ref[...] = rows
+
+    @pl.when(step > 0)
     def _():
-        inner_ref[...] += inner
-
-
-def backward(x, g, factor, gain_q, gain_k, heads):
-    tokens, width = x.shape
-    lanes = heads * HDIM
-    block = pl.BlockSpec((tokens, lanes), lambda i: (0, i))
-    gain = pl.BlockSpec((1, lanes), lambda i: (0, i))
-    row = pl.BlockSpec((1, tokens), lambda i: (0, 0))
-    n = width // HDIM
+        rows_ref[...] += rows
+
+    for p in range(pieces):
+
+        @pl.when(step == p)
+        def _():
+            out_refs[p][...] = stash_ref[1]
+
+
+def opened(current, stash, lanes):
+    tokens, width = current.shape
+    pieces = width // lanes
+    still = lambda *shape: pl.BlockSpec(shape, lambda i: (0, 0))
     return pl.pallas_call(
-        functools.partial(backward_kernel, heads),
-        out_shape=(jax.ShapeDtypeStruct(x.shape, F32), jax.ShapeDtypeStruct((1, tokens), F32)),
-        grid=(width // lanes,),
-        in_specs=[block, block, row, gain, gain],
-        out_specs=(block, row),
-        compiler_params=pltpu.CompilerParams(vmem_limit_bytes=VMEM),
-        cost_estimate=pl.CostEstimate(
-            flops=10 * n * tokens * tokens * HDIM, bytes_accessed=8 * tokens * width,
-            transcendentals=n * tokens * tokens,
-        ),
-        name="backward",
-    )(x, g, factor, gain_q, gain_k)
-
-
-def passed_along(x, axis, by):
-    size = lax.axis_size(axis)
-    return lax.ppermute(x, axis, [(i, (i + by) % size) for i in range(size)])
-
-
-def squares(x):
-    wide = x.astype(F32)
-    return jnp.sum(wide * wide, axis=-1)[None]
+        functools.partial(open_kernel, pieces),
+        out_shape=[jax.ShapeDtypeStruct((3, tokens), F32)] + [jax.ShapeDtypeStruct((tokens, lanes), BF16)] * pieces,
+        grid=(pieces,),
+        in_specs=[
+            pl.BlockSpec((tokens, lanes), lambda i: (0, i)),
+            pl.BlockSpec((None, 2, tokens, lanes), lambda i: (0, 0, 0, i)),
+        ],
+        out_specs=[still(3, tokens)] + [still(tokens, lanes)] * pieces,
+        compiler_params=pltpu.CompilerParams(vmem_limit_bytes=MOST),
+        name="opened",
+    )(current, stash)
+
+
+def send(x, pairs):
+    return lax.ppermute(x, "section", pairs)
 
 
 def local(width_all, layer_input, grad_input, stashed, eviction, query_gain, key_gain):
-    half_sections = lax.axis_size("section") // 2
+    n = lax.axis_size("section")
+    half = n // 2
+    word = lambda *flags: jnp.stack([jnp.asarray(f).astype(jnp.int32) for f in flags])
+    partner = [(s, (s + half) % n) for s in range(n)]
+    prior = [(s, (s - 1) % n) for s in range(n)]
+
     current = layer_input[0]
     upstream = grad_input[0]
-    heads_here = current.shape[1] // HDIM
-    chunks = next(c for c in (4, 3, 2, 1) if heads_here % c == 0)
-    heads = heads_here // chunks
+    tokens, width = current.shape
+    heads = width // HDIM // 3
     step = heads * HDIM
-    evicted = eviction[0] == 1
-    parts = [slice(c * step, (c + 1) * step) for c in range(chunks)]
-    fetched = [passed_along(stashed[0, 1][:, p], "section", -half_sections) for p in parts]
-    totals = lax.psum(
-        jnp.concatenate([squares(current), squares(stashed[0, 0]), squares(stashed[0, 1])], axis=0), "tensor"
-    )
-    fetched_total = passed_along(totals[2:3], "section", -half_sections)
-    chosen_total = jnp.where(evicted, fetched_total, totals[1:2])
-    forward_factor = lax.rsqrt(totals[0:1] / width_all + EPSILON)
-    factor = lax.rsqrt(chosen_total / width_all + EPSILON)
-    output = forward(current, forward_factor, query_gain, key_gain, heads)
-    terms = []
-    inner = 0.0
-    for p, f in zip(parts, fetched):
-        x = jnp.where(evicted, f, stashed[0, 0][:, p])
-        a, part = backward(x, upstream[:, p], factor, query_gain[:, p], key_gain[:, p], heads)
-        terms.append((x, a))
-        inner = inner + part
+
+    rows, *held = opened(current, stashed, step)
+    held_row = send(rows[2:3], partner)
+    fetched = [send(h, partner) for h in held]
+    chosen_row = jnp.where(eviction[0] == 1, held_row, rows[1:2])
+    totals = lax.psum(jnp.concatenate([rows[:1], chosen_row], axis=0), "tensor")
+    factors = lax.rsqrt(totals / width_all + EPSILON)
+    output = forward(current, factors[0:1], query_gain, key_gain, heads)
+    facts = (factors[1:2], query_gain, key_gain)
+    take = word(1, eviction[0], 0, 0)
+    sofar, inner, after = (), 0.0, (output,)
+    own = stashed[0, 0]
+    for p, f in enumerate(fetched):
+        a, x, part = backward(
+            take, [(own, p * step), (f, 0)], [(upstream, p * step)], *facts, heads, p * step, sofar, after
+        )
+        sofar, inner, after = (a, x), inner + part, ()
     inner = lax.psum(inner, "tensor")
-    row = (factor**3 * inner / width_all).T
-    passed = [passed_along((a - x.astype(F32) * row).astype(BF16), "section", -1) for x, a in terms]
-    return (output[None], jnp.concatenate(passed, axis=1)[None])
+    result = finish(a, x, factors[1:2] ** 3 * inner / width_all, step)
+    return (output[None], send(result, prior)[None])
 
 
 def solution(mesh):

time: 145 us -> 148 us (1.021)
  Pallas kernels: 22.4 us -> 29.7 us
  other arithmetic: 6.27 us -> 0.12 us
  waiting for transfers between devices: 78 us -> 83.5 us
  starting transfers between devices: 15.4 us -> 10.5 us
    pallas_call x4 -> x5, Pallas kernels: 14.3 us -> 22.2 us  [the longest x3 16.5 us: backward(): pl.pallas_call(functools.partial(backward_kernel, heads, first, tuple((at...]
    ppermute x9 -> x5, waiting for transfers between devices: 78 us -> 83.5 us  [send(): return lax.ppermute(x, 'section', pairs)]
    ppermute x9 -> x5, starting transfers between devices: 15.4 us -> 10.5 us  [send(): return lax.ppermute(x, 'section', pairs)]
    convert_element_type x1 -> x0, other arithmetic: 2.28 us -> none  [local(): (a - x.astype(F32) * row).astype(BF16)]
    unnamed x20 -> x23, local copies, waits for them, and re-layouts: 4.79 us -> 6.99 us
    select_n x1 -> x0, other arithmetic: 1.61 us -> none  [local(): x = jnp.where(evicted, f, stashed[0, 0][:, p])]
  transfers between devices with their start and end apart: 9 -> 5, of which waited for: 5 -> 2; matrix products, arithmetic and copies ran while one was open for 1% -> 2% of each run, Pallas kernels for 6% -> 12%
where the time goes in v6:
time: 148 us; the launch traced here: 147 us
  waiting for transfers between devices  83.5 us (56%)
  Pallas kernels  29.7 us (20%)
  blocking collectives  11.4 us (8%)
  starting transfers between devices  10.5 us (7%)
  local copies, waits for them, and re-layouts  10.4 us (7%)
    ppermute x5, waiting for transfers between devices, send(): return lax.ppermute(x, 'section', pairs)  83.5 us
    pallas_call x3, Pallas kernels, backward(): pl.pallas_call(functools.partial(backward_kernel, heads, first, tuple((at...  16.5 us
    ppermute x5, starting transfers between devices, send(): return lax.ppermute(x, 'section', pairs)  10.5 us
    pallas_call x1, Pallas kernels, forward(): pl.pallas_call(functools.partial(forward_kernel, heads), out_shape=jax.Sh...  7.46 us
    unnamed x23, local copies, waits for them, and re-layouts  6.99 us
    psum x1, blocking collectives, local(): totals = lax.psum(jnp.concatenate([rows[:1], chosen_row], axis=0), 'tensor')  5.76 us
    psum x1, blocking collectives, local(): inner = lax.psum(inner, 'tensor')  5.66 us
    pallas_call x1, Pallas kernels, opened(): pl.pallas_call(functools.partial(open_kernel, pieces), out_shape=[jax.Sha...  4.81 us
  transfers between devices with their start and end apart: 5, of which 2 were waited for; matrix products, arithmetic and copies ran while one was open for 2% of the time, Pallas kernels for 12%

profile of v6, /device:TPU:0, one launch (start us, length us, event | category | flops | bytes accessed | tf_op | source)
XLA Modules:
  0.0 147.2 jit_solution(2286232501642591517)
XLA Ops:
  0.6 4.8 %opened.1 = (f32[3,512]{1,0:T(4,128)}, bf16[512,512]{1,0:T(8,128)(2,1)}, bf16[512,512]{1,0:T(8,128)(2,1)}, bf16[512,512]{1,0:T(8,128)(2,1)}) custom-call(bf16[512,1536]{1,0:T(8,128)(2,1)} %bitcast.10, bf16[1,2,512,1536]{3,2,1,0:T(8,128)(2,1)} %stash_ref.1), custom_call_target="tpu_custom_call" | custom-call | tf_op jit(solution)/shard_map/opened/pallas_call | solution.py:248
  5.4 0.7 slice.20
  6.1 4.0 %collective-permute-start = (f32[1,512]{1,0:T(1,128)S(1)}, f32[1,512]{1,0:T(1,128)S(1)}, u32[]{:S(2)}, u32[]{:S(2)}) collective-permute-start(f32[1,512]{1,0:T(1,128)S(1)} %slice.20), channel_id=1, source_target_pairs={{0,16},{4,20},{8,24},{12,28},{16,0},{20,4},{24,8},{28,12},{1,17},{... | collective-permute-start | bytes 6152 | tf_op jit(solution)/shard_map/ppermute | solution.py:263
  10.2 0.0 collective-permute-start.1
  10.2 2.9 %collective-permute-start.2 = (bf16[512,512]{1,0:T(8,128)(2,1)}, bf16[512,512]{1,0:T(8,128)(2,1)}, u32[]{:S(2)}, u32[]{:S(2)}) collective-permute-start(bf16[512,512]{1,0:T(8,128)(2,1)} %get-tuple-element.17), channel_id=1, source_target_pairs={{0,16},{4,20},{8,24},{12,28},{16,0},{20,4},{24,8},{28,12},{1,17},{... | collective-permute-start | bytes 1572872 | tf_op jit(solution)/shard_map/ppermute | solution.py:263
  13.1 0.0 copy-start.10
  13.1 0.0 copy-start.4
  13.1 0.0 copy-start.8
  13.1 0.0 copy-start.9
  13.1 0.1 collective-permute-start.3
  13.2 2.7 %slice_bitcast_fusion.refs_0_ = bf16[512,1536]{1,0:T(8,128)(2,1)} fusion(bf16[1,2,512,1536]{3,2,1,0:T(8,128)(2,1)} %stash_ref.1), kind=kLoop, calls=%fused_computation | loop fusion | bytes 3145728 | tf_op jit(solution)/shard_map/squeeze | solution.py:289
  16.6 0.1 pad_add_fusion.pick_ref
  16.7 0.0 collective-permute-done
  16.7 0.0 copy-done.10
  16.7 5.8 %psum.14 = f32[2,512]{1,0:T(2,128)S(1)} all-reduce(f32[2,512]{1,0:T(2,128)S(1)} %pad_maximum_fusion), channel_id=1, replica_groups=mesh['section'=8,'tensor'=4] {'tensor'}, use_global_device_ids=true, to_apply=%region_0.1 | all-reduce | flops 1024 | bytes 8192 | tf_op jit(solution)/shard_map/psum | solution.py:283
  22.5 0.0 copy-done.4
  22.5 0.0 copy-done.8
  22.6 0.0 copy-done.9
  22.6 0.0 copy-start
  22.6 0.0 copy-start.1
  22.6 7.5 %forward.1.refs_6_ = bf16[512,1536]{1,0:T(8,128)(2,1)} custom-call(bf16[512,1536]{1,0:T(8,128)(2,1)S(1)} %bitcast.11, f32[1,512]{1,0:T(1,128)S(1)} %get-tuple-element.31.f_ref, f32[1,1536]{1,0:T(1,128)S(1)} %copy-done.8, f32[1,1536]{1,0:T(1,128)S(1)} %copy-done.9), custom_call_target="tpu_custom_call" | custom-call | tf_op jit(solution)/shard_map/forward/pallas_call | solution.py:98
  30.0 50.8 %collective-permute-done.3.refs_1_ = bf16[512,512]{1,0:T(8,128)(2,1)S(1)} collective-permute-done((bf16[512,512]{1,0:T(8,128)(2,1)}, bf16[512,512]{1,0:T(8,128)(2,1)S(1)}, u32[]{:S(2)}, u32[]{:S(2)}) %collective-permute-start.3) | collective-permute-done | bytes 524320 | tf_op jit(solution)/shard_map/ppermute | solution.py:263
  80.8 0.0 copy-start.6
  80.8 0.8 copy-done.6
  81.7 0.0 copy-done
  81.7 0.0 copy-done.1
  81.7 0.0 copy-start.5
  81.7 1.4 copy-done.5
  83.1 0.0 copy-start.7
  83.1 1.0 copy-done.7
  84.1 5.1 %backward.3 = (f32[512,1536]{1,0:T(8,128)S(1)}, bf16[512,1536]{1,0:T(8,128)(2,1)S(1)}, f32[1,512]{1,0:T(1,128)S(1)}) custom-call(s32[4]{0:T(128)S(1)} %pad_add_fusion.pick_ref, bf16[512,1536]{1,0:T(8,128)(2,1)S(1)} %copy-done, bf16[512,512]{1,0:T(8,128)(2,1)S(1)} %copy-done.7, bf16[512,1536]{1,0:T(8,128)(2,1)S(1)} %bitcast.7, ...), custom_call_target="tpu_custom_call" | custom-call | tf_op jit(solution)/shard_map/backward/pallas_call | solution.py:183
  89.3 0.0 collective-permute-done.2.refs_1_
  89.3 5.7 %backward.4 = (f32[512,1536]{1,0:T(8,128)S(1)}, bf16[512,1536]{1,0:T(8,128)(2,1)S(1)}, f32[1,512]{1,0:T(1,128)S(1)}) custom-call(s32[4]{0:T(128)S(1)} %pad_add_fusion.pick_ref, bf16[512,1536]{1,0:T(8,128)(2,1)S(1)} %copy-done, bf16[512,512]{1,0:T(8,128)(2,1)} %collective-permute-done.2.refs_1_, ...), custom_call_target="tpu_custom_call", output_to_operand_aliasing={{0}: (7, {}), {1}: (8, {})} | custom-call | tf_op jit(solution)/shard_map/backward/pallas_call | solution.py:183
  94.9 0.0 collective-permute-done.1.refs_1_
  95.0 5.7 %backward.5 = (f32[512,1536]{1,0:T(8,128)S(1)}, bf16[512,1536]{1,0:T(8,128)(2,1)S(1)}, f32[1,512]{1,0:T(1,128)S(1)}) custom-call(s32[4]{0:T(128)S(1)} %pad_add_fusion.pick_ref, bf16[512,1536]{1,0:T(8,128)(2,1)S(1)} %copy-done, bf16[512,512]{1,0:T(8,128)(2,1)} %collective-permute-done.1.refs_1_, ...), custom_call_target="tpu_custom_call", output_to_operand_aliasing={{0}: (7, {}), {1}: (8, {})} | custom-call | tf_op jit(solution)/shard_map/backward/pallas_call | solution.py:183
  100.6 0.0 copy-start.2
  100.6 1.1 copy-done.2
  101.8 5.7 %psum.15 = f32[1,512]{1,0:T(1,128)S(1)} all-reduce(f32[1,512]{1,0:T(1,128)S(1)} %add_add_fusion), channel_id=1, replica_groups=mesh['section'=8,'tensor'=4] {'tensor'}, use_global_device_ids=true, to_apply=%region_1.2 | all-reduce | flops 512 | bytes 4096 | tf_op jit(solution)/shard_map/psum | solution.py:295
  107.4 0.0 copy-start.3
  107.4 1.4 copy-done.3
  108.8 1.0 finish.1
  109.8 3.5 %collective-permute-start.4 = (bf16[512,1536]{1,0:T(8,128)(2,1)S(1)}, bf16[512,1536]{1,0:T(8,128)(2,1)S(1)}, u32[]{:S(2)}, u32[]{:S(2)}) collective-permute-start(bf16[512,1536]{1,0:T(8,128)(2,1)S(1)} %finish.1), channel_id=1, source_target_pairs={{0,28},{4,0},{8,4},{12,8},{16,12},{20,16},{24,20},{28,24},{1,29},{... | collective-permute-start | bytes 4718600 | tf_op jit(solution)/shard_map/ppermute | solution.py:263
  113.3 32.7 %collective-permute-done.4 = bf16[512,1536]{1,0:T(8,128)(2,1)S(1)} collective-permute-done((bf16[512,1536]{1,0:T(8,128)(2,1)S(1)}, bf16[512,1536]{1,0:T(8,128)(2,1)S(1)}, u32[]{:S(2)}, u32[]{:S(2)}) %collective-permute-start.4) | collective-permute-done | bytes 1572896 | tf_op jit(solution)/shard_map/ppermute | solution.py:263
  146.0 1.1 copy.18
  (7 shorter events, 0.1 us)
Async XLA Ops:
  6.1 10.6 %collective-permute-start = (f32[1,512]{1,0:T(1,128)S(1)}, f32[1,512]{1,0:T(1,128)S(1)}, u32[]{:S(2)}, u32[]{:S(2)}) collective-permute-start(f32[1,512]{1,0:T(1,128)S(1)} %slice.20), channel_id=1, source_target_pairs={{0,16},{4,20},{8,24},{12,28},{16,0},{20,4},{24,8},{28,12},{1,17},{... | collective-permute-start | bytes 6152 | tf_op jit(solution)/shard_map/ppermute | solution.py:263
  10.2 84.8 %collective-permute-start.1 = (bf16[512,512]{1,0:T(8,128)(2,1)}, bf16[512,512]{1,0:T(8,128)(2,1)}, u32[]{:S(2)}, u32[]{:S(2)}) collective-permute-start(bf16[512,512]{1,0:T(8,128)(2,1)} %get-tuple-element.16), channel_id=1, source_target_pairs={{0,16},{4,20},{8,24},{12,28},{16,0},{20,4},{24,8},{28,12},{1,17},{... | collective-permute-start | bytes 1572872 | tf_op jit(solution)/shard_map/ppermute | solution.py:263
  10.2 79.1 %collective-permute-start.2 = (bf16[512,512]{1,0:T(8,128)(2,1)}, bf16[512,512]{1,0:T(8,128)(2,1)}, u32[]{:S(2)}, u32[]{:S(2)}) collective-permute-start(bf16[512,512]{1,0:T(8,128)(2,1)} %get-tuple-element.17), channel_id=1, source_target_pairs={{0,16},{4,20},{8,24},{12,28},{16,0},{20,4},{24,8},{28,12},{1,17},{... | collective-permute-start | bytes 1572872 | tf_op jit(solution)/shard_map/ppermute | solution.py:263
  13.1 3.6 %copy-start.10 = (f32[3,512]{1,0:T(4,128)S(1)}, f32[3,512]{1,0:T(4,128)}, u32[]{:S(2)}) copy-start(f32[3,512]{1,0:T(4,128)} %get-tuple-element.15) | copy-start | bytes 18436
  13.1 9.4 %copy-start.4 = (bf16[1,512,1536]{2,1,0:T(8,128)(2,1)S(1)}, bf16[1,512,1536]{2,1,0:T(8,128)(2,1)}, u32[]{:S(2)}) copy-start(bf16[1,512,1536]{2,1,0:T(8,128)(2,1)} %param.6) | copy-start | bytes 4718596
  13.1 9.4 %copy-start.8 = (f32[1,1536]{1,0:T(1,128)S(1)}, f32[1,1536]{1,0:T(1,128)}, u32[]{:S(2)}) copy-start(f32[1,1536]{1,0:T(1,128)} %refs_4_.5) | copy-start | bytes 18436
  13.1 9.4 %copy-start.9 = (f32[1,1536]{1,0:T(1,128)S(1)}, f32[1,1536]{1,0:T(1,128)}, u32[]{:S(2)}) copy-start(f32[1,1536]{1,0:T(1,128)} %refs_5_.5) | copy-start | bytes 18436
  13.1 67.7 %collective-permute-start.3 = (bf16[512,512]{1,0:T(8,128)(2,1)}, bf16[512,512]{1,0:T(8,128)(2,1)S(1)}, u32[]{:S(2)}, u32[]{:S(2)}) collective-permute-start(bf16[512,512]{1,0:T(8,128)(2,1)} %get-tuple-element.18), channel_id=1, source_target_pairs={{0,16},{4,20},{8,24},{12,28},{16,0},{20,4},{24,8},{28,12},{1,17},{... | collective-permute-start | bytes 1572872 | tf_op jit(solution)/shard_map/ppermute | solution.py:263
  22.6 59.1 %copy-start = (bf16[512,1536]{1,0:T(8,128)(2,1)S(1)}, bf16[512,1536]{1,0:T(8,128)(2,1)}, u32[]{:S(2)}) copy-start(bf16[512,1536]{1,0:T(8,128)(2,1)} %slice_bitcast_fusion.refs_0_) | copy-start | bytes 4718596
  22.6 59.1 %copy-start.1 = (bf16[1,512,1536]{2,1,0:T(8,128)(2,1)S(1)}, bf16[1,512,1536]{2,1,0:T(8,128)(2,1)}, u32[]{:S(2)}) copy-start(bf16[1,512,1536]{2,1,0:T(8,128)(2,1)} %param.7) | copy-start | bytes 4718596
  80.8 0.8 copy-start.6
  81.7 1.4 copy-start.5
  83.1 1.0 copy-start.7
  100.6 1.1 copy-start.2
  107.4 1.4 copy-start.3
  109.8 36.2 %collective-permute-start.4 = (bf16[512,1536]{1,0:T(8,128)(2,1)S(1)}, bf16[512,1536]{1,0:T(8,128)(2,1)S(1)}, u32[]{:S(2)}, u32[]{:S(2)}) collective-permute-start(bf16[512,1536]{1,0:T(8,128)(2,1)S(1)} %finish.1), channel_id=1, source_target_pairs={{0,28},{4,0},{8,4},{12,8},{16,12},{20,16},{24,20},{28,24},{1,29},{... | collective-permute-start | bytes 4718600 | tf_op jit(solution)/shard_map/ppermute | solution.py:263

commit v7 on v6

v7 whole, which is shorter than its diff:
```python
import functools
import math

import jax
import jax.numpy as jnp
from jax import lax
from jax.experimental import pallas as pl
from jax.experimental.pallas import tpu as pltpu
from jax.sharding import PartitionSpec as P

HDIM = 128
EPSILON = 1e-05
SCALE = 1.0 / math.sqrt(HDIM)
LOG2E = math.log2(math.e)
VMEM = 32 * 1024 * 1024
MOST = 60 * 1024 * 1024

F32 = jnp.float32
BF16 = jnp.bfloat16


def dot(a, b, contract):
    return lax.dot_general(a, b, ((contract[0], contract[1]), ((), ())), preferred_element_type=F32)


def nt(a, b):
    return dot(a, b, ((1,), (1,)))


def nn(a, b):
    return dot(a, b, ((1,), (0,)))


def block_of(tokens):
    return 256 if tokens % 256 == 0 else tokens


def masked(block, kept):
    return jnp.where(kept, block, -1e30)


def kept_keys(size):
    keys = lax.broadcasted_iota(jnp.int32, (size, size), 0)
    return keys <= lax.broadcasted_iota(jnp.int32, (size, size), 1)


def scores_of(keys, queries, j, size, kept):
    mine = queries[j * size : (j + 1) * size]
    diagonal = masked(nt(keys[j * size : (j + 1) * size], mine), kept)
    if j == 0:
        return [diagonal]
    return [nt(keys[: j * size], mine), diagonal]


def exponents(parts):
    top = functools.reduce(jnp.maximum, [jnp.max(p, axis=0, keepdims=True) for p in parts])
    exps = [jnp.exp2((p - top) * (SCALE * LOG2E)) for p in parts]
    total = sum(jnp.sum(e, axis=0, keepdims=True) for e in exps)
    return exps, total


def stacked(parts):
    return parts[0] if len(parts) == 1 else jnp.concatenate(parts, axis=0)


def normed_head(x, factor, gain_q, gain_k):
    wide = x.astype(F32)
    normed = wide * factor
    return wide, (normed * gain_q).astype(BF16), (normed * gain_k).astype(BF16), normed.astype(BF16)


def column_of(row):
    return jnp.broadcast_to(row, (HDIM, row.shape[1])).T[:, 0:1]


def inverse_rms(total, width_all):
    return lax.rsqrt(total / width_all + EPSILON)


def lanes_of(start, size):
    return (slice(None), slice(start, start + size))


def compiler(limit):
    return pltpu.CompilerParams(vmem_limit_bytes=limit)


IN_VMEM = pl.BlockSpec(memory_space=pltpu.VMEM)
ANYWHERE = pl.BlockSpec(memory_space=pl.ANY)


def forward_kernel(heads, width_all, x_ref, t_ref, gq_ref, gk_ref, *rest):
    o_ref = rest[-1]
    tokens = x_ref.shape[0]
    size = block_of(tokens)
    kept = kept_keys(size)
    factor = column_of(inverse_rms(t_ref[0:1, :], width_all))
    for h in range(heads):
        lanes = slice(h * HDIM, (h + 1) * HDIM)
        wide, q, k, v = normed_head(x_ref[:, lanes], factor, gq_ref[:, lanes], gk_ref[:, lanes])
        vt = v.T
        for j in range(tokens // size):
            exps, total = exponents(scores_of(k, q, j, size, kept))
            mixed = nn(vt[:, : (j + 1) * size], stacked(exps).astype(BF16)) * (1.0 / total)
            rows = slice(j * size, (j + 1) * size)
            o_ref[rows, lanes] = (wide[rows] + mixed.T).astype(BF16)


def forward(width_all, x, totals, gain_q, gain_k, heads, after=()):
    tokens, width = x.shape
    lanes = heads * HDIM
    block = pl.BlockSpec((tokens, lanes), lambda i: (0, i))
    gain = pl.BlockSpec((1, lanes), lambda i: (0, i))
    return pl.pallas_call(
        functools.partial(forward_kernel, heads, width_all),
        out_shape=jax.ShapeDtypeStruct(x.shape, BF16),
        grid=(width // lanes,),
        in_specs=[block, pl.BlockSpec(totals.shape, lambda i: (0, 0)), gain, gain] + [ANYWHERE] * len(after),
        out_specs=block,
        compiler_params=compiler(VMEM),
        name="forward",
    )(x, totals, gain_q, gain_k, *after)


def backward_head(x, g, factor, gain_q, gain_k):
    tokens = x.shape[0]
    size = block_of(tokens)
    kept = kept_keys(size)
    wide, q, k, v = normed_head(x, factor, gain_q, gain_k)
    kt = k.T
    blocks = tokens // size
    d_q = []
    d_k = [None] * blocks
    d_v = [None] * blocks
    for j in range(blocks):
        rows = slice(j * size, (j + 1) * size)
        exps, total = exponents(scores_of(k, q, j, size, kept))
        inverse = 1.0 / total
        weights = [e * inverse for e in exps]
        grads = [nt(v[: j * size], g[rows])] if j else []
        grads.append(nt(v[rows], g[rows]))
        delta = sum(jnp.sum(w * d, axis=0, keepdims=True) for w, d in zip(weights, grads))
        scores = stacked([(w * ((d - delta) * SCALE)).astype(BF16) for w, d in zip(weights, grads)])
        rounded = stacked([w.astype(BF16) for w in weights])
        d_q.append(nn(kt[:, : (j + 1) * size], scores).T)
        part_k = nn(scores, q[rows])
        part_v = nn(rounded, g[rows])
        for i in range(j + 1):
            mine = slice(i * size, (i + 1) * size)
            d_k[i] = part_k[mine] if d_k[i] is None else d_k[i] + part_k[mine]
            d_v[i] = part_v[mine] if d_v[i] is None else d_v[i] + part_v[mine]
    d_normed = stacked(d_q) * gain_q + stacked(d_k) * gain_k + stacked(d_v)
    return wide, d_normed


def selected(which, refs, at):
    values = [ref[lanes_of(start + at, HDIM)] for ref, start in refs]
    value = values[0]
    for i, other in enumerate(values[1:]):
        value = jnp.where(which == i + 1, other, value)
    return value


def backward_kernel(first, heads, width_all, x_at, g_at, pick_ref, *refs):
    n_x, n_g = len(x_at), len(g_at)
    unevicted = x_at[-1] is None
    xs = list(zip(refs[:n_x], [at or 0 for at in x_at]))
    gs = list(zip(refs[n_x : n_x + n_g], g_at))
    t_ref, told_ref, past_ref = refs[n_x + n_g : n_x + n_g + 3]
    a_ref, x_ref, inner_ref = refs[-3:]
    tokens, width = a_ref.shape
    factor = column_of(inverse_rms(t_ref[2:3, :], width_all))
    evicted = told_ref[:, tokens + 2 * width :] == 1.0
    ready = jnp.logical_and(pick_ref[2] == 1, jnp.logical_not(evicted))
    part = None
    for h in range(heads):
        at = h * HDIM
        mine = lanes_of(first + at, HDIM)
        gain_q = told_ref[lanes_of(tokens + first + at, HDIM)]
        gain_k = told_ref[lanes_of(tokens + width + first + at, HDIM)]
        if unevicted:
            straight, start = xs[0]
            own, own_start = xs[-1]
            x = jnp.where(evicted, straight[lanes_of(start + at, HDIM)].astype(F32), own[lanes_of(own_start + at, HDIM)].astype(F32))
            x = x.astype(BF16)
            for i, (ref, start) in enumerate(xs[1:-1]):
                x = jnp.where(pick_ref[0] == i + 1, ref[lanes_of(start + at, HDIM)], x)
        else:
            x = selected(pick_ref[0], xs, at)
        g = selected(pick_ref[1], gs, at)
        wide, d_normed = backward_head(x, g, factor, gain_q, gain_k)
        a_ref[mine] = g.astype(F32) + jnp.where(ready, 0.0, factor * d_normed)
        x_ref[mine] = x
        product = d_normed * wide
        part = product if part is None else part + product
    inner = jnp.sum(part.T, axis=0, keepdims=True)
    inner_ref[...] = inner if past_ref is None else inner + past_ref[...]


def backward(width_all, width, pick, xs, gs, totals, told, past, heads, first, sofar=(), after=()):
    tokens = totals.shape[1]
    before = 1 + len(xs) + len(gs) + 3
    return pl.pallas_call(
        functools.partial(
            backward_kernel, first, heads, width_all, tuple(at for _, at in xs), tuple(at for _, at in gs)
        ),
        out_shape=(
            jax.ShapeDtypeStruct((tokens, width), F32),
            jax.ShapeDtypeStruct((tokens, width), BF16),
            jax.ShapeDtypeStruct((1, tokens), F32),
        ),
        in_specs=[pl.BlockSpec(memory_space=pltpu.SMEM)] + [IN_VMEM] * (before - 1 + len(sofar))
        + [ANYWHERE] * len(after),
        out_specs=(IN_VMEM, IN_VMEM, IN_VMEM),
        input_output_aliases={before: 0, before + 1: 1} if sofar else {},
        compiler_params=compiler(VMEM),
        name="backward",
    )(pick, *[x for x, _ in xs], *[g for g, _ in gs], totals, told, past, *sofar, *after)


def early_kernel(heads, width_all, pick_ref, x_ref, g_ref, t_ref, gq_ref, gk_ref, a_ref, inner_ref):
    @pl.when(pl.program_id(0) == 0)
    def _():
        inner_ref[...] = jnp.zeros_like(inner_ref)

    @pl.when(pick_ref[0] == 1)
    def _():
        factor = column_of(inverse_rms(t_ref[1:2, :], width_all))
        part = None
        for h in range(heads):
            mine = lanes_of(h * HDIM, HDIM)
            g = g_ref[mine]
            wide, d_normed = backward_head(x_ref[mine], g, factor, gq_ref[mine], gk_ref[mine])
            a_ref[mine] = g.astype(F32) + factor * d_normed
            product = d_normed * wide
            part = product if part is None else part + product
        inner_ref[...] += jnp.sum(part.T, axis=0, keepdims=True)


def early_backward(width_all, pick, stash, g, totals, gain_q, gain_k, heads):
    tokens, width = g.shape
    lanes = heads * HDIM
    at = lambda i, pick: (0, i * pick[0])
    block = pl.BlockSpec((tokens, lanes), at)
    still = lambda shape: pl.BlockSpec(shape, lambda i, pick: (0, 0))
    gain = pl.BlockSpec((1, lanes), at)
    return pl.pallas_call(
        functools.partial(early_kernel, heads, width_all),
        out_shape=(jax.ShapeDtypeStruct((tokens, width), F32), jax.ShapeDtypeStruct((1, tokens), F32)),
        grid_spec=pltpu.PrefetchScalarGridSpec(
            num_scalar_prefetch=1,
            grid=(width // lanes,),
            in_specs=[
                pl.BlockSpec((None, None, tokens, lanes), lambda i, pick: (0, 0, 0, i * pick[0])),
                block, still(totals.shape), gain, gain,
            ],
            out_specs=(block, still((1, tokens))),
        ),
        compiler_params=compiler(MOST),
        name="early_backward",
    )(pick, stash, g, totals, gain_q, gain_k)


def row_of(total, inner, width_all):
    return inverse_rms(total, width_all) ** 3 * inner / width_all


def finish_kernel(lanes, width_all, pick_ref, a_ref, x_ref, t_ref, told_ref, inner_ref, o_ref):
    tokens, width = a_ref.shape
    evicted = told_ref[:, tokens + 2 * width : tokens + 2 * width + 1] == 1.0
    ready = jnp.logical_and(pick_ref[2] == 1, jnp.logical_not(evicted))
    row = jnp.where(ready, 0.0, row_of(t_ref[2:3, :], inner_ref[...], width_all))
    at = (slice(None), pl.ds(pl.program_id(0) * lanes, lanes))
    o_ref[...] = (a_ref[at] - x_ref[at].astype(F32) * column_of(row)).astype(BF16)


def finish(width_all, pick, a, x, totals, told, inner, lanes):
    tokens, width = a.shape
    return pl.pallas_call(
        functools.partial(finish_kernel, lanes, width_all),
        out_shape=jax.ShapeDtypeStruct(a.shape, BF16),
        grid=(width // lanes,),
        in_specs=[pl.BlockSpec(memory_space=pltpu.SMEM)] + [IN_VMEM] * 5,
        out_specs=pl.BlockSpec((tokens, lanes), lambda i: (0, i)),
        compiler_params=compiler(VMEM),
        name="finish",
    )(pick, a, x, totals, told, inner)


def slot_kernel(width_all, last, pick_ref, a_ref, x_ref, g_ref, t_ref, inner_ref, o_ref, kept_ref):
    special = pick_ref[1] == 1
    step = pl.program_id(0)

    @pl.when(jnp.logical_and(special, pick_ref[0] == 1))
    def _():
        row = column_of(row_of(t_ref[1:2, :], inner_ref[...], width_all))
        o_ref[...] = (a_ref[...] - x_ref[...].astype(F32) * row).astype(BF16)

    @pl.when(jnp.logical_and(special, pick_ref[0] == 0))
    def _():
        o_ref[...] = g_ref[...]

    @pl.when(jnp.logical_and(special, step == 0))
    def _():
        kept_ref[...] = o_ref[...]

    @pl.when(jnp.logical_and(jnp.logical_not(special), step == last))
    def _():
        kept_ref[...] = x_ref[...]


def slot_of(width_all, pick, a, stash, g, totals, inner, lanes):
    tokens, width = g.shape
    last = width // lanes - 1
    block = pl.BlockSpec((tokens, lanes), lambda i, pick: (0, i * pick[1]))
    still = lambda shape: pl.BlockSpec(shape, lambda i, pick: (0, 0))
    return pl.pallas_call(
        functools.partial(slot_kernel, width_all, last),
        out_shape=(jax.ShapeDtypeStruct((tokens, width), BF16), jax.ShapeDtypeStruct((tokens, lanes), BF16)),
        grid_spec=pltpu.PrefetchScalarGridSpec(
            num_scalar_prefetch=1,
            grid=(width // lanes,),
            in_specs=[
                pl.BlockSpec((tokens, lanes), lambda i, pick: (0, i * pick[0])),
                pl.BlockSpec(
                    (None, None, tokens, lanes), lambda i, pick: (0, 0, 0, jnp.where(pick[1] == 1, i, last))
                ),
                block,
                still(totals.shape),
                still(inner.shape),
            ],
            out_specs=(block, still((tokens, lanes))),
        ),
        compiler_params=compiler(MOST),
        name="slot",
    )(pick, a, stash, g, totals, inner)


def choose_kernel(n, mode_ref, *refs):
    outs = refs[-2:]
    sets = (refs[:n], refs[n:-2])
    for i, (out, options) in enumerate(zip(outs, sets)):
        for m, ref in enumerate(options):

            @pl.when(mode_ref[i] == m)
            def _():
                out[...] = ref[...]


def choose(mode, first, second, tokens, step, after=()):
    def spec(array, at):
        if isinstance(at, tuple):
            return pl.BlockSpec((None, None, tokens, step), lambda i, mode: (0, at[0], 0, at[1]))
        return pl.BlockSpec((tokens, step), lambda i, mode: (0, at))

    piece = pl.BlockSpec((tokens, step), lambda i, mode: (0, 0))

    def kernel(mode_ref, *refs):
        used = len(first) + len(second)
        choose_kernel(len(first), mode_ref, *refs[:used], *refs[-2:])

    return pl.pallas_call(
        kernel,
        out_shape=[jax.ShapeDtypeStruct((tokens, step), BF16)] * 2,
        grid_spec=pltpu.PrefetchScalarGridSpec(
            num_scalar_prefetch=1,
            grid=(1,),
            in_specs=[spec(*o) for o in (*first, *second)] + [ANYWHERE] * len(after),
            out_specs=[piece] * 2,
        ),
        compiler_params=compiler(VMEM),
        name="choose",
    )(mode, *[array for array, _ in (*first, *second)], *after)


def sums_kernel(pieces, pick_ref, current_ref, stash_ref, gq_ref, gk_ref, rows_ref, told_ref):
    step = pl.program_id(0)
    tokens = current_ref.shape[0]

    def total(x):
        wide = x.astype(F32)
        square = wide * wide
        sums = sum(square[:, i : i + HDIM] for i in range(0, square.shape[1], HDIM))
        return jnp.sum(sums.T, axis=0, keepdims=True)

    rows = jnp.concatenate([total(current_ref[...]), total(stash_ref[0]), total(stash_ref[1])], axis=0)

    @pl.when(step == 0)
    def _():
        rows_ref[...] = rows

    @pl.when(step > 0)
    def _():
        rows_ref[...] += rows

    @pl.when(step == pieces - 1)
    def _():
        width = gq_ref.shape[1]
        told_ref[:, :tokens] = rows_ref[1:2, :]
        told_ref[:, tokens : tokens + width] = gq_ref[...]
        told_ref[:, tokens + width : tokens + 2 * width] = gk_ref[...]
        told_ref[:, tokens + 2 * width :] = jnp.full((1, HDIM), pick_ref[2].astype(F32))


def sums_of(pick, current, stash, gain_q, gain_k, lanes):
    tokens, width = current.shape
    pieces = width // lanes
    still = lambda *shape: pl.BlockSpec(shape, lambda i, pick: (0, 0))
    told = tokens + 2 * width + HDIM
    return pl.pallas_call(
        functools.partial(sums_kernel, pieces),
        out_shape=(jax.ShapeDtypeStruct((3, tokens), F32), jax.ShapeDtypeStruct((1, told), F32)),
        grid_spec=pltpu.PrefetchScalarGridSpec(
            num_scalar_prefetch=1,
            grid=(pieces,),
            in_specs=[
                pl.BlockSpec((tokens, lanes), lambda i, pick: (0, i)),
                pl.BlockSpec((None, 2, tokens, lanes), lambda i, pick: (0, 0, 0, i)),
                still(1, width),
                still(1, width),
            ],
            out_specs=(still(3, tokens), still(1, told)),
        ),
        compiler_params=compiler(MOST),
        name="sums",
    )(pick, current, stash, gain_q, gain_k)


def pack_kernel(pieces, pick_ref, stash_ref, g_ref, *refs):
    away_ref, first_ref, last_ref = refs[-3:]
    step = pl.program_id(0)

    @pl.when(step == 0)
    def _():
        away_ref[...] = stash_ref[...]

    for mine, out in ((step < pieces - 1, first_ref), (step == pieces - 1, last_ref)):

        @pl.when(jnp.logical_and(mine, pick_ref[1] == 1))
        def _():
            out[...] = stash_ref[...]

        @pl.when(jnp.logical_and(mine, pick_ref[1] == 0))
        def _():
            out[...] = g_ref[...]


def pack(pick, stash, g, lanes, after=()):
    tokens, width = g.shape
    pieces = width // lanes
    piece = pl.BlockSpec((tokens, lanes), lambda i, pick: (0, 0))
    return pl.pallas_call(
        functools.partial(pack_kernel, pieces),
        out_shape=[jax.ShapeDtypeStruct((tokens, w), BF16) for w in (lanes, width - lanes, lanes)],
        grid_spec=pltpu.PrefetchScalarGridSpec(
            num_scalar_prefetch=1,
            grid=(pieces,),
            in_specs=[
                pl.BlockSpec((None, None, tokens, lanes), lambda i, pick: (0, 1, 0, i * pick[1])),
                pl.BlockSpec((tokens, lanes), lambda i, pick: (0, i)),
            ]
            + [ANYWHERE] * len(after),
            out_specs=[
                piece, pl.BlockSpec((tokens, lanes), lambda i, pick: (0, jnp.minimum(i, pieces - 2))), piece
            ],
        ),
        compiler_params=compiler(MOST),
        name="pack",
    )(pick, stash, g, *after)


def join_kernel(rows_ref, told_ref, held_ref, o_ref):
    tokens = rows_ref.shape[1]
    o_ref[0:2, :] = rows_ref[0:2, :]
    evicted = told_ref[:, told_ref.shape[1] - 1 :] == 1.0
    o_ref[2:3, :] = jnp.where(evicted, held_ref[2:3, :], told_ref[:, :tokens])


def join(rows, told, held):
    return pl.pallas_call(
        join_kernel,
        out_shape=jax.ShapeDtypeStruct(rows.shape, F32),
        in_specs=[IN_VMEM] * 3,
        out_specs=IN_VMEM,
        compiler_params=compiler(VMEM),
        name="join",
    )(rows, told, held)


def send(x, pairs):
    return lax.ppermute(x, "section", pairs)


def local(width_all, layer_input, grad_input, stashed, eviction, query_gain, key_gain):
    n = lax.axis_size("section")
    half = n // 2
    special = (0, half)
    me = lax.axis_index("section")

    prior = [(s, (s - 1) % n) for s in range(n)]
    inside = [(s, s - 1) for s in range(n) if s not in special]
    within = inside + [(half, n - 1), (0, half - 1)]
    around = [p for p in within if p[0] not in (half, n - 2)] + [(half, n - 3), (n - 2, n - 1)]
    back = [(n - 1, n - 3), (n - 3, n - 1)]
    to_partner = [(s, (s + half) % n) for s in range(n) if s not in special]
    holder = [((s + half) % n, (s - 1) % n) for s in range(n)]
    direct = [p for p in holder if p[0] not in special] + [(half, half - 1), (0, n - 1)]

    current = layer_input[0]
    upstream = grad_input[0]
    tokens, width = current.shape
    heads = width // HDIM // 3
    step = heads * HDIM

    flag = lambda f: jnp.asarray(f).astype(jnp.int32)
    is_special = jnp.logical_or(me == 0, me == half)
    kept_here = jnp.logical_and(me == half, eviction[0] == 0)
    crossed = jnp.logical_or(me == half - 1, me == n - 1)
    early_pick = jnp.stack([flag(kept_here), flag(is_special), eviction[0]])
    mode = jnp.stack([jnp.where(is_special, 2, eviction[0]), flag(is_special)])
    mode_first = jnp.stack([eviction[0], flag(False)])
    final = flag(me == half - 1)
    take = jnp.stack([
        jnp.where(crossed, jnp.where(me == n - 1, 2, 1), 0),
        jnp.where(crossed, 2, jnp.where(me == n - 3, 1, 0)),
        final,
    ])
    take_first = jnp.stack([flag(crossed), flag(crossed), final])

    rows, told = sums_of(early_pick, current, stashed, query_gain, key_gain, step)
    told = send(told, prior)
    held_rows = send(rows, holder)
    away, early_first, early_last = pack(early_pick, stashed, upstream, step, (told, held_rows))
    fetched = send(away, to_partner)
    early_first = send(early_first, within)
    early_last = send(early_last, around)
    totals = lax.psum(join(rows, told, held_rows), "tensor")

    own_a, own_inner = early_backward(width_all, early_pick, stashed, upstream, totals, query_gain, key_gain, heads)
    sent, away = choose(
        mode_first, [(stashed, (0, 0)), (fetched, 0)], [(stashed, (1, 1))], tokens, step, (own_inner,)
    )
    fetched = send(away, to_partner)
    passed = [send(sent, inside)]
    last_back = send(early_last, back)
    own_inner = lax.psum(own_inner, "tensor")
    slot, last = slot_of(width_all, early_pick, own_a, stashed, upstream, totals, own_inner, step)
    kept = send(last, prior)
    sent, last = choose(
        mode, [(stashed, (0, 1)), (fetched, 0), (slot, 1)], [(stashed, (1, 2)), (slot, 2)], tokens, step
    )
    straight = send(last, direct)
    passed.append(send(sent, prior))
    output = forward(width_all, current, totals, query_gain, key_gain, heads, (sent,))

    share = functools.partial(backward, width_all, width)
    a, x, inner = share(
        take_first, [(passed[0], 0), (early_first, 0)], [(early_first, 0), (kept, 0)], totals, told,
        jnp.zeros((1, tokens), F32), heads, 0, (), (output,),
    )
    a, x, inner = share(
        take_first, [(passed[1], 0), (early_first, step)], [(early_first, step), (passed[1], 0)],
        totals, told, inner, heads, step, (a, x),
    )
    a, x, inner = share(
        take, [(straight, 0), (early_last, 0), (last_back, 0), (kept, None)],
        [(early_last, 0), (last_back, 0), (straight, 0)], totals, told, inner, heads, 2 * step, (a, x),
    )
    inner = lax.psum(inner, "tensor")
    result = finish(width_all, take, a, x, totals, told, inner, step)
    return (output[None], result[None])


def solution(mesh):
    placed = (
        P("section", None, "tensor"),
        P("section", None, "tensor"),
        P("section", None, None, "tensor"),
        P("section"),
        P("section", "tensor"),
        P("section", "tensor"),
    )

    def whole(layer_input, *others):
        return jax.shard_map(
            functools.partial(local, layer_input.shape[-1]),
            mesh=mesh,
            in_specs=placed,
            out_specs=(P("section", None, "tensor"), P("section", None, "tensor")),
            check_vma=False,
        )(layer_input, *others)

    return whole
```

time: 148 us -> 159 us (1.074); the launches traced: 147 us -> 156 us
  waiting for transfers between devices: 83.5 us -> 10.2 us
  starting transfers between devices: 10.5 us -> 60.9 us
  Pallas kernels: 29.7 us -> 53.2 us
  blocking collectives: 11.4 us -> 18.8 us
    ppermute x5 -> x11, waiting for transfers between devices: 83.5 us -> 10.2 us  [send(): return lax.ppermute(x, 'section', pairs)]
    ppermute x5 -> x11, starting transfers between devices: 10.5 us -> 60.9 us  [send(): return lax.ppermute(x, 'section', pairs)]
    pallas_call x6 -> x12, Pallas kernels: 29.7 us -> 53.2 us  [the longest x3 19.6 us: backward(): pl.pallas_call(functools.partial(backward_kernel, first, heads, width_all...]
    psum x1 -> x2, blocking collectives: 5.76 us -> 13.2 us  [the longest x1 6.85 us: local(): own_inner = lax.psum(own_inner, 'tensor')]
    unnamed x23 -> x38, local copies, waits for them, and re-layouts: 6.99 us -> 10.3 us
    squeeze x1 -> x0, local copies, waits for them, and re-layouts: 2.75 us -> none  [local(): own = stashed[0, 0]]
  transfers between devices with their start and end apart: 5 -> 11, of which waited for: 2 -> 2; matrix products, arithmetic and copies ran while one was open for 2% -> 0% of each run, Pallas kernels for 12% -> 22%
where the time goes in v7:
time: 159 us; the launch traced here: 156 us
  starting transfers between devices  60.9 us (38%)
  Pallas kernels  53.2 us (33%)
  blocking collectives  18.8 us (12%)
  local copies, waits for them, and re-layouts  10.3 us (6%)
  waiting for transfers between devices  10.2 us (6%)
    ppermute x11, starting transfers between devices, send(): return lax.ppermute(x, 'section', pairs)  60.9 us
    pallas_call x3, Pallas kernels, backward(): pl.pallas_call(functools.partial(backward_kernel, first, heads, width_all...  19.6 us
    unnamed x38, local copies, waits for them, and re-layouts  10.3 us
    ppermute x11, waiting for transfers between devices, send(): return lax.ppermute(x, 'section', pairs)  10.2 us
    pallas_call x1, Pallas kernels, forward(): pl.pallas_call(functools.partial(forward_kernel, heads, width_all), out_s...  7.46 us
    psum x1, blocking collectives, local(): own_inner = lax.psum(own_inner, 'tensor')  6.85 us
    psum x1, blocking collectives, local(): totals = lax.psum(join(rows, told, held_rows), 'tensor')  6.31 us
    psum x1, blocking collectives, local(): inner = lax.psum(inner, 'tensor')  5.63 us
  transfers between devices with their start and end apart: 11, of which 2 were waited for; matrix products, arithmetic and copies ran while one was open for 0% of the time, Pallas kernels for 22%

profile of v7, /device:TPU:0, one launch (start us, length us, event | category | flops | bytes accessed | tf_op | source)
XLA Modules:
  0.0 155.6 jit_solution(14131876371516949876)
XLA Ops:
  1.3 0.6 pad_add_fusion.pick_ref
  1.8 4.9 %sums.1 = (f32[3,512]{1,0:T(4,128)}, f32[1,3712]{1,0:T(1,128)}) custom-call(s32[3]{0:T(128)} %pad_add_fusion.pick_ref, bf16[512,1536]{1,0:T(8,128)(2,1)} %bitcast.14, bf16[1,2,512,1536]{3,2,1,0:T(8,128)(2,1)} %refs_3_.1, f32[1,1536]{1,0:T(1,128)} %gq_ref.5, f32[1,1536]{1,0:T(1,128)} %gk_ref.5), custom_call_target="tpu_custom_call" | custom-call | tf_op jit(solution)/shard_map/sums/pallas_call | solution.py:410
  6.7 6.0 %collective-permute-start = (f32[1,3712]{1,0:T(1,128)}, f32[1,3712]{1,0:T(1,128)S(1)}, u32[]{:S(2)}, u32[]{:S(2)}) collective-permute-start(f32[1,3712]{1,0:T(1,128)} %get-tuple-element.25), channel_id=1, source_target_pairs={{0,28},{4,0},{8,4},{12,8},{16,12},{20,16},{24,20},{28,24},{1,29},{... | collective-permute-start | bytes 44552 | tf_op jit(solution)/shard_map/ppermute | solution.py:491
  12.7 0.0 collective-permute-start.1
  12.7 5.7 %collective-permute-done.1.held_ref.refs_1_ = f32[3,512]{1,0:T(4,128)S(1)} collective-permute-done((f32[3,512]{1,0:T(4,128)}, f32[3,512]{1,0:T(4,128)S(1)}, u32[]{:S(2)}, u32[]{:S(2)}) %collective-permute-start.1) | collective-permute-done | bytes 6176 | tf_op jit(solution)/shard_map/ppermute | solution.py:491
  18.4 0.0 collective-permute-done.told_ref.refs_0_.refs_5_.refs_8_
  18.4 0.6 copy-done.13
  19.0 0.0 copy-done.7
  19.0 4.8 %pack.1 = (bf16[512,512]{1,0:T(8,128)(2,1)}, bf16[512,1024]{1,0:T(8,128)(2,1)}, bf16[512,512]{1,0:T(8,128)(2,1)}) custom-call(s32[3]{0:T(128)} %pad_add_fusion.pick_ref, bf16[1,2,512,1536]{3,2,1,0:T(8,128)(2,1)} %refs_3_.1, bf16[512,1536]{1,0:T(8,128)(2,1)} %bitcast.17, f32[1,3712]{1,0:T(1,128)} %copy-done.7, f32[3,512]{1,0:T(4,128)} %copy-done.13), custom_call_target="tpu_custom_call" | custom-call | tf_op jit(solution)/shard_map/pack/pallas_call | solution.py:452
  23.8 1.5 collective-permute-start.2
  25.2 0.1 pad_add_fusion.2.mode_ref
  25.3 0.0 copy-done.17
  25.3 0.7 copy-done.8
  26.0 0.7 copy-done.14
  26.7 0.1 join.1
  26.8 6.3 %psum.21.t_ref.refs_4_.refs_7_ = f32[3,512]{1,0:T(4,128)} all-reduce(f32[3,512]{1,0:T(4,128)S(1)} %join.1), channel_id=1, replica_groups=mesh['section'=8,'tensor'=4] {'tensor'}, use_global_device_ids=true, to_apply=%region_0.1 | all-reduce | flops 1536 | bytes 12288 | tf_op jit(solution)/shard_map/psum | solution.py:537
  33.1 3.2 %early_backward.1 = (f32[512,1536]{1,0:T(8,128)}, f32[1,512]{1,0:T(1,128)}) custom-call(s32[3]{0:T(128)} %pad_add_fusion.pick_ref, bf16[1,2,512,1536]{3,2,1,0:T(8,128)(2,1)} %refs_3_.1, bf16[512,1536]{1,0:T(8,128)(2,1)} %bitcast.18, f32[3,512]{1,0:T(4,128)} %psum.21.t_ref.refs_4_.refs_7_, f32[1,1536]{1,0:T(1,128)} %gq_ref.5, f32[1,1536]{1,0:T(1,128)} %gk_ref.5), custom_call_target="tpu_custom_call" | custom-call | tf_op jit(solution)/shard_map/early_backward/pallas_call | solution.py:247
  36.3 2.2 %collective-permute-start.9 = (bf16[512,1024]{1,0:T(8,128)(2,1)}, bf16[512,1024]{1,0:T(8,128)(2,1)}, u32[]{:S(2)}, u32[]{:S(2)}) collective-permute-start(bf16[512,1024]{1,0:T(8,128)(2,1)} %get-tuple-element.35), channel_id=1, source_target_pairs={{4,0},{8,4},{12,8},{20,16},{24,20},{28,24},{16,28},{0,12},{5,1},{9... | collective-permute-start | bytes 3145736 | tf_op jit(solution)/shard_map/ppermute | solution.py:491
  38.4 0.0 collective-permute-done.2.refs_1_
  38.4 0.0 copy-done
  38.4 0.7 copy-done.15
  39.1 2.5 %choose.2 = (bf16[512,512]{1,0:T(8,128)(2,1)S(1)}, bf16[512,512]{1,0:T(8,128)(2,1)}) custom-call(s32[2]{0:T(128)S(1)} %pad_add_fusion.2.mode_ref, bf16[1,2,512,1536]{3,2,1,0:T(8,128)(2,1)S(1)} %copy-done, bf16[512,512]{1,0:T(8,128)(2,1)} %collective-permute-done.2.refs_1_, bf16[1,2,512,1536]{3,2,1,0:T(8,128)(2,1)S(1)} %copy-done, f32[1,512]{1,0:T(1,128)S(1)} %copy-done.15), custom_call_target="tpu_custom_call" | custom-call | tf_op jit(solution)/shard_map/choose/pallas_call | solution.py:362
  41.6 0.8 copy-done.18
  42.4 1.5 collective-permute-start.3
  43.9 0.0 copy-done.16
  43.9 6.8 %psum.22.inner_ref = f32[1,512]{1,0:T(1,128)} all-reduce(f32[1,512]{1,0:T(1,128)S(1)} %copy-done.16), channel_id=1, replica_groups=mesh['section'=8,'tensor'=4] {'tensor'}, use_global_device_ids=true, to_apply=%region_1.2 | all-reduce | flops 512 | bytes 4096 | tf_op jit(solution)/shard_map/psum | solution.py:546
  50.7 14.3 %collective-permute-start.5 = (bf16[512,512]{1,0:T(8,128)(2,1)}, bf16[512,512]{1,0:T(8,128)(2,1)}, u32[]{:S(2)}, u32[]{:S(2)}) collective-permute-start(bf16[512,512]{1,0:T(8,128)(2,1)} %get-tuple-element.33), channel_id=1, source_target_pairs={{4,0},{8,4},{12,8},{20,16},{28,24},{0,12},{16,20},{24,28},{5,1},{9... | collective-permute-start | bytes 1572872 | tf_op jit(solution)/shard_map/ppermute | solution.py:491
  65.0 5.2 %slot.1 = (bf16[512,1536]{1,0:T(8,128)(2,1)}, bf16[512,512]{1,0:T(8,128)(2,1)}) custom-call(s32[3]{0:T(128)} %pad_add_fusion.pick_ref, f32[512,1536]{1,0:T(8,128)} %get-tuple-element.29.a_ref, bf16[1,2,512,1536]{3,2,1,0:T(8,128)(2,1)} %refs_3_.1, bf16[512,1536]{1,0:T(8,128)(2,1)} %bitcast.19, f32[3,512]{1,0:T(4,128)} %psum.21.t_ref.refs_4_.refs_7_, ...), custom_call_target="tpu_custom_call" | custom-call | tf_op jit(solution)/shard_map/slot/pallas_call | solution.py:317
  70.2 0.0 collective-permute-start.7
  70.2 0.1 pad_add_fusion.1.mode_ref
  70.3 1.3 collective-permute-start.10
  71.5 0.0 collective-permute-done.3.refs_1_
  71.6 0.0 copy-done.1
  71.6 0.0 copy-start.4
  71.6 1.4 copy-done.4
  73.0 2.7 %choose.3 = (bf16[512,512]{1,0:T(8,128)(2,1)}, bf16[512,512]{1,0:T(8,128)(2,1)}) custom-call(s32[2]{0:T(128)S(1)} %pad_add_fusion.1.mode_ref, bf16[1,2,512,1536]{3,2,1,0:T(8,128)(2,1)S(1)} %copy-done.1, bf16[512,512]{1,0:T(8,128)(2,1)} %collective-permute-done.3.refs_1_, bf16[512,1536]{1,0:T(8,128)(2,1)S(1)} %copy-done.4, ...), custom_call_target="tpu_custom_call" | custom-call | tf_op jit(solution)/shard_map/choose/pallas_call | solution.py:362
  75.7 9.0 %collective-permute-start.8 = (bf16[512,512]{1,0:T(8,128)(2,1)}, bf16[512,512]{1,0:T(8,128)(2,1)}, u32[]{:S(2)}, u32[]{:S(2)}) collective-permute-start(bf16[512,512]{1,0:T(8,128)(2,1)} %get-tuple-element.31.rest_0_), channel_id=1, source_target_pairs={{0,28},{4,0},{8,4},{12,8},{16,12},{20,16},{24,20},{28,24},{1,29},{... | collective-permute-start | bytes 1572872 | tf_op jit(solution)/shard_map/ppermute | solution.py:491
  84.6 0.0 collective-permute-done.5.refs_1_.refs_4_
  84.6 1.5 collective-permute-start.6
  86.1 4.5 %collective-permute-done.7.refs_3_ = bf16[512,512]{1,0:T(8,128)(2,1)} collective-permute-done((bf16[512,512]{1,0:T(8,128)(2,1)}, bf16[512,512]{1,0:T(8,128)(2,1)}, u32[]{:S(2)}, u32[]{:S(2)}) %collective-permute-start.7) | collective-permute-done | bytes 524320 | tf_op jit(solution)/shard_map/ppermute | solution.py:491
  90.6 23.8 %collective-permute-start.4 = (bf16[512,512]{1,0:T(8,128)(2,1)}, bf16[512,512]{1,0:T(8,128)(2,1)}, u32[]{:S(2)}, u32[]{:S(2)}) collective-permute-start(bf16[512,512]{1,0:T(8,128)(2,1)} %get-tuple-element.32), channel_id=1, source_target_pairs={{20,0},{24,4},{28,8},{4,16},{8,20},{12,24},{16,12},{0,28},{21,1},{... | collective-permute-start | bytes 1572872 | tf_op jit(solution)/shard_map/ppermute | solution.py:491
  114.4 0.1 add_add_fusion.1.pick_ref
  114.5 0.1 add_add_fusion.pick_ref
  114.5 0.0 copy-done.10
  114.5 0.0 copy-done.11
  114.5 0.0 copy-done.12
  114.5 0.0 copy-start.5
  114.6 1.4 copy-done.5
  116.0 7.5 %forward.1.refs_7_ = bf16[512,1536]{1,0:T(8,128)(2,1)} custom-call(bf16[512,1536]{1,0:T(8,128)(2,1)S(1)} %bitcast.15, f32[3,512]{1,0:T(4,128)S(1)} %copy-done.10, f32[1,1536]{1,0:T(1,128)S(1)} %copy-done.11, f32[1,1536]{1,0:T(1,128)S(1)} %copy-done.12, bf16[512,512]{1,0:T(8,128)(2,1)} %get-tuple-element.31.rest_0_), custom_call_target="tpu_custom_call" | custom-call | tf_op jit(solution)/shard_map/forward/pallas_call | solution.py:114
  123.4 0.0 collective-permute-done.10.refs_0_
  123.4 0.0 collective-permute-done.9.refs_1_.refs_2_
  123.5 0.0 copy-start.6
  123.5 1.4 copy-done.6
  124.9 6.4 %backward.3 = (f32[512,1536]{1,0:T(8,128)S(1)}, bf16[512,1536]{1,0:T(8,128)(2,1)S(1)}, f32[1,512]{1,0:T(1,128)S(1)}) custom-call(s32[3]{0:T(128)S(1)} %add_add_fusion.1.pick_ref, bf16[512,512]{1,0:T(8,128)(2,1)} %collective-permute-done.10.refs_0_, bf16[512,1024]{1,0:T(8,128)(2,1)} %collective-permute-done.9.refs_1_.refs_2_, ...), custom_call_target="tpu_custom_call" | custom-call | tf_op jit(solution)/shard_map/backward/pallas_call | solution.py:203
  131.3 0.0 collective-permute-done.8.refs_0_.refs_3_
  131.3 6.6 %backward.4 = (f32[512,1536]{1,0:T(8,128)S(1)}, bf16[512,1536]{1,0:T(8,128)(2,1)S(1)}, f32[1,512]{1,0:T(1,128)S(1)}) custom-call(s32[3]{0:T(128)S(1)} %add_add_fusion.1.pick_ref, bf16[512,512]{1,0:T(8,128)(2,1)} %collective-permute-done.8.refs_0_.refs_3_, ...), custom_call_target="tpu_custom_call", output_to_operand_aliasing={{0}: (8, {}), {1}: (9, {})} | custom-call | tf_op jit(solution)/shard_map/backward/pallas_call | solution.py:203
  137.9 0.0 collective-permute-done.6.refs_2_.refs_5_
  137.9 0.0 collective-permute-done.4.refs_0_.refs_6_
  137.9 6.7 %backward.5 = (f32[512,1536]{1,0:T(8,128)S(1)}, bf16[512,1536]{1,0:T(8,128)(2,1)S(1)}, f32[1,512]{1,0:T(1,128)S(1)}) custom-call(s32[3]{0:T(128)S(1)} %add_add_fusion.pick_ref, bf16[512,512]{1,0:T(8,128)(2,1)} %collective-permute-done.4.refs_0_.refs_6_, ...), custom_call_target="tpu_custom_call", output_to_operand_aliasing={{0}: (11, {}), {1}: (12, {})} | custom-call | tf_op jit(solution)/shard_map/backward/pallas_call | solution.py:203
  144.5 0.0 copy-start.2
  144.6 1.1 copy-done.2
  145.7 5.6 %psum.23.inner_ref = f32[1,512]{1,0:T(1,128)S(1)} all-reduce(f32[1,512]{1,0:T(1,128)S(1)} %get-tuple-element.45), channel_id=1, replica_groups=mesh['section'=8,'tensor'=4] {'tensor'}, use_global_device_ids=true, to_apply=%region_2.3 | all-reduce | flops 512 | bytes 4096 | tf_op jit(solution)/shard_map/psum | solution.py:569
  151.3 1.4 copy-done.3
  152.7 2.9 %finish.1 = bf16[512,1536]{1,0:T(8,128)(2,1)} custom-call(s32[3]{0:T(128)S(1)} %add_add_fusion.pick_ref, f32[512,1536]{1,0:T(8,128)S(1)} %get-tuple-element.43.a_ref, bf16[512,1536]{1,0:T(8,128)(2,1)S(1)} %copy-done.3, f32[3,512]{1,0:T(4,128)S(1)} %copy-done.10, f32[1,3712]{1,0:T(1,128)S(1)} %copy-done.9, f32[1,512]{1,0:T(1,128)S(1)} %psum.23.inner_ref), custom_call_target="tpu_custom_call" | custom-call | tf_op jit(solution)/shard_map/finish/pallas_call | solution.py:279
  (17 shorter events, 0.0 us)
Async XLA Ops:
  6.7 11.7 %collective-permute-start = (f32[1,3712]{1,0:T(1,128)}, f32[1,3712]{1,0:T(1,128)S(1)}, u32[]{:S(2)}, u32[]{:S(2)}) collective-permute-start(f32[1,3712]{1,0:T(1,128)} %get-tuple-element.25), channel_id=1, source_target_pairs={{0,28},{4,0},{8,4},{12,8},{16,12},{20,16},{24,20},{28,24},{1,29},{... | collective-permute-start | bytes 44552 | tf_op jit(solution)/shard_map/ppermute | solution.py:491
  12.7 5.7 %collective-permute-start.1 = (f32[3,512]{1,0:T(4,128)}, f32[3,512]{1,0:T(4,128)S(1)}, u32[]{:S(2)}, u32[]{:S(2)}) collective-permute-start(f32[3,512]{1,0:T(4,128)} %get-tuple-element.24.rows_ref), channel_id=1, source_target_pairs={{16,28},{20,0},{24,4},{28,8},{0,12},{4,16},{8,20},{12,24},{17,29},... | collective-permute-start | bytes 18440 | tf_op jit(solution)/shard_map/ppermute | solution.py:491
  18.4 0.6 copy-start.13
  18.4 0.6 copy-start.7
  19.0 6.3 %copy-start.17 = (f32[3,512]{1,0:T(4,128)S(1)}, f32[3,512]{1,0:T(4,128)}, u32[]{:S(2)}) copy-start(f32[3,512]{1,0:T(4,128)} %get-tuple-element.24.rows_ref) | copy-start | bytes 18436
  23.8 14.7 %collective-permute-start.2 = (bf16[512,512]{1,0:T(8,128)(2,1)}, bf16[512,512]{1,0:T(8,128)(2,1)}, u32[]{:S(2)}, u32[]{:S(2)}) collective-permute-start(bf16[512,512]{1,0:T(8,128)(2,1)} %get-tuple-element.26), channel_id=1, source_target_pairs={{4,20},{8,24},{12,28},{20,4},{24,8},{28,12},{5,21},{9,25},{13,29},... | collective-permute-start | bytes 1572872 | tf_op jit(solution)/shard_map/ppermute | solution.py:491
  25.3 0.7 copy-start.8
  26.0 0.7 copy-start.14
  33.1 5.3 %copy-start = (bf16[1,2,512,1536]{3,2,1,0:T(8,128)(2,1)S(1)}, bf16[1,2,512,1536]{3,2,1,0:T(8,128)(2,1)}, u32[]{:S(2)}) copy-start(bf16[1,2,512,1536]{3,2,1,0:T(8,128)(2,1)} %refs_3_.1) | copy-start | bytes 9437188
  36.3 87.2 %collective-permute-start.9 = (bf16[512,1024]{1,0:T(8,128)(2,1)}, bf16[512,1024]{1,0:T(8,128)(2,1)}, u32[]{:S(2)}, u32[]{:S(2)}) collective-permute-start(bf16[512,1024]{1,0:T(8,128)(2,1)} %get-tuple-element.35), channel_id=1, source_target_pairs={{4,0},{8,4},{12,8},{20,16},{24,20},{28,24},{16,28},{0,12},{5,1},{9... | collective-permute-start | bytes 3145736 | tf_op jit(solution)/shard_map/ppermute | solution.py:491
  38.4 0.7 copy-start.15
  39.1 4.8 %copy-start.16 = (f32[1,512]{1,0:T(1,128)S(1)}, f32[1,512]{1,0:T(1,128)}, u32[]{:S(2)}) copy-start(f32[1,512]{1,0:T(1,128)} %get-tuple-element.27.refs_3_) | copy-start | bytes 6148
  41.6 0.8 copy-start.18
  42.4 29.1 %collective-permute-start.3 = (bf16[512,512]{1,0:T(8,128)(2,1)}, bf16[512,512]{1,0:T(8,128)(2,1)}, u32[]{:S(2)}, u32[]{:S(2)}) collective-permute-start(bf16[512,512]{1,0:T(8,128)(2,1)} %get-tuple-element.28), channel_id=1, source_target_pairs={{4,20},{8,24},{12,28},{20,4},{24,8},{28,12},{5,21},{9,25},{13,29},... | collective-permute-start | bytes 1572872 | tf_op jit(solution)/shard_map/ppermute | solution.py:491
  50.7 33.9 %collective-permute-start.5 = (bf16[512,512]{1,0:T(8,128)(2,1)}, bf16[512,512]{1,0:T(8,128)(2,1)}, u32[]{:S(2)}, u32[]{:S(2)}) collective-permute-start(bf16[512,512]{1,0:T(8,128)(2,1)} %get-tuple-element.33), channel_id=1, source_target_pairs={{4,0},{8,4},{12,8},{20,16},{28,24},{0,12},{16,20},{24,28},{5,1},{9... | collective-permute-start | bytes 1572872 | tf_op jit(solution)/shard_map/ppermute | solution.py:491
  65.0 6.6 %copy-start.1 = (bf16[1,2,512,1536]{3,2,1,0:T(8,128)(2,1)S(1)}, bf16[1,2,512,1536]{3,2,1,0:T(8,128)(2,1)}, u32[]{:S(2)}) copy-start(bf16[1,2,512,1536]{3,2,1,0:T(8,128)(2,1)} %refs_3_.1) | copy-start | bytes 9437188
  70.2 20.4 %collective-permute-start.7 = (bf16[512,512]{1,0:T(8,128)(2,1)}, bf16[512,512]{1,0:T(8,128)(2,1)}, u32[]{:S(2)}, u32[]{:S(2)}) collective-permute-start(bf16[512,512]{1,0:T(8,128)(2,1)} %get-tuple-element.34), channel_id=1, source_target_pairs={{0,28},{4,0},{8,4},{12,8},{16,12},{20,16},{24,20},{28,24},{1,29},{... | collective-permute-start | bytes 1572872 | tf_op jit(solution)/shard_map/ppermute | solution.py:491
  70.3 53.2 %collective-permute-start.10 = (bf16[512,512]{1,0:T(8,128)(2,1)}, bf16[512,512]{1,0:T(8,128)(2,1)}, u32[]{:S(2)}, u32[]{:S(2)}) collective-permute-start(bf16[512,512]{1,0:T(8,128)(2,1)} %copy-done.18), channel_id=1, source_target_pairs={{4,0},{8,4},{12,8},{20,16},{24,20},{28,24},{5,1},{9,5},{13,9},{21,... | collective-permute-start | bytes 1572872 | tf_op jit(solution)/shard_map/ppermute | solution.py:491
  71.6 1.4 copy-start.4
  73.0 41.6 %copy-start.10 = (f32[3,512]{1,0:T(4,128)S(1)}, f32[3,512]{1,0:T(4,128)}, u32[]{:S(2)}) copy-start(f32[3,512]{1,0:T(4,128)} %psum.21.t_ref.refs_4_.refs_7_) | copy-start | bytes 18436
  73.0 41.6 %copy-start.11 = (f32[1,1536]{1,0:T(1,128)S(1)}, f32[1,1536]{1,0:T(1,128)}, u32[]{:S(2)}) copy-start(f32[1,1536]{1,0:T(1,128)} %gq_ref.5) | copy-start | bytes 18436
  73.0 41.6 %copy-start.12 = (f32[1,1536]{1,0:T(1,128)S(1)}, f32[1,1536]{1,0:T(1,128)}, u32[]{:S(2)}) copy-start(f32[1,1536]{1,0:T(1,128)} %gk_ref.5) | copy-start | bytes 18436
  75.7 55.6 %collective-permute-start.8 = (bf16[512,512]{1,0:T(8,128)(2,1)}, bf16[512,512]{1,0:T(8,128)(2,1)}, u32[]{:S(2)}, u32[]{:S(2)}) collective-permute-start(bf16[512,512]{1,0:T(8,128)(2,1)} %get-tuple-element.31.rest_0_), channel_id=1, source_target_pairs={{0,28},{4,0},{8,4},{12,8},{16,12},{20,16},{24,20},{28,24},{1,29},{... | collective-permute-start | bytes 1572872 | tf_op jit(solution)/shard_map/ppermute | solution.py:491
  84.6 53.2 %collective-permute-start.6 = (bf16[512,512]{1,0:T(8,128)(2,1)}, bf16[512,512]{1,0:T(8,128)(2,1)}, u32[]{:S(2)}, u32[]{:S(2)}) collective-permute-start(bf16[512,512]{1,0:T(8,128)(2,1)} %collective-permute-done.5.refs_1_.refs_4_), channel_id=1, source_target_pairs={{28,20},{20,28},{29,21},{21,29},{30,22},{22,30},{31,23},{23,31}} | collective-permute-start | bytes 1572872 | tf_op jit(solution)/shard_map/ppermute | solution.py:491
  90.6 47.3 %collective-permute-start.4 = (bf16[512,512]{1,0:T(8,128)(2,1)}, bf16[512,512]{1,0:T(8,128)(2,1)}, u32[]{:S(2)}, u32[]{:S(2)}) collective-permute-start(bf16[512,512]{1,0:T(8,128)(2,1)} %get-tuple-element.32), channel_id=1, source_target_pairs={{20,0},{24,4},{28,8},{4,16},{8,20},{12,24},{16,12},{0,28},{21,1},{... | collective-permute-start | bytes 1572872 | tf_op jit(solution)/shard_map/ppermute | solution.py:491
  114.5 1.4 copy-start.5
  116.0 7.5 %copy-start.9 = (f32[1,3712]{1,0:T(1,128)S(1)}, f32[1,3712]{1,0:T(1,128)}, u32[]{:S(2)}) copy-start(f32[1,3712]{1,0:T(1,128)} %copy-done.7) | copy-start | bytes 44548
  123.5 1.4 copy-start.6
  144.5 1.1 copy-start.2
  151.3 1.4 copy-start.3

commit v8 on v7

--- a/solution.py
+++ b/solution.py
@@ -169,7 +169,7 @@
     t_ref, told_ref, past_ref = refs[n_x + n_g : n_x + n_g + 3]
     a_ref, x_ref, inner_ref = refs[-3:]
     tokens, width = a_ref.shape
-    factor = column_of(inverse_rms(t_ref[2:3, :], width_all))
+    factor = column_of(inverse_rms(t_ref[...], width_all))
     evicted = told_ref[:, tokens + 2 * width :] == 1.0
     ready = jnp.logical_and(pick_ref[2] == 1, jnp.logical_not(evicted))
     part = None
@@ -269,7 +269,7 @@
     tokens, width = a_ref.shape
     evicted = told_ref[:, tokens + 2 * width : tokens + 2 * width + 1] == 1.0
     ready = jnp.logical_and(pick_ref[2] == 1, jnp.logical_not(evicted))
-    row = jnp.where(ready, 0.0, row_of(t_ref[2:3, :], inner_ref[...], width_all))
+    row = jnp.where(ready, 0.0, row_of(t_ref[...], inner_ref[...], width_all))
     at = (slice(None), pl.ds(pl.program_id(0) * lanes, lanes))
     o_ref[...] = (a_ref[at] - x_ref[at].astype(F32) * column_of(row)).astype(BF16)
 
@@ -373,9 +373,9 @@
     )(mode, *[array for array, _ in (*first, *second)], *after)
 
 
-def sums_kernel(pieces, pick_ref, current_ref, stash_ref, gq_ref, gk_ref, rows_ref, told_ref):
+def open_kernel(pieces, pick_ref, current_ref, stash_ref, g_ref, gq_ref, gk_ref, rows_ref, held_ref, told_ref, away_ref, early_ref):
     step = pl.program_id(0)
-    tokens = current_ref.shape[0]
+    tokens, lanes = current_ref.shape
 
     def total(x):
         wide = x.astype(F32)
@@ -383,15 +383,27 @@
         sums = sum(square[:, i : i + HDIM] for i in range(0, square.shape[1], HDIM))
         return jnp.sum(sums.T, axis=0, keepdims=True)
 
-    rows = jnp.concatenate([total(current_ref[...]), total(stash_ref[0]), total(stash_ref[1])], axis=0)
+    rows = jnp.concatenate([total(current_ref[...]), total(stash_ref[0])], axis=0)
+    held = total(stash_ref[1])
 
     @pl.when(step == 0)
     def _():
         rows_ref[...] = rows
+        held_ref[...] = held
+        away_ref[...] = stash_ref[1]
 
     @pl.when(step > 0)
     def _():
         rows_ref[...] += rows
+        held_ref[...] += held
+
+    @pl.when(pick_ref[1] == 1)
+    def _():
+        early_ref[...] = stash_ref[1]
+
+    @pl.when(pick_ref[1] == 0)
+    def _():
+        early_ref[...] = g_ref[...]
 
     @pl.when(step == pieces - 1)
     def _():
@@ -402,89 +414,53 @@
         told_ref[:, tokens + 2 * width :] = jnp.full((1, HDIM), pick_ref[2].astype(F32))
 
 
-def sums_of(pick, current, stash, gain_q, gain_k, lanes):
+def opened(pick, current, stash, g, gain_q, gain_k, lanes):
     tokens, width = current.shape
     pieces = width // lanes
+    block = pl.BlockSpec((tokens, lanes), lambda i, pick: (0, i))
     still = lambda *shape: pl.BlockSpec(shape, lambda i, pick: (0, 0))
     told = tokens + 2 * width + HDIM
     return pl.pallas_call(
-        functools.partial(sums_kernel, pieces),
-        out_shape=(jax.ShapeDtypeStruct((3, tokens), F32), jax.ShapeDtypeStruct((1, told), F32)),
+        functools.partial(open_kernel, pieces),
+        out_shape=(
+            jax.ShapeDtypeStruct((2, tokens), F32),
+            jax.ShapeDtypeStruct((1, tokens), F32),
+            jax.ShapeDtypeStruct((1, told), F32),
+            jax.ShapeDtypeStruct((tokens, lanes), BF16),
+            jax.ShapeDtypeStruct((tokens, width), BF16),
+        ),
         grid_spec=pltpu.PrefetchScalarGridSpec(
             num_scalar_prefetch=1,
             grid=(pieces,),
             in_specs=[
-                pl.BlockSpec((tokens, lanes), lambda i, pick: (0, i)),
+                block,
                 pl.BlockSpec((None, 2, tokens, lanes), lambda i, pick: (0, 0, 0, i)),
+                block,
                 still(1, width),
                 still(1, width),
             ],
-            out_specs=(still(3, tokens), still(1, told)),
+            out_specs=(still(2, tokens), still(1, tokens), still(1, told), still(tokens, lanes), block),
         ),
         compiler_params=compiler(MOST),
-        name="sums",
-    )(pick, current, stash, gain_q, gain_k)
-
-
-def pack_kernel(pieces, pick_ref, stash_ref, g_ref, *refs):
-    away_ref, first_ref, last_ref = refs[-3:]
-    step = pl.program_id(0)
-
-    @pl.when(step == 0)
-    def _():
-        away_ref[...] = stash_ref[...]
-
-    for mine, out in ((step < pieces - 1, first_ref), (step == pieces - 1, last_ref)):
-
-        @pl.when(jnp.logical_and(mine, pick_ref[1] == 1))
-        def _():
-            out[...] = stash_ref[...]
-
-        @pl.when(jnp.logical_and(mine, pick_ref[1] == 0))
-        def _():
-            out[...] = g_ref[...]
-
-
-def pack(pick, stash, g, lanes, after=()):
-    tokens, width = g.shape
-    pieces = width // lanes
-    piece = pl.BlockSpec((tokens, lanes), lambda i, pick: (0, 0))
-    return pl.pallas_call(
-        functools.partial(pack_kernel, pieces),
-        out_shape=[jax.ShapeDtypeStruct((tokens, w), BF16) for w in (lanes, width - lanes, lanes)],
-        grid_spec=pltpu.PrefetchScalarGridSpec(
-            num_scalar_prefetch=1,
-            grid=(pieces,),
-            in_specs=[
-                pl.BlockSpec((None, None, tokens, lanes), lambda i, pick: (0, 1, 0, i * pick[1])),
-                pl.BlockSpec((tokens, lanes), lambda i, pick: (0, i)),
-            ]
-            + [ANYWHERE] * len(after),
-            out_specs=[
-                piece, pl.BlockSpec((tokens, lanes), lambda i, pick: (0, jnp.minimum(i, pieces - 2))), piece
-            ],
-        ),
-        compiler_params=compiler(MOST),
-        name="pack",
-    )(pick, stash, g, *after)
-
-
-def join_kernel(rows_ref, told_ref, held_ref, o_ref):
-    tokens = rows_ref.shape[1]
-    o_ref[0:2, :] = rows_ref[0:2, :]
+        name="opened",
+    )(pick, current, stash, g, gain_q, gain_k)
+
+
+def join_kernel(told_ref, held_ref, *rest):
+    tokens = held_ref.shape[1]
     evicted = told_ref[:, told_ref.shape[1] - 1 :] == 1.0
-    o_ref[2:3, :] = jnp.where(evicted, held_ref[2:3, :], told_ref[:, :tokens])
-
-
-def join(rows, told, held):
+    rest[-1][...] = jnp.where(evicted, held_ref[...], told_ref[:, :tokens])
+
+
+def join(told, held, after):
     return pl.pallas_call(
         join_kernel,
-        out_shape=jax.ShapeDtypeStruct(rows.shape, F32),
-        in_specs=[IN_VMEM] * 3,
+        out_shape=jax.ShapeDtypeStruct(held.shape, F32),
+        in_specs=[IN_VMEM] * 2 + [ANYWHERE] * len(after),
         out_specs=IN_VMEM,
         compiler_params=compiler(VMEM),
         name="join",
-    )(rows, told, held)
+    )(told, held, *after)
 
 
 def send(x, pairs):
@@ -500,8 +476,6 @@
     prior = [(s, (s - 1) % n) for s in range(n)]
     inside = [(s, s - 1) for s in range(n) if s not in special]
     within = inside + [(half, n - 1), (0, half - 1)]
-    around = [p for p in within if p[0] not in (half, n - 2)] + [(half, n - 3), (n - 2, n - 1)]
-    back = [(n - 1, n - 3), (n - 3, n - 1)]
     to_partner = [(s, (s + half) % n) for s in range(n) if s not in special]
     holder = [((s + half) % n, (s - 1) % n) for s in range(n)]
     direct = [p for p in holder if p[0] not in special] + [(half, half - 1), (0, n - 1)]
@@ -520,54 +494,50 @@
     mode = jnp.stack([jnp.where(is_special, 2, eviction[0]), flag(is_special)])
     mode_first = jnp.stack([eviction[0], flag(False)])
     final = flag(me == half - 1)
-    take = jnp.stack([
-        jnp.where(crossed, jnp.where(me == n - 1, 2, 1), 0),
-        jnp.where(crossed, 2, jnp.where(me == n - 3, 1, 0)),
-        final,
-    ])
-    take_first = jnp.stack([flag(crossed), flag(crossed), final])
-
-    rows, told = sums_of(early_pick, current, stashed, query_gain, key_gain, step)
+    take = jnp.stack([flag(crossed), flag(crossed), final])
+
+    rows, held, told, away, early = opened(early_pick, current, stashed, upstream, query_gain, key_gain, step)
     told = send(told, prior)
-    held_rows = send(rows, holder)
-    away, early_first, early_last = pack(early_pick, stashed, upstream, step, (told, held_rows))
+    held = send(held, holder)
     fetched = send(away, to_partner)
-    early_first = send(early_first, within)
-    early_last = send(early_last, around)
-    totals = lax.psum(join(rows, told, held_rows), "tensor")
+    early = send(early, within)
+    totals = lax.psum(rows, "tensor")
 
     own_a, own_inner = early_backward(width_all, early_pick, stashed, upstream, totals, query_gain, key_gain, heads)
     sent, away = choose(
-        mode_first, [(stashed, (0, 0)), (fetched, 0)], [(stashed, (1, 1))], tokens, step, (own_inner,)
+        mode_first, [(stashed, (0, 0)), (fetched, 0)], [(stashed, (1, 1))], tokens, step, (own_inner, told, held)
     )
     fetched = send(away, to_partner)
     passed = [send(sent, inside)]
-    last_back = send(early_last, back)
     own_inner = lax.psum(own_inner, "tensor")
     slot, last = slot_of(width_all, early_pick, own_a, stashed, upstream, totals, own_inner, step)
     kept = send(last, prior)
+    output = forward(width_all, current, totals, query_gain, key_gain, heads, (last,))
+
     sent, last = choose(
-        mode, [(stashed, (0, 1)), (fetched, 0), (slot, 1)], [(stashed, (1, 2)), (slot, 2)], tokens, step
+        mode, [(stashed, (0, 1)), (fetched, 0), (slot, 1)], [(stashed, (1, 2)), (slot, 2)], tokens, step,
+        (output, passed[0]),
     )
     straight = send(last, direct)
     passed.append(send(sent, prior))
-    output = forward(width_all, current, totals, query_gain, key_gain, heads, (sent,))
+
+    total = lax.psum(join(told, held, (sent,)), "tensor")
 
     share = functools.partial(backward, width_all, width)
     a, x, inner = share(
-        take_first, [(passed[0], 0), (early_first, 0)], [(early_first, 0), (kept, 0)], totals, told,
-        jnp.zeros((1, tokens), F32), heads, 0, (), (output,),
+        take, [(passed[0], 0), (early, 0)], [(early, 0), (kept, 0)], total, told,
+        jnp.zeros((1, tokens), F32), heads, 0,
     )
     a, x, inner = share(
-        take_first, [(passed[1], 0), (early_first, step)], [(early_first, step), (passed[1], 0)],
-        totals, told, inner, heads, step, (a, x),
+        take, [(passed[1], 0), (early, step)], [(early, step), (passed[1], 0)],
+        total, told, inner, heads, step, (a, x),
     )
     a, x, inner = share(
-        take, [(straight, 0), (early_last, 0), (last_back, 0), (kept, None)],
-        [(early_last, 0), (last_back, 0), (straight, 0)], totals, told, inner, heads, 2 * step, (a, x),
+        take, [(straight, 0), (early, 2 * step), (kept, None)], [(early, 2 * step), (straight, 0)],
+        total, told, inner, heads, 2 * step, (a, x),
     )
     inner = lax.psum(inner, "tensor")
-    result = finish(width_all, take, a, x, totals, told, inner, step)
+    result = finish(width_all, take, a, x, total, told, inner, step)
     return (output[None], result[None])
 
 

time: 159 us -> 152 us (0.956)
  the two profiles are of different devices: /device:TPU:0 before, /device:TPU:20 now
where the time goes in v8:
time: 152 us; the launch traced here: 151 us
  Pallas kernels  49 us (32%)
  waiting for transfers between devices  45.8 us (30%)
  blocking collectives  25.6 us (17%)
  starting transfers between devices  20.1 us (13%)
  local copies, waits for them, and re-layouts  8.54 us (6%)
    ppermute x9, waiting for transfers between devices, send(): return lax.ppermute(x, 'section', pairs)  45.8 us
    pallas_call x3, Pallas kernels, backward(): pl.pallas_call(functools.partial(backward_kernel, first, heads, width_all...  20.4 us
    ppermute x9, starting transfers between devices, send(): return lax.ppermute(x, 'section', pairs)  20.1 us
    unnamed x26, local copies, waits for them, and re-layouts  8.54 us
    pallas_call x1, Pallas kernels, forward(): pl.pallas_call(functools.partial(forward_kernel, heads, width_all), out_s...  7.47 us
    psum x1, blocking collectives, local(): totals = lax.psum(rows, 'tensor')  6.83 us
    psum x1, blocking collectives, local(): own_inner = lax.psum(own_inner, 'tensor')  6.64 us
    pallas_call x1, Pallas kernels, opened(): pl.pallas_call(functools.partial(open_kernel, pieces), out_shape=(jax.Sha...  6.2 us
  transfers between devices with their start and end apart: 9, of which 4 were waited for; matrix products, arithmetic and copies ran while one was open for 0% of the time, Pallas kernels for 22%

profile of v8, /device:TPU:20, one launch (start us, length us, event | category | flops | bytes accessed | tf_op | source)
XLA Modules:
  0.0 151.3 jit_solution(16289918703826425434)
XLA Ops:
  1.3 0.7 pad_add_fusion.pick_ref
  2.0 6.2 %opened.1 = (f32[2,512]{1,0:T(2,128)}, f32[1,512]{1,0:T(1,128)}, f32[1,3712]{1,0:T(1,128)}, bf16[512,512]{1,0:T(8,128)(2,1)}, bf16[512,1536]{1,0:T(8,128)(2,1)}) custom-call(s32[3]{0:T(128)} %pad_add_fusion.pick_ref, bf16[512,1536]{1,0:T(8,128)(2,1)} %bitcast.13, bf16[1,2,512,1536]{3,2,1,0:T(8,128)(2,1)} %refs_3_.1, bf16[512,1536]{1,0:T(8,128)(2,1)} %bitcast.15, ...), custom_call_target="tpu_custom_call" | custom-call | tf_op jit(solution)/shard_map/opened/pallas_call | solution.py:423
  8.2 2.2 %collective-permute-start = (bf16[512,512]{1,0:T(8,128)(2,1)}, bf16[512,512]{1,0:T(8,128)(2,1)}, u32[]{:S(2)}, u32[]{:S(2)}) collective-permute-start(bf16[512,512]{1,0:T(8,128)(2,1)} %get-tuple-element.28), channel_id=1, source_target_pairs={{4,20},{8,24},{12,28},{20,4},{24,8},{28,12},{5,21},{9,25},{13,29},... | collective-permute-start | bytes 1572872 | tf_op jit(solution)/shard_map/ppermute | solution.py:467
  10.4 0.1 collective-permute-start.6
  10.5 5.0 %collective-permute-start.2 = (f32[1,512]{1,0:T(1,128)}, f32[1,512]{1,0:T(1,128)S(1)}, u32[]{:S(2)}, u32[]{:S(2)}) collective-permute-start(f32[1,512]{1,0:T(1,128)} %get-tuple-element.30), channel_id=1, source_target_pairs={{16,28},{20,0},{24,4},{28,8},{0,12},{4,16},{8,20},{12,24},{17,29},... | collective-permute-start | bytes 6152 | tf_op jit(solution)/shard_map/ppermute | solution.py:467
  15.5 0.0 collective-permute-start.1
  15.5 0.1 pad_add_fusion.2.mode_ref
  15.6 6.8 %psum.28.t_ref = f32[2,512]{1,0:T(2,128)} all-reduce(f32[2,512]{1,0:T(2,128)} %get-tuple-element.24), channel_id=1, replica_groups=mesh['section'=8,'tensor'=4] {'tensor'}, use_global_device_ids=true, to_apply=%region_0.1 | all-reduce | flops 1024 | bytes 8192 | tf_op jit(solution)/shard_map/psum | solution.py:504
  22.4 0.0 copy-start
  22.4 3.2 %early_backward.1 = (f32[512,1536]{1,0:T(8,128)}, f32[1,512]{1,0:T(1,128)}) custom-call(s32[3]{0:T(128)} %pad_add_fusion.pick_ref, bf16[1,2,512,1536]{3,2,1,0:T(8,128)(2,1)} %refs_3_.1, bf16[512,1536]{1,0:T(8,128)(2,1)} %bitcast.16, f32[2,512]{1,0:T(2,128)} %psum.28.t_ref, f32[1,1536]{1,0:T(1,128)} %gq_ref.5, f32[1,1536]{1,0:T(1,128)} %gk_ref.5), custom_call_target="tpu_custom_call" | custom-call | tf_op jit(solution)/shard_map/early_backward/pallas_call | solution.py:247
  25.6 7.6 %collective-permute-done.2.refs_5_.held_ref = f32[1,512]{1,0:T(1,128)S(1)} collective-permute-done((f32[1,512]{1,0:T(1,128)}, f32[1,512]{1,0:T(1,128)S(1)}, u32[]{:S(2)}, u32[]{:S(2)}) %collective-permute-start.2) | collective-permute-done | bytes 2080 | tf_op jit(solution)/shard_map/ppermute | solution.py:467
  33.2 24.7 %collective-permute-done.1.refs_4_.told_ref.refs_5_.refs_6_ = f32[1,3712]{1,0:T(1,128)S(1)} collective-permute-done((f32[1,3712]{1,0:T(1,128)}, f32[1,3712]{1,0:T(1,128)S(1)}, u32[]{:S(2)}, u32[]{:S(2)}) %collective-permute-start.1) | collective-permute-done | bytes 14880 | tf_op jit(solution)/shard_map/ppermute | solution.py:467
  57.9 0.0 collective-permute-done.refs_1_
  57.9 0.0 copy-done
  57.9 0.0 copy-start.11
  57.9 0.7 copy-done.11
  58.5 0.0 copy-start.12
  58.6 2.7 %choose.2 = (bf16[512,512]{1,0:T(8,128)(2,1)}, bf16[512,512]{1,0:T(8,128)(2,1)}) custom-call(s32[2]{0:T(128)S(1)} %pad_add_fusion.2.mode_ref, bf16[1,2,512,1536]{3,2,1,0:T(8,128)(2,1)S(1)} %copy-done, bf16[512,512]{1,0:T(8,128)(2,1)} %collective-permute-done.refs_1_, bf16[1,2,512,1536]{3,2,1,0:T(8,128)(2,1)S(1)} %copy-done, f32[1,512]{1,0:T(1,128)S(1)} %copy-done.11, ...), custom_call_target="tpu_custom_call" | custom-call | tf_op jit(solution)/shard_map/choose/pallas_call | solution.py:362
  61.3 4.1 %collective-permute-start.3 = (bf16[512,512]{1,0:T(8,128)(2,1)}, bf16[512,512]{1,0:T(8,128)(2,1)}, u32[]{:S(2)}, u32[]{:S(2)}) collective-permute-start(bf16[512,512]{1,0:T(8,128)(2,1)} %get-tuple-element.31), channel_id=1, source_target_pairs={{4,20},{8,24},{12,28},{20,4},{24,8},{28,12},{5,21},{9,25},{13,29},... | collective-permute-start | bytes 1572872 | tf_op jit(solution)/shard_map/ppermute | solution.py:467
  65.4 1.9 %collective-permute-start.4 = (bf16[512,512]{1,0:T(8,128)(2,1)}, bf16[512,512]{1,0:T(8,128)(2,1)}, u32[]{:S(2)}, u32[]{:S(2)}) collective-permute-start(bf16[512,512]{1,0:T(8,128)(2,1)} %get-tuple-element.33), channel_id=1, source_target_pairs={{4,0},{8,4},{12,8},{20,16},{24,20},{28,24},{5,1},{9,5},{13,9},{21,... | collective-permute-start | bytes 1572872 | tf_op jit(solution)/shard_map/ppermute | solution.py:467
  67.3 0.0 copy-done.12
  67.3 6.6 %psum.29.inner_ref = f32[1,512]{1,0:T(1,128)} all-reduce(f32[1,512]{1,0:T(1,128)S(1)} %copy-done.12), channel_id=1, replica_groups=mesh['section'=8,'tensor'=4] {'tensor'}, use_global_device_ids=true, to_apply=%region_1.2 | all-reduce | flops 512 | bytes 4096 | tf_op jit(solution)/shard_map/psum | solution.py:512
  74.0 0.0 copy-start.8
  74.0 0.0 copy-start.9
  74.0 0.0 copy-start.10
  74.0 3.4 %slot.1 = (bf16[512,1536]{1,0:T(8,128)(2,1)}, bf16[512,512]{1,0:T(8,128)(2,1)}) custom-call(s32[3]{0:T(128)} %pad_add_fusion.pick_ref, f32[512,1536]{1,0:T(8,128)} %get-tuple-element.25.a_ref, bf16[1,2,512,1536]{3,2,1,0:T(8,128)(2,1)} %refs_3_.1, bf16[512,1536]{1,0:T(8,128)(2,1)} %bitcast.17, f32[2,512]{1,0:T(2,128)} %psum.28.t_ref, f32[1,512]{1,0:T(1,128)} %psum.29.inner_ref), custom_call_target="tpu_custom_call" | custom-call | tf_op jit(solution)/shard_map/slot/pallas_call | solution.py:317
  77.4 0.0 copy-start.1
  77.4 0.9 collective-permute-start.7
  78.3 0.0 copy-done.8
  78.3 0.0 copy-done.9
  78.3 0.0 copy-done.10
  78.3 0.0 copy-start.6
  78.3 1.4 copy-done.6
  79.7 0.0 copy-start.7
  79.7 1.0 copy-done.7
  80.8 7.5 %forward.1.refs_5_ = bf16[512,1536]{1,0:T(8,128)(2,1)} custom-call(bf16[512,1536]{1,0:T(8,128)(2,1)S(1)} %bitcast.14, f32[2,512]{1,0:T(2,128)S(1)} %copy-done.8, f32[1,1536]{1,0:T(1,128)S(1)} %copy-done.9, f32[1,1536]{1,0:T(1,128)S(1)} %copy-done.10, bf16[512,512]{1,0:T(8,128)(2,1)S(1)} %copy-done.7), custom_call_target="tpu_custom_call" | custom-call | tf_op jit(solution)/shard_map/forward/pallas_call | solution.py:114
  88.2 0.1 pad_add_fusion.1.mode_ref
  88.3 0.0 collective-permute-done.3.refs_1_
  88.3 0.0 collective-permute-done.4.refs_6_.refs_0_
  88.3 0.0 copy-done.1
  88.3 0.0 copy-start.4
  88.3 1.4 copy-done.4
  89.7 0.0 copy-start.5
  89.7 1.4 copy-done.5
  91.2 2.7 %choose.3 = (bf16[512,512]{1,0:T(8,128)(2,1)}, bf16[512,512]{1,0:T(8,128)(2,1)}) custom-call(s32[2]{0:T(128)S(1)} %pad_add_fusion.1.mode_ref, bf16[1,2,512,1536]{3,2,1,0:T(8,128)(2,1)S(1)} %copy-done.1, bf16[512,512]{1,0:T(8,128)(2,1)} %collective-permute-done.3.refs_1_, bf16[512,1536]{1,0:T(8,128)(2,1)S(1)} %copy-done.5, ...), custom_call_target="tpu_custom_call" | custom-call | tf_op jit(solution)/shard_map/choose/pallas_call | solution.py:362
  93.8 3.4 %collective-permute-start.8 = (bf16[512,512]{1,0:T(8,128)(2,1)}, bf16[512,512]{1,0:T(8,128)(2,1)}, u32[]{:S(2)}, u32[]{:S(2)}) collective-permute-start(bf16[512,512]{1,0:T(8,128)(2,1)} %get-tuple-element.36.rest_0_), channel_id=1, source_target_pairs={{0,28},{4,0},{8,4},{12,8},{16,12},{20,16},{24,20},{28,24},{1,29},{... | collective-permute-start | bytes 1572872 | tf_op jit(solution)/shard_map/ppermute | solution.py:467
  97.2 2.4 %collective-permute-start.5 = (bf16[512,512]{1,0:T(8,128)(2,1)}, bf16[512,512]{1,0:T(8,128)(2,1)}, u32[]{:S(2)}, u32[]{:S(2)}) collective-permute-start(bf16[512,512]{1,0:T(8,128)(2,1)} %get-tuple-element.34), channel_id=1, source_target_pairs={{20,0},{24,4},{28,8},{4,16},{8,20},{12,24},{16,12},{0,28},{21,1},{... | collective-permute-start | bytes 1572872 | tf_op jit(solution)/shard_map/ppermute | solution.py:467
  99.6 0.1 add_convert_fusion.pick_ref
  99.7 0.1 join.1
  99.8 6.0 %psum.30.refs_4_.refs_5_.t_ref = f32[1,512]{1,0:T(1,128)S(1)} all-reduce(f32[1,512]{1,0:T(1,128)S(1)} %join.1), channel_id=1, replica_groups=mesh['section'=8,'tensor'=4] {'tensor'}, use_global_device_ids=true, to_apply=%region_2.3 | all-reduce | flops 512 | bytes 4096 | tf_op jit(solution)/shard_map/psum | solution.py:524
  105.8 0.0 collective-permute-done.7.refs_3_.refs_2_
  105.8 0.0 collective-permute-done.6.refs_1_.refs_2_.refs_3_
  105.8 6.7 %backward.3 = (f32[512,1536]{1,0:T(8,128)S(1)}, bf16[512,1536]{1,0:T(8,128)(2,1)S(1)}, f32[1,512]{1,0:T(1,128)S(1)}) custom-call(s32[3]{0:T(128)S(1)} %add_convert_fusion.pick_ref, bf16[512,512]{1,0:T(8,128)(2,1)} %collective-permute-done.4.refs_6_.refs_0_, bf16[512,1536]{1,0:T(8,128)(2,1)} %collective-permute-done.6.refs_1_.refs_2_.refs_3_, ...), custom_call_target="tpu_custom_call" | custom-call | tf_op jit(solution)/shard_map/backward/pallas_call | solution.py:203
  112.5 5.9 %collective-permute-done.8.refs_0_.refs_3_ = bf16[512,512]{1,0:T(8,128)(2,1)} collective-permute-done((bf16[512,512]{1,0:T(8,128)(2,1)}, bf16[512,512]{1,0:T(8,128)(2,1)}, u32[]{:S(2)}, u32[]{:S(2)}) %collective-permute-start.8) | collective-permute-done | bytes 524320 | tf_op jit(solution)/shard_map/ppermute | solution.py:467
  118.4 6.7 %backward.4 = (f32[512,1536]{1,0:T(8,128)S(1)}, bf16[512,1536]{1,0:T(8,128)(2,1)S(1)}, f32[1,512]{1,0:T(1,128)S(1)}) custom-call(s32[3]{0:T(128)S(1)} %add_convert_fusion.pick_ref, bf16[512,512]{1,0:T(8,128)(2,1)} %collective-permute-done.8.refs_0_.refs_3_, ...), custom_call_target="tpu_custom_call", output_to_operand_aliasing={{0}: (8, {}), {1}: (9, {})} | custom-call | tf_op jit(solution)/shard_map/backward/pallas_call | solution.py:203
  125.1 7.6 %collective-permute-done.5.refs_0_.refs_4_ = bf16[512,512]{1,0:T(8,128)(2,1)} collective-permute-done((bf16[512,512]{1,0:T(8,128)(2,1)}, bf16[512,512]{1,0:T(8,128)(2,1)}, u32[]{:S(2)}, u32[]{:S(2)}) %collective-permute-start.5) | collective-permute-done | bytes 524320 | tf_op jit(solution)/shard_map/ppermute | solution.py:467
  132.8 7.0 %backward.5 = (f32[512,1536]{1,0:T(8,128)S(1)}, bf16[512,1536]{1,0:T(8,128)(2,1)S(1)}, f32[1,512]{1,0:T(1,128)S(1)}) custom-call(s32[3]{0:T(128)S(1)} %add_convert_fusion.pick_ref, bf16[512,512]{1,0:T(8,128)(2,1)} %collective-permute-done.5.refs_0_.refs_4_, ...), custom_call_target="tpu_custom_call", output_to_operand_aliasing={{0}: (9, {}), {1}: (10, {})} | custom-call | tf_op jit(solution)/shard_map/backward/pallas_call | solution.py:203
  139.8 0.0 copy-start.2
  139.8 1.1 copy-done.2
  140.9 6.1 %psum.31.inner_ref = f32[1,512]{1,0:T(1,128)S(1)} all-reduce(f32[1,512]{1,0:T(1,128)S(1)} %get-tuple-element.45), channel_id=1, replica_groups=mesh['section'=8,'tensor'=4] {'tensor'}, use_global_device_ids=true, to_apply=%region_3.4 | all-reduce | flops 512 | bytes 4096 | tf_op jit(solution)/shard_map/psum | solution.py:539
  147.0 0.0 copy-start.3
  147.0 1.4 copy-done.3
  148.4 2.9 %finish.1 = bf16[512,1536]{1,0:T(8,128)(2,1)} custom-call(s32[3]{0:T(128)S(1)} %add_convert_fusion.pick_ref, f32[512,1536]{1,0:T(8,128)S(1)} %get-tuple-element.43.a_ref, bf16[512,1536]{1,0:T(8,128)(2,1)S(1)} %copy-done.3, f32[1,512]{1,0:T(1,128)S(1)} %psum.30.refs_4_.refs_5_.t_ref, f32[1,3712]{1,0:T(1,128)S(1)} %collective-permute-done.1.refs_4_.told_ref.refs_5_.refs_6_, ...), custom_call_target="tpu_custom_call" | custom-call | tf_op jit(solution)/shard_map/finish/pallas_call | solution.py:279
  (1 shorter events, 0.0 us)
Async XLA Ops:
  8.2 49.7 %collective-permute-start = (bf16[512,512]{1,0:T(8,128)(2,1)}, bf16[512,512]{1,0:T(8,128)(2,1)}, u32[]{:S(2)}, u32[]{:S(2)}) collective-permute-start(bf16[512,512]{1,0:T(8,128)(2,1)} %get-tuple-element.28), channel_id=1, source_target_pairs={{4,20},{8,24},{12,28},{20,4},{24,8},{28,12},{5,21},{9,25},{13,29},... | collective-permute-start | bytes 1572872 | tf_op jit(solution)/shard_map/ppermute | solution.py:467
  10.4 95.4 %collective-permute-start.6 = (bf16[512,1536]{1,0:T(8,128)(2,1)}, bf16[512,1536]{1,0:T(8,128)(2,1)}, u32[]{:S(2)}, u32[]{:S(2)}) collective-permute-start(bf16[512,1536]{1,0:T(8,128)(2,1)} %get-tuple-element.35), channel_id=1, source_target_pairs={{4,0},{8,4},{12,8},{20,16},{24,20},{28,24},{16,28},{0,12},{5,1},{9... | collective-permute-start | bytes 4718600 | tf_op jit(solution)/shard_map/ppermute | solution.py:467
  10.5 22.7 %collective-permute-start.2 = (f32[1,512]{1,0:T(1,128)}, f32[1,512]{1,0:T(1,128)S(1)}, u32[]{:S(2)}, u32[]{:S(2)}) collective-permute-start(f32[1,512]{1,0:T(1,128)} %get-tuple-element.30), channel_id=1, source_target_pairs={{16,28},{20,0},{24,4},{28,8},{0,12},{4,16},{8,20},{12,24},{17,29},... | collective-permute-start | bytes 6152 | tf_op jit(solution)/shard_map/ppermute | solution.py:467
  15.5 42.3 %collective-permute-start.1 = (f32[1,3712]{1,0:T(1,128)}, f32[1,3712]{1,0:T(1,128)S(1)}, u32[]{:S(2)}, u32[]{:S(2)}) collective-permute-start(f32[1,3712]{1,0:T(1,128)} %get-tuple-element.29), channel_id=1, source_target_pairs={{0,28},{4,0},{8,4},{12,8},{16,12},{20,16},{24,20},{28,24},{1,29},{... | collective-permute-start | bytes 44552 | tf_op jit(solution)/shard_map/ppermute | solution.py:467
  22.4 35.4 %copy-start = (bf16[1,2,512,1536]{3,2,1,0:T(8,128)(2,1)S(1)}, bf16[1,2,512,1536]{3,2,1,0:T(8,128)(2,1)}, u32[]{:S(2)}) copy-start(bf16[1,2,512,1536]{3,2,1,0:T(8,128)(2,1)} %refs_3_.1) | copy-start | bytes 9437188
  57.9 0.7 copy-start.11
  58.5 8.8 %copy-start.12 = (f32[1,512]{1,0:T(1,128)S(1)}, f32[1,512]{1,0:T(1,128)}, u32[]{:S(2)}) copy-start(f32[1,512]{1,0:T(1,128)} %get-tuple-element.26.refs_3_) | copy-start | bytes 6148
  61.3 27.1 %collective-permute-start.3 = (bf16[512,512]{1,0:T(8,128)(2,1)}, bf16[512,512]{1,0:T(8,128)(2,1)}, u32[]{:S(2)}, u32[]{:S(2)}) collective-permute-start(bf16[512,512]{1,0:T(8,128)(2,1)} %get-tuple-element.31), channel_id=1, source_target_pairs={{4,20},{8,24},{12,28},{20,4},{24,8},{28,12},{5,21},{9,25},{13,29},... | collective-permute-start | bytes 1572872 | tf_op jit(solution)/shard_map/ppermute | solution.py:467
  65.4 22.9 %collective-permute-start.4 = (bf16[512,512]{1,0:T(8,128)(2,1)}, bf16[512,512]{1,0:T(8,128)(2,1)}, u32[]{:S(2)}, u32[]{:S(2)}) collective-permute-start(bf16[512,512]{1,0:T(8,128)(2,1)} %get-tuple-element.33), channel_id=1, source_target_pairs={{4,0},{8,4},{12,8},{20,16},{24,20},{28,24},{5,1},{9,5},{13,9},{21,... | collective-permute-start | bytes 1572872 | tf_op jit(solution)/shard_map/ppermute | solution.py:467
  74.0 4.3 %copy-start.8 = (f32[2,512]{1,0:T(2,128)S(1)}, f32[2,512]{1,0:T(2,128)}, u32[]{:S(2)}) copy-start(f32[2,512]{1,0:T(2,128)} %psum.28.t_ref) | copy-start | bytes 12292
  74.0 4.3 %copy-start.9 = (f32[1,1536]{1,0:T(1,128)S(1)}, f32[1,1536]{1,0:T(1,128)}, u32[]{:S(2)}) copy-start(f32[1,1536]{1,0:T(1,128)} %gq_ref.5) | copy-start | bytes 18436
  74.0 4.3 %copy-start.10 = (f32[1,1536]{1,0:T(1,128)S(1)}, f32[1,1536]{1,0:T(1,128)}, u32[]{:S(2)}) copy-start(f32[1,1536]{1,0:T(1,128)} %gk_ref.5) | copy-start | bytes 18436
  77.4 11.0 %copy-start.1 = (bf16[1,2,512,1536]{3,2,1,0:T(8,128)(2,1)S(1)}, bf16[1,2,512,1536]{3,2,1,0:T(8,128)(2,1)}, u32[]{:S(2)}) copy-start(bf16[1,2,512,1536]{3,2,1,0:T(8,128)(2,1)} %refs_3_.1) | copy-start | bytes 9437188
  77.4 28.4 %collective-permute-start.7 = (bf16[512,512]{1,0:T(8,128)(2,1)}, bf16[512,512]{1,0:T(8,128)(2,1)}, u32[]{:S(2)}, u32[]{:S(2)}) collective-permute-start(bf16[512,512]{1,0:T(8,128)(2,1)} %get-tuple-element.27.rest_0_), channel_id=1, source_target_pairs={{0,28},{4,0},{8,4},{12,8},{16,12},{20,16},{24,20},{28,24},{1,29},{... | collective-permute-start | bytes 1572872 | tf_op jit(solution)/shard_map/ppermute | solution.py:467
  78.3 1.4 copy-start.6
  79.7 1.0 copy-start.7
  88.3 1.4 copy-start.4
  89.7 1.4 copy-start.5
  93.8 24.6 %collective-permute-start.8 = (bf16[512,512]{1,0:T(8,128)(2,1)}, bf16[512,512]{1,0:T(8,128)(2,1)}, u32[]{:S(2)}, u32[]{:S(2)}) collective-permute-start(bf16[512,512]{1,0:T(8,128)(2,1)} %get-tuple-element.36.rest_0_), channel_id=1, source_target_pairs={{0,28},{4,0},{8,4},{12,8},{16,12},{20,16},{24,20},{28,24},{1,29},{... | collective-permute-start | bytes 1572872 | tf_op jit(solution)/shard_map/ppermute | solution.py:467
  97.2 35.6 %collective-permute-start.5 = (bf16[512,512]{1,0:T(8,128)(2,1)}, bf16[512,512]{1,0:T(8,128)(2,1)}, u32[]{:S(2)}, u32[]{:S(2)}) collective-permute-start(bf16[512,512]{1,0:T(8,128)(2,1)} %get-tuple-element.34), channel_id=1, source_target_pairs={{20,0},{24,4},{28,8},{4,16},{8,20},{12,24},{16,12},{0,28},{21,1},{... | collective-permute-start | bytes 1572872 | tf_op jit(solution)/shard_map/ppermute | solution.py:467
  139.8 1.1 copy-start.2
  147.0 1.4 copy-start.3

commit v9 on v8

--- a/solution.py
+++ b/solution.py
@@ -87,6 +87,11 @@
 
 IN_VMEM = pl.BlockSpec(memory_space=pltpu.VMEM)
 ANYWHERE = pl.BlockSpec(memory_space=pl.ANY)
+IN_HBM = pl.BlockSpec(memory_space=pltpu.HBM)
+
+
+def in_hbm(x):
+    return pltpu.with_memory_space_constraint(x, pltpu.HBM)
 
 
 def forward_kernel(heads, width_all, x_ref, t_ref, gq_ref, gk_ref, *rest):
@@ -115,11 +120,11 @@
         functools.partial(forward_kernel, heads, width_all),
         out_shape=jax.ShapeDtypeStruct(x.shape, BF16),
         grid=(width // lanes,),
-        in_specs=[block, pl.BlockSpec(totals.shape, lambda i: (0, 0)), gain, gain] + [ANYWHERE] * len(after),
+        in_specs=[block, pl.BlockSpec(totals.shape, lambda i: (0, 0)), gain, gain] + [IN_HBM] * len(after),
         out_specs=block,
         compiler_params=compiler(VMEM),
         name="forward",
-    )(x, totals, gain_q, gain_k, *after)
+    )(in_hbm(x), totals, gain_q, gain_k, *map(in_hbm, after))
 
 
 def backward_head(x, g, factor, gain_q, gain_k):
@@ -169,7 +174,7 @@
     t_ref, told_ref, past_ref = refs[n_x + n_g : n_x + n_g + 3]
     a_ref, x_ref, inner_ref = refs[-3:]
     tokens, width = a_ref.shape
-    factor = column_of(inverse_rms(t_ref[...], width_all))
+    factor = column_of(inverse_rms(t_ref[2:3, :], width_all))
     evicted = told_ref[:, tokens + 2 * width :] == 1.0
     ready = jnp.logical_and(pick_ref[2] == 1, jnp.logical_not(evicted))
     part = None
@@ -210,7 +215,7 @@
             jax.ShapeDtypeStruct((1, tokens), F32),
         ),
         in_specs=[pl.BlockSpec(memory_space=pltpu.SMEM)] + [IN_VMEM] * (before - 1 + len(sofar))
-        + [ANYWHERE] * len(after),
+        + [IN_HBM] * len(after),
         out_specs=(IN_VMEM, IN_VMEM, IN_VMEM),
         input_output_aliases={before: 0, before + 1: 1} if sofar else {},
         compiler_params=compiler(VMEM),
@@ -258,7 +263,7 @@
         ),
         compiler_params=compiler(MOST),
         name="early_backward",
-    )(pick, stash, g, totals, gain_q, gain_k)
+    )(pick, in_hbm(stash), in_hbm(g), totals, gain_q, gain_k)
 
 
 def row_of(total, inner, width_all):
@@ -269,22 +274,23 @@
     tokens, width = a_ref.shape
     evicted = told_ref[:, tokens + 2 * width : tokens + 2 * width + 1] == 1.0
     ready = jnp.logical_and(pick_ref[2] == 1, jnp.logical_not(evicted))
-    row = jnp.where(ready, 0.0, row_of(t_ref[...], inner_ref[...], width_all))
+    row = jnp.where(ready, 0.0, row_of(t_ref[2:3, :], inner_ref[...], width_all))
     at = (slice(None), pl.ds(pl.program_id(0) * lanes, lanes))
-    o_ref[...] = (a_ref[at] - x_ref[at].astype(F32) * column_of(row)).astype(BF16)
+    o_ref[...] = (a_ref[at] - x_ref[...].astype(F32) * column_of(row)).astype(BF16)
 
 
 def finish(width_all, pick, a, x, totals, told, inner, lanes):
     tokens, width = a.shape
+    block = pl.BlockSpec((tokens, lanes), lambda i: (0, i))
     return pl.pallas_call(
         functools.partial(finish_kernel, lanes, width_all),
         out_shape=jax.ShapeDtypeStruct(a.shape, BF16),
         grid=(width // lanes,),
-        in_specs=[pl.BlockSpec(memory_space=pltpu.SMEM)] + [IN_VMEM] * 5,
-        out_specs=pl.BlockSpec((tokens, lanes), lambda i: (0, i)),
+        in_specs=[pl.BlockSpec(memory_space=pltpu.SMEM), IN_VMEM, block] + [IN_VMEM] * 3,
+        out_specs=block,
         compiler_params=compiler(VMEM),
         name="finish",
-    )(pick, a, x, totals, told, inner)
+    )(pick, a, in_hbm(x), totals, told, inner)
 
 
 def slot_kernel(width_all, last, pick_ref, a_ref, x_ref, g_ref, t_ref, inner_ref, o_ref, kept_ref):
@@ -333,69 +339,81 @@
         ),
         compiler_params=compiler(MOST),
         name="slot",
-    )(pick, a, stash, g, totals, inner)
-
-
-def choose_kernel(n, mode_ref, *refs):
-    outs = refs[-2:]
-    sets = (refs[:n], refs[n:-2])
-    for i, (out, options) in enumerate(zip(outs, sets)):
-        for m, ref in enumerate(options):
-
-            @pl.when(mode_ref[i] == m)
-            def _():
-                out[...] = ref[...]
+    )(pick, a, in_hbm(stash), in_hbm(g), totals, inner)
 
 
 def choose(mode, first, second, tokens, step, after=()):
-    def spec(array, at):
-        if isinstance(at, tuple):
-            return pl.BlockSpec((None, None, tokens, step), lambda i, mode: (0, at[0], 0, at[1]))
-        return pl.BlockSpec((tokens, step), lambda i, mode: (0, at))
-
-    piece = pl.BlockSpec((tokens, step), lambda i, mode: (0, 0))
+    options = (first, second)
+    count = len(first) + len(second)
 
     def kernel(mode_ref, *refs):
-        used = len(first) + len(second)
-        choose_kernel(len(first), mode_ref, *refs[:used], *refs[-2:])
+        sems = refs[-1]
+        outs = refs[-3:-1]
+        ins = iter(refs[:count])
+        copies = []
+        for i, (out, chosen) in enumerate(zip(outs, options)):
+            for m, (_, at) in enumerate(chosen):
+                ref = next(ins)
+                if isinstance(at, tuple):
+                    ref = ref.at[0, at[0], :, at[1] * step : (at[1] + 1) * step]
+                else:
+                    ref = ref.at[:, at * step : (at + 1) * step]
+                copies.append((mode_ref[i] == m, pltpu.make_async_copy(ref, out, sems.at[i])))
+        for wanted, copy in copies:
+            pl.when(wanted)(copy.start)
+        for wanted, copy in copies:
+            pl.when(wanted)(copy.wait)
 
     return pl.pallas_call(
         kernel,
         out_shape=[jax.ShapeDtypeStruct((tokens, step), BF16)] * 2,
-        grid_spec=pltpu.PrefetchScalarGridSpec(
-            num_scalar_prefetch=1,
-            grid=(1,),
-            in_specs=[spec(*o) for o in (*first, *second)] + [ANYWHERE] * len(after),
-            out_specs=[piece] * 2,
-        ),
+        in_specs=[pl.BlockSpec(memory_space=pltpu.SMEM)]
+        + [IN_HBM if isinstance(at, tuple) else ANYWHERE for _, at in (*first, *second)]
+        + [ANYWHERE] * len(after),
+        out_specs=[ANYWHERE] * 2,
+        scratch_shapes=[pltpu.SemaphoreType.DMA((2,))],
         compiler_params=compiler(VMEM),
         name="choose",
     )(mode, *[array for array, _ in (*first, *second)], *after)
 
 
-def open_kernel(pieces, pick_ref, current_ref, stash_ref, g_ref, gq_ref, gk_ref, rows_ref, held_ref, told_ref, away_ref, early_ref):
+def hold(arrays, after):
+    n = len(arrays)
+    return pl.pallas_call(
+        lambda *refs: None,
+        out_shape=[jax.ShapeDtypeStruct(x.shape, x.dtype) for x in arrays],
+        in_specs=[IN_HBM] * n + [ANYWHERE] * len(after),
+        out_specs=[IN_HBM] * n,
+        input_output_aliases={i: i for i in range(n)},
+        name="hold",
+    )(*arrays, *after)
+
+
+def open_kernel(
+    pieces, pick_ref, current_ref, stash_ref, g_ref, gq_ref, gk_ref, rows_ref, told_ref, away_ref, early_ref, sums
+):
     step = pl.program_id(0)
     tokens, lanes = current_ref.shape
 
     def total(x):
         wide = x.astype(F32)
         square = wide * wide
-        sums = sum(square[:, i : i + HDIM] for i in range(0, square.shape[1], HDIM))
-        return jnp.sum(sums.T, axis=0, keepdims=True)
-
-    rows = jnp.concatenate([total(current_ref[...]), total(stash_ref[0])], axis=0)
-    held = total(stash_ref[1])
+        return sum(square[:, i : i + HDIM] for i in range(0, square.shape[1], HDIM))
 
     @pl.when(step == 0)
     def _():
-        rows_ref[...] = rows
-        held_ref[...] = held
         away_ref[...] = stash_ref[1]
 
-    @pl.when(step > 0)
-    def _():
-        rows_ref[...] += rows
-        held_ref[...] += held
+    for i, x in enumerate((current_ref[...], stash_ref[0], stash_ref[1])):
+        part = total(x)
+
+        @pl.when(step == 0)
+        def _():
+            sums[i] = part
+
+        @pl.when(step > 0)
+        def _():
+            sums[i] += part
 
     @pl.when(pick_ref[1] == 1)
     def _():
@@ -407,6 +425,8 @@
 
     @pl.when(step == pieces - 1)
     def _():
+        for i in range(3):
+            rows_ref[i : i + 1, :] = jnp.sum(sums[i].T, axis=0, keepdims=True)
         width = gq_ref.shape[1]
         told_ref[:, :tokens] = rows_ref[1:2, :]
         told_ref[:, tokens : tokens + width] = gq_ref[...]
@@ -423,8 +443,7 @@
     return pl.pallas_call(
         functools.partial(open_kernel, pieces),
         out_shape=(
-            jax.ShapeDtypeStruct((2, tokens), F32),
-            jax.ShapeDtypeStruct((1, tokens), F32),
+            jax.ShapeDtypeStruct((3, tokens), F32),
             jax.ShapeDtypeStruct((1, told), F32),
             jax.ShapeDtypeStruct((tokens, lanes), BF16),
             jax.ShapeDtypeStruct((tokens, width), BF16),
@@ -439,28 +458,30 @@
                 still(1, width),
                 still(1, width),
             ],
-            out_specs=(still(2, tokens), still(1, tokens), still(1, told), still(tokens, lanes), block),
+            out_specs=(still(3, tokens), still(1, told), still(tokens, lanes), block),
+            scratch_shapes=[pltpu.VMEM((3, tokens, HDIM), F32)],
         ),
         compiler_params=compiler(MOST),
         name="opened",
-    )(pick, current, stash, g, gain_q, gain_k)
-
-
-def join_kernel(told_ref, held_ref, *rest):
-    tokens = held_ref.shape[1]
+    )(pick, in_hbm(current), in_hbm(stash), in_hbm(g), gain_q, gain_k)
+
+
+def join_kernel(rows_ref, told_ref, held_ref, o_ref):
+    tokens = rows_ref.shape[1]
     evicted = told_ref[:, told_ref.shape[1] - 1 :] == 1.0
-    rest[-1][...] = jnp.where(evicted, held_ref[...], told_ref[:, :tokens])
-
-
-def join(told, held, after):
+    o_ref[0:2, :] = rows_ref[0:2, :]
+    o_ref[2:3, :] = jnp.where(evicted, held_ref[2:3, :], told_ref[:, :tokens])
+
+
+def join(rows, told, held):
     return pl.pallas_call(
         join_kernel,
-        out_shape=jax.ShapeDtypeStruct(held.shape, F32),
-        in_specs=[IN_VMEM] * 2 + [ANYWHERE] * len(after),
+        out_shape=jax.ShapeDtypeStruct(rows.shape, F32),
+        in_specs=[IN_VMEM] * 3,
         out_specs=IN_VMEM,
         compiler_params=compiler(VMEM),
         name="join",
-    )(told, held, *after)
+    )(rows, told, held)
 
 
 def send(x, pairs):
@@ -496,32 +517,33 @@
     final = flag(me == half - 1)
     take = jnp.stack([flag(crossed), flag(crossed), final])
 
-    rows, held, told, away, early = opened(early_pick, current, stashed, upstream, query_gain, key_gain, step)
+    stash = in_hbm(stashed)
+    rows, told, away, early = opened(early_pick, current, stashed, upstream, query_gain, key_gain, step)
     told = send(told, prior)
-    held = send(held, holder)
+    held = send(rows, holder)
+    away, early = hold((away, early), (told, held))
     fetched = send(away, to_partner)
     early = send(early, within)
-    totals = lax.psum(rows, "tensor")
-
-    own_a, own_inner = early_backward(width_all, early_pick, stashed, upstream, totals, query_gain, key_gain, heads)
+    total = lax.psum(join(rows, told, held), "tensor")
+
+    own_a, own_inner = early_backward(width_all, early_pick, stashed, upstream, total, query_gain, key_gain, heads)
     sent, away = choose(
-        mode_first, [(stashed, (0, 0)), (fetched, 0)], [(stashed, (1, 1))], tokens, step, (own_inner, told, held)
+        mode_first, [(stash, (0, 0)), (fetched, 0)], [(stash, (1, 1))], tokens, step, (in_hbm(own_inner),)
     )
     fetched = send(away, to_partner)
     passed = [send(sent, inside)]
     own_inner = lax.psum(own_inner, "tensor")
-    slot, last = slot_of(width_all, early_pick, own_a, stashed, upstream, totals, own_inner, step)
+    slot, last = slot_of(width_all, early_pick, own_a, stashed, upstream, total, own_inner, step)
     kept = send(last, prior)
-    output = forward(width_all, current, totals, query_gain, key_gain, heads, (last,))
+    slot = in_hbm(slot)
+    output = forward(width_all, current, total, query_gain, key_gain, heads, (last,))
 
     sent, last = choose(
-        mode, [(stashed, (0, 1)), (fetched, 0), (slot, 1)], [(stashed, (1, 2)), (slot, 2)], tokens, step,
-        (output, passed[0]),
+        mode, [(stash, (0, 1)), (fetched, 0), (slot, 1)], [(stash, (1, 2)), (slot, 2)], tokens, step,
+        (in_hbm(output), passed[0]),
     )
     straight = send(last, direct)
     passed.append(send(sent, prior))
-
-    total = lax.psum(join(told, held, (sent,)), "tensor")
 
     share = functools.partial(backward, width_all, width)
     a, x, inner = share(

time: 152 us -> 190 us (1.25)
  the two profiles are of different devices: /device:TPU:20 before, /device:TPU:0 now
where the time goes in v9:
time: 190 us; the launch traced here: 188 us
  Pallas kernels  94.9 us (50%)
  starting transfers between devices  43.4 us (23%)
  blocking collectives  20.3 us (11%)
  waiting for transfers between devices  17.5 us (9%)
  local copies, waits for them, and re-layouts  9.6 us (5%)
    pallas_call x2, Pallas kernels, choose(): pl.pallas_call(kernel, out_shape=[jax.ShapeDtypeStruct((tokens, step), BF...  51 us
    ppermute x9, starting transfers between devices, send(): return lax.ppermute(x, 'section', pairs)  43.4 us
    ppermute x9, waiting for transfers between devices, send(): return lax.ppermute(x, 'section', pairs)  17.5 us
    pallas_call x3, Pallas kernels, backward(): pl.pallas_call(functools.partial(backward_kernel, first, heads, width_all...  16.7 us
    unnamed x34, local copies, waits for them, and re-layouts  9.6 us
    pallas_call x1, Pallas kernels, forward(): pl.pallas_call(functools.partial(forward_kernel, heads, width_all), out_s...  8.39 us
    psum x1, blocking collectives, local(): own_inner = lax.psum(own_inner, 'tensor')  6.83 us
    psum x1, blocking collectives, local(): inner = lax.psum(inner, 'tensor')  6.83 us
  transfers between devices with their start and end apart: 9, of which 3 were waited for; matrix products, arithmetic and copies ran while one was open for 0% of the time, Pallas kernels for 42%

profile of v9, /device:TPU:0, one launch (start us, length us, event | category | flops | bytes accessed | tf_op | source)
XLA Modules:
  0.0 187.9 jit_solution(11241833580538842047)
XLA Ops:
  1.3 0.7 pad_add_fusion.pick_ref
  1.9 6.8 %opened.1 = (f32[3,512]{1,0:T(4,128)}, f32[1,3712]{1,0:T(1,128)}, bf16[512,512]{1,0:T(8,128)(2,1)}, bf16[512,1536]{1,0:T(8,128)(2,1)}) custom-call(s32[3]{0:T(128)} %pad_add_fusion.pick_ref, bf16[512,1536]{1,0:T(8,128)(2,1)} %bitcast.16, bf16[1,2,512,1536]{3,2,1,0:T(8,128)(2,1)} %refs_3_.1, bf16[512,1536]{1,0:T(8,128)(2,1)} %bitcast.12, f32[1,1536]{1,0:T(1,128)} %gq_ref.5, ...), custom_call_target="tpu_custom_call" | custom-call | tf_op jit(solution)/shard_map/opened/pallas_call | solution.py:443
  8.8 0.0 copy-start.15
  8.8 6.0 %collective-permute-start = (f32[1,3712]{1,0:T(1,128)}, f32[1,3712]{1,0:T(1,128)S(1)}, u32[]{:S(2)}, u32[]{:S(2)}) collective-permute-start(f32[1,3712]{1,0:T(1,128)} %get-tuple-element.26), channel_id=1, source_target_pairs={{0,28},{4,0},{8,4},{12,8},{16,12},{20,16},{24,20},{28,24},{1,29},{... | collective-permute-start | bytes 44552 | tf_op jit(solution)/shard_map/ppermute | solution.py:488
  14.8 0.0 collective-permute-start.1
  14.8 5.7 %collective-permute-done.1.held_ref.refs_3_ = f32[3,512]{1,0:T(4,128)S(1)} collective-permute-done((f32[3,512]{1,0:T(4,128)}, f32[3,512]{1,0:T(4,128)S(1)}, u32[]{:S(2)}, u32[]{:S(2)}) %collective-permute-start.1) | collective-permute-done | bytes 6176 | tf_op jit(solution)/shard_map/ppermute | solution.py:488
  20.4 0.0 collective-permute-done.told_ref.refs_2_.refs_5_.refs_6_
  20.4 0.0 copy-start.7
  20.4 0.6 copy-done.13
  21.0 0.0 copy-done.7
  21.0 0.7 collective-permute-start.2
  21.7 2.8 %collective-permute-start.6 = (bf16[512,1536]{1,0:T(8,128)(2,1)}, bf16[512,1536]{1,0:T(8,128)(2,1)S(1)}, u32[]{:S(2)}, u32[]{:S(2)}) collective-permute-start(bf16[512,1536]{1,0:T(8,128)(2,1)} %get-tuple-element.37), channel_id=1, source_target_pairs={{4,0},{8,4},{12,8},{20,16},{24,20},{28,24},{16,28},{0,12},{5,1},{9... | collective-permute-start | bytes 4718600 | tf_op jit(solution)/shard_map/ppermute | solution.py:488
  24.5 0.1 pad_add_fusion.2.mode_ref
  24.6 0.0 copy-done.15
  24.6 0.0 copy-start.8
  24.6 0.7 copy-done.8
  25.3 0.0 copy-start.14
  25.3 0.7 copy-done.14
  26.0 0.1 join.1
  26.1 6.6 %psum.21.t_ref.refs_4_.refs_5_ = f32[3,512]{1,0:T(4,128)} all-reduce(f32[3,512]{1,0:T(4,128)S(1)} %join.1), channel_id=1, replica_groups=mesh['section'=8,'tensor'=4] {'tensor'}, use_global_device_ids=true, to_apply=%region_0.1 | all-reduce | flops 1536 | bytes 12288 | tf_op jit(solution)/shard_map/psum | solution.py:527
  32.7 2.9 %early_backward.1 = (f32[512,1536]{1,0:T(8,128)}, f32[1,512]{1,0:T(1,128)}) custom-call(s32[3]{0:T(128)} %pad_add_fusion.pick_ref, bf16[1,2,512,1536]{3,2,1,0:T(8,128)(2,1)} %refs_3_.1, bf16[512,1536]{1,0:T(8,128)(2,1)} %bitcast.13, f32[3,512]{1,0:T(4,128)} %psum.21.t_ref.refs_4_.refs_5_, f32[1,1536]{1,0:T(1,128)} %gq_ref.5, f32[1,1536]{1,0:T(1,128)} %gk_ref.5), custom_call_target="tpu_custom_call" | custom-call | tf_op jit(solution)/shard_map/early_backward/pallas_call | solution.py:252
  35.6 0.0 collective-permute-done.2.refs_1_
  35.6 0.0 copy-start.16
  35.6 17.6 %choose.2 = (bf16[512,512]{1,0:T(8,128)(2,1)}, bf16[512,512]{1,0:T(8,128)(2,1)}) custom-call(s32[2]{0:T(128)S(1)} %pad_add_fusion.2.mode_ref, bf16[1,2,512,1536]{3,2,1,0:T(8,128)(2,1)} %refs_3_.1, bf16[512,512]{1,0:T(8,128)(2,1)S(1)} %collective-permute-done.2.refs_1_, bf16[1,2,512,1536]{3,2,1,0:T(8,128)(2,1)} %refs_3_.1, f32[1,512]{1,0:T(1,128)} %get-tuple-element.28.refs_3_), custom_call_target="tpu_custom_call" | custom-call | tf_op jit(solution)/shard_map/choose/pallas_call | solution.py:367
  53.2 0.7 collective-permute-start.3
  53.9 1.3 collective-permute-start.4
  55.2 0.1 pad_add_fusion.1.mode_ref
  55.3 0.0 copy-done.16
  55.3 6.8 %psum.22.inner_ref = f32[1,512]{1,0:T(1,128)} all-reduce(f32[1,512]{1,0:T(1,128)S(1)} %copy-done.16), channel_id=1, replica_groups=mesh['section'=8,'tensor'=4] {'tensor'}, use_global_device_ids=true, to_apply=%region_1.2 | all-reduce | flops 512 | bytes 4096 | tf_op jit(solution)/shard_map/psum | solution.py:535
  62.1 0.0 copy-start.10
  62.1 0.0 copy-start.11
  62.1 0.0 copy-start.12
  62.1 5.2 %slot.1 = (bf16[512,1536]{1,0:T(8,128)(2,1)}, bf16[512,512]{1,0:T(8,128)(2,1)}) custom-call(s32[3]{0:T(128)} %pad_add_fusion.pick_ref, f32[512,1536]{1,0:T(8,128)} %get-tuple-element.27.a_ref, bf16[1,2,512,1536]{3,2,1,0:T(8,128)(2,1)} %refs_3_.1, bf16[512,1536]{1,0:T(8,128)(2,1)} %bitcast.14, f32[3,512]{1,0:T(4,128)} %psum.21.t_ref.refs_4_.refs_5_, ...), custom_call_target="tpu_custom_call" | custom-call | tf_op jit(solution)/shard_map/slot/pallas_call | solution.py:323
  67.3 28.9 %collective-permute-start.7 = (bf16[512,512]{1,0:T(8,128)(2,1)}, bf16[512,512]{1,0:T(8,128)(2,1)S(1)}, u32[]{:S(2)}, u32[]{:S(2)}) collective-permute-start(bf16[512,512]{1,0:T(8,128)(2,1)} %get-tuple-element.29.rest_0_), channel_id=1, source_target_pairs={{0,28},{4,0},{8,4},{12,8},{16,12},{20,16},{24,20},{28,24},{1,29},{... | collective-permute-start | bytes 1572872 | tf_op jit(solution)/shard_map/ppermute | solution.py:488
  96.2 0.0 copy-done.10
  96.2 0.0 copy-done.11
  96.2 0.0 copy-done.12
  96.2 8.4 %forward.1.refs_5_ = bf16[512,1536]{1,0:T(8,128)(2,1)} custom-call(bf16[512,1536]{1,0:T(8,128)(2,1)} %bitcast.17, f32[3,512]{1,0:T(4,128)S(1)} %copy-done.10, f32[1,1536]{1,0:T(1,128)S(1)} %copy-done.11, f32[1,1536]{1,0:T(1,128)S(1)} %copy-done.12, bf16[512,512]{1,0:T(8,128)(2,1)} %get-tuple-element.29.rest_0_), custom_call_target="tpu_custom_call" | custom-call | tf_op jit(solution)/shard_map/forward/pallas_call | solution.py:119
  104.6 0.0 collective-permute-done.3.refs_1_
  104.6 0.0 collective-permute-done.4.refs_6_.refs_0_
  104.6 0.0 copy-start.9
  104.6 33.4 %choose.3 = (bf16[512,512]{1,0:T(8,128)(2,1)}, bf16[512,512]{1,0:T(8,128)(2,1)}) custom-call(s32[2]{0:T(128)S(1)} %pad_add_fusion.1.mode_ref, bf16[1,2,512,1536]{3,2,1,0:T(8,128)(2,1)} %refs_3_.1, bf16[512,512]{1,0:T(8,128)(2,1)S(1)} %collective-permute-done.3.refs_1_, bf16[512,1536]{1,0:T(8,128)(2,1)} %get-tuple-element.34.refs_2_.refs_4_, ...), custom_call_target="tpu_custom_call" | custom-call | tf_op jit(solution)/shard_map/choose/pallas_call | solution.py:367
  138.1 0.0 copy-done.5
  138.1 2.7 %collective-permute-start.8 = (bf16[512,512]{1,0:T(8,128)(2,1)}, bf16[512,512]{1,0:T(8,128)(2,1)}, u32[]{:S(2)}, u32[]{:S(2)}) collective-permute-start(bf16[512,512]{1,0:T(8,128)(2,1)} %get-tuple-element.38), channel_id=1, source_target_pairs={{0,28},{4,0},{8,4},{12,8},{16,12},{20,16},{24,20},{28,24},{1,29},{... | collective-permute-start | bytes 1572872 | tf_op jit(solution)/shard_map/ppermute | solution.py:488
  140.8 0.2 collective-permute-start.5
  141.0 0.1 add_convert_fusion.pick_ref
  141.1 0.0 collective-permute-done.7.refs_3_.refs_2_
  141.1 0.8 copy-done.3
  141.9 0.0 collective-permute-done.6.refs_1_.refs_2_.refs_3_
  141.9 0.0 copy-done.9
  141.9 0.0 copy-start.4
  141.9 1.0 copy-done.4
  143.0 1.0 copy-done.6
  144.0 5.1 %backward.3 = (f32[512,1536]{1,0:T(8,128)S(1)}, bf16[512,1536]{1,0:T(8,128)(2,1)S(1)}, f32[1,512]{1,0:T(1,128)S(1)}) custom-call(s32[3]{0:T(128)S(1)} %add_convert_fusion.pick_ref, bf16[512,512]{1,0:T(8,128)(2,1)S(1)} %copy-done.6, bf16[512,1536]{1,0:T(8,128)(2,1)S(1)} %collective-permute-done.6.refs_1_.refs_2_.refs_3_, ...), custom_call_target="tpu_custom_call" | custom-call | tf_op jit(solution)/shard_map/backward/pallas_call | solution.py:208
  149.1 4.3 %collective-permute-done.8.refs_0_.refs_3_ = bf16[512,512]{1,0:T(8,128)(2,1)} collective-permute-done((bf16[512,512]{1,0:T(8,128)(2,1)}, bf16[512,512]{1,0:T(8,128)(2,1)}, u32[]{:S(2)}, u32[]{:S(2)}) %collective-permute-start.8) | collective-permute-done | bytes 524320 | tf_op jit(solution)/shard_map/ppermute | solution.py:488
  153.5 5.8 %backward.4 = (f32[512,1536]{1,0:T(8,128)S(1)}, bf16[512,1536]{1,0:T(8,128)(2,1)S(1)}, f32[1,512]{1,0:T(1,128)S(1)}) custom-call(s32[3]{0:T(128)S(1)} %add_convert_fusion.pick_ref, bf16[512,512]{1,0:T(8,128)(2,1)} %collective-permute-done.8.refs_0_.refs_3_, ...), custom_call_target="tpu_custom_call", output_to_operand_aliasing={{0}: (8, {}), {1}: (9, {})} | custom-call | tf_op jit(solution)/shard_map/backward/pallas_call | solution.py:208
  159.2 7.5 %collective-permute-done.5.refs_0_.refs_4_ = bf16[512,512]{1,0:T(8,128)(2,1)} collective-permute-done((bf16[512,512]{1,0:T(8,128)(2,1)}, bf16[512,512]{1,0:T(8,128)(2,1)}, u32[]{:S(2)}, u32[]{:S(2)}) %collective-permute-start.5) | collective-permute-done | bytes 524320 | tf_op jit(solution)/shard_map/ppermute | solution.py:488
  166.7 5.8 %backward.5 = (f32[512,1536]{1,0:T(8,128)S(1)}, bf16[512,1536]{1,0:T(8,128)(2,1)S(1)}, f32[1,512]{1,0:T(1,128)S(1)}) custom-call(s32[3]{0:T(128)S(1)} %add_convert_fusion.pick_ref, bf16[512,512]{1,0:T(8,128)(2,1)} %collective-permute-done.5.refs_0_.refs_4_, ...), custom_call_target="tpu_custom_call", output_to_operand_aliasing={{0}: (9, {}), {1}: (10, {})} | custom-call | tf_op jit(solution)/shard_map/backward/pallas_call | solution.py:208
  172.5 0.0 copy-start
  172.5 1.6 copy-done
  174.1 1.2 copy-done.2
  175.3 6.8 %psum.23.inner_ref = f32[1,512]{1,0:T(1,128)S(1)} all-reduce(f32[1,512]{1,0:T(1,128)S(1)} %get-tuple-element.47), channel_id=1, replica_groups=mesh['section'=8,'tensor'=4] {'tensor'}, use_global_device_ids=true, to_apply=%region_2.3 | all-reduce | flops 512 | bytes 4096 | tf_op jit(solution)/shard_map/psum | solution.py:561
  182.2 1.9 %copy-done.1 = f32[512,1536]{1,0:T(8,128)S(1)} copy-done((f32[512,1536]{1,0:T(8,128)S(1)}, f32[512,1536]{1,0:T(8,128)}, u32[]{:S(2)}) %copy-start.1) | copy-done | bytes 3145752
  184.0 3.8 %finish.1 = bf16[512,1536]{1,0:T(8,128)(2,1)} custom-call(s32[3]{0:T(128)S(1)} %add_convert_fusion.pick_ref, f32[512,1536]{1,0:T(8,128)S(1)} %copy-done.1, bf16[512,1536]{1,0:T(8,128)(2,1)} %copy-done.2, f32[3,512]{1,0:T(4,128)S(1)} %copy-done.10, f32[1,3712]{1,0:T(1,128)S(1)} %copy-done.9, f32[1,512]{1,0:T(1,128)S(1)} %psum.23.inner_ref), custom_call_target="tpu_custom_call" | custom-call | tf_op jit(solution)/shard_map/finish/pallas_call | solution.py:285
  (8 shorter events, 0.0 us)
Async XLA Ops:
  8.8 15.8 %copy-start.15 = (f32[3,512]{1,0:T(4,128)S(1)}, f32[3,512]{1,0:T(4,128)}, u32[]{:S(2)}) copy-start(f32[3,512]{1,0:T(4,128)} %get-tuple-element.25.rows_ref) | copy-start | bytes 18436
  8.8 11.7 %collective-permute-start = (f32[1,3712]{1,0:T(1,128)}, f32[1,3712]{1,0:T(1,128)S(1)}, u32[]{:S(2)}, u32[]{:S(2)}) collective-permute-start(f32[1,3712]{1,0:T(1,128)} %get-tuple-element.26), channel_id=1, source_target_pairs={{0,28},{4,0},{8,4},{12,8},{16,12},{20,16},{24,20},{28,24},{1,29},{... | collective-permute-start | bytes 44552 | tf_op jit(solution)/shard_map/ppermute | solution.py:488
  14.8 5.7 %collective-permute-start.1 = (f32[3,512]{1,0:T(4,128)}, f32[3,512]{1,0:T(4,128)S(1)}, u32[]{:S(2)}, u32[]{:S(2)}) collective-permute-start(f32[3,512]{1,0:T(4,128)} %get-tuple-element.25.rows_ref), channel_id=1, source_target_pairs={{16,28},{20,0},{24,4},{28,8},{0,12},{4,16},{8,20},{12,24},{17,29},... | collective-permute-start | bytes 18440 | tf_op jit(solution)/shard_map/ppermute | solution.py:488
  20.4 0.6 copy-start.13
  20.4 0.6 copy-start.7
  21.0 14.6 %collective-permute-start.2 = (bf16[512,512]{1,0:T(8,128)(2,1)}, bf16[512,512]{1,0:T(8,128)(2,1)S(1)}, u32[]{:S(2)}, u32[]{:S(2)}) collective-permute-start(bf16[512,512]{1,0:T(8,128)(2,1)} %get-tuple-element.32), channel_id=1, source_target_pairs={{4,20},{8,24},{12,28},{20,4},{24,8},{28,12},{5,21},{9,25},{13,29},... | collective-permute-start | bytes 1572872 | tf_op jit(solution)/shard_map/ppermute | solution.py:488
  21.7 120.2 %collective-permute-start.6 = (bf16[512,1536]{1,0:T(8,128)(2,1)}, bf16[512,1536]{1,0:T(8,128)(2,1)S(1)}, u32[]{:S(2)}, u32[]{:S(2)}) collective-permute-start(bf16[512,1536]{1,0:T(8,128)(2,1)} %get-tuple-element.37), channel_id=1, source_target_pairs={{4,0},{8,4},{12,8},{20,16},{24,20},{28,24},{16,28},{0,12},{5,1},{9... | collective-permute-start | bytes 4718600 | tf_op jit(solution)/shard_map/ppermute | solution.py:488
  24.6 0.7 copy-start.8
  25.3 0.7 copy-start.14
  35.6 19.7 %copy-start.16 = (f32[1,512]{1,0:T(1,128)S(1)}, f32[1,512]{1,0:T(1,128)}, u32[]{:S(2)}) copy-start(f32[1,512]{1,0:T(1,128)} %get-tuple-element.28.refs_3_) | copy-start | bytes 6148
  53.2 51.4 %collective-permute-start.3 = (bf16[512,512]{1,0:T(8,128)(2,1)}, bf16[512,512]{1,0:T(8,128)(2,1)S(1)}, u32[]{:S(2)}, u32[]{:S(2)}) collective-permute-start(bf16[512,512]{1,0:T(8,128)(2,1)} %get-tuple-element.33), channel_id=1, source_target_pairs={{4,20},{8,24},{12,28},{20,4},{24,8},{28,12},{5,21},{9,25},{13,29},... | collective-permute-start | bytes 1572872 | tf_op jit(solution)/shard_map/ppermute | solution.py:488
  53.9 50.7 %collective-permute-start.4 = (bf16[512,512]{1,0:T(8,128)(2,1)}, bf16[512,512]{1,0:T(8,128)(2,1)S(1)}, u32[]{:S(2)}, u32[]{:S(2)}) collective-permute-start(bf16[512,512]{1,0:T(8,128)(2,1)} %get-tuple-element.35), channel_id=1, source_target_pairs={{4,0},{8,4},{12,8},{20,16},{24,20},{28,24},{5,1},{9,5},{13,9},{21,... | collective-permute-start | bytes 1572872 | tf_op jit(solution)/shard_map/ppermute | solution.py:488
  62.1 34.1 %copy-start.10 = (f32[3,512]{1,0:T(4,128)S(1)}, f32[3,512]{1,0:T(4,128)}, u32[]{:S(2)}) copy-start(f32[3,512]{1,0:T(4,128)} %psum.21.t_ref.refs_4_.refs_5_) | copy-start | bytes 18436
  62.1 34.1 %copy-start.11 = (f32[1,1536]{1,0:T(1,128)S(1)}, f32[1,1536]{1,0:T(1,128)}, u32[]{:S(2)}) copy-start(f32[1,1536]{1,0:T(1,128)} %gq_ref.5) | copy-start | bytes 18436
  62.1 34.1 %copy-start.12 = (f32[1,1536]{1,0:T(1,128)S(1)}, f32[1,1536]{1,0:T(1,128)}, u32[]{:S(2)}) copy-start(f32[1,1536]{1,0:T(1,128)} %gk_ref.5) | copy-start | bytes 18436
  67.3 73.9 %collective-permute-start.7 = (bf16[512,512]{1,0:T(8,128)(2,1)}, bf16[512,512]{1,0:T(8,128)(2,1)S(1)}, u32[]{:S(2)}, u32[]{:S(2)}) collective-permute-start(bf16[512,512]{1,0:T(8,128)(2,1)} %get-tuple-element.29.rest_0_), channel_id=1, source_target_pairs={{0,28},{4,0},{8,4},{12,8},{16,12},{20,16},{24,20},{28,24},{1,29},{... | collective-permute-start | bytes 1572872 | tf_op jit(solution)/shard_map/ppermute | solution.py:488
  104.6 33.5 %copy-start.5 = (bf16[512,512]{1,0:T(8,128)(2,1)}, bf16[512,512]{1,0:T(8,128)(2,1)S(1)}, u32[]{:S(2)}) copy-start(bf16[512,512]{1,0:T(8,128)(2,1)S(1)} %collective-permute-done.4.refs_6_.refs_0_) | copy-start | bytes 1572868
  104.6 37.3 %copy-start.9 = (f32[1,3712]{1,0:T(1,128)S(1)}, f32[1,3712]{1,0:T(1,128)}, u32[]{:S(2)}) copy-start(f32[1,3712]{1,0:T(1,128)} %copy-done.7) | copy-start | bytes 44548
  138.1 15.4 %collective-permute-start.8 = (bf16[512,512]{1,0:T(8,128)(2,1)}, bf16[512,512]{1,0:T(8,128)(2,1)}, u32[]{:S(2)}, u32[]{:S(2)}) collective-permute-start(bf16[512,512]{1,0:T(8,128)(2,1)} %get-tuple-element.38), channel_id=1, source_target_pairs={{0,28},{4,0},{8,4},{12,8},{16,12},{20,16},{24,20},{28,24},{1,29},{... | collective-permute-start | bytes 1572872 | tf_op jit(solution)/shard_map/ppermute | solution.py:488
  140.8 25.9 %collective-permute-start.5 = (bf16[512,512]{1,0:T(8,128)(2,1)}, bf16[512,512]{1,0:T(8,128)(2,1)}, u32[]{:S(2)}, u32[]{:S(2)}) collective-permute-start(bf16[512,512]{1,0:T(8,128)(2,1)} %get-tuple-element.36), channel_id=1, source_target_pairs={{20,0},{24,4},{28,8},{4,16},{8,20},{12,24},{16,12},{0,28},{21,1},{... | collective-permute-start | bytes 1572872 | tf_op jit(solution)/shard_map/ppermute | solution.py:488
  141.1 0.8 copy-start.3
  141.9 1.0 copy-start.4
  143.0 1.0 copy-start.6
  172.5 1.6 copy-start
  174.1 1.2 copy-start.2
  182.1 1.9 %copy-start.1 = (f32[512,1536]{1,0:T(8,128)S(1)}, f32[512,1536]{1,0:T(8,128)}, u32[]{:S(2)}) copy-start(f32[512,1536]{1,0:T(8,128)} %copy-done) | copy-start | bytes 9437188

commit v10 on v9

--- a/solution.py
+++ b/solution.py
@@ -370,7 +370,7 @@
         in_specs=[pl.BlockSpec(memory_space=pltpu.SMEM)]
         + [IN_HBM if isinstance(at, tuple) else ANYWHERE for _, at in (*first, *second)]
         + [ANYWHERE] * len(after),
-        out_specs=[ANYWHERE] * 2,
+        out_specs=[IN_VMEM] * 2,
         scratch_shapes=[pltpu.SemaphoreType.DMA((2,))],
         compiler_params=compiler(VMEM),
         name="choose",

time: 190 us -> 148 us (0.78)
  the two profiles are of different devices: /device:TPU:0 before, /device:TPU:6 now
where the time goes in v10:
time: 148 us; the launch traced here: 147 us
  waiting for transfers between devices  55.4 us (37%)
  Pallas kernels  47.4 us (32%)
  blocking collectives  19 us (13%)
  starting transfers between devices  13.3 us (9%)
  local copies, waits for them, and re-layouts  9.6 us (6%)
    ppermute x9, waiting for transfers between devices, send(): return lax.ppermute(x, 'section', pairs)  55.4 us
    pallas_call x3, Pallas kernels, backward(): pl.pallas_call(functools.partial(backward_kernel, first, heads, width_all...  16.7 us
    ppermute x9, starting transfers between devices, send(): return lax.ppermute(x, 'section', pairs)  13.3 us
    unnamed x34, local copies, waits for them, and re-layouts  9.6 us
    pallas_call x1, Pallas kernels, forward(): pl.pallas_call(functools.partial(forward_kernel, heads, width_all), out_s...  8.39 us
    pallas_call x1, Pallas kernels, opened(): pl.pallas_call(functools.partial(open_kernel, pieces), out_shape=(jax.Sha...  6.81 us
    psum x1, blocking collectives, local(): total = lax.psum(join(rows, told, held), 'tensor')  6.63 us
    psum x1, blocking collectives, local(): own_inner = lax.psum(own_inner, 'tensor')  6.51 us
  transfers between devices with their start and end apart: 9, of which 6 were waited for; matrix products, arithmetic and copies ran while one was open for 0% of the time, Pallas kernels for 21%

profile of v10, /device:TPU:6, one launch (start us, length us, event | category | flops | bytes accessed | tf_op | source)
XLA Modules:
  0.0 147.0 jit_solution(12777021620005894534)
XLA Ops:
  1.3 0.7 pad_add_fusion.pick_ref
  1.9 6.8 %opened.1 = (f32[3,512]{1,0:T(4,128)}, f32[1,3712]{1,0:T(1,128)}, bf16[512,512]{1,0:T(8,128)(2,1)}, bf16[512,1536]{1,0:T(8,128)(2,1)}) custom-call(s32[3]{0:T(128)} %pad_add_fusion.pick_ref, bf16[512,1536]{1,0:T(8,128)(2,1)} %bitcast.16, bf16[1,2,512,1536]{3,2,1,0:T(8,128)(2,1)} %refs_3_.1, bf16[512,1536]{1,0:T(8,128)(2,1)} %bitcast.12, f32[1,1536]{1,0:T(1,128)} %gq_ref.5, ...), custom_call_target="tpu_custom_call" | custom-call | tf_op jit(solution)/shard_map/opened/pallas_call | solution.py:443
  8.8 0.0 copy-start.15
  8.8 0.5 collective-permute-start
  9.3 3.4 %collective-permute-start.1 = (f32[3,512]{1,0:T(4,128)}, f32[3,512]{1,0:T(4,128)S(1)}, u32[]{:S(2)}, u32[]{:S(2)}) collective-permute-start(f32[3,512]{1,0:T(4,128)} %get-tuple-element.25.rows_ref), channel_id=1, source_target_pairs={{16,28},{20,0},{24,4},{28,8},{0,12},{4,16},{8,20},{12,24},{17,29},... | collective-permute-start | bytes 18440 | tf_op jit(solution)/shard_map/ppermute | solution.py:488
  12.7 3.1 %collective-permute-done.1.held_ref.refs_3_ = f32[3,512]{1,0:T(4,128)S(1)} collective-permute-done((f32[3,512]{1,0:T(4,128)}, f32[3,512]{1,0:T(4,128)S(1)}, u32[]{:S(2)}, u32[]{:S(2)}) %collective-permute-start.1) | collective-permute-done | bytes 6176 | tf_op jit(solution)/shard_map/ppermute | solution.py:488
  15.8 0.0 copy-start.13
  15.8 0.0 collective-permute-done.told_ref.refs_2_.refs_5_.refs_6_
  15.8 0.0 copy-start.7
  15.8 0.6 copy-done.13
  16.4 0.0 copy-done.7
  16.4 3.8 %collective-permute-start.2 = (bf16[512,512]{1,0:T(8,128)(2,1)}, bf16[512,512]{1,0:T(8,128)(2,1)S(1)}, u32[]{:S(2)}, u32[]{:S(2)}) collective-permute-start(bf16[512,512]{1,0:T(8,128)(2,1)} %get-tuple-element.32), channel_id=1, source_target_pairs={{4,20},{8,24},{12,28},{20,4},{24,8},{28,12},{5,21},{9,25},{13,29},... | collective-permute-start | bytes 1572872 | tf_op jit(solution)/shard_map/ppermute | solution.py:488
  20.3 0.6 collective-permute-start.6
  20.8 0.1 pad_add_fusion.2.mode_ref
  20.9 0.0 copy-done.15
  20.9 0.0 copy-start.8
  20.9 0.7 copy-done.8
  21.6 0.0 copy-start.14
  21.6 0.7 copy-done.14
  22.3 0.1 join.1
  22.4 6.6 %psum.21.t_ref.refs_4_.refs_5_ = f32[3,512]{1,0:T(4,128)} all-reduce(f32[3,512]{1,0:T(4,128)S(1)} %join.1), channel_id=1, replica_groups=mesh['section'=8,'tensor'=4] {'tensor'}, use_global_device_ids=true, to_apply=%region_0.1 | all-reduce | flops 1536 | bytes 12288 | tf_op jit(solution)/shard_map/psum | solution.py:527
  29.0 2.9 %early_backward.1 = (f32[512,1536]{1,0:T(8,128)}, f32[1,512]{1,0:T(1,128)}) custom-call(s32[3]{0:T(128)} %pad_add_fusion.pick_ref, bf16[1,2,512,1536]{3,2,1,0:T(8,128)(2,1)} %refs_3_.1, bf16[512,1536]{1,0:T(8,128)(2,1)} %bitcast.13, f32[3,512]{1,0:T(4,128)} %psum.21.t_ref.refs_4_.refs_5_, f32[1,1536]{1,0:T(1,128)} %gq_ref.5, f32[1,1536]{1,0:T(1,128)} %gk_ref.5), custom_call_target="tpu_custom_call" | custom-call | tf_op jit(solution)/shard_map/early_backward/pallas_call | solution.py:252
  32.0 11.2 %collective-permute-done.2.refs_1_ = bf16[512,512]{1,0:T(8,128)(2,1)S(1)} collective-permute-done((bf16[512,512]{1,0:T(8,128)(2,1)}, bf16[512,512]{1,0:T(8,128)(2,1)S(1)}, u32[]{:S(2)}, u32[]{:S(2)}) %collective-permute-start.2) | collective-permute-done | bytes 524320 | tf_op jit(solution)/shard_map/ppermute | solution.py:488
  43.1 0.0 copy-start.16
  43.2 2.6 %choose.2 = (bf16[512,512]{1,0:T(8,128)(2,1)}, bf16[512,512]{1,0:T(8,128)(2,1)}) custom-call(s32[2]{0:T(128)S(1)} %pad_add_fusion.2.mode_ref, bf16[1,2,512,1536]{3,2,1,0:T(8,128)(2,1)} %refs_3_.1, bf16[512,512]{1,0:T(8,128)(2,1)S(1)} %collective-permute-done.2.refs_1_, bf16[1,2,512,1536]{3,2,1,0:T(8,128)(2,1)} %refs_3_.1, f32[1,512]{1,0:T(1,128)} %get-tuple-element.28.refs_3_), custom_call_target="tpu_custom_call" | custom-call | tf_op jit(solution)/shard_map/choose/pallas_call | solution.py:367
  45.8 1.9 %collective-permute-start.3 = (bf16[512,512]{1,0:T(8,128)(2,1)}, bf16[512,512]{1,0:T(8,128)(2,1)S(1)}, u32[]{:S(2)}, u32[]{:S(2)}) collective-permute-start(bf16[512,512]{1,0:T(8,128)(2,1)} %get-tuple-element.33), channel_id=1, source_target_pairs={{4,20},{8,24},{12,28},{20,4},{24,8},{28,12},{5,21},{9,25},{13,29},... | collective-permute-start | bytes 1572872 | tf_op jit(solution)/shard_map/ppermute | solution.py:488
  47.7 1.9 %collective-permute-start.4 = (bf16[512,512]{1,0:T(8,128)(2,1)}, bf16[512,512]{1,0:T(8,128)(2,1)S(1)}, u32[]{:S(2)}, u32[]{:S(2)}) collective-permute-start(bf16[512,512]{1,0:T(8,128)(2,1)} %get-tuple-element.35), channel_id=1, source_target_pairs={{4,0},{8,4},{12,8},{20,16},{24,20},{28,24},{5,1},{9,5},{13,9},{21,... | collective-permute-start | bytes 1572872 | tf_op jit(solution)/shard_map/ppermute | solution.py:488
  49.6 0.1 pad_add_fusion.1.mode_ref
  49.7 0.0 copy-done.16
  49.7 6.5 %psum.22.inner_ref = f32[1,512]{1,0:T(1,128)} all-reduce(f32[1,512]{1,0:T(1,128)S(1)} %copy-done.16), channel_id=1, replica_groups=mesh['section'=8,'tensor'=4] {'tensor'}, use_global_device_ids=true, to_apply=%region_1.2 | all-reduce | flops 512 | bytes 4096 | tf_op jit(solution)/shard_map/psum | solution.py:535
  56.2 0.0 copy-start.10
  56.2 0.0 copy-start.11
  56.2 0.0 copy-start.12
  56.2 3.4 %slot.1 = (bf16[512,1536]{1,0:T(8,128)(2,1)}, bf16[512,512]{1,0:T(8,128)(2,1)}) custom-call(s32[3]{0:T(128)} %pad_add_fusion.pick_ref, f32[512,1536]{1,0:T(8,128)} %get-tuple-element.27.a_ref, bf16[1,2,512,1536]{3,2,1,0:T(8,128)(2,1)} %refs_3_.1, bf16[512,1536]{1,0:T(8,128)(2,1)} %bitcast.14, f32[3,512]{1,0:T(4,128)} %psum.21.t_ref.refs_4_.refs_5_, ...), custom_call_target="tpu_custom_call" | custom-call | tf_op jit(solution)/shard_map/slot/pallas_call | solution.py:323
  59.6 0.0 collective-permute-start.7
  59.6 0.0 copy-done.10
  59.6 0.0 copy-done.11
  59.6 0.0 copy-done.12
  59.6 8.4 %forward.1.refs_5_ = bf16[512,1536]{1,0:T(8,128)(2,1)} custom-call(bf16[512,1536]{1,0:T(8,128)(2,1)} %bitcast.17, f32[3,512]{1,0:T(4,128)S(1)} %copy-done.10, f32[1,1536]{1,0:T(1,128)S(1)} %copy-done.11, f32[1,1536]{1,0:T(1,128)S(1)} %copy-done.12, bf16[512,512]{1,0:T(8,128)(2,1)} %get-tuple-element.29.rest_0_), custom_call_target="tpu_custom_call" | custom-call | tf_op jit(solution)/shard_map/forward/pallas_call | solution.py:119
  68.0 4.9 %collective-permute-done.3.refs_1_ = bf16[512,512]{1,0:T(8,128)(2,1)S(1)} collective-permute-done((bf16[512,512]{1,0:T(8,128)(2,1)}, bf16[512,512]{1,0:T(8,128)(2,1)S(1)}, u32[]{:S(2)}, u32[]{:S(2)}) %collective-permute-start.3) | collective-permute-done | bytes 524320 | tf_op jit(solution)/shard_map/ppermute | solution.py:488
  72.9 0.0 collective-permute-done.4.refs_6_.refs_0_
  72.9 2.7 %choose.3 = (bf16[512,512]{1,0:T(8,128)(2,1)}, bf16[512,512]{1,0:T(8,128)(2,1)}) custom-call(s32[2]{0:T(128)S(1)} %pad_add_fusion.1.mode_ref, bf16[1,2,512,1536]{3,2,1,0:T(8,128)(2,1)} %refs_3_.1, bf16[512,512]{1,0:T(8,128)(2,1)S(1)} %collective-permute-done.3.refs_1_, bf16[512,1536]{1,0:T(8,128)(2,1)} %get-tuple-element.34.refs_2_.refs_4_, ...), custom_call_target="tpu_custom_call" | custom-call | tf_op jit(solution)/shard_map/choose/pallas_call | solution.py:367
  75.6 0.0 copy-done.5
  75.6 0.1 collective-permute-start.8
  75.6 1.1 collective-permute-start.5
  76.7 0.1 add_convert_fusion.pick_ref
  76.8 1.8 %collective-permute-done.7.refs_3_.refs_2_ = bf16[512,512]{1,0:T(8,128)(2,1)S(1)} collective-permute-done((bf16[512,512]{1,0:T(8,128)(2,1)}, bf16[512,512]{1,0:T(8,128)(2,1)S(1)}, u32[]{:S(2)}, u32[]{:S(2)}) %collective-permute-start.7) | collective-permute-done | bytes 524320 | tf_op jit(solution)/shard_map/ppermute | solution.py:488
  78.6 0.8 copy-done.3
  79.4 0.0 collective-permute-done.6.refs_1_.refs_2_.refs_3_
  79.4 0.0 copy-done.9
  79.4 0.0 copy-start.4
  79.4 1.0 copy-done.4
  80.5 1.0 copy-done.6
  81.5 5.1 %backward.3 = (f32[512,1536]{1,0:T(8,128)S(1)}, bf16[512,1536]{1,0:T(8,128)(2,1)S(1)}, f32[1,512]{1,0:T(1,128)S(1)}) custom-call(s32[3]{0:T(128)S(1)} %add_convert_fusion.pick_ref, bf16[512,512]{1,0:T(8,128)(2,1)S(1)} %copy-done.6, bf16[512,1536]{1,0:T(8,128)(2,1)S(1)} %collective-permute-done.6.refs_1_.refs_2_.refs_3_, ...), custom_call_target="tpu_custom_call" | custom-call | tf_op jit(solution)/shard_map/backward/pallas_call | solution.py:208
  86.6 4.5 %collective-permute-done.8.refs_0_.refs_3_ = bf16[512,512]{1,0:T(8,128)(2,1)} collective-permute-done((bf16[512,512]{1,0:T(8,128)(2,1)}, bf16[512,512]{1,0:T(8,128)(2,1)}, u32[]{:S(2)}, u32[]{:S(2)}) %collective-permute-start.8) | collective-permute-done | bytes 524320 | tf_op jit(solution)/shard_map/ppermute | solution.py:488
  91.1 5.8 %backward.4 = (f32[512,1536]{1,0:T(8,128)S(1)}, bf16[512,1536]{1,0:T(8,128)(2,1)S(1)}, f32[1,512]{1,0:T(1,128)S(1)}) custom-call(s32[3]{0:T(128)S(1)} %add_convert_fusion.pick_ref, bf16[512,512]{1,0:T(8,128)(2,1)} %collective-permute-done.8.refs_0_.refs_3_, ...), custom_call_target="tpu_custom_call", output_to_operand_aliasing={{0}: (8, {}), {1}: (9, {})} | custom-call | tf_op jit(solution)/shard_map/backward/pallas_call | solution.py:208
  96.9 29.9 %collective-permute-done.5.refs_0_.refs_4_ = bf16[512,512]{1,0:T(8,128)(2,1)} collective-permute-done((bf16[512,512]{1,0:T(8,128)(2,1)}, bf16[512,512]{1,0:T(8,128)(2,1)}, u32[]{:S(2)}, u32[]{:S(2)}) %collective-permute-start.5) | collective-permute-done | bytes 524320 | tf_op jit(solution)/shard_map/ppermute | solution.py:488
  126.8 5.8 %backward.5 = (f32[512,1536]{1,0:T(8,128)S(1)}, bf16[512,1536]{1,0:T(8,128)(2,1)S(1)}, f32[1,512]{1,0:T(1,128)S(1)}) custom-call(s32[3]{0:T(128)S(1)} %add_convert_fusion.pick_ref, bf16[512,512]{1,0:T(8,128)(2,1)} %collective-permute-done.5.refs_0_.refs_4_, ...), custom_call_target="tpu_custom_call", output_to_operand_aliasing={{0}: (9, {}), {1}: (10, {})} | custom-call | tf_op jit(solution)/shard_map/backward/pallas_call | solution.py:208
  132.6 0.0 copy-start
  132.6 1.6 %copy-done = f32[512,1536]{1,0:T(8,128)} copy-done((f32[512,1536]{1,0:T(8,128)}, f32[512,1536]{1,0:T(8,128)S(1)}, u32[]{:S(2)}) %copy-start) | copy-done | bytes 3145752
  134.2 1.2 copy-done.2
  135.4 5.9 %psum.23.inner_ref = f32[1,512]{1,0:T(1,128)S(1)} all-reduce(f32[1,512]{1,0:T(1,128)S(1)} %get-tuple-element.47), channel_id=1, replica_groups=mesh['section'=8,'tensor'=4] {'tensor'}, use_global_device_ids=true, to_apply=%region_2.3 | all-reduce | flops 512 | bytes 4096 | tf_op jit(solution)/shard_map/psum | solution.py:561
  141.3 1.9 %copy-done.1 = f32[512,1536]{1,0:T(8,128)S(1)} copy-done((f32[512,1536]{1,0:T(8,128)S(1)}, f32[512,1536]{1,0:T(8,128)}, u32[]{:S(2)}) %copy-start.1) | copy-done | bytes 3145752
  143.2 3.8 %finish.1 = bf16[512,1536]{1,0:T(8,128)(2,1)} custom-call(s32[3]{0:T(128)S(1)} %add_convert_fusion.pick_ref, f32[512,1536]{1,0:T(8,128)S(1)} %copy-done.1, bf16[512,1536]{1,0:T(8,128)(2,1)} %copy-done.2, f32[3,512]{1,0:T(4,128)S(1)} %copy-done.10, f32[1,3712]{1,0:T(1,128)S(1)} %copy-done.9, f32[1,512]{1,0:T(1,128)S(1)} %psum.23.inner_ref), custom_call_target="tpu_custom_call" | custom-call | tf_op jit(solution)/shard_map/finish/pallas_call | solution.py:285
  (8 shorter events, 0.0 us)
Async XLA Ops:
  8.8 12.2 %copy-start.15 = (f32[3,512]{1,0:T(4,128)S(1)}, f32[3,512]{1,0:T(4,128)}, u32[]{:S(2)}) copy-start(f32[3,512]{1,0:T(4,128)} %get-tuple-element.25.rows_ref) | copy-start | bytes 18436
  8.8 7.1 %collective-permute-start = (f32[1,3712]{1,0:T(1,128)}, f32[1,3712]{1,0:T(1,128)S(1)}, u32[]{:S(2)}, u32[]{:S(2)}) collective-permute-start(f32[1,3712]{1,0:T(1,128)} %get-tuple-element.26), channel_id=1, source_target_pairs={{0,28},{4,0},{8,4},{12,8},{16,12},{20,16},{24,20},{28,24},{1,29},{... | collective-permute-start | bytes 44552 | tf_op jit(solution)/shard_map/ppermute | solution.py:488
  9.3 6.6 %collective-permute-start.1 = (f32[3,512]{1,0:T(4,128)}, f32[3,512]{1,0:T(4,128)S(1)}, u32[]{:S(2)}, u32[]{:S(2)}) collective-permute-start(f32[3,512]{1,0:T(4,128)} %get-tuple-element.25.rows_ref), channel_id=1, source_target_pairs={{16,28},{20,0},{24,4},{28,8},{0,12},{4,16},{8,20},{12,24},{17,29},... | collective-permute-start | bytes 18440 | tf_op jit(solution)/shard_map/ppermute | solution.py:488
  15.8 0.6 copy-start.13
  15.8 0.6 copy-start.7
  16.4 26.7 %collective-permute-start.2 = (bf16[512,512]{1,0:T(8,128)(2,1)}, bf16[512,512]{1,0:T(8,128)(2,1)S(1)}, u32[]{:S(2)}, u32[]{:S(2)}) collective-permute-start(bf16[512,512]{1,0:T(8,128)(2,1)} %get-tuple-element.32), channel_id=1, source_target_pairs={{4,20},{8,24},{12,28},{20,4},{24,8},{28,12},{5,21},{9,25},{13,29},... | collective-permute-start | bytes 1572872 | tf_op jit(solution)/shard_map/ppermute | solution.py:488
  20.3 59.2 %collective-permute-start.6 = (bf16[512,1536]{1,0:T(8,128)(2,1)}, bf16[512,1536]{1,0:T(8,128)(2,1)S(1)}, u32[]{:S(2)}, u32[]{:S(2)}) collective-permute-start(bf16[512,1536]{1,0:T(8,128)(2,1)} %get-tuple-element.37), channel_id=1, source_target_pairs={{4,0},{8,4},{12,8},{20,16},{24,20},{28,24},{16,28},{0,12},{5,1},{9... | collective-permute-start | bytes 4718600 | tf_op jit(solution)/shard_map/ppermute | solution.py:488
  20.9 0.7 copy-start.8
  21.6 0.7 copy-start.14
  43.1 6.6 %copy-start.16 = (f32[1,512]{1,0:T(1,128)S(1)}, f32[1,512]{1,0:T(1,128)}, u32[]{:S(2)}) copy-start(f32[1,512]{1,0:T(1,128)} %get-tuple-element.28.refs_3_) | copy-start | bytes 6148
  45.8 27.1 %collective-permute-start.3 = (bf16[512,512]{1,0:T(8,128)(2,1)}, bf16[512,512]{1,0:T(8,128)(2,1)S(1)}, u32[]{:S(2)}, u32[]{:S(2)}) collective-permute-start(bf16[512,512]{1,0:T(8,128)(2,1)} %get-tuple-element.33), channel_id=1, source_target_pairs={{4,20},{8,24},{12,28},{20,4},{24,8},{28,12},{5,21},{9,25},{13,29},... | collective-permute-start | bytes 1572872 | tf_op jit(solution)/shard_map/ppermute | solution.py:488
  47.7 25.2 %collective-permute-start.4 = (bf16[512,512]{1,0:T(8,128)(2,1)}, bf16[512,512]{1,0:T(8,128)(2,1)S(1)}, u32[]{:S(2)}, u32[]{:S(2)}) collective-permute-start(bf16[512,512]{1,0:T(8,128)(2,1)} %get-tuple-element.35), channel_id=1, source_target_pairs={{4,0},{8,4},{12,8},{20,16},{24,20},{28,24},{5,1},{9,5},{13,9},{21,... | collective-permute-start | bytes 1572872 | tf_op jit(solution)/shard_map/ppermute | solution.py:488
  56.2 3.4 %copy-start.10 = (f32[3,512]{1,0:T(4,128)S(1)}, f32[3,512]{1,0:T(4,128)}, u32[]{:S(2)}) copy-start(f32[3,512]{1,0:T(4,128)} %psum.21.t_ref.refs_4_.refs_5_) | copy-start | bytes 18436
  56.2 3.4 %copy-start.11 = (f32[1,1536]{1,0:T(1,128)S(1)}, f32[1,1536]{1,0:T(1,128)}, u32[]{:S(2)}) copy-start(f32[1,1536]{1,0:T(1,128)} %gq_ref.5) | copy-start | bytes 18436
  56.2 3.4 %copy-start.12 = (f32[1,1536]{1,0:T(1,128)S(1)}, f32[1,1536]{1,0:T(1,128)}, u32[]{:S(2)}) copy-start(f32[1,1536]{1,0:T(1,128)} %gk_ref.5) | copy-start | bytes 18436
  59.6 19.0 %collective-permute-start.7 = (bf16[512,512]{1,0:T(8,128)(2,1)}, bf16[512,512]{1,0:T(8,128)(2,1)S(1)}, u32[]{:S(2)}, u32[]{:S(2)}) collective-permute-start(bf16[512,512]{1,0:T(8,128)(2,1)} %get-tuple-element.29.rest_0_), channel_id=1, source_target_pairs={{0,28},{4,0},{8,4},{12,8},{16,12},{20,16},{24,20},{28,24},{1,29},{... | collective-permute-start | bytes 1572872 | tf_op jit(solution)/shard_map/ppermute | solution.py:488
  72.9 2.7 %copy-start.5 = (bf16[512,512]{1,0:T(8,128)(2,1)}, bf16[512,512]{1,0:T(8,128)(2,1)S(1)}, u32[]{:S(2)}) copy-start(bf16[512,512]{1,0:T(8,128)(2,1)S(1)} %collective-permute-done.4.refs_6_.refs_0_) | copy-start | bytes 1572868
  72.9 6.5 %copy-start.9 = (f32[1,3712]{1,0:T(1,128)S(1)}, f32[1,3712]{1,0:T(1,128)}, u32[]{:S(2)}) copy-start(f32[1,3712]{1,0:T(1,128)} %copy-done.7) | copy-start | bytes 44548
  75.6 15.6 %collective-permute-start.8 = (bf16[512,512]{1,0:T(8,128)(2,1)}, bf16[512,512]{1,0:T(8,128)(2,1)}, u32[]{:S(2)}, u32[]{:S(2)}) collective-permute-start(bf16[512,512]{1,0:T(8,128)(2,1)} %get-tuple-element.38), channel_id=1, source_target_pairs={{0,28},{4,0},{8,4},{12,8},{16,12},{20,16},{24,20},{28,24},{1,29},{... | collective-permute-start | bytes 1572872 | tf_op jit(solution)/shard_map/ppermute | solution.py:488
  75.6 51.2 %collective-permute-start.5 = (bf16[512,512]{1,0:T(8,128)(2,1)}, bf16[512,512]{1,0:T(8,128)(2,1)}, u32[]{:S(2)}, u32[]{:S(2)}) collective-permute-start(bf16[512,512]{1,0:T(8,128)(2,1)} %get-tuple-element.36), channel_id=1, source_target_pairs={{20,0},{24,4},{28,8},{4,16},{8,20},{12,24},{16,12},{0,28},{21,1},{... | collective-permute-start | bytes 1572872 | tf_op jit(solution)/shard_map/ppermute | solution.py:488
  78.6 0.8 copy-start.3
  79.4 1.0 copy-start.4
  80.5 1.0 copy-start.6
  132.6 1.6 %copy-start = (f32[512,1536]{1,0:T(8,128)}, f32[512,1536]{1,0:T(8,128)S(1)}, u32[]{:S(2)}) copy-start(f32[512,1536]{1,0:T(8,128)S(1)} %get-tuple-element.45.a_ref) | copy-start | bytes 9437188
  134.2 1.2 copy-start.2
  141.3 1.9 %copy-start.1 = (f32[512,1536]{1,0:T(8,128)S(1)}, f32[512,1536]{1,0:T(8,128)}, u32[]{:S(2)}) copy-start(f32[512,1536]{1,0:T(8,128)} %copy-done) | copy-start | bytes 9437188

commit v11 on v10

--- a/solution.py
+++ b/solution.py
@@ -158,66 +158,88 @@
     return wide, d_normed
 
 
-def selected(which, refs, at):
-    values = [ref[lanes_of(start + at, HDIM)] for ref, start in refs]
-    value = values[0]
-    for i, other in enumerate(values[1:]):
-        value = jnp.where(which == i + 1, other, value)
-    return value
-
-
-def backward_kernel(first, heads, width_all, x_at, g_at, pick_ref, *refs):
+def backward_kernel(first, heads, width_all, x_at, g_at, odd, pick_ref, *refs):
     n_x, n_g = len(x_at), len(g_at)
-    unevicted = x_at[-1] is None
-    xs = list(zip(refs[:n_x], [at or 0 for at in x_at]))
-    gs = list(zip(refs[n_x : n_x + n_g], g_at))
+    x_refs, g_refs = refs[:n_x], refs[n_x : n_x + n_g]
     t_ref, told_ref, past_ref = refs[n_x + n_g : n_x + n_g + 3]
-    a_ref, x_ref, inner_ref = refs[-3:]
-    tokens, width = a_ref.shape
+    a_out, x_out, inner_ref, xs, gs, owns, outs, x_sem, g_sem, own_sem, a_sem, out_sem = refs[-12:]
+    tokens, width = a_out.shape
+
+    def piece(ref, start, h):
+        return ref.at[lanes_of(start + h * HDIM, HDIM)]
+
+    copies = {}
+    for h in range(heads):
+        to = lanes_of(h * HDIM, HDIM)
+        copies[h] = [
+            (which == i, pltpu.make_async_copy(piece(ref, at, h), into.at[to], sem.at[h]))
+            for which, sources, starts, into, sem in (
+                (pick_ref[0], x_refs[: n_x - odd], x_at, xs, x_sem),
+                (pick_ref[1], g_refs, g_at, gs, g_sem),
+            )
+            for i, (ref, at) in enumerate(zip(sources, starts))
+        ]
+        for wanted, copy in copies[h]:
+            pl.when(wanted)(copy.start)
+        if odd:
+            own = pltpu.make_async_copy(piece(x_refs[-1], x_at[-1], h), owns.at[to], own_sem.at[h])
+            own.start()
+            copies[h].append((None, own))
+
+    evicted = told_ref[:, tokens + 2 * width :] == 1.0
     factor = column_of(inverse_rms(t_ref[2:3, :], width_all))
-    evicted = told_ref[:, tokens + 2 * width :] == 1.0
     ready = jnp.logical_and(pick_ref[2] == 1, jnp.logical_not(evicted))
     part = None
+    sent = []
     for h in range(heads):
+        for wanted, copy in copies[h]:
+            if wanted is None:
+                copy.wait()
+            else:
+                pl.when(wanted)(copy.wait)
         at = h * HDIM
-        mine = lanes_of(first + at, HDIM)
+        mine = lanes_of(at, HDIM)
         gain_q = told_ref[lanes_of(tokens + first + at, HDIM)]
         gain_k = told_ref[lanes_of(tokens + width + first + at, HDIM)]
-        if unevicted:
-            straight, start = xs[0]
-            own, own_start = xs[-1]
-            x = jnp.where(evicted, straight[lanes_of(start + at, HDIM)].astype(F32), own[lanes_of(own_start + at, HDIM)].astype(F32))
-            x = x.astype(BF16)
-            for i, (ref, start) in enumerate(xs[1:-1]):
-                x = jnp.where(pick_ref[0] == i + 1, ref[lanes_of(start + at, HDIM)], x)
-        else:
-            x = selected(pick_ref[0], xs, at)
-        g = selected(pick_ref[1], gs, at)
+        x, g = xs[mine], gs[mine]
+        if odd:
+            stays = jnp.logical_or(evicted, pick_ref[0] > 0)
+            x = jnp.where(stays, x.astype(F32), owns[mine].astype(F32)).astype(BF16)
+            xs[mine] = x
         wide, d_normed = backward_head(x, g, factor, gain_q, gain_k)
-        a_ref[mine] = g.astype(F32) + jnp.where(ready, 0.0, factor * d_normed)
-        x_ref[mine] = x
+        outs[mine] = g.astype(F32) + jnp.where(ready, 0.0, factor * d_normed)
+        to = lanes_of(first + at, HDIM)
+        sent.append(pltpu.make_async_copy(outs.at[mine], a_out.at[to], a_sem.at[h]))
+        sent.append(pltpu.make_async_copy(xs.at[mine], x_out.at[to], out_sem.at[h]))
+        for copy in sent[-2:]:
+            copy.start()
         product = d_normed * wide
         part = product if part is None else part + product
-    inner = jnp.sum(part.T, axis=0, keepdims=True)
-    inner_ref[...] = inner if past_ref is None else inner + past_ref[...]
-
-
-def backward(width_all, width, pick, xs, gs, totals, told, past, heads, first, sofar=(), after=()):
+    inner_ref[...] = jnp.sum(part.T, axis=0, keepdims=True) + past_ref[...]
+    for copy in sent:
+        copy.wait()
+
+
+def backward(width_all, width, pick, xs, gs, totals, told, past, heads, first, sofar=(), after=(), odd=False):
     tokens = totals.shape[1]
-    before = 1 + len(xs) + len(gs) + 3
+    lanes = heads * HDIM
+    count = 1 + len(xs) + len(gs) + 3
+    dma = pltpu.SemaphoreType.DMA((heads,))
+    small = (tokens, lanes)
     return pl.pallas_call(
         functools.partial(
-            backward_kernel, first, heads, width_all, tuple(at for _, at in xs), tuple(at for _, at in gs)
+            backward_kernel, first, heads, width_all, tuple(at for _, at in xs), tuple(at for _, at in gs), int(odd)
         ),
         out_shape=(
-            jax.ShapeDtypeStruct((tokens, width), F32),
-            jax.ShapeDtypeStruct((tokens, width), BF16),
+            pltpu.HBM((tokens, width), F32),
+            pltpu.HBM((tokens, width), BF16),
             jax.ShapeDtypeStruct((1, tokens), F32),
         ),
-        in_specs=[pl.BlockSpec(memory_space=pltpu.SMEM)] + [IN_VMEM] * (before - 1 + len(sofar))
-        + [IN_HBM] * len(after),
-        out_specs=(IN_VMEM, IN_VMEM, IN_VMEM),
-        input_output_aliases={before: 0, before + 1: 1} if sofar else {},
+        in_specs=[pl.BlockSpec(memory_space=pltpu.SMEM)] + [ANYWHERE] * (len(xs) + len(gs)) + [IN_VMEM] * 3
+        + [IN_HBM] * len(sofar) + [ANYWHERE] * len(after),
+        out_specs=(IN_HBM, IN_HBM, IN_VMEM),
+        input_output_aliases={count: 0, count + 1: 1} if sofar else {},
+        scratch_shapes=[pltpu.VMEM(small, BF16)] * 3 + [pltpu.VMEM(small, F32)] + [dma] * 5,
         compiler_params=compiler(VMEM),
         name="backward",
     )(pick, *[x for x, _ in xs], *[g for g, _ in gs], totals, told, past, *sofar, *after)
@@ -270,27 +292,25 @@
     return inverse_rms(total, width_all) ** 3 * inner / width_all
 
 
-def finish_kernel(lanes, width_all, pick_ref, a_ref, x_ref, t_ref, told_ref, inner_ref, o_ref):
-    tokens, width = a_ref.shape
-    evicted = told_ref[:, tokens + 2 * width : tokens + 2 * width + 1] == 1.0
+def finish_kernel(width_all, pick_ref, a_ref, x_ref, t_ref, told_ref, inner_ref, o_ref):
+    evicted = told_ref[:, told_ref.shape[1] - 1 :] == 1.0
     ready = jnp.logical_and(pick_ref[2] == 1, jnp.logical_not(evicted))
     row = jnp.where(ready, 0.0, row_of(t_ref[2:3, :], inner_ref[...], width_all))
-    at = (slice(None), pl.ds(pl.program_id(0) * lanes, lanes))
-    o_ref[...] = (a_ref[at] - x_ref[...].astype(F32) * column_of(row)).astype(BF16)
+    o_ref[...] = (a_ref[...] - x_ref[...].astype(F32) * column_of(row)).astype(BF16)
 
 
 def finish(width_all, pick, a, x, totals, told, inner, lanes):
     tokens, width = a.shape
     block = pl.BlockSpec((tokens, lanes), lambda i: (0, i))
     return pl.pallas_call(
-        functools.partial(finish_kernel, lanes, width_all),
+        functools.partial(finish_kernel, width_all),
         out_shape=jax.ShapeDtypeStruct(a.shape, BF16),
         grid=(width // lanes,),
-        in_specs=[pl.BlockSpec(memory_space=pltpu.SMEM), IN_VMEM, block] + [IN_VMEM] * 3,
+        in_specs=[pl.BlockSpec(memory_space=pltpu.SMEM), block, block] + [IN_VMEM] * 3,
         out_specs=block,
         compiler_params=compiler(VMEM),
         name="finish",
-    )(pick, a, in_hbm(x), totals, told, inner)
+    )(pick, in_hbm(a), in_hbm(x), totals, told, inner)
 
 
 def slot_kernel(width_all, last, pick_ref, a_ref, x_ref, g_ref, t_ref, inner_ref, o_ref, kept_ref):
@@ -536,27 +556,25 @@
     slot, last = slot_of(width_all, early_pick, own_a, stashed, upstream, total, own_inner, step)
     kept = send(last, prior)
     slot = in_hbm(slot)
-    output = forward(width_all, current, total, query_gain, key_gain, heads, (last,))
-
     sent, last = choose(
         mode, [(stash, (0, 1)), (fetched, 0), (slot, 1)], [(stash, (1, 2)), (slot, 2)], tokens, step,
-        (in_hbm(output), passed[0]),
     )
     straight = send(last, direct)
     passed.append(send(sent, prior))
 
+    output = forward(width_all, current, total, query_gain, key_gain, heads, (sent,))
+
     share = functools.partial(backward, width_all, width)
     a, x, inner = share(
-        take, [(passed[0], 0), (early, 0)], [(early, 0), (kept, 0)], total, told,
-        jnp.zeros((1, tokens), F32), heads, 0,
+        take, [(passed[0], 0), (early, 0)], [(early, 0), (kept, 0)], total, told, jnp.zeros((1, tokens), F32), heads, 0,
+        after=(in_hbm(output),),
     )
     a, x, inner = share(
-        take, [(passed[1], 0), (early, step)], [(early, step), (passed[1], 0)],
-        total, told, inner, heads, step, (a, x),
+        take, [(passed[1], 0), (early, step)], [(early, step), (passed[1], 0)], total, told, inner, heads, step, (a, x),
     )
     a, x, inner = share(
-        take, [(straight, 0), (early, 2 * step), (kept, None)], [(early, 2 * step), (straight, 0)],
-        total, told, inner, heads, 2 * step, (a, x),
+        take, [(straight, 0), (early, 2 * step), (kept, 0)], [(early, 2 * step), (straight, 0)],
+        total, told, inner, heads, 2 * step, (a, x), odd=True,
     )
     inner = lax.psum(inner, "tensor")
     result = finish(width_all, take, a, x, total, told, inner, step)

time: 148 us -> 146 us (0.986)
  local copies, waits for them, and re-layouts: 9.6 us -> 2.04 us
  Pallas kernels: 47.4 us -> 53.1 us
  starting transfers between devices: 13.3 us -> 17.2 us
  waiting for transfers between devices: 55.4 us -> 51.5 us
    unnamed x34 -> x20, local copies, waits for them, and re-layouts: 9.6 us -> 2.03 us
    pallas_call x3, Pallas kernels: 16.7 us -> 21.7 us  [backward(): pl.pallas_call(functools.partial(backward_kernel, first, heads, width_all...]
    ppermute x9, waiting for transfers between devices: 55.4 us -> 51.5 us  [send(): return lax.ppermute(x, 'section', pairs)]
    ppermute x9, starting transfers between devices: 13.3 us -> 17.2 us  [send(): return lax.ppermute(x, 'section', pairs)]
  transfers between devices with their start and end apart: 9 -> 9, of which waited for: 6 -> 6; matrix products, arithmetic and copies ran while one was open for 0% -> 0% of each run, Pallas kernels for 21% -> 24%
where the time goes in v11:
time: 146 us; the launch traced here: 145 us
  Pallas kernels  53.1 us (36%)
  waiting for transfers between devices  51.5 us (35%)
  blocking collectives  19.1 us (13%)
  starting transfers between devices  17.2 us (12%)
  local copies, waits for them, and re-layouts  2.04 us (1%)
    ppermute x9, waiting for transfers between devices, send(): return lax.ppermute(x, 'section', pairs)  51.5 us
    pallas_call x3, Pallas kernels, backward(): pl.pallas_call(functools.partial(backward_kernel, first, heads, width_all...  21.7 us
    ppermute x9, starting transfers between devices, send(): return lax.ppermute(x, 'section', pairs)  17.2 us
    pallas_call x1, Pallas kernels, forward(): pl.pallas_call(functools.partial(forward_kernel, heads, width_all), out_s...  8.4 us
    pallas_call x1, Pallas kernels, opened(): pl.pallas_call(functools.partial(open_kernel, pieces), out_shape=(jax.Sha...  6.81 us
    psum x1, blocking collectives, local(): total = lax.psum(join(rows, told, held), 'tensor')  6.64 us
    psum x1, blocking collectives, local(): own_inner = lax.psum(own_inner, 'tensor')  6.52 us
    psum x1, blocking collectives, local(): inner = lax.psum(inner, 'tensor')  5.91 us
  transfers between devices with their start and end apart: 9, of which 6 were waited for; matrix products, arithmetic and copies ran while one was open for 0% of the time, Pallas kernels for 24%

profile of v11, /device:TPU:6, one launch (start us, length us, event | category | flops | bytes accessed | tf_op | source)
XLA Modules:
  0.0 145.2 jit_solution(2692875454665312276)
XLA Ops:
  1.3 0.7 pad_add_fusion.pick_ref
  2.0 6.8 %opened.1 = (f32[3,512]{1,0:T(4,128)}, f32[1,3712]{1,0:T(1,128)}, bf16[512,512]{1,0:T(8,128)(2,1)}, bf16[512,1536]{1,0:T(8,128)(2,1)}) custom-call(s32[3]{0:T(128)} %pad_add_fusion.pick_ref, bf16[512,1536]{1,0:T(8,128)(2,1)} %bitcast.15, bf16[1,2,512,1536]{3,2,1,0:T(8,128)(2,1)} %refs_3_.1, bf16[512,1536]{1,0:T(8,128)(2,1)} %bitcast.12, f32[1,1536]{1,0:T(1,128)} %gq_ref.5, ...), custom_call_target="tpu_custom_call" | custom-call | tf_op jit(solution)/shard_map/opened/pallas_call | solution.py:463
  8.8 0.0 copy-start.8
  8.8 0.5 collective-permute-start
  9.3 3.4 %collective-permute-start.1 = (f32[3,512]{1,0:T(4,128)}, f32[3,512]{1,0:T(4,128)S(1)}, u32[]{:S(2)}, u32[]{:S(2)}) collective-permute-start(f32[3,512]{1,0:T(4,128)} %get-tuple-element.25.rows_ref), channel_id=1, source_target_pairs={{16,28},{20,0},{24,4},{28,8},{0,12},{4,16},{8,20},{12,24},{17,29},... | collective-permute-start | bytes 18440 | tf_op jit(solution)/shard_map/ppermute | solution.py:508
  12.7 3.1 %collective-permute-done.1.held_ref.refs_3_ = f32[3,512]{1,0:T(4,128)S(1)} collective-permute-done((f32[3,512]{1,0:T(4,128)}, f32[3,512]{1,0:T(4,128)S(1)}, u32[]{:S(2)}, u32[]{:S(2)}) %collective-permute-start.1) | collective-permute-done | bytes 6176 | tf_op jit(solution)/shard_map/ppermute | solution.py:508
  15.8 0.0 copy-start.6
  15.8 0.0 collective-permute-done.told_ref.refs_2_.refs_5_.refs_6_
  15.8 0.0 copy-start
  15.8 0.6 copy-done.6
  16.4 0.0 copy-done
  16.4 3.8 %collective-permute-start.2 = (bf16[512,512]{1,0:T(8,128)(2,1)}, bf16[512,512]{1,0:T(8,128)(2,1)S(1)}, u32[]{:S(2)}, u32[]{:S(2)}) collective-permute-start(bf16[512,512]{1,0:T(8,128)(2,1)} %get-tuple-element.29), channel_id=1, source_target_pairs={{4,20},{8,24},{12,28},{20,4},{24,8},{28,12},{5,21},{9,25},{13,29},... | collective-permute-start | bytes 1572872 | tf_op jit(solution)/shard_map/ppermute | solution.py:508
  20.3 0.6 collective-permute-start.5
  20.8 0.1 pad_add_fusion.2.mode_ref
  20.9 0.0 copy-done.8
  20.9 0.0 copy-start.1
  20.9 0.7 copy-done.1
  21.6 0.0 copy-start.7
  21.6 0.7 copy-done.7
  22.3 0.1 join.1
  22.4 6.6 %psum.21.t_ref.refs_4_.refs_5_ = f32[3,512]{1,0:T(4,128)} all-reduce(f32[3,512]{1,0:T(4,128)S(1)} %join.1), channel_id=1, replica_groups=mesh['section'=8,'tensor'=4] {'tensor'}, use_global_device_ids=true, to_apply=%region_0.1 | all-reduce | flops 1536 | bytes 12288 | tf_op jit(solution)/shard_map/psum | solution.py:547
  29.0 2.9 %early_backward.1 = (f32[512,1536]{1,0:T(8,128)}, f32[1,512]{1,0:T(1,128)}) custom-call(s32[3]{0:T(128)} %pad_add_fusion.pick_ref, bf16[1,2,512,1536]{3,2,1,0:T(8,128)(2,1)} %refs_3_.1, bf16[512,1536]{1,0:T(8,128)(2,1)} %bitcast.13, f32[3,512]{1,0:T(4,128)} %psum.21.t_ref.refs_4_.refs_5_, f32[1,1536]{1,0:T(1,128)} %gq_ref.5, f32[1,1536]{1,0:T(1,128)} %gk_ref.5), custom_call_target="tpu_custom_call" | custom-call | tf_op jit(solution)/shard_map/early_backward/pallas_call | solution.py:274
  32.0 11.2 %collective-permute-done.2.refs_1_ = bf16[512,512]{1,0:T(8,128)(2,1)S(1)} collective-permute-done((bf16[512,512]{1,0:T(8,128)(2,1)}, bf16[512,512]{1,0:T(8,128)(2,1)S(1)}, u32[]{:S(2)}, u32[]{:S(2)}) %collective-permute-start.2) | collective-permute-done | bytes 524320 | tf_op jit(solution)/shard_map/ppermute | solution.py:508
  43.2 0.0 copy-start.9
  43.2 2.6 %choose.2 = (bf16[512,512]{1,0:T(8,128)(2,1)}, bf16[512,512]{1,0:T(8,128)(2,1)S(1)}) custom-call(s32[2]{0:T(128)S(1)} %pad_add_fusion.2.mode_ref, bf16[1,2,512,1536]{3,2,1,0:T(8,128)(2,1)} %refs_3_.1, bf16[512,512]{1,0:T(8,128)(2,1)S(1)} %collective-permute-done.2.refs_1_, bf16[1,2,512,1536]{3,2,1,0:T(8,128)(2,1)} %refs_3_.1, f32[1,512]{1,0:T(1,128)} %get-tuple-element.30.refs_3_), custom_call_target="tpu_custom_call" | custom-call | tf_op jit(solution)/shard_map/choose/pallas_call | solution.py:387
  45.7 1.9 %collective-permute-start.3 = (bf16[512,512]{1,0:T(8,128)(2,1)S(1)}, bf16[512,512]{1,0:T(8,128)(2,1)S(1)}, u32[]{:S(2)}, u32[]{:S(2)}) collective-permute-start(bf16[512,512]{1,0:T(8,128)(2,1)S(1)} %get-tuple-element.31), channel_id=1, source_target_pairs={{4,20},{8,24},{12,28},{20,4},{24,8},{28,12},{5,21},{9,25},{13,29},... | collective-permute-start | bytes 1572872 | tf_op jit(solution)/shard_map/ppermute | solution.py:508
  47.7 0.1 pad_add_fusion.1.mode_ref
  47.7 0.0 copy-done.9
  47.7 6.5 %psum.22.inner_ref = f32[1,512]{1,0:T(1,128)} all-reduce(f32[1,512]{1,0:T(1,128)S(1)} %copy-done.9), channel_id=1, replica_groups=mesh['section'=8,'tensor'=4] {'tensor'}, use_global_device_ids=true, to_apply=%region_1.2 | all-reduce | flops 512 | bytes 4096 | tf_op jit(solution)/shard_map/psum | solution.py:555
  54.3 3.2 %slot.1 = (bf16[512,1536]{1,0:T(8,128)(2,1)}, bf16[512,512]{1,0:T(8,128)(2,1)}) custom-call(s32[3]{0:T(128)} %pad_add_fusion.pick_ref, f32[512,1536]{1,0:T(8,128)} %get-tuple-element.32.a_ref, bf16[1,2,512,1536]{3,2,1,0:T(8,128)(2,1)} %refs_3_.1, bf16[512,1536]{1,0:T(8,128)(2,1)} %bitcast.14, f32[3,512]{1,0:T(4,128)} %psum.21.t_ref.refs_4_.refs_5_, ...), custom_call_target="tpu_custom_call" | custom-call | tf_op jit(solution)/shard_map/slot/pallas_call | solution.py:343
  57.5 0.0 collective-permute-start.6
  57.5 6.2 %collective-permute-start.8 = (bf16[512,512]{1,0:T(8,128)(2,1)}, bf16[512,512]{1,0:T(8,128)(2,1)}, u32[]{:S(2)}, u32[]{:S(2)}) collective-permute-start(bf16[512,512]{1,0:T(8,128)(2,1)} %get-tuple-element.38), channel_id=1, source_target_pairs={{4,0},{8,4},{12,8},{20,16},{24,20},{28,24},{5,1},{9,5},{13,9},{21,... | collective-permute-start | bytes 1572872 | tf_op jit(solution)/shard_map/ppermute | solution.py:508
  63.7 8.9 %collective-permute-done.3.refs_1_ = bf16[512,512]{1,0:T(8,128)(2,1)S(1)} collective-permute-done((bf16[512,512]{1,0:T(8,128)(2,1)S(1)}, bf16[512,512]{1,0:T(8,128)(2,1)S(1)}, u32[]{:S(2)}, u32[]{:S(2)}) %collective-permute-start.3) | collective-permute-done | bytes 524320 | tf_op jit(solution)/shard_map/ppermute | solution.py:508
  72.6 0.0 copy-start.3
  72.6 0.0 copy-start.4
  72.6 0.0 copy-start.5
  72.6 2.8 %choose.3 = (bf16[512,512]{1,0:T(8,128)(2,1)}, bf16[512,512]{1,0:T(8,128)(2,1)}) custom-call(s32[2]{0:T(128)S(1)} %pad_add_fusion.1.mode_ref, bf16[1,2,512,1536]{3,2,1,0:T(8,128)(2,1)} %refs_3_.1, bf16[512,512]{1,0:T(8,128)(2,1)S(1)} %collective-permute-done.3.refs_1_, bf16[512,1536]{1,0:T(8,128)(2,1)} %get-tuple-element.33.refs_2_.refs_4_, ...), custom_call_target="tpu_custom_call" | custom-call | tf_op jit(solution)/shard_map/choose/pallas_call | solution.py:387
  75.4 0.1 collective-permute-start.7
  75.5 0.6 collective-permute-start.4
  76.1 0.1 add_convert_fusion.pick_ref
  76.1 0.0 copy-done.3
  76.1 0.0 copy-done.4
  76.2 0.0 copy-done.5
  76.2 0.0 copy-start.2
  76.2 8.4 %forward.1.refs_7_ = bf16[512,1536]{1,0:T(8,128)(2,1)} custom-call(bf16[512,1536]{1,0:T(8,128)(2,1)} %bitcast.16, f32[3,512]{1,0:T(4,128)S(1)} %copy-done.3, f32[1,1536]{1,0:T(1,128)S(1)} %copy-done.4, f32[1,1536]{1,0:T(1,128)S(1)} %copy-done.5, bf16[512,512]{1,0:T(8,128)(2,1)} %get-tuple-element.34.rest_0_), custom_call_target="tpu_custom_call" | custom-call | tf_op jit(solution)/shard_map/forward/pallas_call | solution.py:119
  84.6 0.0 collective-permute-done.6.refs_3_.refs_2_
  84.6 0.2 collective-permute-done.8.refs_0_
  84.8 0.0 collective-permute-done.5.refs_1_.refs_2_.refs_3_
  84.8 0.0 copy-done.2
  84.8 7.5 %backward.3 = (f32[512,1536]{1,0:T(8,128)}, bf16[512,1536]{1,0:T(8,128)(2,1)}, f32[1,512]{1,0:T(1,128)S(1)}) custom-call(s32[3]{0:T(128)S(1)} %add_convert_fusion.pick_ref, bf16[512,512]{1,0:T(8,128)(2,1)} %collective-permute-done.8.refs_0_, bf16[512,1536]{1,0:T(8,128)(2,1)S(1)} %collective-permute-done.5.refs_1_.refs_2_.refs_3_, ...), custom_call_target="tpu_custom_call" | custom-call | tf_op jit(solution)/shard_map/backward/pallas_call | solution.py:229
  92.3 2.1 %collective-permute-done.7.refs_0_.refs_3_ = bf16[512,512]{1,0:T(8,128)(2,1)S(1)} collective-permute-done((bf16[512,512]{1,0:T(8,128)(2,1)}, bf16[512,512]{1,0:T(8,128)(2,1)S(1)}, u32[]{:S(2)}, u32[]{:S(2)}) %collective-permute-start.7) | collective-permute-done | bytes 524320 | tf_op jit(solution)/shard_map/ppermute | solution.py:508
  94.5 6.9 %backward.4 = (f32[512,1536]{1,0:T(8,128)}, bf16[512,1536]{1,0:T(8,128)(2,1)}, f32[1,512]{1,0:T(1,128)S(1)}) custom-call(s32[3]{0:T(128)S(1)} %add_convert_fusion.pick_ref, bf16[512,512]{1,0:T(8,128)(2,1)S(1)} %collective-permute-done.7.refs_0_.refs_3_, ...), custom_call_target="tpu_custom_call", output_to_operand_aliasing={{0}: (8, {}), {1}: (9, {})} | custom-call | tf_op jit(solution)/shard_map/backward/pallas_call | solution.py:229
  101.4 26.0 %collective-permute-done.4.refs_0_.refs_4_ = bf16[512,512]{1,0:T(8,128)(2,1)S(1)} collective-permute-done((bf16[512,512]{1,0:T(8,128)(2,1)}, bf16[512,512]{1,0:T(8,128)(2,1)S(1)}, u32[]{:S(2)}, u32[]{:S(2)}) %collective-permute-start.4) | collective-permute-done | bytes 524320 | tf_op jit(solution)/shard_map/ppermute | solution.py:508
  127.4 7.3 %backward.5 = (f32[512,1536]{1,0:T(8,128)}, bf16[512,1536]{1,0:T(8,128)(2,1)}, f32[1,512]{1,0:T(1,128)S(1)}) custom-call(s32[3]{0:T(128)S(1)} %add_convert_fusion.pick_ref, bf16[512,512]{1,0:T(8,128)(2,1)S(1)} %collective-permute-done.4.refs_0_.refs_4_, ...), custom_call_target="tpu_custom_call", output_to_operand_aliasing={{0}: (9, {}), {1}: (10, {})} | custom-call | tf_op jit(solution)/shard_map/backward/pallas_call | solution.py:229
  134.6 5.9 %psum.23.inner_ref = f32[1,512]{1,0:T(1,128)S(1)} all-reduce(f32[1,512]{1,0:T(1,128)S(1)} %get-tuple-element.47), channel_id=1, replica_groups=mesh['section'=8,'tensor'=4] {'tensor'}, use_global_device_ids=true, to_apply=%region_2.3 | all-reduce | flops 512 | bytes 4096 | tf_op jit(solution)/shard_map/psum | solution.py:579
  140.5 4.7 %finish.1 = bf16[512,1536]{1,0:T(8,128)(2,1)} custom-call(s32[3]{0:T(128)S(1)} %add_convert_fusion.pick_ref, f32[512,1536]{1,0:T(8,128)} %get-tuple-element.45.a_ref, bf16[512,1536]{1,0:T(8,128)(2,1)} %get-tuple-element.46.x_ref, f32[3,512]{1,0:T(4,128)S(1)} %copy-done.3, f32[1,3712]{1,0:T(1,128)S(1)} %copy-done.2, f32[1,512]{1,0:T(1,128)S(1)} %psum.23.inner_ref), custom_call_target="tpu_custom_call" | custom-call | tf_op jit(solution)/shard_map/finish/pallas_call | solution.py:305
  (2 shorter events, 0.0 us)
Async XLA Ops:
  8.8 12.2 %copy-start.8 = (f32[3,512]{1,0:T(4,128)S(1)}, f32[3,512]{1,0:T(4,128)}, u32[]{:S(2)}) copy-start(f32[3,512]{1,0:T(4,128)} %get-tuple-element.25.rows_ref) | copy-start | bytes 18436
  8.8 7.1 %collective-permute-start = (f32[1,3712]{1,0:T(1,128)}, f32[1,3712]{1,0:T(1,128)S(1)}, u32[]{:S(2)}, u32[]{:S(2)}) collective-permute-start(f32[1,3712]{1,0:T(1,128)} %get-tuple-element.26), channel_id=1, source_target_pairs={{0,28},{4,0},{8,4},{12,8},{16,12},{20,16},{24,20},{28,24},{1,29},{... | collective-permute-start | bytes 44552 | tf_op jit(solution)/shard_map/ppermute | solution.py:508
  9.3 6.6 %collective-permute-start.1 = (f32[3,512]{1,0:T(4,128)}, f32[3,512]{1,0:T(4,128)S(1)}, u32[]{:S(2)}, u32[]{:S(2)}) collective-permute-start(f32[3,512]{1,0:T(4,128)} %get-tuple-element.25.rows_ref), channel_id=1, source_target_pairs={{16,28},{20,0},{24,4},{28,8},{0,12},{4,16},{8,20},{12,24},{17,29},... | collective-permute-start | bytes 18440 | tf_op jit(solution)/shard_map/ppermute | solution.py:508
  15.8 0.6 copy-start.6
  15.8 0.6 copy-start
  16.4 26.7 %collective-permute-start.2 = (bf16[512,512]{1,0:T(8,128)(2,1)}, bf16[512,512]{1,0:T(8,128)(2,1)S(1)}, u32[]{:S(2)}, u32[]{:S(2)}) collective-permute-start(bf16[512,512]{1,0:T(8,128)(2,1)} %get-tuple-element.29), channel_id=1, source_target_pairs={{4,20},{8,24},{12,28},{20,4},{24,8},{28,12},{5,21},{9,25},{13,29},... | collective-permute-start | bytes 1572872 | tf_op jit(solution)/shard_map/ppermute | solution.py:508
  20.3 64.5 %collective-permute-start.5 = (bf16[512,1536]{1,0:T(8,128)(2,1)}, bf16[512,1536]{1,0:T(8,128)(2,1)S(1)}, u32[]{:S(2)}, u32[]{:S(2)}) collective-permute-start(bf16[512,1536]{1,0:T(8,128)(2,1)} %get-tuple-element.36), channel_id=1, source_target_pairs={{4,0},{8,4},{12,8},{20,16},{24,20},{28,24},{16,28},{0,12},{5,1},{9... | collective-permute-start | bytes 4718600 | tf_op jit(solution)/shard_map/ppermute | solution.py:508
  20.9 0.7 copy-start.1
  21.6 0.7 copy-start.7
  43.2 4.6 %copy-start.9 = (f32[1,512]{1,0:T(1,128)S(1)}, f32[1,512]{1,0:T(1,128)}, u32[]{:S(2)}) copy-start(f32[1,512]{1,0:T(1,128)} %get-tuple-element.30.refs_3_) | copy-start | bytes 6148
  45.7 26.9 %collective-permute-start.3 = (bf16[512,512]{1,0:T(8,128)(2,1)S(1)}, bf16[512,512]{1,0:T(8,128)(2,1)S(1)}, u32[]{:S(2)}, u32[]{:S(2)}) collective-permute-start(bf16[512,512]{1,0:T(8,128)(2,1)S(1)} %get-tuple-element.31), channel_id=1, source_target_pairs={{4,20},{8,24},{12,28},{20,4},{24,8},{28,12},{5,21},{9,25},{13,29},... | collective-permute-start | bytes 1572872 | tf_op jit(solution)/shard_map/ppermute | solution.py:508
  57.5 27.1 %collective-permute-start.6 = (bf16[512,512]{1,0:T(8,128)(2,1)}, bf16[512,512]{1,0:T(8,128)(2,1)S(1)}, u32[]{:S(2)}, u32[]{:S(2)}) collective-permute-start(bf16[512,512]{1,0:T(8,128)(2,1)} %get-tuple-element.37), channel_id=1, source_target_pairs={{0,28},{4,0},{8,4},{12,8},{16,12},{20,16},{24,20},{28,24},{1,29},{... | collective-permute-start | bytes 1572872 | tf_op jit(solution)/shard_map/ppermute | solution.py:508
  57.5 27.3 %collective-permute-start.8 = (bf16[512,512]{1,0:T(8,128)(2,1)}, bf16[512,512]{1,0:T(8,128)(2,1)}, u32[]{:S(2)}, u32[]{:S(2)}) collective-permute-start(bf16[512,512]{1,0:T(8,128)(2,1)} %get-tuple-element.38), channel_id=1, source_target_pairs={{4,0},{8,4},{12,8},{20,16},{24,20},{28,24},{5,1},{9,5},{13,9},{21,... | collective-permute-start | bytes 1572872 | tf_op jit(solution)/shard_map/ppermute | solution.py:508
  72.6 3.5 %copy-start.3 = (f32[3,512]{1,0:T(4,128)S(1)}, f32[3,512]{1,0:T(4,128)}, u32[]{:S(2)}) copy-start(f32[3,512]{1,0:T(4,128)} %psum.21.t_ref.refs_4_.refs_5_) | copy-start | bytes 18436
  72.6 3.5 %copy-start.4 = (f32[1,1536]{1,0:T(1,128)S(1)}, f32[1,1536]{1,0:T(1,128)}, u32[]{:S(2)}) copy-start(f32[1,1536]{1,0:T(1,128)} %gq_ref.5) | copy-start | bytes 18436
  72.6 3.5 %copy-start.5 = (f32[1,1536]{1,0:T(1,128)S(1)}, f32[1,1536]{1,0:T(1,128)}, u32[]{:S(2)}) copy-start(f32[1,1536]{1,0:T(1,128)} %gk_ref.5) | copy-start | bytes 18436
  75.4 19.0 %collective-permute-start.7 = (bf16[512,512]{1,0:T(8,128)(2,1)}, bf16[512,512]{1,0:T(8,128)(2,1)S(1)}, u32[]{:S(2)}, u32[]{:S(2)}) collective-permute-start(bf16[512,512]{1,0:T(8,128)(2,1)} %get-tuple-element.34.rest_0_), channel_id=1, source_target_pairs={{0,28},{4,0},{8,4},{12,8},{16,12},{20,16},{24,20},{28,24},{1,29},{... | collective-permute-start | bytes 1572872 | tf_op jit(solution)/shard_map/ppermute | solution.py:508
  75.5 51.9 %collective-permute-start.4 = (bf16[512,512]{1,0:T(8,128)(2,1)}, bf16[512,512]{1,0:T(8,128)(2,1)S(1)}, u32[]{:S(2)}, u32[]{:S(2)}) collective-permute-start(bf16[512,512]{1,0:T(8,128)(2,1)} %get-tuple-element.35), channel_id=1, source_target_pairs={{20,0},{24,4},{28,8},{4,16},{8,20},{12,24},{16,12},{0,28},{21,1},{... | collective-permute-start | bytes 1572872 | tf_op jit(solution)/shard_map/ppermute | solution.py:508
  76.2 8.6 %copy-start.2 = (f32[1,3712]{1,0:T(1,128)S(1)}, f32[1,3712]{1,0:T(1,128)}, u32[]{:S(2)}) copy-start(f32[1,3712]{1,0:T(1,128)} %copy-done) | copy-start | bytes 44548

commit v12 on v1

v12 whole, which is shorter than its diff:
```python
import functools
import math

import jax
import jax.numpy as jnp
from jax import lax
from jax.experimental import pallas as pl
from jax.experimental.pallas import tpu as pltpu
from jax.sharding import PartitionSpec as P

HDIM = 128
EPSILON = 1e-05
SCALE = 1.0 / math.sqrt(HDIM)
LOG2E = math.log2(math.e)
VMEM = 32 * 1024 * 1024
MOST = 60 * 1024 * 1024

F32 = jnp.float32
BF16 = jnp.bfloat16


def dot(a, b, contract):
    return lax.dot_general(a, b, ((contract[0], contract[1]), ((), ())), preferred_element_type=F32)


def nt(a, b):
    return dot(a, b, ((1,), (1,)))


def nn(a, b):
    return dot(a, b, ((1,), (0,)))


def block_of(tokens):
    return 256 if tokens % 256 == 0 else tokens


def masked(block, kept):
    return jnp.where(kept, block, -1e30)


def kept_keys(size):
    keys = lax.broadcasted_iota(jnp.int32, (size, size), 0)
    return keys <= lax.broadcasted_iota(jnp.int32, (size, size), 1)


def scores_of(keys, queries, j, size, kept):
    mine = queries[j * size : (j + 1) * size]
    diagonal = masked(nt(keys[j * size : (j + 1) * size], mine), kept)
    if j == 0:
        return [diagonal]
    return [nt(keys[: j * size], mine), diagonal]


def exponents(parts):
    top = functools.reduce(jnp.maximum, [jnp.max(p, axis=0, keepdims=True) for p in parts])
    exps = [jnp.exp2((p - top) * (SCALE * LOG2E)) for p in parts]
    total = sum(jnp.sum(e, axis=0, keepdims=True) for e in exps)
    return exps, total


def stacked(parts):
    return parts[0] if len(parts) == 1 else jnp.concatenate(parts, axis=0)


def normed_head(x, factor, gain_q, gain_k):
    wide = x.astype(F32)
    normed = wide * factor
    return wide, (normed * gain_q).astype(BF16), (normed * gain_k).astype(BF16), normed.astype(BF16)


def column_of(row):
    return jnp.broadcast_to(row, (HDIM, row.shape[1])).T[:, 0:1]


def inverse_rms(total, width_all):
    return lax.rsqrt(total / width_all + EPSILON)


def lanes_of(start, size):
    return (slice(None), slice(start, start + size))


def compiler(limit):
    return pltpu.CompilerParams(vmem_limit_bytes=limit)


IN_VMEM = pl.BlockSpec(memory_space=pltpu.VMEM)
ANYWHERE = pl.BlockSpec(memory_space=pl.ANY)
IN_HBM = pl.BlockSpec(memory_space=pltpu.HBM)


def in_hbm(x):
    return pltpu.with_memory_space_constraint(x, pltpu.HBM)


def forward_kernel(heads, width_all, x_ref, t_ref, gq_ref, gk_ref, *rest):
    o_ref = rest[-1]
    tokens = x_ref.shape[0]
    size = block_of(tokens)
    kept = kept_keys(size)
    factor = column_of(inverse_rms(t_ref[0:1, :], width_all))
    for h in range(heads):
        lanes = slice(h * HDIM, (h + 1) * HDIM)
        wide, q, k, v = normed_head(x_ref[:, lanes], factor, gq_ref[:, lanes], gk_ref[:, lanes])
        vt = v.T
        for j in range(tokens // size):
            exps, total = exponents(scores_of(k, q, j, size, kept))
            mixed = nn(vt[:, : (j + 1) * size], stacked(exps).astype(BF16)) * (1.0 / total)
            rows = slice(j * size, (j + 1) * size)
            o_ref[rows, lanes] = (wide[rows] + mixed.T).astype(BF16)


def forward(width_all, x, totals, gain_q, gain_k, heads, after=()):
    tokens, width = x.shape
    lanes = heads * HDIM
    block = pl.BlockSpec((tokens, lanes), lambda i: (0, i))
    gain = pl.BlockSpec((1, lanes), lambda i: (0, i))
    return pl.pallas_call(
        functools.partial(forward_kernel, heads, width_all),
        out_shape=jax.ShapeDtypeStruct(x.shape, BF16),
        grid=(width // lanes,),
        in_specs=[block, pl.BlockSpec(totals.shape, lambda i: (0, 0)), gain, gain] + [IN_HBM] * len(after),
        out_specs=block,
        compiler_params=compiler(VMEM),
        name="forward",
    )(in_hbm(x), totals, gain_q, gain_k, *map(in_hbm, after))


def backward_head(x, g, factor, gain_q, gain_k):
    tokens = x.shape[0]
    size = block_of(tokens)
    kept = kept_keys(size)
    wide, q, k, v = normed_head(x, factor, gain_q, gain_k)
    kt = k.T
    blocks = tokens // size
    d_q = []
    d_k = [None] * blocks
    d_v = [None] * blocks
    for j in range(blocks):
        rows = slice(j * size, (j + 1) * size)
        exps, total = exponents(scores_of(k, q, j, size, kept))
        inverse = 1.0 / total
        weights = [e * inverse for e in exps]
        grads = [nt(v[: j * size], g[rows])] if j else []
        grads.append(nt(v[rows], g[rows]))
        delta = sum(jnp.sum(w * d, axis=0, keepdims=True) for w, d in zip(weights, grads))
        scores = stacked([(w * ((d - delta) * SCALE)).astype(BF16) for w, d in zip(weights, grads)])
        rounded = stacked([w.astype(BF16) for w in weights])
        d_q.append(nn(kt[:, : (j + 1) * size], scores).T)
        part_k = nn(scores, q[rows])
        part_v = nn(rounded, g[rows])
        for i in range(j + 1):
            mine = slice(i * size, (i + 1) * size)
            d_k[i] = part_k[mine] if d_k[i] is None else d_k[i] + part_k[mine]
            d_v[i] = part_v[mine] if d_v[i] is None else d_v[i] + part_v[mine]
    d_normed = stacked(d_q) * gain_q + stacked(d_k) * gain_k + stacked(d_v)
    return wide, d_normed


def backward_kernel(first, heads, width_all, evicted_ref, own_ref, far_ref, g_ref, t_ref, held_ref, gq_ref, gk_ref, past_ref, *refs):
    a_out, x_out, inner_ref, xs, gs, outs, x_sem, g_sem, a_sem, out_sem = refs[-10:]
    evicted = evicted_ref[0] == 1
    copies = []
    for h in range(heads):
        to = lanes_of(h * HDIM, HDIM)
        there = lanes_of(first + h * HDIM, HDIM)
        far = pltpu.make_async_copy(far_ref.at[to], xs.at[to], x_sem.at[h])
        near = pltpu.make_async_copy(own_ref.at[(0, 0) + there], xs.at[to], x_sem.at[h])
        g = pltpu.make_async_copy(g_ref.at[(0,) + there], gs.at[to], g_sem.at[h])
        pl.when(evicted)(far.start)
        pl.when(jnp.logical_not(evicted))(near.start)
        g.start()
        copies.append((far, near, g))
    factor = column_of(inverse_rms(total_of(evicted_ref, t_ref, held_ref), width_all))
    part = None
    sent = []
    for h in range(heads):
        far, near, copy = copies[h]
        pl.when(evicted)(far.wait)
        pl.when(jnp.logical_not(evicted))(near.wait)
        copy.wait()
        mine = lanes_of(h * HDIM, HDIM)
        there = lanes_of(first + h * HDIM, HDIM)
        g = gs[mine]
        wide, d_normed = backward_head(xs[mine], g, factor, gq_ref[there], gk_ref[there])
        outs[mine] = g.astype(F32) + factor * d_normed
        sent.append(pltpu.make_async_copy(outs.at[mine], a_out.at[there], a_sem.at[h]))
        sent.append(pltpu.make_async_copy(xs.at[mine], x_out.at[there], out_sem.at[h]))
        for copy in sent[-2:]:
            copy.start()
        product = d_normed * wide
        part = product if part is None else part + product
    inner_ref[...] = jnp.sum(part.T, axis=0, keepdims=True) + past_ref[...]
    for copy in sent:
        copy.wait()


def total_of(evicted_ref, t_ref, held_ref):
    return jnp.where(evicted_ref[0] == 1, held_ref[2:3, :], t_ref[1:2, :])


def backward(width_all, evicted, stash, far, g, totals, held, gain_q, gain_k, past, heads, first, sofar=(), after=()):
    tokens, width = totals.shape[1], gain_q.shape[1]
    small = (tokens, heads * HDIM)
    dma = pltpu.SemaphoreType.DMA((heads,))
    return pl.pallas_call(
        functools.partial(backward_kernel, first, heads, width_all),
        out_shape=(
            pltpu.HBM((tokens, width), F32),
            pltpu.HBM((tokens, width), BF16),
            jax.ShapeDtypeStruct((1, tokens), F32),
        ),
        in_specs=[pl.BlockSpec(memory_space=pltpu.SMEM)] + [ANYWHERE] * 3 + [IN_VMEM] * 5
        + [IN_HBM] * len(sofar) + [ANYWHERE] * len(after),
        out_specs=(IN_HBM, IN_HBM, IN_VMEM),
        input_output_aliases={9: 0, 10: 1} if sofar else {},
        scratch_shapes=[pltpu.VMEM(small, BF16)] * 2 + [pltpu.VMEM(small, F32)] + [dma] * 4,
        compiler_params=compiler(VMEM),
        name="backward",
    )(evicted, in_hbm(stash), far, in_hbm(g), totals, held, gain_q, gain_k, past, *sofar, *after)


def row_of(total, inner, width_all):
    return inverse_rms(total, width_all) ** 3 * inner / width_all


def finish_kernel(width_all, evicted_ref, a_ref, x_ref, t_ref, held_ref, inner_ref, o_ref):
    row = row_of(total_of(evicted_ref, t_ref, held_ref), inner_ref[...], width_all)
    o_ref[...] = (a_ref[...] - x_ref[...].astype(F32) * column_of(row)).astype(BF16)


def finish(width_all, evicted, a, x, totals, held, inner, lanes):
    tokens, width = a.shape
    block = pl.BlockSpec((tokens, lanes), lambda i: (0, i))
    return pl.pallas_call(
        functools.partial(finish_kernel, width_all),
        out_shape=jax.ShapeDtypeStruct(a.shape, BF16),
        grid=(width // lanes,),
        in_specs=[pl.BlockSpec(memory_space=pltpu.SMEM), block, block] + [IN_VMEM] * 3,
        out_specs=block,
        compiler_params=compiler(VMEM),
        name="finish",
    )(evicted, in_hbm(a), in_hbm(x), totals, held, inner)


def squares_kernel(current_ref, stash_ref, *rest):
    rows_ref, sums = rest[-2:]
    step = pl.program_id(0)

    def total(x):
        wide = x.astype(F32)
        square = wide * wide
        return sum(square[:, i : i + HDIM] for i in range(0, square.shape[1], HDIM))

    for i, x in enumerate((current_ref[...], stash_ref[0], stash_ref[1])):
        part = total(x)

        @pl.when(step == 0)
        def _():
            sums[i] = part

        @pl.when(step > 0)
        def _():
            sums[i] += part

    @pl.when(step == pl.num_programs(0) - 1)
    def _():
        for i in range(3):
            rows_ref[i : i + 1, :] = jnp.sum(sums[i].T, axis=0, keepdims=True)


def squares(current, stash, lanes, after=()):
    tokens, width = current.shape
    return pl.pallas_call(
        squares_kernel,
        out_shape=jax.ShapeDtypeStruct((3, tokens), F32),
        grid=(width // lanes,),
        in_specs=[
            pl.BlockSpec((tokens, lanes), lambda i: (0, i)),
            pl.BlockSpec((None, 2, tokens, lanes), lambda i: (0, 0, 0, i)),
        ] + [ANYWHERE] * len(after),
        out_specs=pl.BlockSpec((3, tokens), lambda i: (0, 0)),
        scratch_shapes=[pltpu.VMEM((3, tokens, HDIM), F32)],
        compiler_params=compiler(MOST),
        name="squares",
    )(in_hbm(current), in_hbm(stash), *after)


def piece_kernel(starts, sizes, stash_ref, *rest):
    outs, mark, sems = rest[-2 - len(sizes) : -2], rest[-2], rest[-1]
    mark[...] = jnp.zeros_like(mark)
    copies = [
        pltpu.make_async_copy(stash_ref.at[(0, 1) + lanes_of(start, size)], out, sems.at[i])
        for i, (start, size, out) in enumerate(zip(starts, sizes, outs))
    ]
    for copy in copies:
        copy.start()
    for copy in copies:
        copy.wait()


def pieces_of(stash, starts, sizes, after=()):
    tokens = stash.shape[2]
    return pl.pallas_call(
        functools.partial(piece_kernel, starts, sizes),
        out_shape=[jax.ShapeDtypeStruct((tokens, size), BF16) for size in sizes] + [jax.ShapeDtypeStruct((8, HDIM), F32)],
        in_specs=[IN_HBM] + [ANYWHERE] * len(after),
        out_specs=[IN_VMEM] * (len(sizes) + 1),
        scratch_shapes=[pltpu.SemaphoreType.DMA((len(sizes),))],
        compiler_params=compiler(VMEM),
        name="pieces",
    )(in_hbm(stash), *after)


def send(x, pairs):
    return lax.ppermute(x, "section", pairs)


def local(width_all, layer_input, grad_input, stashed, eviction, query_gain, key_gain):
    n = lax.axis_size("section")
    partner = [(s, (s + n // 2) % n) for s in range(n)]
    prior = [(s, (s - 1) % n) for s in range(n)]
    current = layer_input[0]
    tokens, width = current.shape
    count = width // HDIM
    heads = (max(1, count // 3), count - max(1, count // 3) - max(1, count // 4), max(1, count // 4))
    sizes = [h * HDIM for h in heads]
    starts = [sum(sizes[:i]) for i in range(3)]
    third = count // 3 * HDIM

    *away, mark = pieces_of(stashed, starts[:2], sizes[:2])
    fetched = [send(x, partner) for x in away]
    totals = lax.psum(squares(current, stashed, third, (mark,)), "tensor")
    held = send(totals, partner)
    output = forward(width_all, current, totals, query_gain, key_gain, third // HDIM)
    fetched.append(send(pieces_of(stashed, starts[2:], sizes[2:], (fetched[0], in_hbm(output)))[0], partner))

    sofar, inner, after = (), jnp.zeros((1, tokens), F32), (in_hbm(output),)
    for h, start, far in zip(heads, starts, fetched):
        *sofar, inner = backward(
            width_all, eviction, stashed, far, grad_input, totals, held, query_gain, key_gain, inner, h, start,
            tuple(sofar), after,
        )
        after = ()
    inner = lax.psum(inner, "tensor")
    result = finish(width_all, eviction, *sofar, totals, held, inner, third)
    return (output[None], send(result, prior)[None])


def solution(mesh):
    placed = (
        P("section", None, "tensor"),
        P("section", None, "tensor"),
        P("section", None, None, "tensor"),
        P("section"),
        P("section", "tensor"),
        P("section", "tensor"),
    )

    def whole(layer_input, *others):
        return jax.shard_map(
            functools.partial(local, layer_input.shape[-1]),
            mesh=mesh,
            in_specs=placed,
            out_specs=(P("section", None, "tensor"), P("section", None, "tensor")),
            check_vma=False,
        )(layer_input, *others)

    return whole
```

time: 145 us -> 144 us (level)
  Pallas kernels: 22.4 us -> 40.2 us
  local copies, waits for them, and re-layouts: 9.37 us -> 1.16 us
  other arithmetic: 6.27 us -> 0 us
  starting transfers between devices: 15.4 us -> 12.8 us
  waiting for transfers between devices: 78 us -> 75.9 us
    pallas_call x5 -> x8, Pallas kernels: 22.4 us -> 40.2 us  [the longest x3 20.7 us: backward(): pl.pallas_call(functools.partial(backward_kernel, first, heads, width_all...]
    unnamed x20 -> x7, local copies, waits for them, and re-layouts: 4.79 us -> 1.16 us
    squeeze x1 -> x0, local copies, waits for them, and re-layouts: 3.23 us -> none  [local(): stashed[0, 0]]
    ppermute x9 -> x5, starting transfers between devices: 15.4 us -> 12.8 us  [send(): return lax.ppermute(x, 'section', pairs)]
    convert_element_type x1 -> x0, other arithmetic: 2.28 us -> none  [local(): (a - x.astype(F32) * row).astype(BF16)]
    ppermute x9 -> x5, waiting for transfers between devices: 78 us -> 75.9 us  [send(): return lax.ppermute(x, 'section', pairs)]
    select_n x1 -> x0, other arithmetic: 1.61 us -> none  [local(): x = jnp.where(evicted, f, stashed[0, 0][:, p])]
  transfers between devices with their start and end apart: 9 -> 5, of which waited for: 5 -> 3; matrix products, arithmetic and copies ran while one was open for 1% -> 0% of each run, Pallas kernels for 6% -> 21%
where the time goes in v12:
time: 144 us
  waiting for transfers between devices  75.9 us (53%)
  Pallas kernels  40.2 us (28%)
  starting transfers between devices  12.8 us (9%)
  blocking collectives  12.3 us (9%)
    ppermute x5, waiting for transfers between devices, send(): return lax.ppermute(x, 'section', pairs)  75.9 us
    pallas_call x3, Pallas kernels, backward(): pl.pallas_call(functools.partial(backward_kernel, first, heads, width_all...  20.7 us
    ppermute x5, starting transfers between devices, send(): return lax.ppermute(x, 'section', pairs)  12.8 us
    pallas_call x1, Pallas kernels, forward(): pl.pallas_call(functools.partial(forward_kernel, heads, width_all), out_s...  8.39 us
    psum x1, blocking collectives, local(): totals = lax.psum(squares(current, stashed, third, (mark,)), 'tensor')  6.51 us
    psum x1, blocking collectives, local(): inner = lax.psum(inner, 'tensor')  5.79 us
    pallas_call x1, Pallas kernels, squares(): pl.pallas_call(squares_kernel, out_shape=jax.ShapeDtypeStruct((3, tokens)...  4.76 us
    pallas_call x1, Pallas kernels, finish(): pl.pallas_call(functools.partial(finish_kernel, width_all), out_shape=jax...  3.45 us
  transfers between devices with their start and end apart: 5, of which 3 were waited for; matrix products, arithmetic and copies ran while one was open for 0% of the time, Pallas kernels for 21%

profile of v12, /device:TPU:0, one launch (start us, length us, event | category | flops | bytes accessed | tf_op | source)
XLA Modules:
  0.0 143.7 jit_solution(4317813072508224391)
XLA Ops:
  0.6 1.3 pieces.2
  1.9 0.0 copy-start.2
  1.9 4.1 %collective-permute-start = (bf16[512,512]{1,0:T(8,128)(2,1)S(1)}, bf16[512,512]{1,0:T(8,128)(2,1)S(1)}, u32[]{:S(2)}, u32[]{:S(2)}) collective-permute-start(bf16[512,512]{1,0:T(8,128)(2,1)S(1)} %get-tuple-element.16), channel_id=1, source_target_pairs={{0,16},{4,20},{8,24},{12,28},{16,0},{20,4},{24,8},{28,12},{1,17},{... | collective-permute-start | bytes 1572872 | tf_op jit(solution)/shard_map/ppermute | solution.py:317
  6.0 0.1 collective-permute-start.3
  6.1 0.0 copy-done.2
  6.1 0.0 copy-start
  6.1 0.0 copy-start.1
  6.1 4.8 %squares.1 = f32[3,512]{1,0:T(4,128)} custom-call(bf16[512,1536]{1,0:T(8,128)(2,1)} %bitcast.4, bf16[1,2,512,1536]{3,2,1,0:T(8,128)(2,1)} %own_ref.5, f32[8,128]{1,0:T(8,128)} %copy-done.2), custom_call_target="tpu_custom_call" | custom-call | tf_op jit(solution)/shard_map/squares/pallas_call | solution.py:275
  10.9 6.5 %psum.14.t_ref = f32[3,512]{1,0:T(4,128)S(1)} all-reduce(f32[3,512]{1,0:T(4,128)} %squares.1), channel_id=1, replica_groups=mesh['section'=8,'tensor'=4] {'tensor'}, use_global_device_ids=true, to_apply=%region_0.0 | all-reduce | flops 1536 | bytes 12288 | tf_op jit(solution)/shard_map/psum | solution.py:334
  17.4 0.0 copy-done
  17.4 0.0 copy-done.1
  17.4 8.4 %forward.1.rest_1_.refs_0_ = bf16[512,1536]{1,0:T(8,128)(2,1)} custom-call(bf16[512,1536]{1,0:T(8,128)(2,1)} %bitcast.5, f32[3,512]{1,0:T(4,128)S(1)} %psum.14.t_ref, f32[1,1536]{1,0:T(1,128)S(1)} %copy-done, f32[1,1536]{1,0:T(1,128)S(1)} %copy-done.1), custom_call_target="tpu_custom_call" | custom-call | tf_op jit(solution)/shard_map/forward/pallas_call | solution.py:119
  25.8 18.2 %collective-permute-done.rest_0_.far_ref = bf16[512,512]{1,0:T(8,128)(2,1)S(1)} collective-permute-done((bf16[512,512]{1,0:T(8,128)(2,1)S(1)}, bf16[512,512]{1,0:T(8,128)(2,1)S(1)}, u32[]{:S(2)}, u32[]{:S(2)}) %collective-permute-start) | collective-permute-done | bytes 524320 | tf_op jit(solution)/shard_map/ppermute | solution.py:317
  44.1 1.6 %pieces.3 = (bf16[512,384]{1,0:T(8,128)(2,1)S(1)}, f32[8,128]{1,0:T(8,128)}) custom-call(bf16[1,2,512,1536]{3,2,1,0:T(8,128)(2,1)} %own_ref.5, bf16[512,512]{1,0:T(8,128)(2,1)S(1)} %collective-permute-done.rest_0_.far_ref, bf16[512,1536]{1,0:T(8,128)(2,1)} %forward.1.rest_1_.refs_0_), custom_call_target="tpu_custom_call" | custom-call | tf_op jit(solution)/shard_map/pieces/pallas_call | solution.py:305
  45.7 0.1 collective-permute-start.1
  45.7 2.9 %collective-permute-start.2 = (f32[3,512]{1,0:T(4,128)S(1)}, f32[3,512]{1,0:T(4,128)S(1)}, u32[]{:S(2)}, u32[]{:S(2)}) collective-permute-start(f32[3,512]{1,0:T(4,128)S(1)} %psum.14.t_ref), channel_id=1, source_target_pairs={{0,16},{4,20},{8,24},{12,28},{16,0},{20,4},{24,8},{28,12},{1,17},{... | collective-permute-start | bytes 18440 | tf_op jit(solution)/shard_map/ppermute | solution.py:317
  49.3 25.2 %collective-permute-done.2.held_ref = f32[3,512]{1,0:T(4,128)S(1)} collective-permute-done((f32[3,512]{1,0:T(4,128)S(1)}, f32[3,512]{1,0:T(4,128)S(1)}, u32[]{:S(2)}, u32[]{:S(2)}) %collective-permute-start.2) | collective-permute-done | bytes 6176 | tf_op jit(solution)/shard_map/ppermute | solution.py:317
  74.5 6.9 %backward.3 = (f32[512,1536]{1,0:T(8,128)}, bf16[512,1536]{1,0:T(8,128)(2,1)}, f32[1,512]{1,0:T(1,128)S(1)}) custom-call(s32[1]{0:T(128)S(6)} %copy.17.evicted_ref, bf16[1,2,512,1536]{3,2,1,0:T(8,128)(2,1)} %own_ref.5, bf16[512,512]{1,0:T(8,128)(2,1)S(1)} %collective-permute-done.rest_0_.far_ref, bf16[1,512,1536]{2,1,0:T(8,128)(2,1)} %g_ref.5, ...), custom_call_target="tpu_custom_call" | custom-call | tf_op jit(solution)/shard_map/backward/pallas_call | solution.py:207
  81.4 0.0 collective-permute-done.3.far_ref
  81.4 8.2 %backward.4 = (f32[512,1536]{1,0:T(8,128)}, bf16[512,1536]{1,0:T(8,128)(2,1)}, f32[1,512]{1,0:T(1,128)S(1)}) custom-call(s32[1]{0:T(128)S(6)} %copy.17.evicted_ref, bf16[1,2,512,1536]{3,2,1,0:T(8,128)(2,1)} %own_ref.5, bf16[512,640]{1,0:T(8,128)(2,1)S(1)} %collective-permute-done.3.far_ref, ...), custom_call_target="tpu_custom_call", output_to_operand_aliasing={{0}: (9, {}), {1}: (10, {})} | custom-call | tf_op jit(solution)/shard_map/backward/pallas_call | solution.py:207
  89.6 0.0 collective-permute-done.1.far_ref
  89.6 5.6 %backward.5 = (f32[512,1536]{1,0:T(8,128)}, bf16[512,1536]{1,0:T(8,128)(2,1)}, f32[1,512]{1,0:T(1,128)S(1)}) custom-call(s32[1]{0:T(128)S(6)} %copy.17.evicted_ref, bf16[1,2,512,1536]{3,2,1,0:T(8,128)(2,1)} %own_ref.5, bf16[512,384]{1,0:T(8,128)(2,1)S(1)} %collective-permute-done.1.far_ref, ...), custom_call_target="tpu_custom_call", output_to_operand_aliasing={{0}: (9, {}), {1}: (10, {})} | custom-call | tf_op jit(solution)/shard_map/backward/pallas_call | solution.py:207
  95.3 5.8 %psum.15.inner_ref = f32[1,512]{1,0:T(1,128)S(1)} all-reduce(f32[1,512]{1,0:T(1,128)S(1)} %get-tuple-element.27), channel_id=1, replica_groups=mesh['section'=8,'tensor'=4] {'tensor'}, use_global_device_ids=true, to_apply=%region_1.0 | all-reduce | flops 512 | bytes 4096 | tf_op jit(solution)/shard_map/psum | solution.py:346
  101.0 3.4 %finish.1 = bf16[512,1536]{1,0:T(8,128)(2,1)S(1)} custom-call(s32[1]{0:T(128)S(6)} %copy.17.evicted_ref, f32[512,1536]{1,0:T(8,128)} %get-tuple-element.25.a_ref, bf16[512,1536]{1,0:T(8,128)(2,1)} %get-tuple-element.26.x_ref, f32[3,512]{1,0:T(4,128)S(1)} %psum.14.t_ref, f32[3,512]{1,0:T(4,128)S(1)} %collective-permute-done.2.held_ref, ...), custom_call_target="tpu_custom_call" | custom-call | tf_op jit(solution)/shard_map/finish/pallas_call | solution.py:236
  104.5 5.6 %collective-permute-start.4 = (bf16[512,1536]{1,0:T(8,128)(2,1)S(1)}, bf16[512,1536]{1,0:T(8,128)(2,1)S(1)}, u32[]{:S(2)}, u32[]{:S(2)}) collective-permute-start(bf16[512,1536]{1,0:T(8,128)(2,1)S(1)} %finish.1), channel_id=1, source_target_pairs={{0,28},{4,0},{8,4},{12,8},{16,12},{20,16},{24,20},{28,24},{1,29},{... | collective-permute-start | bytes 4718600 | tf_op jit(solution)/shard_map/ppermute | solution.py:317
  110.1 32.5 %collective-permute-done.4 = bf16[512,1536]{1,0:T(8,128)(2,1)S(1)} collective-permute-done((bf16[512,1536]{1,0:T(8,128)(2,1)S(1)}, bf16[512,1536]{1,0:T(8,128)(2,1)S(1)}, u32[]{:S(2)}, u32[]{:S(2)}) %collective-permute-start.4) | collective-permute-done | bytes 1572896 | tf_op jit(solution)/shard_map/ppermute | solution.py:317
  142.6 1.1 copy.18
  (1 shorter events, 0.0 us)
Async XLA Ops:
  1.9 4.2 %copy-start.2 = (f32[8,128]{1,0:T(8,128)}, f32[8,128]{1,0:T(8,128)S(1)}, u32[]{:S(2)}) copy-start(f32[8,128]{1,0:T(8,128)S(1)} %get-tuple-element.15.rest_0_) | copy-start | bytes 12292
  1.9 42.1 %collective-permute-start = (bf16[512,512]{1,0:T(8,128)(2,1)S(1)}, bf16[512,512]{1,0:T(8,128)(2,1)S(1)}, u32[]{:S(2)}, u32[]{:S(2)}) collective-permute-start(bf16[512,512]{1,0:T(8,128)(2,1)S(1)} %get-tuple-element.16), channel_id=1, source_target_pairs={{0,16},{4,20},{8,24},{12,28},{16,0},{20,4},{24,8},{28,12},{1,17},{... | collective-permute-start | bytes 1572872 | tf_op jit(solution)/shard_map/ppermute | solution.py:317
  6.0 75.4 %collective-permute-start.3 = (bf16[512,640]{1,0:T(8,128)(2,1)S(1)}, bf16[512,640]{1,0:T(8,128)(2,1)S(1)}, u32[]{:S(2)}, u32[]{:S(2)}) collective-permute-start(bf16[512,640]{1,0:T(8,128)(2,1)S(1)} %get-tuple-element.18), channel_id=1, source_target_pairs={{0,16},{4,20},{8,24},{12,28},{16,0},{20,4},{24,8},{28,12},{1,17},{... | collective-permute-start | bytes 1966088 | tf_op jit(solution)/shard_map/ppermute | solution.py:317
  6.1 11.3 %copy-start = (f32[1,1536]{1,0:T(1,128)S(1)}, f32[1,1536]{1,0:T(1,128)}, u32[]{:S(2)}) copy-start(f32[1,1536]{1,0:T(1,128)} %gq_ref.7) | copy-start | bytes 18436
  6.1 11.3 %copy-start.1 = (f32[1,1536]{1,0:T(1,128)S(1)}, f32[1,1536]{1,0:T(1,128)}, u32[]{:S(2)}) copy-start(f32[1,1536]{1,0:T(1,128)} %gk_ref.7) | copy-start | bytes 18436
  45.7 44.0 %collective-permute-start.1 = (bf16[512,384]{1,0:T(8,128)(2,1)S(1)}, bf16[512,384]{1,0:T(8,128)(2,1)S(1)}, u32[]{:S(2)}, u32[]{:S(2)}) collective-permute-start(bf16[512,384]{1,0:T(8,128)(2,1)S(1)} %get-tuple-element.17), channel_id=1, source_target_pairs={{0,16},{4,20},{8,24},{12,28},{16,0},{20,4},{24,8},{28,12},{1,17},{... | collective-permute-start | bytes 1179656 | tf_op jit(solution)/shard_map/ppermute | solution.py:317
  45.7 28.7 %collective-permute-start.2 = (f32[3,512]{1,0:T(4,128)S(1)}, f32[3,512]{1,0:T(4,128)S(1)}, u32[]{:S(2)}, u32[]{:S(2)}) collective-permute-start(f32[3,512]{1,0:T(4,128)S(1)} %psum.14.t_ref), channel_id=1, source_target_pairs={{0,16},{4,20},{8,24},{12,28},{16,0},{20,4},{24,8},{28,12},{1,17},{... | collective-permute-start | bytes 18440 | tf_op jit(solution)/shard_map/ppermute | solution.py:317
  104.5 38.1 %collective-permute-start.4 = (bf16[512,1536]{1,0:T(8,128)(2,1)S(1)}, bf16[512,1536]{1,0:T(8,128)(2,1)S(1)}, u32[]{:S(2)}, u32[]{:S(2)}) collective-permute-start(bf16[512,1536]{1,0:T(8,128)(2,1)S(1)} %finish.1), channel_id=1, source_target_pairs={{0,28},{4,0},{8,4},{12,8},{16,12},{20,16},{24,20},{28,24},{1,29},{... | collective-permute-start | bytes 4718600 | tf_op jit(solution)/shard_map/ppermute | solution.py:317

commit v13 on v12

--- a/solution.py
+++ b/solution.py
@@ -334,7 +334,7 @@
     totals = lax.psum(squares(current, stashed, third, (mark,)), "tensor")
     held = send(totals, partner)
     output = forward(width_all, current, totals, query_gain, key_gain, third // HDIM)
-    fetched.append(send(pieces_of(stashed, starts[2:], sizes[2:], (fetched[0], in_hbm(output)))[0], partner))
+    fetched.append(send(pieces_of(stashed, starts[2:], sizes[2:], (fetched[0], held, in_hbm(output)))[0], partner))
 
     sofar, inner, after = (), jnp.zeros((1, tokens), F32), (in_hbm(output),)
     for h, start, far in zip(heads, starts, fetched):

time: 144 us -> 131 us (0.910)
  waiting for transfers between devices: 75.9 us -> 65.7 us
  starting transfers between devices: 12.8 us -> 10.4 us
    ppermute x5, waiting for transfers between devices: 75.9 us -> 65.7 us  [send(): return lax.ppermute(x, 'section', pairs)]
    ppermute x5, starting transfers between devices: 12.8 us -> 10.4 us  [send(): return lax.ppermute(x, 'section', pairs)]
  transfers between devices with their start and end apart: 5 -> 5, of which waited for: 3 -> 3; matrix products, arithmetic and copies ran while one was open for 0% -> 0% of each run, Pallas kernels for 21% -> 23%
where the time goes in v13:
time: 131 us
  waiting for transfers between devices  65.7 us (50%)
  Pallas kernels  40.2 us (31%)
  blocking collectives  12.2 us (9%)
  starting transfers between devices  10.4 us (8%)
  between operations  1.37 us (1%)
    ppermute x5, waiting for transfers between devices, send(): return lax.ppermute(x, 'section', pairs)  65.7 us
    pallas_call x3, Pallas kernels, backward(): pl.pallas_call(functools.partial(backward_kernel, first, heads, width_all...  20.7 us
    ppermute x5, starting transfers between devices, send(): return lax.ppermute(x, 'section', pairs)  10.4 us
    pallas_call x1, Pallas kernels, forward(): pl.pallas_call(functools.partial(forward_kernel, heads, width_all), out_s...  8.39 us
    psum x1, blocking collectives, local(): totals = lax.psum(squares(current, stashed, third, (mark,)), 'tensor')  6.51 us
    psum x1, blocking collectives, local(): inner = lax.psum(inner, 'tensor')  5.67 us
    pallas_call x1, Pallas kernels, squares(): pl.pallas_call(squares_kernel, out_shape=jax.ShapeDtypeStruct((3, tokens)...  4.76 us
    pallas_call x1, Pallas kernels, finish(): pl.pallas_call(functools.partial(finish_kernel, width_all), out_shape=jax...  3.45 us
  transfers between devices with their start and end apart: 5, of which 3 were waited for; matrix products, arithmetic and copies ran while one was open for 0% of the time, Pallas kernels for 23%

profile of v13, /device:TPU:0, one launch (start us, length us, event | category | flops | bytes accessed | tf_op | source)
XLA Modules:
  0.0 131.0 jit_solution(8642332093468598275)
XLA Ops:
  0.6 1.3 pieces.2
  1.9 0.0 copy-start.2
  1.9 4.1 %collective-permute-start = (bf16[512,512]{1,0:T(8,128)(2,1)S(1)}, bf16[512,512]{1,0:T(8,128)(2,1)S(1)}, u32[]{:S(2)}, u32[]{:S(2)}) collective-permute-start(bf16[512,512]{1,0:T(8,128)(2,1)S(1)} %get-tuple-element.16), channel_id=1, source_target_pairs={{0,16},{4,20},{8,24},{12,28},{16,0},{20,4},{24,8},{28,12},{1,17},{... | collective-permute-start | bytes 1572872 | tf_op jit(solution)/shard_map/ppermute | solution.py:317
  6.0 0.1 collective-permute-start.3
  6.1 0.0 copy-done.2
  6.1 0.0 copy-start
  6.1 0.0 copy-start.1
  6.1 4.8 %squares.1 = f32[3,512]{1,0:T(4,128)} custom-call(bf16[512,1536]{1,0:T(8,128)(2,1)} %bitcast.4, bf16[1,2,512,1536]{3,2,1,0:T(8,128)(2,1)} %own_ref.5, f32[8,128]{1,0:T(8,128)} %copy-done.2), custom_call_target="tpu_custom_call" | custom-call | tf_op jit(solution)/shard_map/squares/pallas_call | solution.py:275
  10.9 6.5 %psum.14.t_ref = f32[3,512]{1,0:T(4,128)S(1)} all-reduce(f32[3,512]{1,0:T(4,128)} %squares.1), channel_id=1, replica_groups=mesh['section'=8,'tensor'=4] {'tensor'}, use_global_device_ids=true, to_apply=%region_0.0 | all-reduce | flops 1536 | bytes 12288 | tf_op jit(solution)/shard_map/psum | solution.py:334
  17.4 2.9 %collective-permute-start.1 = (f32[3,512]{1,0:T(4,128)S(1)}, f32[3,512]{1,0:T(4,128)S(1)}, u32[]{:S(2)}, u32[]{:S(2)}) collective-permute-start(f32[3,512]{1,0:T(4,128)S(1)} %psum.14.t_ref), channel_id=1, source_target_pairs={{0,16},{4,20},{8,24},{12,28},{16,0},{20,4},{24,8},{28,12},{1,17},{... | collective-permute-start | bytes 18440 | tf_op jit(solution)/shard_map/ppermute | solution.py:317
  20.3 0.0 copy-done
  20.3 0.0 copy-done.1
  20.3 8.4 %forward.1.rest_2_.refs_0_ = bf16[512,1536]{1,0:T(8,128)(2,1)} custom-call(bf16[512,1536]{1,0:T(8,128)(2,1)} %bitcast.5, f32[3,512]{1,0:T(4,128)S(1)} %psum.14.t_ref, f32[1,1536]{1,0:T(1,128)S(1)} %copy-done, f32[1,1536]{1,0:T(1,128)S(1)} %copy-done.1), custom_call_target="tpu_custom_call" | custom-call | tf_op jit(solution)/shard_map/forward/pallas_call | solution.py:119
  28.7 28.9 %collective-permute-done.1.rest_1_.held_ref = f32[3,512]{1,0:T(4,128)S(1)} collective-permute-done((f32[3,512]{1,0:T(4,128)S(1)}, f32[3,512]{1,0:T(4,128)S(1)}, u32[]{:S(2)}, u32[]{:S(2)}) %collective-permute-start.1) | collective-permute-done | bytes 6176 | tf_op jit(solution)/shard_map/ppermute | solution.py:317
  57.6 0.0 collective-permute-done.rest_0_.far_ref
  57.6 1.6 %pieces.3 = (bf16[512,384]{1,0:T(8,128)(2,1)S(1)}, f32[8,128]{1,0:T(8,128)}) custom-call(bf16[1,2,512,1536]{3,2,1,0:T(8,128)(2,1)} %own_ref.5, bf16[512,512]{1,0:T(8,128)(2,1)S(1)} %collective-permute-done.rest_0_.far_ref, f32[3,512]{1,0:T(4,128)S(1)} %collective-permute-done.1.rest_1_.held_ref, bf16[512,1536]{1,0:T(8,128)(2,1)} %forward.1.rest_2_.refs_0_), custom_call_target="tpu_custom_call" | custom-call | tf_op jit(solution)/shard_map/pieces/pallas_call | solution.py:305
  59.2 0.1 collective-permute-start.2
  60.0 6.9 %backward.3 = (f32[512,1536]{1,0:T(8,128)}, bf16[512,1536]{1,0:T(8,128)(2,1)}, f32[1,512]{1,0:T(1,128)S(1)}) custom-call(s32[1]{0:T(128)S(6)} %copy.17.evicted_ref, bf16[1,2,512,1536]{3,2,1,0:T(8,128)(2,1)} %own_ref.5, bf16[512,512]{1,0:T(8,128)(2,1)S(1)} %collective-permute-done.rest_0_.far_ref, bf16[1,512,1536]{2,1,0:T(8,128)(2,1)} %g_ref.5, ...), custom_call_target="tpu_custom_call" | custom-call | tf_op jit(solution)/shard_map/backward/pallas_call | solution.py:207
  66.9 0.0 collective-permute-done.3.far_ref
  66.9 8.2 %backward.4 = (f32[512,1536]{1,0:T(8,128)}, bf16[512,1536]{1,0:T(8,128)(2,1)}, f32[1,512]{1,0:T(1,128)S(1)}) custom-call(s32[1]{0:T(128)S(6)} %copy.17.evicted_ref, bf16[1,2,512,1536]{3,2,1,0:T(8,128)(2,1)} %own_ref.5, bf16[512,640]{1,0:T(8,128)(2,1)S(1)} %collective-permute-done.3.far_ref, ...), custom_call_target="tpu_custom_call", output_to_operand_aliasing={{0}: (9, {}), {1}: (10, {})} | custom-call | tf_op jit(solution)/shard_map/backward/pallas_call | solution.py:207
  75.1 3.8 %collective-permute-done.2.far_ref = bf16[512,384]{1,0:T(8,128)(2,1)S(1)} collective-permute-done((bf16[512,384]{1,0:T(8,128)(2,1)S(1)}, bf16[512,384]{1,0:T(8,128)(2,1)S(1)}, u32[]{:S(2)}, u32[]{:S(2)}) %collective-permute-start.2) | collective-permute-done | bytes 393248 | tf_op jit(solution)/shard_map/ppermute | solution.py:317
  78.9 5.6 %backward.5 = (f32[512,1536]{1,0:T(8,128)}, bf16[512,1536]{1,0:T(8,128)(2,1)}, f32[1,512]{1,0:T(1,128)S(1)}) custom-call(s32[1]{0:T(128)S(6)} %copy.17.evicted_ref, bf16[1,2,512,1536]{3,2,1,0:T(8,128)(2,1)} %own_ref.5, bf16[512,384]{1,0:T(8,128)(2,1)S(1)} %collective-permute-done.2.far_ref, ...), custom_call_target="tpu_custom_call", output_to_operand_aliasing={{0}: (9, {}), {1}: (10, {})} | custom-call | tf_op jit(solution)/shard_map/backward/pallas_call | solution.py:207
  84.5 5.7 %psum.15.inner_ref = f32[1,512]{1,0:T(1,128)S(1)} all-reduce(f32[1,512]{1,0:T(1,128)S(1)} %get-tuple-element.27), channel_id=1, replica_groups=mesh['section'=8,'tensor'=4] {'tensor'}, use_global_device_ids=true, to_apply=%region_1.0 | all-reduce | flops 512 | bytes 4096 | tf_op jit(solution)/shard_map/psum | solution.py:346
  90.2 3.4 %finish.1 = bf16[512,1536]{1,0:T(8,128)(2,1)S(1)} custom-call(s32[1]{0:T(128)S(6)} %copy.17.evicted_ref, f32[512,1536]{1,0:T(8,128)} %get-tuple-element.25.a_ref, bf16[512,1536]{1,0:T(8,128)(2,1)} %get-tuple-element.26.x_ref, f32[3,512]{1,0:T(4,128)S(1)} %psum.14.t_ref, f32[3,512]{1,0:T(4,128)S(1)} %collective-permute-done.1.rest_1_.held_ref, ...), custom_call_target="tpu_custom_call" | custom-call | tf_op jit(solution)/shard_map/finish/pallas_call | solution.py:236
  93.7 3.2 %collective-permute-start.4 = (bf16[512,1536]{1,0:T(8,128)(2,1)S(1)}, bf16[512,1536]{1,0:T(8,128)(2,1)S(1)}, u32[]{:S(2)}, u32[]{:S(2)}) collective-permute-start(bf16[512,1536]{1,0:T(8,128)(2,1)S(1)} %finish.1), channel_id=1, source_target_pairs={{0,28},{4,0},{8,4},{12,8},{16,12},{20,16},{24,20},{28,24},{1,29},{... | collective-permute-start | bytes 4718600 | tf_op jit(solution)/shard_map/ppermute | solution.py:317
  96.8 33.0 %collective-permute-done.4 = bf16[512,1536]{1,0:T(8,128)(2,1)S(1)} collective-permute-done((bf16[512,1536]{1,0:T(8,128)(2,1)S(1)}, bf16[512,1536]{1,0:T(8,128)(2,1)S(1)}, u32[]{:S(2)}, u32[]{:S(2)}) %collective-permute-start.4) | collective-permute-done | bytes 1572896 | tf_op jit(solution)/shard_map/ppermute | solution.py:317
  129.9 1.1 copy.18
  (1 shorter events, 0.0 us)
Async XLA Ops:
  1.9 4.2 %copy-start.2 = (f32[8,128]{1,0:T(8,128)}, f32[8,128]{1,0:T(8,128)S(1)}, u32[]{:S(2)}) copy-start(f32[8,128]{1,0:T(8,128)S(1)} %get-tuple-element.15.rest_0_) | copy-start | bytes 12292
  1.9 55.7 %collective-permute-start = (bf16[512,512]{1,0:T(8,128)(2,1)S(1)}, bf16[512,512]{1,0:T(8,128)(2,1)S(1)}, u32[]{:S(2)}, u32[]{:S(2)}) collective-permute-start(bf16[512,512]{1,0:T(8,128)(2,1)S(1)} %get-tuple-element.16), channel_id=1, source_target_pairs={{0,16},{4,20},{8,24},{12,28},{16,0},{20,4},{24,8},{28,12},{1,17},{... | collective-permute-start | bytes 1572872 | tf_op jit(solution)/shard_map/ppermute | solution.py:317
  6.0 60.9 %collective-permute-start.3 = (bf16[512,640]{1,0:T(8,128)(2,1)S(1)}, bf16[512,640]{1,0:T(8,128)(2,1)S(1)}, u32[]{:S(2)}, u32[]{:S(2)}) collective-permute-start(bf16[512,640]{1,0:T(8,128)(2,1)S(1)} %get-tuple-element.18), channel_id=1, source_target_pairs={{0,16},{4,20},{8,24},{12,28},{16,0},{20,4},{24,8},{28,12},{1,17},{... | collective-permute-start | bytes 1966088 | tf_op jit(solution)/shard_map/ppermute | solution.py:317
  6.1 14.2 %copy-start = (f32[1,1536]{1,0:T(1,128)S(1)}, f32[1,1536]{1,0:T(1,128)}, u32[]{:S(2)}) copy-start(f32[1,1536]{1,0:T(1,128)} %gq_ref.7) | copy-start | bytes 18436
  6.1 14.2 %copy-start.1 = (f32[1,1536]{1,0:T(1,128)S(1)}, f32[1,1536]{1,0:T(1,128)}, u32[]{:S(2)}) copy-start(f32[1,1536]{1,0:T(1,128)} %gk_ref.7) | copy-start | bytes 18436
  17.4 40.2 %collective-permute-start.1 = (f32[3,512]{1,0:T(4,128)S(1)}, f32[3,512]{1,0:T(4,128)S(1)}, u32[]{:S(2)}, u32[]{:S(2)}) collective-permute-start(f32[3,512]{1,0:T(4,128)S(1)} %psum.14.t_ref), channel_id=1, source_target_pairs={{0,16},{4,20},{8,24},{12,28},{16,0},{20,4},{24,8},{28,12},{1,17},{... | collective-permute-start | bytes 18440 | tf_op jit(solution)/shard_map/ppermute | solution.py:317
  59.2 19.7 %collective-permute-start.2 = (bf16[512,384]{1,0:T(8,128)(2,1)S(1)}, bf16[512,384]{1,0:T(8,128)(2,1)S(1)}, u32[]{:S(2)}, u32[]{:S(2)}) collective-permute-start(bf16[512,384]{1,0:T(8,128)(2,1)S(1)} %get-tuple-element.17), channel_id=1, source_target_pairs={{0,16},{4,20},{8,24},{12,28},{16,0},{20,4},{24,8},{28,12},{1,17},{... | collective-permute-start | bytes 1179656 | tf_op jit(solution)/shard_map/ppermute | solution.py:317
  93.7 36.2 %collective-permute-start.4 = (bf16[512,1536]{1,0:T(8,128)(2,1)S(1)}, bf16[512,1536]{1,0:T(8,128)(2,1)S(1)}, u32[]{:S(2)}, u32[]{:S(2)}) collective-permute-start(bf16[512,1536]{1,0:T(8,128)(2,1)S(1)} %finish.1), channel_id=1, source_target_pairs={{0,28},{4,0},{8,4},{12,8},{16,12},{20,16},{24,20},{28,24},{1,29},{... | collective-permute-start | bytes 4718600 | tf_op jit(solution)/shard_map/ppermute | solution.py:317

commit v14 on v13

--- a/solution.py
+++ b/solution.py
@@ -158,9 +158,15 @@
     return wide, d_normed
 
 
-def backward_kernel(first, heads, width_all, evicted_ref, own_ref, far_ref, g_ref, t_ref, held_ref, gq_ref, gk_ref, past_ref, *refs):
-    a_out, x_out, inner_ref, xs, gs, outs, x_sem, g_sem, a_sem, out_sem = refs[-10:]
+def backward_kernel(
+    first, base, heads, ahead, width_all,
+    evicted_ref, own_ref, far_ref, g_ref, t_ref, held_ref, gq_ref, gk_ref, past_ref, *refs,
+):
     evicted = evicted_ref[0] == 1
+    if ahead:
+        pair, inner_ref, xs, gs, x_sem, g_sem = refs[-6:]
+    else:
+        a_out, x_out, inner_ref, xs, gs, outs, x_sem, g_sem, a_sem, out_sem = refs[-10:]
     copies = []
     for h in range(heads):
         to = lanes_of(h * HDIM, HDIM)
@@ -184,11 +190,17 @@
         there = lanes_of(first + h * HDIM, HDIM)
         g = gs[mine]
         wide, d_normed = backward_head(xs[mine], g, factor, gq_ref[there], gk_ref[there])
-        outs[mine] = g.astype(F32) + factor * d_normed
-        sent.append(pltpu.make_async_copy(outs.at[mine], a_out.at[there], a_sem.at[h]))
-        sent.append(pltpu.make_async_copy(xs.at[mine], x_out.at[there], out_sem.at[h]))
-        for copy in sent[-2:]:
-            copy.start()
+        term = g.astype(F32) + factor * d_normed
+        if ahead:
+            pair[mine] = term.astype(BF16)
+            pair[lanes_of((heads + h) * HDIM, HDIM)] = xs[mine]
+        else:
+            outs[mine] = term
+            to = lanes_of(first - base + h * HDIM, HDIM)
+            sent.append(pltpu.make_async_copy(outs.at[mine], a_out.at[to], a_sem.at[h]))
+            sent.append(pltpu.make_async_copy(xs.at[mine], x_out.at[to], out_sem.at[h]))
+            for copy in sent[-2:]:
+                copy.start()
         product = d_normed * wide
         part = product if part is None else part + product
     inner_ref[...] = jnp.sum(part.T, axis=0, keepdims=True) + past_ref[...]
@@ -200,22 +212,28 @@
     return jnp.where(evicted_ref[0] == 1, held_ref[2:3, :], t_ref[1:2, :])
 
 
-def backward(width_all, evicted, stash, far, g, totals, held, gain_q, gain_k, past, heads, first, sofar=(), after=()):
+def backward(
+    width_all, evicted, stash, far, g, totals, held, gain_q, gain_k, past, heads, first, base, sofar=(), after=()
+):
     tokens, width = totals.shape[1], gain_q.shape[1]
+    ahead = first < base
     small = (tokens, heads * HDIM)
     dma = pltpu.SemaphoreType.DMA((heads,))
-    return pl.pallas_call(
-        functools.partial(backward_kernel, first, heads, width_all),
-        out_shape=(
-            pltpu.HBM((tokens, width), F32),
-            pltpu.HBM((tokens, width), BF16),
-            jax.ShapeDtypeStruct((1, tokens), F32),
-        ),
+    inner = jax.ShapeDtypeStruct((1, tokens), F32)
+    if ahead:
+        shapes = (jax.ShapeDtypeStruct((tokens, 2 * heads * HDIM), BF16), inner)
+        scratch = [pltpu.VMEM(small, BF16)] * 2 + [dma] * 2
+    else:
+        shapes = (pltpu.HBM((tokens, width - base), F32), pltpu.HBM((tokens, width - base), BF16), inner)
+        scratch = [pltpu.VMEM(small, BF16)] * 2 + [pltpu.VMEM(small, F32)] + [dma] * 4
+    return pl.pallas_call(
+        functools.partial(backward_kernel, first, base, heads, ahead, width_all),
+        out_shape=shapes,
         in_specs=[pl.BlockSpec(memory_space=pltpu.SMEM)] + [ANYWHERE] * 3 + [IN_VMEM] * 5
         + [IN_HBM] * len(sofar) + [ANYWHERE] * len(after),
-        out_specs=(IN_HBM, IN_HBM, IN_VMEM),
+        out_specs=(IN_VMEM, IN_VMEM) if ahead else (IN_HBM, IN_HBM, IN_VMEM),
         input_output_aliases={9: 0, 10: 1} if sofar else {},
-        scratch_shapes=[pltpu.VMEM(small, BF16)] * 2 + [pltpu.VMEM(small, F32)] + [dma] * 4,
+        scratch_shapes=scratch,
         compiler_params=compiler(VMEM),
         name="backward",
     )(evicted, in_hbm(stash), far, in_hbm(g), totals, held, gain_q, gain_k, past, *sofar, *after)
@@ -225,8 +243,9 @@
     return inverse_rms(total, width_all) ** 3 * inner / width_all
 
 
-def finish_kernel(width_all, evicted_ref, a_ref, x_ref, t_ref, held_ref, inner_ref, o_ref):
+def finish_kernel(width_all, evicted_ref, a_ref, x_ref, t_ref, held_ref, inner_ref, o_ref, row_ref):
     row = row_of(total_of(evicted_ref, t_ref, held_ref), inner_ref[...], width_all)
+    row_ref[...] = row
     o_ref[...] = (a_ref[...] - x_ref[...].astype(F32) * column_of(row)).astype(BF16)
 
 
@@ -235,13 +254,43 @@
     block = pl.BlockSpec((tokens, lanes), lambda i: (0, i))
     return pl.pallas_call(
         functools.partial(finish_kernel, width_all),
-        out_shape=jax.ShapeDtypeStruct(a.shape, BF16),
+        out_shape=(jax.ShapeDtypeStruct(a.shape, BF16), jax.ShapeDtypeStruct((1, tokens), F32)),
         grid=(width // lanes,),
         in_specs=[pl.BlockSpec(memory_space=pltpu.SMEM), block, block] + [IN_VMEM] * 3,
-        out_specs=block,
+        out_specs=(block, pl.BlockSpec((1, tokens), lambda i: (0, 0))),
         compiler_params=compiler(VMEM),
         name="finish",
     )(evicted, in_hbm(a), in_hbm(x), totals, held, inner)
+
+
+def place_kernel(ahead, pair_ref, row_ref, rest_ref, o_ref):
+    step = pl.program_id(0)
+
+    @pl.when(step < ahead)
+    def _():
+        at = pl.multiple_of(step * HDIM, HDIM)
+        term = pair_ref[:, pl.ds(at, HDIM)]
+        x = pair_ref[:, pl.ds(at + ahead * HDIM, HDIM)]
+        o_ref[...] = (term.astype(F32) - x.astype(F32) * column_of(row_ref[...])).astype(BF16)
+
+    @pl.when(step >= ahead)
+    def _():
+        o_ref[...] = rest_ref[:, pl.ds(pl.multiple_of((step - ahead) * HDIM, HDIM), HDIM)]
+
+
+def place(pair, row, rest):
+    tokens = rest.shape[0]
+    ahead = pair.shape[1] // HDIM // 2
+    width = rest.shape[1] + ahead * HDIM
+    return pl.pallas_call(
+        functools.partial(place_kernel, ahead),
+        out_shape=jax.ShapeDtypeStruct((tokens, width), BF16),
+        grid=(width // HDIM,),
+        in_specs=[IN_VMEM] * 3,
+        out_specs=pl.BlockSpec((tokens, HDIM), lambda i: (0, i)),
+        compiler_params=compiler(VMEM),
+        name="place",
+    )(pair, row, rest)
 
 
 def squares_kernel(current_ref, stash_ref, *rest):
@@ -324,7 +373,7 @@
     current = layer_input[0]
     tokens, width = current.shape
     count = width // HDIM
-    heads = (max(1, count // 3), count - max(1, count // 3) - max(1, count // 4), max(1, count // 4))
+    heads = (max(1, count // 3), count - max(1, count // 3) - max(1, count // 6), max(1, count // 6))
     sizes = [h * HDIM for h in heads]
     starts = [sum(sizes[:i]) for i in range(3)]
     third = count // 3 * HDIM
@@ -336,16 +385,21 @@
     output = forward(width_all, current, totals, query_gain, key_gain, third // HDIM)
     fetched.append(send(pieces_of(stashed, starts[2:], sizes[2:], (fetched[0], held, in_hbm(output)))[0], partner))
 
-    sofar, inner, after = (), jnp.zeros((1, tokens), F32), (in_hbm(output),)
-    for h, start, far in zip(heads, starts, fetched):
-        *sofar, inner = backward(
-            width_all, eviction, stashed, far, grad_input, totals, held, query_gain, key_gain, inner, h, start,
-            tuple(sofar), after,
-        )
-        after = ()
+    share = functools.partial(backward, width_all, eviction, stashed)
+    facts = (grad_input, totals, held, query_gain, key_gain)
+    base = starts[1]
+    pair, inner = share(
+        fetched[0], *facts, jnp.zeros((1, tokens), F32), heads[0], 0, base, (), (in_hbm(output),)
+    )
+    pair = send(pair, prior)
+    sofar = ()
+    for h, start, far in zip(heads[1:], starts[1:], fetched[1:]):
+        *sofar, inner = share(far, *facts, inner, h, start, base, tuple(sofar))
     inner = lax.psum(inner, "tensor")
-    result = finish(width_all, eviction, *sofar, totals, held, inner, third)
-    return (output[None], send(result, prior)[None])
+    lanes = next(c for c in (2, 1) if (width - base) % (c * HDIM) == 0) * HDIM
+    result, row = finish(width_all, eviction, *sofar, totals, held, inner, lanes)
+    result = place(pair, send(row, prior), send(result, prior))
+    return (output[None], result[None])
 
 
 def solution(mesh):

time: 131 us -> 130 us (level)
  waiting for transfers between devices: 65.7 us -> 56.8 us
  Pallas kernels: 40.2 us -> 45 us
  starting transfers between devices: 10.4 us -> 13.3 us
    ppermute x5 -> x7, waiting for transfers between devices: 65.7 us -> 56.8 us  [send(): return lax.ppermute(x, 'section', pairs)]
    pallas_call x4 -> x5, Pallas kernels: 24.2 us -> 28.1 us  [the longest x3 20.2 us: backward(): pl.pallas_call(functools.partial(backward_kernel, first, base, heads, ahe...]
    ppermute x5 -> x7, starting transfers between devices: 10.4 us -> 13.3 us  [send(): return lax.ppermute(x, 'section', pairs)]
  transfers between devices with their start and end apart: 5 -> 7, of which waited for: 3 -> 2; matrix products, arithmetic and copies ran while one was open for 0% -> 0% of each run, Pallas kernels for 23% -> 29%
where the time goes in v14:
time: 130 us
  waiting for transfers between devices  56.8 us (44%)
  Pallas kernels  45 us (35%)
  starting transfers between devices  13.3 us (10%)
  blocking collectives  13.3 us (10%)
  between operations  1.37 us (1%)
    ppermute x7, waiting for transfers between devices, send(): return lax.ppermute(x, 'section', pairs)  56.8 us
    pallas_call x3, Pallas kernels, backward(): pl.pallas_call(functools.partial(backward_kernel, first, base, heads, ahe...  20.2 us
    ppermute x7, starting transfers between devices, send(): return lax.ppermute(x, 'section', pairs)  13.3 us
    pallas_call x1, Pallas kernels, forward(): pl.pallas_call(functools.partial(forward_kernel, heads, width_all), out_s...  8.38 us
    psum x1, blocking collectives, local(): inner = lax.psum(inner, 'tensor')  6.8 us
    psum x1, blocking collectives, local(): totals = lax.psum(squares(current, stashed, third, (mark,)), 'tensor')  6.51 us
    pallas_call x1, Pallas kernels, place(): pl.pallas_call(functools.partial(place_kernel, ahead), out_shape=jax.Shap...  4.76 us
    pallas_call x1, Pallas kernels, squares(): pl.pallas_call(squares_kernel, out_shape=jax.ShapeDtypeStruct((3, tokens)...  4.76 us
  transfers between devices with their start and end apart: 7, of which 2 were waited for; matrix products, arithmetic and copies ran while one was open for 0% of the time, Pallas kernels for 29%

profile of v14, /device:TPU:0, one launch (start us, length us, event | category | flops | bytes accessed | tf_op | source)
XLA Modules:
  0.0 129.8 jit_solution(6043565002603959772)
XLA Ops:
  0.6 2.2 %pieces.2 = (bf16[512,512]{1,0:T(8,128)(2,1)S(1)}, bf16[512,768]{1,0:T(8,128)(2,1)}, f32[8,128]{1,0:T(8,128)S(1)}) custom-call(bf16[1,2,512,1536]{3,2,1,0:T(8,128)(2,1)} %own_ref.5), custom_call_target="tpu_custom_call" | custom-call | tf_op jit(solution)/shard_map/pieces/pallas_call | solution.py:354
  2.8 0.0 copy-start.2
  2.8 4.1 %collective-permute-start = (bf16[512,512]{1,0:T(8,128)(2,1)S(1)}, bf16[512,512]{1,0:T(8,128)(2,1)S(1)}, u32[]{:S(2)}, u32[]{:S(2)}) collective-permute-start(bf16[512,512]{1,0:T(8,128)(2,1)S(1)} %get-tuple-element.17), channel_id=1, source_target_pairs={{0,16},{4,20},{8,24},{12,28},{16,0},{20,4},{24,8},{28,12},{1,17},{... | collective-permute-start | bytes 1572872 | tf_op jit(solution)/shard_map/ppermute | solution.py:366
  6.9 0.1 collective-permute-start.4
  7.0 0.0 copy-done.2
  7.0 0.0 copy-start
  7.0 0.0 copy-start.1
  7.0 4.8 %squares.1 = f32[3,512]{1,0:T(4,128)} custom-call(bf16[512,1536]{1,0:T(8,128)(2,1)} %bitcast.4, bf16[1,2,512,1536]{3,2,1,0:T(8,128)(2,1)} %own_ref.5, f32[8,128]{1,0:T(8,128)} %copy-done.2), custom_call_target="tpu_custom_call" | custom-call | tf_op jit(solution)/shard_map/squares/pallas_call | solution.py:324
  11.8 6.5 %psum.14.t_ref = f32[3,512]{1,0:T(4,128)S(1)} all-reduce(f32[3,512]{1,0:T(4,128)} %squares.1), channel_id=1, replica_groups=mesh['section'=8,'tensor'=4] {'tensor'}, use_global_device_ids=true, to_apply=%region_0.0 | all-reduce | flops 1536 | bytes 12288 | tf_op jit(solution)/shard_map/psum | solution.py:383
  18.3 2.9 %collective-permute-start.1 = (f32[3,512]{1,0:T(4,128)S(1)}, f32[3,512]{1,0:T(4,128)S(1)}, u32[]{:S(2)}, u32[]{:S(2)}) collective-permute-start(f32[3,512]{1,0:T(4,128)S(1)} %psum.14.t_ref), channel_id=1, source_target_pairs={{0,16},{4,20},{8,24},{12,28},{16,0},{20,4},{24,8},{28,12},{1,17},{... | collective-permute-start | bytes 18440 | tf_op jit(solution)/shard_map/ppermute | solution.py:366
  21.2 0.0 copy-done
  21.2 0.0 copy-done.1
  21.2 8.4 %forward.1.refs_0_.rest_2_ = bf16[512,1536]{1,0:T(8,128)(2,1)} custom-call(bf16[512,1536]{1,0:T(8,128)(2,1)} %bitcast.5, f32[3,512]{1,0:T(4,128)S(1)} %psum.14.t_ref, f32[1,1536]{1,0:T(1,128)S(1)} %copy-done, f32[1,1536]{1,0:T(1,128)S(1)} %copy-done.1), custom_call_target="tpu_custom_call" | custom-call | tf_op jit(solution)/shard_map/forward/pallas_call | solution.py:119
  29.6 34.5 %collective-permute-done.1.held_ref.rest_1_ = f32[3,512]{1,0:T(4,128)S(1)} collective-permute-done((f32[3,512]{1,0:T(4,128)S(1)}, f32[3,512]{1,0:T(4,128)S(1)}, u32[]{:S(2)}, u32[]{:S(2)}) %collective-permute-start.1) | collective-permute-done | bytes 6176 | tf_op jit(solution)/shard_map/ppermute | solution.py:366
  64.2 0.0 collective-permute-done.far_ref.rest_0_
  64.2 1.5 %pieces.3 = (bf16[512,256]{1,0:T(8,128)(2,1)S(1)}, f32[8,128]{1,0:T(8,128)}) custom-call(bf16[1,2,512,1536]{3,2,1,0:T(8,128)(2,1)} %own_ref.5, bf16[512,512]{1,0:T(8,128)(2,1)S(1)} %collective-permute-done.far_ref.rest_0_, f32[3,512]{1,0:T(4,128)S(1)} %collective-permute-done.1.held_ref.rest_1_, bf16[512,1536]{1,0:T(8,128)(2,1)} %forward.1.refs_0_.rest_2_), custom_call_target="tpu_custom_call" | custom-call | tf_op jit(solution)/shard_map/pieces/pallas_call | solution.py:354
  65.7 0.1 collective-permute-start.3
  66.5 6.4 %backward.3 = (bf16[512,1024]{1,0:T(8,128)(2,1)S(1)}, f32[1,512]{1,0:T(1,128)S(1)}) custom-call(s32[1]{0:T(128)S(6)} %copy.12.evicted_ref, bf16[1,2,512,1536]{3,2,1,0:T(8,128)(2,1)} %own_ref.5, bf16[512,512]{1,0:T(8,128)(2,1)S(1)} %collective-permute-done.far_ref.rest_0_, bf16[1,512,1536]{2,1,0:T(8,128)(2,1)} %g_ref.5, f32[3,512]{1,0:T(4,128)S(1)} %psum.14.t_ref, ...), custom_call_target="tpu_custom_call" | custom-call | tf_op jit(solution)/shard_map/backward/pallas_call | solution.py:229
  72.8 4.5 %collective-permute-start.2 = (bf16[512,1024]{1,0:T(8,128)(2,1)S(1)}, bf16[512,1024]{1,0:T(8,128)(2,1)S(1)}, u32[]{:S(2)}, u32[]{:S(2)}) collective-permute-start(bf16[512,1024]{1,0:T(8,128)(2,1)S(1)} %get-tuple-element.18), channel_id=1, source_target_pairs={{0,28},{4,0},{8,4},{12,8},{16,12},{20,16},{24,20},{28,24},{1,29},{... | collective-permute-start | bytes 3145736 | tf_op jit(solution)/shard_map/ppermute | solution.py:366
  77.4 0.0 collective-permute-done.4.far_ref
  77.4 9.5 %backward.4 = (f32[512,1024]{1,0:T(8,128)}, bf16[512,1024]{1,0:T(8,128)(2,1)}, f32[1,512]{1,0:T(1,128)S(1)}) custom-call(s32[1]{0:T(128)S(6)} %copy.12.evicted_ref, bf16[1,2,512,1536]{3,2,1,0:T(8,128)(2,1)} %own_ref.5, bf16[512,768]{1,0:T(8,128)(2,1)S(1)} %collective-permute-done.4.far_ref, bf16[1,512,1536]{2,1,0:T(8,128)(2,1)} %g_ref.5, ...), custom_call_target="tpu_custom_call" | custom-call | tf_op jit(solution)/shard_map/backward/pallas_call | solution.py:229
  86.9 0.0 collective-permute-done.3.far_ref
  86.9 4.3 %backward.5 = (f32[512,1024]{1,0:T(8,128)}, bf16[512,1024]{1,0:T(8,128)(2,1)}, f32[1,512]{1,0:T(1,128)S(1)}) custom-call(s32[1]{0:T(128)S(6)} %copy.12.evicted_ref, bf16[1,2,512,1536]{3,2,1,0:T(8,128)(2,1)} %own_ref.5, bf16[512,256]{1,0:T(8,128)(2,1)S(1)} %collective-permute-done.3.far_ref, ...), custom_call_target="tpu_custom_call", output_to_operand_aliasing={{0}: (9, {}), {1}: (10, {})} | custom-call | tf_op jit(solution)/shard_map/backward/pallas_call | solution.py:229
  91.2 6.8 %psum.15.inner_ref = f32[1,512]{1,0:T(1,128)S(1)} all-reduce(f32[1,512]{1,0:T(1,128)S(1)} %get-tuple-element.27), channel_id=1, replica_groups=mesh['section'=8,'tensor'=4] {'tensor'}, use_global_device_ids=true, to_apply=%region_1.0 | all-reduce | flops 512 | bytes 4096 | tf_op jit(solution)/shard_map/psum | solution.py:398
  98.0 3.1 %finish.1 = (bf16[512,1024]{1,0:T(8,128)(2,1)S(1)}, f32[1,512]{1,0:T(1,128)S(1)}) custom-call(s32[1]{0:T(128)S(6)} %copy.12.evicted_ref, f32[512,1024]{1,0:T(8,128)} %get-tuple-element.25.a_ref, bf16[512,1024]{1,0:T(8,128)(2,1)} %get-tuple-element.26.x_ref, f32[3,512]{1,0:T(4,128)S(1)} %psum.14.t_ref, f32[3,512]{1,0:T(4,128)S(1)} %collective-permute-done.1.held_ref.rest_1_, ...), custom_call_target="tpu_custom_call" | custom-call | tf_op jit(solution)/shard_map/finish/pallas_call | solution.py:255
  101.2 0.5 collective-permute-start.6
  101.7 1.1 collective-permute-start.5
  102.8 22.3 %collective-permute-done.5.row_ref = f32[1,512]{1,0:T(1,128)S(1)} collective-permute-done((f32[1,512]{1,0:T(1,128)S(1)}, f32[1,512]{1,0:T(1,128)S(1)}, u32[]{:S(2)}, u32[]{:S(2)}) %collective-permute-start.5) | collective-permute-done | bytes 2080 | tf_op jit(solution)/shard_map/ppermute | solution.py:366
  125.1 0.0 collective-permute-done.2.pair_ref
  125.1 0.0 collective-permute-done.6.rest_ref
  125.1 4.8 %place.1 = bf16[512,1536]{1,0:T(8,128)(2,1)} custom-call(bf16[512,1024]{1,0:T(8,128)(2,1)S(1)} %collective-permute-done.2.pair_ref, f32[1,512]{1,0:T(1,128)S(1)} %collective-permute-done.5.row_ref, bf16[512,1024]{1,0:T(8,128)(2,1)S(1)} %collective-permute-done.6.rest_ref), custom_call_target="tpu_custom_call" | custom-call | tf_op jit(solution)/shard_map/place/pallas_call | solution.py:285
  (1 shorter events, 0.0 us)
Async XLA Ops:
  2.8 4.2 %copy-start.2 = (f32[8,128]{1,0:T(8,128)}, f32[8,128]{1,0:T(8,128)S(1)}, u32[]{:S(2)}) copy-start(f32[8,128]{1,0:T(8,128)S(1)} %get-tuple-element.16.rest_0_) | copy-start | bytes 12292
  2.8 61.3 %collective-permute-start = (bf16[512,512]{1,0:T(8,128)(2,1)S(1)}, bf16[512,512]{1,0:T(8,128)(2,1)S(1)}, u32[]{:S(2)}, u32[]{:S(2)}) collective-permute-start(bf16[512,512]{1,0:T(8,128)(2,1)S(1)} %get-tuple-element.17), channel_id=1, source_target_pairs={{0,16},{4,20},{8,24},{12,28},{16,0},{20,4},{24,8},{28,12},{1,17},{... | collective-permute-start | bytes 1572872 | tf_op jit(solution)/shard_map/ppermute | solution.py:366
  6.9 70.4 %collective-permute-start.4 = (bf16[512,768]{1,0:T(8,128)(2,1)}, bf16[512,768]{1,0:T(8,128)(2,1)S(1)}, u32[]{:S(2)}, u32[]{:S(2)}) collective-permute-start(bf16[512,768]{1,0:T(8,128)(2,1)} %get-tuple-element.20), channel_id=1, source_target_pairs={{0,16},{4,20},{8,24},{12,28},{16,0},{20,4},{24,8},{28,12},{1,17},{... | collective-permute-start | bytes 2359304 | tf_op jit(solution)/shard_map/ppermute | solution.py:366
  7.0 14.2 %copy-start = (f32[1,1536]{1,0:T(1,128)S(1)}, f32[1,1536]{1,0:T(1,128)}, u32[]{:S(2)}) copy-start(f32[1,1536]{1,0:T(1,128)} %gq_ref.7) | copy-start | bytes 18436
  7.0 14.2 %copy-start.1 = (f32[1,1536]{1,0:T(1,128)S(1)}, f32[1,1536]{1,0:T(1,128)}, u32[]{:S(2)}) copy-start(f32[1,1536]{1,0:T(1,128)} %gk_ref.7) | copy-start | bytes 18436
  18.3 45.8 %collective-permute-start.1 = (f32[3,512]{1,0:T(4,128)S(1)}, f32[3,512]{1,0:T(4,128)S(1)}, u32[]{:S(2)}, u32[]{:S(2)}) collective-permute-start(f32[3,512]{1,0:T(4,128)S(1)} %psum.14.t_ref), channel_id=1, source_target_pairs={{0,16},{4,20},{8,24},{12,28},{16,0},{20,4},{24,8},{28,12},{1,17},{... | collective-permute-start | bytes 18440 | tf_op jit(solution)/shard_map/ppermute | solution.py:366
  65.7 21.2 %collective-permute-start.3 = (bf16[512,256]{1,0:T(8,128)(2,1)S(1)}, bf16[512,256]{1,0:T(8,128)(2,1)S(1)}, u32[]{:S(2)}, u32[]{:S(2)}) collective-permute-start(bf16[512,256]{1,0:T(8,128)(2,1)S(1)} %get-tuple-element.19), channel_id=1, source_target_pairs={{0,16},{4,20},{8,24},{12,28},{16,0},{20,4},{24,8},{28,12},{1,17},{... | collective-permute-start | bytes 786440 | tf_op jit(solution)/shard_map/ppermute | solution.py:366
  72.8 52.2 %collective-permute-start.2 = (bf16[512,1024]{1,0:T(8,128)(2,1)S(1)}, bf16[512,1024]{1,0:T(8,128)(2,1)S(1)}, u32[]{:S(2)}, u32[]{:S(2)}) collective-permute-start(bf16[512,1024]{1,0:T(8,128)(2,1)S(1)} %get-tuple-element.18), channel_id=1, source_target_pairs={{0,28},{4,0},{8,4},{12,8},{16,12},{20,16},{24,20},{28,24},{1,29},{... | collective-permute-start | bytes 3145736 | tf_op jit(solution)/shard_map/ppermute | solution.py:366
  101.2 23.9 %collective-permute-start.6 = (bf16[512,1024]{1,0:T(8,128)(2,1)S(1)}, bf16[512,1024]{1,0:T(8,128)(2,1)S(1)}, u32[]{:S(2)}, u32[]{:S(2)}) collective-permute-start(bf16[512,1024]{1,0:T(8,128)(2,1)S(1)} %get-tuple-element.29), channel_id=1, source_target_pairs={{0,28},{4,0},{8,4},{12,8},{16,12},{20,16},{24,20},{28,24},{1,29},{... | collective-permute-start | bytes 3145736 | tf_op jit(solution)/shard_map/ppermute | solution.py:366
  101.7 23.3 %collective-permute-start.5 = (f32[1,512]{1,0:T(1,128)S(1)}, f32[1,512]{1,0:T(1,128)S(1)}, u32[]{:S(2)}, u32[]{:S(2)}) collective-permute-start(f32[1,512]{1,0:T(1,128)S(1)} %get-tuple-element.28), channel_id=1, source_target_pairs={{0,28},{4,0},{8,4},{12,8},{16,12},{20,16},{24,20},{28,24},{1,29},{... | collective-permute-start | bytes 6152 | tf_op jit(solution)/shard_map/ppermute | solution.py:366

commit v15 on v14

--- a/solution.py
+++ b/solution.py
@@ -159,10 +159,10 @@
 
 
 def backward_kernel(
-    first, base, heads, ahead, width_all,
-    evicted_ref, own_ref, far_ref, g_ref, t_ref, held_ref, gq_ref, gk_ref, past_ref, *refs,
+    first, base, heads, ahead, pieces, width_all, evicted_ref, own_ref, g_ref, t_ref, held_ref, gq_ref, gk_ref, past_ref, *refs
 ):
     evicted = evicted_ref[0] == 1
+    far_refs, each = refs[:pieces], heads // pieces
     if ahead:
         pair, inner_ref, xs, gs, x_sem, g_sem = refs[-6:]
     else:
@@ -171,7 +171,8 @@
     for h in range(heads):
         to = lanes_of(h * HDIM, HDIM)
         there = lanes_of(first + h * HDIM, HDIM)
-        far = pltpu.make_async_copy(far_ref.at[to], xs.at[to], x_sem.at[h])
+        far_ref = far_refs[h // each].at[: t_ref.shape[1], h % each * HDIM : (h % each + 1) * HDIM]
+        far = pltpu.make_async_copy(far_ref, xs.at[to], x_sem.at[h])
         near = pltpu.make_async_copy(own_ref.at[(0, 0) + there], xs.at[to], x_sem.at[h])
         g = pltpu.make_async_copy(g_ref.at[(0,) + there], gs.at[to], g_sem.at[h])
         pl.when(evicted)(far.start)
@@ -209,7 +210,7 @@
 
 
 def total_of(evicted_ref, t_ref, held_ref):
-    return jnp.where(evicted_ref[0] == 1, held_ref[2:3, :], t_ref[1:2, :])
+    return jnp.where(evicted_ref[0] == 1, held_ref[...], t_ref[1:2, :])
 
 
 def backward(
@@ -227,16 +228,16 @@
         shapes = (pltpu.HBM((tokens, width - base), F32), pltpu.HBM((tokens, width - base), BF16), inner)
         scratch = [pltpu.VMEM(small, BF16)] * 2 + [pltpu.VMEM(small, F32)] + [dma] * 4
     return pl.pallas_call(
-        functools.partial(backward_kernel, first, base, heads, ahead, width_all),
+        functools.partial(backward_kernel, first, base, heads, ahead, len(far), width_all),
         out_shape=shapes,
-        in_specs=[pl.BlockSpec(memory_space=pltpu.SMEM)] + [ANYWHERE] * 3 + [IN_VMEM] * 5
-        + [IN_HBM] * len(sofar) + [ANYWHERE] * len(after),
+        in_specs=[pl.BlockSpec(memory_space=pltpu.SMEM)] + [ANYWHERE] * 2 + [IN_VMEM] * 5
+        + [ANYWHERE] * len(far) + [IN_HBM] * len(sofar) + [ANYWHERE] * len(after),
         out_specs=(IN_VMEM, IN_VMEM) if ahead else (IN_HBM, IN_HBM, IN_VMEM),
-        input_output_aliases={9: 0, 10: 1} if sofar else {},
+        input_output_aliases={8 + len(far): 0, 9 + len(far): 1} if sofar else {},
         scratch_shapes=scratch,
         compiler_params=compiler(VMEM),
         name="backward",
-    )(evicted, in_hbm(stash), far, in_hbm(g), totals, held, gain_q, gain_k, past, *sofar, *after)
+    )(evicted, in_hbm(stash), in_hbm(g), totals, held, gain_q, gain_k, past, *far, *sofar, *after)
 
 
 def row_of(total, inner, width_all):
@@ -263,34 +264,51 @@
     )(evicted, in_hbm(a), in_hbm(x), totals, held, inner)
 
 
-def place_kernel(ahead, pair_ref, row_ref, rest_ref, o_ref):
-    step = pl.program_id(0)
-
-    @pl.when(step < ahead)
-    def _():
-        at = pl.multiple_of(step * HDIM, HDIM)
-        term = pair_ref[:, pl.ds(at, HDIM)]
-        x = pair_ref[:, pl.ds(at + ahead * HDIM, HDIM)]
-        o_ref[...] = (term.astype(F32) - x.astype(F32) * column_of(row_ref[...])).astype(BF16)
-
-    @pl.when(step >= ahead)
-    def _():
-        o_ref[...] = rest_ref[:, pl.ds(pl.multiple_of((step - ahead) * HDIM, HDIM), HDIM)]
+def place_kernel(ahead, pair_ref, row_ref, rest_ref, o_ref, outs, sems):
+    lanes = ahead * HDIM
+    width = o_ref.shape[1]
+    rest = pltpu.make_async_copy(rest_ref, o_ref.at[lanes_of(lanes, width - lanes)], sems.at[ahead])
+    rest.start()
+    row = column_of(row_ref[...])
+    copies = [rest]
+    for h in range(ahead):
+        mine = lanes_of(h * HDIM, HDIM)
+        x = pair_ref[lanes_of(lanes + h * HDIM, HDIM)]
+        outs[mine] = (pair_ref[mine].astype(F32) - x.astype(F32) * row).astype(BF16)
+        copies.append(pltpu.make_async_copy(outs.at[mine], o_ref.at[mine], sems.at[h]))
+        copies[-1].start()
+    for copy in copies:
+        copy.wait()
 
 
 def place(pair, row, rest):
     tokens = rest.shape[0]
     ahead = pair.shape[1] // HDIM // 2
-    width = rest.shape[1] + ahead * HDIM
     return pl.pallas_call(
         functools.partial(place_kernel, ahead),
-        out_shape=jax.ShapeDtypeStruct((tokens, width), BF16),
-        grid=(width // HDIM,),
+        out_shape=jax.ShapeDtypeStruct((tokens, rest.shape[1] + ahead * HDIM), BF16),
         in_specs=[IN_VMEM] * 3,
-        out_specs=pl.BlockSpec((tokens, HDIM), lambda i: (0, i)),
+        out_specs=ANYWHERE,
+        scratch_shapes=[pltpu.VMEM((tokens, ahead * HDIM), BF16), pltpu.SemaphoreType.DMA((ahead + 1,))],
         compiler_params=compiler(VMEM),
         name="place",
     )(pair, row, rest)
+
+
+def hold_kernel(x_ref, *rest):
+    pass
+
+
+def hold(x, after):
+    return pl.pallas_call(
+        hold_kernel,
+        out_shape=jax.ShapeDtypeStruct(x.shape, x.dtype),
+        in_specs=[IN_VMEM] + [ANYWHERE] * len(after),
+        out_specs=IN_VMEM,
+        input_output_aliases={0: 0},
+        compiler_params=compiler(VMEM),
+        name="hold",
+    )(x, *after)
 
 
 def squares_kernel(current_ref, stash_ref, *rest):
@@ -362,6 +380,62 @@
     )(in_hbm(stash), *after)
 
 
+def in_rows(row, size):
+    tokens = row.shape[1]
+    rows = []
+    for _ in range(3):
+        term = row.astype(BF16)
+        row = row - term.astype(F32)
+        rows += [term[:, i : i + size] for i in range(0, tokens, size)]
+    fill = -len(rows) % 16
+    return jnp.concatenate(rows + [jnp.zeros((fill, size), BF16)] * (fill > 0), axis=0)
+
+
+def row_kernel(extra_ref, o_ref):
+    tokens, size = o_ref.shape[1], extra_ref.shape[1]
+    each = tokens // size
+    extra = extra_ref[...].astype(F32)
+    for i in range(each):
+        o_ref[:, i * size : (i + 1) * size] = sum(extra[p * each + i : p * each + i + 1] for p in range(3))
+
+
+def row_from(piece, tokens):
+    extra = piece.shape[0] - tokens
+    size = piece.shape[1]
+    return pl.pallas_call(
+        row_kernel,
+        out_shape=jax.ShapeDtypeStruct((1, tokens), F32),
+        grid=(1,),
+        in_specs=[pl.BlockSpec((extra, size), lambda i: (tokens // extra, 0))],
+        out_specs=pl.BlockSpec((1, tokens), lambda i: (0, 0)),
+        compiler_params=compiler(VMEM),
+        name="row",
+    )(piece)
+
+
+def piece_and_row_kernel(start, stash_ref, t_ref, *rest):
+    out, sem = rest[-2:]
+    tokens, size = stash_ref.shape[2], out.shape[1]
+    copy = pltpu.make_async_copy(stash_ref.at[(0, 1) + lanes_of(start, size)], out.at[:tokens, :], sem.at[0])
+    copy.start()
+    out[tokens:, :] = in_rows(t_ref[2:3, :], size)
+    copy.wait()
+
+
+def piece_and_row(stash, totals, start, size, after):
+    tokens = stash.shape[2]
+    extra = -(-3 * tokens // size // 16) * 16
+    return pl.pallas_call(
+        functools.partial(piece_and_row_kernel, start),
+        out_shape=jax.ShapeDtypeStruct((tokens + extra, size), BF16),
+        in_specs=[IN_HBM, IN_VMEM] + [ANYWHERE] * len(after),
+        out_specs=IN_VMEM,
+        scratch_shapes=[pltpu.SemaphoreType.DMA((1,))],
+        compiler_params=compiler(VMEM),
+        name="piece_and_row",
+    )(in_hbm(stash), totals, *after)
+
+
 def send(x, pairs):
     return lax.ppermute(x, "section", pairs)
 
@@ -373,28 +447,39 @@
     current = layer_input[0]
     tokens, width = current.shape
     count = width // HDIM
-    heads = (max(1, count // 3), count - max(1, count // 3) - max(1, count // 6), max(1, count // 6))
-    sizes = [h * HDIM for h in heads]
-    starts = [sum(sizes[:i]) for i in range(3)]
+    each = max(1, count // 6)
+    pieces = count // each
+    size = each * HDIM
     third = count // 3 * HDIM
 
-    *away, mark = pieces_of(stashed, starts[:2], sizes[:2])
+    *away, mark = pieces_of(stashed, (0, size), (size, size))
     fetched = [send(x, partner) for x in away]
     totals = lax.psum(squares(current, stashed, third, (mark,)), "tensor")
-    held = send(totals, partner)
     output = forward(width_all, current, totals, query_gain, key_gain, third // HDIM)
-    fetched.append(send(pieces_of(stashed, starts[2:], sizes[2:], (fetched[0], held, in_hbm(output)))[0], partner))
-
+
+    def fetch(p, after):
+        away, mark = pieces_of(stashed, (p * size,), (size,), (fetched[p - 2], after))
+        fetched.append(send(away, partner))
+        return mark
+
+    fetched.append(send(piece_and_row(stashed, totals, 2 * size, size, (fetched[0],)), partner))
+    held = row_from(fetched[2], tokens)
+    marks = [fetch(p, in_hbm(output)) for p in range(3, min(5, pieces))]
     share = functools.partial(backward, width_all, eviction, stashed)
     facts = (grad_input, totals, held, query_gain, key_gain)
-    base = starts[1]
+    group = max(1, pieces // 3)
+    base = group * size
     pair, inner = share(
-        fetched[0], *facts, jnp.zeros((1, tokens), F32), heads[0], 0, base, (), (in_hbm(output),)
+        fetched[:group], *facts, jnp.zeros((1, tokens), F32), group * each, 0, base, (), (in_hbm(output), *marks)
     )
-    pair = send(pair, prior)
+    marks = [fetch(p, inner) for p in range(len(fetched), pieces)]
+    pair = send(hold(pair, (fetched[-1],)), prior)
     sofar = ()
-    for h, start, far in zip(heads[1:], starts[1:], fetched[1:]):
-        *sofar, inner = share(far, *facts, inner, h, start, base, tuple(sofar))
+    for first, last in [(group, 2 * group)] + [(p, p + 1) for p in range(2 * group, pieces)]:
+        *sofar, inner = share(
+            fetched[first:last], *facts, inner, (last - first) * each, first * size, base, tuple(sofar), tuple(marks)
+        )
+        marks = []
     inner = lax.psum(inner, "tensor")
     lanes = next(c for c in (2, 1) if (width - base) % (c * HDIM) == 0) * HDIM
     result, row = finish(width_all, eviction, *sofar, totals, held, inner, lanes)

time: 130 us -> 142 us (1.092)
  the two profiles are of different devices: /device:TPU:0 before, /device:TPU:24 now
where the time goes in v15:
time: 142 us; the launch traced here: 141 us
  waiting for transfers between devices  71.3 us (50%)
  Pallas kernels  44.3 us (31%)
  blocking collectives  12.9 us (9%)
  starting transfers between devices  10.4 us (7%)
  between operations  1.61 us (1%)
    ppermute x9, waiting for transfers between devices, send(): return lax.ppermute(x, 'section', pairs)  71.3 us
    pallas_call x4, Pallas kernels, backward(): pl.pallas_call(functools.partial(backward_kernel, first, base, heads, ahe...  21.9 us
    ppermute x9, starting transfers between devices, send(): return lax.ppermute(x, 'section', pairs)  10.4 us
    pallas_call x1, Pallas kernels, forward(): pl.pallas_call(functools.partial(forward_kernel, heads, width_all), out_s...  8.39 us
    psum x1, blocking collectives, local(): inner = lax.psum(inner, 'tensor')  6.63 us
    psum x1, blocking collectives, local(): totals = lax.psum(squares(current, stashed, third, (mark,)), 'tensor')  6.24 us
    pallas_call x1, Pallas kernels, squares(): pl.pallas_call(squares_kernel, out_shape=jax.ShapeDtypeStruct((3, tokens)...  4.74 us
    pallas_call x4, Pallas kernels, pieces_of(): pl.pallas_call(functools.partial(piece_kernel, starts, sizes), out_shape=...  3.94 us
  transfers between devices with their start and end apart: 9, of which 6 were waited for; matrix products, arithmetic and copies ran while one was open for 0% of the time, Pallas kernels for 29%

profile of v15, /device:TPU:24, one launch (start us, length us, event | category | flops | bytes accessed | tf_op | source)
XLA Modules:
  0.0 141.0 jit_solution(11108086584721253395)
XLA Ops:
  0.6 1.1 pieces.4
  1.7 0.0 copy-start.2
  1.7 0.6 copy-done.2
  2.3 0.3 collective-permute-start
  2.6 2.6 %collective-permute-start.2 = (bf16[512,256]{1,0:T(8,128)(2,1)S(1)}, bf16[512,256]{1,0:T(8,128)(2,1)S(1)}, u32[]{:S(2)}, u32[]{:S(2)}) collective-permute-start(bf16[512,256]{1,0:T(8,128)(2,1)S(1)} %get-tuple-element.26), channel_id=1, source_target_pairs={{0,16},{4,20},{8,24},{12,28},{16,0},{20,4},{24,8},{28,12},{1,17},{... | collective-permute-start | bytes 786440 | tf_op jit(solution)/shard_map/ppermute | solution.py:440
  5.2 4.7 %squares.1 = f32[3,512]{1,0:T(4,128)} custom-call(bf16[512,1536]{1,0:T(8,128)(2,1)} %bitcast.4, bf16[1,2,512,1536]{3,2,1,0:T(8,128)(2,1)} %own_ref.7, f32[8,128]{1,0:T(8,128)} %copy-done.2), custom_call_target="tpu_custom_call" | custom-call | tf_op jit(solution)/shard_map/squares/pallas_call | solution.py:342
  10.0 0.0 copy-start
  10.0 0.0 copy-start.1
  10.0 6.2 %psum.14.t_ref = f32[3,512]{1,0:T(4,128)S(1)} all-reduce(f32[3,512]{1,0:T(4,128)} %squares.1), channel_id=1, replica_groups=mesh['section'=8,'tensor'=4] {'tensor'}, use_global_device_ids=true, to_apply=%region_0.0 | all-reduce | flops 1536 | bytes 12288 | tf_op jit(solution)/shard_map/psum | solution.py:457
  16.2 6.2 %collective-permute-done.rest_0_.refs_0_ = bf16[512,256]{1,0:T(8,128)(2,1)S(1)} collective-permute-done((bf16[512,256]{1,0:T(8,128)(2,1)S(1)}, bf16[512,256]{1,0:T(8,128)(2,1)S(1)}, u32[]{:S(2)}, u32[]{:S(2)}) %collective-permute-start) | collective-permute-done | bytes 262176 | tf_op jit(solution)/shard_map/ppermute | solution.py:440
  22.4 1.0 piece_and_row.1
  23.4 0.1 collective-permute-start.1
  23.5 0.0 copy-done
  23.5 0.0 copy-done.1
  23.5 8.4 %forward.1.rest_1_.refs_2_ = bf16[512,1536]{1,0:T(8,128)(2,1)} custom-call(bf16[512,1536]{1,0:T(8,128)(2,1)} %bitcast.5, f32[3,512]{1,0:T(4,128)S(1)} %psum.14.t_ref, f32[1,1536]{1,0:T(1,128)S(1)} %copy-done, f32[1,1536]{1,0:T(1,128)S(1)} %copy-done.1), custom_call_target="tpu_custom_call" | custom-call | tf_op jit(solution)/shard_map/forward/pallas_call | solution.py:119
  31.9 1.9 %collective-permute-done.2.rest_0_.refs_1_ = bf16[512,256]{1,0:T(8,128)(2,1)S(1)} collective-permute-done((bf16[512,256]{1,0:T(8,128)(2,1)S(1)}, bf16[512,256]{1,0:T(8,128)(2,1)S(1)}, u32[]{:S(2)}, u32[]{:S(2)}) %collective-permute-start.2) | collective-permute-done | bytes 262176 | tf_op jit(solution)/shard_map/ppermute | solution.py:440
  33.9 1.0 pieces.5
  34.8 1.0 collective-permute-start.3
  36.5 8.8 %collective-permute-done.1.extra_ref.rest_0_.refs_0_ = bf16[528,256]{1,0:T(8,128)(2,1)S(1)} collective-permute-done((bf16[528,256]{1,0:T(8,128)(2,1)S(1)}, bf16[528,256]{1,0:T(8,128)(2,1)S(1)}, u32[]{:S(2)}, u32[]{:S(2)}) %collective-permute-start.1) | collective-permute-done | bytes 270368 | tf_op jit(solution)/shard_map/ppermute | solution.py:440
  45.3 1.0 pieces.6
  46.3 6.4 %backward.4 = (bf16[512,1024]{1,0:T(8,128)(2,1)S(1)}, f32[1,512]{1,0:T(1,128)S(1)}) custom-call(s32[1]{0:T(128)S(6)} %copy.18.evicted_ref, bf16[1,2,512,1536]{3,2,1,0:T(8,128)(2,1)} %own_ref.7, bf16[1,512,1536]{2,1,0:T(8,128)(2,1)} %g_ref.7, f32[3,512]{1,0:T(4,128)S(1)} %psum.14.t_ref, f32[1,512]{1,0:T(1,128)S(1)} %row.1.held_ref, f32[1,1536]{1,0:T(1,128)S(1)} %copy-done, ...), custom_call_target="tpu_custom_call" | custom-call | tf_op jit(solution)/shard_map/backward/pallas_call | solution.py:230
  52.6 0.0 collective-permute-done.3.rest_0_.refs_1_
  52.7 1.0 pieces.7
  53.6 0.1 collective-permute-start.4
  53.7 2.9 %collective-permute-start.6 = (bf16[512,256]{1,0:T(8,128)(2,1)S(1)}, bf16[512,256]{1,0:T(8,128)(2,1)S(1)}, u32[]{:S(2)}, u32[]{:S(2)}) collective-permute-start(bf16[512,256]{1,0:T(8,128)(2,1)S(1)} %get-tuple-element.35), channel_id=1, source_target_pairs={{0,16},{4,20},{8,24},{12,28},{16,0},{20,4},{24,8},{28,12},{1,17},{... | collective-permute-start | bytes 786440 | tf_op jit(solution)/shard_map/ppermute | solution.py:440
  56.6 6.9 %backward.5 = (f32[512,1024]{1,0:T(8,128)}, bf16[512,1024]{1,0:T(8,128)(2,1)}, f32[1,512]{1,0:T(1,128)S(1)}) custom-call(s32[1]{0:T(128)S(6)} %copy.18.evicted_ref, bf16[1,2,512,1536]{3,2,1,0:T(8,128)(2,1)} %own_ref.7, bf16[1,512,1536]{2,1,0:T(8,128)(2,1)} %g_ref.7, f32[3,512]{1,0:T(4,128)S(1)} %psum.14.t_ref, f32[1,512]{1,0:T(1,128)S(1)} %row.1.held_ref, ...), custom_call_target="tpu_custom_call" | custom-call | tf_op jit(solution)/shard_map/backward/pallas_call | solution.py:230
  63.5 5.7 %collective-permute-done.4.rest_0_.refs_0_ = bf16[512,256]{1,0:T(8,128)(2,1)S(1)} collective-permute-done((bf16[512,256]{1,0:T(8,128)(2,1)S(1)}, bf16[512,256]{1,0:T(8,128)(2,1)S(1)}, u32[]{:S(2)}, u32[]{:S(2)}) %collective-permute-start.4) | collective-permute-done | bytes 262176 | tf_op jit(solution)/shard_map/ppermute | solution.py:440
  69.2 3.2 %collective-permute-start.5 = (bf16[512,1024]{1,0:T(8,128)(2,1)S(1)}, bf16[512,1024]{1,0:T(8,128)(2,1)S(1)}, u32[]{:S(2)}, u32[]{:S(2)}) collective-permute-start(bf16[512,1024]{1,0:T(8,128)(2,1)S(1)} %hold.1), channel_id=1, source_target_pairs={{0,28},{4,0},{8,4},{12,8},{16,12},{20,16},{24,20},{28,24},{1,29},{... | collective-permute-start | bytes 3145736 | tf_op jit(solution)/shard_map/ppermute | solution.py:440
  72.4 24.7 %collective-permute-done.6.refs_0_ = bf16[512,256]{1,0:T(8,128)(2,1)S(1)} collective-permute-done((bf16[512,256]{1,0:T(8,128)(2,1)S(1)}, bf16[512,256]{1,0:T(8,128)(2,1)S(1)}, u32[]{:S(2)}, u32[]{:S(2)}) %collective-permute-start.6) | collective-permute-done | bytes 262176 | tf_op jit(solution)/shard_map/ppermute | solution.py:440
  97.2 4.3 %backward.6 = (f32[512,1024]{1,0:T(8,128)}, bf16[512,1024]{1,0:T(8,128)(2,1)}, f32[1,512]{1,0:T(1,128)S(1)}) custom-call(s32[1]{0:T(128)S(6)} %copy.18.evicted_ref, bf16[1,2,512,1536]{3,2,1,0:T(8,128)(2,1)} %own_ref.7, bf16[1,512,1536]{2,1,0:T(8,128)(2,1)} %g_ref.7, f32[3,512]{1,0:T(4,128)S(1)} %psum.14.t_ref, ...), custom_call_target="tpu_custom_call", output_to_operand_aliasing={{0}: (9, {}), {1}: (10, {})} | custom-call | tf_op jit(solution)/shard_map/backward/pallas_call | solution.py:230
  101.5 4.4 %backward.7 = (f32[512,1024]{1,0:T(8,128)}, bf16[512,1024]{1,0:T(8,128)(2,1)}, f32[1,512]{1,0:T(1,128)S(1)}) custom-call(s32[1]{0:T(128)S(6)} %copy.18.evicted_ref, bf16[1,2,512,1536]{3,2,1,0:T(8,128)(2,1)} %own_ref.7, bf16[1,512,1536]{2,1,0:T(8,128)(2,1)} %g_ref.7, f32[3,512]{1,0:T(4,128)S(1)} %psum.14.t_ref, ...), custom_call_target="tpu_custom_call", output_to_operand_aliasing={{0}: (9, {}), {1}: (10, {})} | custom-call | tf_op jit(solution)/shard_map/backward/pallas_call | solution.py:230
  105.8 6.6 %psum.15.inner_ref = f32[1,512]{1,0:T(1,128)S(1)} all-reduce(f32[1,512]{1,0:T(1,128)S(1)} %get-tuple-element.43), channel_id=1, replica_groups=mesh['section'=8,'tensor'=4] {'tensor'}, use_global_device_ids=true, to_apply=%region_1.0 | all-reduce | flops 512 | bytes 4096 | tf_op jit(solution)/shard_map/psum | solution.py:483
  112.5 3.1 %finish.1 = (bf16[512,1024]{1,0:T(8,128)(2,1)S(1)}, f32[1,512]{1,0:T(1,128)S(1)}) custom-call(s32[1]{0:T(128)S(6)} %copy.18.evicted_ref, f32[512,1024]{1,0:T(8,128)} %get-tuple-element.41.a_ref, bf16[512,1024]{1,0:T(8,128)(2,1)} %get-tuple-element.42.x_ref, f32[3,512]{1,0:T(4,128)S(1)} %psum.14.t_ref, f32[1,512]{1,0:T(1,128)S(1)} %row.1.held_ref, ...), custom_call_target="tpu_custom_call" | custom-call | tf_op jit(solution)/shard_map/finish/pallas_call | solution.py:256
  115.6 0.1 collective-permute-start.8
  115.7 0.1 collective-permute-start.7
  115.8 23.9 %collective-permute-done.7.row_ref = f32[1,512]{1,0:T(1,128)S(1)} collective-permute-done((f32[1,512]{1,0:T(1,128)S(1)}, f32[1,512]{1,0:T(1,128)S(1)}, u32[]{:S(2)}, u32[]{:S(2)}) %collective-permute-start.7) | collective-permute-done | bytes 2080 | tf_op jit(solution)/shard_map/ppermute | solution.py:440
  139.7 0.0 collective-permute-done.5.pair_ref
  139.7 0.0 collective-permute-done.8.rest_ref
  139.7 1.2 place.1
  (3 shorter events, 0.0 us)
Async XLA Ops:
  1.7 0.6 copy-start.2
  2.3 20.2 %collective-permute-start = (bf16[512,256]{1,0:T(8,128)(2,1)S(1)}, bf16[512,256]{1,0:T(8,128)(2,1)S(1)}, u32[]{:S(2)}, u32[]{:S(2)}) collective-permute-start(bf16[512,256]{1,0:T(8,128)(2,1)S(1)} %get-tuple-element.25), channel_id=1, source_target_pairs={{0,16},{4,20},{8,24},{12,28},{16,0},{20,4},{24,8},{28,12},{1,17},{... | collective-permute-start | bytes 786440 | tf_op jit(solution)/shard_map/ppermute | solution.py:440
  2.6 31.2 %collective-permute-start.2 = (bf16[512,256]{1,0:T(8,128)(2,1)S(1)}, bf16[512,256]{1,0:T(8,128)(2,1)S(1)}, u32[]{:S(2)}, u32[]{:S(2)}) collective-permute-start(bf16[512,256]{1,0:T(8,128)(2,1)S(1)} %get-tuple-element.26), channel_id=1, source_target_pairs={{0,16},{4,20},{8,24},{12,28},{16,0},{20,4},{24,8},{28,12},{1,17},{... | collective-permute-start | bytes 786440 | tf_op jit(solution)/shard_map/ppermute | solution.py:440
  10.0 13.5 %copy-start = (f32[1,1536]{1,0:T(1,128)S(1)}, f32[1,1536]{1,0:T(1,128)}, u32[]{:S(2)}) copy-start(f32[1,1536]{1,0:T(1,128)} %gq_ref.9) | copy-start | bytes 18436
  10.0 13.5 %copy-start.1 = (f32[1,1536]{1,0:T(1,128)S(1)}, f32[1,1536]{1,0:T(1,128)}, u32[]{:S(2)}) copy-start(f32[1,1536]{1,0:T(1,128)} %gk_ref.9) | copy-start | bytes 18436
  23.4 21.9 %collective-permute-start.1 = (bf16[528,256]{1,0:T(8,128)(2,1)S(1)}, bf16[528,256]{1,0:T(8,128)(2,1)S(1)}, u32[]{:S(2)}, u32[]{:S(2)}) collective-permute-start(bf16[528,256]{1,0:T(8,128)(2,1)S(1)} %piece_and_row.1), channel_id=1, source_target_pairs={{0,16},{4,20},{8,24},{12,28},{16,0},{20,4},{24,8},{28,12},{1,17},{... | collective-permute-start | bytes 811016 | tf_op jit(solution)/shard_map/ppermute | solution.py:440
  34.8 17.8 %collective-permute-start.3 = (bf16[512,256]{1,0:T(8,128)(2,1)S(1)}, bf16[512,256]{1,0:T(8,128)(2,1)S(1)}, u32[]{:S(2)}, u32[]{:S(2)}) collective-permute-start(bf16[512,256]{1,0:T(8,128)(2,1)S(1)} %get-tuple-element.30), channel_id=1, source_target_pairs={{0,16},{4,20},{8,24},{12,28},{16,0},{20,4},{24,8},{28,12},{1,17},{... | collective-permute-start | bytes 786440 | tf_op jit(solution)/shard_map/ppermute | solution.py:440
  53.6 15.6 %collective-permute-start.4 = (bf16[512,256]{1,0:T(8,128)(2,1)S(1)}, bf16[512,256]{1,0:T(8,128)(2,1)S(1)}, u32[]{:S(2)}, u32[]{:S(2)}) collective-permute-start(bf16[512,256]{1,0:T(8,128)(2,1)S(1)} %get-tuple-element.32), channel_id=1, source_target_pairs={{0,16},{4,20},{8,24},{12,28},{16,0},{20,4},{24,8},{28,12},{1,17},{... | collective-permute-start | bytes 786440 | tf_op jit(solution)/shard_map/ppermute | solution.py:440
  53.7 43.5 %collective-permute-start.6 = (bf16[512,256]{1,0:T(8,128)(2,1)S(1)}, bf16[512,256]{1,0:T(8,128)(2,1)S(1)}, u32[]{:S(2)}, u32[]{:S(2)}) collective-permute-start(bf16[512,256]{1,0:T(8,128)(2,1)S(1)} %get-tuple-element.35), channel_id=1, source_target_pairs={{0,16},{4,20},{8,24},{12,28},{16,0},{20,4},{24,8},{28,12},{1,17},{... | collective-permute-start | bytes 786440 | tf_op jit(solution)/shard_map/ppermute | solution.py:440
  69.2 70.5 %collective-permute-start.5 = (bf16[512,1024]{1,0:T(8,128)(2,1)S(1)}, bf16[512,1024]{1,0:T(8,128)(2,1)S(1)}, u32[]{:S(2)}, u32[]{:S(2)}) collective-permute-start(bf16[512,1024]{1,0:T(8,128)(2,1)S(1)} %hold.1), channel_id=1, source_target_pairs={{0,28},{4,0},{8,4},{12,8},{16,12},{20,16},{24,20},{28,24},{1,29},{... | collective-permute-start | bytes 3145736 | tf_op jit(solution)/shard_map/ppermute | solution.py:440
  115.6 24.1 %collective-permute-start.8 = (bf16[512,1024]{1,0:T(8,128)(2,1)S(1)}, bf16[512,1024]{1,0:T(8,128)(2,1)S(1)}, u32[]{:S(2)}, u32[]{:S(2)}) collective-permute-start(bf16[512,1024]{1,0:T(8,128)(2,1)S(1)} %get-tuple-element.45), channel_id=1, source_target_pairs={{0,28},{4,0},{8,4},{12,8},{16,12},{20,16},{24,20},{28,24},{1,29},{... | collective-permute-start | bytes 3145736 | tf_op jit(solution)/shard_map/ppermute | solution.py:440
  115.7 24.0 %collective-permute-start.7 = (f32[1,512]{1,0:T(1,128)S(1)}, f32[1,512]{1,0:T(1,128)S(1)}, u32[]{:S(2)}, u32[]{:S(2)}) collective-permute-start(f32[1,512]{1,0:T(1,128)S(1)} %get-tuple-element.44), channel_id=1, source_target_pairs={{0,28},{4,0},{8,4},{12,8},{16,12},{20,16},{24,20},{28,24},{1,29},{... | collective-permute-start | bytes 6152 | tf_op jit(solution)/shard_map/ppermute | solution.py:440

commit v16 on v15

--- a/solution.py
+++ b/solution.py
@@ -473,7 +473,7 @@
         fetched[:group], *facts, jnp.zeros((1, tokens), F32), group * each, 0, base, (), (in_hbm(output), *marks)
     )
     marks = [fetch(p, inner) for p in range(len(fetched), pieces)]
-    pair = send(hold(pair, (fetched[-1],)), prior)
+    pair = send(hold(pair, tuple(fetched[-2:])), prior)
     sofar = ()
     for first, last in [(group, 2 * group)] + [(p, p + 1) for p in range(2 * group, pieces)]:
         *sofar, inner = share(

time: 142 us -> 126 us (0.89)
  the two profiles are of different devices: /device:TPU:24 before, /device:TPU:0 now
where the time goes in v16:
time: 126 us
  waiting for transfers between devices  52.4 us (42%)
  Pallas kernels  44.3 us (35%)
  starting transfers between devices  13.6 us (11%)
  blocking collectives  13.3 us (11%)
  between operations  1.61 us (1%)
    ppermute x9, waiting for transfers between devices, send(): return lax.ppermute(x, 'section', pairs)  52.4 us
    pallas_call x4, Pallas kernels, backward(): pl.pallas_call(functools.partial(backward_kernel, first, base, heads, ahe...  21.9 us
    ppermute x9, starting transfers between devices, send(): return lax.ppermute(x, 'section', pairs)  13.6 us
    pallas_call x1, Pallas kernels, forward(): pl.pallas_call(functools.partial(forward_kernel, heads, width_all), out_s...  8.39 us
    psum x1, blocking collectives, local(): inner = lax.psum(inner, 'tensor')  6.78 us
    psum x1, blocking collectives, local(): totals = lax.psum(squares(current, stashed, third, (mark,)), 'tensor')  6.54 us
    pallas_call x1, Pallas kernels, squares(): pl.pallas_call(squares_kernel, out_shape=jax.ShapeDtypeStruct((3, tokens)...  4.74 us
    pallas_call x4, Pallas kernels, pieces_of(): pl.pallas_call(functools.partial(piece_kernel, starts, sizes), out_shape=...  3.94 us
  transfers between devices with their start and end apart: 9, of which 5 were waited for; matrix products, arithmetic and copies ran while one was open for 0% of the time, Pallas kernels for 33%

profile of v16, /device:TPU:0, one launch (start us, length us, event | category | flops | bytes accessed | tf_op | source)
XLA Modules:
  0.0 125.7 jit_solution(360838077694585397)
XLA Ops:
  0.6 1.1 pieces.4
  1.7 0.0 copy-start.2
  1.7 0.6 copy-done.2
  2.3 4.0 %collective-permute-start = (bf16[512,256]{1,0:T(8,128)(2,1)S(1)}, bf16[512,256]{1,0:T(8,128)(2,1)S(1)}, u32[]{:S(2)}, u32[]{:S(2)}) collective-permute-start(bf16[512,256]{1,0:T(8,128)(2,1)S(1)} %get-tuple-element.25), channel_id=1, source_target_pairs={{0,16},{4,20},{8,24},{12,28},{16,0},{20,4},{24,8},{28,12},{1,17},{... | collective-permute-start | bytes 786440 | tf_op jit(solution)/shard_map/ppermute | solution.py:440
  6.3 0.0 collective-permute-start.2
  6.4 4.7 %squares.1 = f32[3,512]{1,0:T(4,128)} custom-call(bf16[512,1536]{1,0:T(8,128)(2,1)} %bitcast.4, bf16[1,2,512,1536]{3,2,1,0:T(8,128)(2,1)} %own_ref.7, f32[8,128]{1,0:T(8,128)} %copy-done.2), custom_call_target="tpu_custom_call" | custom-call | tf_op jit(solution)/shard_map/squares/pallas_call | solution.py:342
  11.1 0.0 copy-start
  11.1 0.0 copy-start.1
  11.1 6.5 %psum.14.t_ref = f32[3,512]{1,0:T(4,128)S(1)} all-reduce(f32[3,512]{1,0:T(4,128)} %squares.1), channel_id=1, replica_groups=mesh['section'=8,'tensor'=4] {'tensor'}, use_global_device_ids=true, to_apply=%region_0.0 | all-reduce | flops 1536 | bytes 12288 | tf_op jit(solution)/shard_map/psum | solution.py:457
  17.7 7.0 %collective-permute-done.rest_0_.refs_0_ = bf16[512,256]{1,0:T(8,128)(2,1)S(1)} collective-permute-done((bf16[512,256]{1,0:T(8,128)(2,1)S(1)}, bf16[512,256]{1,0:T(8,128)(2,1)S(1)}, u32[]{:S(2)}, u32[]{:S(2)}) %collective-permute-start) | collective-permute-done | bytes 262176 | tf_op jit(solution)/shard_map/ppermute | solution.py:440
  24.7 1.0 piece_and_row.1
  25.7 0.1 collective-permute-start.1
  25.7 0.0 copy-done
  25.7 0.0 copy-done.1
  25.8 8.4 %forward.1.rest_1_.refs_2_ = bf16[512,1536]{1,0:T(8,128)(2,1)} custom-call(bf16[512,1536]{1,0:T(8,128)(2,1)} %bitcast.5, f32[3,512]{1,0:T(4,128)S(1)} %psum.14.t_ref, f32[1,1536]{1,0:T(1,128)S(1)} %copy-done, f32[1,1536]{1,0:T(1,128)S(1)} %copy-done.1), custom_call_target="tpu_custom_call" | custom-call | tf_op jit(solution)/shard_map/forward/pallas_call | solution.py:119
  34.1 2.0 %collective-permute-done.2.rest_0_.refs_1_ = bf16[512,256]{1,0:T(8,128)(2,1)S(1)} collective-permute-done((bf16[512,256]{1,0:T(8,128)(2,1)S(1)}, bf16[512,256]{1,0:T(8,128)(2,1)S(1)}, u32[]{:S(2)}, u32[]{:S(2)}) %collective-permute-start.2) | collective-permute-done | bytes 262176 | tf_op jit(solution)/shard_map/ppermute | solution.py:440
  36.1 1.0 pieces.5
  37.1 1.0 collective-permute-start.4
  38.7 8.8 %collective-permute-done.1.extra_ref.rest_0_.refs_0_ = bf16[528,256]{1,0:T(8,128)(2,1)S(1)} collective-permute-done((bf16[528,256]{1,0:T(8,128)(2,1)S(1)}, bf16[528,256]{1,0:T(8,128)(2,1)S(1)}, u32[]{:S(2)}, u32[]{:S(2)}) %collective-permute-start.1) | collective-permute-done | bytes 270368 | tf_op jit(solution)/shard_map/ppermute | solution.py:440
  47.5 1.0 pieces.6
  48.5 0.1 collective-permute-start.3
  48.6 6.4 %backward.4 = (bf16[512,1024]{1,0:T(8,128)(2,1)S(1)}, f32[1,512]{1,0:T(1,128)S(1)}) custom-call(s32[1]{0:T(128)S(6)} %copy.18.evicted_ref, bf16[1,2,512,1536]{3,2,1,0:T(8,128)(2,1)} %own_ref.7, bf16[1,512,1536]{2,1,0:T(8,128)(2,1)} %g_ref.7, f32[3,512]{1,0:T(4,128)S(1)} %psum.14.t_ref, f32[1,512]{1,0:T(1,128)S(1)} %row.1.held_ref, f32[1,1536]{1,0:T(1,128)S(1)} %copy-done, ...), custom_call_target="tpu_custom_call" | custom-call | tf_op jit(solution)/shard_map/backward/pallas_call | solution.py:230
  55.0 0.0 collective-permute-done.4.rest_0_.refs_1_
  55.0 1.0 pieces.7
  55.9 3.0 %collective-permute-start.5 = (bf16[512,256]{1,0:T(8,128)(2,1)S(1)}, bf16[512,256]{1,0:T(8,128)(2,1)S(1)}, u32[]{:S(2)}, u32[]{:S(2)}) collective-permute-start(bf16[512,256]{1,0:T(8,128)(2,1)S(1)} %get-tuple-element.33), channel_id=1, source_target_pairs={{0,16},{4,20},{8,24},{12,28},{16,0},{20,4},{24,8},{28,12},{1,17},{... | collective-permute-start | bytes 786440 | tf_op jit(solution)/shard_map/ppermute | solution.py:440
  59.0 6.9 %backward.5 = (f32[512,1024]{1,0:T(8,128)}, bf16[512,1024]{1,0:T(8,128)(2,1)}, f32[1,512]{1,0:T(1,128)S(1)}) custom-call(s32[1]{0:T(128)S(6)} %copy.18.evicted_ref, bf16[1,2,512,1536]{3,2,1,0:T(8,128)(2,1)} %own_ref.7, bf16[1,512,1536]{2,1,0:T(8,128)(2,1)} %g_ref.7, f32[3,512]{1,0:T(4,128)S(1)} %psum.14.t_ref, f32[1,512]{1,0:T(1,128)S(1)} %row.1.held_ref, ...), custom_call_target="tpu_custom_call" | custom-call | tf_op jit(solution)/shard_map/backward/pallas_call | solution.py:230
  65.9 0.0 collective-permute-done.3.rest_0_.refs_0_
  65.9 8.9 %collective-permute-done.5.rest_1_.refs_0_ = bf16[512,256]{1,0:T(8,128)(2,1)S(1)} collective-permute-done((bf16[512,256]{1,0:T(8,128)(2,1)S(1)}, bf16[512,256]{1,0:T(8,128)(2,1)S(1)}, u32[]{:S(2)}, u32[]{:S(2)}) %collective-permute-start.5) | collective-permute-done | bytes 262176 | tf_op jit(solution)/shard_map/ppermute | solution.py:440
  74.8 4.5 %collective-permute-start.6 = (bf16[512,1024]{1,0:T(8,128)(2,1)S(1)}, bf16[512,1024]{1,0:T(8,128)(2,1)S(1)}, u32[]{:S(2)}, u32[]{:S(2)}) collective-permute-start(bf16[512,1024]{1,0:T(8,128)(2,1)S(1)} %hold.1), channel_id=1, source_target_pairs={{0,28},{4,0},{8,4},{12,8},{16,12},{20,16},{24,20},{28,24},{1,29},{... | collective-permute-start | bytes 3145736 | tf_op jit(solution)/shard_map/ppermute | solution.py:440
  79.3 4.3 %backward.6 = (f32[512,1024]{1,0:T(8,128)}, bf16[512,1024]{1,0:T(8,128)(2,1)}, f32[1,512]{1,0:T(1,128)S(1)}) custom-call(s32[1]{0:T(128)S(6)} %copy.18.evicted_ref, bf16[1,2,512,1536]{3,2,1,0:T(8,128)(2,1)} %own_ref.7, bf16[1,512,1536]{2,1,0:T(8,128)(2,1)} %g_ref.7, f32[3,512]{1,0:T(4,128)S(1)} %psum.14.t_ref, ...), custom_call_target="tpu_custom_call", output_to_operand_aliasing={{0}: (9, {}), {1}: (10, {})} | custom-call | tf_op jit(solution)/shard_map/backward/pallas_call | solution.py:230
  83.6 4.4 %backward.7 = (f32[512,1024]{1,0:T(8,128)}, bf16[512,1024]{1,0:T(8,128)(2,1)}, f32[1,512]{1,0:T(1,128)S(1)}) custom-call(s32[1]{0:T(128)S(6)} %copy.18.evicted_ref, bf16[1,2,512,1536]{3,2,1,0:T(8,128)(2,1)} %own_ref.7, bf16[1,512,1536]{2,1,0:T(8,128)(2,1)} %g_ref.7, f32[3,512]{1,0:T(4,128)S(1)} %psum.14.t_ref, ...), custom_call_target="tpu_custom_call", output_to_operand_aliasing={{0}: (9, {}), {1}: (10, {})} | custom-call | tf_op jit(solution)/shard_map/backward/pallas_call | solution.py:230
  87.9 6.8 %psum.15.inner_ref = f32[1,512]{1,0:T(1,128)S(1)} all-reduce(f32[1,512]{1,0:T(1,128)S(1)} %get-tuple-element.43), channel_id=1, replica_groups=mesh['section'=8,'tensor'=4] {'tensor'}, use_global_device_ids=true, to_apply=%region_1.0 | all-reduce | flops 512 | bytes 4096 | tf_op jit(solution)/shard_map/psum | solution.py:483
  94.7 3.1 %finish.1 = (bf16[512,1024]{1,0:T(8,128)(2,1)S(1)}, f32[1,512]{1,0:T(1,128)S(1)}) custom-call(s32[1]{0:T(128)S(6)} %copy.18.evicted_ref, f32[512,1024]{1,0:T(8,128)} %get-tuple-element.41.a_ref, bf16[512,1024]{1,0:T(8,128)(2,1)} %get-tuple-element.42.x_ref, f32[3,512]{1,0:T(4,128)S(1)} %psum.14.t_ref, f32[1,512]{1,0:T(1,128)S(1)} %row.1.held_ref, ...), custom_call_target="tpu_custom_call" | custom-call | tf_op jit(solution)/shard_map/finish/pallas_call | solution.py:256
  97.9 0.6 collective-permute-start.8
  98.5 0.2 collective-permute-start.7
  98.7 25.7 %collective-permute-done.7.row_ref = f32[1,512]{1,0:T(1,128)S(1)} collective-permute-done((f32[1,512]{1,0:T(1,128)S(1)}, f32[1,512]{1,0:T(1,128)S(1)}, u32[]{:S(2)}, u32[]{:S(2)}) %collective-permute-start.7) | collective-permute-done | bytes 2080 | tf_op jit(solution)/shard_map/ppermute | solution.py:440
  124.4 0.0 collective-permute-done.6.pair_ref
  124.4 0.0 collective-permute-done.8.rest_ref
  124.4 1.2 place.1
  (3 shorter events, 0.0 us)
Async XLA Ops:
  1.7 0.6 copy-start.2
  2.3 22.4 %collective-permute-start = (bf16[512,256]{1,0:T(8,128)(2,1)S(1)}, bf16[512,256]{1,0:T(8,128)(2,1)S(1)}, u32[]{:S(2)}, u32[]{:S(2)}) collective-permute-start(bf16[512,256]{1,0:T(8,128)(2,1)S(1)} %get-tuple-element.25), channel_id=1, source_target_pairs={{0,16},{4,20},{8,24},{12,28},{16,0},{20,4},{24,8},{28,12},{1,17},{... | collective-permute-start | bytes 786440 | tf_op jit(solution)/shard_map/ppermute | solution.py:440
  6.3 29.8 %collective-permute-start.2 = (bf16[512,256]{1,0:T(8,128)(2,1)S(1)}, bf16[512,256]{1,0:T(8,128)(2,1)S(1)}, u32[]{:S(2)}, u32[]{:S(2)}) collective-permute-start(bf16[512,256]{1,0:T(8,128)(2,1)S(1)} %get-tuple-element.26), channel_id=1, source_target_pairs={{0,16},{4,20},{8,24},{12,28},{16,0},{20,4},{24,8},{28,12},{1,17},{... | collective-permute-start | bytes 786440 | tf_op jit(solution)/shard_map/ppermute | solution.py:440
  11.1 14.6 %copy-start = (f32[1,1536]{1,0:T(1,128)S(1)}, f32[1,1536]{1,0:T(1,128)}, u32[]{:S(2)}) copy-start(f32[1,1536]{1,0:T(1,128)} %gq_ref.9) | copy-start | bytes 18436
  11.1 14.6 %copy-start.1 = (f32[1,1536]{1,0:T(1,128)S(1)}, f32[1,1536]{1,0:T(1,128)}, u32[]{:S(2)}) copy-start(f32[1,1536]{1,0:T(1,128)} %gk_ref.9) | copy-start | bytes 18436
  25.7 21.9 %collective-permute-start.1 = (bf16[528,256]{1,0:T(8,128)(2,1)S(1)}, bf16[528,256]{1,0:T(8,128)(2,1)S(1)}, u32[]{:S(2)}, u32[]{:S(2)}) collective-permute-start(bf16[528,256]{1,0:T(8,128)(2,1)S(1)} %piece_and_row.1), channel_id=1, source_target_pairs={{0,16},{4,20},{8,24},{12,28},{16,0},{20,4},{24,8},{28,12},{1,17},{... | collective-permute-start | bytes 811016 | tf_op jit(solution)/shard_map/ppermute | solution.py:440
  37.1 17.9 %collective-permute-start.4 = (bf16[512,256]{1,0:T(8,128)(2,1)S(1)}, bf16[512,256]{1,0:T(8,128)(2,1)S(1)}, u32[]{:S(2)}, u32[]{:S(2)}) collective-permute-start(bf16[512,256]{1,0:T(8,128)(2,1)S(1)} %get-tuple-element.31), channel_id=1, source_target_pairs={{0,16},{4,20},{8,24},{12,28},{16,0},{20,4},{24,8},{28,12},{1,17},{... | collective-permute-start | bytes 786440 | tf_op jit(solution)/shard_map/ppermute | solution.py:440
  48.5 17.4 %collective-permute-start.3 = (bf16[512,256]{1,0:T(8,128)(2,1)S(1)}, bf16[512,256]{1,0:T(8,128)(2,1)S(1)}, u32[]{:S(2)}, u32[]{:S(2)}) collective-permute-start(bf16[512,256]{1,0:T(8,128)(2,1)S(1)} %get-tuple-element.30), channel_id=1, source_target_pairs={{0,16},{4,20},{8,24},{12,28},{16,0},{20,4},{24,8},{28,12},{1,17},{... | collective-permute-start | bytes 786440 | tf_op jit(solution)/shard_map/ppermute | solution.py:440
  55.9 18.8 %collective-permute-start.5 = (bf16[512,256]{1,0:T(8,128)(2,1)S(1)}, bf16[512,256]{1,0:T(8,128)(2,1)S(1)}, u32[]{:S(2)}, u32[]{:S(2)}) collective-permute-start(bf16[512,256]{1,0:T(8,128)(2,1)S(1)} %get-tuple-element.33), channel_id=1, source_target_pairs={{0,16},{4,20},{8,24},{12,28},{16,0},{20,4},{24,8},{28,12},{1,17},{... | collective-permute-start | bytes 786440 | tf_op jit(solution)/shard_map/ppermute | solution.py:440
  74.8 49.6 %collective-permute-start.6 = (bf16[512,1024]{1,0:T(8,128)(2,1)S(1)}, bf16[512,1024]{1,0:T(8,128)(2,1)S(1)}, u32[]{:S(2)}, u32[]{:S(2)}) collective-permute-start(bf16[512,1024]{1,0:T(8,128)(2,1)S(1)} %hold.1), channel_id=1, source_target_pairs={{0,28},{4,0},{8,4},{12,8},{16,12},{20,16},{24,20},{28,24},{1,29},{... | collective-permute-start | bytes 3145736 | tf_op jit(solution)/shard_map/ppermute | solution.py:440
  97.9 26.5 %collective-permute-start.8 = (bf16[512,1024]{1,0:T(8,128)(2,1)S(1)}, bf16[512,1024]{1,0:T(8,128)(2,1)S(1)}, u32[]{:S(2)}, u32[]{:S(2)}) collective-permute-start(bf16[512,1024]{1,0:T(8,128)(2,1)S(1)} %get-tuple-element.45), channel_id=1, source_target_pairs={{0,28},{4,0},{8,4},{12,8},{16,12},{20,16},{24,20},{28,24},{1,29},{... | collective-permute-start | bytes 3145736 | tf_op jit(solution)/shard_map/ppermute | solution.py:440
  98.5 25.9 %collective-permute-start.7 = (f32[1,512]{1,0:T(1,128)S(1)}, f32[1,512]{1,0:T(1,128)S(1)}, u32[]{:S(2)}, u32[]{:S(2)}) collective-permute-start(f32[1,512]{1,0:T(1,128)S(1)} %get-tuple-element.44), channel_id=1, source_target_pairs={{0,28},{4,0},{8,4},{12,8},{16,12},{20,16},{24,20},{28,24},{1,29},{... | collective-permute-start | bytes 6152 | tf_op jit(solution)/shard_map/ppermute | solution.py:440

commit v17 on v16

--- a/solution.py
+++ b/solution.py
@@ -159,20 +159,20 @@
 
 
 def backward_kernel(
-    first, base, heads, ahead, pieces, width_all, evicted_ref, own_ref, g_ref, t_ref, held_ref, gq_ref, gk_ref, past_ref, *refs
+    first, base, found, width_all, evicted_ref, own_ref, g_ref, t_ref, held_ref, gq_ref, gk_ref, past_ref, *refs
 ):
     evicted = evicted_ref[0] == 1
-    far_refs, each = refs[:pieces], heads // pieces
+    heads = len(found)
+    ahead = first < base
     if ahead:
-        pair, inner_ref, xs, gs, x_sem, g_sem = refs[-6:]
+        outs, inner_ref, xs, gs, x_sem, g_sem = refs[-6:]
     else:
         a_out, x_out, inner_ref, xs, gs, outs, x_sem, g_sem, a_sem, out_sem = refs[-10:]
     copies = []
-    for h in range(heads):
+    for h, (p, lane) in enumerate(found):
         to = lanes_of(h * HDIM, HDIM)
         there = lanes_of(first + h * HDIM, HDIM)
-        far_ref = far_refs[h // each].at[: t_ref.shape[1], h % each * HDIM : (h % each + 1) * HDIM]
-        far = pltpu.make_async_copy(far_ref, xs.at[to], x_sem.at[h])
+        far = pltpu.make_async_copy(refs[p].at[: t_ref.shape[1], lane : lane + HDIM], xs.at[to], x_sem.at[h])
         near = pltpu.make_async_copy(own_ref.at[(0, 0) + there], xs.at[to], x_sem.at[h])
         g = pltpu.make_async_copy(g_ref.at[(0,) + there], gs.at[to], g_sem.at[h])
         pl.when(evicted)(far.start)
@@ -191,12 +191,8 @@
         there = lanes_of(first + h * HDIM, HDIM)
         g = gs[mine]
         wide, d_normed = backward_head(xs[mine], g, factor, gq_ref[there], gk_ref[there])
-        term = g.astype(F32) + factor * d_normed
-        if ahead:
-            pair[mine] = term.astype(BF16)
-            pair[lanes_of((heads + h) * HDIM, HDIM)] = xs[mine]
-        else:
-            outs[mine] = term
+        outs[mine] = (g.astype(F32) + factor * d_normed).astype(outs.dtype)
+        if not ahead:
             to = lanes_of(first - base + h * HDIM, HDIM)
             sent.append(pltpu.make_async_copy(outs.at[mine], a_out.at[to], a_sem.at[h]))
             sent.append(pltpu.make_async_copy(xs.at[mine], x_out.at[to], out_sem.at[h]))
@@ -213,26 +209,25 @@
     return jnp.where(evicted_ref[0] == 1, held_ref[...], t_ref[1:2, :])
 
 
-def backward(
-    width_all, evicted, stash, far, g, totals, held, gain_q, gain_k, past, heads, first, base, sofar=(), after=()
-):
+def backward(width_all, evicted, stash, g, totals, held, gain_q, gain_k, past, far, first, base, sofar=(), after=()):
     tokens, width = totals.shape[1], gain_q.shape[1]
-    ahead = first < base
+    found = tuple((p, lane) for p, piece in enumerate(far) for lane in range(0, piece.shape[1], HDIM))
+    heads = len(found)
     small = (tokens, heads * HDIM)
     dma = pltpu.SemaphoreType.DMA((heads,))
     inner = jax.ShapeDtypeStruct((1, tokens), F32)
-    if ahead:
-        shapes = (jax.ShapeDtypeStruct((tokens, 2 * heads * HDIM), BF16), inner)
+    if first < base:
+        shapes = (jax.ShapeDtypeStruct(small, BF16), inner)
         scratch = [pltpu.VMEM(small, BF16)] * 2 + [dma] * 2
     else:
         shapes = (pltpu.HBM((tokens, width - base), F32), pltpu.HBM((tokens, width - base), BF16), inner)
         scratch = [pltpu.VMEM(small, BF16)] * 2 + [pltpu.VMEM(small, F32)] + [dma] * 4
     return pl.pallas_call(
-        functools.partial(backward_kernel, first, base, heads, ahead, len(far), width_all),
+        functools.partial(backward_kernel, first, base, found, width_all),
         out_shape=shapes,
         in_specs=[pl.BlockSpec(memory_space=pltpu.SMEM)] + [ANYWHERE] * 2 + [IN_VMEM] * 5
         + [ANYWHERE] * len(far) + [IN_HBM] * len(sofar) + [ANYWHERE] * len(after),
-        out_specs=(IN_VMEM, IN_VMEM) if ahead else (IN_HBM, IN_HBM, IN_VMEM),
+        out_specs=(IN_VMEM,) * 2 if first < base else (IN_HBM, IN_HBM, IN_VMEM),
         input_output_aliases={8 + len(far): 0, 9 + len(far): 1} if sofar else {},
         scratch_shapes=scratch,
         compiler_params=compiler(VMEM),
@@ -264,35 +259,50 @@
     )(evicted, in_hbm(a), in_hbm(x), totals, held, inner)
 
 
-def place_kernel(ahead, pair_ref, row_ref, rest_ref, o_ref, outs, sems):
-    lanes = ahead * HDIM
-    width = o_ref.shape[1]
-    rest = pltpu.make_async_copy(rest_ref, o_ref.at[lanes_of(lanes, width - lanes)], sems.at[ahead])
-    rest.start()
+def place_ahead_kernel(crossed_ref, a_ref, x_ref, y_ref, row_ref, o_ref, outs, sems):
     row = column_of(row_ref[...])
-    copies = [rest]
-    for h in range(ahead):
+    copies = []
+    for h in range(a_ref.shape[1] // HDIM):
         mine = lanes_of(h * HDIM, HDIM)
-        x = pair_ref[lanes_of(lanes + h * HDIM, HDIM)]
-        outs[mine] = (pair_ref[mine].astype(F32) - x.astype(F32) * row).astype(BF16)
+        x = jnp.where(crossed_ref[0] == 1, y_ref[mine], x_ref[mine])
+        outs[mine] = (a_ref[mine].astype(F32) - x.astype(F32) * row).astype(BF16)
         copies.append(pltpu.make_async_copy(outs.at[mine], o_ref.at[mine], sems.at[h]))
         copies[-1].start()
     for copy in copies:
         copy.wait()
 
 
-def place(pair, row, rest):
-    tokens = rest.shape[0]
-    ahead = pair.shape[1] // HDIM // 2
-    return pl.pallas_call(
-        functools.partial(place_kernel, ahead),
-        out_shape=jax.ShapeDtypeStruct((tokens, rest.shape[1] + ahead * HDIM), BF16),
-        in_specs=[IN_VMEM] * 3,
-        out_specs=ANYWHERE,
-        scratch_shapes=[pltpu.VMEM((tokens, ahead * HDIM), BF16), pltpu.SemaphoreType.DMA((ahead + 1,))],
-        compiler_params=compiler(VMEM),
-        name="place",
-    )(pair, row, rest)
+def place_ahead(crossed, a, x, y, row, width):
+    tokens, lanes = a.shape
+    return pl.pallas_call(
+        place_ahead_kernel,
+        out_shape=pltpu.HBM((tokens, width), BF16),
+        in_specs=[pl.BlockSpec(memory_space=pltpu.SMEM)] + [IN_VMEM] * 4,
+        out_specs=IN_HBM,
+        scratch_shapes=[pltpu.VMEM((tokens, lanes), BF16), pltpu.SemaphoreType.DMA((lanes // HDIM,))],
+        compiler_params=compiler(VMEM),
+        name="place_ahead",
+    )(crossed, a, x, y, row)
+
+
+def place_rest_kernel(rest_ref, front_ref, o_ref, sem):
+    size = rest_ref.shape[1]
+    copy = pltpu.make_async_copy(rest_ref, o_ref.at[lanes_of(o_ref.shape[1] - size, size)], sem.at[0])
+    copy.start()
+    copy.wait()
+
+
+def place_rest(rest, front):
+    return pl.pallas_call(
+        place_rest_kernel,
+        out_shape=pltpu.HBM(front.shape, BF16),
+        in_specs=[IN_VMEM, IN_HBM],
+        out_specs=IN_HBM,
+        input_output_aliases={1: 0},
+        scratch_shapes=[pltpu.SemaphoreType.DMA((1,))],
+        compiler_params=compiler(VMEM),
+        name="place_rest",
+    )(rest, front)
 
 
 def hold_kernel(x_ref, *rest):
@@ -414,7 +424,8 @@
 
 
 def piece_and_row_kernel(start, stash_ref, t_ref, *rest):
-    out, sem = rest[-2:]
+    out, mark, sem = rest[-3:]
+    mark[...] = jnp.zeros_like(mark)
     tokens, size = stash_ref.shape[2], out.shape[1]
     copy = pltpu.make_async_copy(stash_ref.at[(0, 1) + lanes_of(start, size)], out.at[:tokens, :], sem.at[0])
     copy.start()
@@ -427,63 +438,118 @@
     extra = -(-3 * tokens // size // 16) * 16
     return pl.pallas_call(
         functools.partial(piece_and_row_kernel, start),
-        out_shape=jax.ShapeDtypeStruct((tokens + extra, size), BF16),
+        out_shape=(jax.ShapeDtypeStruct((tokens + extra, size), BF16), jax.ShapeDtypeStruct((8, HDIM), F32)),
         in_specs=[IN_HBM, IN_VMEM] + [ANYWHERE] * len(after),
-        out_specs=IN_VMEM,
+        out_specs=(IN_VMEM, IN_VMEM),
         scratch_shapes=[pltpu.SemaphoreType.DMA((1,))],
         compiler_params=compiler(VMEM),
         name="piece_and_row",
     )(in_hbm(stash), totals, *after)
 
 
+def chosen_kernel(n, evicted_ref, own_ref, *refs):
+    far_refs, out, sem = refs[:n], refs[-2], refs[-1]
+    evicted = evicted_ref[0] == 1
+    own = pltpu.make_async_copy(own_ref.at[(0, 0) + lanes_of(0, out.shape[1])], out, sem.at[0])
+    copies, at = [], 0
+    for i, ref in enumerate(far_refs):
+        size = ref.shape[1]
+        copies.append(pltpu.make_async_copy(ref, out.at[lanes_of(at, size)], sem.at[i + 1]))
+        at += size
+
+    @pl.when(evicted)
+    def _():
+        for copy in copies:
+            copy.start()
+        for copy in copies:
+            copy.wait()
+
+    @pl.when(jnp.logical_not(evicted))
+    def _():
+        own.start()
+        own.wait()
+
+
+def chosen_of(evicted, stash, far, after):
+    shape = (stash.shape[2], sum(f.shape[1] for f in far))
+    return pl.pallas_call(
+        functools.partial(chosen_kernel, len(far)),
+        out_shape=jax.ShapeDtypeStruct(shape, BF16),
+        in_specs=[pl.BlockSpec(memory_space=pltpu.SMEM), IN_HBM] + [ANYWHERE] * (len(far) + len(after)),
+        out_specs=IN_VMEM,
+        scratch_shapes=[pltpu.SemaphoreType.DMA((len(far) + 1,))],
+        compiler_params=compiler(VMEM),
+        name="chosen",
+    )(evicted, in_hbm(stash), *far, *after)
+
+
 def send(x, pairs):
     return lax.ppermute(x, "section", pairs)
 
 
 def local(width_all, layer_input, grad_input, stashed, eviction, query_gain, key_gain):
     n = lax.axis_size("section")
-    partner = [(s, (s + n // 2) % n) for s in range(n)]
+    half = n // 2
+    me = lax.axis_index("section")
+    partner = [(s, (s + half) % n) for s in range(n)]
     prior = [(s, (s - 1) % n) for s in range(n)]
+    within = [(s, (s - 1) % half + s // half * half) for s in range(n)]
+    beyond = [(half - 1, n - 1), (n - 1, half - 1)]
+    crossed = jnp.logical_or(me == n - 1, me == half - 1).astype(jnp.int32)[None]
+
     current = layer_input[0]
     tokens, width = current.shape
     count = width // HDIM
-    each = max(1, count // 6)
-    pieces = count // each
-    size = each * HDIM
     third = count // 3 * HDIM
-
-    *away, mark = pieces_of(stashed, (0, size), (size, size))
+    small, large = max(1, count // 6), max(1, count // 3)
+    pieces, at = [(large, small), (0, large)], small + large
+    while count - at > small:
+        pieces.append((at, small))
+        at += small
+    left = count - at
+    pieces += [(at, left // 2), (at + left // 2, left - left // 2)] if left > 1 else [(at, left)]
+    pieces = [(first * HDIM, heads * HDIM) for first, heads in pieces]
+    base = (small + large) * HDIM
+
+    *away, mark = pieces_of(stashed, *zip(*pieces[:2]))
     fetched = [send(x, partner) for x in away]
     totals = lax.psum(squares(current, stashed, third, (mark,)), "tensor")
-    output = forward(width_all, current, totals, query_gain, key_gain, third // HDIM)
 
     def fetch(p, after):
-        away, mark = pieces_of(stashed, (p * size,), (size,), (fetched[p - 2], after))
+        away, mark = pieces_of(stashed, *zip(pieces[p]), (fetched[p - 2], after))
         fetched.append(send(away, partner))
         return mark
 
-    fetched.append(send(piece_and_row(stashed, totals, 2 * size, size, (fetched[0],)), partner))
+    away, mark = piece_and_row(stashed, totals, *pieces[2], (fetched[0],))
+    fetched.append(send(away, partner))
+    output = forward(width_all, current, totals, query_gain, key_gain, third // HDIM, (mark,))
     held = row_from(fetched[2], tokens)
-    marks = [fetch(p, in_hbm(output)) for p in range(3, min(5, pieces))]
-    share = functools.partial(backward, width_all, eviction, stashed)
-    facts = (grad_input, totals, held, query_gain, key_gain)
-    group = max(1, pieces // 3)
-    base = group * size
-    pair, inner = share(
-        fetched[:group], *facts, jnp.zeros((1, tokens), F32), group * each, 0, base, (), (in_hbm(output), *marks)
+    marks = [fetch(p, in_hbm(output)) for p in range(3, min(5, len(pieces)))]
+    share = functools.partial(
+        backward, width_all, eviction, stashed, grad_input, totals, held, query_gain, key_gain
     )
-    marks = [fetch(p, inner) for p in range(len(fetched), pieces)]
-    pair = send(hold(pair, tuple(fetched[-2:])), prior)
-    sofar = ()
-    for first, last in [(group, 2 * group)] + [(p, p + 1) for p in range(2 * group, pieces)]:
+    x = chosen_of(eviction, stashed, [fetched[1], fetched[0]], (in_hbm(output),))
+    x_within = send(x, within)
+    a, inner = share(jnp.zeros((1, tokens), F32), [x], 0, base, (), (in_hbm(output), *marks))
+    marks = [fetch(p, inner) for p in range(len(fetched), len(pieces))]
+
+    split = max(3, len(pieces) - 2)
+    groups = [range(2, split)] + [[p] for p in range(split, len(pieces))]
+    sofar, inners = (), []
+    for group in groups:
         *sofar, inner = share(
-            fetched[first:last], *facts, inner, (last - first) * each, first * size, base, tuple(sofar), tuple(marks)
+            inner, [fetched[p] for p in group], pieces[group[0]][0], base, tuple(sofar), tuple(marks)
         )
+        inners.append(inner)
         marks = []
+    gone = (*fetched[-2:], inners[max(0, len(inners) - 2)])
+    x_beyond = send(hold(x_within, gone), beyond)
+    a = send(hold(a, gone), prior)
     inner = lax.psum(inner, "tensor")
     lanes = next(c for c in (2, 1) if (width - base) % (c * HDIM) == 0) * HDIM
     result, row = finish(width_all, eviction, *sofar, totals, held, inner, lanes)
-    result = place(pair, send(row, prior), send(result, prior))
+    front = place_ahead(crossed, a, x_within, x_beyond, send(row, prior), width)
+    result = place_rest(send(result, prior), front)
     return (output[None], result[None])
 
 

time: 126 us -> 143 us (1.13)
  starting transfers between devices: 13.6 us -> 22 us
  waiting for transfers between devices: 52.4 us -> 57.2 us
  Pallas kernels: 44.3 us -> 48.3 us
    ppermute x9 -> x11, starting transfers between devices: 13.6 us -> 22 us  [send(): return lax.ppermute(x, 'section', pairs)]
    ppermute x9 -> x11, waiting for transfers between devices: 52.4 us -> 57.2 us  [send(): return lax.ppermute(x, 'section', pairs)]
    pallas_call x5 -> x7, Pallas kernels: 23.1 us -> 26.5 us  [the longest x4 21.9 us: backward(): pl.pallas_call(functools.partial(backward_kernel, first, base, found, wid...]
  transfers between devices with their start and end apart: 9 -> 11, of which waited for: 5 -> 3; matrix products, arithmetic and copies ran while one was open for 0% -> 0% of each run, Pallas kernels for 33% -> 32%
where the time goes in v17:
time: 143 us
  waiting for transfers between devices  57.2 us (40%)
  Pallas kernels  48.3 us (34%)
  starting transfers between devices  22 us (15%)
  blocking collectives  12.5 us (9%)
  between operations  1.65 us (1%)
    ppermute x11, waiting for transfers between devices, send(): return lax.ppermute(x, 'section', pairs)  57.2 us
    ppermute x11, starting transfers between devices, send(): return lax.ppermute(x, 'section', pairs)  22 us
    pallas_call x4, Pallas kernels, backward(): pl.pallas_call(functools.partial(backward_kernel, first, base, found, wid...  21.9 us
    pallas_call x1, Pallas kernels, forward(): pl.pallas_call(functools.partial(forward_kernel, heads, width_all), out_s...  8.39 us
    psum x1, blocking collectives, local(): totals = lax.psum(squares(current, stashed, third, (mark,)), 'tensor')  6.53 us
    psum x1, blocking collectives, local(): inner = lax.psum(inner, 'tensor')  5.96 us
    pallas_call x1, Pallas kernels, squares(): pl.pallas_call(squares_kernel, out_shape=jax.ShapeDtypeStruct((3, tokens)...  4.75 us
    pallas_call x4, Pallas kernels, pieces_of(): pl.pallas_call(functools.partial(piece_kernel, starts, sizes), out_shape=...  3.94 us
  transfers between devices with their start and end apart: 11, of which 3 were waited for; matrix products, arithmetic and copies ran while one was open for 0% of the time, Pallas kernels for 32%

profile of v17, /device:TPU:0, one launch (start us, length us, event | category | flops | bytes accessed | tf_op | source)
XLA Modules:
  0.0 142.8 jit_solution(7783091376416901723)
XLA Ops:
  0.6 1.1 pieces.4
  1.8 0.0 copy-start.3
  1.8 0.6 copy-done.3
  2.4 4.0 %collective-permute-start.2 = (bf16[512,512]{1,0:T(8,128)(2,1)S(1)}, bf16[512,512]{1,0:T(8,128)(2,1)S(1)}, u32[]{:S(2)}, u32[]{:S(2)}) collective-permute-start(bf16[512,512]{1,0:T(8,128)(2,1)S(1)} %get-tuple-element.30), channel_id=1, source_target_pairs={{0,16},{4,20},{8,24},{12,28},{16,0},{20,4},{24,8},{28,12},{1,17},{... | collective-permute-start | bytes 1572872 | tf_op jit(solution)/shard_map/ppermute | solution.py:487
  6.4 0.0 collective-permute-start
  7.1 4.8 %squares.1 = f32[3,512]{1,0:T(4,128)} custom-call(bf16[512,1536]{1,0:T(8,128)(2,1)} %bitcast.5, bf16[1,2,512,1536]{3,2,1,0:T(8,128)(2,1)} %own_ref.9, f32[8,128]{1,0:T(8,128)} %copy-done.3), custom_call_target="tpu_custom_call" | custom-call | tf_op jit(solution)/shard_map/squares/pallas_call | solution.py:352
  11.9 6.5 %psum.14.t_ref = f32[3,512]{1,0:T(4,128)S(1)} all-reduce(f32[3,512]{1,0:T(4,128)} %squares.1), channel_id=1, replica_groups=mesh['section'=8,'tensor'=4] {'tensor'}, use_global_device_ids=true, to_apply=%region_0.0 | all-reduce | flops 1536 | bytes 12288 | tf_op jit(solution)/shard_map/psum | solution.py:516
  18.4 0.0 copy-start
  18.4 0.0 copy-start.1
  18.4 22.4 %collective-permute-done.rest_0_.refs_1_ = bf16[512,256]{1,0:T(8,128)(2,1)S(1)} collective-permute-done((bf16[512,256]{1,0:T(8,128)(2,1)S(1)}, bf16[512,256]{1,0:T(8,128)(2,1)S(1)}, u32[]{:S(2)}, u32[]{:S(2)}) %collective-permute-start) | collective-permute-done | bytes 262176 | tf_op jit(solution)/shard_map/ppermute | solution.py:487
  40.8 1.0 piece_and_row.1
  41.8 0.0 copy-start.2
  41.8 0.6 copy-done.2
  42.4 0.0 copy-done
  42.4 0.0 copy-done.1
  42.4 8.4 %forward.1.refs_2_.rest_1_.refs_1_ = bf16[512,1536]{1,0:T(8,128)(2,1)} custom-call(bf16[512,1536]{1,0:T(8,128)(2,1)} %bitcast.6, f32[3,512]{1,0:T(4,128)S(1)} %psum.14.t_ref, f32[1,1536]{1,0:T(1,128)S(1)} %copy-done, f32[1,1536]{1,0:T(1,128)S(1)} %copy-done.1, f32[8,128]{1,0:T(8,128)} %copy-done.2), custom_call_target="tpu_custom_call" | custom-call | tf_op jit(solution)/shard_map/forward/pallas_call | solution.py:119
  50.8 0.0 collective-permute-done.2.refs_0_.rest_0_
  50.8 0.1 chosen.1.refs_0_
  50.9 1.7 %collective-permute-start.8 = (bf16[512,768]{1,0:T(8,128)(2,1)S(1)}, bf16[512,768]{1,0:T(8,128)(2,1)S(1)}, u32[]{:S(2)}, u32[]{:S(2)}) collective-permute-start(bf16[512,768]{1,0:T(8,128)(2,1)S(1)} %chosen.1.refs_0_), channel_id=1, source_target_pairs={{0,12},{4,0},{8,4},{12,8},{16,28},{20,16},{24,20},{28,24},{1,13},{... | collective-permute-start | bytes 2359304 | tf_op jit(solution)/shard_map/ppermute | solution.py:487
  52.6 4.5 %collective-permute-start.1 = (bf16[528,256]{1,0:T(8,128)(2,1)S(1)}, bf16[528,256]{1,0:T(8,128)(2,1)S(1)}, u32[]{:S(2)}, u32[]{:S(2)}) collective-permute-start(bf16[528,256]{1,0:T(8,128)(2,1)S(1)} %get-tuple-element.29), channel_id=1, source_target_pairs={{0,16},{4,20},{8,24},{12,28},{16,0},{20,4},{24,8},{28,12},{1,17},{... | collective-permute-start | bytes 811016 | tf_op jit(solution)/shard_map/ppermute | solution.py:487
  57.0 1.0 pieces.5
  58.0 0.1 collective-permute-start.3
  58.1 18.2 %collective-permute-done.1.extra_ref.rest_0_.refs_0_ = bf16[528,256]{1,0:T(8,128)(2,1)S(1)} collective-permute-done((bf16[528,256]{1,0:T(8,128)(2,1)S(1)}, bf16[528,256]{1,0:T(8,128)(2,1)S(1)}, u32[]{:S(2)}, u32[]{:S(2)}) %collective-permute-start.1) | collective-permute-done | bytes 270368 | tf_op jit(solution)/shard_map/ppermute | solution.py:487
  76.3 0.9 pieces.6
  77.2 3.4 %collective-permute-start.4 = (bf16[512,128]{1,0:T(8,128)(2,1)S(1)}, bf16[512,128]{1,0:T(8,128)(2,1)S(1)}, u32[]{:S(2)}, u32[]{:S(2)}) collective-permute-start(bf16[512,128]{1,0:T(8,128)(2,1)S(1)} %get-tuple-element.37), channel_id=1, source_target_pairs={{0,16},{4,20},{8,24},{12,28},{16,0},{20,4},{24,8},{28,12},{1,17},{... | collective-permute-start | bytes 393224 | tf_op jit(solution)/shard_map/ppermute | solution.py:487
  80.7 8.8 %backward.4 = (bf16[512,768]{1,0:T(8,128)(2,1)S(1)}, f32[1,512]{1,0:T(1,128)S(1)}) custom-call(s32[1]{0:T(128)S(6)} %copy.22.evicted_ref, bf16[1,2,512,1536]{3,2,1,0:T(8,128)(2,1)} %own_ref.9, bf16[1,512,1536]{2,1,0:T(8,128)(2,1)} %g_ref.7, f32[3,512]{1,0:T(4,128)S(1)} %psum.14.t_ref, f32[1,512]{1,0:T(1,128)S(1)} %row.1.held_ref, f32[1,1536]{1,0:T(1,128)S(1)} %copy-done, ...), custom_call_target="tpu_custom_call" | custom-call | tf_op jit(solution)/shard_map/backward/pallas_call | solution.py:225
  89.5 0.0 collective-permute-done.3.rest_0_.refs_1_
  89.5 0.9 pieces.7
  90.4 0.1 collective-permute-start.5
  90.5 6.9 %backward.5 = (f32[512,768]{1,0:T(8,128)}, bf16[512,768]{1,0:T(8,128)(2,1)}, f32[1,512]{1,0:T(1,128)S(1)}) custom-call(s32[1]{0:T(128)S(6)} %copy.22.evicted_ref, bf16[1,2,512,1536]{3,2,1,0:T(8,128)(2,1)} %own_ref.9, bf16[1,512,1536]{2,1,0:T(8,128)(2,1)} %g_ref.7, f32[3,512]{1,0:T(4,128)S(1)} %psum.14.t_ref, f32[1,512]{1,0:T(1,128)S(1)} %row.1.held_ref, ...), custom_call_target="tpu_custom_call" | custom-call | tf_op jit(solution)/shard_map/backward/pallas_call | solution.py:225
  97.4 0.0 collective-permute-done.4.refs_0_.rest_0_
  97.4 3.1 %backward.6 = (f32[512,768]{1,0:T(8,128)}, bf16[512,768]{1,0:T(8,128)(2,1)}, f32[1,512]{1,0:T(1,128)S(1)}) custom-call(s32[1]{0:T(128)S(6)} %copy.22.evicted_ref, bf16[1,2,512,1536]{3,2,1,0:T(8,128)(2,1)} %own_ref.9, bf16[1,512,1536]{2,1,0:T(8,128)(2,1)} %g_ref.7, f32[3,512]{1,0:T(4,128)S(1)} %psum.14.t_ref, ...), custom_call_target="tpu_custom_call", output_to_operand_aliasing={{0}: (9, {}), {1}: (10, {})} | custom-call | tf_op jit(solution)/shard_map/backward/pallas_call | solution.py:225
  100.5 0.0 collective-permute-done.5.refs_0_.rest_1_
  100.5 0.1 collective-permute-start.7
  100.6 3.1 %backward.7 = (f32[512,768]{1,0:T(8,128)}, bf16[512,768]{1,0:T(8,128)(2,1)}, f32[1,512]{1,0:T(1,128)S(1)}) custom-call(s32[1]{0:T(128)S(6)} %copy.22.evicted_ref, bf16[1,2,512,1536]{3,2,1,0:T(8,128)(2,1)} %own_ref.9, bf16[1,512,1536]{2,1,0:T(8,128)(2,1)} %g_ref.7, f32[3,512]{1,0:T(4,128)S(1)} %psum.14.t_ref, ...), custom_call_target="tpu_custom_call", output_to_operand_aliasing={{0}: (9, {}), {1}: (10, {})} | custom-call | tf_op jit(solution)/shard_map/backward/pallas_call | solution.py:225
  103.8 6.0 %psum.15.inner_ref = f32[1,512]{1,0:T(1,128)S(1)} all-reduce(f32[1,512]{1,0:T(1,128)S(1)} %get-tuple-element.46), channel_id=1, replica_groups=mesh['section'=8,'tensor'=4] {'tensor'}, use_global_device_ids=true, to_apply=%region_1.0 | all-reduce | flops 512 | bytes 4096 | tf_op jit(solution)/shard_map/psum | solution.py:548
  109.7 0.0 collective-permute-done.8.x_ref
  109.7 0.1 copy.20.x_ref
  109.8 1.6 %collective-permute-start.9 = (bf16[512,768]{1,0:T(8,128)(2,1)S(1)}, bf16[512,768]{1,0:T(8,128)(2,1)}, u32[]{:S(2)}, u32[]{:S(2)}) collective-permute-start(bf16[512,768]{1,0:T(8,128)(2,1)S(1)} %hold.3), channel_id=1, source_target_pairs={{12,28},{28,12},{13,29},{29,13},{14,30},{30,14},{15,31},{31,15}} | collective-permute-start | bytes 2359304 | tf_op jit(solution)/shard_map/ppermute | solution.py:487
  111.3 3.7 %finish.1 = (bf16[512,768]{1,0:T(8,128)(2,1)}, f32[1,512]{1,0:T(1,128)S(1)}) custom-call(s32[1]{0:T(128)S(6)} %copy.22.evicted_ref, f32[512,768]{1,0:T(8,128)} %get-tuple-element.44.a_ref, bf16[512,768]{1,0:T(8,128)(2,1)} %get-tuple-element.45.x_ref, f32[3,512]{1,0:T(4,128)S(1)} %psum.14.t_ref, f32[1,512]{1,0:T(1,128)S(1)} %row.1.held_ref, ...), custom_call_target="tpu_custom_call" | custom-call | tf_op jit(solution)/shard_map/finish/pallas_call | solution.py:251
  115.0 6.5 %collective-permute-start.6 = (bf16[512,768]{1,0:T(8,128)(2,1)}, bf16[512,768]{1,0:T(8,128)(2,1)}, u32[]{:S(2)}, u32[]{:S(2)}) collective-permute-start(bf16[512,768]{1,0:T(8,128)(2,1)} %get-tuple-element.47), channel_id=1, source_target_pairs={{0,28},{4,0},{8,4},{12,8},{16,12},{20,16},{24,20},{28,24},{1,29},{... | collective-permute-start | bytes 2359304 | tf_op jit(solution)/shard_map/ppermute | solution.py:487
  121.5 0.0 collective-permute-start.10
  121.5 16.6 %collective-permute-done.10.row_ref = f32[1,512]{1,0:T(1,128)S(1)} collective-permute-done((f32[1,512]{1,0:T(1,128)S(1)}, f32[1,512]{1,0:T(1,128)S(1)}, u32[]{:S(2)}, u32[]{:S(2)}) %collective-permute-start.10) | collective-permute-done | bytes 2080 | tf_op jit(solution)/shard_map/ppermute | solution.py:487
  138.1 0.0 collective-permute-done.7.a_ref
  138.1 0.0 collective-permute-done.9.y_ref
  138.1 2.5 %place_ahead.1.front_ref = bf16[512,1536]{1,0:T(8,128)(2,1)} custom-call(s32[1]{0:T(128)} %bitcast.2.crossed_ref, bf16[512,768]{1,0:T(8,128)(2,1)S(1)} %collective-permute-done.7.a_ref, bf16[512,768]{1,0:T(8,128)(2,1)S(1)} %collective-permute-done.8.x_ref, bf16[512,768]{1,0:T(8,128)(2,1)} %collective-permute-done.9.y_ref, ...), custom_call_target="tpu_custom_call" | custom-call | tf_op jit(solution)/shard_map/place_ahead/pallas_call | solution.py:277
  140.6 0.0 collective-permute-done.6.rest_ref
  140.6 2.0 %place_rest.1 = bf16[512,1536]{1,0:T(8,128)(2,1)} custom-call(bf16[512,768]{1,0:T(8,128)(2,1)} %collective-permute-done.6.rest_ref, bf16[512,1536]{1,0:T(8,128)(2,1)} %place_ahead.1.front_ref), custom_call_target="tpu_custom_call", output_to_operand_aliasing={{}: (1, {})} | custom-call | tf_op jit(solution)/shard_map/place_rest/pallas_call | solution.py:296
  (4 shorter events, 0.0 us)
Async XLA Ops:
  1.8 0.6 copy-start.3
  2.4 48.4 %collective-permute-start.2 = (bf16[512,512]{1,0:T(8,128)(2,1)S(1)}, bf16[512,512]{1,0:T(8,128)(2,1)S(1)}, u32[]{:S(2)}, u32[]{:S(2)}) collective-permute-start(bf16[512,512]{1,0:T(8,128)(2,1)S(1)} %get-tuple-element.30), channel_id=1, source_target_pairs={{0,16},{4,20},{8,24},{12,28},{16,0},{20,4},{24,8},{28,12},{1,17},{... | collective-permute-start | bytes 1572872 | tf_op jit(solution)/shard_map/ppermute | solution.py:487
  6.4 34.4 %collective-permute-start = (bf16[512,256]{1,0:T(8,128)(2,1)S(1)}, bf16[512,256]{1,0:T(8,128)(2,1)S(1)}, u32[]{:S(2)}, u32[]{:S(2)}) collective-permute-start(bf16[512,256]{1,0:T(8,128)(2,1)S(1)} %get-tuple-element.27), channel_id=1, source_target_pairs={{0,16},{4,20},{8,24},{12,28},{16,0},{20,4},{24,8},{28,12},{1,17},{... | collective-permute-start | bytes 786440 | tf_op jit(solution)/shard_map/ppermute | solution.py:487
  18.4 24.0 %copy-start = (f32[1,1536]{1,0:T(1,128)S(1)}, f32[1,1536]{1,0:T(1,128)}, u32[]{:S(2)}) copy-start(f32[1,1536]{1,0:T(1,128)} %gq_ref.9) | copy-start | bytes 18436
  18.4 24.0 %copy-start.1 = (f32[1,1536]{1,0:T(1,128)S(1)}, f32[1,1536]{1,0:T(1,128)}, u32[]{:S(2)}) copy-start(f32[1,1536]{1,0:T(1,128)} %gk_ref.9) | copy-start | bytes 18436
  41.8 0.6 copy-start.2
  50.9 58.9 %collective-permute-start.8 = (bf16[512,768]{1,0:T(8,128)(2,1)S(1)}, bf16[512,768]{1,0:T(8,128)(2,1)S(1)}, u32[]{:S(2)}, u32[]{:S(2)}) collective-permute-start(bf16[512,768]{1,0:T(8,128)(2,1)S(1)} %chosen.1.refs_0_), channel_id=1, source_target_pairs={{0,12},{4,0},{8,4},{12,8},{16,28},{20,16},{24,20},{28,24},{1,13},{... | collective-permute-start | bytes 2359304 | tf_op jit(solution)/shard_map/ppermute | solution.py:487
  52.6 23.7 %collective-permute-start.1 = (bf16[528,256]{1,0:T(8,128)(2,1)S(1)}, bf16[528,256]{1,0:T(8,128)(2,1)S(1)}, u32[]{:S(2)}, u32[]{:S(2)}) collective-permute-start(bf16[528,256]{1,0:T(8,128)(2,1)S(1)} %get-tuple-element.29), channel_id=1, source_target_pairs={{0,16},{4,20},{8,24},{12,28},{16,0},{20,4},{24,8},{28,12},{1,17},{... | collective-permute-start | bytes 811016 | tf_op jit(solution)/shard_map/ppermute | solution.py:487
  58.0 31.5 %collective-permute-start.3 = (bf16[512,256]{1,0:T(8,128)(2,1)S(1)}, bf16[512,256]{1,0:T(8,128)(2,1)S(1)}, u32[]{:S(2)}, u32[]{:S(2)}) collective-permute-start(bf16[512,256]{1,0:T(8,128)(2,1)S(1)} %get-tuple-element.34), channel_id=1, source_target_pairs={{0,16},{4,20},{8,24},{12,28},{16,0},{20,4},{24,8},{28,12},{1,17},{... | collective-permute-start | bytes 786440 | tf_op jit(solution)/shard_map/ppermute | solution.py:487
  77.2 20.2 %collective-permute-start.4 = (bf16[512,128]{1,0:T(8,128)(2,1)S(1)}, bf16[512,128]{1,0:T(8,128)(2,1)S(1)}, u32[]{:S(2)}, u32[]{:S(2)}) collective-permute-start(bf16[512,128]{1,0:T(8,128)(2,1)S(1)} %get-tuple-element.37), channel_id=1, source_target_pairs={{0,16},{4,20},{8,24},{12,28},{16,0},{20,4},{24,8},{28,12},{1,17},{... | collective-permute-start | bytes 393224 | tf_op jit(solution)/shard_map/ppermute | solution.py:487
  90.4 10.1 %collective-permute-start.5 = (bf16[512,128]{1,0:T(8,128)(2,1)S(1)}, bf16[512,128]{1,0:T(8,128)(2,1)S(1)}, u32[]{:S(2)}, u32[]{:S(2)}) collective-permute-start(bf16[512,128]{1,0:T(8,128)(2,1)S(1)} %get-tuple-element.41), channel_id=1, source_target_pairs={{0,16},{4,20},{8,24},{12,28},{16,0},{20,4},{24,8},{28,12},{1,17},{... | collective-permute-start | bytes 393224 | tf_op jit(solution)/shard_map/ppermute | solution.py:487
  100.5 37.6 %collective-permute-start.7 = (bf16[512,768]{1,0:T(8,128)(2,1)S(1)}, bf16[512,768]{1,0:T(8,128)(2,1)S(1)}, u32[]{:S(2)}, u32[]{:S(2)}) collective-permute-start(bf16[512,768]{1,0:T(8,128)(2,1)S(1)} %hold.2), channel_id=1, source_target_pairs={{0,28},{4,0},{8,4},{12,8},{16,12},{20,16},{24,20},{28,24},{1,29},{... | collective-permute-start | bytes 2359304 | tf_op jit(solution)/shard_map/ppermute | solution.py:487
  109.8 28.3 %collective-permute-start.9 = (bf16[512,768]{1,0:T(8,128)(2,1)S(1)}, bf16[512,768]{1,0:T(8,128)(2,1)}, u32[]{:S(2)}, u32[]{:S(2)}) collective-permute-start(bf16[512,768]{1,0:T(8,128)(2,1)S(1)} %hold.3), channel_id=1, source_target_pairs={{12,28},{28,12},{13,29},{29,13},{14,30},{30,14},{15,31},{31,15}} | collective-permute-start | bytes 2359304 | tf_op jit(solution)/shard_map/ppermute | solution.py:487
  115.0 25.6 %collective-permute-start.6 = (bf16[512,768]{1,0:T(8,128)(2,1)}, bf16[512,768]{1,0:T(8,128)(2,1)}, u32[]{:S(2)}, u32[]{:S(2)}) collective-permute-start(bf16[512,768]{1,0:T(8,128)(2,1)} %get-tuple-element.47), channel_id=1, source_target_pairs={{0,28},{4,0},{8,4},{12,8},{16,12},{20,16},{24,20},{28,24},{1,29},{... | collective-permute-start | bytes 2359304 | tf_op jit(solution)/shard_map/ppermute | solution.py:487
  121.5 16.6 %collective-permute-start.10 = (f32[1,512]{1,0:T(1,128)S(1)}, f32[1,512]{1,0:T(1,128)S(1)}, u32[]{:S(2)}, u32[]{:S(2)}) collective-permute-start(f32[1,512]{1,0:T(1,128)S(1)} %get-tuple-element.49), channel_id=1, source_target_pairs={{0,28},{4,0},{8,4},{12,8},{16,12},{20,16},{24,20},{28,24},{1,29},{... | collective-permute-start | bytes 6152 | tf_op jit(solution)/shard_map/ppermute | solution.py:487

commit v18 on v16

--- a/solution.py
+++ b/solution.py
@@ -159,20 +159,20 @@
 
 
 def backward_kernel(
-    first, base, heads, ahead, pieces, width_all, evicted_ref, own_ref, g_ref, t_ref, held_ref, gq_ref, gk_ref, past_ref, *refs
+    first, base, found, width_all, evicted_ref, own_ref, g_ref, t_ref, held_ref, gq_ref, gk_ref, past_ref, *refs
 ):
     evicted = evicted_ref[0] == 1
-    far_refs, each = refs[:pieces], heads // pieces
+    heads = len(found)
+    ahead = first < base
     if ahead:
-        pair, inner_ref, xs, gs, x_sem, g_sem = refs[-6:]
+        outs, inner_ref, xs, gs, x_sem, g_sem = refs[-6:]
     else:
         a_out, x_out, inner_ref, xs, gs, outs, x_sem, g_sem, a_sem, out_sem = refs[-10:]
     copies = []
-    for h in range(heads):
+    for h, (p, lane) in enumerate(found):
         to = lanes_of(h * HDIM, HDIM)
         there = lanes_of(first + h * HDIM, HDIM)
-        far_ref = far_refs[h // each].at[: t_ref.shape[1], h % each * HDIM : (h % each + 1) * HDIM]
-        far = pltpu.make_async_copy(far_ref, xs.at[to], x_sem.at[h])
+        far = pltpu.make_async_copy(refs[p].at[: t_ref.shape[1], lane : lane + HDIM], xs.at[to], x_sem.at[h])
         near = pltpu.make_async_copy(own_ref.at[(0, 0) + there], xs.at[to], x_sem.at[h])
         g = pltpu.make_async_copy(g_ref.at[(0,) + there], gs.at[to], g_sem.at[h])
         pl.when(evicted)(far.start)
@@ -193,8 +193,8 @@
         wide, d_normed = backward_head(xs[mine], g, factor, gq_ref[there], gk_ref[there])
         term = g.astype(F32) + factor * d_normed
         if ahead:
-            pair[mine] = term.astype(BF16)
-            pair[lanes_of((heads + h) * HDIM, HDIM)] = xs[mine]
+            outs[mine] = term.astype(BF16)
+            outs[lanes_of((heads + h) * HDIM, HDIM)] = xs[mine]
         else:
             outs[mine] = term
             to = lanes_of(first - base + h * HDIM, HDIM)
@@ -214,25 +214,25 @@
 
 
 def backward(
-    width_all, evicted, stash, far, g, totals, held, gain_q, gain_k, past, heads, first, base, sofar=(), after=()
+    width_all, evicted, stash, g, totals, held, gain_q, gain_k, past, far, found, first, base, sofar=(), after=()
 ):
     tokens, width = totals.shape[1], gain_q.shape[1]
-    ahead = first < base
+    heads = len(found)
     small = (tokens, heads * HDIM)
     dma = pltpu.SemaphoreType.DMA((heads,))
     inner = jax.ShapeDtypeStruct((1, tokens), F32)
-    if ahead:
+    if first < base:
         shapes = (jax.ShapeDtypeStruct((tokens, 2 * heads * HDIM), BF16), inner)
         scratch = [pltpu.VMEM(small, BF16)] * 2 + [dma] * 2
     else:
         shapes = (pltpu.HBM((tokens, width - base), F32), pltpu.HBM((tokens, width - base), BF16), inner)
         scratch = [pltpu.VMEM(small, BF16)] * 2 + [pltpu.VMEM(small, F32)] + [dma] * 4
     return pl.pallas_call(
-        functools.partial(backward_kernel, first, base, heads, ahead, len(far), width_all),
+        functools.partial(backward_kernel, first, base, found, width_all),
         out_shape=shapes,
         in_specs=[pl.BlockSpec(memory_space=pltpu.SMEM)] + [ANYWHERE] * 2 + [IN_VMEM] * 5
         + [ANYWHERE] * len(far) + [IN_HBM] * len(sofar) + [ANYWHERE] * len(after),
-        out_specs=(IN_VMEM, IN_VMEM) if ahead else (IN_HBM, IN_HBM, IN_VMEM),
+        out_specs=(IN_VMEM,) * 2 if first < base else (IN_HBM, IN_HBM, IN_VMEM),
         input_output_aliases={8 + len(far): 0, 9 + len(far): 1} if sofar else {},
         scratch_shapes=scratch,
         compiler_params=compiler(VMEM),
@@ -250,27 +250,31 @@
     o_ref[...] = (a_ref[...] - x_ref[...].astype(F32) * column_of(row)).astype(BF16)
 
 
-def finish(width_all, evicted, a, x, totals, held, inner, lanes):
-    tokens, width = a.shape
-    block = pl.BlockSpec((tokens, lanes), lambda i: (0, i))
+def finish(width_all, evicted, a, x, totals, held, inner, first, last):
+    tokens = a.shape[0]
+    lanes = HDIM
+    block = pl.BlockSpec((tokens, lanes), lambda i: (0, first // lanes + i))
     return pl.pallas_call(
         functools.partial(finish_kernel, width_all),
-        out_shape=(jax.ShapeDtypeStruct(a.shape, BF16), jax.ShapeDtypeStruct((1, tokens), F32)),
-        grid=(width // lanes,),
+        out_shape=(jax.ShapeDtypeStruct((tokens, last - first), BF16), jax.ShapeDtypeStruct((1, tokens), F32)),
+        grid=((last - first) // lanes,),
         in_specs=[pl.BlockSpec(memory_space=pltpu.SMEM), block, block] + [IN_VMEM] * 3,
-        out_specs=(block, pl.BlockSpec((1, tokens), lambda i: (0, 0))),
+        out_specs=(pl.BlockSpec((tokens, lanes), lambda i: (0, i)), pl.BlockSpec((1, tokens), lambda i: (0, 0))),
         compiler_params=compiler(VMEM),
         name="finish",
     )(evicted, in_hbm(a), in_hbm(x), totals, held, inner)
 
 
-def place_kernel(ahead, pair_ref, row_ref, rest_ref, o_ref, outs, sems):
-    lanes = ahead * HDIM
-    width = o_ref.shape[1]
-    rest = pltpu.make_async_copy(rest_ref, o_ref.at[lanes_of(lanes, width - lanes)], sems.at[ahead])
-    rest.start()
+def place_kernel(pair_ref, row_ref, *refs):
+    rest_refs, (o_ref, outs, sems) = refs[:-3], refs[-3:]
+    lanes = outs.shape[1]
+    ahead = lanes // HDIM
+    copies, at = [], lanes
+    for i, ref in enumerate(rest_refs):
+        copies.append(pltpu.make_async_copy(ref, o_ref.at[lanes_of(at, ref.shape[1])], sems.at[ahead + i]))
+        copies[-1].start()
+        at += ref.shape[1]
     row = column_of(row_ref[...])
-    copies = [rest]
     for h in range(ahead):
         mine = lanes_of(h * HDIM, HDIM)
         x = pair_ref[lanes_of(lanes + h * HDIM, HDIM)]
@@ -281,18 +285,17 @@
         copy.wait()
 
 
-def place(pair, row, rest):
-    tokens = rest.shape[0]
-    ahead = pair.shape[1] // HDIM // 2
-    return pl.pallas_call(
-        functools.partial(place_kernel, ahead),
-        out_shape=jax.ShapeDtypeStruct((tokens, rest.shape[1] + ahead * HDIM), BF16),
-        in_specs=[IN_VMEM] * 3,
+def place(pair, row, *rest):
+    tokens, lanes = pair.shape[0], pair.shape[1] // 2
+    return pl.pallas_call(
+        place_kernel,
+        out_shape=jax.ShapeDtypeStruct((tokens, lanes + sum(r.shape[1] for r in rest)), BF16),
+        in_specs=[IN_VMEM] * (2 + len(rest)),
         out_specs=ANYWHERE,
-        scratch_shapes=[pltpu.VMEM((tokens, ahead * HDIM), BF16), pltpu.SemaphoreType.DMA((ahead + 1,))],
+        scratch_shapes=[pltpu.VMEM((tokens, lanes), BF16), pltpu.SemaphoreType.DMA((lanes // HDIM + len(rest),))],
         compiler_params=compiler(VMEM),
         name="place",
-    )(pair, row, rest)
+    )(pair, row, *rest)
 
 
 def hold_kernel(x_ref, *rest):
@@ -465,25 +468,35 @@
     fetched.append(send(piece_and_row(stashed, totals, 2 * size, size, (fetched[0],)), partner))
     held = row_from(fetched[2], tokens)
     marks = [fetch(p, in_hbm(output)) for p in range(3, min(5, pieces))]
-    share = functools.partial(backward, width_all, eviction, stashed)
-    facts = (grad_input, totals, held, query_gain, key_gain)
-    group = max(1, pieces // 3)
-    base = group * size
-    pair, inner = share(
-        fetched[:group], *facts, jnp.zeros((1, tokens), F32), group * each, 0, base, (), (in_hbm(output), *marks)
-    )
+    base = max(1, count // 4) * HDIM
+
+    def share(inner, first, last, sofar, after):
+        heads = range(first // HDIM, last // HDIM)
+        used = sorted({h // each for h in heads})
+        found = tuple((used.index(h // each), h % each * HDIM) for h in heads)
+        return backward(
+            width_all, eviction, stashed, grad_input, totals, held, query_gain, key_gain, inner,
+            [fetched[p] for p in used], found, first, base, sofar, after,
+        )
+
+    pair, inner = share(jnp.zeros((1, tokens), F32), 0, base, (), (in_hbm(output), *marks))
     marks = [fetch(p, inner) for p in range(len(fetched), pieces)]
-    pair = send(hold(pair, tuple(fetched[-2:])), prior)
-    sofar = ()
-    for first, last in [(group, 2 * group)] + [(p, p + 1) for p in range(2 * group, pieces)]:
-        *sofar, inner = share(
-            fetched[first:last], *facts, inner, (last - first) * each, first * size, base, tuple(sofar), tuple(marks)
-        )
-        marks = []
+    sofar, inners = (), [inner]
+    ends = [base, width - 2 * size, width - size, width]
+    for first, last in zip(ends[:-1], ends[1:]):
+        if first < last:
+            *sofar, inner = share(inner, first, last, tuple(sofar), tuple(marks))
+            inners.append(inner)
+            marks = []
+    pair = send(hold(pair, (*fetched[-2:], inners[-2])), prior)
     inner = lax.psum(inner, "tensor")
-    lanes = next(c for c in (2, 1) if (width - base) % (c * HDIM) == 0) * HDIM
-    result, row = finish(width_all, eviction, *sofar, totals, held, inner, lanes)
-    result = place(pair, send(row, prior), send(result, prior))
+    left = width - base
+    cut = (left // HDIM + 1) // 2 * HDIM
+    ends = (*sofar, totals, held, inner)
+    early, row = finish(width_all, eviction, *ends, 0, cut)
+    early = send(early, prior)
+    late, _ = finish(width_all, eviction, *ends, cut, left)
+    result = place(pair, send(row, prior), early, send(late, prior))
     return (output[None], result[None])
 
 

time: 126 us -> 126 us (level)
  waiting for transfers between devices: 52.4 us -> 45.4 us
  Pallas kernels: 44.3 us -> 48.2 us
  starting transfers between devices: 13.6 us -> 16.6 us
    ppermute x9 -> x10, waiting for transfers between devices: 52.4 us -> 45.4 us  [send(): return lax.ppermute(x, 'section', pairs)]
    pallas_call x1 -> x2, Pallas kernels: 3.15 us -> 7.23 us  [finish(): pl.pallas_call(functools.partial(finish_kernel, width_all), out_shape=(ja...]
    ppermute x9 -> x10, starting transfers between devices: 13.6 us -> 16.6 us  [send(): return lax.ppermute(x, 'section', pairs)]
  transfers between devices with their start and end apart: 9 -> 10, of which waited for: 5 -> 5; matrix products, arithmetic and copies ran while one was open for 0% -> 0% of each run, Pallas kernels for 33% -> 37%
where the time goes in v18:
time: 126 us; the launch traced here: 125 us
  Pallas kernels  48.2 us (38%)
  waiting for transfers between devices  45.4 us (36%)
  starting transfers between devices  16.6 us (13%)
  blocking collectives  12.9 us (10%)
  between operations  1.63 us (1%)
    ppermute x10, waiting for transfers between devices, send(): return lax.ppermute(x, 'section', pairs)  45.4 us
    pallas_call x4, Pallas kernels, backward(): pl.pallas_call(functools.partial(backward_kernel, first, base, found, wid...  21.8 us
    ppermute x10, starting transfers between devices, send(): return lax.ppermute(x, 'section', pairs)  16.6 us
    pallas_call x1, Pallas kernels, forward(): pl.pallas_call(functools.partial(forward_kernel, heads, width_all), out_s...  8.39 us
    pallas_call x2, Pallas kernels, finish(): pl.pallas_call(functools.partial(finish_kernel, width_all), out_shape=(ja...  7.23 us
    psum x1, blocking collectives, local(): totals = lax.psum(squares(current, stashed, third, (mark,)), 'tensor')  6.53 us
    psum x1, blocking collectives, local(): inner = lax.psum(inner, 'tensor')  6.39 us
    pallas_call x1, Pallas kernels, squares(): pl.pallas_call(squares_kernel, out_shape=jax.ShapeDtypeStruct((3, tokens)...  4.74 us
  transfers between devices with their start and end apart: 10, of which 5 were waited for; matrix products, arithmetic and copies ran while one was open for 0% of the time, Pallas kernels for 37%

profile of v18, /device:TPU:0, one launch (start us, length us, event | category | flops | bytes accessed | tf_op | source)
XLA Modules:
  0.0 125.3 jit_solution(6561226534943892108)
XLA Ops:
  0.6 1.1 pieces.4
  1.7 0.0 copy-start.2
  1.7 0.6 copy-done.2
  2.3 4.0 %collective-permute-start = (bf16[512,256]{1,0:T(8,128)(2,1)S(1)}, bf16[512,256]{1,0:T(8,128)(2,1)S(1)}, u32[]{:S(2)}, u32[]{:S(2)}) collective-permute-start(bf16[512,256]{1,0:T(8,128)(2,1)S(1)} %get-tuple-element.26), channel_id=1, source_target_pairs={{0,16},{4,20},{8,24},{12,28},{16,0},{20,4},{24,8},{28,12},{1,17},{... | collective-permute-start | bytes 786440 | tf_op jit(solution)/shard_map/ppermute | solution.py:443
  6.3 0.0 collective-permute-start.2
  6.4 4.7 %squares.1 = f32[3,512]{1,0:T(4,128)} custom-call(bf16[512,1536]{1,0:T(8,128)(2,1)} %bitcast.4, bf16[1,2,512,1536]{3,2,1,0:T(8,128)(2,1)} %own_ref.7, f32[8,128]{1,0:T(8,128)} %copy-done.2), custom_call_target="tpu_custom_call" | custom-call | tf_op jit(solution)/shard_map/squares/pallas_call | solution.py:345
  11.1 6.5 %psum.14.t_ref = f32[3,512]{1,0:T(4,128)S(1)} all-reduce(f32[3,512]{1,0:T(4,128)} %squares.1), channel_id=1, replica_groups=mesh['section'=8,'tensor'=4] {'tensor'}, use_global_device_ids=true, to_apply=%region_0.0 | all-reduce | flops 1536 | bytes 12288 | tf_op jit(solution)/shard_map/psum | solution.py:460
  17.6 0.0 copy-start
  17.7 0.0 copy-start.1
  17.7 7.0 %collective-permute-done.rest_0_.refs_0_ = bf16[512,256]{1,0:T(8,128)(2,1)S(1)} collective-permute-done((bf16[512,256]{1,0:T(8,128)(2,1)S(1)}, bf16[512,256]{1,0:T(8,128)(2,1)S(1)}, u32[]{:S(2)}, u32[]{:S(2)}) %collective-permute-start) | collective-permute-done | bytes 262176 | tf_op jit(solution)/shard_map/ppermute | solution.py:443
  24.7 1.0 piece_and_row.1
  25.7 0.1 collective-permute-start.1
  25.7 0.0 copy-done
  25.7 0.0 copy-done.1
  25.8 8.4 %forward.1.rest_1_.refs_2_ = bf16[512,1536]{1,0:T(8,128)(2,1)} custom-call(bf16[512,1536]{1,0:T(8,128)(2,1)} %bitcast.5, f32[3,512]{1,0:T(4,128)S(1)} %psum.14.t_ref, f32[1,1536]{1,0:T(1,128)S(1)} %copy-done, f32[1,1536]{1,0:T(1,128)S(1)} %copy-done.1), custom_call_target="tpu_custom_call" | custom-call | tf_op jit(solution)/shard_map/forward/pallas_call | solution.py:119
  34.1 2.0 %collective-permute-done.2.rest_0_.refs_1_.refs_0_ = bf16[512,256]{1,0:T(8,128)(2,1)S(1)} collective-permute-done((bf16[512,256]{1,0:T(8,128)(2,1)S(1)}, bf16[512,256]{1,0:T(8,128)(2,1)S(1)}, u32[]{:S(2)}, u32[]{:S(2)}) %collective-permute-start.2) | collective-permute-done | bytes 262176 | tf_op jit(solution)/shard_map/ppermute | solution.py:443
  36.1 1.0 pieces.5
  37.1 1.0 collective-permute-start.4
  38.7 8.8 %collective-permute-done.1.extra_ref.rest_0_.refs_1_ = bf16[528,256]{1,0:T(8,128)(2,1)S(1)} collective-permute-done((bf16[528,256]{1,0:T(8,128)(2,1)S(1)}, bf16[528,256]{1,0:T(8,128)(2,1)S(1)}, u32[]{:S(2)}, u32[]{:S(2)}) %collective-permute-start.1) | collective-permute-done | bytes 270368 | tf_op jit(solution)/shard_map/ppermute | solution.py:443
  47.5 1.0 pieces.6
  48.5 0.1 collective-permute-start.3
  48.6 5.0 %backward.4 = (bf16[512,768]{1,0:T(8,128)(2,1)S(1)}, f32[1,512]{1,0:T(1,128)S(1)}) custom-call(s32[1]{0:T(128)S(6)} %copy.18.evicted_ref, bf16[1,2,512,1536]{3,2,1,0:T(8,128)(2,1)} %own_ref.7, bf16[1,512,1536]{2,1,0:T(8,128)(2,1)} %g_ref.7, f32[3,512]{1,0:T(4,128)S(1)} %psum.14.t_ref, f32[1,512]{1,0:T(1,128)S(1)} %row.1.held_ref, f32[1,1536]{1,0:T(1,128)S(1)} %copy-done, ...), custom_call_target="tpu_custom_call" | custom-call | tf_op jit(solution)/shard_map/backward/pallas_call | solution.py:230
  53.6 0.0 collective-permute-done.4.rest_0_.refs_2_
  53.6 1.0 pieces.7
  54.6 3.0 %collective-permute-start.5 = (bf16[512,256]{1,0:T(8,128)(2,1)S(1)}, bf16[512,256]{1,0:T(8,128)(2,1)S(1)}, u32[]{:S(2)}, u32[]{:S(2)}) collective-permute-start(bf16[512,256]{1,0:T(8,128)(2,1)S(1)} %get-tuple-element.34), channel_id=1, source_target_pairs={{0,16},{4,20},{8,24},{12,28},{16,0},{20,4},{24,8},{28,12},{1,17},{... | collective-permute-start | bytes 786440 | tf_op jit(solution)/shard_map/ppermute | solution.py:443
  57.6 8.1 %backward.5 = (f32[512,1152]{1,0:T(8,128)}, bf16[512,1152]{1,0:T(8,128)(2,1)}, f32[1,512]{1,0:T(1,128)S(1)}) custom-call(s32[1]{0:T(128)S(6)} %copy.18.evicted_ref, bf16[1,2,512,1536]{3,2,1,0:T(8,128)(2,1)} %own_ref.7, bf16[1,512,1536]{2,1,0:T(8,128)(2,1)} %g_ref.7, f32[3,512]{1,0:T(4,128)S(1)} %psum.14.t_ref, f32[1,512]{1,0:T(1,128)S(1)} %row.1.held_ref, ...), custom_call_target="tpu_custom_call" | custom-call | tf_op jit(solution)/shard_map/backward/pallas_call | solution.py:230
  65.7 0.0 collective-permute-done.3.refs_0_.rest_0_
  65.7 4.3 %backward.6 = (f32[512,1152]{1,0:T(8,128)}, bf16[512,1152]{1,0:T(8,128)(2,1)}, f32[1,512]{1,0:T(1,128)S(1)}) custom-call(s32[1]{0:T(128)S(6)} %copy.18.evicted_ref, bf16[1,2,512,1536]{3,2,1,0:T(8,128)(2,1)} %own_ref.7, bf16[1,512,1536]{2,1,0:T(8,128)(2,1)} %g_ref.7, f32[3,512]{1,0:T(4,128)S(1)} %psum.14.t_ref, ...), custom_call_target="tpu_custom_call", output_to_operand_aliasing={{0}: (9, {}), {1}: (10, {})} | custom-call | tf_op jit(solution)/shard_map/backward/pallas_call | solution.py:230
  70.1 4.7 %collective-permute-done.5.rest_1_.refs_0_ = bf16[512,256]{1,0:T(8,128)(2,1)S(1)} collective-permute-done((bf16[512,256]{1,0:T(8,128)(2,1)S(1)}, bf16[512,256]{1,0:T(8,128)(2,1)S(1)}, u32[]{:S(2)}, u32[]{:S(2)}) %collective-permute-start.5) | collective-permute-done | bytes 262176 | tf_op jit(solution)/shard_map/ppermute | solution.py:443
  74.8 7.0 %collective-permute-start.6 = (bf16[512,768]{1,0:T(8,128)(2,1)S(1)}, bf16[512,768]{1,0:T(8,128)(2,1)S(1)}, u32[]{:S(2)}, u32[]{:S(2)}) collective-permute-start(bf16[512,768]{1,0:T(8,128)(2,1)S(1)} %hold.1), channel_id=1, source_target_pairs={{0,28},{4,0},{8,4},{12,8},{16,12},{20,16},{24,20},{28,24},{1,29},{... | collective-permute-start | bytes 2359304 | tf_op jit(solution)/shard_map/ppermute | solution.py:443
  81.8 4.3 %backward.7 = (f32[512,1152]{1,0:T(8,128)}, bf16[512,1152]{1,0:T(8,128)(2,1)}, f32[1,512]{1,0:T(1,128)S(1)}) custom-call(s32[1]{0:T(128)S(6)} %copy.18.evicted_ref, bf16[1,2,512,1536]{3,2,1,0:T(8,128)(2,1)} %own_ref.7, bf16[1,512,1536]{2,1,0:T(8,128)(2,1)} %g_ref.7, f32[3,512]{1,0:T(4,128)S(1)} %psum.14.t_ref, ...), custom_call_target="tpu_custom_call", output_to_operand_aliasing={{0}: (9, {}), {1}: (10, {})} | custom-call | tf_op jit(solution)/shard_map/backward/pallas_call | solution.py:230
  86.1 6.4 %psum.15.inner_ref = f32[1,512]{1,0:T(1,128)S(1)} all-reduce(f32[1,512]{1,0:T(1,128)S(1)} %get-tuple-element.44), channel_id=1, replica_groups=mesh['section'=8,'tensor'=4] {'tensor'}, use_global_device_ids=true, to_apply=%region_1.0 | all-reduce | flops 512 | bytes 4096 | tf_op jit(solution)/shard_map/psum | solution.py:492
  92.5 3.8 %finish.2 = (bf16[512,640]{1,0:T(8,128)(2,1)S(1)}, f32[1,512]{1,0:T(1,128)S(1)}) custom-call(s32[1]{0:T(128)S(6)} %copy.18.evicted_ref, f32[512,1152]{1,0:T(8,128)} %get-tuple-element.42.a_ref, bf16[512,1152]{1,0:T(8,128)(2,1)} %get-tuple-element.43.x_ref, f32[3,512]{1,0:T(4,128)S(1)} %psum.14.t_ref, f32[1,512]{1,0:T(1,128)S(1)} %row.1.held_ref, ...), custom_call_target="tpu_custom_call" | custom-call | tf_op jit(solution)/shard_map/finish/pallas_call | solution.py:257
  96.3 0.9 collective-permute-start.8
  97.2 3.4 %finish.3 = (bf16[512,512]{1,0:T(8,128)(2,1)S(1)}, f32[1,512]{1,0:T(1,128)}) custom-call(s32[1]{0:T(128)S(6)} %copy.18.evicted_ref, f32[512,1152]{1,0:T(8,128)} %get-tuple-element.42.a_ref, bf16[512,1152]{1,0:T(8,128)(2,1)} %get-tuple-element.43.x_ref, f32[3,512]{1,0:T(4,128)S(1)} %psum.14.t_ref, f32[1,512]{1,0:T(1,128)S(1)} %row.1.held_ref, ...), custom_call_target="tpu_custom_call" | custom-call | tf_op jit(solution)/shard_map/finish/pallas_call | solution.py:257
  100.7 0.3 collective-permute-start.9
  101.0 0.0 collective-permute-start.7
  101.1 22.9 %collective-permute-done.7.row_ref = f32[1,512]{1,0:T(1,128)S(1)} collective-permute-done((f32[1,512]{1,0:T(1,128)S(1)}, f32[1,512]{1,0:T(1,128)S(1)}, u32[]{:S(2)}, u32[]{:S(2)}) %collective-permute-start.7) | collective-permute-done | bytes 2080 | tf_op jit(solution)/shard_map/ppermute | solution.py:443
  124.0 0.0 collective-permute-done.9.refs_1_
  124.0 0.0 collective-permute-done.8.refs_0_
  124.0 0.0 collective-permute-done.6.pair_ref
  124.0 1.2 place.1
  (3 shorter events, 0.0 us)
Async XLA Ops:
  1.7 0.6 copy-start.2
  2.3 22.4 %collective-permute-start = (bf16[512,256]{1,0:T(8,128)(2,1)S(1)}, bf16[512,256]{1,0:T(8,128)(2,1)S(1)}, u32[]{:S(2)}, u32[]{:S(2)}) collective-permute-start(bf16[512,256]{1,0:T(8,128)(2,1)S(1)} %get-tuple-element.26), channel_id=1, source_target_pairs={{0,16},{4,20},{8,24},{12,28},{16,0},{20,4},{24,8},{28,12},{1,17},{... | collective-permute-start | bytes 786440 | tf_op jit(solution)/shard_map/ppermute | solution.py:443
  6.3 29.8 %collective-permute-start.2 = (bf16[512,256]{1,0:T(8,128)(2,1)S(1)}, bf16[512,256]{1,0:T(8,128)(2,1)S(1)}, u32[]{:S(2)}, u32[]{:S(2)}) collective-permute-start(bf16[512,256]{1,0:T(8,128)(2,1)S(1)} %get-tuple-element.27), channel_id=1, source_target_pairs={{0,16},{4,20},{8,24},{12,28},{16,0},{20,4},{24,8},{28,12},{1,17},{... | collective-permute-start | bytes 786440 | tf_op jit(solution)/shard_map/ppermute | solution.py:443
  17.6 8.1 %copy-start = (f32[1,1536]{1,0:T(1,128)S(1)}, f32[1,1536]{1,0:T(1,128)}, u32[]{:S(2)}) copy-start(f32[1,1536]{1,0:T(1,128)} %gq_ref.9) | copy-start | bytes 18436
  17.7 8.1 %copy-start.1 = (f32[1,1536]{1,0:T(1,128)S(1)}, f32[1,1536]{1,0:T(1,128)}, u32[]{:S(2)}) copy-start(f32[1,1536]{1,0:T(1,128)} %gk_ref.9) | copy-start | bytes 18436
  25.7 21.9 %collective-permute-start.1 = (bf16[528,256]{1,0:T(8,128)(2,1)S(1)}, bf16[528,256]{1,0:T(8,128)(2,1)S(1)}, u32[]{:S(2)}, u32[]{:S(2)}) collective-permute-start(bf16[528,256]{1,0:T(8,128)(2,1)S(1)} %piece_and_row.1), channel_id=1, source_target_pairs={{0,16},{4,20},{8,24},{12,28},{16,0},{20,4},{24,8},{28,12},{1,17},{... | collective-permute-start | bytes 811016 | tf_op jit(solution)/shard_map/ppermute | solution.py:443
  37.1 16.5 %collective-permute-start.4 = (bf16[512,256]{1,0:T(8,128)(2,1)S(1)}, bf16[512,256]{1,0:T(8,128)(2,1)S(1)}, u32[]{:S(2)}, u32[]{:S(2)}) collective-permute-start(bf16[512,256]{1,0:T(8,128)(2,1)S(1)} %get-tuple-element.32), channel_id=1, source_target_pairs={{0,16},{4,20},{8,24},{12,28},{16,0},{20,4},{24,8},{28,12},{1,17},{... | collective-permute-start | bytes 786440 | tf_op jit(solution)/shard_map/ppermute | solution.py:443
  48.5 17.2 %collective-permute-start.3 = (bf16[512,256]{1,0:T(8,128)(2,1)S(1)}, bf16[512,256]{1,0:T(8,128)(2,1)S(1)}, u32[]{:S(2)}, u32[]{:S(2)}) collective-permute-start(bf16[512,256]{1,0:T(8,128)(2,1)S(1)} %get-tuple-element.31), channel_id=1, source_target_pairs={{0,16},{4,20},{8,24},{12,28},{16,0},{20,4},{24,8},{28,12},{1,17},{... | collective-permute-start | bytes 786440 | tf_op jit(solution)/shard_map/ppermute | solution.py:443
  54.6 20.2 %collective-permute-start.5 = (bf16[512,256]{1,0:T(8,128)(2,1)S(1)}, bf16[512,256]{1,0:T(8,128)(2,1)S(1)}, u32[]{:S(2)}, u32[]{:S(2)}) collective-permute-start(bf16[512,256]{1,0:T(8,128)(2,1)S(1)} %get-tuple-element.34), channel_id=1, source_target_pairs={{0,16},{4,20},{8,24},{12,28},{16,0},{20,4},{24,8},{28,12},{1,17},{... | collective-permute-start | bytes 786440 | tf_op jit(solution)/shard_map/ppermute | solution.py:443
  74.8 49.2 %collective-permute-start.6 = (bf16[512,768]{1,0:T(8,128)(2,1)S(1)}, bf16[512,768]{1,0:T(8,128)(2,1)S(1)}, u32[]{:S(2)}, u32[]{:S(2)}) collective-permute-start(bf16[512,768]{1,0:T(8,128)(2,1)S(1)} %hold.1), channel_id=1, source_target_pairs={{0,28},{4,0},{8,4},{12,8},{16,12},{20,16},{24,20},{28,24},{1,29},{... | collective-permute-start | bytes 2359304 | tf_op jit(solution)/shard_map/ppermute | solution.py:443
  96.3 27.7 %collective-permute-start.8 = (bf16[512,640]{1,0:T(8,128)(2,1)S(1)}, bf16[512,640]{1,0:T(8,128)(2,1)S(1)}, u32[]{:S(2)}, u32[]{:S(2)}) collective-permute-start(bf16[512,640]{1,0:T(8,128)(2,1)S(1)} %get-tuple-element.46), channel_id=1, source_target_pairs={{0,28},{4,0},{8,4},{12,8},{16,12},{20,16},{24,20},{28,24},{1,29},{... | collective-permute-start | bytes 1966088 | tf_op jit(solution)/shard_map/ppermute | solution.py:443
  100.7 23.3 %collective-permute-start.9 = (bf16[512,512]{1,0:T(8,128)(2,1)S(1)}, bf16[512,512]{1,0:T(8,128)(2,1)S(1)}, u32[]{:S(2)}, u32[]{:S(2)}) collective-permute-start(bf16[512,512]{1,0:T(8,128)(2,1)S(1)} %get-tuple-element.47), channel_id=1, source_target_pairs={{0,28},{4,0},{8,4},{12,8},{16,12},{20,16},{24,20},{28,24},{1,29},{... | collective-permute-start | bytes 1572872 | tf_op jit(solution)/shard_map/ppermute | solution.py:443
  101.0 23.0 %collective-permute-start.7 = (f32[1,512]{1,0:T(1,128)S(1)}, f32[1,512]{1,0:T(1,128)S(1)}, u32[]{:S(2)}, u32[]{:S(2)}) collective-permute-start(f32[1,512]{1,0:T(1,128)S(1)} %get-tuple-element.45), channel_id=1, source_target_pairs={{0,28},{4,0},{8,4},{12,8},{16,12},{20,16},{24,20},{28,24},{1,29},{... | collective-permute-start | bytes 6152 | tf_op jit(solution)/shard_map/ppermute | solution.py:443

commit v19 on v18

--- a/solution.py
+++ b/solution.py
@@ -244,22 +244,41 @@
     return inverse_rms(total, width_all) ** 3 * inner / width_all
 
 
-def finish_kernel(width_all, evicted_ref, a_ref, x_ref, t_ref, held_ref, inner_ref, o_ref, row_ref):
+def finish_kernel(
+    first, width_all, evicted_ref, a_ref, x_ref, t_ref, held_ref, inner_ref, o_ref, row_ref, terms, xs, a_sem, x_sem
+):
+    heads = o_ref.shape[1] // HDIM
+    copies = []
+    for h in range(heads):
+        mine = lanes_of(h * HDIM, HDIM)
+        there = lanes_of(first + h * HDIM, HDIM)
+        copies.append(
+            (
+                pltpu.make_async_copy(a_ref.at[there], terms.at[mine], a_sem.at[h]),
+                pltpu.make_async_copy(x_ref.at[there], xs.at[mine], x_sem.at[h]),
+            )
+        )
+        for copy in copies[-1]:
+            copy.start()
     row = row_of(total_of(evicted_ref, t_ref, held_ref), inner_ref[...], width_all)
     row_ref[...] = row
-    o_ref[...] = (a_ref[...] - x_ref[...].astype(F32) * column_of(row)).astype(BF16)
+    column = column_of(row)
+    for h in range(heads):
+        mine = lanes_of(h * HDIM, HDIM)
+        for copy in copies[h]:
+            copy.wait()
+        o_ref[mine] = (terms[mine] - xs[mine].astype(F32) * column).astype(BF16)
 
 
 def finish(width_all, evicted, a, x, totals, held, inner, first, last):
-    tokens = a.shape[0]
-    lanes = HDIM
-    block = pl.BlockSpec((tokens, lanes), lambda i: (0, first // lanes + i))
-    return pl.pallas_call(
-        functools.partial(finish_kernel, width_all),
-        out_shape=(jax.ShapeDtypeStruct((tokens, last - first), BF16), jax.ShapeDtypeStruct((1, tokens), F32)),
-        grid=((last - first) // lanes,),
-        in_specs=[pl.BlockSpec(memory_space=pltpu.SMEM), block, block] + [IN_VMEM] * 3,
-        out_specs=(pl.BlockSpec((tokens, lanes), lambda i: (0, i)), pl.BlockSpec((1, tokens), lambda i: (0, 0))),
+    shape = (a.shape[0], last - first)
+    dma = pltpu.SemaphoreType.DMA(((last - first) // HDIM,))
+    return pl.pallas_call(
+        functools.partial(finish_kernel, first, width_all),
+        out_shape=(jax.ShapeDtypeStruct(shape, BF16), jax.ShapeDtypeStruct((1, a.shape[0]), F32)),
+        in_specs=[pl.BlockSpec(memory_space=pltpu.SMEM)] + [IN_HBM] * 2 + [IN_VMEM] * 3,
+        out_specs=(IN_VMEM, IN_VMEM),
+        scratch_shapes=[pltpu.VMEM(shape, F32), pltpu.VMEM(shape, BF16), dma, dma],
         compiler_params=compiler(VMEM),
         name="finish",
     )(evicted, in_hbm(a), in_hbm(x), totals, held, inner)
@@ -480,14 +499,13 @@
         )
 
     pair, inner = share(jnp.zeros((1, tokens), F32), 0, base, (), (in_hbm(output), *marks))
-    marks = [fetch(p, inner) for p in range(len(fetched), pieces)]
+    marks = []
     sofar, inners = (), [inner]
-    ends = [base, width - 2 * size, width - size, width]
+    ends = sorted({base, max(base, 3 * size), *(p * size for p in range(4, pieces + 1))})
     for first, last in zip(ends[:-1], ends[1:]):
-        if first < last:
-            *sofar, inner = share(inner, first, last, tuple(sofar), tuple(marks))
-            inners.append(inner)
-            marks = []
+        *sofar, inner = share(inner, first, last, tuple(sofar), tuple(marks))
+        inners.append(inner)
+        marks = [fetch(p, inner) for p in range(len(fetched), pieces)]
     pair = send(hold(pair, (*fetched[-2:], inners[-2])), prior)
     inner = lax.psum(inner, "tensor")
     left = width - base

time: 126 us -> 123 us (0.976)
  starting transfers between devices: 16.6 us -> 14 us
  waiting for transfers between devices: 45.4 us -> 47.2 us
  Pallas kernels: 48.2 us -> 46.5 us
    pallas_call x2, Pallas kernels: 7.23 us -> 3.76 us  [finish(): pl.pallas_call(functools.partial(finish_kernel, first, width_all), out_sh...]
    ppermute x10, starting transfers between devices: 16.6 us -> 14 us  [send(): return lax.ppermute(x, 'section', pairs)]
    ppermute x10, waiting for transfers between devices: 45.4 us -> 47.2 us  [send(): return lax.ppermute(x, 'section', pairs)]
    pallas_call x4 -> x5, Pallas kernels: 21.8 us -> 23.5 us  [backward(): pl.pallas_call(functools.partial(backward_kernel, first, base, found, wid...]
  transfers between devices with their start and end apart: 10 -> 10, of which waited for: 5 -> 5; matrix products, arithmetic and copies ran while one was open for 0% -> 0% of each run, Pallas kernels for 37% -> 36%
where the time goes in v19:
time: 123 us
  waiting for transfers between devices  47.2 us (38%)
  Pallas kernels  46.5 us (38%)
  starting transfers between devices  14 us (11%)
  blocking collectives  13 us (11%)
  between operations  1.64 us (1%)
    ppermute x10, waiting for transfers between devices, send(): return lax.ppermute(x, 'section', pairs)  47.2 us
    pallas_call x5, Pallas kernels, backward(): pl.pallas_call(functools.partial(backward_kernel, first, base, found, wid...  23.5 us
    ppermute x10, starting transfers between devices, send(): return lax.ppermute(x, 'section', pairs)  14 us
    pallas_call x1, Pallas kernels, forward(): pl.pallas_call(functools.partial(forward_kernel, heads, width_all), out_s...  8.39 us
    psum x1, blocking collectives, local(): totals = lax.psum(squares(current, stashed, third, (mark,)), 'tensor')  6.53 us
    psum x1, blocking collectives, local(): inner = lax.psum(inner, 'tensor')  6.49 us
    pallas_call x1, Pallas kernels, squares(): pl.pallas_call(squares_kernel, out_shape=jax.ShapeDtypeStruct((3, tokens)...  4.74 us
    pallas_call x4, Pallas kernels, pieces_of(): pl.pallas_call(functools.partial(piece_kernel, starts, sizes), out_shape=...  3.94 us
  transfers between devices with their start and end apart: 10, of which 5 were waited for; matrix products, arithmetic and copies ran while one was open for 0% of the time, Pallas kernels for 36%

profile of v19, /device:TPU:0, one launch (start us, length us, event | category | flops | bytes accessed | tf_op | source)
XLA Modules:
  0.0 122.9 jit_solution(10319434643073378362)
XLA Ops:
  0.6 1.1 pieces.4
  1.7 0.0 copy-start.2
  1.7 0.6 copy-done.2
  2.3 4.0 %collective-permute-start = (bf16[512,256]{1,0:T(8,128)(2,1)S(1)}, bf16[512,256]{1,0:T(8,128)(2,1)S(1)}, u32[]{:S(2)}, u32[]{:S(2)}) collective-permute-start(bf16[512,256]{1,0:T(8,128)(2,1)S(1)} %get-tuple-element.29), channel_id=1, source_target_pairs={{0,16},{4,20},{8,24},{12,28},{16,0},{20,4},{24,8},{28,12},{1,17},{... | collective-permute-start | bytes 786440 | tf_op jit(solution)/shard_map/ppermute | solution.py:462
  6.3 0.0 collective-permute-start.2
  6.4 4.7 %squares.1 = f32[3,512]{1,0:T(4,128)} custom-call(bf16[512,1536]{1,0:T(8,128)(2,1)} %bitcast.4, bf16[1,2,512,1536]{3,2,1,0:T(8,128)(2,1)} %own_ref.9, f32[8,128]{1,0:T(8,128)} %copy-done.2), custom_call_target="tpu_custom_call" | custom-call | tf_op jit(solution)/shard_map/squares/pallas_call | solution.py:364
  11.1 6.5 %psum.14.t_ref = f32[3,512]{1,0:T(4,128)S(1)} all-reduce(f32[3,512]{1,0:T(4,128)} %squares.1), channel_id=1, replica_groups=mesh['section'=8,'tensor'=4] {'tensor'}, use_global_device_ids=true, to_apply=%region_0.0 | all-reduce | flops 1536 | bytes 12288 | tf_op jit(solution)/shard_map/psum | solution.py:479
  17.6 0.0 copy-start
  17.7 0.0 copy-start.1
  17.7 7.0 %collective-permute-done.rest_0_.refs_0_ = bf16[512,256]{1,0:T(8,128)(2,1)S(1)} collective-permute-done((bf16[512,256]{1,0:T(8,128)(2,1)S(1)}, bf16[512,256]{1,0:T(8,128)(2,1)S(1)}, u32[]{:S(2)}, u32[]{:S(2)}) %collective-permute-start) | collective-permute-done | bytes 262176 | tf_op jit(solution)/shard_map/ppermute | solution.py:462
  24.7 1.0 piece_and_row.1
  25.7 0.1 collective-permute-start.1
  25.7 0.0 copy-done
  25.7 0.0 copy-done.1
  25.8 8.4 %forward.1.rest_1_.refs_2_ = bf16[512,1536]{1,0:T(8,128)(2,1)} custom-call(bf16[512,1536]{1,0:T(8,128)(2,1)} %bitcast.5, f32[3,512]{1,0:T(4,128)S(1)} %psum.14.t_ref, f32[1,1536]{1,0:T(1,128)S(1)} %copy-done, f32[1,1536]{1,0:T(1,128)S(1)} %copy-done.1), custom_call_target="tpu_custom_call" | custom-call | tf_op jit(solution)/shard_map/forward/pallas_call | solution.py:119
  34.1 2.0 %collective-permute-done.2.rest_0_.refs_1_.refs_0_ = bf16[512,256]{1,0:T(8,128)(2,1)S(1)} collective-permute-done((bf16[512,256]{1,0:T(8,128)(2,1)S(1)}, bf16[512,256]{1,0:T(8,128)(2,1)S(1)}, u32[]{:S(2)}, u32[]{:S(2)}) %collective-permute-start.2) | collective-permute-done | bytes 262176 | tf_op jit(solution)/shard_map/ppermute | solution.py:462
  36.1 1.0 pieces.5
  37.1 1.0 collective-permute-start.4
  38.7 8.8 %collective-permute-done.1.extra_ref.rest_0_.refs_1_ = bf16[528,256]{1,0:T(8,128)(2,1)S(1)} collective-permute-done((bf16[528,256]{1,0:T(8,128)(2,1)S(1)}, bf16[528,256]{1,0:T(8,128)(2,1)S(1)}, u32[]{:S(2)}, u32[]{:S(2)}) %collective-permute-start.1) | collective-permute-done | bytes 270368 | tf_op jit(solution)/shard_map/ppermute | solution.py:462
  47.5 1.0 pieces.6
  48.5 0.1 collective-permute-start.3
  48.6 5.0 %backward.5 = (bf16[512,768]{1,0:T(8,128)(2,1)S(1)}, f32[1,512]{1,0:T(1,128)S(1)}) custom-call(s32[1]{0:T(128)S(6)} %copy.22.evicted_ref, bf16[1,2,512,1536]{3,2,1,0:T(8,128)(2,1)} %own_ref.9, bf16[1,512,1536]{2,1,0:T(8,128)(2,1)} %g_ref.9, f32[3,512]{1,0:T(4,128)S(1)} %psum.14.t_ref, f32[1,512]{1,0:T(1,128)S(1)} %row.1.held_ref, f32[1,1536]{1,0:T(1,128)S(1)} %copy-done, ...), custom_call_target="tpu_custom_call" | custom-call | tf_op jit(solution)/shard_map/backward/pallas_call | solution.py:230
  53.6 5.6 %backward.6 = (f32[512,1152]{1,0:T(8,128)}, bf16[512,1152]{1,0:T(8,128)(2,1)}, f32[1,512]{1,0:T(1,128)S(1)}) custom-call(s32[1]{0:T(128)S(6)} %copy.22.evicted_ref, bf16[1,2,512,1536]{3,2,1,0:T(8,128)(2,1)} %own_ref.9, bf16[1,512,1536]{2,1,0:T(8,128)(2,1)} %g_ref.9, f32[3,512]{1,0:T(4,128)S(1)} %psum.14.t_ref, f32[1,512]{1,0:T(1,128)S(1)} %row.1.held_ref, ...), custom_call_target="tpu_custom_call" | custom-call | tf_op jit(solution)/shard_map/backward/pallas_call | solution.py:230
  59.2 0.0 collective-permute-done.4.rest_0_.refs_0_
  59.2 1.0 pieces.7
  60.2 3.0 %collective-permute-start.5 = (bf16[512,256]{1,0:T(8,128)(2,1)S(1)}, bf16[512,256]{1,0:T(8,128)(2,1)S(1)}, u32[]{:S(2)}, u32[]{:S(2)}) collective-permute-start(bf16[512,256]{1,0:T(8,128)(2,1)S(1)} %get-tuple-element.38), channel_id=1, source_target_pairs={{0,16},{4,20},{8,24},{12,28},{16,0},{20,4},{24,8},{28,12},{1,17},{... | collective-permute-start | bytes 786440 | tf_op jit(solution)/shard_map/ppermute | solution.py:462
  63.1 4.3 %backward.7 = (f32[512,1152]{1,0:T(8,128)}, bf16[512,1152]{1,0:T(8,128)(2,1)}, f32[1,512]{1,0:T(1,128)S(1)}) custom-call(s32[1]{0:T(128)S(6)} %copy.22.evicted_ref, bf16[1,2,512,1536]{3,2,1,0:T(8,128)(2,1)} %own_ref.9, bf16[1,512,1536]{2,1,0:T(8,128)(2,1)} %g_ref.9, f32[3,512]{1,0:T(4,128)S(1)} %psum.14.t_ref, ...), custom_call_target="tpu_custom_call", output_to_operand_aliasing={{0}: (9, {}), {1}: (10, {})} | custom-call | tf_op jit(solution)/shard_map/backward/pallas_call | solution.py:230
  67.5 0.0 collective-permute-done.3.refs_0_.rest_0_
  67.5 4.3 %backward.8 = (f32[512,1152]{1,0:T(8,128)}, bf16[512,1152]{1,0:T(8,128)(2,1)}, f32[1,512]{1,0:T(1,128)S(1)}) custom-call(s32[1]{0:T(128)S(6)} %copy.22.evicted_ref, bf16[1,2,512,1536]{3,2,1,0:T(8,128)(2,1)} %own_ref.9, bf16[1,512,1536]{2,1,0:T(8,128)(2,1)} %g_ref.9, f32[3,512]{1,0:T(4,128)S(1)} %psum.14.t_ref, ...), custom_call_target="tpu_custom_call", output_to_operand_aliasing={{0}: (9, {}), {1}: (10, {})} | custom-call | tf_op jit(solution)/shard_map/backward/pallas_call | solution.py:230
  71.8 3.0 %collective-permute-done.5.rest_1_.refs_0_ = bf16[512,256]{1,0:T(8,128)(2,1)S(1)} collective-permute-done((bf16[512,256]{1,0:T(8,128)(2,1)S(1)}, bf16[512,256]{1,0:T(8,128)(2,1)S(1)}, u32[]{:S(2)}, u32[]{:S(2)}) %collective-permute-start.5) | collective-permute-done | bytes 262176 | tf_op jit(solution)/shard_map/ppermute | solution.py:462
  74.8 4.5 %collective-permute-start.6 = (bf16[512,768]{1,0:T(8,128)(2,1)S(1)}, bf16[512,768]{1,0:T(8,128)(2,1)S(1)}, u32[]{:S(2)}, u32[]{:S(2)}) collective-permute-start(bf16[512,768]{1,0:T(8,128)(2,1)S(1)} %hold.1), channel_id=1, source_target_pairs={{0,28},{4,0},{8,4},{12,8},{16,12},{20,16},{24,20},{28,24},{1,29},{... | collective-permute-start | bytes 2359304 | tf_op jit(solution)/shard_map/ppermute | solution.py:462
  79.3 4.3 %backward.9 = (f32[512,1152]{1,0:T(8,128)}, bf16[512,1152]{1,0:T(8,128)(2,1)}, f32[1,512]{1,0:T(1,128)S(1)}) custom-call(s32[1]{0:T(128)S(6)} %copy.22.evicted_ref, bf16[1,2,512,1536]{3,2,1,0:T(8,128)(2,1)} %own_ref.9, bf16[1,512,1536]{2,1,0:T(8,128)(2,1)} %g_ref.9, f32[3,512]{1,0:T(4,128)S(1)} %psum.14.t_ref, ...), custom_call_target="tpu_custom_call", output_to_operand_aliasing={{0}: (9, {}), {1}: (10, {})} | custom-call | tf_op jit(solution)/shard_map/backward/pallas_call | solution.py:230
  83.6 6.5 %psum.15.inner_ref = f32[1,512]{1,0:T(1,128)S(1)} all-reduce(f32[1,512]{1,0:T(1,128)S(1)} %get-tuple-element.50), channel_id=1, replica_groups=mesh['section'=8,'tensor'=4] {'tensor'}, use_global_device_ids=true, to_apply=%region_1.0 | all-reduce | flops 512 | bytes 4096 | tf_op jit(solution)/shard_map/psum | solution.py:510
  90.1 1.7 %finish.2 = (bf16[512,640]{1,0:T(8,128)(2,1)S(1)}, f32[1,512]{1,0:T(1,128)S(1)}) custom-call(s32[1]{0:T(128)S(6)} %copy.22.evicted_ref, f32[512,1152]{1,0:T(8,128)} %get-tuple-element.48.a_ref, bf16[512,1152]{1,0:T(8,128)(2,1)} %get-tuple-element.49.x_ref, f32[3,512]{1,0:T(4,128)S(1)} %psum.14.t_ref, f32[1,512]{1,0:T(1,128)S(1)} %row.1.held_ref, ...), custom_call_target="tpu_custom_call" | custom-call | tf_op jit(solution)/shard_map/finish/pallas_call | solution.py:276
  91.8 0.9 collective-permute-start.8
  92.6 2.0 %finish.3 = (bf16[512,512]{1,0:T(8,128)(2,1)S(1)}, f32[1,512]{1,0:T(1,128)}) custom-call(s32[1]{0:T(128)S(6)} %copy.22.evicted_ref, f32[512,1152]{1,0:T(8,128)} %get-tuple-element.48.a_ref, bf16[512,1152]{1,0:T(8,128)(2,1)} %get-tuple-element.49.x_ref, f32[3,512]{1,0:T(4,128)S(1)} %psum.14.t_ref, f32[1,512]{1,0:T(1,128)S(1)} %row.1.held_ref, ...), custom_call_target="tpu_custom_call" | custom-call | tf_op jit(solution)/shard_map/finish/pallas_call | solution.py:276
  94.7 0.4 collective-permute-start.9
  95.1 0.1 collective-permute-start.7
  95.1 26.4 %collective-permute-done.7.row_ref = f32[1,512]{1,0:T(1,128)S(1)} collective-permute-done((f32[1,512]{1,0:T(1,128)S(1)}, f32[1,512]{1,0:T(1,128)S(1)}, u32[]{:S(2)}, u32[]{:S(2)}) %collective-permute-start.7) | collective-permute-done | bytes 2080 | tf_op jit(solution)/shard_map/ppermute | solution.py:462
  121.6 0.0 collective-permute-done.9.refs_1_
  121.6 0.0 collective-permute-done.8.refs_0_
  121.6 0.0 collective-permute-done.6.pair_ref
  121.6 1.2 place.1
  (3 shorter events, 0.0 us)
Async XLA Ops:
  1.7 0.6 copy-start.2
  2.3 22.4 %collective-permute-start = (bf16[512,256]{1,0:T(8,128)(2,1)S(1)}, bf16[512,256]{1,0:T(8,128)(2,1)S(1)}, u32[]{:S(2)}, u32[]{:S(2)}) collective-permute-start(bf16[512,256]{1,0:T(8,128)(2,1)S(1)} %get-tuple-element.29), channel_id=1, source_target_pairs={{0,16},{4,20},{8,24},{12,28},{16,0},{20,4},{24,8},{28,12},{1,17},{... | collective-permute-start | bytes 786440 | tf_op jit(solution)/shard_map/ppermute | solution.py:462
  6.3 29.8 %collective-permute-start.2 = (bf16[512,256]{1,0:T(8,128)(2,1)S(1)}, bf16[512,256]{1,0:T(8,128)(2,1)S(1)}, u32[]{:S(2)}, u32[]{:S(2)}) collective-permute-start(bf16[512,256]{1,0:T(8,128)(2,1)S(1)} %get-tuple-element.30), channel_id=1, source_target_pairs={{0,16},{4,20},{8,24},{12,28},{16,0},{20,4},{24,8},{28,12},{1,17},{... | collective-permute-start | bytes 786440 | tf_op jit(solution)/shard_map/ppermute | solution.py:462
  17.6 8.1 %copy-start = (f32[1,1536]{1,0:T(1,128)S(1)}, f32[1,1536]{1,0:T(1,128)}, u32[]{:S(2)}) copy-start(f32[1,1536]{1,0:T(1,128)} %gq_ref.11) | copy-start | bytes 18436
  17.7 8.1 %copy-start.1 = (f32[1,1536]{1,0:T(1,128)S(1)}, f32[1,1536]{1,0:T(1,128)}, u32[]{:S(2)}) copy-start(f32[1,1536]{1,0:T(1,128)} %gk_ref.11) | copy-start | bytes 18436
  25.7 21.9 %collective-permute-start.1 = (bf16[528,256]{1,0:T(8,128)(2,1)S(1)}, bf16[528,256]{1,0:T(8,128)(2,1)S(1)}, u32[]{:S(2)}, u32[]{:S(2)}) collective-permute-start(bf16[528,256]{1,0:T(8,128)(2,1)S(1)} %piece_and_row.1), channel_id=1, source_target_pairs={{0,16},{4,20},{8,24},{12,28},{16,0},{20,4},{24,8},{28,12},{1,17},{... | collective-permute-start | bytes 811016 | tf_op jit(solution)/shard_map/ppermute | solution.py:462
  37.1 22.1 %collective-permute-start.4 = (bf16[512,256]{1,0:T(8,128)(2,1)S(1)}, bf16[512,256]{1,0:T(8,128)(2,1)S(1)}, u32[]{:S(2)}, u32[]{:S(2)}) collective-permute-start(bf16[512,256]{1,0:T(8,128)(2,1)S(1)} %get-tuple-element.35), channel_id=1, source_target_pairs={{0,16},{4,20},{8,24},{12,28},{16,0},{20,4},{24,8},{28,12},{1,17},{... | collective-permute-start | bytes 786440 | tf_op jit(solution)/shard_map/ppermute | solution.py:462
  48.5 19.0 %collective-permute-start.3 = (bf16[512,256]{1,0:T(8,128)(2,1)S(1)}, bf16[512,256]{1,0:T(8,128)(2,1)S(1)}, u32[]{:S(2)}, u32[]{:S(2)}) collective-permute-start(bf16[512,256]{1,0:T(8,128)(2,1)S(1)} %get-tuple-element.34), channel_id=1, source_target_pairs={{0,16},{4,20},{8,24},{12,28},{16,0},{20,4},{24,8},{28,12},{1,17},{... | collective-permute-start | bytes 786440 | tf_op jit(solution)/shard_map/ppermute | solution.py:462
  60.2 14.6 %collective-permute-start.5 = (bf16[512,256]{1,0:T(8,128)(2,1)S(1)}, bf16[512,256]{1,0:T(8,128)(2,1)S(1)}, u32[]{:S(2)}, u32[]{:S(2)}) collective-permute-start(bf16[512,256]{1,0:T(8,128)(2,1)S(1)} %get-tuple-element.38), channel_id=1, source_target_pairs={{0,16},{4,20},{8,24},{12,28},{16,0},{20,4},{24,8},{28,12},{1,17},{... | collective-permute-start | bytes 786440 | tf_op jit(solution)/shard_map/ppermute | solution.py:462
  74.8 46.8 %collective-permute-start.6 = (bf16[512,768]{1,0:T(8,128)(2,1)S(1)}, bf16[512,768]{1,0:T(8,128)(2,1)S(1)}, u32[]{:S(2)}, u32[]{:S(2)}) collective-permute-start(bf16[512,768]{1,0:T(8,128)(2,1)S(1)} %hold.1), channel_id=1, source_target_pairs={{0,28},{4,0},{8,4},{12,8},{16,12},{20,16},{24,20},{28,24},{1,29},{... | collective-permute-start | bytes 2359304 | tf_op jit(solution)/shard_map/ppermute | solution.py:462
  91.8 29.8 %collective-permute-start.8 = (bf16[512,640]{1,0:T(8,128)(2,1)S(1)}, bf16[512,640]{1,0:T(8,128)(2,1)S(1)}, u32[]{:S(2)}, u32[]{:S(2)}) collective-permute-start(bf16[512,640]{1,0:T(8,128)(2,1)S(1)} %get-tuple-element.52), channel_id=1, source_target_pairs={{0,28},{4,0},{8,4},{12,8},{16,12},{20,16},{24,20},{28,24},{1,29},{... | collective-permute-start | bytes 1966088 | tf_op jit(solution)/shard_map/ppermute | solution.py:462
  94.7 26.9 %collective-permute-start.9 = (bf16[512,512]{1,0:T(8,128)(2,1)S(1)}, bf16[512,512]{1,0:T(8,128)(2,1)S(1)}, u32[]{:S(2)}, u32[]{:S(2)}) collective-permute-start(bf16[512,512]{1,0:T(8,128)(2,1)S(1)} %get-tuple-element.53), channel_id=1, source_target_pairs={{0,28},{4,0},{8,4},{12,8},{16,12},{20,16},{24,20},{28,24},{1,29},{... | collective-permute-start | bytes 1572872 | tf_op jit(solution)/shard_map/ppermute | solution.py:462
  95.1 26.5 %collective-permute-start.7 = (f32[1,512]{1,0:T(1,128)S(1)}, f32[1,512]{1,0:T(1,128)S(1)}, u32[]{:S(2)}, u32[]{:S(2)}) collective-permute-start(f32[1,512]{1,0:T(1,128)S(1)} %get-tuple-element.51), channel_id=1, source_target_pairs={{0,28},{4,0},{8,4},{12,8},{16,12},{20,16},{24,20},{28,24},{1,29},{... | collective-permute-start | bytes 6152 | tf_op jit(solution)/shard_map/ppermute | solution.py:462

commit v20 on v19

--- a/solution.py
+++ b/solution.py
@@ -284,7 +284,7 @@
     )(evicted, in_hbm(a), in_hbm(x), totals, held, inner)
 
 
-def place_kernel(pair_ref, row_ref, *refs):
+def place_kernel(crossed_ref, far_ref, near_ref, row_ref, *refs):
     rest_refs, (o_ref, outs, sems) = refs[:-3], refs[-3:]
     lanes = outs.shape[1]
     ahead = lanes // HDIM
@@ -296,25 +296,28 @@
     row = column_of(row_ref[...])
     for h in range(ahead):
         mine = lanes_of(h * HDIM, HDIM)
-        x = pair_ref[lanes_of(lanes + h * HDIM, HDIM)]
-        outs[mine] = (pair_ref[mine].astype(F32) - x.astype(F32) * row).astype(BF16)
+        term, x = (
+            jnp.where(crossed_ref[0] == 1, far_ref[at], near_ref[at])
+            for at in (mine, lanes_of(lanes + h * HDIM, HDIM))
+        )
+        outs[mine] = (term.astype(F32) - x.astype(F32) * row).astype(BF16)
         copies.append(pltpu.make_async_copy(outs.at[mine], o_ref.at[mine], sems.at[h]))
         copies[-1].start()
     for copy in copies:
         copy.wait()
 
 
-def place(pair, row, *rest):
-    tokens, lanes = pair.shape[0], pair.shape[1] // 2
+def place(crossed, pairs, row, *rest):
+    tokens, lanes = pairs[0].shape[0], pairs[0].shape[1] // 2
     return pl.pallas_call(
         place_kernel,
         out_shape=jax.ShapeDtypeStruct((tokens, lanes + sum(r.shape[1] for r in rest)), BF16),
-        in_specs=[IN_VMEM] * (2 + len(rest)),
+        in_specs=[pl.BlockSpec(memory_space=pltpu.SMEM)] + [IN_VMEM] * (3 + len(rest)),
         out_specs=ANYWHERE,
         scratch_shapes=[pltpu.VMEM((tokens, lanes), BF16), pltpu.SemaphoreType.DMA((lanes // HDIM + len(rest),))],
         compiler_params=compiler(VMEM),
         name="place",
-    )(pair, row, *rest)
+    )(crossed, *pairs, row, *rest)
 
 
 def hold_kernel(x_ref, *rest):
@@ -466,6 +469,9 @@
     n = lax.axis_size("section")
     partner = [(s, (s + n // 2) % n) for s in range(n)]
     prior = [(s, (s - 1) % n) for s in range(n)]
+    crossing = [(0, n - 1), (n // 2, n // 2 - 1)]
+    me = lax.axis_index("section")
+    crossed = jnp.logical_or(me == n - 1, me == n // 2 - 1).astype(jnp.int32)[None]
     current = layer_input[0]
     tokens, width = current.shape
     count = width // HDIM
@@ -506,7 +512,8 @@
         *sofar, inner = share(inner, first, last, tuple(sofar), tuple(marks))
         inners.append(inner)
         marks = [fetch(p, inner) for p in range(len(fetched), pieces)]
-    pair = send(hold(pair, (*fetched[-2:], inners[-2])), prior)
+    pair = hold(pair, (*fetched[-2:], inners[-2]))
+    pairs = [send(pair, crossing), send(pair, [p for p in prior if p not in crossing])]
     inner = lax.psum(inner, "tensor")
     left = width - base
     cut = (left // HDIM + 1) // 2 * HDIM
@@ -514,7 +521,7 @@
     early, row = finish(width_all, eviction, *ends, 0, cut)
     early = send(early, prior)
     late, _ = finish(width_all, eviction, *ends, cut, left)
-    result = place(pair, send(row, prior), early, send(late, prior))
+    result = place(crossed, pairs, send(row, prior), early, send(late, prior))
     return (output[None], result[None])
 
 

time: 123 us -> 130 us (1.057)
  starting transfers between devices: 14 us -> 22.4 us
  waiting for transfers between devices: 47.2 us -> 43.4 us
    ppermute x10 -> x11, starting transfers between devices: 14 us -> 22.4 us  [send(): return lax.ppermute(x, 'section', pairs)]
    ppermute x10 -> x11, waiting for transfers between devices: 47.2 us -> 43.4 us  [send(): return lax.ppermute(x, 'section', pairs)]
  transfers between devices with their start and end apart: 10 -> 11, of which waited for: 5 -> 4; matrix products, arithmetic and copies ran while one was open for 0% -> 0% of each run, Pallas kernels for 36% -> 35%
where the time goes in v20:
time: 130 us; the launch traced here: 129 us
  Pallas kernels  47.6 us (37%)
  waiting for transfers between devices  43.4 us (33%)
  starting transfers between devices  22.4 us (17%)
  blocking collectives  13.3 us (10%)
  between operations  1.69 us (1%)
    ppermute x11, waiting for transfers between devices, send(): return lax.ppermute(x, 'section', pairs)  43.4 us
    pallas_call x5, Pallas kernels, backward(): pl.pallas_call(functools.partial(backward_kernel, first, base, found, wid...  23.5 us
    ppermute x11, starting transfers between devices, send(): return lax.ppermute(x, 'section', pairs)  22.4 us
    pallas_call x1, Pallas kernels, forward(): pl.pallas_call(functools.partial(forward_kernel, heads, width_all), out_s...  8.39 us
    psum x1, blocking collectives, local(): inner = lax.psum(inner, 'tensor')  6.78 us
    psum x1, blocking collectives, local(): totals = lax.psum(squares(current, stashed, third, (mark,)), 'tensor')  6.53 us
    pallas_call x2, Pallas kernels, finish(): pl.pallas_call(functools.partial(finish_kernel, first, width_all), out_sh...  4.91 us
    pallas_call x1, Pallas kernels, squares(): pl.pallas_call(squares_kernel, out_shape=jax.ShapeDtypeStruct((3, tokens)...  4.74 us
  transfers between devices with their start and end apart: 11, of which 4 were waited for; matrix products, arithmetic and copies ran while one was open for 0% of the time, Pallas kernels for 35%

profile of v20, /device:TPU:0, one launch (start us, length us, event | category | flops | bytes accessed | tf_op | source)
XLA Modules:
  0.0 129.0 jit_solution(5691425983902259467)
XLA Ops:
  0.6 1.1 pieces.4
  1.7 0.0 copy-start.2
  1.7 0.6 copy-done.2
  2.3 4.0 %collective-permute-start = (bf16[512,256]{1,0:T(8,128)(2,1)S(1)}, bf16[512,256]{1,0:T(8,128)(2,1)S(1)}, u32[]{:S(2)}, u32[]{:S(2)}) collective-permute-start(bf16[512,256]{1,0:T(8,128)(2,1)S(1)} %get-tuple-element.29), channel_id=1, source_target_pairs={{0,16},{4,20},{8,24},{12,28},{16,0},{20,4},{24,8},{28,12},{1,17},{... | collective-permute-start | bytes 786440 | tf_op jit(solution)/shard_map/ppermute | solution.py:465
  6.3 0.0 collective-permute-start.2
  6.4 4.7 %squares.1 = f32[3,512]{1,0:T(4,128)} custom-call(bf16[512,1536]{1,0:T(8,128)(2,1)} %bitcast.5, bf16[1,2,512,1536]{3,2,1,0:T(8,128)(2,1)} %own_ref.9, f32[8,128]{1,0:T(8,128)} %copy-done.2), custom_call_target="tpu_custom_call" | custom-call | tf_op jit(solution)/shard_map/squares/pallas_call | solution.py:367
  11.1 6.5 %psum.14.t_ref = f32[3,512]{1,0:T(4,128)S(1)} all-reduce(f32[3,512]{1,0:T(4,128)} %squares.1), channel_id=1, replica_groups=mesh['section'=8,'tensor'=4] {'tensor'}, use_global_device_ids=true, to_apply=%region_0.0 | all-reduce | flops 1536 | bytes 12288 | tf_op jit(solution)/shard_map/psum | solution.py:485
  17.6 0.0 copy-start
  17.7 0.0 copy-start.1
  17.7 7.0 %collective-permute-done.rest_0_.refs_0_ = bf16[512,256]{1,0:T(8,128)(2,1)S(1)} collective-permute-done((bf16[512,256]{1,0:T(8,128)(2,1)S(1)}, bf16[512,256]{1,0:T(8,128)(2,1)S(1)}, u32[]{:S(2)}, u32[]{:S(2)}) %collective-permute-start) | collective-permute-done | bytes 262176 | tf_op jit(solution)/shard_map/ppermute | solution.py:465
  24.7 1.0 piece_and_row.1
  25.7 0.1 collective-permute-start.1
  25.7 0.0 copy-done
  25.7 0.0 copy-done.1
  25.8 8.4 %forward.1.rest_1_.refs_2_ = bf16[512,1536]{1,0:T(8,128)(2,1)} custom-call(bf16[512,1536]{1,0:T(8,128)(2,1)} %bitcast.6, f32[3,512]{1,0:T(4,128)S(1)} %psum.14.t_ref, f32[1,1536]{1,0:T(1,128)S(1)} %copy-done, f32[1,1536]{1,0:T(1,128)S(1)} %copy-done.1), custom_call_target="tpu_custom_call" | custom-call | tf_op jit(solution)/shard_map/forward/pallas_call | solution.py:119
  34.1 2.0 %collective-permute-done.2.rest_0_.refs_1_.refs_0_ = bf16[512,256]{1,0:T(8,128)(2,1)S(1)} collective-permute-done((bf16[512,256]{1,0:T(8,128)(2,1)S(1)}, bf16[512,256]{1,0:T(8,128)(2,1)S(1)}, u32[]{:S(2)}, u32[]{:S(2)}) %collective-permute-start.2) | collective-permute-done | bytes 262176 | tf_op jit(solution)/shard_map/ppermute | solution.py:465
  36.1 1.0 pieces.5
  37.1 1.0 collective-permute-start.4
  38.7 8.8 %collective-permute-done.1.extra_ref.rest_0_.refs_1_ = bf16[528,256]{1,0:T(8,128)(2,1)S(1)} collective-permute-done((bf16[528,256]{1,0:T(8,128)(2,1)S(1)}, bf16[528,256]{1,0:T(8,128)(2,1)S(1)}, u32[]{:S(2)}, u32[]{:S(2)}) %collective-permute-start.1) | collective-permute-done | bytes 270368 | tf_op jit(solution)/shard_map/ppermute | solution.py:465
  47.5 1.0 pieces.6
  48.5 0.1 collective-permute-start.3
  48.6 5.0 %backward.5 = (bf16[512,768]{1,0:T(8,128)(2,1)S(1)}, f32[1,512]{1,0:T(1,128)S(1)}) custom-call(s32[1]{0:T(128)S(6)} %copy.22.evicted_ref, bf16[1,2,512,1536]{3,2,1,0:T(8,128)(2,1)} %own_ref.9, bf16[1,512,1536]{2,1,0:T(8,128)(2,1)} %g_ref.9, f32[3,512]{1,0:T(4,128)S(1)} %psum.14.t_ref, f32[1,512]{1,0:T(1,128)S(1)} %row.1.held_ref, f32[1,1536]{1,0:T(1,128)S(1)} %copy-done, ...), custom_call_target="tpu_custom_call" | custom-call | tf_op jit(solution)/shard_map/backward/pallas_call | solution.py:230
  53.6 5.6 %backward.6 = (f32[512,1152]{1,0:T(8,128)}, bf16[512,1152]{1,0:T(8,128)(2,1)}, f32[1,512]{1,0:T(1,128)S(1)}) custom-call(s32[1]{0:T(128)S(6)} %copy.22.evicted_ref, bf16[1,2,512,1536]{3,2,1,0:T(8,128)(2,1)} %own_ref.9, bf16[1,512,1536]{2,1,0:T(8,128)(2,1)} %g_ref.9, f32[3,512]{1,0:T(4,128)S(1)} %psum.14.t_ref, f32[1,512]{1,0:T(1,128)S(1)} %row.1.held_ref, ...), custom_call_target="tpu_custom_call" | custom-call | tf_op jit(solution)/shard_map/backward/pallas_call | solution.py:230
  59.2 0.0 collective-permute-done.4.rest_0_.refs_0_
  59.2 1.0 pieces.7
  60.2 3.1 %collective-permute-start.5 = (bf16[512,256]{1,0:T(8,128)(2,1)S(1)}, bf16[512,256]{1,0:T(8,128)(2,1)S(1)}, u32[]{:S(2)}, u32[]{:S(2)}) collective-permute-start(bf16[512,256]{1,0:T(8,128)(2,1)S(1)} %get-tuple-element.38), channel_id=1, source_target_pairs={{0,16},{4,20},{8,24},{12,28},{16,0},{20,4},{24,8},{28,12},{1,17},{... | collective-permute-start | bytes 786440 | tf_op jit(solution)/shard_map/ppermute | solution.py:465
  63.2 4.3 %backward.7 = (f32[512,1152]{1,0:T(8,128)}, bf16[512,1152]{1,0:T(8,128)(2,1)}, f32[1,512]{1,0:T(1,128)S(1)}) custom-call(s32[1]{0:T(128)S(6)} %copy.22.evicted_ref, bf16[1,2,512,1536]{3,2,1,0:T(8,128)(2,1)} %own_ref.9, bf16[1,512,1536]{2,1,0:T(8,128)(2,1)} %g_ref.9, f32[3,512]{1,0:T(4,128)S(1)} %psum.14.t_ref, ...), custom_call_target="tpu_custom_call", output_to_operand_aliasing={{0}: (9, {}), {1}: (10, {})} | custom-call | tf_op jit(solution)/shard_map/backward/pallas_call | solution.py:230
  67.5 0.0 collective-permute-done.3.refs_0_.rest_0_
  67.5 4.3 %backward.8 = (f32[512,1152]{1,0:T(8,128)}, bf16[512,1152]{1,0:T(8,128)(2,1)}, f32[1,512]{1,0:T(1,128)S(1)}) custom-call(s32[1]{0:T(128)S(6)} %copy.22.evicted_ref, bf16[1,2,512,1536]{3,2,1,0:T(8,128)(2,1)} %own_ref.9, bf16[1,512,1536]{2,1,0:T(8,128)(2,1)} %g_ref.9, f32[3,512]{1,0:T(4,128)S(1)} %psum.14.t_ref, ...), custom_call_target="tpu_custom_call", output_to_operand_aliasing={{0}: (9, {}), {1}: (10, {})} | custom-call | tf_op jit(solution)/shard_map/backward/pallas_call | solution.py:230
  71.9 0.0 collective-permute-done.5.rest_1_.refs_0_
  71.9 9.3 %collective-permute-start.6 = (bf16[512,768]{1,0:T(8,128)(2,1)S(1)}, bf16[512,768]{1,0:T(8,128)(2,1)S(1)}, u32[]{:S(2)}, u32[]{:S(2)}) collective-permute-start(bf16[512,768]{1,0:T(8,128)(2,1)S(1)} %hold.1), channel_id=1, source_target_pairs={{0,28},{16,12},{1,29},{17,13},{2,30},{18,14},{3,31},{19,15}} | collective-permute-start | bytes 2359304 | tf_op jit(solution)/shard_map/ppermute | solution.py:465
  81.2 1.3 %collective-permute-start.7 = (bf16[512,768]{1,0:T(8,128)(2,1)S(1)}, bf16[512,768]{1,0:T(8,128)(2,1)S(1)}, u32[]{:S(2)}, u32[]{:S(2)}) collective-permute-start(bf16[512,768]{1,0:T(8,128)(2,1)S(1)} %hold.1), channel_id=1, source_target_pairs={{4,0},{8,4},{12,8},{20,16},{24,20},{28,24},{5,1},{9,5},{13,9},{21,... | collective-permute-start | bytes 2359304 | tf_op jit(solution)/shard_map/ppermute | solution.py:465
  82.5 4.3 %backward.9 = (f32[512,1152]{1,0:T(8,128)}, bf16[512,1152]{1,0:T(8,128)(2,1)}, f32[1,512]{1,0:T(1,128)S(1)}) custom-call(s32[1]{0:T(128)S(6)} %copy.22.evicted_ref, bf16[1,2,512,1536]{3,2,1,0:T(8,128)(2,1)} %own_ref.9, bf16[1,512,1536]{2,1,0:T(8,128)(2,1)} %g_ref.9, f32[3,512]{1,0:T(4,128)S(1)} %psum.14.t_ref, ...), custom_call_target="tpu_custom_call", output_to_operand_aliasing={{0}: (9, {}), {1}: (10, {})} | custom-call | tf_op jit(solution)/shard_map/backward/pallas_call | solution.py:230
  86.8 6.8 %psum.15.inner_ref = f32[1,512]{1,0:T(1,128)S(1)} all-reduce(f32[1,512]{1,0:T(1,128)S(1)} %get-tuple-element.50), channel_id=1, replica_groups=mesh['section'=8,'tensor'=4] {'tensor'}, use_global_device_ids=true, to_apply=%region_1.0 | all-reduce | flops 512 | bytes 4096 | tf_op jit(solution)/shard_map/psum | solution.py:517
  93.6 2.6 %finish.2 = (bf16[512,640]{1,0:T(8,128)(2,1)}, f32[1,512]{1,0:T(1,128)S(1)}) custom-call(s32[1]{0:T(128)S(6)} %copy.22.evicted_ref, f32[512,1152]{1,0:T(8,128)} %get-tuple-element.48.a_ref, bf16[512,1152]{1,0:T(8,128)(2,1)} %get-tuple-element.49.x_ref, f32[3,512]{1,0:T(4,128)S(1)} %psum.14.t_ref, f32[1,512]{1,0:T(1,128)S(1)} %row.1.held_ref, ...), custom_call_target="tpu_custom_call" | custom-call | tf_op jit(solution)/shard_map/finish/pallas_call | solution.py:276
  96.2 0.1 collective-permute-start.9
  96.3 2.3 %finish.3 = (bf16[512,512]{1,0:T(8,128)(2,1)}, f32[1,512]{1,0:T(1,128)}) custom-call(s32[1]{0:T(128)S(6)} %copy.22.evicted_ref, f32[512,1152]{1,0:T(8,128)} %get-tuple-element.48.a_ref, bf16[512,1152]{1,0:T(8,128)(2,1)} %get-tuple-element.49.x_ref, f32[3,512]{1,0:T(4,128)S(1)} %psum.14.t_ref, f32[1,512]{1,0:T(1,128)S(1)} %row.1.held_ref, ...), custom_call_target="tpu_custom_call" | custom-call | tf_op jit(solution)/shard_map/finish/pallas_call | solution.py:276
  98.6 0.2 collective-permute-start.10
  98.9 3.2 %collective-permute-start.8 = (f32[1,512]{1,0:T(1,128)S(1)}, f32[1,512]{1,0:T(1,128)S(1)}, u32[]{:S(2)}, u32[]{:S(2)}) collective-permute-start(f32[1,512]{1,0:T(1,128)S(1)} %get-tuple-element.51), channel_id=1, source_target_pairs={{0,28},{4,0},{8,4},{12,8},{16,12},{20,16},{24,20},{28,24},{1,29},{... | collective-permute-start | bytes 6152 | tf_op jit(solution)/shard_map/ppermute | solution.py:465
  102.0 25.6 %collective-permute-done.8.row_ref = f32[1,512]{1,0:T(1,128)S(1)} collective-permute-done((f32[1,512]{1,0:T(1,128)S(1)}, f32[1,512]{1,0:T(1,128)S(1)}, u32[]{:S(2)}, u32[]{:S(2)}) %collective-permute-start.8) | collective-permute-done | bytes 2080 | tf_op jit(solution)/shard_map/ppermute | solution.py:465
  127.6 0.0 collective-permute-done.10.refs_1_
  127.6 0.0 collective-permute-done.9.refs_0_
  127.6 0.0 collective-permute-done.6.far_ref
  127.6 0.0 collective-permute-done.7.near_ref
  127.6 1.2 place.1
  (3 shorter events, 0.0 us)
Async XLA Ops:
  1.7 0.6 copy-start.2
  2.3 22.4 %collective-permute-start = (bf16[512,256]{1,0:T(8,128)(2,1)S(1)}, bf16[512,256]{1,0:T(8,128)(2,1)S(1)}, u32[]{:S(2)}, u32[]{:S(2)}) collective-permute-start(bf16[512,256]{1,0:T(8,128)(2,1)S(1)} %get-tuple-element.29), channel_id=1, source_target_pairs={{0,16},{4,20},{8,24},{12,28},{16,0},{20,4},{24,8},{28,12},{1,17},{... | collective-permute-start | bytes 786440 | tf_op jit(solution)/shard_map/ppermute | solution.py:465
  6.3 29.8 %collective-permute-start.2 = (bf16[512,256]{1,0:T(8,128)(2,1)S(1)}, bf16[512,256]{1,0:T(8,128)(2,1)S(1)}, u32[]{:S(2)}, u32[]{:S(2)}) collective-permute-start(bf16[512,256]{1,0:T(8,128)(2,1)S(1)} %get-tuple-element.30), channel_id=1, source_target_pairs={{0,16},{4,20},{8,24},{12,28},{16,0},{20,4},{24,8},{28,12},{1,17},{... | collective-permute-start | bytes 786440 | tf_op jit(solution)/shard_map/ppermute | solution.py:465
  17.6 8.1 %copy-start = (f32[1,1536]{1,0:T(1,128)S(1)}, f32[1,1536]{1,0:T(1,128)}, u32[]{:S(2)}) copy-start(f32[1,1536]{1,0:T(1,128)} %gq_ref.11) | copy-start | bytes 18436
  17.7 8.1 %copy-start.1 = (f32[1,1536]{1,0:T(1,128)S(1)}, f32[1,1536]{1,0:T(1,128)}, u32[]{:S(2)}) copy-start(f32[1,1536]{1,0:T(1,128)} %gk_ref.11) | copy-start | bytes 18436
  25.7 21.9 %collective-permute-start.1 = (bf16[528,256]{1,0:T(8,128)(2,1)S(1)}, bf16[528,256]{1,0:T(8,128)(2,1)S(1)}, u32[]{:S(2)}, u32[]{:S(2)}) collective-permute-start(bf16[528,256]{1,0:T(8,128)(2,1)S(1)} %piece_and_row.1), channel_id=1, source_target_pairs={{0,16},{4,20},{8,24},{12,28},{16,0},{20,4},{24,8},{28,12},{1,17},{... | collective-permute-start | bytes 811016 | tf_op jit(solution)/shard_map/ppermute | solution.py:465
  37.1 22.1 %collective-permute-start.4 = (bf16[512,256]{1,0:T(8,128)(2,1)S(1)}, bf16[512,256]{1,0:T(8,128)(2,1)S(1)}, u32[]{:S(2)}, u32[]{:S(2)}) collective-permute-start(bf16[512,256]{1,0:T(8,128)(2,1)S(1)} %get-tuple-element.35), channel_id=1, source_target_pairs={{0,16},{4,20},{8,24},{12,28},{16,0},{20,4},{24,8},{28,12},{1,17},{... | collective-permute-start | bytes 786440 | tf_op jit(solution)/shard_map/ppermute | solution.py:465
  48.5 19.1 %collective-permute-start.3 = (bf16[512,256]{1,0:T(8,128)(2,1)S(1)}, bf16[512,256]{1,0:T(8,128)(2,1)S(1)}, u32[]{:S(2)}, u32[]{:S(2)}) collective-permute-start(bf16[512,256]{1,0:T(8,128)(2,1)S(1)} %get-tuple-element.34), channel_id=1, source_target_pairs={{0,16},{4,20},{8,24},{12,28},{16,0},{20,4},{24,8},{28,12},{1,17},{... | collective-permute-start | bytes 786440 | tf_op jit(solution)/shard_map/ppermute | solution.py:465
  60.2 11.7 %collective-permute-start.5 = (bf16[512,256]{1,0:T(8,128)(2,1)S(1)}, bf16[512,256]{1,0:T(8,128)(2,1)S(1)}, u32[]{:S(2)}, u32[]{:S(2)}) collective-permute-start(bf16[512,256]{1,0:T(8,128)(2,1)S(1)} %get-tuple-element.38), channel_id=1, source_target_pairs={{0,16},{4,20},{8,24},{12,28},{16,0},{20,4},{24,8},{28,12},{1,17},{... | collective-permute-start | bytes 786440 | tf_op jit(solution)/shard_map/ppermute | solution.py:465
  71.9 55.7 %collective-permute-start.6 = (bf16[512,768]{1,0:T(8,128)(2,1)S(1)}, bf16[512,768]{1,0:T(8,128)(2,1)S(1)}, u32[]{:S(2)}, u32[]{:S(2)}) collective-permute-start(bf16[512,768]{1,0:T(8,128)(2,1)S(1)} %hold.1), channel_id=1, source_target_pairs={{0,28},{16,12},{1,29},{17,13},{2,30},{18,14},{3,31},{19,15}} | collective-permute-start | bytes 2359304 | tf_op jit(solution)/shard_map/ppermute | solution.py:465
  81.2 46.4 %collective-permute-start.7 = (bf16[512,768]{1,0:T(8,128)(2,1)S(1)}, bf16[512,768]{1,0:T(8,128)(2,1)S(1)}, u32[]{:S(2)}, u32[]{:S(2)}) collective-permute-start(bf16[512,768]{1,0:T(8,128)(2,1)S(1)} %hold.1), channel_id=1, source_target_pairs={{4,0},{8,4},{12,8},{20,16},{24,20},{28,24},{5,1},{9,5},{13,9},{21,... | collective-permute-start | bytes 2359304 | tf_op jit(solution)/shard_map/ppermute | solution.py:465
  96.2 31.4 %collective-permute-start.9 = (bf16[512,640]{1,0:T(8,128)(2,1)}, bf16[512,640]{1,0:T(8,128)(2,1)S(1)}, u32[]{:S(2)}, u32[]{:S(2)}) collective-permute-start(bf16[512,640]{1,0:T(8,128)(2,1)} %get-tuple-element.52), channel_id=1, source_target_pairs={{0,28},{4,0},{8,4},{12,8},{16,12},{20,16},{24,20},{28,24},{1,29},{... | collective-permute-start | bytes 1966088 | tf_op jit(solution)/shard_map/ppermute | solution.py:465
  98.6 29.0 %collective-permute-start.10 = (bf16[512,512]{1,0:T(8,128)(2,1)}, bf16[512,512]{1,0:T(8,128)(2,1)S(1)}, u32[]{:S(2)}, u32[]{:S(2)}) collective-permute-start(bf16[512,512]{1,0:T(8,128)(2,1)} %get-tuple-element.53), channel_id=1, source_target_pairs={{0,28},{4,0},{8,4},{12,8},{16,12},{20,16},{24,20},{28,24},{1,29},{... | collective-permute-start | bytes 1572872 | tf_op jit(solution)/shard_map/ppermute | solution.py:465
  98.9 28.8 %collective-permute-start.8 = (f32[1,512]{1,0:T(1,128)S(1)}, f32[1,512]{1,0:T(1,128)S(1)}, u32[]{:S(2)}, u32[]{:S(2)}) collective-permute-start(f32[1,512]{1,0:T(1,128)S(1)} %get-tuple-element.51), channel_id=1, source_target_pairs={{0,28},{4,0},{8,4},{12,8},{16,12},{20,16},{24,20},{28,24},{1,29},{... | collective-permute-start | bytes 6152 | tf_op jit(solution)/shard_map/ppermute | solution.py:465

commit v21 on v19

--- a/solution.py
+++ b/solution.py
@@ -506,7 +506,7 @@
         *sofar, inner = share(inner, first, last, tuple(sofar), tuple(marks))
         inners.append(inner)
         marks = [fetch(p, inner) for p in range(len(fetched), pieces)]
-    pair = send(hold(pair, (*fetched[-2:], inners[-2])), prior)
+    pair = send(hold(pair, (inners[-2],)), prior)
     inner = lax.psum(inner, "tensor")
     left = width - base
     cut = (left // HDIM + 1) // 2 * HDIM

time: 123 us -> 123 us (level)
  waiting for transfers between devices: 47.2 us -> 44.1 us
  starting transfers between devices: 14 us -> 16.9 us
    ppermute x10, waiting for transfers between devices: 47.2 us -> 44.1 us  [send(): return lax.ppermute(x, 'section', pairs)]
    ppermute x10, starting transfers between devices: 14 us -> 16.9 us  [send(): return lax.ppermute(x, 'section', pairs)]
  transfers between devices with their start and end apart: 10 -> 10, of which waited for: 5 -> 4; matrix products, arithmetic and copies ran while one was open for 0% -> 0% of each run, Pallas kernels for 36% -> 36%
where the time goes in v21:
time: 123 us; the launch traced here: 122 us
  Pallas kernels  46.5 us (38%)
  waiting for transfers between devices  44.1 us (36%)
  starting transfers between devices  16.9 us (14%)
  blocking collectives  12.4 us (10%)
  between operations  1.64 us (1%)
    ppermute x10, waiting for transfers between devices, send(): return lax.ppermute(x, 'section', pairs)  44.1 us
    pallas_call x5, Pallas kernels, backward(): pl.pallas_call(functools.partial(backward_kernel, first, base, found, wid...  23.5 us
    ppermute x10, starting transfers between devices, send(): return lax.ppermute(x, 'section', pairs)  16.9 us
    pallas_call x1, Pallas kernels, forward(): pl.pallas_call(functools.partial(forward_kernel, heads, width_all), out_s...  8.39 us
    psum x1, blocking collectives, local(): totals = lax.psum(squares(current, stashed, third, (mark,)), 'tensor')  6.53 us
    psum x1, blocking collectives, local(): inner = lax.psum(inner, 'tensor')  5.83 us
    pallas_call x1, Pallas kernels, squares(): pl.pallas_call(squares_kernel, out_shape=jax.ShapeDtypeStruct((3, tokens)...  4.74 us
    pallas_call x4, Pallas kernels, pieces_of(): pl.pallas_call(functools.partial(piece_kernel, starts, sizes), out_shape=...  3.94 us
  transfers between devices with their start and end apart: 10, of which 4 were waited for; matrix products, arithmetic and copies ran while one was open for 0% of the time, Pallas kernels for 36%

profile of v21, /device:TPU:0, one launch (start us, length us, event | category | flops | bytes accessed | tf_op | source)
XLA Modules:
  0.0 122.2 jit_solution(623688609455668071)
XLA Ops:
  0.6 1.1 pieces.4
  1.7 0.0 copy-start.2
  1.7 0.6 copy-done.2
  2.3 4.0 %collective-permute-start = (bf16[512,256]{1,0:T(8,128)(2,1)S(1)}, bf16[512,256]{1,0:T(8,128)(2,1)S(1)}, u32[]{:S(2)}, u32[]{:S(2)}) collective-permute-start(bf16[512,256]{1,0:T(8,128)(2,1)S(1)} %get-tuple-element.29), channel_id=1, source_target_pairs={{0,16},{4,20},{8,24},{12,28},{16,0},{20,4},{24,8},{28,12},{1,17},{... | collective-permute-start | bytes 786440 | tf_op jit(solution)/shard_map/ppermute | solution.py:462
  6.3 0.0 collective-permute-start.2
  6.4 4.7 %squares.1 = f32[3,512]{1,0:T(4,128)} custom-call(bf16[512,1536]{1,0:T(8,128)(2,1)} %bitcast.4, bf16[1,2,512,1536]{3,2,1,0:T(8,128)(2,1)} %own_ref.9, f32[8,128]{1,0:T(8,128)} %copy-done.2), custom_call_target="tpu_custom_call" | custom-call | tf_op jit(solution)/shard_map/squares/pallas_call | solution.py:364
  11.1 6.5 %psum.14.t_ref = f32[3,512]{1,0:T(4,128)S(1)} all-reduce(f32[3,512]{1,0:T(4,128)} %squares.1), channel_id=1, replica_groups=mesh['section'=8,'tensor'=4] {'tensor'}, use_global_device_ids=true, to_apply=%region_0.0 | all-reduce | flops 1536 | bytes 12288 | tf_op jit(solution)/shard_map/psum | solution.py:479
  17.6 0.0 copy-start
  17.7 0.0 copy-start.1
  17.7 7.0 %collective-permute-done.rest_0_.refs_0_ = bf16[512,256]{1,0:T(8,128)(2,1)S(1)} collective-permute-done((bf16[512,256]{1,0:T(8,128)(2,1)S(1)}, bf16[512,256]{1,0:T(8,128)(2,1)S(1)}, u32[]{:S(2)}, u32[]{:S(2)}) %collective-permute-start) | collective-permute-done | bytes 262176 | tf_op jit(solution)/shard_map/ppermute | solution.py:462
  24.7 1.0 piece_and_row.1
  25.7 0.1 collective-permute-start.1
  25.7 0.0 copy-done
  25.7 0.0 copy-done.1
  25.8 8.4 %forward.1.rest_1_.refs_2_ = bf16[512,1536]{1,0:T(8,128)(2,1)} custom-call(bf16[512,1536]{1,0:T(8,128)(2,1)} %bitcast.5, f32[3,512]{1,0:T(4,128)S(1)} %psum.14.t_ref, f32[1,1536]{1,0:T(1,128)S(1)} %copy-done, f32[1,1536]{1,0:T(1,128)S(1)} %copy-done.1), custom_call_target="tpu_custom_call" | custom-call | tf_op jit(solution)/shard_map/forward/pallas_call | solution.py:119
  34.1 2.0 %collective-permute-done.2.rest_0_.refs_1_.refs_0_ = bf16[512,256]{1,0:T(8,128)(2,1)S(1)} collective-permute-done((bf16[512,256]{1,0:T(8,128)(2,1)S(1)}, bf16[512,256]{1,0:T(8,128)(2,1)S(1)}, u32[]{:S(2)}, u32[]{:S(2)}) %collective-permute-start.2) | collective-permute-done | bytes 262176 | tf_op jit(solution)/shard_map/ppermute | solution.py:462
  36.1 1.0 pieces.5
  37.1 1.0 collective-permute-start.3
  38.1 9.4 %collective-permute-done.1.extra_ref.rest_0_.refs_1_ = bf16[528,256]{1,0:T(8,128)(2,1)S(1)} collective-permute-done((bf16[528,256]{1,0:T(8,128)(2,1)S(1)}, bf16[528,256]{1,0:T(8,128)(2,1)S(1)}, u32[]{:S(2)}, u32[]{:S(2)}) %collective-permute-start.1) | collective-permute-done | bytes 270368 | tf_op jit(solution)/shard_map/ppermute | solution.py:462
  47.5 1.0 pieces.6
  48.5 0.1 collective-permute-start.4
  49.2 5.0 %backward.5 = (bf16[512,768]{1,0:T(8,128)(2,1)S(1)}, f32[1,512]{1,0:T(1,128)S(1)}) custom-call(s32[1]{0:T(128)S(6)} %copy.22.evicted_ref, bf16[1,2,512,1536]{3,2,1,0:T(8,128)(2,1)} %own_ref.9, bf16[1,512,1536]{2,1,0:T(8,128)(2,1)} %g_ref.9, f32[3,512]{1,0:T(4,128)S(1)} %psum.14.t_ref, f32[1,512]{1,0:T(1,128)S(1)} %row.1.held_ref, f32[1,1536]{1,0:T(1,128)S(1)} %copy-done, ...), custom_call_target="tpu_custom_call" | custom-call | tf_op jit(solution)/shard_map/backward/pallas_call | solution.py:230
  54.2 5.6 %backward.6 = (f32[512,1152]{1,0:T(8,128)}, bf16[512,1152]{1,0:T(8,128)(2,1)}, f32[1,512]{1,0:T(1,128)S(1)}) custom-call(s32[1]{0:T(128)S(6)} %copy.22.evicted_ref, bf16[1,2,512,1536]{3,2,1,0:T(8,128)(2,1)} %own_ref.9, bf16[1,512,1536]{2,1,0:T(8,128)(2,1)} %g_ref.9, f32[3,512]{1,0:T(4,128)S(1)} %psum.14.t_ref, f32[1,512]{1,0:T(1,128)S(1)} %row.1.held_ref, ...), custom_call_target="tpu_custom_call" | custom-call | tf_op jit(solution)/shard_map/backward/pallas_call | solution.py:230
  59.8 0.0 collective-permute-done.3.rest_0_.refs_0_
  59.9 1.0 pieces.7
  60.8 3.1 %collective-permute-start.6 = (bf16[512,256]{1,0:T(8,128)(2,1)S(1)}, bf16[512,256]{1,0:T(8,128)(2,1)S(1)}, u32[]{:S(2)}, u32[]{:S(2)}) collective-permute-start(bf16[512,256]{1,0:T(8,128)(2,1)S(1)} %get-tuple-element.45), channel_id=1, source_target_pairs={{0,16},{4,20},{8,24},{12,28},{16,0},{20,4},{24,8},{28,12},{1,17},{... | collective-permute-start | bytes 786440 | tf_op jit(solution)/shard_map/ppermute | solution.py:462
  63.9 4.3 %backward.7 = (f32[512,1152]{1,0:T(8,128)}, bf16[512,1152]{1,0:T(8,128)(2,1)}, f32[1,512]{1,0:T(1,128)S(1)}) custom-call(s32[1]{0:T(128)S(6)} %copy.22.evicted_ref, bf16[1,2,512,1536]{3,2,1,0:T(8,128)(2,1)} %own_ref.9, bf16[1,512,1536]{2,1,0:T(8,128)(2,1)} %g_ref.9, f32[3,512]{1,0:T(4,128)S(1)} %psum.14.t_ref, ...), custom_call_target="tpu_custom_call", output_to_operand_aliasing={{0}: (9, {}), {1}: (10, {})} | custom-call | tf_op jit(solution)/shard_map/backward/pallas_call | solution.py:230
  68.2 0.0 collective-permute-done.4.refs_0_
  68.2 4.3 %backward.8 = (f32[512,1152]{1,0:T(8,128)}, bf16[512,1152]{1,0:T(8,128)(2,1)}, f32[1,512]{1,0:T(1,128)S(1)}) custom-call(s32[1]{0:T(128)S(6)} %copy.22.evicted_ref, bf16[1,2,512,1536]{3,2,1,0:T(8,128)(2,1)} %own_ref.9, bf16[1,512,1536]{2,1,0:T(8,128)(2,1)} %g_ref.9, f32[3,512]{1,0:T(4,128)S(1)} %psum.14.t_ref, ...), custom_call_target="tpu_custom_call", output_to_operand_aliasing={{0}: (9, {}), {1}: (10, {})} | custom-call | tf_op jit(solution)/shard_map/backward/pallas_call | solution.py:230
  72.6 6.6 %collective-permute-start.5 = (bf16[512,768]{1,0:T(8,128)(2,1)S(1)}, bf16[512,768]{1,0:T(8,128)(2,1)S(1)}, u32[]{:S(2)}, u32[]{:S(2)}) collective-permute-start(bf16[512,768]{1,0:T(8,128)(2,1)S(1)} %hold.1), channel_id=1, source_target_pairs={{0,28},{4,0},{8,4},{12,8},{16,12},{20,16},{24,20},{28,24},{1,29},{... | collective-permute-start | bytes 2359304 | tf_op jit(solution)/shard_map/ppermute | solution.py:462
  79.2 0.0 collective-permute-done.6.refs_0_
  79.2 4.3 %backward.9 = (f32[512,1152]{1,0:T(8,128)}, bf16[512,1152]{1,0:T(8,128)(2,1)}, f32[1,512]{1,0:T(1,128)S(1)}) custom-call(s32[1]{0:T(128)S(6)} %copy.22.evicted_ref, bf16[1,2,512,1536]{3,2,1,0:T(8,128)(2,1)} %own_ref.9, bf16[1,512,1536]{2,1,0:T(8,128)(2,1)} %g_ref.9, f32[3,512]{1,0:T(4,128)S(1)} %psum.14.t_ref, ...), custom_call_target="tpu_custom_call", output_to_operand_aliasing={{0}: (9, {}), {1}: (10, {})} | custom-call | tf_op jit(solution)/shard_map/backward/pallas_call | solution.py:230
  83.5 5.8 %psum.15.inner_ref = f32[1,512]{1,0:T(1,128)S(1)} all-reduce(f32[1,512]{1,0:T(1,128)S(1)} %get-tuple-element.50), channel_id=1, replica_groups=mesh['section'=8,'tensor'=4] {'tensor'}, use_global_device_ids=true, to_apply=%region_1.0 | all-reduce | flops 512 | bytes 4096 | tf_op jit(solution)/shard_map/psum | solution.py:510
  89.3 1.7 %finish.2 = (bf16[512,640]{1,0:T(8,128)(2,1)S(1)}, f32[1,512]{1,0:T(1,128)S(1)}) custom-call(s32[1]{0:T(128)S(6)} %copy.22.evicted_ref, f32[512,1152]{1,0:T(8,128)} %get-tuple-element.48.a_ref, bf16[512,1152]{1,0:T(8,128)(2,1)} %get-tuple-element.49.x_ref, f32[3,512]{1,0:T(4,128)S(1)} %psum.14.t_ref, f32[1,512]{1,0:T(1,128)S(1)} %row.1.held_ref, ...), custom_call_target="tpu_custom_call" | custom-call | tf_op jit(solution)/shard_map/finish/pallas_call | solution.py:276
  91.1 1.4 %collective-permute-start.8 = (bf16[512,640]{1,0:T(8,128)(2,1)S(1)}, bf16[512,640]{1,0:T(8,128)(2,1)S(1)}, u32[]{:S(2)}, u32[]{:S(2)}) collective-permute-start(bf16[512,640]{1,0:T(8,128)(2,1)S(1)} %get-tuple-element.52), channel_id=1, source_target_pairs={{0,28},{4,0},{8,4},{12,8},{16,12},{20,16},{24,20},{28,24},{1,29},{... | collective-permute-start | bytes 1966088 | tf_op jit(solution)/shard_map/ppermute | solution.py:462
  92.5 2.0 %finish.3 = (bf16[512,512]{1,0:T(8,128)(2,1)S(1)}, f32[1,512]{1,0:T(1,128)}) custom-call(s32[1]{0:T(128)S(6)} %copy.22.evicted_ref, f32[512,1152]{1,0:T(8,128)} %get-tuple-element.48.a_ref, bf16[512,1152]{1,0:T(8,128)(2,1)} %get-tuple-element.49.x_ref, f32[3,512]{1,0:T(4,128)S(1)} %psum.14.t_ref, f32[1,512]{1,0:T(1,128)S(1)} %row.1.held_ref, ...), custom_call_target="tpu_custom_call" | custom-call | tf_op jit(solution)/shard_map/finish/pallas_call | solution.py:276
  94.5 0.6 collective-permute-start.9
  95.1 0.1 collective-permute-start.7
  95.1 25.7 %collective-permute-done.7.row_ref = f32[1,512]{1,0:T(1,128)S(1)} collective-permute-done((f32[1,512]{1,0:T(1,128)S(1)}, f32[1,512]{1,0:T(1,128)S(1)}, u32[]{:S(2)}, u32[]{:S(2)}) %collective-permute-start.7) | collective-permute-done | bytes 2080 | tf_op jit(solution)/shard_map/ppermute | solution.py:462
  120.8 0.0 collective-permute-done.9.refs_1_
  120.8 0.0 collective-permute-done.8.refs_0_
  120.9 0.0 collective-permute-done.5.pair_ref
  120.9 1.2 place.1
  (3 shorter events, 0.0 us)
Async XLA Ops:
  1.7 0.6 copy-start.2
  2.3 22.4 %collective-permute-start = (bf16[512,256]{1,0:T(8,128)(2,1)S(1)}, bf16[512,256]{1,0:T(8,128)(2,1)S(1)}, u32[]{:S(2)}, u32[]{:S(2)}) collective-permute-start(bf16[512,256]{1,0:T(8,128)(2,1)S(1)} %get-tuple-element.29), channel_id=1, source_target_pairs={{0,16},{4,20},{8,24},{12,28},{16,0},{20,4},{24,8},{28,12},{1,17},{... | collective-permute-start | bytes 786440 | tf_op jit(solution)/shard_map/ppermute | solution.py:462
  6.3 29.8 %collective-permute-start.2 = (bf16[512,256]{1,0:T(8,128)(2,1)S(1)}, bf16[512,256]{1,0:T(8,128)(2,1)S(1)}, u32[]{:S(2)}, u32[]{:S(2)}) collective-permute-start(bf16[512,256]{1,0:T(8,128)(2,1)S(1)} %get-tuple-element.30), channel_id=1, source_target_pairs={{0,16},{4,20},{8,24},{12,28},{16,0},{20,4},{24,8},{28,12},{1,17},{... | collective-permute-start | bytes 786440 | tf_op jit(solution)/shard_map/ppermute | solution.py:462
  17.6 8.1 %copy-start = (f32[1,1536]{1,0:T(1,128)S(1)}, f32[1,1536]{1,0:T(1,128)}, u32[]{:S(2)}) copy-start(f32[1,1536]{1,0:T(1,128)} %gq_ref.11) | copy-start | bytes 18436
  17.7 8.1 %copy-start.1 = (f32[1,1536]{1,0:T(1,128)S(1)}, f32[1,1536]{1,0:T(1,128)}, u32[]{:S(2)}) copy-start(f32[1,1536]{1,0:T(1,128)} %gk_ref.11) | copy-start | bytes 18436
  25.7 21.9 %collective-permute-start.1 = (bf16[528,256]{1,0:T(8,128)(2,1)S(1)}, bf16[528,256]{1,0:T(8,128)(2,1)S(1)}, u32[]{:S(2)}, u32[]{:S(2)}) collective-permute-start(bf16[528,256]{1,0:T(8,128)(2,1)S(1)} %piece_and_row.1), channel_id=1, source_target_pairs={{0,16},{4,20},{8,24},{12,28},{16,0},{20,4},{24,8},{28,12},{1,17},{... | collective-permute-start | bytes 811016 | tf_op jit(solution)/shard_map/ppermute | solution.py:462
  37.1 22.8 %collective-permute-start.3 = (bf16[512,256]{1,0:T(8,128)(2,1)S(1)}, bf16[512,256]{1,0:T(8,128)(2,1)S(1)}, u32[]{:S(2)}, u32[]{:S(2)}) collective-permute-start(bf16[512,256]{1,0:T(8,128)(2,1)S(1)} %get-tuple-element.36), channel_id=1, source_target_pairs={{0,16},{4,20},{8,24},{12,28},{16,0},{20,4},{24,8},{28,12},{1,17},{... | collective-permute-start | bytes 786440 | tf_op jit(solution)/shard_map/ppermute | solution.py:462
  48.5 19.7 %collective-permute-start.4 = (bf16[512,256]{1,0:T(8,128)(2,1)S(1)}, bf16[512,256]{1,0:T(8,128)(2,1)S(1)}, u32[]{:S(2)}, u32[]{:S(2)}) collective-permute-start(bf16[512,256]{1,0:T(8,128)(2,1)S(1)} %get-tuple-element.41), channel_id=1, source_target_pairs={{0,16},{4,20},{8,24},{12,28},{16,0},{20,4},{24,8},{28,12},{1,17},{... | collective-permute-start | bytes 786440 | tf_op jit(solution)/shard_map/ppermute | solution.py:462
  60.8 18.4 %collective-permute-start.6 = (bf16[512,256]{1,0:T(8,128)(2,1)S(1)}, bf16[512,256]{1,0:T(8,128)(2,1)S(1)}, u32[]{:S(2)}, u32[]{:S(2)}) collective-permute-start(bf16[512,256]{1,0:T(8,128)(2,1)S(1)} %get-tuple-element.45), channel_id=1, source_target_pairs={{0,16},{4,20},{8,24},{12,28},{16,0},{20,4},{24,8},{28,12},{1,17},{... | collective-permute-start | bytes 786440 | tf_op jit(solution)/shard_map/ppermute | solution.py:462
  72.6 48.3 %collective-permute-start.5 = (bf16[512,768]{1,0:T(8,128)(2,1)S(1)}, bf16[512,768]{1,0:T(8,128)(2,1)S(1)}, u32[]{:S(2)}, u32[]{:S(2)}) collective-permute-start(bf16[512,768]{1,0:T(8,128)(2,1)S(1)} %hold.1), channel_id=1, source_target_pairs={{0,28},{4,0},{8,4},{12,8},{16,12},{20,16},{24,20},{28,24},{1,29},{... | collective-permute-start | bytes 2359304 | tf_op jit(solution)/shard_map/ppermute | solution.py:462
  91.1 29.8 %collective-permute-start.8 = (bf16[512,640]{1,0:T(8,128)(2,1)S(1)}, bf16[512,640]{1,0:T(8,128)(2,1)S(1)}, u32[]{:S(2)}, u32[]{:S(2)}) collective-permute-start(bf16[512,640]{1,0:T(8,128)(2,1)S(1)} %get-tuple-element.52), channel_id=1, source_target_pairs={{0,28},{4,0},{8,4},{12,8},{16,12},{20,16},{24,20},{28,24},{1,29},{... | collective-permute-start | bytes 1966088 | tf_op jit(solution)/shard_map/ppermute | solution.py:462
  94.5 26.3 %collective-permute-start.9 = (bf16[512,512]{1,0:T(8,128)(2,1)S(1)}, bf16[512,512]{1,0:T(8,128)(2,1)S(1)}, u32[]{:S(2)}, u32[]{:S(2)}) collective-permute-start(bf16[512,512]{1,0:T(8,128)(2,1)S(1)} %get-tuple-element.53), channel_id=1, source_target_pairs={{0,28},{4,0},{8,4},{12,8},{16,12},{20,16},{24,20},{28,24},{1,29},{... | collective-permute-start | bytes 1572872 | tf_op jit(solution)/shard_map/ppermute | solution.py:462
  95.1 25.8 %collective-permute-start.7 = (f32[1,512]{1,0:T(1,128)S(1)}, f32[1,512]{1,0:T(1,128)S(1)}, u32[]{:S(2)}, u32[]{:S(2)}) collective-permute-start(f32[1,512]{1,0:T(1,128)S(1)} %get-tuple-element.51), channel_id=1, source_target_pairs={{0,28},{4,0},{8,4},{12,8},{16,12},{20,16},{24,20},{28,24},{1,29},{... | collective-permute-start | bytes 6152 | tf_op jit(solution)/shard_map/ppermute | solution.py:462

commit v22 on v21

--- a/solution.py
+++ b/solution.py
@@ -14,6 +14,7 @@
 LOG2E = math.log2(math.e)
 VMEM = 32 * 1024 * 1024
 MOST = 60 * 1024 * 1024
+PARTS = 4
 
 F32 = jnp.float32
 BF16 = jnp.bfloat16
@@ -245,8 +246,9 @@
 
 
 def finish_kernel(
-    first, width_all, evicted_ref, a_ref, x_ref, t_ref, held_ref, inner_ref, o_ref, row_ref, terms, xs, a_sem, x_sem
+    first, width_all, evicted_ref, a_ref, x_ref, t_ref, held_ref, inner_ref, o_ref, terms, xs, a_sem, x_sem
 ):
+    tokens = a_ref.shape[0]
     heads = o_ref.shape[1] // HDIM
     copies = []
     for h in range(heads):
@@ -261,38 +263,42 @@
         for copy in copies[-1]:
             copy.start()
     row = row_of(total_of(evicted_ref, t_ref, held_ref), inner_ref[...], width_all)
-    row_ref[...] = row
+    if o_ref.shape[0] > tokens:
+        o_ref[tokens:, :] = in_rows(row, o_ref.shape[1])
     column = column_of(row)
     for h in range(heads):
         mine = lanes_of(h * HDIM, HDIM)
         for copy in copies[h]:
             copy.wait()
-        o_ref[mine] = (terms[mine] - xs[mine].astype(F32) * column).astype(BF16)
-
-
-def finish(width_all, evicted, a, x, totals, held, inner, first, last):
-    shape = (a.shape[0], last - first)
+        o_ref[:tokens, mine[1]] = (terms[mine] - xs[mine].astype(F32) * column).astype(BF16)
+
+
+def finish(width_all, evicted, a, x, totals, held, inner, first, last, carry):
+    tokens = a.shape[0]
+    shape = (tokens, last - first)
     dma = pltpu.SemaphoreType.DMA(((last - first) // HDIM,))
     return pl.pallas_call(
         functools.partial(finish_kernel, first, width_all),
-        out_shape=(jax.ShapeDtypeStruct(shape, BF16), jax.ShapeDtypeStruct((1, a.shape[0]), F32)),
+        out_shape=jax.ShapeDtypeStruct((tokens + carry * below(tokens, last - first), last - first), BF16),
         in_specs=[pl.BlockSpec(memory_space=pltpu.SMEM)] + [IN_HBM] * 2 + [IN_VMEM] * 3,
-        out_specs=(IN_VMEM, IN_VMEM),
+        out_specs=IN_VMEM,
         scratch_shapes=[pltpu.VMEM(shape, F32), pltpu.VMEM(shape, BF16), dma, dma],
         compiler_params=compiler(VMEM),
         name="finish",
     )(evicted, in_hbm(a), in_hbm(x), totals, held, inner)
 
 
-def place_kernel(pair_ref, row_ref, *refs):
-    rest_refs, (o_ref, outs, sems) = refs[:-3], refs[-3:]
-    lanes = outs.shape[1]
+def place_kernel(pair_ref, *refs):
+    rest_refs, (o_ref, outs, row_ref, sems) = refs[:-4], refs[-4:]
+    tokens, lanes = outs.shape
     ahead = lanes // HDIM
     copies, at = [], lanes
     for i, ref in enumerate(rest_refs):
-        copies.append(pltpu.make_async_copy(ref, o_ref.at[lanes_of(at, ref.shape[1])], sems.at[ahead + i]))
+        to = o_ref.at[lanes_of(at, ref.shape[1])]
+        copies.append(pltpu.make_async_copy(ref.at[:tokens, :], to, sems.at[ahead + i]))
         copies[-1].start()
         at += ref.shape[1]
+    row_out_of(rest_refs[-1][tokens:, :], row_ref)
     row = column_of(row_ref[...])
     for h in range(ahead):
         mine = lanes_of(h * HDIM, HDIM)
@@ -304,17 +310,21 @@
         copy.wait()
 
 
-def place(pair, row, *rest):
+def place(pair, *rest):
     tokens, lanes = pair.shape[0], pair.shape[1] // 2
     return pl.pallas_call(
         place_kernel,
         out_shape=jax.ShapeDtypeStruct((tokens, lanes + sum(r.shape[1] for r in rest)), BF16),
-        in_specs=[IN_VMEM] * (2 + len(rest)),
+        in_specs=[IN_VMEM] * (1 + len(rest)),
         out_specs=ANYWHERE,
-        scratch_shapes=[pltpu.VMEM((tokens, lanes), BF16), pltpu.SemaphoreType.DMA((lanes // HDIM + len(rest),))],
+        scratch_shapes=[
+            pltpu.VMEM((tokens, lanes), BF16),
+            pltpu.VMEM((1, tokens), F32),
+            pltpu.SemaphoreType.DMA((lanes // HDIM + len(rest),)),
+        ],
         compiler_params=compiler(VMEM),
         name="place",
-    )(pair, row, *rest)
+    )(pair, *rest)
 
 
 def hold_kernel(x_ref, *rest):
@@ -413,12 +423,20 @@
     return jnp.concatenate(rows + [jnp.zeros((fill, size), BF16)] * (fill > 0), axis=0)
 
 
+def below(tokens, size):
+    return -(-3 * tokens // size // 16) * 16
+
+
+def row_out_of(extra, row_ref):
+    tokens, size = row_ref.shape[1], extra.shape[1]
+    each = tokens // size
+    extra = extra.astype(F32)
+    for i in range(each):
+        row_ref[:, i * size : (i + 1) * size] = sum(extra[p * each + i : p * each + i + 1] for p in range(3))
+
+
 def row_kernel(extra_ref, o_ref):
-    tokens, size = o_ref.shape[1], extra_ref.shape[1]
-    each = tokens // size
-    extra = extra_ref[...].astype(F32)
-    for i in range(each):
-        o_ref[:, i * size : (i + 1) * size] = sum(extra[p * each + i : p * each + i + 1] for p in range(3))
+    row_out_of(extra_ref[...], o_ref)
 
 
 def row_from(piece, tokens):
@@ -446,7 +464,7 @@
 
 def piece_and_row(stash, totals, start, size, after):
     tokens = stash.shape[2]
-    extra = -(-3 * tokens // size // 16) * 16
+    extra = below(tokens, size)
     return pl.pallas_call(
         functools.partial(piece_and_row_kernel, start),
         out_shape=jax.ShapeDtypeStruct((tokens + extra, size), BF16),
@@ -487,7 +505,7 @@
     fetched.append(send(piece_and_row(stashed, totals, 2 * size, size, (fetched[0],)), partner))
     held = row_from(fetched[2], tokens)
     marks = [fetch(p, in_hbm(output)) for p in range(3, min(5, pieces))]
-    base = max(1, count // 4) * HDIM
+    base = each * HDIM
 
     def share(inner, first, last, sofar, after):
         heads = range(first // HDIM, last // HDIM)
@@ -508,13 +526,15 @@
         marks = [fetch(p, inner) for p in range(len(fetched), pieces)]
     pair = send(hold(pair, (inners[-2],)), prior)
     inner = lax.psum(inner, "tensor")
-    left = width - base
-    cut = (left // HDIM + 1) // 2 * HDIM
+    left = (width - base) // HDIM
     ends = (*sofar, totals, held, inner)
-    early, row = finish(width_all, eviction, *ends, 0, cut)
-    early = send(early, prior)
-    late, _ = finish(width_all, eviction, *ends, cut, left)
-    result = place(pair, send(row, prior), early, send(late, prior))
+    cuts = [-(-left * i // PARTS) * HDIM for i in range(PARTS + 1)]
+    cuts = sorted(set(cuts))
+    rests = [
+        send(finish(width_all, eviction, *ends, first, last, last == cuts[-1]), prior)
+        for first, last in zip(cuts[:-1], cuts[1:])
+    ]
+    result = place(pair, *rests)
     return (output[None], result[None])
 
 

time: 123 us -> 125 us (1.016)
  starting transfers between devices: 16.9 us -> 18.8 us
  waiting for transfers between devices: 44.1 us -> 42.6 us
  Pallas kernels: 46.5 us -> 47.9 us
    ppermute x10 -> x11, starting transfers between devices: 16.9 us -> 18.8 us  [send(): return lax.ppermute(x, 'section', pairs)]
    ppermute x10 -> x11, waiting for transfers between devices: 44.1 us -> 42.6 us  [send(): return lax.ppermute(x, 'section', pairs)]
    pallas_call x2 -> x4, Pallas kernels: 3.76 us -> 5.13 us  [finish(): pl.pallas_call(functools.partial(finish_kernel, first, width_all), out_sh...]
  transfers between devices with their start and end apart: 10 -> 11, of which waited for: 4 -> 4; matrix products, arithmetic and copies ran while one was open for 0% -> 0% of each run, Pallas kernels for 36% -> 37%
where the time goes in v22:
time: 125 us; the launch traced here: 124 us
  Pallas kernels  47.9 us (38%)
  waiting for transfers between devices  42.6 us (34%)
  starting transfers between devices  18.8 us (15%)
  blocking collectives  12.4 us (10%)
  between operations  1.67 us (1%)
    ppermute x11, waiting for transfers between devices, send(): return lax.ppermute(x, 'section', pairs)  42.6 us
    pallas_call x5, Pallas kernels, backward(): pl.pallas_call(functools.partial(backward_kernel, first, base, found, wid...  23.5 us
    ppermute x11, starting transfers between devices, send(): return lax.ppermute(x, 'section', pairs)  18.8 us
    pallas_call x1, Pallas kernels, forward(): pl.pallas_call(functools.partial(forward_kernel, heads, width_all), out_s...  8.39 us
    psum x1, blocking collectives, local(): totals = lax.psum(squares(current, stashed, third, (mark,)), 'tensor')  6.53 us
    psum x1, blocking collectives, local(): inner = lax.psum(inner, 'tensor')  5.84 us
    pallas_call x4, Pallas kernels, finish(): pl.pallas_call(functools.partial(finish_kernel, first, width_all), out_sh...  5.13 us
    pallas_call x1, Pallas kernels, squares(): pl.pallas_call(squares_kernel, out_shape=jax.ShapeDtypeStruct((3, tokens)...  4.74 us
  transfers between devices with their start and end apart: 11, of which 4 were waited for; matrix products, arithmetic and copies ran while one was open for 0% of the time, Pallas kernels for 37%

profile of v22, /device:TPU:0, one launch (start us, length us, event | category | flops | bytes accessed | tf_op | source)
XLA Modules:
  0.0 124.0 jit_solution(14187269797851670305)
XLA Ops:
  0.6 1.1 pieces.4
  1.7 0.0 copy-start.2
  1.7 0.6 copy-done.2
  2.3 4.0 %collective-permute-start = (bf16[512,256]{1,0:T(8,128)(2,1)S(1)}, bf16[512,256]{1,0:T(8,128)(2,1)S(1)}, u32[]{:S(2)}, u32[]{:S(2)}) collective-permute-start(bf16[512,256]{1,0:T(8,128)(2,1)S(1)} %get-tuple-element.26), channel_id=1, source_target_pairs={{0,16},{4,20},{8,24},{12,28},{16,0},{20,4},{24,8},{28,12},{1,17},{... | collective-permute-start | bytes 786440 | tf_op jit(solution)/shard_map/ppermute | solution.py:480
  6.3 0.0 collective-permute-start.2
  6.4 4.7 %squares.1 = f32[3,512]{1,0:T(4,128)} custom-call(bf16[512,1536]{1,0:T(8,128)(2,1)} %bitcast.4, bf16[1,2,512,1536]{3,2,1,0:T(8,128)(2,1)} %own_ref.9, f32[8,128]{1,0:T(8,128)} %copy-done.2), custom_call_target="tpu_custom_call" | custom-call | tf_op jit(solution)/shard_map/squares/pallas_call | solution.py:374
  11.1 6.5 %psum.14.t_ref = f32[3,512]{1,0:T(4,128)S(1)} all-reduce(f32[3,512]{1,0:T(4,128)} %squares.1), channel_id=1, replica_groups=mesh['section'=8,'tensor'=4] {'tensor'}, use_global_device_ids=true, to_apply=%region_0.0 | all-reduce | flops 1536 | bytes 12288 | tf_op jit(solution)/shard_map/psum | solution.py:497
  17.6 0.0 copy-start
  17.7 0.0 copy-start.1
  17.7 7.0 %collective-permute-done.rest_0_.refs_0_ = bf16[512,256]{1,0:T(8,128)(2,1)S(1)} collective-permute-done((bf16[512,256]{1,0:T(8,128)(2,1)S(1)}, bf16[512,256]{1,0:T(8,128)(2,1)S(1)}, u32[]{:S(2)}, u32[]{:S(2)}) %collective-permute-start) | collective-permute-done | bytes 262176 | tf_op jit(solution)/shard_map/ppermute | solution.py:480
  24.7 1.0 piece_and_row.1
  25.7 0.1 collective-permute-start.1
  25.7 0.0 copy-done
  25.7 0.0 copy-done.1
  25.8 8.4 %forward.1.rest_1_.refs_1_ = bf16[512,1536]{1,0:T(8,128)(2,1)} custom-call(bf16[512,1536]{1,0:T(8,128)(2,1)} %bitcast.5, f32[3,512]{1,0:T(4,128)S(1)} %psum.14.t_ref, f32[1,1536]{1,0:T(1,128)S(1)} %copy-done, f32[1,1536]{1,0:T(1,128)S(1)} %copy-done.1), custom_call_target="tpu_custom_call" | custom-call | tf_op jit(solution)/shard_map/forward/pallas_call | solution.py:120
  34.1 2.0 %collective-permute-done.2.rest_0_.refs_0_ = bf16[512,256]{1,0:T(8,128)(2,1)S(1)} collective-permute-done((bf16[512,256]{1,0:T(8,128)(2,1)S(1)}, bf16[512,256]{1,0:T(8,128)(2,1)S(1)}, u32[]{:S(2)}, u32[]{:S(2)}) %collective-permute-start.2) | collective-permute-done | bytes 262176 | tf_op jit(solution)/shard_map/ppermute | solution.py:480
  36.1 1.0 pieces.5
  37.1 1.0 collective-permute-start.3
  38.1 9.4 %collective-permute-done.1.extra_ref.rest_0_.refs_1_ = bf16[528,256]{1,0:T(8,128)(2,1)S(1)} collective-permute-done((bf16[528,256]{1,0:T(8,128)(2,1)S(1)}, bf16[528,256]{1,0:T(8,128)(2,1)S(1)}, u32[]{:S(2)}, u32[]{:S(2)}) %collective-permute-start.1) | collective-permute-done | bytes 270368 | tf_op jit(solution)/shard_map/ppermute | solution.py:480
  47.5 1.0 pieces.6
  48.5 0.1 collective-permute-start.4
  49.2 3.7 %backward.5 = (bf16[512,512]{1,0:T(8,128)(2,1)S(1)}, f32[1,512]{1,0:T(1,128)S(1)}) custom-call(s32[1]{0:T(128)S(6)} %copy.22.evicted_ref, bf16[1,2,512,1536]{3,2,1,0:T(8,128)(2,1)} %own_ref.9, bf16[1,512,1536]{2,1,0:T(8,128)(2,1)} %g_ref.9, f32[3,512]{1,0:T(4,128)S(1)} %psum.14.t_ref, f32[1,512]{1,0:T(1,128)S(1)} %row.1.held_ref, f32[1,1536]{1,0:T(1,128)S(1)} %copy-done, ...), custom_call_target="tpu_custom_call" | custom-call | tf_op jit(solution)/shard_map/backward/pallas_call | solution.py:231
  52.9 6.9 %backward.6 = (f32[512,1280]{1,0:T(8,128)}, bf16[512,1280]{1,0:T(8,128)(2,1)}, f32[1,512]{1,0:T(1,128)S(1)}) custom-call(s32[1]{0:T(128)S(6)} %copy.22.evicted_ref, bf16[1,2,512,1536]{3,2,1,0:T(8,128)(2,1)} %own_ref.9, bf16[1,512,1536]{2,1,0:T(8,128)(2,1)} %g_ref.9, f32[3,512]{1,0:T(4,128)S(1)} %psum.14.t_ref, f32[1,512]{1,0:T(1,128)S(1)} %row.1.held_ref, ...), custom_call_target="tpu_custom_call" | custom-call | tf_op jit(solution)/shard_map/backward/pallas_call | solution.py:231
  59.9 0.0 collective-permute-done.3.rest_0_.refs_0_
  59.9 1.0 pieces.7
  60.8 3.1 %collective-permute-start.6 = (bf16[512,256]{1,0:T(8,128)(2,1)S(1)}, bf16[512,256]{1,0:T(8,128)(2,1)S(1)}, u32[]{:S(2)}, u32[]{:S(2)}) collective-permute-start(bf16[512,256]{1,0:T(8,128)(2,1)S(1)} %get-tuple-element.42), channel_id=1, source_target_pairs={{0,16},{4,20},{8,24},{12,28},{16,0},{20,4},{24,8},{28,12},{1,17},{... | collective-permute-start | bytes 786440 | tf_op jit(solution)/shard_map/ppermute | solution.py:480
  63.9 4.3 %backward.7 = (f32[512,1280]{1,0:T(8,128)}, bf16[512,1280]{1,0:T(8,128)(2,1)}, f32[1,512]{1,0:T(1,128)S(1)}) custom-call(s32[1]{0:T(128)S(6)} %copy.22.evicted_ref, bf16[1,2,512,1536]{3,2,1,0:T(8,128)(2,1)} %own_ref.9, bf16[1,512,1536]{2,1,0:T(8,128)(2,1)} %g_ref.9, f32[3,512]{1,0:T(4,128)S(1)} %psum.14.t_ref, ...), custom_call_target="tpu_custom_call", output_to_operand_aliasing={{0}: (9, {}), {1}: (10, {})} | custom-call | tf_op jit(solution)/shard_map/backward/pallas_call | solution.py:231
  68.2 0.0 collective-permute-done.4.refs_0_
  68.3 4.3 %backward.8 = (f32[512,1280]{1,0:T(8,128)}, bf16[512,1280]{1,0:T(8,128)(2,1)}, f32[1,512]{1,0:T(1,128)S(1)}) custom-call(s32[1]{0:T(128)S(6)} %copy.22.evicted_ref, bf16[1,2,512,1536]{3,2,1,0:T(8,128)(2,1)} %own_ref.9, bf16[1,512,1536]{2,1,0:T(8,128)(2,1)} %g_ref.9, f32[3,512]{1,0:T(4,128)S(1)} %psum.14.t_ref, ...), custom_call_target="tpu_custom_call", output_to_operand_aliasing={{0}: (9, {}), {1}: (10, {})} | custom-call | tf_op jit(solution)/shard_map/backward/pallas_call | solution.py:231
  72.6 6.5 %collective-permute-start.5 = (bf16[512,512]{1,0:T(8,128)(2,1)S(1)}, bf16[512,512]{1,0:T(8,128)(2,1)S(1)}, u32[]{:S(2)}, u32[]{:S(2)}) collective-permute-start(bf16[512,512]{1,0:T(8,128)(2,1)S(1)} %hold.1), channel_id=1, source_target_pairs={{0,28},{4,0},{8,4},{12,8},{16,12},{20,16},{24,20},{28,24},{1,29},{... | collective-permute-start | bytes 1572872 | tf_op jit(solution)/shard_map/ppermute | solution.py:480
  79.1 0.0 collective-permute-done.6.refs_0_
  79.1 4.3 %backward.9 = (f32[512,1280]{1,0:T(8,128)}, bf16[512,1280]{1,0:T(8,128)(2,1)}, f32[1,512]{1,0:T(1,128)S(1)}) custom-call(s32[1]{0:T(128)S(6)} %copy.22.evicted_ref, bf16[1,2,512,1536]{3,2,1,0:T(8,128)(2,1)} %own_ref.9, bf16[1,512,1536]{2,1,0:T(8,128)(2,1)} %g_ref.9, f32[3,512]{1,0:T(4,128)S(1)} %psum.14.t_ref, ...), custom_call_target="tpu_custom_call", output_to_operand_aliasing={{0}: (9, {}), {1}: (10, {})} | custom-call | tf_op jit(solution)/shard_map/backward/pallas_call | solution.py:231
  83.4 5.8 %psum.15.inner_ref = f32[1,512]{1,0:T(1,128)S(1)} all-reduce(f32[1,512]{1,0:T(1,128)S(1)} %get-tuple-element.47), channel_id=1, replica_groups=mesh['section'=8,'tensor'=4] {'tensor'}, use_global_device_ids=true, to_apply=%region_1.0 | all-reduce | flops 512 | bytes 4096 | tf_op jit(solution)/shard_map/psum | solution.py:528
  89.3 1.4 %finish.6 = bf16[512,384]{1,0:T(8,128)(2,1)S(1)} custom-call(s32[1]{0:T(128)S(6)} %copy.22.evicted_ref, f32[512,1280]{1,0:T(8,128)} %get-tuple-element.45.a_ref, bf16[512,1280]{1,0:T(8,128)(2,1)} %get-tuple-element.46.x_ref, f32[3,512]{1,0:T(4,128)S(1)} %psum.14.t_ref, f32[1,512]{1,0:T(1,128)S(1)} %row.1.held_ref, f32[1,512]{1,0:T(1,128)S(1)} %psum.15.inner_ref), custom_call_target="tpu_custom_call" | custom-call | tf_op jit(solution)/shard_map/finish/pallas_call | solution.py:280
  90.6 1.4 %finish.4 = bf16[512,384]{1,0:T(8,128)(2,1)S(1)} custom-call(s32[1]{0:T(128)S(6)} %copy.22.evicted_ref, f32[512,1280]{1,0:T(8,128)} %get-tuple-element.45.a_ref, bf16[512,1280]{1,0:T(8,128)(2,1)} %get-tuple-element.46.x_ref, f32[3,512]{1,0:T(4,128)S(1)} %psum.14.t_ref, f32[1,512]{1,0:T(1,128)S(1)} %row.1.held_ref, f32[1,512]{1,0:T(1,128)S(1)} %psum.15.inner_ref), custom_call_target="tpu_custom_call" | custom-call | tf_op jit(solution)/shard_map/finish/pallas_call | solution.py:280
  92.0 1.4 %collective-permute-start.7 = (bf16[512,384]{1,0:T(8,128)(2,1)S(1)}, bf16[512,384]{1,0:T(8,128)(2,1)S(1)}, u32[]{:S(2)}, u32[]{:S(2)}) collective-permute-start(bf16[512,384]{1,0:T(8,128)(2,1)S(1)} %finish.4), channel_id=1, source_target_pairs={{0,28},{4,0},{8,4},{12,8},{16,12},{20,16},{24,20},{28,24},{1,29},{... | collective-permute-start | bytes 1179656 | tf_op jit(solution)/shard_map/ppermute | solution.py:480
  93.4 0.5 collective-permute-start.9
  93.9 1.2 finish.7
  95.1 0.1 collective-permute-start.10
  95.2 1.2 finish.5
  96.5 2.0 %collective-permute-start.8 = (bf16[512,256]{1,0:T(8,128)(2,1)S(1)}, bf16[512,256]{1,0:T(8,128)(2,1)S(1)}, u32[]{:S(2)}, u32[]{:S(2)}) collective-permute-start(bf16[512,256]{1,0:T(8,128)(2,1)S(1)} %finish.5), channel_id=1, source_target_pairs={{0,28},{4,0},{8,4},{12,8},{16,12},{20,16},{24,20},{28,24},{1,29},{... | collective-permute-start | bytes 786440 | tf_op jit(solution)/shard_map/ppermute | solution.py:480
  98.4 24.2 %collective-permute-done.8.refs_1_ = bf16[512,256]{1,0:T(8,128)(2,1)S(1)} collective-permute-done((bf16[512,256]{1,0:T(8,128)(2,1)S(1)}, bf16[512,256]{1,0:T(8,128)(2,1)S(1)}, u32[]{:S(2)}, u32[]{:S(2)}) %collective-permute-start.8) | collective-permute-done | bytes 262176 | tf_op jit(solution)/shard_map/ppermute | solution.py:480
  122.6 0.0 collective-permute-done.10.refs_3_
  122.6 0.0 collective-permute-done.7.refs_0_
  122.6 0.0 collective-permute-done.9.refs_2_
  122.6 0.0 collective-permute-done.5.pair_ref
  122.6 1.2 place.1
  (3 shorter events, 0.0 us)
Async XLA Ops:
  1.7 0.6 copy-start.2
  2.3 22.4 %collective-permute-start = (bf16[512,256]{1,0:T(8,128)(2,1)S(1)}, bf16[512,256]{1,0:T(8,128)(2,1)S(1)}, u32[]{:S(2)}, u32[]{:S(2)}) collective-permute-start(bf16[512,256]{1,0:T(8,128)(2,1)S(1)} %get-tuple-element.26), channel_id=1, source_target_pairs={{0,16},{4,20},{8,24},{12,28},{16,0},{20,4},{24,8},{28,12},{1,17},{... | collective-permute-start | bytes 786440 | tf_op jit(solution)/shard_map/ppermute | solution.py:480
  6.3 29.8 %collective-permute-start.2 = (bf16[512,256]{1,0:T(8,128)(2,1)S(1)}, bf16[512,256]{1,0:T(8,128)(2,1)S(1)}, u32[]{:S(2)}, u32[]{:S(2)}) collective-permute-start(bf16[512,256]{1,0:T(8,128)(2,1)S(1)} %get-tuple-element.27), channel_id=1, source_target_pairs={{0,16},{4,20},{8,24},{12,28},{16,0},{20,4},{24,8},{28,12},{1,17},{... | collective-permute-start | bytes 786440 | tf_op jit(solution)/shard_map/ppermute | solution.py:480
  17.6 8.1 %copy-start = (f32[1,1536]{1,0:T(1,128)S(1)}, f32[1,1536]{1,0:T(1,128)}, u32[]{:S(2)}) copy-start(f32[1,1536]{1,0:T(1,128)} %gq_ref.11) | copy-start | bytes 18436
  17.7 8.1 %copy-start.1 = (f32[1,1536]{1,0:T(1,128)S(1)}, f32[1,1536]{1,0:T(1,128)}, u32[]{:S(2)}) copy-start(f32[1,1536]{1,0:T(1,128)} %gk_ref.11) | copy-start | bytes 18436
  25.7 21.9 %collective-permute-start.1 = (bf16[528,256]{1,0:T(8,128)(2,1)S(1)}, bf16[528,256]{1,0:T(8,128)(2,1)S(1)}, u32[]{:S(2)}, u32[]{:S(2)}) collective-permute-start(bf16[528,256]{1,0:T(8,128)(2,1)S(1)} %piece_and_row.1), channel_id=1, source_target_pairs={{0,16},{4,20},{8,24},{12,28},{16,0},{20,4},{24,8},{28,12},{1,17},{... | collective-permute-start | bytes 811016 | tf_op jit(solution)/shard_map/ppermute | solution.py:480
  37.1 22.8 %collective-permute-start.3 = (bf16[512,256]{1,0:T(8,128)(2,1)S(1)}, bf16[512,256]{1,0:T(8,128)(2,1)S(1)}, u32[]{:S(2)}, u32[]{:S(2)}) collective-permute-start(bf16[512,256]{1,0:T(8,128)(2,1)S(1)} %get-tuple-element.33), channel_id=1, source_target_pairs={{0,16},{4,20},{8,24},{12,28},{16,0},{20,4},{24,8},{28,12},{1,17},{... | collective-permute-start | bytes 786440 | tf_op jit(solution)/shard_map/ppermute | solution.py:480
  48.5 19.8 %collective-permute-start.4 = (bf16[512,256]{1,0:T(8,128)(2,1)S(1)}, bf16[512,256]{1,0:T(8,128)(2,1)S(1)}, u32[]{:S(2)}, u32[]{:S(2)}) collective-permute-start(bf16[512,256]{1,0:T(8,128)(2,1)S(1)} %get-tuple-element.38), channel_id=1, source_target_pairs={{0,16},{4,20},{8,24},{12,28},{16,0},{20,4},{24,8},{28,12},{1,17},{... | collective-permute-start | bytes 786440 | tf_op jit(solution)/shard_map/ppermute | solution.py:480
  60.8 18.3 %collective-permute-start.6 = (bf16[512,256]{1,0:T(8,128)(2,1)S(1)}, bf16[512,256]{1,0:T(8,128)(2,1)S(1)}, u32[]{:S(2)}, u32[]{:S(2)}) collective-permute-start(bf16[512,256]{1,0:T(8,128)(2,1)S(1)} %get-tuple-element.42), channel_id=1, source_target_pairs={{0,16},{4,20},{8,24},{12,28},{16,0},{20,4},{24,8},{28,12},{1,17},{... | collective-permute-start | bytes 786440 | tf_op jit(solution)/shard_map/ppermute | solution.py:480
  72.6 50.0 %collective-permute-start.5 = (bf16[512,512]{1,0:T(8,128)(2,1)S(1)}, bf16[512,512]{1,0:T(8,128)(2,1)S(1)}, u32[]{:S(2)}, u32[]{:S(2)}) collective-permute-start(bf16[512,512]{1,0:T(8,128)(2,1)S(1)} %hold.1), channel_id=1, source_target_pairs={{0,28},{4,0},{8,4},{12,8},{16,12},{20,16},{24,20},{28,24},{1,29},{... | collective-permute-start | bytes 1572872 | tf_op jit(solution)/shard_map/ppermute | solution.py:480
  92.0 30.6 %collective-permute-start.7 = (bf16[512,384]{1,0:T(8,128)(2,1)S(1)}, bf16[512,384]{1,0:T(8,128)(2,1)S(1)}, u32[]{:S(2)}, u32[]{:S(2)}) collective-permute-start(bf16[512,384]{1,0:T(8,128)(2,1)S(1)} %finish.4), channel_id=1, source_target_pairs={{0,28},{4,0},{8,4},{12,8},{16,12},{20,16},{24,20},{28,24},{1,29},{... | collective-permute-start | bytes 1179656 | tf_op jit(solution)/shard_map/ppermute | solution.py:480
  93.4 29.2 %collective-permute-start.9 = (bf16[512,384]{1,0:T(8,128)(2,1)S(1)}, bf16[512,384]{1,0:T(8,128)(2,1)S(1)}, u32[]{:S(2)}, u32[]{:S(2)}) collective-permute-start(bf16[512,384]{1,0:T(8,128)(2,1)S(1)} %finish.6), channel_id=1, source_target_pairs={{0,28},{4,0},{8,4},{12,8},{16,12},{20,16},{24,20},{28,24},{1,29},{... | collective-permute-start | bytes 1179656 | tf_op jit(solution)/shard_map/ppermute | solution.py:480
  95.1 27.5 %collective-permute-start.10 = (bf16[528,256]{1,0:T(8,128)(2,1)S(1)}, bf16[528,256]{1,0:T(8,128)(2,1)S(1)}, u32[]{:S(2)}, u32[]{:S(2)}) collective-permute-start(bf16[528,256]{1,0:T(8,128)(2,1)S(1)} %finish.7), channel_id=1, source_target_pairs={{0,28},{4,0},{8,4},{12,8},{16,12},{20,16},{24,20},{28,24},{1,29},{... | collective-permute-start | bytes 811016 | tf_op jit(solution)/shard_map/ppermute | solution.py:480
  96.5 26.1 %collective-permute-start.8 = (bf16[512,256]{1,0:T(8,128)(2,1)S(1)}, bf16[512,256]{1,0:T(8,128)(2,1)S(1)}, u32[]{:S(2)}, u32[]{:S(2)}) collective-permute-start(bf16[512,256]{1,0:T(8,128)(2,1)S(1)} %finish.5), channel_id=1, source_target_pairs={{0,28},{4,0},{8,4},{12,8},{16,12},{20,16},{24,20},{28,24},{1,29},{... | collective-permute-start | bytes 786440 | tf_op jit(solution)/shard_map/ppermute | solution.py:480

commit v23 on v21

--- a/solution.py
+++ b/solution.py
@@ -501,7 +501,7 @@
     pair, inner = share(jnp.zeros((1, tokens), F32), 0, base, (), (in_hbm(output), *marks))
     marks = []
     sofar, inners = (), [inner]
-    ends = sorted({base, max(base, 3 * size), *(p * size for p in range(4, pieces + 1))})
+    ends = sorted({base, max(base, 3 * size), min(4, pieces) * size, width})
     for first, last in zip(ends[:-1], ends[1:]):
         *sofar, inner = share(inner, first, last, tuple(sofar), tuple(marks))
         inners.append(inner)

time: 123 us -> 134 us (1.089)
  the two profiles are of different devices: /device:TPU:0 before, /device:TPU:26 now
where the time goes in v23:
time: 134 us
  waiting for transfers between devices  67.3 us (50%)
  Pallas kernels  44.8 us (33%)
  blocking collectives  12 us (9%)
  starting transfers between devices  7.27 us (5%)
  between operations  1.67 us (1%)
    ppermute x10, waiting for transfers between devices, send(): return lax.ppermute(x, 'section', pairs)  67.3 us
    pallas_call x4, Pallas kernels, backward(): pl.pallas_call(functools.partial(backward_kernel, first, base, found, wid...  21.8 us
    pallas_call x1, Pallas kernels, forward(): pl.pallas_call(functools.partial(forward_kernel, heads, width_all), out_s...  8.39 us
    ppermute x10, starting transfers between devices, send(): return lax.ppermute(x, 'section', pairs)  7.27 us
    psum x1, blocking collectives, local(): totals = lax.psum(squares(current, stashed, third, (mark,)), 'tensor')  6.12 us
    psum x1, blocking collectives, local(): inner = lax.psum(inner, 'tensor')  5.91 us
    pallas_call x1, Pallas kernels, squares(): pl.pallas_call(squares_kernel, out_shape=jax.ShapeDtypeStruct((3, tokens)...  4.74 us
    pallas_call x4, Pallas kernels, pieces_of(): pl.pallas_call(functools.partial(piece_kernel, starts, sizes), out_shape=...  3.94 us
  transfers between devices with their start and end apart: 10, of which 5 were waited for; matrix products, arithmetic and copies ran while one was open for 0% of the time, Pallas kernels for 32%

profile of v23, /device:TPU:26, one launch (start us, length us, event | category | flops | bytes accessed | tf_op | source)
XLA Modules:
  0.0 133.6 jit_solution(3074564660978290940)
XLA Ops:
  0.6 1.1 pieces.4
  1.7 0.0 copy-start.2
  1.7 0.6 copy-done.2
  2.3 0.3 collective-permute-start
  2.6 2.6 %collective-permute-start.2 = (bf16[512,256]{1,0:T(8,128)(2,1)S(1)}, bf16[512,256]{1,0:T(8,128)(2,1)S(1)}, u32[]{:S(2)}, u32[]{:S(2)}) collective-permute-start(bf16[512,256]{1,0:T(8,128)(2,1)S(1)} %get-tuple-element.27), channel_id=1, source_target_pairs={{0,16},{4,20},{8,24},{12,28},{16,0},{20,4},{24,8},{28,12},{1,17},{... | collective-permute-start | bytes 786440 | tf_op jit(solution)/shard_map/ppermute | solution.py:462
  5.2 4.7 %squares.1 = f32[3,512]{1,0:T(4,128)} custom-call(bf16[512,1536]{1,0:T(8,128)(2,1)} %bitcast.4, bf16[1,2,512,1536]{3,2,1,0:T(8,128)(2,1)} %own_ref.7, f32[8,128]{1,0:T(8,128)} %copy-done.2), custom_call_target="tpu_custom_call" | custom-call | tf_op jit(solution)/shard_map/squares/pallas_call | solution.py:364
  10.0 6.1 %psum.14.t_ref = f32[3,512]{1,0:T(4,128)S(1)} all-reduce(f32[3,512]{1,0:T(4,128)} %squares.1), channel_id=1, replica_groups=mesh['section'=8,'tensor'=4] {'tensor'}, use_global_device_ids=true, to_apply=%region_0.0 | all-reduce | flops 1536 | bytes 12288 | tf_op jit(solution)/shard_map/psum | solution.py:479
  16.1 0.0 copy-start
  16.1 0.0 copy-start.1
  16.1 6.3 %collective-permute-done.rest_0_.refs_0_ = bf16[512,256]{1,0:T(8,128)(2,1)S(1)} collective-permute-done((bf16[512,256]{1,0:T(8,128)(2,1)S(1)}, bf16[512,256]{1,0:T(8,128)(2,1)S(1)}, u32[]{:S(2)}, u32[]{:S(2)}) %collective-permute-start) | collective-permute-done | bytes 262176 | tf_op jit(solution)/shard_map/ppermute | solution.py:462
  22.4 1.0 piece_and_row.1
  23.4 0.1 collective-permute-start.1
  23.5 0.0 copy-done
  23.5 0.0 copy-done.1
  23.5 8.4 %forward.1.rest_1_.refs_2_ = bf16[512,1536]{1,0:T(8,128)(2,1)} custom-call(bf16[512,1536]{1,0:T(8,128)(2,1)} %bitcast.5, f32[3,512]{1,0:T(4,128)S(1)} %psum.14.t_ref, f32[1,1536]{1,0:T(1,128)S(1)} %copy-done, f32[1,1536]{1,0:T(1,128)S(1)} %copy-done.1), custom_call_target="tpu_custom_call" | custom-call | tf_op jit(solution)/shard_map/forward/pallas_call | solution.py:119
  31.9 1.9 %collective-permute-done.2.rest_0_.refs_1_.refs_0_ = bf16[512,256]{1,0:T(8,128)(2,1)S(1)} collective-permute-done((bf16[512,256]{1,0:T(8,128)(2,1)S(1)}, bf16[512,256]{1,0:T(8,128)(2,1)S(1)}, u32[]{:S(2)}, u32[]{:S(2)}) %collective-permute-start.2) | collective-permute-done | bytes 262176 | tf_op jit(solution)/shard_map/ppermute | solution.py:462
  33.9 1.0 pieces.5
  34.8 1.0 collective-permute-start.3
  36.5 11.6 %collective-permute-done.1.extra_ref.rest_0_.refs_1_ = bf16[528,256]{1,0:T(8,128)(2,1)S(1)} collective-permute-done((bf16[528,256]{1,0:T(8,128)(2,1)S(1)}, bf16[528,256]{1,0:T(8,128)(2,1)S(1)}, u32[]{:S(2)}, u32[]{:S(2)}) %collective-permute-start.1) | collective-permute-done | bytes 270368 | tf_op jit(solution)/shard_map/ppermute | solution.py:462
  48.1 1.0 pieces.6
  49.0 0.1 collective-permute-start.5
  49.1 5.0 %backward.4 = (bf16[512,768]{1,0:T(8,128)(2,1)S(1)}, f32[1,512]{1,0:T(1,128)S(1)}) custom-call(s32[1]{0:T(128)S(6)} %copy.18.evicted_ref, bf16[1,2,512,1536]{3,2,1,0:T(8,128)(2,1)} %own_ref.7, bf16[1,512,1536]{2,1,0:T(8,128)(2,1)} %g_ref.7, f32[3,512]{1,0:T(4,128)S(1)} %psum.14.t_ref, f32[1,512]{1,0:T(1,128)S(1)} %row.1.held_ref, f32[1,1536]{1,0:T(1,128)S(1)} %copy-done, ...), custom_call_target="tpu_custom_call" | custom-call | tf_op jit(solution)/shard_map/backward/pallas_call | solution.py:230
  54.1 5.6 %backward.5 = (f32[512,1152]{1,0:T(8,128)}, bf16[512,1152]{1,0:T(8,128)(2,1)}, f32[1,512]{1,0:T(1,128)S(1)}) custom-call(s32[1]{0:T(128)S(6)} %copy.18.evicted_ref, bf16[1,2,512,1536]{3,2,1,0:T(8,128)(2,1)} %own_ref.7, bf16[1,512,1536]{2,1,0:T(8,128)(2,1)} %g_ref.7, f32[3,512]{1,0:T(4,128)S(1)} %psum.14.t_ref, f32[1,512]{1,0:T(1,128)S(1)} %row.1.held_ref, ...), custom_call_target="tpu_custom_call" | custom-call | tf_op jit(solution)/shard_map/backward/pallas_call | solution.py:230
  59.8 0.0 collective-permute-done.3.rest_0_.refs_0_
  59.8 1.0 pieces.7
  60.8 3.0 %collective-permute-start.6 = (bf16[512,256]{1,0:T(8,128)(2,1)S(1)}, bf16[512,256]{1,0:T(8,128)(2,1)S(1)}, u32[]{:S(2)}, u32[]{:S(2)}) collective-permute-start(bf16[512,256]{1,0:T(8,128)(2,1)S(1)} %get-tuple-element.39), channel_id=1, source_target_pairs={{0,16},{4,20},{8,24},{12,28},{16,0},{20,4},{24,8},{28,12},{1,17},{... | collective-permute-start | bytes 786440 | tf_op jit(solution)/shard_map/ppermute | solution.py:462
  63.7 4.3 %backward.6 = (f32[512,1152]{1,0:T(8,128)}, bf16[512,1152]{1,0:T(8,128)(2,1)}, f32[1,512]{1,0:T(1,128)S(1)}) custom-call(s32[1]{0:T(128)S(6)} %copy.18.evicted_ref, bf16[1,2,512,1536]{3,2,1,0:T(8,128)(2,1)} %own_ref.7, bf16[1,512,1536]{2,1,0:T(8,128)(2,1)} %g_ref.7, f32[3,512]{1,0:T(4,128)S(1)} %psum.14.t_ref, ...), custom_call_target="tpu_custom_call", output_to_operand_aliasing={{0}: (9, {}), {1}: (10, {})} | custom-call | tf_op jit(solution)/shard_map/backward/pallas_call | solution.py:230
  68.0 0.1 collective-permute-start.4
  68.1 0.0 collective-permute-done.5.refs_0_
  68.1 22.0 %collective-permute-done.6.refs_1_ = bf16[512,256]{1,0:T(8,128)(2,1)S(1)} collective-permute-done((bf16[512,256]{1,0:T(8,128)(2,1)S(1)}, bf16[512,256]{1,0:T(8,128)(2,1)S(1)}, u32[]{:S(2)}, u32[]{:S(2)}) %collective-permute-start.6) | collective-permute-done | bytes 262176 | tf_op jit(solution)/shard_map/ppermute | solution.py:462
  90.1 6.9 %backward.7 = (f32[512,1152]{1,0:T(8,128)}, bf16[512,1152]{1,0:T(8,128)(2,1)}, f32[1,512]{1,0:T(1,128)S(1)}) custom-call(s32[1]{0:T(128)S(6)} %copy.18.evicted_ref, bf16[1,2,512,1536]{3,2,1,0:T(8,128)(2,1)} %own_ref.7, bf16[1,512,1536]{2,1,0:T(8,128)(2,1)} %g_ref.7, f32[3,512]{1,0:T(4,128)S(1)} %psum.14.t_ref, ...), custom_call_target="tpu_custom_call", output_to_operand_aliasing={{0}: (10, {}), {1}: (11, {})} | custom-call | tf_op jit(solution)/shard_map/backward/pallas_call | solution.py:230
  97.0 5.9 %psum.15.inner_ref = f32[1,512]{1,0:T(1,128)S(1)} all-reduce(f32[1,512]{1,0:T(1,128)S(1)} %get-tuple-element.44), channel_id=1, replica_groups=mesh['section'=8,'tensor'=4] {'tensor'}, use_global_device_ids=true, to_apply=%region_1.0 | all-reduce | flops 512 | bytes 4096 | tf_op jit(solution)/shard_map/psum | solution.py:510
  102.9 1.7 %finish.2 = (bf16[512,640]{1,0:T(8,128)(2,1)S(1)}, f32[1,512]{1,0:T(1,128)S(1)}) custom-call(s32[1]{0:T(128)S(6)} %copy.18.evicted_ref, f32[512,1152]{1,0:T(8,128)} %get-tuple-element.42.a_ref, bf16[512,1152]{1,0:T(8,128)(2,1)} %get-tuple-element.43.x_ref, f32[3,512]{1,0:T(4,128)S(1)} %psum.14.t_ref, f32[1,512]{1,0:T(1,128)S(1)} %row.1.held_ref, ...), custom_call_target="tpu_custom_call" | custom-call | tf_op jit(solution)/shard_map/finish/pallas_call | solution.py:276
  104.7 0.1 collective-permute-start.8
  104.7 2.1 %finish.3 = (bf16[512,512]{1,0:T(8,128)(2,1)S(1)}, f32[1,512]{1,0:T(1,128)}) custom-call(s32[1]{0:T(128)S(6)} %copy.18.evicted_ref, f32[512,1152]{1,0:T(8,128)} %get-tuple-element.42.a_ref, bf16[512,1152]{1,0:T(8,128)(2,1)} %get-tuple-element.43.x_ref, f32[3,512]{1,0:T(4,128)S(1)} %psum.14.t_ref, f32[1,512]{1,0:T(1,128)S(1)} %row.1.held_ref, ...), custom_call_target="tpu_custom_call" | custom-call | tf_op jit(solution)/shard_map/finish/pallas_call | solution.py:276
  106.8 0.1 collective-permute-start.9
  106.9 0.1 collective-permute-start.7
  106.9 25.3 %collective-permute-done.7.row_ref = f32[1,512]{1,0:T(1,128)S(1)} collective-permute-done((f32[1,512]{1,0:T(1,128)S(1)}, f32[1,512]{1,0:T(1,128)S(1)}, u32[]{:S(2)}, u32[]{:S(2)}) %collective-permute-start.7) | collective-permute-done | bytes 2080 | tf_op jit(solution)/shard_map/ppermute | solution.py:462
  132.3 0.0 collective-permute-done.9.refs_1_
  132.3 0.0 collective-permute-done.4.pair_ref
  132.3 0.0 collective-permute-done.8.refs_0_
  132.3 1.2 place.1
  (3 shorter events, 0.0 us)
Async XLA Ops:
  1.7 0.6 copy-start.2
  2.3 20.2 %collective-permute-start = (bf16[512,256]{1,0:T(8,128)(2,1)S(1)}, bf16[512,256]{1,0:T(8,128)(2,1)S(1)}, u32[]{:S(2)}, u32[]{:S(2)}) collective-permute-start(bf16[512,256]{1,0:T(8,128)(2,1)S(1)} %get-tuple-element.26), channel_id=1, source_target_pairs={{0,16},{4,20},{8,24},{12,28},{16,0},{20,4},{24,8},{28,12},{1,17},{... | collective-permute-start | bytes 786440 | tf_op jit(solution)/shard_map/ppermute | solution.py:462
  2.6 31.2 %collective-permute-start.2 = (bf16[512,256]{1,0:T(8,128)(2,1)S(1)}, bf16[512,256]{1,0:T(8,128)(2,1)S(1)}, u32[]{:S(2)}, u32[]{:S(2)}) collective-permute-start(bf16[512,256]{1,0:T(8,128)(2,1)S(1)} %get-tuple-element.27), channel_id=1, source_target_pairs={{0,16},{4,20},{8,24},{12,28},{16,0},{20,4},{24,8},{28,12},{1,17},{... | collective-permute-start | bytes 786440 | tf_op jit(solution)/shard_map/ppermute | solution.py:462
  16.1 7.4 %copy-start = (f32[1,1536]{1,0:T(1,128)S(1)}, f32[1,1536]{1,0:T(1,128)}, u32[]{:S(2)}) copy-start(f32[1,1536]{1,0:T(1,128)} %gq_ref.9) | copy-start | bytes 18436
  16.1 7.4 %copy-start.1 = (f32[1,1536]{1,0:T(1,128)S(1)}, f32[1,1536]{1,0:T(1,128)}, u32[]{:S(2)}) copy-start(f32[1,1536]{1,0:T(1,128)} %gk_ref.9) | copy-start | bytes 18436
  23.4 24.7 %collective-permute-start.1 = (bf16[528,256]{1,0:T(8,128)(2,1)S(1)}, bf16[528,256]{1,0:T(8,128)(2,1)S(1)}, u32[]{:S(2)}, u32[]{:S(2)}) collective-permute-start(bf16[528,256]{1,0:T(8,128)(2,1)S(1)} %piece_and_row.1), channel_id=1, source_target_pairs={{0,16},{4,20},{8,24},{12,28},{16,0},{20,4},{24,8},{28,12},{1,17},{... | collective-permute-start | bytes 811016 | tf_op jit(solution)/shard_map/ppermute | solution.py:462
  34.8 24.9 %collective-permute-start.3 = (bf16[512,256]{1,0:T(8,128)(2,1)S(1)}, bf16[512,256]{1,0:T(8,128)(2,1)S(1)}, u32[]{:S(2)}, u32[]{:S(2)}) collective-permute-start(bf16[512,256]{1,0:T(8,128)(2,1)S(1)} %get-tuple-element.33), channel_id=1, source_target_pairs={{0,16},{4,20},{8,24},{12,28},{16,0},{20,4},{24,8},{28,12},{1,17},{... | collective-permute-start | bytes 786440 | tf_op jit(solution)/shard_map/ppermute | solution.py:462
  49.0 19.0 %collective-permute-start.5 = (bf16[512,256]{1,0:T(8,128)(2,1)S(1)}, bf16[512,256]{1,0:T(8,128)(2,1)S(1)}, u32[]{:S(2)}, u32[]{:S(2)}) collective-permute-start(bf16[512,256]{1,0:T(8,128)(2,1)S(1)} %get-tuple-element.38), channel_id=1, source_target_pairs={{0,16},{4,20},{8,24},{12,28},{16,0},{20,4},{24,8},{28,12},{1,17},{... | collective-permute-start | bytes 786440 | tf_op jit(solution)/shard_map/ppermute | solution.py:462
  60.8 29.4 %collective-permute-start.6 = (bf16[512,256]{1,0:T(8,128)(2,1)S(1)}, bf16[512,256]{1,0:T(8,128)(2,1)S(1)}, u32[]{:S(2)}, u32[]{:S(2)}) collective-permute-start(bf16[512,256]{1,0:T(8,128)(2,1)S(1)} %get-tuple-element.39), channel_id=1, source_target_pairs={{0,16},{4,20},{8,24},{12,28},{16,0},{20,4},{24,8},{28,12},{1,17},{... | collective-permute-start | bytes 786440 | tf_op jit(solution)/shard_map/ppermute | solution.py:462
  68.0 64.3 %collective-permute-start.4 = (bf16[512,768]{1,0:T(8,128)(2,1)S(1)}, bf16[512,768]{1,0:T(8,128)(2,1)S(1)}, u32[]{:S(2)}, u32[]{:S(2)}) collective-permute-start(bf16[512,768]{1,0:T(8,128)(2,1)S(1)} %hold.1), channel_id=1, source_target_pairs={{0,28},{4,0},{8,4},{12,8},{16,12},{20,16},{24,20},{28,24},{1,29},{... | collective-permute-start | bytes 2359304 | tf_op jit(solution)/shard_map/ppermute | solution.py:462
  104.7 27.6 %collective-permute-start.8 = (bf16[512,640]{1,0:T(8,128)(2,1)S(1)}, bf16[512,640]{1,0:T(8,128)(2,1)S(1)}, u32[]{:S(2)}, u32[]{:S(2)}) collective-permute-start(bf16[512,640]{1,0:T(8,128)(2,1)S(1)} %get-tuple-element.46), channel_id=1, source_target_pairs={{0,28},{4,0},{8,4},{12,8},{16,12},{20,16},{24,20},{28,24},{1,29},{... | collective-permute-start | bytes 1966088 | tf_op jit(solution)/shard_map/ppermute | solution.py:462
  106.8 25.5 %collective-permute-start.9 = (bf16[512,512]{1,0:T(8,128)(2,1)S(1)}, bf16[512,512]{1,0:T(8,128)(2,1)S(1)}, u32[]{:S(2)}, u32[]{:S(2)}) collective-permute-start(bf16[512,512]{1,0:T(8,128)(2,1)S(1)} %get-tuple-element.47), channel_id=1, source_target_pairs={{0,28},{4,0},{8,4},{12,8},{16,12},{20,16},{24,20},{28,24},{1,29},{... | collective-permute-start | bytes 1572872 | tf_op jit(solution)/shard_map/ppermute | solution.py:462
  106.9 25.4 %collective-permute-start.7 = (f32[1,512]{1,0:T(1,128)S(1)}, f32[1,512]{1,0:T(1,128)S(1)}, u32[]{:S(2)}, u32[]{:S(2)}) collective-permute-start(f32[1,512]{1,0:T(1,128)S(1)} %get-tuple-element.45), channel_id=1, source_target_pairs={{0,28},{4,0},{8,4},{12,8},{16,12},{20,16},{24,20},{28,24},{1,29},{... | collective-permute-start | bytes 6152 | tf_op jit(solution)/shard_map/ppermute | solution.py:462

commit v24 on v21

--- a/solution.py
+++ b/solution.py
@@ -145,7 +145,7 @@
         grads = [nt(v[: j * size], g[rows])] if j else []
         grads.append(nt(v[rows], g[rows]))
         delta = sum(jnp.sum(w * d, axis=0, keepdims=True) for w, d in zip(weights, grads))
-        scores = stacked([(w * ((d - delta) * SCALE)).astype(BF16) for w, d in zip(weights, grads)])
+        scores = stacked([(w * (d - delta)).astype(BF16) for w, d in zip(weights, grads)])
         rounded = stacked([w.astype(BF16) for w in weights])
         d_q.append(nn(kt[:, : (j + 1) * size], scores).T)
         part_k = nn(scores, q[rows])
@@ -154,7 +154,7 @@
             mine = slice(i * size, (i + 1) * size)
             d_k[i] = part_k[mine] if d_k[i] is None else d_k[i] + part_k[mine]
             d_v[i] = part_v[mine] if d_v[i] is None else d_v[i] + part_v[mine]
-    d_normed = stacked(d_q) * gain_q + stacked(d_k) * gain_k + stacked(d_v)
+    d_normed = stacked(d_q) * (gain_q * SCALE) + stacked(d_k) * (gain_k * SCALE) + stacked(d_v)
     return wide, d_normed
 
 

time: 123 us -> 122 us (level)
  no operation moved by 1% of the time
where the time goes in v24:
time: 122 us
  Pallas kernels  46.2 us (38%)
  waiting for transfers between devices  43.9 us (36%)
  starting transfers between devices  17.2 us (14%)
  blocking collectives  12.4 us (10%)
  between operations  1.64 us (1%)
    ppermute x10, waiting for transfers between devices, send(): return lax.ppermute(x, 'section', pairs)  43.9 us
    pallas_call x5, Pallas kernels, backward(): pl.pallas_call(functools.partial(backward_kernel, first, base, found, wid...  23.2 us
    ppermute x10, starting transfers between devices, send(): return lax.ppermute(x, 'section', pairs)  17.2 us
    pallas_call x1, Pallas kernels, forward(): pl.pallas_call(functools.partial(forward_kernel, heads, width_all), out_s...  8.39 us
    psum x1, blocking collectives, local(): totals = lax.psum(squares(current, stashed, third, (mark,)), 'tensor')  6.53 us
    psum x1, blocking collectives, local(): inner = lax.psum(inner, 'tensor')  5.83 us
    pallas_call x1, Pallas kernels, squares(): pl.pallas_call(squares_kernel, out_shape=jax.ShapeDtypeStruct((3, tokens)...  4.74 us
    pallas_call x4, Pallas kernels, pieces_of(): pl.pallas_call(functools.partial(piece_kernel, starts, sizes), out_shape=...  3.94 us
  transfers between devices with their start and end apart: 10, of which 4 were waited for; matrix products, arithmetic and copies ran while one was open for 0% of the time, Pallas kernels for 36%

profile of v24, /device:TPU:0, one launch (start us, length us, event | category | flops | bytes accessed | tf_op | source)
XLA Modules:
  0.0 121.8 jit_solution(967982814107616391)
XLA Ops:
  0.6 1.1 pieces.4
  1.7 0.0 copy-start.2
  1.7 0.6 copy-done.2
  2.3 4.0 %collective-permute-start = (bf16[512,256]{1,0:T(8,128)(2,1)S(1)}, bf16[512,256]{1,0:T(8,128)(2,1)S(1)}, u32[]{:S(2)}, u32[]{:S(2)}) collective-permute-start(bf16[512,256]{1,0:T(8,128)(2,1)S(1)} %get-tuple-element.29), channel_id=1, source_target_pairs={{0,16},{4,20},{8,24},{12,28},{16,0},{20,4},{24,8},{28,12},{1,17},{... | collective-permute-start | bytes 786440 | tf_op jit(solution)/shard_map/ppermute | solution.py:462
  6.3 0.0 collective-permute-start.2
  6.4 4.7 %squares.1 = f32[3,512]{1,0:T(4,128)} custom-call(bf16[512,1536]{1,0:T(8,128)(2,1)} %bitcast.4, bf16[1,2,512,1536]{3,2,1,0:T(8,128)(2,1)} %own_ref.9, f32[8,128]{1,0:T(8,128)} %copy-done.2), custom_call_target="tpu_custom_call" | custom-call | tf_op jit(solution)/shard_map/squares/pallas_call | solution.py:364
  11.1 6.5 %psum.14.t_ref = f32[3,512]{1,0:T(4,128)S(1)} all-reduce(f32[3,512]{1,0:T(4,128)} %squares.1), channel_id=1, replica_groups=mesh['section'=8,'tensor'=4] {'tensor'}, use_global_device_ids=true, to_apply=%region_0.0 | all-reduce | flops 1536 | bytes 12288 | tf_op jit(solution)/shard_map/psum | solution.py:479
  17.6 0.0 copy-start
  17.7 0.0 copy-start.1
  17.7 7.0 %collective-permute-done.rest_0_.refs_0_ = bf16[512,256]{1,0:T(8,128)(2,1)S(1)} collective-permute-done((bf16[512,256]{1,0:T(8,128)(2,1)S(1)}, bf16[512,256]{1,0:T(8,128)(2,1)S(1)}, u32[]{:S(2)}, u32[]{:S(2)}) %collective-permute-start) | collective-permute-done | bytes 262176 | tf_op jit(solution)/shard_map/ppermute | solution.py:462
  24.7 1.0 piece_and_row.1
  25.7 0.1 collective-permute-start.1
  25.7 0.0 copy-done
  25.7 0.0 copy-done.1
  25.8 8.4 %forward.1.rest_1_.refs_2_ = bf16[512,1536]{1,0:T(8,128)(2,1)} custom-call(bf16[512,1536]{1,0:T(8,128)(2,1)} %bitcast.5, f32[3,512]{1,0:T(4,128)S(1)} %psum.14.t_ref, f32[1,1536]{1,0:T(1,128)S(1)} %copy-done, f32[1,1536]{1,0:T(1,128)S(1)} %copy-done.1), custom_call_target="tpu_custom_call" | custom-call | tf_op jit(solution)/shard_map/forward/pallas_call | solution.py:119
  34.1 2.0 %collective-permute-done.2.rest_0_.refs_1_.refs_0_ = bf16[512,256]{1,0:T(8,128)(2,1)S(1)} collective-permute-done((bf16[512,256]{1,0:T(8,128)(2,1)S(1)}, bf16[512,256]{1,0:T(8,128)(2,1)S(1)}, u32[]{:S(2)}, u32[]{:S(2)}) %collective-permute-start.2) | collective-permute-done | bytes 262176 | tf_op jit(solution)/shard_map/ppermute | solution.py:462
  36.1 1.0 pieces.5
  37.1 1.0 collective-permute-start.3
  38.1 9.4 %collective-permute-done.1.extra_ref.rest_0_.refs_1_ = bf16[528,256]{1,0:T(8,128)(2,1)S(1)} collective-permute-done((bf16[528,256]{1,0:T(8,128)(2,1)S(1)}, bf16[528,256]{1,0:T(8,128)(2,1)S(1)}, u32[]{:S(2)}, u32[]{:S(2)}) %collective-permute-start.1) | collective-permute-done | bytes 270368 | tf_op jit(solution)/shard_map/ppermute | solution.py:462
  47.5 1.0 pieces.6
  48.5 0.1 collective-permute-start.4
  49.2 4.9 %backward.5 = (bf16[512,768]{1,0:T(8,128)(2,1)S(1)}, f32[1,512]{1,0:T(1,128)S(1)}) custom-call(s32[1]{0:T(128)S(6)} %copy.22.evicted_ref, bf16[1,2,512,1536]{3,2,1,0:T(8,128)(2,1)} %own_ref.9, bf16[1,512,1536]{2,1,0:T(8,128)(2,1)} %g_ref.9, f32[3,512]{1,0:T(4,128)S(1)} %psum.14.t_ref, f32[1,512]{1,0:T(1,128)S(1)} %row.1.held_ref, f32[1,1536]{1,0:T(1,128)S(1)} %copy-done, ...), custom_call_target="tpu_custom_call" | custom-call | tf_op jit(solution)/shard_map/backward/pallas_call | solution.py:230
  54.1 5.5 %backward.6 = (f32[512,1152]{1,0:T(8,128)}, bf16[512,1152]{1,0:T(8,128)(2,1)}, f32[1,512]{1,0:T(1,128)S(1)}) custom-call(s32[1]{0:T(128)S(6)} %copy.22.evicted_ref, bf16[1,2,512,1536]{3,2,1,0:T(8,128)(2,1)} %own_ref.9, bf16[1,512,1536]{2,1,0:T(8,128)(2,1)} %g_ref.9, f32[3,512]{1,0:T(4,128)S(1)} %psum.14.t_ref, f32[1,512]{1,0:T(1,128)S(1)} %row.1.held_ref, ...), custom_call_target="tpu_custom_call" | custom-call | tf_op jit(solution)/shard_map/backward/pallas_call | solution.py:230
  59.7 0.0 collective-permute-done.3.rest_0_.refs_0_
  59.7 1.0 pieces.7
  60.7 3.0 %collective-permute-start.6 = (bf16[512,256]{1,0:T(8,128)(2,1)S(1)}, bf16[512,256]{1,0:T(8,128)(2,1)S(1)}, u32[]{:S(2)}, u32[]{:S(2)}) collective-permute-start(bf16[512,256]{1,0:T(8,128)(2,1)S(1)} %get-tuple-element.45), channel_id=1, source_target_pairs={{0,16},{4,20},{8,24},{12,28},{16,0},{20,4},{24,8},{28,12},{1,17},{... | collective-permute-start | bytes 786440 | tf_op jit(solution)/shard_map/ppermute | solution.py:462
  63.6 4.3 %backward.7 = (f32[512,1152]{1,0:T(8,128)}, bf16[512,1152]{1,0:T(8,128)(2,1)}, f32[1,512]{1,0:T(1,128)S(1)}) custom-call(s32[1]{0:T(128)S(6)} %copy.22.evicted_ref, bf16[1,2,512,1536]{3,2,1,0:T(8,128)(2,1)} %own_ref.9, bf16[1,512,1536]{2,1,0:T(8,128)(2,1)} %g_ref.9, f32[3,512]{1,0:T(4,128)S(1)} %psum.14.t_ref, ...), custom_call_target="tpu_custom_call", output_to_operand_aliasing={{0}: (9, {}), {1}: (10, {})} | custom-call | tf_op jit(solution)/shard_map/backward/pallas_call | solution.py:230
  67.9 0.0 collective-permute-done.4.refs_0_
  67.9 4.3 %backward.8 = (f32[512,1152]{1,0:T(8,128)}, bf16[512,1152]{1,0:T(8,128)(2,1)}, f32[1,512]{1,0:T(1,128)S(1)}) custom-call(s32[1]{0:T(128)S(6)} %copy.22.evicted_ref, bf16[1,2,512,1536]{3,2,1,0:T(8,128)(2,1)} %own_ref.9, bf16[1,512,1536]{2,1,0:T(8,128)(2,1)} %g_ref.9, f32[3,512]{1,0:T(4,128)S(1)} %psum.14.t_ref, ...), custom_call_target="tpu_custom_call", output_to_operand_aliasing={{0}: (9, {}), {1}: (10, {})} | custom-call | tf_op jit(solution)/shard_map/backward/pallas_call | solution.py:230
  72.2 6.6 %collective-permute-start.5 = (bf16[512,768]{1,0:T(8,128)(2,1)S(1)}, bf16[512,768]{1,0:T(8,128)(2,1)S(1)}, u32[]{:S(2)}, u32[]{:S(2)}) collective-permute-start(bf16[512,768]{1,0:T(8,128)(2,1)S(1)} %hold.1), channel_id=1, source_target_pairs={{0,28},{4,0},{8,4},{12,8},{16,12},{20,16},{24,20},{28,24},{1,29},{... | collective-permute-start | bytes 2359304 | tf_op jit(solution)/shard_map/ppermute | solution.py:462
  78.8 0.0 collective-permute-done.6.refs_0_
  78.8 4.2 %backward.9 = (f32[512,1152]{1,0:T(8,128)}, bf16[512,1152]{1,0:T(8,128)(2,1)}, f32[1,512]{1,0:T(1,128)S(1)}) custom-call(s32[1]{0:T(128)S(6)} %copy.22.evicted_ref, bf16[1,2,512,1536]{3,2,1,0:T(8,128)(2,1)} %own_ref.9, bf16[1,512,1536]{2,1,0:T(8,128)(2,1)} %g_ref.9, f32[3,512]{1,0:T(4,128)S(1)} %psum.14.t_ref, ...), custom_call_target="tpu_custom_call", output_to_operand_aliasing={{0}: (9, {}), {1}: (10, {})} | custom-call | tf_op jit(solution)/shard_map/backward/pallas_call | solution.py:230
  83.1 5.8 %psum.15.inner_ref = f32[1,512]{1,0:T(1,128)S(1)} all-reduce(f32[1,512]{1,0:T(1,128)S(1)} %get-tuple-element.50), channel_id=1, replica_groups=mesh['section'=8,'tensor'=4] {'tensor'}, use_global_device_ids=true, to_apply=%region_1.0 | all-reduce | flops 512 | bytes 4096 | tf_op jit(solution)/shard_map/psum | solution.py:510
  88.9 1.7 %finish.2 = (bf16[512,640]{1,0:T(8,128)(2,1)S(1)}, f32[1,512]{1,0:T(1,128)S(1)}) custom-call(s32[1]{0:T(128)S(6)} %copy.22.evicted_ref, f32[512,1152]{1,0:T(8,128)} %get-tuple-element.48.a_ref, bf16[512,1152]{1,0:T(8,128)(2,1)} %get-tuple-element.49.x_ref, f32[3,512]{1,0:T(4,128)S(1)} %psum.14.t_ref, f32[1,512]{1,0:T(1,128)S(1)} %row.1.held_ref, ...), custom_call_target="tpu_custom_call" | custom-call | tf_op jit(solution)/shard_map/finish/pallas_call | solution.py:276
  90.6 1.7 %collective-permute-start.8 = (bf16[512,640]{1,0:T(8,128)(2,1)S(1)}, bf16[512,640]{1,0:T(8,128)(2,1)S(1)}, u32[]{:S(2)}, u32[]{:S(2)}) collective-permute-start(bf16[512,640]{1,0:T(8,128)(2,1)S(1)} %get-tuple-element.52), channel_id=1, source_target_pairs={{0,28},{4,0},{8,4},{12,8},{16,12},{20,16},{24,20},{28,24},{1,29},{... | collective-permute-start | bytes 1966088 | tf_op jit(solution)/shard_map/ppermute | solution.py:462
  92.4 2.0 %finish.3 = (bf16[512,512]{1,0:T(8,128)(2,1)S(1)}, f32[1,512]{1,0:T(1,128)}) custom-call(s32[1]{0:T(128)S(6)} %copy.22.evicted_ref, f32[512,1152]{1,0:T(8,128)} %get-tuple-element.48.a_ref, bf16[512,1152]{1,0:T(8,128)(2,1)} %get-tuple-element.49.x_ref, f32[3,512]{1,0:T(4,128)S(1)} %psum.14.t_ref, f32[1,512]{1,0:T(1,128)S(1)} %row.1.held_ref, ...), custom_call_target="tpu_custom_call" | custom-call | tf_op jit(solution)/shard_map/finish/pallas_call | solution.py:276
  94.4 0.6 collective-permute-start.9
  95.0 0.1 collective-permute-start.7
  95.0 25.5 %collective-permute-done.7.row_ref = f32[1,512]{1,0:T(1,128)S(1)} collective-permute-done((f32[1,512]{1,0:T(1,128)S(1)}, f32[1,512]{1,0:T(1,128)S(1)}, u32[]{:S(2)}, u32[]{:S(2)}) %collective-permute-start.7) | collective-permute-done | bytes 2080 | tf_op jit(solution)/shard_map/ppermute | solution.py:462
  120.5 0.0 collective-permute-done.9.refs_1_
  120.5 0.0 collective-permute-done.8.refs_0_
  120.5 0.0 collective-permute-done.5.pair_ref
  120.5 1.2 place.1
  (3 shorter events, 0.0 us)
Async XLA Ops:
  1.7 0.6 copy-start.2
  2.3 22.4 %collective-permute-start = (bf16[512,256]{1,0:T(8,128)(2,1)S(1)}, bf16[512,256]{1,0:T(8,128)(2,1)S(1)}, u32[]{:S(2)}, u32[]{:S(2)}) collective-permute-start(bf16[512,256]{1,0:T(8,128)(2,1)S(1)} %get-tuple-element.29), channel_id=1, source_target_pairs={{0,16},{4,20},{8,24},{12,28},{16,0},{20,4},{24,8},{28,12},{1,17},{... | collective-permute-start | bytes 786440 | tf_op jit(solution)/shard_map/ppermute | solution.py:462
  6.3 29.8 %collective-permute-start.2 = (bf16[512,256]{1,0:T(8,128)(2,1)S(1)}, bf16[512,256]{1,0:T(8,128)(2,1)S(1)}, u32[]{:S(2)}, u32[]{:S(2)}) collective-permute-start(bf16[512,256]{1,0:T(8,128)(2,1)S(1)} %get-tuple-element.30), channel_id=1, source_target_pairs={{0,16},{4,20},{8,24},{12,28},{16,0},{20,4},{24,8},{28,12},{1,17},{... | collective-permute-start | bytes 786440 | tf_op jit(solution)/shard_map/ppermute | solution.py:462
  17.6 8.1 %copy-start = (f32[1,1536]{1,0:T(1,128)S(1)}, f32[1,1536]{1,0:T(1,128)}, u32[]{:S(2)}) copy-start(f32[1,1536]{1,0:T(1,128)} %gq_ref.11) | copy-start | bytes 18436
  17.7 8.1 %copy-start.1 = (f32[1,1536]{1,0:T(1,128)S(1)}, f32[1,1536]{1,0:T(1,128)}, u32[]{:S(2)}) copy-start(f32[1,1536]{1,0:T(1,128)} %gk_ref.11) | copy-start | bytes 18436
  25.7 21.9 %collective-permute-start.1 = (bf16[528,256]{1,0:T(8,128)(2,1)S(1)}, bf16[528,256]{1,0:T(8,128)(2,1)S(1)}, u32[]{:S(2)}, u32[]{:S(2)}) collective-permute-start(bf16[528,256]{1,0:T(8,128)(2,1)S(1)} %piece_and_row.1), channel_id=1, source_target_pairs={{0,16},{4,20},{8,24},{12,28},{16,0},{20,4},{24,8},{28,12},{1,17},{... | collective-permute-start | bytes 811016 | tf_op jit(solution)/shard_map/ppermute | solution.py:462
  37.1 22.6 %collective-permute-start.3 = (bf16[512,256]{1,0:T(8,128)(2,1)S(1)}, bf16[512,256]{1,0:T(8,128)(2,1)S(1)}, u32[]{:S(2)}, u32[]{:S(2)}) collective-permute-start(bf16[512,256]{1,0:T(8,128)(2,1)S(1)} %get-tuple-element.36), channel_id=1, source_target_pairs={{0,16},{4,20},{8,24},{12,28},{16,0},{20,4},{24,8},{28,12},{1,17},{... | collective-permute-start | bytes 786440 | tf_op jit(solution)/shard_map/ppermute | solution.py:462
  48.5 19.4 %collective-permute-start.4 = (bf16[512,256]{1,0:T(8,128)(2,1)S(1)}, bf16[512,256]{1,0:T(8,128)(2,1)S(1)}, u32[]{:S(2)}, u32[]{:S(2)}) collective-permute-start(bf16[512,256]{1,0:T(8,128)(2,1)S(1)} %get-tuple-element.41), channel_id=1, source_target_pairs={{0,16},{4,20},{8,24},{12,28},{16,0},{20,4},{24,8},{28,12},{1,17},{... | collective-permute-start | bytes 786440 | tf_op jit(solution)/shard_map/ppermute | solution.py:462
  60.7 18.2 %collective-permute-start.6 = (bf16[512,256]{1,0:T(8,128)(2,1)S(1)}, bf16[512,256]{1,0:T(8,128)(2,1)S(1)}, u32[]{:S(2)}, u32[]{:S(2)}) collective-permute-start(bf16[512,256]{1,0:T(8,128)(2,1)S(1)} %get-tuple-element.45), channel_id=1, source_target_pairs={{0,16},{4,20},{8,24},{12,28},{16,0},{20,4},{24,8},{28,12},{1,17},{... | collective-permute-start | bytes 786440 | tf_op jit(solution)/shard_map/ppermute | solution.py:462
  72.2 48.3 %collective-permute-start.5 = (bf16[512,768]{1,0:T(8,128)(2,1)S(1)}, bf16[512,768]{1,0:T(8,128)(2,1)S(1)}, u32[]{:S(2)}, u32[]{:S(2)}) collective-permute-start(bf16[512,768]{1,0:T(8,128)(2,1)S(1)} %hold.1), channel_id=1, source_target_pairs={{0,28},{4,0},{8,4},{12,8},{16,12},{20,16},{24,20},{28,24},{1,29},{... | collective-permute-start | bytes 2359304 | tf_op jit(solution)/shard_map/ppermute | solution.py:462
  90.6 29.8 %collective-permute-start.8 = (bf16[512,640]{1,0:T(8,128)(2,1)S(1)}, bf16[512,640]{1,0:T(8,128)(2,1)S(1)}, u32[]{:S(2)}, u32[]{:S(2)}) collective-permute-start(bf16[512,640]{1,0:T(8,128)(2,1)S(1)} %get-tuple-element.52), channel_id=1, source_target_pairs={{0,28},{4,0},{8,4},{12,8},{16,12},{20,16},{24,20},{28,24},{1,29},{... | collective-permute-start | bytes 1966088 | tf_op jit(solution)/shard_map/ppermute | solution.py:462
  94.4 26.1 %collective-permute-start.9 = (bf16[512,512]{1,0:T(8,128)(2,1)S(1)}, bf16[512,512]{1,0:T(8,128)(2,1)S(1)}, u32[]{:S(2)}, u32[]{:S(2)}) collective-permute-start(bf16[512,512]{1,0:T(8,128)(2,1)S(1)} %get-tuple-element.53), channel_id=1, source_target_pairs={{0,28},{4,0},{8,4},{12,8},{16,12},{20,16},{24,20},{28,24},{1,29},{... | collective-permute-start | bytes 1572872 | tf_op jit(solution)/shard_map/ppermute | solution.py:462
  95.0 25.5 %collective-permute-start.7 = (f32[1,512]{1,0:T(1,128)S(1)}, f32[1,512]{1,0:T(1,128)S(1)}, u32[]{:S(2)}, u32[]{:S(2)}) collective-permute-start(f32[1,512]{1,0:T(1,128)S(1)} %get-tuple-element.51), channel_id=1, source_target_pairs={{0,28},{4,0},{8,4},{12,8},{16,12},{20,16},{24,20},{28,24},{1,29},{... | collective-permute-start | bytes 6152 | tf_op jit(solution)/shard_map/ppermute | solution.py:462

commit v25 on v24

--- a/solution.py
+++ b/solution.py
@@ -509,7 +509,7 @@
     pair = send(hold(pair, (inners[-2],)), prior)
     inner = lax.psum(inner, "tensor")
     left = width - base
-    cut = (left // HDIM + 1) // 2 * HDIM
+    cut = max(1, left // HDIM // 2) * HDIM
     ends = (*sofar, totals, held, inner)
     early, row = finish(width_all, eviction, *ends, 0, cut)
     early = send(early, prior)

time: 122 us -> 122 us (level)
  no operation moved by 1% of the time
where the time goes in v25:
time: 122 us
  Pallas kernels  46.2 us (38%)
  waiting for transfers between devices  44 us (36%)
  starting transfers between devices  17.2 us (14%)
  blocking collectives  12.4 us (10%)
  between operations  1.64 us (1%)
    ppermute x10, waiting for transfers between devices, send(): return lax.ppermute(x, 'section', pairs)  44 us
    pallas_call x5, Pallas kernels, backward(): pl.pallas_call(functools.partial(backward_kernel, first, base, found, wid...  23.2 us
    ppermute x10, starting transfers between devices, send(): return lax.ppermute(x, 'section', pairs)  17.2 us
    pallas_call x1, Pallas kernels, forward(): pl.pallas_call(functools.partial(forward_kernel, heads, width_all), out_s...  8.39 us
    psum x1, blocking collectives, local(): totals = lax.psum(squares(current, stashed, third, (mark,)), 'tensor')  6.53 us
    psum x1, blocking collectives, local(): inner = lax.psum(inner, 'tensor')  5.83 us
    pallas_call x1, Pallas kernels, squares(): pl.pallas_call(squares_kernel, out_shape=jax.ShapeDtypeStruct((3, tokens)...  4.74 us
    pallas_call x4, Pallas kernels, pieces_of(): pl.pallas_call(functools.partial(piece_kernel, starts, sizes), out_shape=...  3.94 us
  transfers between devices with their start and end apart: 10, of which 4 were waited for; matrix products, arithmetic and copies ran while one was open for 0% of the time, Pallas kernels for 36%

profile of v25, /device:TPU:0, one launch (start us, length us, event | category | flops | bytes accessed | tf_op | source)
XLA Modules:
  0.0 122.0 jit_solution(5043581809079229246)
XLA Ops:
  0.6 1.1 pieces.4
  1.7 0.0 copy-start.2
  1.7 0.6 copy-done.2
  2.3 4.0 %collective-permute-start = (bf16[512,256]{1,0:T(8,128)(2,1)S(1)}, bf16[512,256]{1,0:T(8,128)(2,1)S(1)}, u32[]{:S(2)}, u32[]{:S(2)}) collective-permute-start(bf16[512,256]{1,0:T(8,128)(2,1)S(1)} %get-tuple-element.29), channel_id=1, source_target_pairs={{0,16},{4,20},{8,24},{12,28},{16,0},{20,4},{24,8},{28,12},{1,17},{... | collective-permute-start | bytes 786440 | tf_op jit(solution)/shard_map/ppermute | solution.py:462
  6.3 0.0 collective-permute-start.2
  6.4 4.7 %squares.1 = f32[3,512]{1,0:T(4,128)} custom-call(bf16[512,1536]{1,0:T(8,128)(2,1)} %bitcast.4, bf16[1,2,512,1536]{3,2,1,0:T(8,128)(2,1)} %own_ref.9, f32[8,128]{1,0:T(8,128)} %copy-done.2), custom_call_target="tpu_custom_call" | custom-call | tf_op jit(solution)/shard_map/squares/pallas_call | solution.py:364
  11.1 6.5 %psum.14.t_ref = f32[3,512]{1,0:T(4,128)S(1)} all-reduce(f32[3,512]{1,0:T(4,128)} %squares.1), channel_id=1, replica_groups=mesh['section'=8,'tensor'=4] {'tensor'}, use_global_device_ids=true, to_apply=%region_0.0 | all-reduce | flops 1536 | bytes 12288 | tf_op jit(solution)/shard_map/psum | solution.py:479
  17.6 0.0 copy-start
  17.7 0.0 copy-start.1
  17.7 7.0 %collective-permute-done.rest_0_.refs_0_ = bf16[512,256]{1,0:T(8,128)(2,1)S(1)} collective-permute-done((bf16[512,256]{1,0:T(8,128)(2,1)S(1)}, bf16[512,256]{1,0:T(8,128)(2,1)S(1)}, u32[]{:S(2)}, u32[]{:S(2)}) %collective-permute-start) | collective-permute-done | bytes 262176 | tf_op jit(solution)/shard_map/ppermute | solution.py:462
  24.7 1.0 piece_and_row.1
  25.7 0.1 collective-permute-start.1
  25.7 0.0 copy-done
  25.7 0.0 copy-done.1
  25.8 8.4 %forward.1.rest_1_.refs_2_ = bf16[512,1536]{1,0:T(8,128)(2,1)} custom-call(bf16[512,1536]{1,0:T(8,128)(2,1)} %bitcast.5, f32[3,512]{1,0:T(4,128)S(1)} %psum.14.t_ref, f32[1,1536]{1,0:T(1,128)S(1)} %copy-done, f32[1,1536]{1,0:T(1,128)S(1)} %copy-done.1), custom_call_target="tpu_custom_call" | custom-call | tf_op jit(solution)/shard_map/forward/pallas_call | solution.py:119
  34.1 2.0 %collective-permute-done.2.rest_0_.refs_1_.refs_0_ = bf16[512,256]{1,0:T(8,128)(2,1)S(1)} collective-permute-done((bf16[512,256]{1,0:T(8,128)(2,1)S(1)}, bf16[512,256]{1,0:T(8,128)(2,1)S(1)}, u32[]{:S(2)}, u32[]{:S(2)}) %collective-permute-start.2) | collective-permute-done | bytes 262176 | tf_op jit(solution)/shard_map/ppermute | solution.py:462
  36.1 1.0 pieces.5
  37.1 1.0 collective-permute-start.3
  38.1 9.4 %collective-permute-done.1.extra_ref.rest_0_.refs_1_ = bf16[528,256]{1,0:T(8,128)(2,1)S(1)} collective-permute-done((bf16[528,256]{1,0:T(8,128)(2,1)S(1)}, bf16[528,256]{1,0:T(8,128)(2,1)S(1)}, u32[]{:S(2)}, u32[]{:S(2)}) %collective-permute-start.1) | collective-permute-done | bytes 270368 | tf_op jit(solution)/shard_map/ppermute | solution.py:462
  47.5 1.0 pieces.6
  48.5 0.1 collective-permute-start.4
  49.2 4.9 %backward.5 = (bf16[512,768]{1,0:T(8,128)(2,1)S(1)}, f32[1,512]{1,0:T(1,128)S(1)}) custom-call(s32[1]{0:T(128)S(6)} %copy.22.evicted_ref, bf16[1,2,512,1536]{3,2,1,0:T(8,128)(2,1)} %own_ref.9, bf16[1,512,1536]{2,1,0:T(8,128)(2,1)} %g_ref.9, f32[3,512]{1,0:T(4,128)S(1)} %psum.14.t_ref, f32[1,512]{1,0:T(1,128)S(1)} %row.1.held_ref, f32[1,1536]{1,0:T(1,128)S(1)} %copy-done, ...), custom_call_target="tpu_custom_call" | custom-call | tf_op jit(solution)/shard_map/backward/pallas_call | solution.py:230
  54.1 5.5 %backward.6 = (f32[512,1152]{1,0:T(8,128)}, bf16[512,1152]{1,0:T(8,128)(2,1)}, f32[1,512]{1,0:T(1,128)S(1)}) custom-call(s32[1]{0:T(128)S(6)} %copy.22.evicted_ref, bf16[1,2,512,1536]{3,2,1,0:T(8,128)(2,1)} %own_ref.9, bf16[1,512,1536]{2,1,0:T(8,128)(2,1)} %g_ref.9, f32[3,512]{1,0:T(4,128)S(1)} %psum.14.t_ref, f32[1,512]{1,0:T(1,128)S(1)} %row.1.held_ref, ...), custom_call_target="tpu_custom_call" | custom-call | tf_op jit(solution)/shard_map/backward/pallas_call | solution.py:230
  59.7 0.0 collective-permute-done.3.rest_0_.refs_0_
  59.7 1.0 pieces.7
  60.7 3.0 %collective-permute-start.6 = (bf16[512,256]{1,0:T(8,128)(2,1)S(1)}, bf16[512,256]{1,0:T(8,128)(2,1)S(1)}, u32[]{:S(2)}, u32[]{:S(2)}) collective-permute-start(bf16[512,256]{1,0:T(8,128)(2,1)S(1)} %get-tuple-element.45), channel_id=1, source_target_pairs={{0,16},{4,20},{8,24},{12,28},{16,0},{20,4},{24,8},{28,12},{1,17},{... | collective-permute-start | bytes 786440 | tf_op jit(solution)/shard_map/ppermute | solution.py:462
  63.6 4.3 %backward.7 = (f32[512,1152]{1,0:T(8,128)}, bf16[512,1152]{1,0:T(8,128)(2,1)}, f32[1,512]{1,0:T(1,128)S(1)}) custom-call(s32[1]{0:T(128)S(6)} %copy.22.evicted_ref, bf16[1,2,512,1536]{3,2,1,0:T(8,128)(2,1)} %own_ref.9, bf16[1,512,1536]{2,1,0:T(8,128)(2,1)} %g_ref.9, f32[3,512]{1,0:T(4,128)S(1)} %psum.14.t_ref, ...), custom_call_target="tpu_custom_call", output_to_operand_aliasing={{0}: (9, {}), {1}: (10, {})} | custom-call | tf_op jit(solution)/shard_map/backward/pallas_call | solution.py:230
  67.9 0.0 collective-permute-done.4.refs_0_
  67.9 4.3 %backward.8 = (f32[512,1152]{1,0:T(8,128)}, bf16[512,1152]{1,0:T(8,128)(2,1)}, f32[1,512]{1,0:T(1,128)S(1)}) custom-call(s32[1]{0:T(128)S(6)} %copy.22.evicted_ref, bf16[1,2,512,1536]{3,2,1,0:T(8,128)(2,1)} %own_ref.9, bf16[1,512,1536]{2,1,0:T(8,128)(2,1)} %g_ref.9, f32[3,512]{1,0:T(4,128)S(1)} %psum.14.t_ref, ...), custom_call_target="tpu_custom_call", output_to_operand_aliasing={{0}: (9, {}), {1}: (10, {})} | custom-call | tf_op jit(solution)/shard_map/backward/pallas_call | solution.py:230
  72.2 6.8 %collective-permute-start.5 = (bf16[512,768]{1,0:T(8,128)(2,1)S(1)}, bf16[512,768]{1,0:T(8,128)(2,1)S(1)}, u32[]{:S(2)}, u32[]{:S(2)}) collective-permute-start(bf16[512,768]{1,0:T(8,128)(2,1)S(1)} %hold.1), channel_id=1, source_target_pairs={{0,28},{4,0},{8,4},{12,8},{16,12},{20,16},{24,20},{28,24},{1,29},{... | collective-permute-start | bytes 2359304 | tf_op jit(solution)/shard_map/ppermute | solution.py:462
  79.0 0.0 collective-permute-done.6.refs_0_
  79.0 4.2 %backward.9 = (f32[512,1152]{1,0:T(8,128)}, bf16[512,1152]{1,0:T(8,128)(2,1)}, f32[1,512]{1,0:T(1,128)S(1)}) custom-call(s32[1]{0:T(128)S(6)} %copy.22.evicted_ref, bf16[1,2,512,1536]{3,2,1,0:T(8,128)(2,1)} %own_ref.9, bf16[1,512,1536]{2,1,0:T(8,128)(2,1)} %g_ref.9, f32[3,512]{1,0:T(4,128)S(1)} %psum.14.t_ref, ...), custom_call_target="tpu_custom_call", output_to_operand_aliasing={{0}: (9, {}), {1}: (10, {})} | custom-call | tf_op jit(solution)/shard_map/backward/pallas_call | solution.py:230
  83.3 5.8 %psum.15.inner_ref = f32[1,512]{1,0:T(1,128)S(1)} all-reduce(f32[1,512]{1,0:T(1,128)S(1)} %get-tuple-element.50), channel_id=1, replica_groups=mesh['section'=8,'tensor'=4] {'tensor'}, use_global_device_ids=true, to_apply=%region_1.0 | all-reduce | flops 512 | bytes 4096 | tf_op jit(solution)/shard_map/psum | solution.py:510
  89.1 2.2 %finish.3 = (bf16[512,640]{1,0:T(8,128)(2,1)S(1)}, f32[1,512]{1,0:T(1,128)}) custom-call(s32[1]{0:T(128)S(6)} %copy.22.evicted_ref, f32[512,1152]{1,0:T(8,128)} %get-tuple-element.48.a_ref, bf16[512,1152]{1,0:T(8,128)(2,1)} %get-tuple-element.49.x_ref, f32[3,512]{1,0:T(4,128)S(1)} %psum.14.t_ref, f32[1,512]{1,0:T(1,128)S(1)} %row.1.held_ref, ...), custom_call_target="tpu_custom_call" | custom-call | tf_op jit(solution)/shard_map/finish/pallas_call | solution.py:276
  91.3 1.6 %collective-permute-start.9 = (bf16[512,640]{1,0:T(8,128)(2,1)S(1)}, bf16[512,640]{1,0:T(8,128)(2,1)S(1)}, u32[]{:S(2)}, u32[]{:S(2)}) collective-permute-start(bf16[512,640]{1,0:T(8,128)(2,1)S(1)} %get-tuple-element.53), channel_id=1, source_target_pairs={{0,28},{4,0},{8,4},{12,8},{16,12},{20,16},{24,20},{28,24},{1,29},{... | collective-permute-start | bytes 1966088 | tf_op jit(solution)/shard_map/ppermute | solution.py:462
  92.9 1.6 %finish.2 = (bf16[512,512]{1,0:T(8,128)(2,1)S(1)}, f32[1,512]{1,0:T(1,128)S(1)}) custom-call(s32[1]{0:T(128)S(6)} %copy.22.evicted_ref, f32[512,1152]{1,0:T(8,128)} %get-tuple-element.48.a_ref, bf16[512,1152]{1,0:T(8,128)(2,1)} %get-tuple-element.49.x_ref, f32[3,512]{1,0:T(4,128)S(1)} %psum.14.t_ref, f32[1,512]{1,0:T(1,128)S(1)} %row.1.held_ref, ...), custom_call_target="tpu_custom_call" | custom-call | tf_op jit(solution)/shard_map/finish/pallas_call | solution.py:276
  94.5 0.5 collective-permute-start.8
  95.0 0.1 collective-permute-start.7
  95.1 25.6 %collective-permute-done.7.row_ref = f32[1,512]{1,0:T(1,128)S(1)} collective-permute-done((f32[1,512]{1,0:T(1,128)S(1)}, f32[1,512]{1,0:T(1,128)S(1)}, u32[]{:S(2)}, u32[]{:S(2)}) %collective-permute-start.7) | collective-permute-done | bytes 2080 | tf_op jit(solution)/shard_map/ppermute | solution.py:462
  120.7 0.0 collective-permute-done.8.refs_0_
  120.7 0.0 collective-permute-done.9.refs_1_
  120.7 0.0 collective-permute-done.5.pair_ref
  120.7 1.2 place.1
  (3 shorter events, 0.0 us)
Async XLA Ops:
  1.7 0.6 copy-start.2
  2.3 22.4 %collective-permute-start = (bf16[512,256]{1,0:T(8,128)(2,1)S(1)}, bf16[512,256]{1,0:T(8,128)(2,1)S(1)}, u32[]{:S(2)}, u32[]{:S(2)}) collective-permute-start(bf16[512,256]{1,0:T(8,128)(2,1)S(1)} %get-tuple-element.29), channel_id=1, source_target_pairs={{0,16},{4,20},{8,24},{12,28},{16,0},{20,4},{24,8},{28,12},{1,17},{... | collective-permute-start | bytes 786440 | tf_op jit(solution)/shard_map/ppermute | solution.py:462
  6.3 29.8 %collective-permute-start.2 = (bf16[512,256]{1,0:T(8,128)(2,1)S(1)}, bf16[512,256]{1,0:T(8,128)(2,1)S(1)}, u32[]{:S(2)}, u32[]{:S(2)}) collective-permute-start(bf16[512,256]{1,0:T(8,128)(2,1)S(1)} %get-tuple-element.30), channel_id=1, source_target_pairs={{0,16},{4,20},{8,24},{12,28},{16,0},{20,4},{24,8},{28,12},{1,17},{... | collective-permute-start | bytes 786440 | tf_op jit(solution)/shard_map/ppermute | solution.py:462
  17.6 8.1 %copy-start = (f32[1,1536]{1,0:T(1,128)S(1)}, f32[1,1536]{1,0:T(1,128)}, u32[]{:S(2)}) copy-start(f32[1,1536]{1,0:T(1,128)} %gq_ref.11) | copy-start | bytes 18436
  17.7 8.1 %copy-start.1 = (f32[1,1536]{1,0:T(1,128)S(1)}, f32[1,1536]{1,0:T(1,128)}, u32[]{:S(2)}) copy-start(f32[1,1536]{1,0:T(1,128)} %gk_ref.11) | copy-start | bytes 18436
  25.7 21.9 %collective-permute-start.1 = (bf16[528,256]{1,0:T(8,128)(2,1)S(1)}, bf16[528,256]{1,0:T(8,128)(2,1)S(1)}, u32[]{:S(2)}, u32[]{:S(2)}) collective-permute-start(bf16[528,256]{1,0:T(8,128)(2,1)S(1)} %piece_and_row.1), channel_id=1, source_target_pairs={{0,16},{4,20},{8,24},{12,28},{16,0},{20,4},{24,8},{28,12},{1,17},{... | collective-permute-start | bytes 811016 | tf_op jit(solution)/shard_map/ppermute | solution.py:462
  37.1 22.6 %collective-permute-start.3 = (bf16[512,256]{1,0:T(8,128)(2,1)S(1)}, bf16[512,256]{1,0:T(8,128)(2,1)S(1)}, u32[]{:S(2)}, u32[]{:S(2)}) collective-permute-start(bf16[512,256]{1,0:T(8,128)(2,1)S(1)} %get-tuple-element.36), channel_id=1, source_target_pairs={{0,16},{4,20},{8,24},{12,28},{16,0},{20,4},{24,8},{28,12},{1,17},{... | collective-permute-start | bytes 786440 | tf_op jit(solution)/shard_map/ppermute | solution.py:462
  48.5 19.4 %collective-permute-start.4 = (bf16[512,256]{1,0:T(8,128)(2,1)S(1)}, bf16[512,256]{1,0:T(8,128)(2,1)S(1)}, u32[]{:S(2)}, u32[]{:S(2)}) collective-permute-start(bf16[512,256]{1,0:T(8,128)(2,1)S(1)} %get-tuple-element.41), channel_id=1, source_target_pairs={{0,16},{4,20},{8,24},{12,28},{16,0},{20,4},{24,8},{28,12},{1,17},{... | collective-permute-start | bytes 786440 | tf_op jit(solution)/shard_map/ppermute | solution.py:462
  60.7 18.4 %collective-permute-start.6 = (bf16[512,256]{1,0:T(8,128)(2,1)S(1)}, bf16[512,256]{1,0:T(8,128)(2,1)S(1)}, u32[]{:S(2)}, u32[]{:S(2)}) collective-permute-start(bf16[512,256]{1,0:T(8,128)(2,1)S(1)} %get-tuple-element.45), channel_id=1, source_target_pairs={{0,16},{4,20},{8,24},{12,28},{16,0},{20,4},{24,8},{28,12},{1,17},{... | collective-permute-start | bytes 786440 | tf_op jit(solution)/shard_map/ppermute | solution.py:462
  72.2 48.5 %collective-permute-start.5 = (bf16[512,768]{1,0:T(8,128)(2,1)S(1)}, bf16[512,768]{1,0:T(8,128)(2,1)S(1)}, u32[]{:S(2)}, u32[]{:S(2)}) collective-permute-start(bf16[512,768]{1,0:T(8,128)(2,1)S(1)} %hold.1), channel_id=1, source_target_pairs={{0,28},{4,0},{8,4},{12,8},{16,12},{20,16},{24,20},{28,24},{1,29},{... | collective-permute-start | bytes 2359304 | tf_op jit(solution)/shard_map/ppermute | solution.py:462
  91.3 29.4 %collective-permute-start.9 = (bf16[512,640]{1,0:T(8,128)(2,1)S(1)}, bf16[512,640]{1,0:T(8,128)(2,1)S(1)}, u32[]{:S(2)}, u32[]{:S(2)}) collective-permute-start(bf16[512,640]{1,0:T(8,128)(2,1)S(1)} %get-tuple-element.53), channel_id=1, source_target_pairs={{0,28},{4,0},{8,4},{12,8},{16,12},{20,16},{24,20},{28,24},{1,29},{... | collective-permute-start | bytes 1966088 | tf_op jit(solution)/shard_map/ppermute | solution.py:462
  94.5 26.2 %collective-permute-start.8 = (bf16[512,512]{1,0:T(8,128)(2,1)S(1)}, bf16[512,512]{1,0:T(8,128)(2,1)S(1)}, u32[]{:S(2)}, u32[]{:S(2)}) collective-permute-start(bf16[512,512]{1,0:T(8,128)(2,1)S(1)} %get-tuple-element.52), channel_id=1, source_target_pairs={{0,28},{4,0},{8,4},{12,8},{16,12},{20,16},{24,20},{28,24},{1,29},{... | collective-permute-start | bytes 1572872 | tf_op jit(solution)/shard_map/ppermute | solution.py:462
  95.0 25.6 %collective-permute-start.7 = (f32[1,512]{1,0:T(1,128)S(1)}, f32[1,512]{1,0:T(1,128)S(1)}, u32[]{:S(2)}, u32[]{:S(2)}) collective-permute-start(f32[1,512]{1,0:T(1,128)S(1)} %get-tuple-element.51), channel_id=1, source_target_pairs={{0,28},{4,0},{8,4},{12,8},{16,12},{20,16},{24,20},{28,24},{1,29},{... | collective-permute-start | bytes 6152 | tf_op jit(solution)/shard_map/ppermute | solution.py:462
